TPU v7x, 32 devices: a whole 2x2x4 slice. The times are simulated.
32 devices in a mesh: grp: 2 (over y), seq: 8 (over z, x), ch: 2 (over core).
Axes of the slice: x: 2, y: 2, z: 4, core: 2. Of those that a mesh axis runs over, the one named last changes fastest.
Arguments:
- tokens: bfloat16 [2048, 2048], P(('grp', 'seq'), 'ch'), parts along dimension 0, may hold values from -6 to 6
- gate_q: bfloat16 [2048, 2048], P(('grp', 'seq'), 'ch'), parts along dimension 0, may hold values from -6 to 6
- gate_k: bfloat16 [2048, 2048], P(('grp', 'seq'), 'ch'), parts along dimension 0, may hold values from -6 to 6
- w_value: bfloat16 [2048, 2048], P('seq', 'ch'), may hold values from -0.125 to 0.125
- skip: float32 [2048], P('ch'), may hold values from 0.5 to 1.5
- filter_spectrum: bfloat16 [2, 16, 128, 2048], P(None, 'seq', None, 'ch'), may hold values from -12 to 12
- w_out: bfloat16 [2048, 2048], P('seq', 'ch'), may hold values from -0.125 to 0.125
Outputs:
- mixed: bfloat16 [2048, 2048], P(('grp', 'seq'), 'ch'), parts along dimension 0
There are 2 independent parts, one for each index of `grp`. A program takes and returns all parts, laid end to end along the dimension named above; an argument that names none is the same for every part. Nothing has to cross between parts.
All inputs are finite; a program needn't handle non-finite values.
Results may differ from a plain program's by a relative error of at most 0.009.
Values may be sent and summed in bfloat16 or wider, within the bound.
No kernel may reach another device: no remote copies, remote signals or barrier semaphores. Data moves between devices by JAX's collectives and lax.ppermute only.
A program may use at most 64 MiB of HBM per device.

v0:
```python
import math

import jax
import jax.numpy as jnp
from jax import lax
from jax.sharding import PartitionSpec as P


def angles(count, first, second):
    phase = 2.0 * math.pi / count * (first[:, None] * second[None, :] % count).astype(jnp.float32)
    return (jnp.cos(phase), jnp.sin(phase))


def widened(values):
    return lax.optimization_barrier(values).astype(jnp.float32)


def shards(tokens, gate_q, gate_k, w_value, skip, filter_spectrum, w_out):
    seq_count = lax.axis_size("seq")
    position = lax.axis_index("seq")
    length_b = tokens.shape[0]
    columns_each = length_b // seq_count
    freq_rows = 2 * seq_count
    freqs_each = freq_rows // seq_count
    fft_length = freq_rows * length_b
    features = lax.all_gather(tokens, "ch", axis=1, tiled=True)
    value_weight, out_weight = (
        lax.all_gather(w_value, "seq", axis=0, tiled=True),
        lax.all_gather(w_out, "seq", axis=0, tiled=True),
    )
    value = jnp.dot(features, value_weight, preferred_element_type=jnp.float32)
    value = value.astype(jnp.bfloat16)
    drive = (gate_k.astype(jnp.float32) * widened(value)).astype(jnp.bfloat16)
    channels = drive.shape[1]
    columns = lax.all_to_all(drive[None], "seq", split_axis=1, concat_axis=0, tiled=True)
    index_rows = jnp.arange(freq_rows, dtype=jnp.int32)
    index_seq = jnp.arange(seq_count, dtype=jnp.int32)
    index_b = jnp.arange(length_b, dtype=jnp.int32)
    cos_first, sin_first = angles(freq_rows, index_rows, index_seq)
    cos_first = cos_first.astype(jnp.bfloat16)
    sin_first = sin_first.astype(jnp.bfloat16)
    flattened = columns.reshape(seq_count, columns_each * channels)
    real_part = jnp.dot(cos_first, flattened, preferred_element_type=jnp.float32)
    imag_part = jnp.dot(-sin_first, flattened, preferred_element_type=jnp.float32)
    real_part = real_part.reshape(freq_rows, columns_each, channels)
    imag_part = imag_part.reshape(freq_rows, columns_each, channels)
    mine_b = position * columns_each + jnp.arange(columns_each, dtype=jnp.int32)
    twist_cos, twist_sin = angles(fft_length, index_rows, mine_b)
    twist_cos = twist_cos[:, :, None]
    twist_sin = twist_sin[:, :, None]
    section = jnp.stack(
        [
            real_part * twist_cos + imag_part * twist_sin,
            imag_part * twist_cos - real_part * twist_sin,
        ]
    ).astype(jnp.bfloat16)
    spectral = lax.all_to_all(section, "seq", split_axis=1, concat_axis=2, tiled=True)
    cos_seq, sin_seq = angles(length_b, index_b, index_b)
    cos_seq = cos_seq.astype(jnp.bfloat16)
    sin_seq = sin_seq.astype(jnp.bfloat16)
    spectrum_real = jnp.einsum(
        "qb,kbc->kqc", cos_seq, spectral[0], preferred_element_type=jnp.float32
    ) + jnp.einsum("qb,kbc->kqc", sin_seq, spectral[1], preferred_element_type=jnp.float32)
    spectrum_imag = jnp.einsum(
        "qb,kbc->kqc", cos_seq, spectral[1], preferred_element_type=jnp.float32
    ) - jnp.einsum("qb,kbc->kqc", sin_seq, spectral[0], preferred_element_type=jnp.float32)
    filter_real = filter_spectrum[0].astype(jnp.float32)
    filter_imag = filter_spectrum[1].astype(jnp.float32)
    product = jnp.stack(
        [
            spectrum_real * filter_real - spectrum_imag * filter_imag,
            spectrum_real * filter_imag + spectrum_imag * filter_real,
        ]
    ).astype(jnp.bfloat16)
    inverse_real = jnp.einsum(
        "qb,kqc->kbc", cos_seq, product[0], preferred_element_type=jnp.float32
    ) - jnp.einsum("qb,kqc->kbc", sin_seq, product[1], preferred_element_type=jnp.float32)
    inverse_imag = jnp.einsum(
        "qb,kqc->kbc", sin_seq, product[0], preferred_element_type=jnp.float32
    ) + jnp.einsum("qb,kqc->kbc", cos_seq, product[1], preferred_element_type=jnp.float32)
    mine_k = position * freqs_each + jnp.arange(freqs_each, dtype=jnp.int32)
    back_cos, back_sin = angles(fft_length, mine_k, index_b)
    back_cos = back_cos[:, :, None]
    back_sin = back_sin[:, :, None]
    back = jnp.stack(
        [
            inverse_real * back_cos - inverse_imag * back_sin,
            inverse_real * back_sin + inverse_imag * back_cos,
        ]
    ).astype(jnp.bfloat16)
    returned = lax.all_to_all(back, "seq", split_axis=2, concat_axis=1, tiled=True)
    flat_real = returned[0].reshape(freq_rows, columns_each * channels)
    flat_imag = returned[1].reshape(freq_rows, columns_each * channels)
    conv = jnp.dot(cos_first.T, flat_real, preferred_element_type=jnp.float32) - jnp.dot(
        sin_first.T, flat_imag, preferred_element_type=jnp.float32
    )
    conv = (
        (conv * (1.0 / fft_length)).reshape(seq_count, columns_each, channels).astype(jnp.bfloat16)
    )
    conv_rows = lax.all_to_all(conv, "seq", split_axis=0, concat_axis=1, tiled=True)[0]
    gated = (
        gate_q.astype(jnp.float32) * (widened(conv_rows) + skip[None, :] * widened(drive))
    ).astype(jnp.bfloat16)
    partial_value = lax.dot_general(
        gated, out_weight, (((1,), (1,)), ((), ())), preferred_element_type=jnp.float32
    )
    return lax.psum_scatter(
        partial_value.astype(jnp.bfloat16), "ch", scatter_dimension=1, tiled=True
    )


def solution(mesh):
    placed = (
        P(("grp", "seq"), "ch"),
        P(("grp", "seq"), "ch"),
        P(("grp", "seq"), "ch"),
        P("seq", "ch"),
        P("ch"),
        P(None, "seq", None, "ch"),
        P("seq", "ch"),
    )
    return jax.shard_map(
        shards, mesh=mesh, in_specs=placed, out_specs=P(("grp", "seq"), "ch"), check_vma=False
    )
```

profile of v0, /device:TPU:0, one launch (start us, length us, event | category | flops | bytes accessed | tf_op | source)
XLA Modules:
  0.0 246.9 jit_solution(12928465206806638230)
XLA Ops:
  6.5 0.0 copy-start
  6.5 0.0 all-gather.3.cloned.1.call-start
  6.5 0.7 all-gather.3.cloned.1.call-update
  7.3 2.5 %all_gather.9 = bf16[128,2048]{1,0:T(8,128)(2,1)S(1)} all-gather(bf16[128,1024]{1,0:T(8,128)(2,1)} %param.7), channel_id=1, replica_groups=mesh['grp'=2,'seq'=8,'ch'=2] {'ch'}, dimensions={1}, use_global_device_ids=true | all-gather | bytes 786432 | tf_op jit(solution)/shard_map/all_gather | solution.py:26
  9.7 75.9 %all-gather.3.cloned.1.call-done = bf16[2048,1024]{1,0:T(8,128)(2,1)} async-done(((bf16[256,1024]{1,0:T(8,128)(2,1)}), bf16[2048,1024]{1,0:T(8,128)(2,1)}) %all-gather.3.cloned.1.call-update) | async-done | bytes 4194320 | tf_op jit(solution)/shard_map/all_gather | solution.py:28
  85.6 2.9 %convolution_convert_fusion.1 = bf16[128,1024]{1,0:T(8,128)(2,1)S(1)} fusion(bf16[128,2048]{1,0:T(8,128)(2,1)S(1)} %all_gather.9, bf16[2048,1024]{1,0:T(8,128)(2,1)} %all-gather.3.cloned.1.call-done), kind=kOutput, calls=%fused_computation.14 | convolution fusion | flops 537001984 | bytes 4980736 | tf_op jit(solution)/shard_map/dot_general | solution.py:31
  88.5 0.0 copy-done
  88.5 0.1 multiply_convert_fusion.1
  88.6 0.4 copy.62
  89.0 0.5 broadcast.208
  89.5 2.1 reduce.2
  91.7 0.9 reshape.152
  92.6 3.4 %all-to-all-start = ((bf16[8,2,8192]{2,1,0:T(2,128)(2,1)}), bf16[8,2,8192]{2,1,0:T(2,128)(2,1)S(1)}, u32[]{:S(2)}, u32[]{:S(2)}) async-start(bf16[8,2,8192]{2,1,0:T(2,128)(2,1)} %reshape.152), calls=%async_computation | async-start | bytes 524288 | tf_op jit(solution)/shard_map/all_to_all | solution.py:35
  96.0 0.1 fusion.43
  96.1 8.4 %all-to-all-done = bf16[8,2,8192]{2,1,0:T(2,128)(2,1)S(1)} async-done(((bf16[8,2,8192]{2,1,0:T(2,128)(2,1)}), bf16[8,2,8192]{2,1,0:T(2,128)(2,1)S(1)}, u32[]{:S(2)}, u32[]{:S(2)}) %all-to-all-start) | async-done | bytes 262176 | tf_op jit(solution)/shard_map/all_to_all | solution.py:35
  104.5 0.3 reshape.153
  104.8 1.5 bitcast_reduce_fusion
  106.3 0.1 reshape.144
  106.4 0.4 fusion.47
  106.8 0.5 fusion.8
  107.3 0.1 pad_maximum_fusion
  107.4 1.6 copy.38
  109.0 3.6 %all-to-all-start.1 = ((bf16[2,16,16,1024]{3,2,0,1:T(8,128)(2,1)}), bf16[2,16,16,1024]{3,2,0,1:T(8,128)(2,1)S(1)}, u32[]{:S(2)}, u32[]{:S(2)}) async-start(bf16[2,16,16,1024]{3,2,0,1:T(8,128)(2,1)} %copy.38), calls=%async_computation.1 | async-start | bytes 2097152 | tf_op jit(solution)/shard_map/all_to_all | solution.py:57
  112.6 0.2 all-gather.5.cloned.1.call-start
  112.8 0.5 all-gather.5.cloned.1.call-update
  113.3 1.3 fusion.107
  114.6 0.3 copy.57
  114.9 0.3 copy.58
  115.2 0.1 fusion.57
  115.3 37.6 %all-to-all-done.1 = bf16[2,16,16,1024]{3,2,0,1:T(8,128)(2,1)S(1)} async-done(((bf16[2,16,16,1024]{3,2,0,1:T(8,128)(2,1)}), bf16[2,16,16,1024]{3,2,0,1:T(8,128)(2,1)S(1)}, u32[]{:S(2)}, u32[]{:S(2)}) %all-to-all-start.1) | async-done | bytes 1048608 | tf_op jit(solution)/shard_map/all_to_all | solution.py:57
  152.9 0.1 copy.39
  153.0 0.1 fusion.108
  153.2 0.5 fusion.29
  153.7 0.5 fusion.31
  154.3 0.6 fusion.2
  154.8 0.8 fusion.7
  155.6 0.5 fusion.21
  156.2 0.5 fusion.27
  156.7 0.5 convolution_add_fusion
  157.2 0.7 fusion.10
  158.0 0.1 pad_maximum_fusion.1
  158.1 1.0 copy.48
  159.1 55.6 %all_to_all.48 = bf16[2,2,128,1024]{3,1,0,2:T(2,128)(2,1)S(1)} all-to-all(bf16[2,2,128,1024]{3,1,0,2:T(2,128)(2,1)S(1)} %copy.48), channel_id=1, replica_groups=mesh['grp'=2,'seq'=8,'ch'=2] {'seq'}, dimensions={2} | all-to-all | bytes 2097152 | tf_op jit(solution)/shard_map/all_to_all | solution.py:91
  214.6 0.3 copy.49
  214.9 0.1 fusion.106
  215.0 0.0 copy-start.1
  215.1 0.0 copy-start.2
  215.1 0.3 copy.59
  215.5 0.3 copy.60
  215.8 0.3 fusion.52
  216.0 0.3 fusion.1
  216.3 0.9 copy.52
  217.2 3.4 %all-to-all-start.3 = ((bf16[8,16,1024]{2,1,0:T(8,128)(2,1)}), bf16[8,16,1024]{2,1,0:T(8,128)(2,1)S(1)}, u32[]{:S(2)}, u32[]{:S(2)}) async-start(bf16[8,16,1024]{2,1,0:T(8,128)(2,1)} %copy.52), calls=%async_computation.3 | async-start | bytes 524288 | tf_op jit(solution)/shard_map/all_to_all | solution.py:100
  220.6 0.0 reduce-scatter.2.cloned.1.call-start
  220.6 8.3 %all-to-all-done.3 = bf16[8,16,1024]{2,1,0:T(8,128)(2,1)S(1)} async-done(((bf16[8,16,1024]{2,1,0:T(8,128)(2,1)}), bf16[8,16,1024]{2,1,0:T(8,128)(2,1)S(1)}, u32[]{:S(2)}, u32[]{:S(2)}) %all-to-all-start.3) | async-done | bytes 262176 | tf_op jit(solution)/shard_map/all_to_all | solution.py:100
  229.0 0.0 all-gather.5.cloned.1.call-done
  229.0 0.0 copy-done.1
  229.0 0.0 copy-done.2
  229.0 4.5 %convolution_convert_fusion = bf16[128,2048]{1,0:T(8,128)(2,1)} fusion(bf16[2048,1024]{1,0:T(8,128)(2,1)} %all-gather.5.cloned.1.call-done, bf16[128,1024]{1,0:T(8,128)(2,1)S(1)} %multiply_convert_fusion.1, bf16[128,1024]{1,0:T(8,128)(2,1)S(1)} %bitcast.102, bf16[128,1024]{1,0:T(8,128)(2,1)S(1)} %copy-done.1, f32[1024]{0:T(1024)S(1)} %copy-done.2), kind=kOutput, calls=%fused_computation.3 | convolution fusion | flops 538050560 | bytes 5509120 | tf_op jit(solution)/shard_map/dot_general | solution.py:104
  233.5 0.0 reduce-scatter.2.cloned.1.call-update
  233.5 6.9 %reduce-scatter.2.cloned.1.call-done = bf16[128,1024]{1,0:T(8,128)(2,1)} async-done(((bf16[128,2048]{1,0:T(8,128)(2,1)}), bf16[128,1024]{1,0:T(8,128)(2,1)}) %reduce-scatter.2.cloned.1.call-update) | async-done | bytes 262160 | tf_op jit(solution)/shard_map/reduce_scatter | solution.py:107
  (6 shorter events, 0.2 us)
Async XLA Ops:
  6.5 82.0 %copy-start = (bf16[128,1024]{1,0:T(8,128)(2,1)S(1)}, bf16[128,1024]{1,0:T(8,128)(2,1)}, u32[]{:S(2)}) copy-start(bf16[128,1024]{1,0:T(8,128)(2,1)} %param.9) | copy-start | bytes 786436
  6.5 79.1 %all-gather.3.cloned.1.call-start = ((), (), s32[]{:S(2)}) async-start(), calls=%async_computation.5 | async-start | bytes 4718592 | tf_op jit(solution)/shard_map/all_gather | solution.py:28
  92.6 11.9 %all-to-all-start = ((bf16[8,2,8192]{2,1,0:T(2,128)(2,1)}), bf16[8,2,8192]{2,1,0:T(2,128)(2,1)S(1)}, u32[]{:S(2)}, u32[]{:S(2)}) async-start(bf16[8,2,8192]{2,1,0:T(2,128)(2,1)} %reshape.152), calls=%async_computation | async-start | bytes 524288 | tf_op jit(solution)/shard_map/all_to_all | solution.py:35
  109.0 43.9 %all-to-all-start.1 = ((bf16[2,16,16,1024]{3,2,0,1:T(8,128)(2,1)}), bf16[2,16,16,1024]{3,2,0,1:T(8,128)(2,1)S(1)}, u32[]{:S(2)}, u32[]{:S(2)}) async-start(bf16[2,16,16,1024]{3,2,0,1:T(8,128)(2,1)} %copy.38), calls=%async_computation.1 | async-start | bytes 2097152 | tf_op jit(solution)/shard_map/all_to_all | solution.py:57
  112.6 116.4 %all-gather.5.cloned.1.call-start = ((), (), s32[]{:S(2)}) async-start(), calls=%async_computation.6 | async-start | bytes 4718592 | tf_op jit(solution)/shard_map/all_gather | solution.py:29
  215.0 13.9 %copy-start.1 = (bf16[128,1024]{1,0:T(8,128)(2,1)S(1)}, bf16[128,1024]{1,0:T(8,128)(2,1)}, u32[]{:S(2)}) copy-start(bf16[128,1024]{1,0:T(8,128)(2,1)} %param.8) | copy-start | bytes 786436
  215.1 13.9 %copy-start.2 = (f32[1024]{0:T(1024)S(1)}, f32[1024]{0:T(1024)}, u32[]{:S(2)}) copy-start(f32[1024]{0:T(1024)} %param.11) | copy-start | bytes 12292
  217.2 11.8 %all-to-all-start.3 = ((bf16[8,16,1024]{2,1,0:T(8,128)(2,1)}), bf16[8,16,1024]{2,1,0:T(8,128)(2,1)S(1)}, u32[]{:S(2)}, u32[]{:S(2)}) async-start(bf16[8,16,1024]{2,1,0:T(8,128)(2,1)} %copy.52), calls=%async_computation.3 | async-start | bytes 524288 | tf_op jit(solution)/shard_map/all_to_all | solution.py:100
  220.6 19.8 %reduce-scatter.2.cloned.1.call-start = ((), (), s32[]{:S(2)}) async-start(), calls=%async_computation.7 | async-start | bytes 786432 | tf_op jit(solution)/shard_map/reduce_scatter | solution.py:107
Sparse Core Ops, SparseCore 0:
  9.5 76.0 all-gather.2
  115.5 103.5 all-gather.4
  233.6 6.7 reduce-scatter.1
where the time goes:
time: 247 us
  waiting for transfers between devices  138 us (56%)
  blocking collectives  58 us (23%)
  matrix products  13.6 us (6%)
  between operations  13.4 us (5%)
  starting transfers between devices  10.7 us (4%)
  local copies, waits for them, and re-layouts  10.3 us (4%)
  other arithmetic  2.67 us (1%)
    all_gather x1, waiting for transfers between devices, shards(): lax.all_gather(w_value, 'seq', axis=0, tiled=True)  75.9 us
    all_to_all x1, blocking collectives, shards(): lax.all_to_all(back, 'seq', split_axis=2, concat_axis=1, tiled=True)  55.6 us
    all_to_all x1, waiting for transfers between devices, shards(): lax.all_to_all(section, 'seq', split_axis=1, concat_axis=2, tiled=True)  37.6 us
    all_to_all x1, waiting for transfers between devices, shards(): lax.all_to_all(drive[None], 'seq', split_axis=1, concat_axis=0, tiled=True)  8.36 us
    all_to_all x1, waiting for transfers between devices, shards(): lax.all_to_all(conv, 'seq', split_axis=0, concat_axis=1, tiled=True)[0]  8.33 us
    reduce_scatter x1, waiting for transfers between devices, shards(): lax.psum_scatter(partial_value.astype(jnp.bfloat16), 'ch', scatter_dimens...  6.93 us
  transfers between devices with their start and end apart: 6, of which 5 were waited for; matrix products, arithmetic and copies ran while one was open for 4% of the time, Pallas kernels for 0%

commit v1 on v0

--- a/solution.py
+++ b/solution.py
@@ -1,9 +1,17 @@
+import functools
 import math
 
 import jax
 import jax.numpy as jnp
+import numpy as np
 from jax import lax
+from jax.experimental import pallas as pl
+from jax.experimental.pallas import tpu as pltpu
 from jax.sharding import PartitionSpec as P
+
+AXES = ("grp", "seq", "ch")
+BF16 = jnp.bfloat16
+F32 = jnp.float32
 
 
 def angles(count, first, second):
@@ -13,6 +21,334 @@
 
 def widened(values):
     return lax.optimization_barrier(values).astype(jnp.float32)
+
+
+def dot(a, b):
+    return jnp.dot(a, b, preferred_element_type=F32)
+
+
+def dot_t(a, b):
+    return lax.dot_general(a, b, (((1,), (1,)), ((), ())), preferred_element_type=F32)
+
+
+def in_vmem(kernel, out_shape, scratch=(), smem=1, flops=0, moved=0):
+    def call(*operands):
+        specs = [pl.BlockSpec(memory_space=pltpu.SMEM)] * smem
+        specs += [pl.BlockSpec(memory_space=pltpu.VMEM)] * (len(operands) - smem)
+        return pl.pallas_call(
+            kernel,
+            out_shape=out_shape,
+            in_specs=specs,
+            out_specs=jax.tree.map(lambda _: pl.BlockSpec(memory_space=pltpu.VMEM), out_shape),
+            scratch_shapes=list(scratch),
+            compiler_params=pltpu.CompilerParams(vmem_limit_bytes=48 * 1024 * 1024),
+            cost_estimate=pl.CostEstimate(flops=flops, bytes_accessed=moved, transcendentals=0),
+        )(*operands)
+
+    return call
+
+
+def low_lanes(shape):
+    return lax.broadcasted_iota(jnp.int32, shape, len(shape) - 1) < 64
+
+
+def half_turn(values):
+    return pltpu.roll(values, 64, values.ndim - 1)
+
+
+def pack_filter(where, filt, out):
+    y = where[0]
+    low = low_lanes((128, 128))
+    for x in range(2):
+        for j in range(2):
+            base = pl.multiple_of(y * 512 + x * 256 + j * 128, 128)
+            for part in range(2):
+                even = filt[part, 0, :, pl.ds(base, 128)].astype(F32)
+                odd = filt[part, 1, :, pl.ds(base, 128)].astype(F32)
+                out[2 * (2 * j) + x, part] = jnp.where(low, even, half_turn(odd)).astype(BF16)
+                out[2 * (2 * j + 1) + x, part] = jnp.where(low, half_turn(even), odd).astype(BF16)
+
+
+def value_kernel(where, mine, other, *refs):
+    pieces, gates = refs[:8], refs[8:12]
+    drive, outs = refs[12], refs[13:17]
+    acc, packed = refs[17], refs[18]
+    x, z, c = where[1], where[2], where[3]
+    acc[...] = jnp.zeros_like(acc)
+    for r in range(4):
+        owner = lax.rem(z - r + 4, 4)
+        for k in range(2):
+            row = jnp.where(k == 0, x, 1 - x)
+            off = pl.multiple_of(lax.rem(owner, 2) * 512 + row * 256, 256)
+            piece = pieces[2 * r + k]
+
+            @pl.when(owner // 2 == c)
+            def _():
+                acc[...] += dot(mine[:, pl.ds(off, 256)], piece[...])
+
+            @pl.when(owner // 2 != c)
+            def _():
+                acc[...] += dot(other[:, pl.ds(off, 256)], piece[...])
+
+    for p in range(4):
+        rows = pl.ds(p * 128, 128)
+        value = acc[rows, :].astype(BF16).astype(F32)
+        drive[rows, :] = (gates[p][...].astype(F32) * value).astype(BF16)
+    low = low_lanes((256, 128))
+    for j in range(2):
+        lanes = pl.ds(j * 128, 128)
+        first = drive[pl.ds(0, 256), lanes].astype(F32)
+        second = drive[pl.ds(256, 256), lanes].astype(F32)
+        packed[2 * j] = jnp.where(low, first, half_turn(second)).astype(BF16)
+        packed[2 * j + 1] = jnp.where(low, half_turn(first), second).astype(BF16)
+    for r in range(4):
+        outs[r][...] = packed[lax.rem(z + r, 4)]
+
+
+def add(a, b):
+    return b if a is None else a if b is None else a + b
+
+
+def sub(a, b):
+    return a if b is None else -b if a is None else a - b
+
+
+def scaled(a, s):
+    if a is None or abs(s) < 1e-9:
+        return None
+    if abs(s - 1) < 1e-9:
+        return a
+    if abs(s + 1) < 1e-9:
+        return -a
+    return a * np.float32(s)
+
+
+def cmul(a, angle):
+    co, si = math.cos(angle), math.sin(angle)
+    return (sub(scaled(a[0], co), scaled(a[1], si)), add(scaled(a[0], si), scaled(a[1], co)))
+
+
+def cadd(a, b):
+    return (add(a[0], b[0]), add(a[1], b[1]))
+
+
+def conj(a):
+    return (a[0], None if a[1] is None else -a[1])
+
+
+def short_transform(values, count, rows):
+    if len(values) == 1:
+        return [(values[0], None)] * rows
+    half = count // 2
+    need = half // 2 + 1
+    even = short_transform(values[0::2], half, need)
+    odd = short_transform(values[1::2], half, need)
+
+    def at(t, k):
+        k %= half
+        return t[k] if k < need else conj(t[half - k])
+
+    return [cadd(at(even, k), cmul(at(odd, k), -2 * math.pi * k / count)) for k in range(rows)]
+
+
+def conv_kernel(where, d0, d1, d2, d3, filt, table, table_t, o0, o1, o2, o3, data, first, sums):
+    x, z = where[1], where[2]
+    for r, block in enumerate((d0, d1, d2, d3)):
+        base = 2 * lax.rem(z - r + 4, 4)
+        data[base + x] = block[pl.ds(0, 128), :]
+        data[base + 1 - x] = block[pl.ds(128, 128), :]
+    for i in range(8):
+        rows = pl.ds(16 * i, 16)
+        values = [data[a, rows, :].astype(F32) for a in range(8)]
+        spectrum = short_transform(values, 16, 9)
+        for k in range(9):
+            re, im = spectrum[k]
+            first[k, rows, :] = re.astype(BF16)
+            if im is None:
+                im = jnp.zeros_like(re)
+            first[k, pl.ds(128 + 16 * i, 16), :] = im.astype(BF16)
+            if 0 < k < 8:
+                first[16 - k, rows, :] = re.astype(BF16)
+                first[16 - k, pl.ds(128 + 16 * i, 16), :] = (-im).astype(BF16)
+    low = low_lanes((128, 128))
+
+    def back(k):
+        spectrum = dot(table[k], first[k])
+        re, im = spectrum[:128], spectrum[128:]
+        pair = [filt[k // 2, part].astype(F32) for part in range(2)]
+        if k % 2 == 0:
+            fr, fi = [jnp.where(low, f, half_turn(f)) for f in pair]
+        else:
+            fr, fi = [jnp.where(low, half_turn(f), f) for f in pair]
+        product = jnp.concatenate([re * fr - im * fi, re * fi + im * fr], axis=0).astype(BF16)
+        return dot(table_t[k], product)
+
+    sums[0] = back(0)
+    sums[8] = back(8)
+    for k in range(1, 8):
+        one, two = back(k), back(16 - k)
+        sums[k, pl.ds(0, 128)] = one[:128] + two[:128]
+        sums[k, pl.ds(128, 128)] = one[128:] - two[128:]
+    for i in range(16):
+        rows, below = pl.ds(8 * i, 8), pl.ds(128 + 8 * i, 8)
+        scale = 1.0 / 2048
+        re = [sums[k, rows, :] * scale for k in range(9)]
+        im = [None] + [sums[k, below, :] * scale for k in range(1, 8)] + [None]
+        for a in range(5):
+            groups = [None] * 4
+            for k in range(9):
+                ang = 2 * math.pi * (k * a % 16) / 16
+                groups[k % 2] = add(groups[k % 2], scaled(re[k], math.cos(ang)))
+                groups[2 + k % 2] = sub(groups[2 + k % 2], scaled(im[k], math.sin(ang)))
+            ec, oc, es, os = groups
+            data[a, rows, :] = add(add(ec, oc), add(es, os)).astype(BF16)
+            if 0 < a < 4:
+                data[8 - a, rows, :] = sub(sub(add(ec, os), oc), es).astype(BF16)
+    for r, out in enumerate((o0, o1, o2, o3)):
+        base = 2 * lax.rem(z + r, 4)
+        out[pl.ds(0, 128), :] = data[base + x]
+        out[pl.ds(128, 128), :] = data[base + 1 - x]
+
+
+def gate_kernel(where, e0, e1, e2, e3, drive, skip, g0, g1, g2, g3, gated, conv):
+    z = where[2]
+    for r, block in enumerate((e0, e1, e2, e3)):
+        conv[lax.rem(z - r + 4, 4)] = block[...]
+    low = low_lanes((256, 128))
+    for j in range(2):
+        lanes = pl.ds(j * 128, 128)
+        even, odd = conv[2 * j].astype(F32), conv[2 * j + 1].astype(F32)
+        parts = (jnp.where(low, even, half_turn(odd)), jnp.where(low, half_turn(even), odd))
+        for p, gate in enumerate((g0, g1, g2, g3)):
+            rows = pl.ds(p * 128, 128)
+            own = parts[p // 2][(p % 2) * 128 : (p % 2) * 128 + 128]
+            direct = skip[:, lanes] * drive[rows, lanes].astype(F32)
+            gated[rows, lanes] = (gate[:, lanes].astype(F32) * (own + direct)).astype(BF16)
+
+
+def out_kernel(where, gated, other, *refs):
+    mine, theirs = refs[:4], refs[4:8]
+    own, sends = refs[8], refs[9:12]
+    for p in (3, 2, 1, 0):
+        rows = pl.ds(p * 128, 128)
+        for i in range(4):
+            total = dot_t(gated[rows, :], mine[i][...]) + dot_t(other[rows, :], theirs[i][...])
+            lanes = pl.ds(i * 256, 256)
+            if p == 0:
+                own[:, lanes] = total
+            else:
+                sends[p - 1][:, lanes] = total.astype(BF16)
+
+
+def tables():
+    k = np.arange(16)[:, None, None] + 16 * np.arange(128)[None, :, None]
+    phase = 2 * np.pi / 2048 * (k * np.arange(128)[None, None, :] % 2048)
+    co, si = np.cos(phase), np.sin(phase)
+    table = np.concatenate([np.concatenate([co, si], 2), np.concatenate([-si, co], 2)], 1)
+    table = table.astype(jnp.bfloat16)
+    return table, np.ascontiguousarray(table.transpose(0, 2, 1))
+
+
+def planes(tokens, gate_q, gate_k, w_value, skip, filter_spectrum, w_out):
+    y, s, c = (lax.axis_index(a) for a in AXES)
+    x, z = s % 2, s // 2
+    seq, deep = 8, 4
+    where = jnp.stack([y, x, z, c]).astype(jnp.int32)
+
+    def permute(values, move):
+        pairs = []
+        for g in range(2):
+            for i in range(seq):
+                for k in range(2):
+                    g2, z2, x2, k2 = move(g, i // 2, i % 2, k)
+                    pairs.append(((g * seq + i) * 2 + k, (g2 * seq + z2 * 2 + x2) * 2 + k2))
+        return lax.ppermute(values, AXES, pairs)
+
+    def to_x(values):
+        return permute(values, lambda g, z, x, k: (g, z, 1 - x, k))
+
+    def to_core(values):
+        return permute(values, lambda g, z, x, k: (g, z, x, 1 - k))
+
+    def to_z(values, r):
+        return permute(values, lambda g, z, x, k: (g, (z + r) % deep, x, k))
+
+    def to_peer(values, p):
+        return permute(values, lambda g, z, x, k: (g ^ (p // 2), z, x ^ (p % 2), k))
+
+    def quarter(values, p=0):
+        q = (y ^ (p // 2)) * 2 + (x ^ (p % 2))
+        return lax.dynamic_slice_in_dim(values, q * 256, 256, axis=values.ndim - 1)
+
+    def around(weight):
+        pieces = [quarter(weight), to_x(quarter(weight, 1))]
+        for _ in range(3):
+            pieces += [to_z(pieces[-2], 1), to_z(pieces[-1], 1)]
+        return pieces
+
+    value_pieces = around(w_value)
+    received = [
+        to_peer(jnp.concatenate([tokens, quarter(gate_k, p), quarter(gate_q, p)], axis=1), p)
+        for p in (1, 2, 3)
+    ]
+    keys = [quarter(gate_k)] + [m[:, 1024:1280] for m in received]
+    queries = [quarter(gate_q)] + [m[:, 1280:] for m in received]
+    mine = jnp.concatenate([tokens] + [m[:, :1024] for m in received], axis=0)
+    other = to_core(mine)
+    shape = jax.ShapeDtypeStruct
+    packed = in_vmem(pack_filter, shape((8, 2, 128, 128), BF16), moved=1 << 20)(where, filter_spectrum)
+    filters = lax.all_to_all(packed, "seq", split_axis=0, concat_axis=0, tiled=True)
+    block = shape((256, 128), BF16)
+    drive, *sends = in_vmem(
+        value_kernel,
+        [shape((512, 256), BF16)] + [block] * 4,
+        [pltpu.VMEM((512, 256), F32), pltpu.VMEM((4, 256, 128), BF16)],
+        flops=1 << 29,
+        moved=4 << 20,
+    )(where, mine, other, *value_pieces, *keys)
+    columns = [sends[0]] + [to_z(sends[r], r) for r in (1, 2, 3)]
+    table, table_t = tables()
+    sends = in_vmem(
+        conv_kernel,
+        [block] * 4,
+        [
+            pltpu.VMEM((8, 128, 128), BF16),
+            pltpu.VMEM((16, 256, 128), BF16),
+            pltpu.VMEM((9, 256, 128), F32),
+        ],
+        flops=1 << 30,
+        moved=5 << 20,
+    )(where, *columns, filters, table, table_t)
+    rows = [sends[0]] + [to_z(sends[r], r) for r in (1, 2, 3)]
+
+    out_pieces = around(w_out)
+    order = []
+    for i in range(deep):
+        r = (z - i) % deep
+        for k in range(2):
+            which = (x + k) % 2
+            order.append(2 * r + which)
+    stacked = jnp.stack(out_pieces)
+    ordered = [lax.dynamic_index_in_dim(stacked, o, 0, keepdims=False) for o in order]
+    halves = jnp.stack(ordered).reshape(2, 4, 256, 256)
+    keep = lax.dynamic_index_in_dim(halves, c, 0, keepdims=False)
+    give = lax.dynamic_index_in_dim(halves, 1 - c, 0, keepdims=False)
+    theirs = to_core(give)
+    gated = in_vmem(
+        gate_kernel, shape((512, 256), BF16), [pltpu.VMEM((4, 256, 128), BF16)], moved=1 << 20
+    )(where, *rows, drive, quarter(skip)[None, :], *queries)
+    gated_other = to_core(gated)
+    own, *sends = in_vmem(
+        out_kernel,
+        [shape((128, 1024), F32)] + [shape((128, 1024), BF16)] * 3,
+        flops=1 << 30,
+        moved=4 << 20,
+    )(where, gated, gated_other, *[keep[i] for i in range(4)], *[theirs[i] for i in range(4)])
+    parts = [to_peer(sends[p - 1], p) for p in (3, 2, 1)]
+    total = own
+    for part in parts:
+        total = total + part.astype(F32)
+    return total.astype(BF16)
 
 
 def shards(tokens, gate_q, gate_k, w_value, skip, filter_spectrum, w_out):
@@ -119,6 +455,8 @@
         P(None, "seq", None, "ch"),
         P("seq", "ch"),
     )
+    sizes = mesh.shape
+    body = planes if (sizes["grp"], sizes["seq"], sizes["ch"]) == (2, 8, 2) else shards
     return jax.shard_map(
-        shards, mesh=mesh, in_specs=placed, out_specs=P(("grp", "seq"), "ch"), check_vma=False
-    )
+        body, mesh=mesh, in_specs=placed, out_specs=P(("grp", "seq"), "ch"), check_vma=False
+    )

time: 247 us -> 117 us (0.47)
  waiting for transfers between devices: 138 us -> 60.2 us
  blocking collectives: 58 us -> 0 us
  starting transfers between devices: 10.7 us -> 28.8 us
  matrix products: 13.6 us -> 0 us
  between operations: 13.4 us -> 0.5 us
  Pallas kernels: 0 us -> 10.8 us
  local copies, waits for them, and re-layouts: 10.3 us -> 14.3 us
    all_gather x2 -> x0, waiting for transfers between devices: 75.9 us -> none  [the longest x1 75.9 us: shards(): lax.all_gather(w_value, 'seq', axis=0, tiled=True)]
    ppermute x0 -> x29, waiting for transfers between devices: none -> 60.2 us  [permute(): return lax.ppermute(values, AXES, pairs)]
    all_to_all x1 -> x0, blocking collectives: 55.6 us -> none  [shards(): lax.all_to_all(back, 'seq', split_axis=2, concat_axis=1, tiled=True)]
    all_to_all x3 -> x1, waiting for transfers between devices: 54.3 us -> 0.01 us  [planes(): lax.all_to_all(packed, 'seq', split_axis=0, concat_axis=0, tiled=True)]
    ppermute x0 -> x29, starting transfers between devices: none -> 24.9 us  [permute(): return lax.ppermute(values, AXES, pairs)]
    dot_general x14 -> x0, matrix products: 13.6 us -> none  [the longest x1 4.49 us: shards(): lax.dot_general(gated, out_weight, (((1,), (1,)), ((), ())), preferred_el...]
    pallas_call x0 -> x5, Pallas kernels: none -> 10.8 us  [call(): pl.pallas_call(kernel, out_shape=out_shape, in_specs=specs, out_specs=jax...]
    reduce_scatter x1 -> x0, waiting for transfers between devices: 6.93 us -> none  [shards(): lax.psum_scatter(partial_value.astype(jnp.bfloat16), 'ch', scatter_dimens...]
  transfers between devices with their start and end apart: 6 -> 30, of which waited for: 5 -> 16; matrix products, arithmetic and copies ran while one was open for 4% -> 9% of each run, Pallas kernels for 0% -> 8%
where the time goes in v1:
time: 117 us
  waiting for transfers between devices  60.2 us (51%)
  starting transfers between devices  28.8 us (25%)
  local copies, waits for them, and re-layouts  14.3 us (12%)
  Pallas kernels  10.8 us (9%)
  other arithmetic  2.04 us (2%)
    ppermute x29, waiting for transfers between devices, permute(): return lax.ppermute(values, AXES, pairs)  60.2 us
    ppermute x29, starting transfers between devices, permute(): return lax.ppermute(values, AXES, pairs)  24.9 us
    pallas_call x5, Pallas kernels, call(): pl.pallas_call(kernel, out_shape=out_shape, in_specs=specs, out_specs=jax...  10.8 us
    dynamic_slice x5, local copies, waits for them, and re-layouts, quarter(): return lax.dynamic_slice_in_dim(values, q * 256, 256, axis=values.ndim - 1)  4.4 us
    all_to_all x1, starting transfers between devices, planes(): lax.all_to_all(packed, 'seq', split_axis=0, concat_axis=0, tiled=True)  3.87 us
    unnamed x30, local copies, waits for them, and re-layouts  2.73 us
  transfers between devices with their start and end apart: 30, of which 16 were waited for; matrix products, arithmetic and copies ran while one was open for 9% of the time, Pallas kernels for 8%

profile of v1, /device:TPU:0, one launch (start us, length us, event | category | flops | bytes accessed | tf_op | source)
XLA Modules:
  0.0 116.6 jit_solution(1909698385539665863)
XLA Ops:
  0.0 1.1 constant_dynamic-slice_fusion.2
  1.1 1.0 constant_dynamic-slice_fusion.3
  2.1 1.0 fusion
  3.1 4.0 %collective-permute-start.2 = (bf16[128,1536]{1,0:T(8,128)(2,1)S(1)}, bf16[128,1536]{1,0:T(8,128)(2,1)}, u32[]{:S(2)}, u32[]{:S(2)}) collective-permute-start(bf16[128,1536]{1,0:T(8,128)(2,1)S(1)} %get-tuple-element.59), channel_id=1, source_target_pairs={{0,18},{1,19},{2,16},{3,17},{4,22},{5,23},{6,20},{7,21},{8,26},{9,... | collective-permute-start | bytes 1179656 | tf_op jit(solution)/shard_map/ppermute | solution.py:265
  7.1 0.5 collective-permute-start.1
  7.6 0.7 constant_dynamic-slice_fusion.4
  8.3 0.1 collective-permute-start.4
  8.4 2.0 %collective-permute-start.5 = (bf16[256,256]{1,0:T(8,128)(2,1)S(1)}, bf16[256,256]{1,0:T(8,128)(2,1)S(1)}, u32[]{:S(2)}, u32[]{:S(2)}) collective-permute-start(bf16[256,256]{1,0:T(8,128)(2,1)S(1)} %get-tuple-element.42.refs_0_), channel_id=1, source_target_pairs={{0,4},{1,5},{2,6},{3,7},{4,8},{5,9},{6,10},{7,11},{8,12},{9,13},{1... | collective-permute-start | bytes 393224 | tf_op jit(solution)/shard_map/ppermute | solution.py:265
  10.4 0.9 constant_dynamic-slice_fusion
  11.3 1.6 %collective-permute-start.18 = (bf16[256,256]{1,0:T(8,128)(2,1)S(1)}, bf16[256,256]{1,0:T(8,128)(2,1)S(1)}, u32[]{:S(2)}, u32[]{:S(2)}) collective-permute-start(bf16[256,256]{1,0:T(8,128)(2,1)S(1)} %constant_dynamic-slice_fusion), channel_id=1, source_target_pairs={{0,2},{1,3},{2,0},{3,1},{4,6},{5,7},{6,4},{7,5},{8,10},{9,11},{10,... | collective-permute-start | bytes 393224 | tf_op jit(solution)/shard_map/ppermute | solution.py:265
  12.8 0.1 pad_add_fusion.where
  12.9 1.6 %shard_map.92 = bf16[8,2,128,128]{3,2,1,0:T(8,128)(2,1)} custom-call(s32[4]{0:T(128)S(1)} %pad_add_fusion.where, bf16[2,2,128,1024]{3,2,1,0:T(8,128)(2,1)S(1)} %copy-done.2), custom_call_target="tpu_custom_call" | custom-call | bytes 1048576 | tf_op jit(solution)/shard_map/pallas_call | solution.py:38
  14.5 3.9 %all-to-all-start = ((bf16[8,2,128,128]{3,2,1,0:T(8,128)(2,1)}), bf16[8,2,128,128]{3,2,1,0:T(8,128)(2,1)S(1)}, u32[]{:S(2)}, u32[]{:S(2)}) async-start(bf16[8,2,128,128]{3,2,1,0:T(8,128)(2,1)} %shard_map.92), calls=%async_computation | async-start | bytes 1048576 | tf_op jit(solution)/shard_map/all_to_all | solution.py:300
  18.5 0.9 bitcast_dynamic-update-slice_fusion.7
  19.4 5.2 %collective-permute-done.18 = bf16[256,256]{1,0:T(8,128)(2,1)S(1)} collective-permute-done((bf16[256,256]{1,0:T(8,128)(2,1)S(1)}, bf16[256,256]{1,0:T(8,128)(2,1)S(1)}, u32[]{:S(2)}, u32[]{:S(2)}) %collective-permute-start.18) | collective-permute-done | bytes 131104 | tf_op jit(solution)/shard_map/ppermute | solution.py:265
  24.7 2.5 %collective-permute-start.19 = (bf16[256,256]{1,0:T(8,128)(2,1)S(1)}, bf16[256,256]{1,0:T(8,128)(2,1)S(1)}, u32[]{:S(2)}, u32[]{:S(2)}) collective-permute-start(bf16[256,256]{1,0:T(8,128)(2,1)S(1)} %get-tuple-element.32), channel_id=1, source_target_pairs={{0,4},{1,5},{2,6},{3,7},{4,8},{5,9},{6,10},{7,11},{8,12},{9,13},{1... | collective-permute-start | bytes 393224 | tf_op jit(solution)/shard_map/ppermute | solution.py:265
  27.2 6.5 %collective-permute-done.19 = bf16[256,256]{1,0:T(8,128)(2,1)S(1)} collective-permute-done((bf16[256,256]{1,0:T(8,128)(2,1)S(1)}, bf16[256,256]{1,0:T(8,128)(2,1)S(1)}, u32[]{:S(2)}, u32[]{:S(2)}) %collective-permute-start.19) | collective-permute-done | bytes 131104 | tf_op jit(solution)/shard_map/ppermute | solution.py:265
  33.7 0.0 collective-permute-start.20
  33.7 0.0 collective-permute-done.4.refs_1_
  33.7 1.5 %collective-permute-start.21 = (bf16[256,256]{1,0:T(8,128)(2,1)S(1)}, bf16[256,256]{1,0:T(8,128)(2,1)S(1)}, u32[]{:S(2)}, u32[]{:S(2)}) collective-permute-start(bf16[256,256]{1,0:T(8,128)(2,1)S(1)} %collective-permute-done.19), channel_id=1, source_target_pairs={{0,4},{1,5},{2,6},{3,7},{4,8},{5,9},{6,10},{7,11},{8,12},{9,13},{1... | collective-permute-start | bytes 393224 | tf_op jit(solution)/shard_map/ppermute | solution.py:265
  35.2 5.2 %collective-permute-done.20 = bf16[256,256]{1,0:T(8,128)(2,1)S(1)} collective-permute-done((bf16[256,256]{1,0:T(8,128)(2,1)S(1)}, bf16[256,256]{1,0:T(8,128)(2,1)S(1)}, u32[]{:S(2)}, u32[]{:S(2)}) %collective-permute-start.20) | collective-permute-done | bytes 131104 | tf_op jit(solution)/shard_map/ppermute | solution.py:265
  40.4 0.0 collective-permute-start.6
  40.4 2.4 %collective-permute-done.21 = bf16[256,256]{1,0:T(8,128)(2,1)S(1)} collective-permute-done((bf16[256,256]{1,0:T(8,128)(2,1)S(1)}, bf16[256,256]{1,0:T(8,128)(2,1)S(1)}, u32[]{:S(2)}, u32[]{:S(2)}) %collective-permute-start.21) | collective-permute-done | bytes 131104 | tf_op jit(solution)/shard_map/ppermute | solution.py:265
  42.9 0.0 copy-start.3
  42.9 0.9 collective-permute-start
  43.8 3.4 %collective-permute-done.6.refs_3_ = bf16[256,256]{1,0:T(8,128)(2,1)S(1)} collective-permute-done((bf16[256,256]{1,0:T(8,128)(2,1)S(1)}, bf16[256,256]{1,0:T(8,128)(2,1)S(1)}, u32[]{:S(2)}, u32[]{:S(2)}) %collective-permute-start.6) | collective-permute-done | bytes 131104 | tf_op jit(solution)/shard_map/ppermute | solution.py:265
  47.2 3.8 %collective-permute-done.22 = bf16[256,256]{1,0:T(8,128)(2,1)S(1)} collective-permute-done((bf16[256,256]{1,0:T(8,128)(2,1)S(1)}, bf16[256,256]{1,0:T(8,128)(2,1)S(1)}, u32[]{:S(2)}, u32[]{:S(2)}) %collective-permute-start.22) | collective-permute-done | bytes 131104 | tf_op jit(solution)/shard_map/ppermute | solution.py:265
  51.0 0.0 collective-permute-start.23
  51.0 3.0 %collective-permute-done.7.refs_4_ = bf16[256,256]{1,0:T(8,128)(2,1)S(1)} collective-permute-done((bf16[256,256]{1,0:T(8,128)(2,1)S(1)}, bf16[256,256]{1,0:T(8,128)(2,1)S(1)}, u32[]{:S(2)}, u32[]{:S(2)}) %collective-permute-start.7) | collective-permute-done | bytes 131104 | tf_op jit(solution)/shard_map/ppermute | solution.py:265
  54.0 4.7 %collective-permute-done.23 = bf16[256,256]{1,0:T(8,128)(2,1)S(1)} collective-permute-done((bf16[256,256]{1,0:T(8,128)(2,1)S(1)}, bf16[256,256]{1,0:T(8,128)(2,1)S(1)}, u32[]{:S(2)}, u32[]{:S(2)}) %collective-permute-start.23) | collective-permute-done | bytes 131104 | tf_op jit(solution)/shard_map/ppermute | solution.py:265
  58.7 3.1 %collective-permute-done.8.refs_5_ = bf16[256,256]{1,0:T(8,128)(2,1)S(1)} collective-permute-done((bf16[256,256]{1,0:T(8,128)(2,1)S(1)}, bf16[256,256]{1,0:T(8,128)(2,1)S(1)}, u32[]{:S(2)}, u32[]{:S(2)}) %collective-permute-start.8) | collective-permute-done | bytes 131104 | tf_op jit(solution)/shard_map/ppermute | solution.py:265
  61.8 1.0 slice.74
  62.8 1.0 slice.73
  63.8 0.1 pad_maximum_fusion.mine
  63.9 0.1 collective-permute-start.3
  64.0 0.0 copy-start.4
  64.0 0.9 fusion.4
  64.9 3.6 %collective-permute-done.24 = bf16[256,256]{1,0:T(8,128)(2,1)S(1)} collective-permute-done((bf16[256,256]{1,0:T(8,128)(2,1)S(1)}, bf16[256,256]{1,0:T(8,128)(2,1)S(1)}, u32[]{:S(2)}, u32[]{:S(2)}) %collective-permute-start.24) | collective-permute-done | bytes 131104 | tf_op jit(solution)/shard_map/ppermute | solution.py:265
  68.8 0.9 dynamic-slice_bitcast_fusion
  69.7 1.0 fusion.3
  70.8 3.4 %shard_map.91 = (bf16[512,256]{1,0:T(8,128)(2,1)S(1)}, bf16[256,128]{1,0:T(8,128)(2,1)S(1)}, bf16[256,128]{1,0:T(8,128)(2,1)}, bf16[256,128]{1,0:T(8,128)(2,1)}, bf16[256,128]{1,0:T(8,128)(2,1)}) custom-call(s32[4]{0:T(128)S(1)} %pad_add_fusion.where, bf16[512,1024]{1,0:T(8,128)(2,1)S(1)} %pad_maximum_fusion.mine, ...), custom_call_target="tpu_custom_call" | custom-call | flops 536870912 | bytes 4194304 | tf_op jit(solution)/shard_map/pallas_call | solution.py:38
  74.1 1.3 %collective-permute-start.12 = (bf16[256,128]{1,0:T(8,128)(2,1)}, bf16[256,128]{1,0:T(8,128)(2,1)S(1)}, u32[]{:S(2)}, u32[]{:S(2)}) collective-permute-start(bf16[256,128]{1,0:T(8,128)(2,1)} %get-tuple-element.20), channel_id=1, source_target_pairs={{0,8},{1,9},{2,10},{3,11},{4,12},{5,13},{6,14},{7,15},{8,0},{9,1},... | collective-permute-start | bytes 196616 | tf_op jit(solution)/shard_map/ppermute | solution.py:265
  75.4 2.9 %collective-permute-start.13 = (bf16[256,128]{1,0:T(8,128)(2,1)}, bf16[256,128]{1,0:T(8,128)(2,1)S(1)}, u32[]{:S(2)}, u32[]{:S(2)}) collective-permute-start(bf16[256,128]{1,0:T(8,128)(2,1)} %get-tuple-element.21), channel_id=1, source_target_pairs={{0,12},{1,13},{2,14},{3,15},{4,0},{5,1},{6,2},{7,3},{8,4},{9,5},{1... | collective-permute-start | bytes 196616 | tf_op jit(solution)/shard_map/ppermute | solution.py:265
  78.3 2.9 %collective-permute-done.11.d1 = bf16[256,128]{1,0:T(8,128)(2,1)S(1)} collective-permute-done((bf16[256,128]{1,0:T(8,128)(2,1)}, bf16[256,128]{1,0:T(8,128)(2,1)S(1)}, u32[]{:S(2)}, u32[]{:S(2)}) %collective-permute-start.11) | collective-permute-done | bytes 65568 | tf_op jit(solution)/shard_map/ppermute | solution.py:265
  81.2 1.7 %collective-permute-done.12.d2 = bf16[256,128]{1,0:T(8,128)(2,1)S(1)} collective-permute-done((bf16[256,128]{1,0:T(8,128)(2,1)}, bf16[256,128]{1,0:T(8,128)(2,1)S(1)}, u32[]{:S(2)}, u32[]{:S(2)}) %collective-permute-start.12) | collective-permute-done | bytes 65568 | tf_op jit(solution)/shard_map/ppermute | solution.py:265
  82.8 1.6 %copy-done.1 = bf16[16,256,256]{2,1,0:T(8,128)(2,1)S(1)} copy-done((bf16[16,256,256]{2,1,0:T(8,128)(2,1)S(1)}, bf16[16,256,256]{2,1,0:T(8,128)(2,1)}, u32[]{:S(2)}) %copy-start.1) | copy-done | bytes 2097176
  84.4 3.1 %shard_map.93 = (bf16[256,128]{1,0:T(8,128)(2,1)S(1)}, bf16[256,128]{1,0:T(8,128)(2,1)}, bf16[256,128]{1,0:T(8,128)(2,1)}, bf16[256,128]{1,0:T(8,128)(2,1)}) custom-call(s32[4]{0:T(128)S(1)} %pad_add_fusion.where, bf16[256,128]{1,0:T(8,128)(2,1)S(1)} %get-tuple-element.18.d0, bf16[256,128]{1,0:T(8,128)(2,1)S(1)} %collective-permute-done.11.d1, ...), custom_call_target="tpu_custom_call" | custom-call | flops 1073741824 | bytes 5242880 | tf_op jit(solution)/shard_map/pallas_call | solution.py:38
  87.5 1.6 %collective-permute-start.14 = (bf16[256,128]{1,0:T(8,128)(2,1)}, bf16[256,128]{1,0:T(8,128)(2,1)S(1)}, u32[]{:S(2)}, u32[]{:S(2)}) collective-permute-start(bf16[256,128]{1,0:T(8,128)(2,1)} %get-tuple-element.23), channel_id=1, source_target_pairs={{0,4},{1,5},{2,6},{3,7},{4,8},{5,9},{6,10},{7,11},{8,12},{9,13},{1... | collective-permute-start | bytes 196616 | tf_op jit(solution)/shard_map/ppermute | solution.py:265
  89.1 1.2 %collective-permute-start.15 = (bf16[256,128]{1,0:T(8,128)(2,1)}, bf16[256,128]{1,0:T(8,128)(2,1)S(1)}, u32[]{:S(2)}, u32[]{:S(2)}) collective-permute-start(bf16[256,128]{1,0:T(8,128)(2,1)} %get-tuple-element.24), channel_id=1, source_target_pairs={{0,8},{1,9},{2,10},{3,11},{4,12},{5,13},{6,14},{7,15},{8,0},{9,1},... | collective-permute-start | bytes 196616 | tf_op jit(solution)/shard_map/ppermute | solution.py:265
  90.3 1.3 %collective-permute-start.16 = (bf16[256,128]{1,0:T(8,128)(2,1)}, bf16[256,128]{1,0:T(8,128)(2,1)S(1)}, u32[]{:S(2)}, u32[]{:S(2)}) collective-permute-start(bf16[256,128]{1,0:T(8,128)(2,1)} %get-tuple-element.25), channel_id=1, source_target_pairs={{0,12},{1,13},{2,14},{3,15},{4,0},{5,1},{6,2},{7,3},{8,4},{9,5},{1... | collective-permute-start | bytes 196616 | tf_op jit(solution)/shard_map/ppermute | solution.py:265
  91.5 0.8 dynamic_slice.80
  92.3 1.9 %collective-permute-done.14.e1 = bf16[256,128]{1,0:T(8,128)(2,1)S(1)} collective-permute-done((bf16[256,128]{1,0:T(8,128)(2,1)}, bf16[256,128]{1,0:T(8,128)(2,1)S(1)}, u32[]{:S(2)}, u32[]{:S(2)}) %collective-permute-start.14) | collective-permute-done | bytes 65568 | tf_op jit(solution)/shard_map/ppermute | solution.py:265
  94.2 1.9 %collective-permute-done.15.e2 = bf16[256,128]{1,0:T(8,128)(2,1)S(1)} collective-permute-done((bf16[256,128]{1,0:T(8,128)(2,1)}, bf16[256,128]{1,0:T(8,128)(2,1)S(1)}, u32[]{:S(2)}, u32[]{:S(2)}) %collective-permute-start.15) | collective-permute-done | bytes 65568 | tf_op jit(solution)/shard_map/ppermute | solution.py:265
  96.2 0.8 shard_map.94.gated
  96.9 0.1 collective-permute-start.17
  97.0 1.1 dynamic-slice_bitcast_fusion.1
  98.2 1.1 slice_bitcast_fusion
  99.3 2.0 %shard_map.95 = (f32[128,1024]{1,0:T(8,128)S(1)}, bf16[128,1024]{1,0:T(8,128)(2,1)S(1)}, bf16[128,1024]{1,0:T(8,128)(2,1)S(1)}, bf16[128,1024]{1,0:T(8,128)(2,1)S(1)}) custom-call(s32[4]{0:T(128)S(1)} %pad_add_fusion.where, bf16[512,256]{1,0:T(8,128)(2,1)S(1)} %shard_map.94.gated, bf16[512,256]{1,0:T(8,128)(2,1)S(1)} %collective-permute-done.17.other, ...), custom_call_target="tpu_custom_call" | custom-call | flops 1073741824 | bytes 4194304 | tf_op jit(solution)/shard_map/pallas_call | solution.py:38
  101.3 0.1 collective-permute-start.28
  101.4 0.7 collective-permute-start.27
  102.1 2.7 %collective-permute-start.26 = (bf16[128,1024]{1,0:T(8,128)(2,1)S(1)}, bf16[128,1024]{1,0:T(8,128)(2,1)S(1)}, u32[]{:S(2)}, u32[]{:S(2)}) collective-permute-start(bf16[128,1024]{1,0:T(8,128)(2,1)S(1)} %get-tuple-element.28), channel_id=1, source_target_pairs={{0,18},{1,19},{2,16},{3,17},{4,22},{5,23},{6,20},{7,21},{8,26},{9,... | collective-permute-start | bytes 786440 | tf_op jit(solution)/shard_map/ppermute | solution.py:265
  104.9 5.6 %collective-permute-done.28 = bf16[128,1024]{1,0:T(8,128)(2,1)S(1)} collective-permute-done((bf16[128,1024]{1,0:T(8,128)(2,1)S(1)}, bf16[128,1024]{1,0:T(8,128)(2,1)S(1)}, u32[]{:S(2)}, u32[]{:S(2)}) %collective-permute-start.28) | collective-permute-done | bytes 262176 | tf_op jit(solution)/shard_map/ppermute | solution.py:265
  110.5 5.3 %collective-permute-done.27 = bf16[128,1024]{1,0:T(8,128)(2,1)S(1)} collective-permute-done((bf16[128,1024]{1,0:T(8,128)(2,1)S(1)}, bf16[128,1024]{1,0:T(8,128)(2,1)S(1)}, u32[]{:S(2)}, u32[]{:S(2)}) %collective-permute-start.27) | collective-permute-done | bytes 262176 | tf_op jit(solution)/shard_map/ppermute | solution.py:265
  115.8 0.9 add_convert_fusion
  (51 shorter events, 0.3 us)
Async XLA Ops:
  0.0 7.6 %copy-start.7 = (bf16[256,1024]{1,0:T(8,128)(2,1)S(1)}, bf16[256,1024]{1,0:T(8,128)(2,1)}, u32[]{:S(2)}) copy-start(bf16[256,1024]{1,0:T(8,128)(2,1)} %param.12) | copy-start | bytes 1572868
  0.0 12.9 %copy-start.2 = (bf16[2,2,128,1024]{3,2,1,0:T(8,128)(2,1)S(1)}, bf16[2,2,128,1024]{3,2,1,0:T(8,128)(2,1)}, u32[]{:S(2)}) copy-start(bf16[2,2,128,1024]{3,2,1,0:T(8,128)(2,1)} %filt.1) | copy-start | bytes 3145732
  3.1 58.7 %collective-permute-start.2 = (bf16[128,1536]{1,0:T(8,128)(2,1)S(1)}, bf16[128,1536]{1,0:T(8,128)(2,1)}, u32[]{:S(2)}, u32[]{:S(2)}) collective-permute-start(bf16[128,1536]{1,0:T(8,128)(2,1)S(1)} %get-tuple-element.59), channel_id=1, source_target_pairs={{0,18},{1,19},{2,16},{3,17},{4,22},{5,23},{6,20},{7,21},{8,26},{9,... | collective-permute-start | bytes 1179656 | tf_op jit(solution)/shard_map/ppermute | solution.py:265
  7.1 55.7 %collective-permute-start.1 = (bf16[128,1536]{1,0:T(8,128)(2,1)S(1)}, bf16[128,1536]{1,0:T(8,128)(2,1)}, u32[]{:S(2)}, u32[]{:S(2)}) collective-permute-start(bf16[128,1536]{1,0:T(8,128)(2,1)S(1)} %get-tuple-element.58), channel_id=1, source_target_pairs={{0,16},{1,17},{2,18},{3,19},{4,20},{5,21},{6,22},{7,23},{8,24},{9,... | collective-permute-start | bytes 1179656 | tf_op jit(solution)/shard_map/ppermute | solution.py:265
  8.3 25.4 %collective-permute-start.4 = (bf16[256,256]{1,0:T(8,128)(2,1)}, bf16[256,256]{1,0:T(8,128)(2,1)S(1)}, u32[]{:S(2)}, u32[]{:S(2)}) collective-permute-start(bf16[256,256]{1,0:T(8,128)(2,1)} %get-tuple-element.41), channel_id=1, source_target_pairs={{0,2},{1,3},{2,0},{3,1},{4,6},{5,7},{6,4},{7,5},{8,10},{9,11},{10,... | collective-permute-start | bytes 393224 | tf_op jit(solution)/shard_map/ppermute | solution.py:265
  8.4 34.5 %collective-permute-start.5 = (bf16[256,256]{1,0:T(8,128)(2,1)S(1)}, bf16[256,256]{1,0:T(8,128)(2,1)S(1)}, u32[]{:S(2)}, u32[]{:S(2)}) collective-permute-start(bf16[256,256]{1,0:T(8,128)(2,1)S(1)} %get-tuple-element.42.refs_0_), channel_id=1, source_target_pairs={{0,4},{1,5},{2,6},{3,7},{4,8},{5,9},{6,10},{7,11},{8,12},{9,13},{1... | collective-permute-start | bytes 393224 | tf_op jit(solution)/shard_map/ppermute | solution.py:265
  11.3 13.4 %collective-permute-start.18 = (bf16[256,256]{1,0:T(8,128)(2,1)S(1)}, bf16[256,256]{1,0:T(8,128)(2,1)S(1)}, u32[]{:S(2)}, u32[]{:S(2)}) collective-permute-start(bf16[256,256]{1,0:T(8,128)(2,1)S(1)} %constant_dynamic-slice_fusion), channel_id=1, source_target_pairs={{0,2},{1,3},{2,0},{3,1},{4,6},{5,7},{6,4},{7,5},{8,10},{9,11},{10,... | collective-permute-start | bytes 393224 | tf_op jit(solution)/shard_map/ppermute | solution.py:265
  14.5 63.8 %all-to-all-start = ((bf16[8,2,128,128]{3,2,1,0:T(8,128)(2,1)}), bf16[8,2,128,128]{3,2,1,0:T(8,128)(2,1)S(1)}, u32[]{:S(2)}, u32[]{:S(2)}) async-start(bf16[8,2,128,128]{3,2,1,0:T(8,128)(2,1)} %shard_map.92), calls=%async_computation | async-start | bytes 1048576 | tf_op jit(solution)/shard_map/all_to_all | solution.py:300
  18.4 45.4 %copy-start.6 = (bf16[128,1024]{1,0:T(8,128)(2,1)S(1)}, bf16[128,1024]{1,0:T(8,128)(2,1)}, u32[]{:S(2)}) copy-start(bf16[128,1024]{1,0:T(8,128)(2,1)} %param.9) | copy-start | bytes 786436
  24.7 9.0 %collective-permute-start.19 = (bf16[256,256]{1,0:T(8,128)(2,1)S(1)}, bf16[256,256]{1,0:T(8,128)(2,1)S(1)}, u32[]{:S(2)}, u32[]{:S(2)}) collective-permute-start(bf16[256,256]{1,0:T(8,128)(2,1)S(1)} %get-tuple-element.32), channel_id=1, source_target_pairs={{0,4},{1,5},{2,6},{3,7},{4,8},{5,9},{6,10},{7,11},{8,12},{9,13},{1... | collective-permute-start | bytes 393224 | tf_op jit(solution)/shard_map/ppermute | solution.py:265
  33.7 6.8 %collective-permute-start.20 = (bf16[256,256]{1,0:T(8,128)(2,1)S(1)}, bf16[256,256]{1,0:T(8,128)(2,1)S(1)}, u32[]{:S(2)}, u32[]{:S(2)}) collective-permute-start(bf16[256,256]{1,0:T(8,128)(2,1)S(1)} %collective-permute-done.18), channel_id=1, source_target_pairs={{0,4},{1,5},{2,6},{3,7},{4,8},{5,9},{6,10},{7,11},{8,12},{9,13},{1... | collective-permute-start | bytes 393224 | tf_op jit(solution)/shard_map/ppermute | solution.py:265
  33.7 9.2 %collective-permute-start.21 = (bf16[256,256]{1,0:T(8,128)(2,1)S(1)}, bf16[256,256]{1,0:T(8,128)(2,1)S(1)}, u32[]{:S(2)}, u32[]{:S(2)}) collective-permute-start(bf16[256,256]{1,0:T(8,128)(2,1)S(1)} %collective-permute-done.19), channel_id=1, source_target_pairs={{0,4},{1,5},{2,6},{3,7},{4,8},{5,9},{6,10},{7,11},{8,12},{9,13},{1... | collective-permute-start | bytes 393224 | tf_op jit(solution)/shard_map/ppermute | solution.py:265
  40.4 6.8 %collective-permute-start.6 = (bf16[256,256]{1,0:T(8,128)(2,1)S(1)}, bf16[256,256]{1,0:T(8,128)(2,1)S(1)}, u32[]{:S(2)}, u32[]{:S(2)}) collective-permute-start(bf16[256,256]{1,0:T(8,128)(2,1)S(1)} %collective-permute-done.4.refs_1_), channel_id=1, source_target_pairs={{0,4},{1,5},{2,6},{3,7},{4,8},{5,9},{6,10},{7,11},{8,12},{9,13},{1... | collective-permute-start | bytes 393224 | tf_op jit(solution)/shard_map/ppermute | solution.py:265
  42.8 8.1 %collective-permute-start.22 = (bf16[256,256]{1,0:T(8,128)(2,1)S(1)}, bf16[256,256]{1,0:T(8,128)(2,1)S(1)}, u32[]{:S(2)}, u32[]{:S(2)}) collective-permute-start(bf16[256,256]{1,0:T(8,128)(2,1)S(1)} %collective-permute-done.20), channel_id=1, source_target_pairs={{0,4},{1,5},{2,6},{3,7},{4,8},{5,9},{6,10},{7,11},{8,12},{9,13},{1... | collective-permute-start | bytes 393224 | tf_op jit(solution)/shard_map/ppermute | solution.py:265
  42.9 21.0 %copy-start.3 = (bf16[256,256]{1,0:T(8,128)(2,1)}, bf16[256,256]{1,0:T(8,128)(2,1)S(1)}, u32[]{:S(2)}) copy-start(bf16[256,256]{1,0:T(8,128)(2,1)S(1)} %collective-permute-done.5.refs_2_) | copy-start | bytes 393220
  42.9 20.9 %collective-permute-start = (bf16[128,1536]{1,0:T(8,128)(2,1)S(1)}, bf16[128,1536]{1,0:T(8,128)(2,1)S(1)}, u32[]{:S(2)}, u32[]{:S(2)}) collective-permute-start(bf16[128,1536]{1,0:T(8,128)(2,1)S(1)} %get-tuple-element.57), channel_id=1, source_target_pairs={{0,2},{1,3},{2,0},{3,1},{4,6},{5,7},{6,4},{7,5},{8,10},{9,11},{10,... | collective-permute-start | bytes 1179656 | tf_op jit(solution)/shard_map/ppermute | solution.py:265
  47.2 6.8 %collective-permute-start.7 = (bf16[256,256]{1,0:T(8,128)(2,1)S(1)}, bf16[256,256]{1,0:T(8,128)(2,1)S(1)}, u32[]{:S(2)}, u32[]{:S(2)}) collective-permute-start(bf16[256,256]{1,0:T(8,128)(2,1)S(1)} %collective-permute-done.5.refs_2_), channel_id=1, source_target_pairs={{0,4},{1,5},{2,6},{3,7},{4,8},{5,9},{6,10},{7,11},{8,12},{9,13},{1... | collective-permute-start | bytes 393224 | tf_op jit(solution)/shard_map/ppermute | solution.py:265
  51.0 7.7 %collective-permute-start.23 = (bf16[256,256]{1,0:T(8,128)(2,1)S(1)}, bf16[256,256]{1,0:T(8,128)(2,1)S(1)}, u32[]{:S(2)}, u32[]{:S(2)}) collective-permute-start(bf16[256,256]{1,0:T(8,128)(2,1)S(1)} %collective-permute-done.21), channel_id=1, source_target_pairs={{0,4},{1,5},{2,6},{3,7},{4,8},{5,9},{6,10},{7,11},{8,12},{9,13},{1... | collective-permute-start | bytes 393224 | tf_op jit(solution)/shard_map/ppermute | solution.py:265
  54.0 7.8 %collective-permute-start.8 = (bf16[256,256]{1,0:T(8,128)(2,1)S(1)}, bf16[256,256]{1,0:T(8,128)(2,1)S(1)}, u32[]{:S(2)}, u32[]{:S(2)}) collective-permute-start(bf16[256,256]{1,0:T(8,128)(2,1)S(1)} %collective-permute-done.6.refs_3_), channel_id=1, source_target_pairs={{0,4},{1,5},{2,6},{3,7},{4,8},{5,9},{6,10},{7,11},{8,12},{9,13},{1... | collective-permute-start | bytes 393224 | tf_op jit(solution)/shard_map/ppermute | solution.py:265
  58.7 12.1 %collective-permute-start.9 = (bf16[256,256]{1,0:T(8,128)(2,1)S(1)}, bf16[256,256]{1,0:T(8,128)(2,1)S(1)}, u32[]{:S(2)}, u32[]{:S(2)}) collective-permute-start(bf16[256,256]{1,0:T(8,128)(2,1)S(1)} %collective-permute-done.7.refs_4_), channel_id=1, source_target_pairs={{0,4},{1,5},{2,6},{3,7},{4,8},{5,9},{6,10},{7,11},{8,12},{9,13},{1... | collective-permute-start | bytes 393224 | tf_op jit(solution)/shard_map/ppermute | solution.py:265
  61.8 6.8 %collective-permute-start.24 = (bf16[256,256]{1,0:T(8,128)(2,1)S(1)}, bf16[256,256]{1,0:T(8,128)(2,1)S(1)}, u32[]{:S(2)}, u32[]{:S(2)}) collective-permute-start(bf16[256,256]{1,0:T(8,128)(2,1)S(1)} %collective-permute-done.22), channel_id=1, source_target_pairs={{0,4},{1,5},{2,6},{3,7},{4,8},{5,9},{6,10},{7,11},{8,12},{9,13},{1... | collective-permute-start | bytes 393224 | tf_op jit(solution)/shard_map/ppermute | solution.py:265
  61.8 9.0 %collective-permute-start.10 = (bf16[256,256]{1,0:T(8,128)(2,1)S(1)}, bf16[256,256]{1,0:T(8,128)(2,1)S(1)}, u32[]{:S(2)}, u32[]{:S(2)}) collective-permute-start(bf16[256,256]{1,0:T(8,128)(2,1)S(1)} %collective-permute-done.8.refs_5_), channel_id=1, source_target_pairs={{0,4},{1,5},{2,6},{3,7},{4,8},{5,9},{6,10},{7,11},{8,12},{9,13},{1... | collective-permute-start | bytes 393224 | tf_op jit(solution)/shard_map/ppermute | solution.py:265
  63.9 6.9 %collective-permute-start.3 = (bf16[512,1024]{1,0:T(8,128)(2,1)S(1)}, bf16[512,1024]{1,0:T(8,128)(2,1)S(1)}, u32[]{:S(2)}, u32[]{:S(2)}) collective-permute-start(bf16[512,1024]{1,0:T(8,128)(2,1)S(1)} %pad_maximum_fusion.mine), channel_id=1, source_target_pairs={{0,1},{1,0},{2,3},{3,2},{4,5},{5,4},{6,7},{7,6},{8,9},{9,8},{10,11... | collective-permute-start | bytes 3145736 | tf_op jit(solution)/shard_map/ppermute | solution.py:265
  64.0 6.8 %copy-start.4 = (bf16[256,256]{1,0:T(8,128)(2,1)S(1)}, bf16[256,256]{1,0:T(8,128)(2,1)}, u32[]{:S(2)}) copy-start(bf16[256,256]{1,0:T(8,128)(2,1)} %copy-done.3) | copy-start | bytes 393220
  68.8 2.0 %copy-start.5 = (bf16[8,256,256]{2,1,0:T(8,128)(2,1)}, bf16[8,256,256]{2,1,0:T(8,128)(2,1)S(1)}, u32[]{:S(2)}) copy-start(bf16[8,256,256]{2,1,0:T(8,128)(2,1)S(1)} %dynamic-slice_dynamic-update-slice_fusion) | copy-start | bytes 3145732
  69.7 13.1 %copy-start = (bf16[16,256,256]{2,1,0:T(8,128)(2,1)S(1)}, bf16[16,256,256]{2,1,0:T(8,128)(2,1)}, u32[]{:S(2)}) copy-start(bf16[16,256,256]{2,1,0:T(8,128)(2,1)} %constant.120.clone.table) | copy-start | bytes 6291460
  69.7 28.4 %collective-permute-start.25 = (bf16[4,256,256]{2,1,0:T(8,128)(2,1)}, bf16[4,256,256]{2,1,0:T(8,128)(2,1)}, u32[]{:S(2)}, u32[]{:S(2)}) collective-permute-start(bf16[4,256,256]{2,1,0:T(8,128)(2,1)} %dynamic-slice_bitcast_fusion), channel_id=1, source_target_pairs={{0,1},{1,0},{2,3},{3,2},{4,5},{5,4},{6,7},{7,6},{8,9},{9,8},{10,11... | collective-permute-start | bytes 1572872 | tf_op jit(solution)/shard_map/ppermute | solution.py:265
  74.1 7.0 %collective-permute-start.11 = (bf16[256,128]{1,0:T(8,128)(2,1)}, bf16[256,128]{1,0:T(8,128)(2,1)S(1)}, u32[]{:S(2)}, u32[]{:S(2)}) collective-permute-start(bf16[256,128]{1,0:T(8,128)(2,1)} %get-tuple-element.19), channel_id=1, source_target_pairs={{0,4},{1,5},{2,6},{3,7},{4,8},{5,9},{6,10},{7,11},{8,12},{9,13},{1... | collective-permute-start | bytes 196616 | tf_op jit(solution)/shard_map/ppermute | solution.py:265
  74.1 8.7 %collective-permute-start.12 = (bf16[256,128]{1,0:T(8,128)(2,1)}, bf16[256,128]{1,0:T(8,128)(2,1)S(1)}, u32[]{:S(2)}, u32[]{:S(2)}) collective-permute-start(bf16[256,128]{1,0:T(8,128)(2,1)} %get-tuple-element.20), channel_id=1, source_target_pairs={{0,8},{1,9},{2,10},{3,11},{4,12},{5,13},{6,14},{7,15},{8,0},{9,1},... | collective-permute-start | bytes 196616 | tf_op jit(solution)/shard_map/ppermute | solution.py:265
  75.4 7.4 %collective-permute-start.13 = (bf16[256,128]{1,0:T(8,128)(2,1)}, bf16[256,128]{1,0:T(8,128)(2,1)S(1)}, u32[]{:S(2)}, u32[]{:S(2)}) collective-permute-start(bf16[256,128]{1,0:T(8,128)(2,1)} %get-tuple-element.21), channel_id=1, source_target_pairs={{0,12},{1,13},{2,14},{3,15},{4,0},{5,1},{6,2},{7,3},{8,4},{9,5},{1... | collective-permute-start | bytes 196616 | tf_op jit(solution)/shard_map/ppermute | solution.py:265
  82.8 1.6 %copy-start.1 = (bf16[16,256,256]{2,1,0:T(8,128)(2,1)S(1)}, bf16[16,256,256]{2,1,0:T(8,128)(2,1)}, u32[]{:S(2)}) copy-start(bf16[16,256,256]{2,1,0:T(8,128)(2,1)} %constant.121.clone.table_t) | copy-start | bytes 6291460
  87.5 6.7 %collective-permute-start.14 = (bf16[256,128]{1,0:T(8,128)(2,1)}, bf16[256,128]{1,0:T(8,128)(2,1)S(1)}, u32[]{:S(2)}, u32[]{:S(2)}) collective-permute-start(bf16[256,128]{1,0:T(8,128)(2,1)} %get-tuple-element.23), channel_id=1, source_target_pairs={{0,4},{1,5},{2,6},{3,7},{4,8},{5,9},{6,10},{7,11},{8,12},{9,13},{1... | collective-permute-start | bytes 196616 | tf_op jit(solution)/shard_map/ppermute | solution.py:265
  89.1 7.1 %collective-permute-start.15 = (bf16[256,128]{1,0:T(8,128)(2,1)}, bf16[256,128]{1,0:T(8,128)(2,1)S(1)}, u32[]{:S(2)}, u32[]{:S(2)}) collective-permute-start(bf16[256,128]{1,0:T(8,128)(2,1)} %get-tuple-element.24), channel_id=1, source_target_pairs={{0,8},{1,9},{2,10},{3,11},{4,12},{5,13},{6,14},{7,15},{8,0},{9,1},... | collective-permute-start | bytes 196616 | tf_op jit(solution)/shard_map/ppermute | solution.py:265
  90.3 5.9 %collective-permute-start.16 = (bf16[256,128]{1,0:T(8,128)(2,1)}, bf16[256,128]{1,0:T(8,128)(2,1)S(1)}, u32[]{:S(2)}, u32[]{:S(2)}) collective-permute-start(bf16[256,128]{1,0:T(8,128)(2,1)} %get-tuple-element.25), channel_id=1, source_target_pairs={{0,12},{1,13},{2,14},{3,15},{4,0},{5,1},{6,2},{7,3},{8,4},{9,5},{1... | collective-permute-start | bytes 196616 | tf_op jit(solution)/shard_map/ppermute | solution.py:265
  96.9 2.4 %collective-permute-start.17 = (bf16[512,256]{1,0:T(8,128)(2,1)S(1)}, bf16[512,256]{1,0:T(8,128)(2,1)S(1)}, u32[]{:S(2)}, u32[]{:S(2)}) collective-permute-start(bf16[512,256]{1,0:T(8,128)(2,1)S(1)} %shard_map.94.gated), channel_id=1, source_target_pairs={{0,1},{1,0},{2,3},{3,2},{4,5},{5,4},{6,7},{7,6},{8,9},{9,8},{10,11... | collective-permute-start | bytes 786440 | tf_op jit(solution)/shard_map/ppermute | solution.py:265
  101.3 9.2 %collective-permute-start.28 = (bf16[128,1024]{1,0:T(8,128)(2,1)S(1)}, bf16[128,1024]{1,0:T(8,128)(2,1)S(1)}, u32[]{:S(2)}, u32[]{:S(2)}) collective-permute-start(bf16[128,1024]{1,0:T(8,128)(2,1)S(1)} %get-tuple-element.30), channel_id=1, source_target_pairs={{0,2},{1,3},{2,0},{3,1},{4,6},{5,7},{6,4},{7,5},{8,10},{9,11},{10,... | collective-permute-start | bytes 786440 | tf_op jit(solution)/shard_map/ppermute | solution.py:265
  101.4 14.4 %collective-permute-start.27 = (bf16[128,1024]{1,0:T(8,128)(2,1)S(1)}, bf16[128,1024]{1,0:T(8,128)(2,1)S(1)}, u32[]{:S(2)}, u32[]{:S(2)}) collective-permute-start(bf16[128,1024]{1,0:T(8,128)(2,1)S(1)} %get-tuple-element.29), channel_id=1, source_target_pairs={{0,16},{1,17},{2,18},{3,19},{4,20},{5,21},{6,22},{7,23},{8,24},{9,... | collective-permute-start | bytes 786440 | tf_op jit(solution)/shard_map/ppermute | solution.py:265
  102.1 13.6 %collective-permute-start.26 = (bf16[128,1024]{1,0:T(8,128)(2,1)S(1)}, bf16[128,1024]{1,0:T(8,128)(2,1)S(1)}, u32[]{:S(2)}, u32[]{:S(2)}) collective-permute-start(bf16[128,1024]{1,0:T(8,128)(2,1)S(1)} %get-tuple-element.28), channel_id=1, source_target_pairs={{0,18},{1,19},{2,16},{3,17},{4,22},{5,23},{6,20},{7,21},{8,26},{9,... | collective-permute-start | bytes 786440 | tf_op jit(solution)/shard_map/ppermute | solution.py:265

commit v2 on v1

--- a/solution.py
+++ b/solution.py
@@ -56,51 +56,83 @@
     return pltpu.roll(values, 64, values.ndim - 1)
 
 
-def pack_filter(where, filt, out):
-    y = where[0]
+def both(first, second, low):
+    return (
+        jnp.where(low, first, half_turn(second)).astype(BF16),
+        jnp.where(low, half_turn(first), second).astype(BF16),
+    )
+
+
+def pack_weight(where, weight, own, away):
+    y, x = where[0], where[1]
+    own[...] = weight[:, pl.ds(pl.multiple_of(y * 512 + x * 256, 256), 256)]
+    away[...] = weight[:, pl.ds(pl.multiple_of(y * 512 + 256 - x * 256, 256), 256)]
+
+
+def pack_messages(where, tokens, key, query, after, m1, m2, m3, own):
+    y, x = where[0], where[1]
+    for p, out in enumerate((own, m1, m2, m3)):
+        row = 1 - y if p // 2 else y
+        column = 1 - x if p % 2 else x
+        lanes = pl.ds(pl.multiple_of(row * 512 + column * 256, 256), 256)
+        if p:
+            out[:, pl.ds(0, 1024)] = tokens[...]
+        base = 1024 if p else 0
+        out[:, pl.ds(base, 256)] = key[:, lanes]
+        out[:, pl.ds(base + 256, 256)] = query[:, lanes]
+
+
+def pack_filter(where, filt, after, own, away):
+    y, x, z = where[0], where[1], where[2]
     low = low_lanes((128, 128))
-    for x in range(2):
+    for k, out in enumerate((own, away)):
+        column = 1 - x if k else x
         for j in range(2):
-            base = pl.multiple_of(y * 512 + x * 256 + j * 128, 128)
+            base = pl.multiple_of(y * 512 + column * 256 + j * 128, 128)
             for part in range(2):
                 even = filt[part, 0, :, pl.ds(base, 128)].astype(F32)
                 odd = filt[part, 1, :, pl.ds(base, 128)].astype(F32)
-                out[2 * (2 * j) + x, part] = jnp.where(low, even, half_turn(odd)).astype(BF16)
-                out[2 * (2 * j + 1) + x, part] = jnp.where(low, half_turn(even), odd).astype(BF16)
-
-
-def value_kernel(where, mine, other, *refs):
-    pieces, gates = refs[:8], refs[8:12]
-    drive, outs = refs[12], refs[13:17]
-    acc, packed = refs[17], refs[18]
+                one, two = both(even, odd, low)
+                out[lax.rem(2 * j - z + 4, 4), part] = one
+                out[lax.rem(2 * j + 1 - z + 4, 4), part] = two
+
+
+def value_kernel(where, *refs):
+    mine, other, gates, pieces = refs[:4], refs[4:8], refs[8], refs[9:17]
+    drive, outs = refs[17], refs[18:22]
+    acc, packed = refs[22], refs[23]
     x, z, c = where[1], where[2], where[3]
     acc[...] = jnp.zeros_like(acc)
+
+    def gather(blocks, lanes):
+        return jnp.concatenate([b[:, lanes] for b in blocks], axis=0)
+
     for r in range(4):
         owner = lax.rem(z - r + 4, 4)
         for k in range(2):
-            row = jnp.where(k == 0, x, 1 - x)
-            off = pl.multiple_of(lax.rem(owner, 2) * 512 + row * 256, 256)
+            row = 1 - x if k else x
+            lanes = pl.ds(pl.multiple_of(lax.rem(owner, 2) * 512 + row * 256, 256), 256)
             piece = pieces[2 * r + k]
 
             @pl.when(owner // 2 == c)
             def _():
-                acc[...] += dot(mine[:, pl.ds(off, 256)], piece[...])
+                acc[...] += dot(gather(mine, lanes), piece[...])
 
             @pl.when(owner // 2 != c)
             def _():
-                acc[...] += dot(other[:, pl.ds(off, 256)], piece[...])
+                acc[...] += dot(gather(other, lanes), piece[...])
 
     for p in range(4):
         rows = pl.ds(p * 128, 128)
+        gate = mine[p][:, 1024:1280] if p else gates[:, 0:256]
         value = acc[rows, :].astype(BF16).astype(F32)
-        drive[rows, :] = (gates[p][...].astype(F32) * value).astype(BF16)
+        drive[rows, :] = (gate.astype(F32) * value).astype(BF16)
     low = low_lanes((256, 128))
     for j in range(2):
         lanes = pl.ds(j * 128, 128)
         first = drive[pl.ds(0, 256), lanes].astype(F32)
         second = drive[pl.ds(256, 256), lanes].astype(F32)
-        packed[2 * j] = jnp.where(low, first, half_turn(second)).astype(BF16)
-        packed[2 * j + 1] = jnp.where(low, half_turn(first), second).astype(BF16)
+        packed[2 * j], packed[2 * j + 1] = both(first, second, low)
     for r in range(4):
         outs[r][...] = packed[lax.rem(z + r, 4)]
 
@@ -151,10 +183,14 @@
     return [cadd(at(even, k), cmul(at(odd, k), -2 * math.pi * k / count)) for k in range(rows)]
 
 
-def conv_kernel(where, d0, d1, d2, d3, filt, table, table_t, o0, o1, o2, o3, data, first, sums):
+def conv_kernel(where, *refs):
+    drives, filters, (table, table_t) = refs[:4], refs[4:8], refs[8:10]
+    outs, (data, filt, first, sums) = refs[10:14], refs[14:]
     x, z = where[1], where[2]
-    for r, block in enumerate((d0, d1, d2, d3)):
+    for r, block in enumerate(drives):
         base = 2 * lax.rem(z - r + 4, 4)
+        filt[base + x] = filters[r][0]
+        filt[base + 1 - x] = filters[r][1]
         data[base + x] = block[pl.ds(0, 128), :]
         data[base + 1 - x] = block[pl.ds(128, 128), :]
     for i in range(8):
@@ -163,32 +199,34 @@
         spectrum = short_transform(values, 16, 9)
         for k in range(9):
             re, im = spectrum[k]
-            first[k, rows, :] = re.astype(BF16)
             if im is None:
                 im = jnp.zeros_like(re)
-            first[k, pl.ds(128 + 16 * i, 16), :] = im.astype(BF16)
+            first[k, rows, 0:128] = re.astype(BF16)
+            first[k, rows, 128:256] = im.astype(BF16)
             if 0 < k < 8:
-                first[16 - k, rows, :] = re.astype(BF16)
-                first[16 - k, pl.ds(128 + 16 * i, 16), :] = (-im).astype(BF16)
+                first[16 - k, rows, 0:128] = re.astype(BF16)
+                first[16 - k, rows, 128:256] = (-im).astype(BF16)
     low = low_lanes((128, 128))
 
     def back(k):
-        spectrum = dot(table[k], first[k])
-        re, im = spectrum[:128], spectrum[128:]
+        four = dot(table[k], first[k])
+        re = four[:128, :128] + four[128:, 128:]
+        im = four[:128, 128:] - four[128:, :128]
         pair = [filt[k // 2, part].astype(F32) for part in range(2)]
         if k % 2 == 0:
             fr, fi = [jnp.where(low, f, half_turn(f)) for f in pair]
         else:
             fr, fi = [jnp.where(low, half_turn(f), f) for f in pair]
-        product = jnp.concatenate([re * fr - im * fi, re * fi + im * fr], axis=0).astype(BF16)
-        return dot(table_t[k], product)
-
-    sums[0] = back(0)
-    sums[8] = back(8)
+        product = jnp.concatenate([re * fr - im * fi, re * fi + im * fr], axis=1).astype(BF16)
+        four = dot(table_t[k], product)
+        return four[:128, :128] - four[128:, 128:], four[128:, :128] + four[:128, 128:]
+
+    sums[0, pl.ds(0, 128)] = back(0)[0]
+    sums[8, pl.ds(0, 128)] = back(8)[0]
     for k in range(1, 8):
         one, two = back(k), back(16 - k)
-        sums[k, pl.ds(0, 128)] = one[:128] + two[:128]
-        sums[k, pl.ds(128, 128)] = one[128:] - two[128:]
+        sums[k, pl.ds(0, 128)] = one[0] + two[0]
+        sums[k, pl.ds(128, 128)] = one[1] - two[1]
     for i in range(16):
         rows, below = pl.ds(8 * i, 8), pl.ds(128 + 8 * i, 8)
         scale = 1.0 / 2048
@@ -204,13 +242,13 @@
             data[a, rows, :] = add(add(ec, oc), add(es, os)).astype(BF16)
             if 0 < a < 4:
                 data[8 - a, rows, :] = sub(sub(add(ec, os), oc), es).astype(BF16)
-    for r, out in enumerate((o0, o1, o2, o3)):
+    for r, out in enumerate(outs):
         base = 2 * lax.rem(z + r, 4)
         out[pl.ds(0, 128), :] = data[base + x]
         out[pl.ds(128, 128), :] = data[base + 1 - x]
 
 
-def gate_kernel(where, e0, e1, e2, e3, drive, skip, g0, g1, g2, g3, gated, conv):
+def gate_kernel(where, e0, e1, e2, e3, drive, skip, gates, g1, g2, g3, gated, conv):
     z = where[2]
     for r, block in enumerate((e0, e1, e2, e3)):
         conv[lax.rem(z - r + 4, 4)] = block[...]
@@ -219,20 +257,36 @@
         lanes = pl.ds(j * 128, 128)
         even, odd = conv[2 * j].astype(F32), conv[2 * j + 1].astype(F32)
         parts = (jnp.where(low, even, half_turn(odd)), jnp.where(low, half_turn(even), odd))
-        for p, gate in enumerate((g0, g1, g2, g3)):
+        for p, gate in enumerate((gates, g1, g2, g3)):
             rows = pl.ds(p * 128, 128)
             own = parts[p // 2][(p % 2) * 128 : (p % 2) * 128 + 128]
             direct = skip[:, lanes] * drive[rows, lanes].astype(F32)
-            gated[rows, lanes] = (gate[:, lanes].astype(F32) * (own + direct)).astype(BF16)
-
-
-def out_kernel(where, gated, other, *refs):
-    mine, theirs = refs[:4], refs[4:8]
-    own, sends = refs[8], refs[9:12]
+            query = gate[:, pl.ds((1280 if p else 256) + j * 128, 128)].astype(F32)
+            gated[rows, lanes] = (query * (own + direct)).astype(BF16)
+
+
+def sort_weight(where, *refs):
+    pieces, keep, give = refs[:4], refs[4], refs[5]
+    x, z, c = where[1], where[2], where[3]
+    for r in range(4):
+        owner = lax.rem(z - r + 4, 4)
+        for k in range(2):
+            to = 2 * lax.rem(owner, 2) + (1 - x if k else x)
+
+            @pl.when(owner // 2 == c)
+            def _():
+                keep[to] = pieces[r][k]
+
+            @pl.when(owner // 2 != c)
+            def _():
+                give[to] = pieces[r][k]
+
+
+def out_kernel(gated, other, keep, theirs, own, *sends):
     for p in (3, 2, 1, 0):
         rows = pl.ds(p * 128, 128)
         for i in range(4):
-            total = dot_t(gated[rows, :], mine[i][...]) + dot_t(other[rows, :], theirs[i][...])
+            total = dot_t(gated[rows, :], keep[i]) + dot_t(other[rows, :], theirs[i])
             lanes = pl.ds(i * 256, 256)
             if p == 0:
                 own[:, lanes] = total
@@ -244,9 +298,8 @@
     k = np.arange(16)[:, None, None] + 16 * np.arange(128)[None, :, None]
     phase = 2 * np.pi / 2048 * (k * np.arange(128)[None, None, :] % 2048)
     co, si = np.cos(phase), np.sin(phase)
-    table = np.concatenate([np.concatenate([co, si], 2), np.concatenate([-si, co], 2)], 1)
-    table = table.astype(jnp.bfloat16)
-    return table, np.ascontiguousarray(table.transpose(0, 2, 1))
+    back = np.concatenate([co.transpose(0, 2, 1), si.transpose(0, 2, 1)], 1)
+    return np.concatenate([co, si], 1).astype(jnp.bfloat16), back.astype(jnp.bfloat16)
 
 
 def planes(tokens, gate_q, gate_k, w_value, skip, filter_spectrum, w_out):
@@ -276,36 +329,41 @@
     def to_peer(values, p):
         return permute(values, lambda g, z, x, k: (g ^ (p // 2), z, x ^ (p % 2), k))
 
-    def quarter(values, p=0):
-        q = (y ^ (p // 2)) * 2 + (x ^ (p % 2))
-        return lax.dynamic_slice_in_dim(values, q * 256, 256, axis=values.ndim - 1)
-
-    def around(weight):
-        pieces = [quarter(weight), to_x(quarter(weight, 1))]
-        for _ in range(3):
-            pieces += [to_z(pieces[-2], 1), to_z(pieces[-1], 1)]
-        return pieces
-
-    value_pieces = around(w_value)
-    received = [
-        to_peer(jnp.concatenate([tokens, quarter(gate_k, p), quarter(gate_q, p)], axis=1), p)
-        for p in (1, 2, 3)
-    ]
-    keys = [quarter(gate_k)] + [m[:, 1024:1280] for m in received]
-    queries = [quarter(gate_q)] + [m[:, 1280:] for m in received]
-    mine = jnp.concatenate([tokens] + [m[:, :1024] for m in received], axis=0)
-    other = to_core(mine)
+    def after(values, *done):
+        return lax.optimization_barrier((values,) + done)[0]
+
     shape = jax.ShapeDtypeStruct
-    packed = in_vmem(pack_filter, shape((8, 2, 128, 128), BF16), moved=1 << 20)(where, filter_spectrum)
-    filters = lax.all_to_all(packed, "seq", split_axis=0, concat_axis=0, tiled=True)
-    block = shape((256, 128), BF16)
+    block, square = shape((256, 128), BF16), shape((256, 256), BF16)
+    message = shape((128, 1536), BF16)
+    split = in_vmem(pack_weight, [square] * 2, moved=1 << 20)
+    own_first, away = split(where, w_value)
+    ring = [own_first, to_x(away)]
+    *messages, gates = in_vmem(
+        pack_messages, [message] * 3 + [shape((128, 512), BF16)], moved=2 << 20
+    )(where, tokens, gate_k, gate_q, own_first[:16, :128])
+    received = [to_peer(messages[p - 1], p) for p in (1, 2, 3)]
+    by_plane = shape((4, 2, 128, 128), BF16)
+    packed, away = in_vmem(pack_filter, [by_plane] * 2, moved=1 << 20)(
+        where, filter_spectrum, messages[0][:16, :128]
+    )
+    got = to_x(away)
+    filters = [jnp.stack([packed[r], got[r]]) for r in range(4)]
+    filters = filters[:1] + [to_z(filters[r], r) for r in (1, 2, 3)]
+    mine = [tokens] + received
+    other = [to_core(m) for m in mine]
+    ring += [to_z(ring[0], 1), to_z(ring[1], 1)]
+    ring += [to_z(ring[2], 1), to_z(ring[3], 1)]
+    ring += [to_z(after(ring[4], *received), 1), to_z(ring[5], 1)]
+    own_out, away = split(where, after(w_out, messages[0]))
+    pair = jnp.stack([own_out, to_x(after(away, got))])
+    gates = after(gates, *filters)
     drive, *sends = in_vmem(
         value_kernel,
         [shape((512, 256), BF16)] + [block] * 4,
         [pltpu.VMEM((512, 256), F32), pltpu.VMEM((4, 256, 128), BF16)],
         flops=1 << 29,
         moved=4 << 20,
-    )(where, mine, other, *value_pieces, *keys)
+    )(where, *mine, *other, gates, *ring)
     columns = [sends[0]] + [to_z(sends[r], r) for r in (1, 2, 3)]
     table, table_t = tables()
     sends = in_vmem(
@@ -313,41 +371,37 @@
         [block] * 4,
         [
             pltpu.VMEM((8, 128, 128), BF16),
-            pltpu.VMEM((16, 256, 128), BF16),
+            pltpu.VMEM((8, 2, 128, 128), BF16),
+            pltpu.VMEM((16, 128, 256), BF16),
             pltpu.VMEM((9, 256, 128), F32),
         ],
         flops=1 << 30,
         moved=5 << 20,
-    )(where, *columns, filters, table, table_t)
+    )(where, *columns, *filters, table, table_t)
     rows = [sends[0]] + [to_z(sends[r], r) for r in (1, 2, 3)]
 
-    out_pieces = around(w_out)
-    order = []
-    for i in range(deep):
-        r = (z - i) % deep
-        for k in range(2):
-            which = (x + k) % 2
-            order.append(2 * r + which)
-    stacked = jnp.stack(out_pieces)
-    ordered = [lax.dynamic_index_in_dim(stacked, o, 0, keepdims=False) for o in order]
-    halves = jnp.stack(ordered).reshape(2, 4, 256, 256)
-    keep = lax.dynamic_index_in_dim(halves, c, 0, keepdims=False)
-    give = lax.dynamic_index_in_dim(halves, 1 - c, 0, keepdims=False)
+    hops = [after(pair, ring[6], ring[7])]
+    hops.append(to_z(hops[0], 1))
+    hops.append(to_z(after(hops[1], drive), 1))
+    hops.append(to_z(after(hops[2], sends[0]), 1))
+    quad = shape((4, 256, 256), BF16)
+    keep, give = in_vmem(sort_weight, [quad] * 2, moved=2 << 20)(where, *hops)
     theirs = to_core(give)
+    channels = lax.dynamic_slice_in_dim(skip, (y * 2 + x) * 256, 256)[None, :]
     gated = in_vmem(
         gate_kernel, shape((512, 256), BF16), [pltpu.VMEM((4, 256, 128), BF16)], moved=1 << 20
-    )(where, *rows, drive, quarter(skip)[None, :], *queries)
+    )(where, *rows, drive, channels, gates, *received)
     gated_other = to_core(gated)
     own, *sends = in_vmem(
         out_kernel,
         [shape((128, 1024), F32)] + [shape((128, 1024), BF16)] * 3,
+        smem=0,
         flops=1 << 30,
         moved=4 << 20,
-    )(where, gated, gated_other, *[keep[i] for i in range(4)], *[theirs[i] for i in range(4)])
-    parts = [to_peer(sends[p - 1], p) for p in (3, 2, 1)]
+    )(gated, gated_other, keep, theirs)
     total = own
-    for part in parts:
-        total = total + part.astype(F32)
+    for p in (3, 2, 1):
+        total = total + to_peer(sends[p - 1], p).astype(F32)
     return total.astype(BF16)
 
 

time: 117 us -> 112 us (0.957)
  starting transfers between devices: 28.8 us -> 39.3 us
  local copies, waits for them, and re-layouts: 14.3 us -> 4.79 us
  waiting for transfers between devices: 60.2 us -> 54.8 us
    ppermute x29 -> x33, starting transfers between devices: 24.9 us -> 39.3 us  [permute(): return lax.ppermute(values, AXES, pairs)]
    ppermute x29 -> x33, waiting for transfers between devices: 60.2 us -> 54.8 us  [permute(): return lax.ppermute(values, AXES, pairs)]
    slice x6 -> x4, local copies, waits for them, and re-layouts: 3.92 us -> 0.04 us  [the longest x2 0.04 us: planes(): filters = [jnp.stack([packed[r], got[r]]) for r in range(4)]]
    all_to_all x1 -> x0, starting transfers between devices: 3.87 us -> none  [planes(): lax.all_to_all(packed, 'seq', split_axis=0, concat_axis=0, tiled=True)]
    dynamic_slice x5 -> x1, local copies, waits for them, and re-layouts: 4.4 us -> 0.76 us  [planes(): channels = lax.dynamic_slice_in_dim(skip, (y * 2 + x) * 256, 256)[None, :]]
    squeeze x3 -> x0, local copies, waits for them, and re-layouts: 3.19 us -> none  [the longest x1 1.14 us: planes(): keep[i]]
    unnamed x30 -> x18, local copies, waits for them, and re-layouts: 2.73 us -> 3.99 us
    pallas_call x5 -> x9, Pallas kernels: 10.8 us -> 11.2 us  [call(): pl.pallas_call(kernel, out_shape=out_shape, in_specs=specs, out_specs=jax...]
  transfers between devices with their start and end apart: 30 -> 33, of which waited for: 16 -> 17; matrix products, arithmetic and copies ran while one was open for 9% -> 1% of each run, Pallas kernels for 8% -> 8%
where the time goes in v2:
time: 112 us; the launch traced here: 111 us
  waiting for transfers between devices  54.8 us (49%)
  starting transfers between devices  39.3 us (35%)
  Pallas kernels  11.2 us (10%)
  local copies, waits for them, and re-layouts  4.79 us (4%)
    ppermute x33, waiting for transfers between devices, permute(): return lax.ppermute(values, AXES, pairs)  54.8 us
    ppermute x33, starting transfers between devices, permute(): return lax.ppermute(values, AXES, pairs)  39.3 us
    pallas_call x9, Pallas kernels, call(): pl.pallas_call(kernel, out_shape=out_shape, in_specs=specs, out_specs=jax...  11.2 us
    unnamed x18, local copies, waits for them, and re-layouts  3.99 us
  transfers between devices with their start and end apart: 33, of which 17 were waited for; matrix products, arithmetic and copies ran while one was open for 1% of the time, Pallas kernels for 8%

profile of v2, /device:TPU:0, one launch (start us, length us, event | category | flops | bytes accessed | tf_op | source)
XLA Modules:
  0.0 111.4 jit_solution(13650179835093580617)
XLA Ops:
  0.0 0.1 pad_add_fusion.where
  0.1 1.1 %copy-done.3 = bf16[256,1024]{1,0:T(8,128)(2,1)S(1)} copy-done((bf16[256,1024]{1,0:T(8,128)(2,1)S(1)}, bf16[256,1024]{1,0:T(8,128)(2,1)}, u32[]{:S(2)}) %copy-start.3) | copy-done | bytes 524312
  1.2 0.6 shard_map.91
  1.8 3.0 %collective-permute-start.11 = (bf16[256,256]{1,0:T(8,128)(2,1)S(1)}, bf16[256,256]{1,0:T(8,128)(2,1)S(1)}, u32[]{:S(2)}, u32[]{:S(2)}) collective-permute-start(bf16[256,256]{1,0:T(8,128)(2,1)S(1)} %get-tuple-element.45), channel_id=1, source_target_pairs={{0,2},{1,3},{2,0},{3,1},{4,6},{5,7},{6,4},{7,5},{8,10},{9,11},{10,... | collective-permute-start | bytes 393224 | tf_op jit(solution)/shard_map/ppermute | solution.py:318
  4.8 0.9 copy-done.1
  5.7 0.9 copy-done.5
  6.7 0.9 copy-done.6
  7.6 0.6 shard_map.92
  8.3 0.0 copy-start.4
  8.3 0.8 shard_map.93
  9.1 0.1 collective-permute-start.7
  9.2 2.1 %collective-permute-start.12 = (bf16[256,256]{1,0:T(8,128)(2,1)S(1)}, bf16[256,256]{1,0:T(8,128)(2,1)S(1)}, u32[]{:S(2)}, u32[]{:S(2)}) collective-permute-start(bf16[256,256]{1,0:T(8,128)(2,1)S(1)} %get-tuple-element.37.refs_9_), channel_id=1, source_target_pairs={{0,4},{1,5},{2,6},{3,7},{4,8},{5,9},{6,10},{7,11},{8,12},{9,13},{1... | collective-permute-start | bytes 393224 | tf_op jit(solution)/shard_map/ppermute | solution.py:318
  11.3 1.5 %collective-permute-start = (bf16[128,1536]{1,0:T(8,128)(2,1)S(1)}, bf16[128,1536]{1,0:T(8,128)(2,1)S(1)}, u32[]{:S(2)}, u32[]{:S(2)}) collective-permute-start(bf16[128,1536]{1,0:T(8,128)(2,1)S(1)} %get-tuple-element.38), channel_id=1, source_target_pairs={{0,2},{1,3},{2,0},{3,1},{4,6},{5,7},{6,4},{7,5},{8,10},{9,11},{10,... | collective-permute-start | bytes 1179656 | tf_op jit(solution)/shard_map/ppermute | solution.py:318
  12.8 1.5 %collective-permute-start.1 = (bf16[128,1536]{1,0:T(8,128)(2,1)S(1)}, bf16[128,1536]{1,0:T(8,128)(2,1)S(1)}, u32[]{:S(2)}, u32[]{:S(2)}) collective-permute-start(bf16[128,1536]{1,0:T(8,128)(2,1)S(1)} %get-tuple-element.39), channel_id=1, source_target_pairs={{0,16},{1,17},{2,18},{3,19},{4,20},{5,21},{6,22},{7,23},{8,24},{9,... | collective-permute-start | bytes 1179656 | tf_op jit(solution)/shard_map/ppermute | solution.py:318
  14.3 0.6 shard_map.97
  14.9 0.0 collective-permute-done.11.refs_10_
  14.9 1.6 %collective-permute-start.13 = (bf16[256,256]{1,0:T(8,128)(2,1)S(1)}, bf16[256,256]{1,0:T(8,128)(2,1)S(1)}, u32[]{:S(2)}, u32[]{:S(2)}) collective-permute-start(bf16[256,256]{1,0:T(8,128)(2,1)S(1)} %collective-permute-done.11.refs_10_), channel_id=1, source_target_pairs={{0,4},{1,5},{2,6},{3,7},{4,8},{5,9},{6,10},{7,11},{8,12},{9,13},{1... | collective-permute-start | bytes 393224 | tf_op jit(solution)/shard_map/ppermute | solution.py:318
  16.6 3.1 %collective-permute-start.2 = (bf16[128,1536]{1,0:T(8,128)(2,1)S(1)}, bf16[128,1536]{1,0:T(8,128)(2,1)S(1)}, u32[]{:S(2)}, u32[]{:S(2)}) collective-permute-start(bf16[128,1536]{1,0:T(8,128)(2,1)S(1)} %get-tuple-element.40), channel_id=1, source_target_pairs={{0,18},{1,19},{2,16},{3,17},{4,22},{5,23},{6,20},{7,21},{8,26},{9,... | collective-permute-start | bytes 1179656 | tf_op jit(solution)/shard_map/ppermute | solution.py:318
  19.6 2.1 %collective-permute-done.13.refs_12_ = bf16[256,256]{1,0:T(8,128)(2,1)S(1)} collective-permute-done((bf16[256,256]{1,0:T(8,128)(2,1)S(1)}, bf16[256,256]{1,0:T(8,128)(2,1)S(1)}, u32[]{:S(2)}, u32[]{:S(2)}) %collective-permute-start.13) | collective-permute-done | bytes 131104 | tf_op jit(solution)/shard_map/ppermute | solution.py:318
  21.7 1.4 %collective-permute-start.15 = (bf16[256,256]{1,0:T(8,128)(2,1)S(1)}, bf16[256,256]{1,0:T(8,128)(2,1)S(1)}, u32[]{:S(2)}, u32[]{:S(2)}) collective-permute-start(bf16[256,256]{1,0:T(8,128)(2,1)S(1)} %collective-permute-done.13.refs_12_), channel_id=1, source_target_pairs={{0,4},{1,5},{2,6},{3,7},{4,8},{5,9},{6,10},{7,11},{8,12},{9,13},{1... | collective-permute-start | bytes 393224 | tf_op jit(solution)/shard_map/ppermute | solution.py:318
  23.1 0.0 copy-start.2
  23.2 5.3 %collective-permute-done.14.refs_13_ = bf16[256,256]{1,0:T(8,128)(2,1)S(1)} collective-permute-done((bf16[256,256]{1,0:T(8,128)(2,1)S(1)}, bf16[256,256]{1,0:T(8,128)(2,1)S(1)}, u32[]{:S(2)}, u32[]{:S(2)}) %collective-permute-start.14) | collective-permute-done | bytes 131104 | tf_op jit(solution)/shard_map/ppermute | solution.py:318
  28.5 0.5 collective-permute-start.25
  29.0 0.9 collective-permute-done.15.refs_14_
  29.9 0.0 collective-permute-start.8
  29.9 1.5 %collective-permute-start.9 = (bf16[2,2,128,128]{3,2,1,0:T(8,128)(2,1)S(1)}, bf16[2,2,128,128]{3,2,1,0:T(8,128)(2,1)S(1)}, u32[]{:S(2)}, u32[]{:S(2)}) collective-permute-start(bf16[2,2,128,128]{3,2,1,0:T(8,128)(2,1)S(1)} %pad_maximum_fusion.3), channel_id=1, source_target_pairs={{0,8},{1,9},{2,10},{3,11},{4,12},{5,13},{6,14},{7,15},{8,0},{9,1},... | collective-permute-start | bytes 393224 | tf_op jit(solution)/shard_map/ppermute | solution.py:318
  31.5 4.7 %collective-permute-done.2.refs_3_.g3 = bf16[128,1536]{1,0:T(8,128)(2,1)S(1)} collective-permute-done((bf16[128,1536]{1,0:T(8,128)(2,1)S(1)}, bf16[128,1536]{1,0:T(8,128)(2,1)S(1)}, u32[]{:S(2)}, u32[]{:S(2)}) %collective-permute-start.2) | collective-permute-done | bytes 393248 | tf_op jit(solution)/shard_map/ppermute | solution.py:318
  36.2 1.6 %collective-permute-start.17 = (bf16[256,256]{1,0:T(8,128)(2,1)S(1)}, bf16[256,256]{1,0:T(8,128)(2,1)S(1)}, u32[]{:S(2)}, u32[]{:S(2)}) collective-permute-start(bf16[256,256]{1,0:T(8,128)(2,1)S(1)} %collective-permute-done.15.refs_14_), channel_id=1, source_target_pairs={{0,4},{1,5},{2,6},{3,7},{4,8},{5,9},{6,10},{7,11},{8,12},{9,13},{1... | collective-permute-start | bytes 393224 | tf_op jit(solution)/shard_map/ppermute | solution.py:318
  37.7 1.6 %collective-permute-start.16 = (bf16[256,256]{1,0:T(8,128)(2,1)S(1)}, bf16[256,256]{1,0:T(8,128)(2,1)S(1)}, u32[]{:S(2)}, u32[]{:S(2)}) collective-permute-start(bf16[256,256]{1,0:T(8,128)(2,1)S(1)} %collective-permute-done.14.refs_13_), channel_id=1, source_target_pairs={{0,4},{1,5},{2,6},{3,7},{4,8},{5,9},{6,10},{7,11},{8,12},{9,13},{1... | collective-permute-start | bytes 393224 | tf_op jit(solution)/shard_map/ppermute | solution.py:318
  39.3 0.5 collective-permute-start.6
  39.8 1.6 %collective-permute-done.9.refs_6_ = bf16[2,2,128,128]{3,2,1,0:T(8,128)(2,1)S(1)} collective-permute-done((bf16[2,2,128,128]{3,2,1,0:T(8,128)(2,1)S(1)}, bf16[2,2,128,128]{3,2,1,0:T(8,128)(2,1)S(1)}, u32[]{:S(2)}, u32[]{:S(2)}) %collective-permute-start.9) | collective-permute-done | bytes 131104 | tf_op jit(solution)/shard_map/ppermute | solution.py:318
  41.4 1.5 %collective-permute-done.17.refs_16_ = bf16[256,256]{1,0:T(8,128)(2,1)S(1)} collective-permute-done((bf16[256,256]{1,0:T(8,128)(2,1)S(1)}, bf16[256,256]{1,0:T(8,128)(2,1)S(1)}, u32[]{:S(2)}, u32[]{:S(2)}) %collective-permute-start.17) | collective-permute-done | bytes 131104 | tf_op jit(solution)/shard_map/ppermute | solution.py:318
  42.9 1.8 %collective-permute-start.10 = (bf16[2,2,128,128]{3,2,1,0:T(8,128)(2,1)S(1)}, bf16[2,2,128,128]{3,2,1,0:T(8,128)(2,1)S(1)}, u32[]{:S(2)}, u32[]{:S(2)}) collective-permute-start(bf16[2,2,128,128]{3,2,1,0:T(8,128)(2,1)S(1)} %pad_maximum_fusion.4), channel_id=1, source_target_pairs={{0,12},{1,13},{2,14},{3,15},{4,0},{5,1},{6,2},{7,3},{8,4},{9,5},{1... | collective-permute-start | bytes 393224 | tf_op jit(solution)/shard_map/ppermute | solution.py:318
  44.7 0.6 collective-permute-done.16.refs_15_
  45.4 2.5 %collective-permute-done.10.refs_7_ = bf16[2,2,128,128]{3,2,1,0:T(8,128)(2,1)S(1)} collective-permute-done((bf16[2,2,128,128]{3,2,1,0:T(8,128)(2,1)S(1)}, bf16[2,2,128,128]{3,2,1,0:T(8,128)(2,1)S(1)}, u32[]{:S(2)}, u32[]{:S(2)}) %collective-permute-start.10) | collective-permute-done | bytes 131104 | tf_op jit(solution)/shard_map/ppermute | solution.py:318
  47.9 0.2 collective-permute-start.26
  48.1 0.0 copy-start.7
  48.1 0.0 copy-start.8
  48.2 2.7 %shard_map.94 = (bf16[512,256]{1,0:T(8,128)(2,1)S(1)}, bf16[256,128]{1,0:T(8,128)(2,1)S(1)}, bf16[256,128]{1,0:T(8,128)(2,1)S(1)}, bf16[256,128]{1,0:T(8,128)(2,1)S(1)}, bf16[256,128]{1,0:T(8,128)(2,1)S(1)}) custom-call(s32[4]{0:T(128)S(1)} %pad_add_fusion.where, bf16[128,1024]{1,0:T(8,128)(2,1)S(1)} %copy-done.2, ...), custom_call_target="tpu_custom_call" | custom-call | flops 536870912 | bytes 4194304 | tf_op jit(solution)/shard_map/pallas_call | solution.py:38
  50.8 5.4 %collective-permute-done.26.refs_1_ = bf16[2,256,256]{2,1,0:T(8,128)(2,1)S(1)} collective-permute-done((bf16[2,256,256]{2,1,0:T(8,128)(2,1)S(1)}, bf16[2,256,256]{2,1,0:T(8,128)(2,1)S(1)}, u32[]{:S(2)}, u32[]{:S(2)}) %collective-permute-start.26) | collective-permute-done | bytes 262176 | tf_op jit(solution)/shard_map/ppermute | solution.py:318
  56.2 1.5 %collective-permute-start.18 = (bf16[256,128]{1,0:T(8,128)(2,1)S(1)}, bf16[256,128]{1,0:T(8,128)(2,1)S(1)}, u32[]{:S(2)}, u32[]{:S(2)}) collective-permute-start(bf16[256,128]{1,0:T(8,128)(2,1)S(1)} %get-tuple-element.48), channel_id=1, source_target_pairs={{0,4},{1,5},{2,6},{3,7},{4,8},{5,9},{6,10},{7,11},{8,12},{9,13},{1... | collective-permute-start | bytes 196616 | tf_op jit(solution)/shard_map/ppermute | solution.py:318
  57.7 2.9 %collective-permute-start.19 = (bf16[256,128]{1,0:T(8,128)(2,1)S(1)}, bf16[256,128]{1,0:T(8,128)(2,1)S(1)}, u32[]{:S(2)}, u32[]{:S(2)}) collective-permute-start(bf16[256,128]{1,0:T(8,128)(2,1)S(1)} %get-tuple-element.49), channel_id=1, source_target_pairs={{0,8},{1,9},{2,10},{3,11},{4,12},{5,13},{6,14},{7,15},{8,0},{9,1},... | collective-permute-start | bytes 196616 | tf_op jit(solution)/shard_map/ppermute | solution.py:318
  60.6 1.9 %collective-permute-start.20 = (bf16[256,128]{1,0:T(8,128)(2,1)S(1)}, bf16[256,128]{1,0:T(8,128)(2,1)S(1)}, u32[]{:S(2)}, u32[]{:S(2)}) collective-permute-start(bf16[256,128]{1,0:T(8,128)(2,1)S(1)} %get-tuple-element.50), channel_id=1, source_target_pairs={{0,12},{1,13},{2,14},{3,15},{4,0},{5,1},{6,2},{7,3},{8,4},{9,5},{1... | collective-permute-start | bytes 196616 | tf_op jit(solution)/shard_map/ppermute | solution.py:318
  62.5 4.0 %collective-permute-done.18.refs_1_ = bf16[256,128]{1,0:T(8,128)(2,1)S(1)} collective-permute-done((bf16[256,128]{1,0:T(8,128)(2,1)S(1)}, bf16[256,128]{1,0:T(8,128)(2,1)S(1)}, u32[]{:S(2)}, u32[]{:S(2)}) %collective-permute-start.18) | collective-permute-done | bytes 65568 | tf_op jit(solution)/shard_map/ppermute | solution.py:318
  66.6 1.4 %collective-permute-done.19.refs_2_ = bf16[256,128]{1,0:T(8,128)(2,1)S(1)} collective-permute-done((bf16[256,128]{1,0:T(8,128)(2,1)S(1)}, bf16[256,128]{1,0:T(8,128)(2,1)S(1)}, u32[]{:S(2)}, u32[]{:S(2)}) %collective-permute-start.19) | collective-permute-done | bytes 65568 | tf_op jit(solution)/shard_map/ppermute | solution.py:318
  68.0 3.0 %shard_map.95 = (bf16[256,128]{1,0:T(8,128)(2,1)S(1)}, bf16[256,128]{1,0:T(8,128)(2,1)}, bf16[256,128]{1,0:T(8,128)(2,1)S(1)}, bf16[256,128]{1,0:T(8,128)(2,1)S(1)}) custom-call(s32[4]{0:T(128)S(1)} %pad_add_fusion.where, bf16[256,128]{1,0:T(8,128)(2,1)S(1)} %get-tuple-element.47.refs_0_, bf16[256,128]{1,0:T(8,128)(2,1)S(1)} %collective-permute-done.18.refs_1_, ...), custom_call_target="tpu_custom_call" | custom-call | flops 1073741824 | bytes 5242880 | tf_op jit(solution)/shard_map/pallas_call | solution.py:38
  71.0 1.9 %collective-permute-start.28 = (bf16[2,256,256]{2,1,0:T(8,128)(2,1)S(1)}, bf16[2,256,256]{2,1,0:T(8,128)(2,1)S(1)}, u32[]{:S(2)}, u32[]{:S(2)}) collective-permute-start(bf16[2,256,256]{2,1,0:T(8,128)(2,1)S(1)} %collective-permute-done.27.refs_2_), channel_id=1, source_target_pairs={{0,4},{1,5},{2,6},{3,7},{4,8},{5,9},{6,10},{7,11},{8,12},{9,13},{1... | collective-permute-start | bytes 786440 | tf_op jit(solution)/shard_map/ppermute | solution.py:318
  72.9 8.1 %collective-permute-done.28.refs_3_ = bf16[2,256,256]{2,1,0:T(8,128)(2,1)S(1)} collective-permute-done((bf16[2,256,256]{2,1,0:T(8,128)(2,1)S(1)}, bf16[2,256,256]{2,1,0:T(8,128)(2,1)S(1)}, u32[]{:S(2)}, u32[]{:S(2)}) %collective-permute-start.28) | collective-permute-done | bytes 262176 | tf_op jit(solution)/shard_map/ppermute | solution.py:318
  81.0 0.7 shard_map.98
  81.7 0.1 collective-permute-start.29
  81.8 0.2 collective-permute-start.21
  82.0 3.7 %collective-permute-start.23 = (bf16[256,128]{1,0:T(8,128)(2,1)S(1)}, bf16[256,128]{1,0:T(8,128)(2,1)S(1)}, u32[]{:S(2)}, u32[]{:S(2)}) collective-permute-start(bf16[256,128]{1,0:T(8,128)(2,1)S(1)} %get-tuple-element.54), channel_id=1, source_target_pairs={{0,12},{1,13},{2,14},{3,15},{4,0},{5,1},{6,2},{7,3},{8,4},{9,5},{1... | collective-permute-start | bytes 196616 | tf_op jit(solution)/shard_map/ppermute | solution.py:318
  85.6 0.8 dynamic_slice.3
  86.4 2.4 %collective-permute-done.21.e1 = bf16[256,128]{1,0:T(8,128)(2,1)S(1)} collective-permute-done((bf16[256,128]{1,0:T(8,128)(2,1)}, bf16[256,128]{1,0:T(8,128)(2,1)S(1)}, u32[]{:S(2)}, u32[]{:S(2)}) %collective-permute-start.21) | collective-permute-done | bytes 65568 | tf_op jit(solution)/shard_map/ppermute | solution.py:318
  88.8 1.2 %collective-permute-done.22.e2 = bf16[256,128]{1,0:T(8,128)(2,1)S(1)} collective-permute-done((bf16[256,128]{1,0:T(8,128)(2,1)S(1)}, bf16[256,128]{1,0:T(8,128)(2,1)S(1)}, u32[]{:S(2)}, u32[]{:S(2)}) %collective-permute-start.22) | collective-permute-done | bytes 65568 | tf_op jit(solution)/shard_map/ppermute | solution.py:318
  90.0 0.8 shard_map.96.gated
  90.8 0.1 collective-permute-start.24
  90.9 1.5 %collective-permute-done.24.other = bf16[512,256]{1,0:T(8,128)(2,1)S(1)} collective-permute-done((bf16[512,256]{1,0:T(8,128)(2,1)S(1)}, bf16[512,256]{1,0:T(8,128)(2,1)S(1)}, u32[]{:S(2)}, u32[]{:S(2)}) %collective-permute-start.24) | collective-permute-done | bytes 262176 | tf_op jit(solution)/shard_map/ppermute | solution.py:318
  92.4 1.5 %shard_map.99 = (f32[128,1024]{1,0:T(8,128)S(1)}, bf16[128,1024]{1,0:T(8,128)(2,1)S(1)}, bf16[128,1024]{1,0:T(8,128)(2,1)S(1)}, bf16[128,1024]{1,0:T(8,128)(2,1)S(1)}) custom-call(bf16[512,256]{1,0:T(8,128)(2,1)S(1)} %shard_map.96.gated, bf16[512,256]{1,0:T(8,128)(2,1)S(1)} %collective-permute-done.24.other, ...), custom_call_target="tpu_custom_call" | custom-call | flops 1073741824 | bytes 4194304 | tf_op jit(solution)/shard_map/pallas_call | solution.py:38
  93.9 4.4 %collective-permute-start.30 = (bf16[128,1024]{1,0:T(8,128)(2,1)S(1)}, bf16[128,1024]{1,0:T(8,128)(2,1)S(1)}, u32[]{:S(2)}, u32[]{:S(2)}) collective-permute-start(bf16[128,1024]{1,0:T(8,128)(2,1)S(1)} %get-tuple-element.66), channel_id=1, source_target_pairs={{0,18},{1,19},{2,16},{3,17},{4,22},{5,23},{6,20},{7,21},{8,26},{9,... | collective-permute-start | bytes 786440 | tf_op jit(solution)/shard_map/ppermute | solution.py:318
  98.3 0.6 collective-permute-start.32
  99.0 6.5 %collective-permute-done.30 = bf16[128,1024]{1,0:T(8,128)(2,1)S(1)} collective-permute-done((bf16[128,1024]{1,0:T(8,128)(2,1)S(1)}, bf16[128,1024]{1,0:T(8,128)(2,1)S(1)}, u32[]{:S(2)}, u32[]{:S(2)}) %collective-permute-start.30) | collective-permute-done | bytes 262176 | tf_op jit(solution)/shard_map/ppermute | solution.py:318
  105.4 5.1 %collective-permute-done.31 = bf16[128,1024]{1,0:T(8,128)(2,1)S(1)} collective-permute-done((bf16[128,1024]{1,0:T(8,128)(2,1)S(1)}, bf16[128,1024]{1,0:T(8,128)(2,1)S(1)}, u32[]{:S(2)}, u32[]{:S(2)}) %collective-permute-start.31) | collective-permute-done | bytes 262176 | tf_op jit(solution)/shard_map/ppermute | solution.py:318
  110.5 0.8 add_convert_fusion
  (41 shorter events, 0.2 us)
Async XLA Ops:
  0.0 8.3 %copy-start = (bf16[2,2,128,1024]{3,2,1,0:T(8,128)(2,1)S(1)}, bf16[2,2,128,1024]{3,2,1,0:T(8,128)(2,1)}, u32[]{:S(2)}) copy-start(bf16[2,2,128,1024]{3,2,1,0:T(8,128)(2,1)} %filt.1) | copy-start | bytes 3145732
  0.1 1.1 %copy-start.3 = (bf16[256,1024]{1,0:T(8,128)(2,1)S(1)}, bf16[256,1024]{1,0:T(8,128)(2,1)}, u32[]{:S(2)}) copy-start(bf16[256,1024]{1,0:T(8,128)(2,1)} %weight.1) | copy-start | bytes 1572868
  1.8 13.1 %collective-permute-start.11 = (bf16[256,256]{1,0:T(8,128)(2,1)S(1)}, bf16[256,256]{1,0:T(8,128)(2,1)S(1)}, u32[]{:S(2)}, u32[]{:S(2)}) collective-permute-start(bf16[256,256]{1,0:T(8,128)(2,1)S(1)} %get-tuple-element.45), channel_id=1, source_target_pairs={{0,2},{1,3},{2,0},{3,1},{4,6},{5,7},{6,4},{7,5},{8,10},{9,11},{10,... | collective-permute-start | bytes 393224 | tf_op jit(solution)/shard_map/ppermute | solution.py:318
  4.8 0.9 copy-start.1
  5.7 0.9 copy-start.5
  6.7 0.9 copy-start.6
  8.3 6.0 %copy-start.4 = (bf16[256,1024]{1,0:T(8,128)(2,1)S(1)}, bf16[256,1024]{1,0:T(8,128)(2,1)}, u32[]{:S(2)}) copy-start(bf16[256,1024]{1,0:T(8,128)(2,1)} %weight.2) | copy-start | bytes 1572868
  9.1 12.6 %collective-permute-start.7 = (bf16[4,2,128,128]{3,2,1,0:T(8,128)(2,1)S(1)}, bf16[4,2,128,128]{3,2,1,0:T(8,128)(2,1)S(1)}, u32[]{:S(2)}, u32[]{:S(2)}) collective-permute-start(bf16[4,2,128,128]{3,2,1,0:T(8,128)(2,1)S(1)} %get-tuple-element.43), channel_id=1, source_target_pairs={{0,2},{1,3},{2,0},{3,1},{4,6},{5,7},{6,4},{7,5},{8,10},{9,11},{10,... | collective-permute-start | bytes 786440 | tf_op jit(solution)/shard_map/ppermute | solution.py:318
  9.2 7.4 %collective-permute-start.12 = (bf16[256,256]{1,0:T(8,128)(2,1)S(1)}, bf16[256,256]{1,0:T(8,128)(2,1)S(1)}, u32[]{:S(2)}, u32[]{:S(2)}) collective-permute-start(bf16[256,256]{1,0:T(8,128)(2,1)S(1)} %get-tuple-element.37.refs_9_), channel_id=1, source_target_pairs={{0,4},{1,5},{2,6},{3,7},{4,8},{5,9},{6,10},{7,11},{8,12},{9,13},{1... | collective-permute-start | bytes 393224 | tf_op jit(solution)/shard_map/ppermute | solution.py:318
  11.3 26.4 %collective-permute-start = (bf16[128,1536]{1,0:T(8,128)(2,1)S(1)}, bf16[128,1536]{1,0:T(8,128)(2,1)S(1)}, u32[]{:S(2)}, u32[]{:S(2)}) collective-permute-start(bf16[128,1536]{1,0:T(8,128)(2,1)S(1)} %get-tuple-element.38), channel_id=1, source_target_pairs={{0,2},{1,3},{2,0},{3,1},{4,6},{5,7},{6,4},{7,5},{8,10},{9,11},{10,... | collective-permute-start | bytes 1179656 | tf_op jit(solution)/shard_map/ppermute | solution.py:318
  12.8 17.2 %collective-permute-start.1 = (bf16[128,1536]{1,0:T(8,128)(2,1)S(1)}, bf16[128,1536]{1,0:T(8,128)(2,1)S(1)}, u32[]{:S(2)}, u32[]{:S(2)}) collective-permute-start(bf16[128,1536]{1,0:T(8,128)(2,1)S(1)} %get-tuple-element.39), channel_id=1, source_target_pairs={{0,16},{1,17},{2,18},{3,19},{4,20},{5,21},{6,22},{7,23},{8,24},{9,... | collective-permute-start | bytes 1179656 | tf_op jit(solution)/shard_map/ppermute | solution.py:318
  14.9 6.8 %collective-permute-start.13 = (bf16[256,256]{1,0:T(8,128)(2,1)S(1)}, bf16[256,256]{1,0:T(8,128)(2,1)S(1)}, u32[]{:S(2)}, u32[]{:S(2)}) collective-permute-start(bf16[256,256]{1,0:T(8,128)(2,1)S(1)} %collective-permute-done.11.refs_10_), channel_id=1, source_target_pairs={{0,4},{1,5},{2,6},{3,7},{4,8},{5,9},{6,10},{7,11},{8,12},{9,13},{1... | collective-permute-start | bytes 393224 | tf_op jit(solution)/shard_map/ppermute | solution.py:318
  16.6 19.6 %collective-permute-start.2 = (bf16[128,1536]{1,0:T(8,128)(2,1)S(1)}, bf16[128,1536]{1,0:T(8,128)(2,1)S(1)}, u32[]{:S(2)}, u32[]{:S(2)}) collective-permute-start(bf16[128,1536]{1,0:T(8,128)(2,1)S(1)} %get-tuple-element.40), channel_id=1, source_target_pairs={{0,18},{1,19},{2,16},{3,17},{4,22},{5,23},{6,20},{7,21},{8,26},{9,... | collective-permute-start | bytes 1179656 | tf_op jit(solution)/shard_map/ppermute | solution.py:318
  21.7 6.8 %collective-permute-start.14 = (bf16[256,256]{1,0:T(8,128)(2,1)S(1)}, bf16[256,256]{1,0:T(8,128)(2,1)S(1)}, u32[]{:S(2)}, u32[]{:S(2)}) collective-permute-start(bf16[256,256]{1,0:T(8,128)(2,1)S(1)} %collective-permute-done.12.refs_11_), channel_id=1, source_target_pairs={{0,4},{1,5},{2,6},{3,7},{4,8},{5,9},{6,10},{7,11},{8,12},{9,13},{1... | collective-permute-start | bytes 393224 | tf_op jit(solution)/shard_map/ppermute | solution.py:318
  21.7 8.2 %collective-permute-start.15 = (bf16[256,256]{1,0:T(8,128)(2,1)S(1)}, bf16[256,256]{1,0:T(8,128)(2,1)S(1)}, u32[]{:S(2)}, u32[]{:S(2)}) collective-permute-start(bf16[256,256]{1,0:T(8,128)(2,1)S(1)} %collective-permute-done.13.refs_12_), channel_id=1, source_target_pairs={{0,4},{1,5},{2,6},{3,7},{4,8},{5,9},{6,10},{7,11},{8,12},{9,13},{1... | collective-permute-start | bytes 393224 | tf_op jit(solution)/shard_map/ppermute | solution.py:318
  23.1 22.3 %copy-start.2 = (bf16[128,1024]{1,0:T(8,128)(2,1)S(1)}, bf16[128,1024]{1,0:T(8,128)(2,1)}, u32[]{:S(2)}) copy-start(bf16[128,1024]{1,0:T(8,128)(2,1)} %refs_0_.1) | copy-start | bytes 786436
  28.5 10.8 %collective-permute-start.25 = (bf16[256,256]{1,0:T(8,128)(2,1)S(1)}, bf16[256,256]{1,0:T(8,128)(2,1)S(1)}, u32[]{:S(2)}, u32[]{:S(2)}) collective-permute-start(bf16[256,256]{1,0:T(8,128)(2,1)S(1)} %get-tuple-element.59), channel_id=1, source_target_pairs={{0,2},{1,3},{2,0},{3,1},{4,6},{5,7},{6,4},{7,5},{8,10},{9,11},{10,... | collective-permute-start | bytes 393224 | tf_op jit(solution)/shard_map/ppermute | solution.py:318
  29.9 9.4 %collective-permute-start.8 = (bf16[2,2,128,128]{3,2,1,0:T(8,128)(2,1)S(1)}, bf16[2,2,128,128]{3,2,1,0:T(8,128)(2,1)S(1)}, u32[]{:S(2)}, u32[]{:S(2)}) collective-permute-start(bf16[2,2,128,128]{3,2,1,0:T(8,128)(2,1)S(1)} %pad_maximum_fusion.2), channel_id=1, source_target_pairs={{0,4},{1,5},{2,6},{3,7},{4,8},{5,9},{6,10},{7,11},{8,12},{9,13},{1... | collective-permute-start | bytes 393224 | tf_op jit(solution)/shard_map/ppermute | solution.py:318
  29.9 11.5 %collective-permute-start.9 = (bf16[2,2,128,128]{3,2,1,0:T(8,128)(2,1)S(1)}, bf16[2,2,128,128]{3,2,1,0:T(8,128)(2,1)S(1)}, u32[]{:S(2)}, u32[]{:S(2)}) collective-permute-start(bf16[2,2,128,128]{3,2,1,0:T(8,128)(2,1)S(1)} %pad_maximum_fusion.3), channel_id=1, source_target_pairs={{0,8},{1,9},{2,10},{3,11},{4,12},{5,13},{6,14},{7,15},{8,0},{9,1},... | collective-permute-start | bytes 393224 | tf_op jit(solution)/shard_map/ppermute | solution.py:318
  36.2 6.8 %collective-permute-start.17 = (bf16[256,256]{1,0:T(8,128)(2,1)S(1)}, bf16[256,256]{1,0:T(8,128)(2,1)S(1)}, u32[]{:S(2)}, u32[]{:S(2)}) collective-permute-start(bf16[256,256]{1,0:T(8,128)(2,1)S(1)} %collective-permute-done.15.refs_14_), channel_id=1, source_target_pairs={{0,4},{1,5},{2,6},{3,7},{4,8},{5,9},{6,10},{7,11},{8,12},{9,13},{1... | collective-permute-start | bytes 393224 | tf_op jit(solution)/shard_map/ppermute | solution.py:318
  37.7 7.6 %collective-permute-start.16 = (bf16[256,256]{1,0:T(8,128)(2,1)S(1)}, bf16[256,256]{1,0:T(8,128)(2,1)S(1)}, u32[]{:S(2)}, u32[]{:S(2)}) collective-permute-start(bf16[256,256]{1,0:T(8,128)(2,1)S(1)} %collective-permute-done.14.refs_13_), channel_id=1, source_target_pairs={{0,4},{1,5},{2,6},{3,7},{4,8},{5,9},{6,10},{7,11},{8,12},{9,13},{1... | collective-permute-start | bytes 393224 | tf_op jit(solution)/shard_map/ppermute | solution.py:318
  39.3 8.8 %collective-permute-start.5 = (bf16[128,1536]{1,0:T(8,128)(2,1)S(1)}, bf16[128,1536]{1,0:T(8,128)(2,1)S(1)}, u32[]{:S(2)}, u32[]{:S(2)}) collective-permute-start(bf16[128,1536]{1,0:T(8,128)(2,1)S(1)} %collective-permute-done.1.refs_2_.g2), channel_id=1, source_target_pairs={{0,1},{1,0},{2,3},{3,2},{4,5},{5,4},{6,7},{7,6},{8,9},{9,8},{10,11... | collective-permute-start | bytes 1179656 | tf_op jit(solution)/shard_map/ppermute | solution.py:318
  39.3 8.8 %collective-permute-start.6 = (bf16[128,1536]{1,0:T(8,128)(2,1)S(1)}, bf16[128,1536]{1,0:T(8,128)(2,1)S(1)}, u32[]{:S(2)}, u32[]{:S(2)}) collective-permute-start(bf16[128,1536]{1,0:T(8,128)(2,1)S(1)} %collective-permute-done.2.refs_3_.g3), channel_id=1, source_target_pairs={{0,1},{1,0},{2,3},{3,2},{4,5},{5,4},{6,7},{7,6},{8,9},{9,8},{10,11... | collective-permute-start | bytes 1179656 | tf_op jit(solution)/shard_map/ppermute | solution.py:318
  41.4 6.7 %collective-permute-start.4 = (bf16[128,1536]{1,0:T(8,128)(2,1)S(1)}, bf16[128,1536]{1,0:T(8,128)(2,1)S(1)}, u32[]{:S(2)}, u32[]{:S(2)}) collective-permute-start(bf16[128,1536]{1,0:T(8,128)(2,1)S(1)} %collective-permute-done.refs_1_.g1), channel_id=1, source_target_pairs={{0,1},{1,0},{2,3},{3,2},{4,5},{5,4},{6,7},{7,6},{8,9},{9,8},{10,11... | collective-permute-start | bytes 1179656 | tf_op jit(solution)/shard_map/ppermute | solution.py:318
  42.9 5.0 %collective-permute-start.10 = (bf16[2,2,128,128]{3,2,1,0:T(8,128)(2,1)S(1)}, bf16[2,2,128,128]{3,2,1,0:T(8,128)(2,1)S(1)}, u32[]{:S(2)}, u32[]{:S(2)}) collective-permute-start(bf16[2,2,128,128]{3,2,1,0:T(8,128)(2,1)S(1)} %pad_maximum_fusion.4), channel_id=1, source_target_pairs={{0,12},{1,13},{2,14},{3,15},{4,0},{5,1},{6,2},{7,3},{8,4},{9,5},{1... | collective-permute-start | bytes 393224 | tf_op jit(solution)/shard_map/ppermute | solution.py:318
  45.4 2.7 %collective-permute-start.3 = (bf16[128,1024]{1,0:T(8,128)(2,1)S(1)}, bf16[128,1024]{1,0:T(8,128)(2,1)S(1)}, u32[]{:S(2)}, u32[]{:S(2)}) collective-permute-start(bf16[128,1024]{1,0:T(8,128)(2,1)S(1)} %copy-done.2), channel_id=1, source_target_pairs={{0,1},{1,0},{2,3},{3,2},{4,5},{5,4},{6,7},{7,6},{8,9},{9,8},{10,11... | collective-permute-start | bytes 786440 | tf_op jit(solution)/shard_map/ppermute | solution.py:318
  47.9 8.3 %collective-permute-start.26 = (bf16[2,256,256]{2,1,0:T(8,128)(2,1)S(1)}, bf16[2,256,256]{2,1,0:T(8,128)(2,1)S(1)}, u32[]{:S(2)}, u32[]{:S(2)}) collective-permute-start(bf16[2,256,256]{2,1,0:T(8,128)(2,1)S(1)} %pad_maximum_fusion.refs_0_), channel_id=1, source_target_pairs={{0,4},{1,5},{2,6},{3,7},{4,8},{5,9},{6,10},{7,11},{8,12},{9,13},{1... | collective-permute-start | bytes 786440 | tf_op jit(solution)/shard_map/ppermute | solution.py:318
  48.1 19.9 %copy-start.7 = (bf16[16,256,128]{2,1,0:T(8,128)(2,1)S(1)}, bf16[16,256,128]{2,1,0:T(8,128)(2,1)}, u32[]{:S(2)}) copy-start(bf16[16,256,128]{2,1,0:T(8,128)(2,1)} %constant.46.clone.refs_9_) | copy-start | bytes 3145732
  48.1 19.9 %copy-start.8 = (bf16[16,256,128]{2,1,0:T(8,128)(2,1)S(1)}, bf16[16,256,128]{2,1,0:T(8,128)(2,1)}, u32[]{:S(2)}) copy-start(bf16[16,256,128]{2,1,0:T(8,128)(2,1)} %constant.45.clone.refs_8_) | copy-start | bytes 3145732
  56.2 14.8 %collective-permute-start.27 = (bf16[2,256,256]{2,1,0:T(8,128)(2,1)S(1)}, bf16[2,256,256]{2,1,0:T(8,128)(2,1)S(1)}, u32[]{:S(2)}, u32[]{:S(2)}) collective-permute-start(bf16[2,256,256]{2,1,0:T(8,128)(2,1)S(1)} %collective-permute-done.26.refs_1_), channel_id=1, source_target_pairs={{0,4},{1,5},{2,6},{3,7},{4,8},{5,9},{6,10},{7,11},{8,12},{9,13},{1... | collective-permute-start | bytes 786440 | tf_op jit(solution)/shard_map/ppermute | solution.py:318
  56.2 10.4 %collective-permute-start.18 = (bf16[256,128]{1,0:T(8,128)(2,1)S(1)}, bf16[256,128]{1,0:T(8,128)(2,1)S(1)}, u32[]{:S(2)}, u32[]{:S(2)}) collective-permute-start(bf16[256,128]{1,0:T(8,128)(2,1)S(1)} %get-tuple-element.48), channel_id=1, source_target_pairs={{0,4},{1,5},{2,6},{3,7},{4,8},{5,9},{6,10},{7,11},{8,12},{9,13},{1... | collective-permute-start | bytes 196616 | tf_op jit(solution)/shard_map/ppermute | solution.py:318
  57.7 10.3 %collective-permute-start.19 = (bf16[256,128]{1,0:T(8,128)(2,1)S(1)}, bf16[256,128]{1,0:T(8,128)(2,1)S(1)}, u32[]{:S(2)}, u32[]{:S(2)}) collective-permute-start(bf16[256,128]{1,0:T(8,128)(2,1)S(1)} %get-tuple-element.49), channel_id=1, source_target_pairs={{0,8},{1,9},{2,10},{3,11},{4,12},{5,13},{6,14},{7,15},{8,0},{9,1},... | collective-permute-start | bytes 196616 | tf_op jit(solution)/shard_map/ppermute | solution.py:318
  60.6 7.4 %collective-permute-start.20 = (bf16[256,128]{1,0:T(8,128)(2,1)S(1)}, bf16[256,128]{1,0:T(8,128)(2,1)S(1)}, u32[]{:S(2)}, u32[]{:S(2)}) collective-permute-start(bf16[256,128]{1,0:T(8,128)(2,1)S(1)} %get-tuple-element.50), channel_id=1, source_target_pairs={{0,12},{1,13},{2,14},{3,15},{4,0},{5,1},{6,2},{7,3},{8,4},{9,5},{1... | collective-permute-start | bytes 196616 | tf_op jit(solution)/shard_map/ppermute | solution.py:318
  71.0 9.9 %collective-permute-start.28 = (bf16[2,256,256]{2,1,0:T(8,128)(2,1)S(1)}, bf16[2,256,256]{2,1,0:T(8,128)(2,1)S(1)}, u32[]{:S(2)}, u32[]{:S(2)}) collective-permute-start(bf16[2,256,256]{2,1,0:T(8,128)(2,1)S(1)} %collective-permute-done.27.refs_2_), channel_id=1, source_target_pairs={{0,4},{1,5},{2,6},{3,7},{4,8},{5,9},{6,10},{7,11},{8,12},{9,13},{1... | collective-permute-start | bytes 786440 | tf_op jit(solution)/shard_map/ppermute | solution.py:318
  81.7 10.7 %collective-permute-start.29 = (bf16[4,256,256]{2,1,0:T(8,128)(2,1)S(1)}, bf16[4,256,256]{2,1,0:T(8,128)(2,1)S(1)}, u32[]{:S(2)}, u32[]{:S(2)}) collective-permute-start(bf16[4,256,256]{2,1,0:T(8,128)(2,1)S(1)} %get-tuple-element.64), channel_id=1, source_target_pairs={{0,1},{1,0},{2,3},{3,2},{4,5},{5,4},{6,7},{7,6},{8,9},{9,8},{10,11... | collective-permute-start | bytes 1572872 | tf_op jit(solution)/shard_map/ppermute | solution.py:318
  81.8 7.1 %collective-permute-start.21 = (bf16[256,128]{1,0:T(8,128)(2,1)}, bf16[256,128]{1,0:T(8,128)(2,1)S(1)}, u32[]{:S(2)}, u32[]{:S(2)}) collective-permute-start(bf16[256,128]{1,0:T(8,128)(2,1)} %get-tuple-element.52), channel_id=1, source_target_pairs={{0,4},{1,5},{2,6},{3,7},{4,8},{5,9},{6,10},{7,11},{8,12},{9,13},{1... | collective-permute-start | bytes 196616 | tf_op jit(solution)/shard_map/ppermute | solution.py:318
  82.0 8.1 %collective-permute-start.22 = (bf16[256,128]{1,0:T(8,128)(2,1)S(1)}, bf16[256,128]{1,0:T(8,128)(2,1)S(1)}, u32[]{:S(2)}, u32[]{:S(2)}) collective-permute-start(bf16[256,128]{1,0:T(8,128)(2,1)S(1)} %get-tuple-element.53), channel_id=1, source_target_pairs={{0,8},{1,9},{2,10},{3,11},{4,12},{5,13},{6,14},{7,15},{8,0},{9,1},... | collective-permute-start | bytes 196616 | tf_op jit(solution)/shard_map/ppermute | solution.py:318
  82.0 8.1 %collective-permute-start.23 = (bf16[256,128]{1,0:T(8,128)(2,1)S(1)}, bf16[256,128]{1,0:T(8,128)(2,1)S(1)}, u32[]{:S(2)}, u32[]{:S(2)}) collective-permute-start(bf16[256,128]{1,0:T(8,128)(2,1)S(1)} %get-tuple-element.54), channel_id=1, source_target_pairs={{0,12},{1,13},{2,14},{3,15},{4,0},{5,1},{6,2},{7,3},{8,4},{9,5},{1... | collective-permute-start | bytes 196616 | tf_op jit(solution)/shard_map/ppermute | solution.py:318
  90.8 1.6 %collective-permute-start.24 = (bf16[512,256]{1,0:T(8,128)(2,1)S(1)}, bf16[512,256]{1,0:T(8,128)(2,1)S(1)}, u32[]{:S(2)}, u32[]{:S(2)}) collective-permute-start(bf16[512,256]{1,0:T(8,128)(2,1)S(1)} %shard_map.96.gated), channel_id=1, source_target_pairs={{0,1},{1,0},{2,3},{3,2},{4,5},{5,4},{6,7},{7,6},{8,9},{9,8},{10,11... | collective-permute-start | bytes 786440 | tf_op jit(solution)/shard_map/ppermute | solution.py:318
  93.9 11.6 %collective-permute-start.30 = (bf16[128,1024]{1,0:T(8,128)(2,1)S(1)}, bf16[128,1024]{1,0:T(8,128)(2,1)S(1)}, u32[]{:S(2)}, u32[]{:S(2)}) collective-permute-start(bf16[128,1024]{1,0:T(8,128)(2,1)S(1)} %get-tuple-element.66), channel_id=1, source_target_pairs={{0,18},{1,19},{2,16},{3,17},{4,22},{5,23},{6,20},{7,21},{8,26},{9,... | collective-permute-start | bytes 786440 | tf_op jit(solution)/shard_map/ppermute | solution.py:318
  98.3 12.2 %collective-permute-start.31 = (bf16[128,1024]{1,0:T(8,128)(2,1)S(1)}, bf16[128,1024]{1,0:T(8,128)(2,1)S(1)}, u32[]{:S(2)}, u32[]{:S(2)}) collective-permute-start(bf16[128,1024]{1,0:T(8,128)(2,1)S(1)} %get-tuple-element.67), channel_id=1, source_target_pairs={{0,16},{1,17},{2,18},{3,19},{4,20},{5,21},{6,22},{7,23},{8,24},{9,... | collective-permute-start | bytes 786440 | tf_op jit(solution)/shard_map/ppermute | solution.py:318
  98.3 12.2 %collective-permute-start.32 = (bf16[128,1024]{1,0:T(8,128)(2,1)S(1)}, bf16[128,1024]{1,0:T(8,128)(2,1)S(1)}, u32[]{:S(2)}, u32[]{:S(2)}) collective-permute-start(bf16[128,1024]{1,0:T(8,128)(2,1)S(1)} %get-tuple-element.68), channel_id=1, source_target_pairs={{0,2},{1,3},{2,0},{3,1},{4,6},{5,7},{6,4},{7,5},{8,10},{9,11},{10,... | collective-permute-start | bytes 786440 | tf_op jit(solution)/shard_map/ppermute | solution.py:318

commit v3 on v2

--- a/solution.py
+++ b/solution.py
@@ -63,38 +63,46 @@
     )
 
 
-def pack_weight(where, weight, own, away):
+def prologue(where, tokens, key, query, value, out, filt, *refs):
+    own_v, away_v, own_o, away_o, to_x, to_y, own, away_f, sem = refs
     y, x = where[0], where[1]
-    own[...] = weight[:, pl.ds(pl.multiple_of(y * 512 + x * 256, 256), 256)]
-    away[...] = weight[:, pl.ds(pl.multiple_of(y * 512 + 256 - x * 256, 256), 256)]
-
-
-def pack_messages(where, tokens, key, query, after, m1, m2, m3, own):
-    y, x = where[0], where[1]
-    for p, out in enumerate((own, m1, m2, m3)):
+
+    def lanes(p):
         row = 1 - y if p // 2 else y
         column = 1 - x if p % 2 else x
-        lanes = pl.ds(pl.multiple_of(row * 512 + column * 256, 256), 256)
-        if p:
-            out[:, pl.ds(0, 1024)] = tokens[...]
-        base = 1024 if p else 0
-        out[:, pl.ds(base, 256)] = key[:, lanes]
-        out[:, pl.ds(base + 256, 256)] = query[:, lanes]
-
-
-def pack_filter(where, filt, after, own, away):
+        return pl.ds(pl.multiple_of(row * 512 + column * 256, 256), 256)
+
+    moves = [(value.at[:, lanes(0)], own_v), (value.at[:, lanes(1)], away_v)]
+    moves += [(out.at[:, lanes(0)], own_o), (out.at[:, lanes(1)], away_o)]
+    moves.append((filt.at[:, :, :, lanes(1)], away_f))
+    moves += [(tokens, m.at[:, pl.ds(512, 1024)]) for m in (to_x, to_y)]
+    for p, target, base in ((0, own, 0), (1, to_x, 0), (2, to_y, 0), (3, to_x, 1536)):
+        moves.append((key.at[:, lanes(p)], target.at[:, pl.ds(base, 256)]))
+        moves.append((query.at[:, lanes(p)], target.at[:, pl.ds(base + 256, 256)]))
+    copies = [pltpu.make_async_copy(a, b, sem.at[i]) for i, (a, b) in enumerate(moves)]
+    for copy in copies:
+        copy.start()
+    for copy in copies:
+        copy.wait()
+
+
+def pack_filter(where, filt, near, *outs):
     y, x, z = where[0], where[1], where[2]
+    packed, outs = outs[4], outs[:4]
     low = low_lanes((128, 128))
-    for k, out in enumerate((own, away)):
-        column = 1 - x if k else x
+    for k in range(2):
         for j in range(2):
-            base = pl.multiple_of(y * 512 + column * 256 + j * 128, 128)
+            base = pl.multiple_of(y * 512 + x * 256 + j * 128, 128)
             for part in range(2):
-                even = filt[part, 0, :, pl.ds(base, 128)].astype(F32)
-                odd = filt[part, 1, :, pl.ds(base, 128)].astype(F32)
-                one, two = both(even, odd, low)
-                out[lax.rem(2 * j - z + 4, 4), part] = one
-                out[lax.rem(2 * j + 1 - z + 4, 4), part] = two
+                if k:
+                    pair = [near[part, i, :, pl.ds(j * 128, 128)].astype(F32) for i in range(2)]
+                else:
+                    pair = [filt[part, i, :, pl.ds(base, 128)].astype(F32) for i in range(2)]
+                one, two = both(*pair, low)
+                packed[2 * j, k, part] = one
+                packed[2 * j + 1, k, part] = two
+    for r in range(4):
+        outs[r][...] = packed[lax.rem(z + r, 4)]
 
 
 def value_kernel(where, *refs):
@@ -104,27 +112,28 @@
     x, z, c = where[1], where[2], where[3]
     acc[...] = jnp.zeros_like(acc)
 
-    def gather(blocks, lanes):
-        return jnp.concatenate([b[:, lanes] for b in blocks], axis=0)
+    def gather(blocks, base):
+        lanes = [pl.ds(pl.multiple_of(base + (512 if p else 0), 256), 256) for p in range(4)]
+        return jnp.concatenate([b[:, at] for b, at in zip(blocks, lanes)], axis=0)
 
     for r in range(4):
         owner = lax.rem(z - r + 4, 4)
         for k in range(2):
             row = 1 - x if k else x
-            lanes = pl.ds(pl.multiple_of(lax.rem(owner, 2) * 512 + row * 256, 256), 256)
+            base = lax.rem(owner, 2) * 512 + row * 256
             piece = pieces[2 * r + k]
 
             @pl.when(owner // 2 == c)
             def _():
-                acc[...] += dot(gather(mine, lanes), piece[...])
+                acc[...] += dot(gather(mine, base), piece[...])
 
             @pl.when(owner // 2 != c)
             def _():
-                acc[...] += dot(gather(other, lanes), piece[...])
+                acc[...] += dot(gather(other, base), piece[...])
 
     for p in range(4):
         rows = pl.ds(p * 128, 128)
-        gate = mine[p][:, 1024:1280] if p else gates[:, 0:256]
+        gate = mine[p][:, 1536:1792] if p == 3 else (mine[p] if p else gates)[:, 0:256]
         value = acc[rows, :].astype(BF16).astype(F32)
         drive[rows, :] = (gate.astype(F32) * value).astype(BF16)
     low = low_lanes((256, 128))
@@ -261,7 +270,7 @@
             rows = pl.ds(p * 128, 128)
             own = parts[p // 2][(p % 2) * 128 : (p % 2) * 128 + 128]
             direct = skip[:, lanes] * drive[rows, lanes].astype(F32)
-            query = gate[:, pl.ds((1280 if p else 256) + j * 128, 128)].astype(F32)
+            query = gate[:, pl.ds((1792 if p == 3 else 256) + j * 128, 128)].astype(F32)
             gated[rows, lanes] = (query * (own + direct)).astype(BF16)
 
 
@@ -334,28 +343,38 @@
 
     shape = jax.ShapeDtypeStruct
     block, square = shape((256, 128), BF16), shape((256, 256), BF16)
-    message = shape((128, 1536), BF16)
-    split = in_vmem(pack_weight, [square] * 2, moved=1 << 20)
-    own_first, away = split(where, w_value)
-    ring = [own_first, to_x(away)]
-    *messages, gates = in_vmem(
-        pack_messages, [message] * 3 + [shape((128, 512), BF16)], moved=2 << 20
-    )(where, tokens, gate_k, gate_q, own_first[:16, :128])
-    received = [to_peer(messages[p - 1], p) for p in (1, 2, 3)]
-    by_plane = shape((4, 2, 128, 128), BF16)
-    packed, away = in_vmem(pack_filter, [by_plane] * 2, moved=1 << 20)(
-        where, filter_spectrum, messages[0][:16, :128]
-    )
-    got = to_x(away)
-    filters = [jnp.stack([packed[r], got[r]]) for r in range(4)]
-    filters = filters[:1] + [to_z(filters[r], r) for r in (1, 2, 3)]
+    inside = pl.BlockSpec(memory_space=pltpu.MemorySpace.HBM)
+    laid = [square] * 4 + [shape((128, w), BF16) for w in (2048, 1536, 512)]
+    laid.append(shape((2, 2, 128, 256), BF16))
+    own_v, away_v, own_o, away_o, message_x, message_y, gates, away_f = pl.pallas_call(
+        prologue,
+        out_shape=laid,
+        in_specs=[pl.BlockSpec(memory_space=pltpu.SMEM)] + [inside] * 6,
+        out_specs=[inside] * 8,
+        scratch_shapes=[pltpu.SemaphoreType.DMA((15,))],
+        compiler_params=pltpu.CompilerParams(vmem_limit_bytes=62 * 1024 * 1024),
+    )(where, tokens, gate_k, gate_q, w_value, w_out, filter_spectrum)
+    ring = [own_v, to_x(away_v)]
+    from_x = to_peer(message_x, 1)
+    from_y = to_peer(message_y, 2)
+    ring += [to_z(ring[0], 1), to_z(ring[1], 1)]
+    received = [from_x, from_y, to_peer(after(from_x, from_y, ring[2]), 2)]
+    got = to_x(away_f)
+    filters = in_vmem(
+        pack_filter,
+        [shape((2, 2, 128, 128), BF16)] * 4,
+        [pltpu.VMEM((4, 2, 2, 128, 128), BF16)],
+        moved=1 << 20,
+    )(where, filter_spectrum, got)
+    filters = [filters[0]] + [to_z(filters[r], r) for r in (1, 2, 3)]
     mine = [tokens] + received
     other = [to_core(m) for m in mine]
-    ring += [to_z(ring[0], 1), to_z(ring[1], 1)]
     ring += [to_z(ring[2], 1), to_z(ring[3], 1)]
-    ring += [to_z(after(ring[4], *received), 1), to_z(ring[5], 1)]
-    own_out, away = split(where, after(w_out, messages[0]))
-    pair = jnp.stack([own_out, to_x(after(away, got))])
+    ring += [to_z(ring[4], 1), to_z(ring[5], 1)]
+    pair = jnp.stack([own_o, to_x(after(away_o, got))])
+    hops = [after(pair, ring[4], ring[5])]
+    hops.append(to_z(hops[0], 1))
+    hops.append(to_z(after(hops[1], ring[6], ring[7]), 1))
     gates = after(gates, *filters)
     drive, *sends = in_vmem(
         value_kernel,
@@ -380,10 +399,8 @@
     )(where, *columns, *filters, table, table_t)
     rows = [sends[0]] + [to_z(sends[r], r) for r in (1, 2, 3)]
 
-    hops = [after(pair, ring[6], ring[7])]
-    hops.append(to_z(hops[0], 1))
-    hops.append(to_z(after(hops[1], drive), 1))
     hops.append(to_z(after(hops[2], sends[0]), 1))
+    hops[3] = after(hops[3], *rows[1:])
     quad = shape((4, 256, 256), BF16)
     keep, give = in_vmem(sort_weight, [quad] * 2, moved=2 << 20)(where, *hops)
     theirs = to_core(give)

time: 112 us -> 181 us (1.62)
  Pallas kernels: 11.2 us -> 68.3 us
  waiting for transfers between devices: 54.8 us -> 73.5 us
  local copies, waits for them, and re-layouts: 4.79 us -> 0.79 us
  starting transfers between devices: 39.3 us -> 36.3 us
    pallas_call x0 -> x1, Pallas kernels: none -> 57.6 us  [planes(): pl.pallas_call(prologue, out_shape=laid, in_specs=[pl.BlockSpec(memory_sp...]
    ppermute x33, waiting for transfers between devices: 54.8 us -> 73.5 us  [permute(): return lax.ppermute(values, AXES, pairs)]
    unnamed x18 -> x16, local copies, waits for them, and re-layouts: 3.99 us -> 0.03 us
    ppermute x33, starting transfers between devices: 39.3 us -> 36.3 us  [permute(): return lax.ppermute(values, AXES, pairs)]
    pallas_call x9 -> x6, Pallas kernels: 11.2 us -> 10.7 us  [call(): pl.pallas_call(kernel, out_shape=out_shape, in_specs=specs, out_specs=jax...]
  transfers between devices with their start and end apart: 33 -> 33, of which waited for: 17 -> 17; matrix products, arithmetic and copies ran while one was open for 1% -> 0% of each run, Pallas kernels for 8% -> 4%
where the time goes in v3:
time: 181 us
  waiting for transfers between devices  73.5 us (41%)
  Pallas kernels  68.3 us (38%)
  starting transfers between devices  36.3 us (20%)
    ppermute x33, waiting for transfers between devices, permute(): return lax.ppermute(values, AXES, pairs)  73.5 us
    pallas_call x1, Pallas kernels, planes(): pl.pallas_call(prologue, out_shape=laid, in_specs=[pl.BlockSpec(memory_sp...  57.6 us
    ppermute x33, starting transfers between devices, permute(): return lax.ppermute(values, AXES, pairs)  36.3 us
    pallas_call x6, Pallas kernels, call(): pl.pallas_call(kernel, out_shape=out_shape, in_specs=specs, out_specs=jax...  10.7 us
  transfers between devices with their start and end apart: 33, of which 17 were waited for; matrix products, arithmetic and copies ran while one was open for 0% of the time, Pallas kernels for 4%

profile of v3, /device:TPU:0, one launch (start us, length us, event | category | flops | bytes accessed | tf_op | source)
XLA Modules:
  0.0 180.6 jit_solution(8525715115700935893)
XLA Ops:
  0.0 0.6 pad_add_fusion.where
  0.6 57.6 %shard_map.91 = (bf16[256,256]{1,0:T(8,128)(2,1)}, bf16[256,256]{1,0:T(8,128)(2,1)}, bf16[256,256]{1,0:T(8,128)(2,1)}, bf16[256,256]{1,0:T(8,128)(2,1)}, bf16[12...) custom-call(s32[4]{0:T(128)} %pad_add_fusion.where, ...), custom_call_target="tpu_custom_call" | custom-call | tf_op jit(solution)/shard_map/pallas_call | solution.py:349
  58.2 3.0 %collective-permute-start = (bf16[128,2048]{1,0:T(8,128)(2,1)}, bf16[128,2048]{1,0:T(8,128)(2,1)S(1)}, u32[]{:S(2)}, u32[]{:S(2)}) collective-permute-start(bf16[128,2048]{1,0:T(8,128)(2,1)} %get-tuple-element.39), channel_id=1, source_target_pairs={{0,2},{1,3},{2,0},{3,1},{4,6},{5,7},{6,4},{7,5},{8,10},{9,11},{10,... | collective-permute-start | bytes 1572872 | tf_op jit(solution)/shard_map/ppermute | solution.py:327
  61.2 1.5 collective-permute-start.1
  62.8 1.6 collective-permute-start.2
  64.3 5.4 %collective-permute-done.2.refs_11_ = bf16[256,256]{1,0:T(8,128)(2,1)S(1)} collective-permute-done((bf16[256,256]{1,0:T(8,128)(2,1)}, bf16[256,256]{1,0:T(8,128)(2,1)S(1)}, u32[]{:S(2)}, u32[]{:S(2)}) %collective-permute-start.2) | collective-permute-done | bytes 131104 | tf_op jit(solution)/shard_map/ppermute | solution.py:327
  69.7 2.3 %collective-permute-done.1.refs_2_.g2 = bf16[128,1536]{1,0:T(8,128)(2,1)S(1)} collective-permute-done((bf16[128,1536]{1,0:T(8,128)(2,1)}, bf16[128,1536]{1,0:T(8,128)(2,1)S(1)}, u32[]{:S(2)}, u32[]{:S(2)}) %collective-permute-start.1) | collective-permute-done | bytes 393248 | tf_op jit(solution)/shard_map/ppermute | solution.py:327
  72.0 1.3 collective-permute-done.refs_1_.g1
  73.4 1.8 collective-permute-start.3
  75.1 1.5 collective-permute-start.8
  76.6 0.5 collective-permute-start.12
  77.2 7.9 %collective-permute-done.12.refs_10_ = bf16[256,256]{1,0:T(8,128)(2,1)S(1)} collective-permute-done((bf16[256,256]{1,0:T(8,128)(2,1)}, bf16[256,256]{1,0:T(8,128)(2,1)S(1)}, u32[]{:S(2)}, u32[]{:S(2)}) %collective-permute-start.12) | collective-permute-done | bytes 131104 | tf_op jit(solution)/shard_map/ppermute | solution.py:327
  85.1 1.6 collective-permute-start.13
  86.6 1.6 collective-permute-start.14
  88.2 3.6 %collective-permute-done.13.refs_12_ = bf16[256,256]{1,0:T(8,128)(2,1)S(1)} collective-permute-done((bf16[256,256]{1,0:T(8,128)(2,1)S(1)}, bf16[256,256]{1,0:T(8,128)(2,1)S(1)}, u32[]{:S(2)}, u32[]{:S(2)}) %collective-permute-start.13) | collective-permute-done | bytes 131104 | tf_op jit(solution)/shard_map/ppermute | solution.py:327
  91.8 0.0 collective-permute-start.15
  91.8 1.5 collective-permute-start.25
  93.3 0.9 shard_map.92
  94.2 2.2 %collective-permute-start.9 = (bf16[2,2,128,128]{3,2,1,0:T(8,128)(2,1)S(1)}, bf16[2,2,128,128]{3,2,1,0:T(8,128)(2,1)S(1)}, u32[]{:S(2)}, u32[]{:S(2)}) collective-permute-start(bf16[2,2,128,128]{3,2,1,0:T(8,128)(2,1)S(1)} %get-tuple-element.46), channel_id=1, source_target_pairs={{0,4},{1,5},{2,6},{3,7},{4,8},{5,9},{6,10},{7,11},{8,12},{9,13},{1... | collective-permute-start | bytes 393224 | tf_op jit(solution)/shard_map/ppermute | solution.py:327
  96.4 0.0 collective-permute-done.14.refs_13_
  96.4 2.2 %collective-permute-start.10 = (bf16[2,2,128,128]{3,2,1,0:T(8,128)(2,1)S(1)}, bf16[2,2,128,128]{3,2,1,0:T(8,128)(2,1)S(1)}, u32[]{:S(2)}, u32[]{:S(2)}) collective-permute-start(bf16[2,2,128,128]{3,2,1,0:T(8,128)(2,1)S(1)} %get-tuple-element.47), channel_id=1, source_target_pairs={{0,8},{1,9},{2,10},{3,11},{4,12},{5,13},{6,14},{7,15},{8,0},{9,1},... | collective-permute-start | bytes 393224 | tf_op jit(solution)/shard_map/ppermute | solution.py:327
  98.6 0.9 collective-permute-done.15.refs_14_
  99.5 0.0 collective-permute-start.16
  99.5 0.0 collective-permute-done.25
  99.6 0.5 collective-permute-start.7
  100.1 2.0 %collective-permute-done.9.refs_5_ = bf16[2,2,128,128]{3,2,1,0:T(8,128)(2,1)S(1)} collective-permute-done((bf16[2,2,128,128]{3,2,1,0:T(8,128)(2,1)S(1)}, bf16[2,2,128,128]{3,2,1,0:T(8,128)(2,1)S(1)}, u32[]{:S(2)}, u32[]{:S(2)}) %collective-permute-start.9) | collective-permute-done | bytes 131104 | tf_op jit(solution)/shard_map/ppermute | solution.py:327
  102.1 1.2 collective-permute-start.26
  103.4 9.9 %collective-permute-done.10.refs_6_ = bf16[2,2,128,128]{3,2,1,0:T(8,128)(2,1)S(1)} collective-permute-done((bf16[2,2,128,128]{3,2,1,0:T(8,128)(2,1)S(1)}, bf16[2,2,128,128]{3,2,1,0:T(8,128)(2,1)S(1)}, u32[]{:S(2)}, u32[]{:S(2)}) %collective-permute-start.10) | collective-permute-done | bytes 131104 | tf_op jit(solution)/shard_map/ppermute | solution.py:327
  113.3 0.0 collective-permute-start.6
  113.3 7.2 %collective-permute-done.17.refs_16_ = bf16[256,256]{1,0:T(8,128)(2,1)S(1)} collective-permute-done((bf16[256,256]{1,0:T(8,128)(2,1)S(1)}, bf16[256,256]{1,0:T(8,128)(2,1)S(1)}, u32[]{:S(2)}, u32[]{:S(2)}) %collective-permute-start.17) | collective-permute-done | bytes 131104 | tf_op jit(solution)/shard_map/ppermute | solution.py:327
  120.5 0.0 collective-permute-start.4
  120.5 0.0 collective-permute-done.26.refs_1_
  120.5 0.1 collective-permute-start.11
  120.6 5.8 %collective-permute-done.11.refs_7_ = bf16[2,2,128,128]{3,2,1,0:T(8,128)(2,1)S(1)} collective-permute-done((bf16[2,2,128,128]{3,2,1,0:T(8,128)(2,1)S(1)}, bf16[2,2,128,128]{3,2,1,0:T(8,128)(2,1)S(1)}, u32[]{:S(2)}, u32[]{:S(2)}) %collective-permute-start.11) | collective-permute-done | bytes 131104 | tf_op jit(solution)/shard_map/ppermute | solution.py:327
  126.4 0.0 collective-permute-done.4.refs_4_
  126.4 0.0 collective-permute-done.6.refs_6_
  126.4 0.0 collective-permute-done.5.refs_5_
  126.5 2.7 %shard_map.93 = (bf16[512,256]{1,0:T(8,128)(2,1)S(1)}, bf16[256,128]{1,0:T(8,128)(2,1)S(1)}, bf16[256,128]{1,0:T(8,128)(2,1)S(1)}, bf16[256,128]{1,0:T(8,128)(2,1)S(1)}, bf16[256,128]{1,0:T(8,128)(2,1)S(1)}) custom-call(s32[4]{0:T(128)S(1)} %copy-done.4, bf16[128,1024]{1,0:T(8,128)(2,1)S(1)} %copy-done.1, ...), custom_call_target="tpu_custom_call" | custom-call | flops 536870912 | bytes 4194304 | tf_op jit(solution)/shard_map/pallas_call | solution.py:38
  129.2 0.1 collective-permute-start.18
  129.2 4.4 %collective-permute-start.19 = (bf16[256,128]{1,0:T(8,128)(2,1)S(1)}, bf16[256,128]{1,0:T(8,128)(2,1)S(1)}, u32[]{:S(2)}, u32[]{:S(2)}) collective-permute-start(bf16[256,128]{1,0:T(8,128)(2,1)S(1)} %get-tuple-element.53), channel_id=1, source_target_pairs={{0,8},{1,9},{2,10},{3,11},{4,12},{5,13},{6,14},{7,15},{8,0},{9,1},... | collective-permute-start | bytes 196616 | tf_op jit(solution)/shard_map/ppermute | solution.py:327
  133.6 1.2 collective-permute-start.20
  134.8 4.1 %collective-permute-done.18.refs_1_ = bf16[256,128]{1,0:T(8,128)(2,1)S(1)} collective-permute-done((bf16[256,128]{1,0:T(8,128)(2,1)S(1)}, bf16[256,128]{1,0:T(8,128)(2,1)S(1)}, u32[]{:S(2)}, u32[]{:S(2)}) %collective-permute-start.18) | collective-permute-done | bytes 65568 | tf_op jit(solution)/shard_map/ppermute | solution.py:327
  138.9 1.5 collective-permute-done.19.refs_2_
  140.4 0.0 collective-permute-done.20.refs_3_
  140.4 2.4 %shard_map.94 = (bf16[256,128]{1,0:T(8,128)(2,1)S(1)}, bf16[256,128]{1,0:T(8,128)(2,1)S(1)}, bf16[256,128]{1,0:T(8,128)(2,1)S(1)}, bf16[256,128]{1,0:T(8,128)(2,1)S(1)}) custom-call(s32[4]{0:T(128)S(1)} %copy-done.4, bf16[256,128]{1,0:T(8,128)(2,1)S(1)} %get-tuple-element.51.refs_0_, bf16[256,128]{1,0:T(8,128)(2,1)S(1)} %collective-permute-done.18.refs_1_, ...), custom_call_target="tpu_custom_call" | custom-call | flops 1073741824 | bytes 5242880 | tf_op jit(solution)/shard_map/pallas_call | solution.py:38
  142.8 1.9 %collective-permute-start.28 = (bf16[2,256,256]{2,1,0:T(8,128)(2,1)S(1)}, bf16[2,256,256]{2,1,0:T(8,128)(2,1)S(1)}, u32[]{:S(2)}, u32[]{:S(2)}) collective-permute-start(bf16[2,256,256]{2,1,0:T(8,128)(2,1)S(1)} %collective-permute-done.27.refs_2_), channel_id=1, source_target_pairs={{0,4},{1,5},{2,6},{3,7},{4,8},{5,9},{6,10},{7,11},{8,12},{9,13},{1... | collective-permute-start | bytes 786440 | tf_op jit(solution)/shard_map/ppermute | solution.py:327
  144.8 0.1 collective-permute-start.21
  144.8 2.5 %collective-permute-start.22 = (bf16[256,128]{1,0:T(8,128)(2,1)S(1)}, bf16[256,128]{1,0:T(8,128)(2,1)S(1)}, u32[]{:S(2)}, u32[]{:S(2)}) collective-permute-start(bf16[256,128]{1,0:T(8,128)(2,1)S(1)} %get-tuple-element.57), channel_id=1, source_target_pairs={{0,8},{1,9},{2,10},{3,11},{4,12},{5,13},{6,14},{7,15},{8,0},{9,1},... | collective-permute-start | bytes 196616 | tf_op jit(solution)/shard_map/ppermute | solution.py:327
  147.3 1.3 collective-permute-start.23
  148.6 6.8 %collective-permute-done.21.e1 = bf16[256,128]{1,0:T(8,128)(2,1)S(1)} collective-permute-done((bf16[256,128]{1,0:T(8,128)(2,1)S(1)}, bf16[256,128]{1,0:T(8,128)(2,1)S(1)}, u32[]{:S(2)}, u32[]{:S(2)}) %collective-permute-start.21) | collective-permute-done | bytes 65568 | tf_op jit(solution)/shard_map/ppermute | solution.py:327
  155.4 1.8 collective-permute-done.22.e2
  157.2 1.5 shard_map.96
  158.7 0.0 collective-permute-start.29
  158.7 0.8 dynamic_slice.3
  159.4 0.8 shard_map.95.gated
  160.2 0.6 collective-permute-start.24
  160.8 1.2 collective-permute-done.24.other
  162.0 2.5 %shard_map.97 = (f32[128,1024]{1,0:T(8,128)S(1)}, bf16[128,1024]{1,0:T(8,128)(2,1)S(1)}, bf16[128,1024]{1,0:T(8,128)(2,1)S(1)}, bf16[128,1024]{1,0:T(8,128)(2,1)S(1)}) custom-call(bf16[512,256]{1,0:T(8,128)(2,1)S(1)} %shard_map.95.gated, bf16[512,256]{1,0:T(8,128)(2,1)S(1)} %collective-permute-done.24.other, ...), custom_call_target="tpu_custom_call" | custom-call | flops 1073741824 | bytes 4194304 | tf_op jit(solution)/shard_map/pallas_call | solution.py:38
  164.5 1.3 collective-permute-start.32
  165.8 0.5 collective-permute-start.31
  166.3 1.7 collective-permute-start.30
  168.0 5.6 %collective-permute-done.32 = bf16[128,1024]{1,0:T(8,128)(2,1)S(1)} collective-permute-done((bf16[128,1024]{1,0:T(8,128)(2,1)S(1)}, bf16[128,1024]{1,0:T(8,128)(2,1)S(1)}, u32[]{:S(2)}, u32[]{:S(2)}) %collective-permute-start.32) | collective-permute-done | bytes 262176 | tf_op jit(solution)/shard_map/ppermute | solution.py:327
  173.7 6.1 %collective-permute-done.31 = bf16[128,1024]{1,0:T(8,128)(2,1)S(1)} collective-permute-done((bf16[128,1024]{1,0:T(8,128)(2,1)S(1)}, bf16[128,1024]{1,0:T(8,128)(2,1)S(1)}, u32[]{:S(2)}, u32[]{:S(2)}) %collective-permute-start.31) | collective-permute-done | bytes 262176 | tf_op jit(solution)/shard_map/ppermute | solution.py:327
  179.7 0.8 add_convert_fusion
  (29 shorter events, 0.1 us)
Async XLA Ops:
  0.6 92.7 %copy-start = (bf16[2,2,128,1024]{3,2,1,0:T(8,128)(2,1)S(1)}, bf16[2,2,128,1024]{3,2,1,0:T(8,128)(2,1)}, u32[]{:S(2)}) copy-start(bf16[2,2,128,1024]{3,2,1,0:T(8,128)(2,1)} %filt.3) | copy-start | bytes 3145732
  58.2 15.1 %collective-permute-start = (bf16[128,2048]{1,0:T(8,128)(2,1)}, bf16[128,2048]{1,0:T(8,128)(2,1)S(1)}, u32[]{:S(2)}, u32[]{:S(2)}) collective-permute-start(bf16[128,2048]{1,0:T(8,128)(2,1)} %get-tuple-element.39), channel_id=1, source_target_pairs={{0,2},{1,3},{2,0},{3,1},{4,6},{5,7},{6,4},{7,5},{8,10},{9,11},{10,... | collective-permute-start | bytes 1572872 | tf_op jit(solution)/shard_map/ppermute | solution.py:327
  61.2 10.8 %collective-permute-start.1 = (bf16[128,1536]{1,0:T(8,128)(2,1)}, bf16[128,1536]{1,0:T(8,128)(2,1)S(1)}, u32[]{:S(2)}, u32[]{:S(2)}) collective-permute-start(bf16[128,1536]{1,0:T(8,128)(2,1)} %get-tuple-element.40), channel_id=1, source_target_pairs={{0,16},{1,17},{2,18},{3,19},{4,20},{5,21},{6,22},{7,23},{8,24},{9,... | collective-permute-start | bytes 1179656 | tf_op jit(solution)/shard_map/ppermute | solution.py:327
  62.8 7.0 %collective-permute-start.2 = (bf16[256,256]{1,0:T(8,128)(2,1)}, bf16[256,256]{1,0:T(8,128)(2,1)S(1)}, u32[]{:S(2)}, u32[]{:S(2)}) collective-permute-start(bf16[256,256]{1,0:T(8,128)(2,1)} %get-tuple-element.41.refs_9_), channel_id=1, source_target_pairs={{0,4},{1,5},{2,6},{3,7},{4,8},{5,9},{6,10},{7,11},{8,12},{9,13},{1... | collective-permute-start | bytes 393224 | tf_op jit(solution)/shard_map/ppermute | solution.py:327
  73.4 26.2 %collective-permute-start.3 = (bf16[128,2048]{1,0:T(8,128)(2,1)S(1)}, bf16[128,2048]{1,0:T(8,128)(2,1)S(1)}, u32[]{:S(2)}, u32[]{:S(2)}) collective-permute-start(bf16[128,2048]{1,0:T(8,128)(2,1)S(1)} %collective-permute-done.refs_1_.g1), channel_id=1, source_target_pairs={{0,16},{1,17},{2,18},{3,19},{4,20},{5,21},{6,22},{7,23},{8,24},{9,... | collective-permute-start | bytes 1572872 | tf_op jit(solution)/shard_map/ppermute | solution.py:327
  75.1 13.1 %collective-permute-start.8 = (bf16[2,2,128,256]{3,2,1,0:T(8,128)(2,1)}, bf16[2,2,128,256]{3,2,1,0:T(8,128)(2,1)S(1)}, u32[]{:S(2)}, u32[]{:S(2)}) collective-permute-start(bf16[2,2,128,256]{3,2,1,0:T(8,128)(2,1)} %get-tuple-element.44), channel_id=1, source_target_pairs={{0,2},{1,3},{2,0},{3,1},{4,6},{5,7},{6,4},{7,5},{8,10},{9,11},{10,... | collective-permute-start | bytes 786440 | tf_op jit(solution)/shard_map/ppermute | solution.py:327
  76.6 16.7 %copy-start.4 = (s32[4]{0:T(128)S(1)}, s32[4]{0:T(128)}, u32[]{:S(2)}) copy-start(s32[4]{0:T(128)} %pad_add_fusion.where) | copy-start | bytes 52
  76.6 8.4 %collective-permute-start.12 = (bf16[256,256]{1,0:T(8,128)(2,1)}, bf16[256,256]{1,0:T(8,128)(2,1)S(1)}, u32[]{:S(2)}, u32[]{:S(2)}) collective-permute-start(bf16[256,256]{1,0:T(8,128)(2,1)} %get-tuple-element.50), channel_id=1, source_target_pairs={{0,2},{1,3},{2,0},{3,1},{4,6},{5,7},{6,4},{7,5},{8,10},{9,11},{10,... | collective-permute-start | bytes 393224 | tf_op jit(solution)/shard_map/ppermute | solution.py:327
  85.1 6.8 %collective-permute-start.13 = (bf16[256,256]{1,0:T(8,128)(2,1)S(1)}, bf16[256,256]{1,0:T(8,128)(2,1)S(1)}, u32[]{:S(2)}, u32[]{:S(2)}) collective-permute-start(bf16[256,256]{1,0:T(8,128)(2,1)S(1)} %collective-permute-done.12.refs_10_), channel_id=1, source_target_pairs={{0,4},{1,5},{2,6},{3,7},{4,8},{5,9},{6,10},{7,11},{8,12},{9,13},{1... | collective-permute-start | bytes 393224 | tf_op jit(solution)/shard_map/ppermute | solution.py:327
  86.6 9.8 %collective-permute-start.14 = (bf16[256,256]{1,0:T(8,128)(2,1)S(1)}, bf16[256,256]{1,0:T(8,128)(2,1)S(1)}, u32[]{:S(2)}, u32[]{:S(2)}) collective-permute-start(bf16[256,256]{1,0:T(8,128)(2,1)S(1)} %collective-permute-done.2.refs_11_), channel_id=1, source_target_pairs={{0,4},{1,5},{2,6},{3,7},{4,8},{5,9},{6,10},{7,11},{8,12},{9,13},{1... | collective-permute-start | bytes 393224 | tf_op jit(solution)/shard_map/ppermute | solution.py:327
  88.2 11.9 %copy-start.7 = (bf16[256,256]{1,0:T(8,128)(2,1)S(1)}, bf16[256,256]{1,0:T(8,128)(2,1)}, u32[]{:S(2)}) copy-start(bf16[256,256]{1,0:T(8,128)(2,1)} %get-tuple-element.60) | copy-start | bytes 393220
  91.8 7.7 %collective-permute-start.15 = (bf16[256,256]{1,0:T(8,128)(2,1)S(1)}, bf16[256,256]{1,0:T(8,128)(2,1)S(1)}, u32[]{:S(2)}, u32[]{:S(2)}) collective-permute-start(bf16[256,256]{1,0:T(8,128)(2,1)S(1)} %collective-permute-done.13.refs_12_), channel_id=1, source_target_pairs={{0,4},{1,5},{2,6},{3,7},{4,8},{5,9},{6,10},{7,11},{8,12},{9,13},{1... | collective-permute-start | bytes 393224 | tf_op jit(solution)/shard_map/ppermute | solution.py:327
  91.8 7.7 %collective-permute-start.25 = (bf16[256,256]{1,0:T(8,128)(2,1)}, bf16[256,256]{1,0:T(8,128)(2,1)S(1)}, u32[]{:S(2)}, u32[]{:S(2)}) collective-permute-start(bf16[256,256]{1,0:T(8,128)(2,1)} %get-tuple-element.62), channel_id=1, source_target_pairs={{0,2},{1,3},{2,0},{3,1},{4,6},{5,7},{6,4},{7,5},{8,10},{9,11},{10,... | collective-permute-start | bytes 393224 | tf_op jit(solution)/shard_map/ppermute | solution.py:327
  94.2 8.0 %collective-permute-start.9 = (bf16[2,2,128,128]{3,2,1,0:T(8,128)(2,1)S(1)}, bf16[2,2,128,128]{3,2,1,0:T(8,128)(2,1)S(1)}, u32[]{:S(2)}, u32[]{:S(2)}) collective-permute-start(bf16[2,2,128,128]{3,2,1,0:T(8,128)(2,1)S(1)} %get-tuple-element.46), channel_id=1, source_target_pairs={{0,4},{1,5},{2,6},{3,7},{4,8},{5,9},{6,10},{7,11},{8,12},{9,13},{1... | collective-permute-start | bytes 393224 | tf_op jit(solution)/shard_map/ppermute | solution.py:327
  96.4 16.8 %collective-permute-start.10 = (bf16[2,2,128,128]{3,2,1,0:T(8,128)(2,1)S(1)}, bf16[2,2,128,128]{3,2,1,0:T(8,128)(2,1)S(1)}, u32[]{:S(2)}, u32[]{:S(2)}) collective-permute-start(bf16[2,2,128,128]{3,2,1,0:T(8,128)(2,1)S(1)} %get-tuple-element.47), channel_id=1, source_target_pairs={{0,8},{1,9},{2,10},{3,11},{4,12},{5,13},{6,14},{7,15},{8,0},{9,1},... | collective-permute-start | bytes 393224 | tf_op jit(solution)/shard_map/ppermute | solution.py:327
  99.5 13.7 %collective-permute-start.16 = (bf16[256,256]{1,0:T(8,128)(2,1)S(1)}, bf16[256,256]{1,0:T(8,128)(2,1)S(1)}, u32[]{:S(2)}, u32[]{:S(2)}) collective-permute-start(bf16[256,256]{1,0:T(8,128)(2,1)S(1)} %collective-permute-done.14.refs_13_), channel_id=1, source_target_pairs={{0,4},{1,5},{2,6},{3,7},{4,8},{5,9},{6,10},{7,11},{8,12},{9,13},{1... | collective-permute-start | bytes 393224 | tf_op jit(solution)/shard_map/ppermute | solution.py:327
  99.5 26.9 %collective-permute-start.5 = (bf16[128,2048]{1,0:T(8,128)(2,1)S(1)}, bf16[128,2048]{1,0:T(8,128)(2,1)S(1)}, u32[]{:S(2)}, u32[]{:S(2)}) collective-permute-start(bf16[128,2048]{1,0:T(8,128)(2,1)S(1)} %collective-permute-done.refs_1_.g1), channel_id=1, source_target_pairs={{0,1},{1,0},{2,3},{3,2},{4,5},{5,4},{6,7},{7,6},{8,9},{9,8},{10,11... | collective-permute-start | bytes 1572872 | tf_op jit(solution)/shard_map/ppermute | solution.py:327
  99.6 26.9 %collective-permute-start.7 = (bf16[128,2048]{1,0:T(8,128)(2,1)S(1)}, bf16[128,2048]{1,0:T(8,128)(2,1)S(1)}, u32[]{:S(2)}, u32[]{:S(2)}) collective-permute-start(bf16[128,2048]{1,0:T(8,128)(2,1)S(1)} %collective-permute-done.3.refs_3_.g3), channel_id=1, source_target_pairs={{0,1},{1,0},{2,3},{3,2},{4,5},{5,4},{6,7},{7,6},{8,9},{9,8},{10,11... | collective-permute-start | bytes 1572872 | tf_op jit(solution)/shard_map/ppermute | solution.py:327
  100.1 20.4 %copy-start.1 = (bf16[128,1024]{1,0:T(8,128)(2,1)S(1)}, bf16[128,1024]{1,0:T(8,128)(2,1)}, u32[]{:S(2)}) copy-start(bf16[128,1024]{1,0:T(8,128)(2,1)} %refs_0_.1) | copy-start | bytes 786436
  100.1 26.4 %copy-start.2 = (bf16[128,512]{1,0:T(8,128)(2,1)S(1)}, bf16[128,512]{1,0:T(8,128)(2,1)}, u32[]{:S(2)}) copy-start(bf16[128,512]{1,0:T(8,128)(2,1)} %get-tuple-element.49.refs_8_.gates) | copy-start | bytes 393220
  100.1 26.4 %copy-start.3 = (bf16[256,256]{1,0:T(8,128)(2,1)S(1)}, bf16[256,256]{1,0:T(8,128)(2,1)}, u32[]{:S(2)}) copy-start(bf16[256,256]{1,0:T(8,128)(2,1)} %get-tuple-element.41.refs_9_) | copy-start | bytes 393220
  102.1 18.4 %collective-permute-start.26 = (bf16[2,256,256]{2,1,0:T(8,128)(2,1)S(1)}, bf16[2,256,256]{2,1,0:T(8,128)(2,1)S(1)}, u32[]{:S(2)}, u32[]{:S(2)}) collective-permute-start(bf16[2,256,256]{2,1,0:T(8,128)(2,1)S(1)} %pad_maximum_fusion.refs_0_), channel_id=1, source_target_pairs={{0,4},{1,5},{2,6},{3,7},{4,8},{5,9},{6,10},{7,11},{8,12},{9,13},{1... | collective-permute-start | bytes 786440 | tf_op jit(solution)/shard_map/ppermute | solution.py:327
  113.3 7.2 %collective-permute-start.17 = (bf16[256,256]{1,0:T(8,128)(2,1)S(1)}, bf16[256,256]{1,0:T(8,128)(2,1)S(1)}, u32[]{:S(2)}, u32[]{:S(2)}) collective-permute-start(bf16[256,256]{1,0:T(8,128)(2,1)S(1)} %collective-permute-done.15.refs_14_), channel_id=1, source_target_pairs={{0,4},{1,5},{2,6},{3,7},{4,8},{5,9},{6,10},{7,11},{8,12},{9,13},{1... | collective-permute-start | bytes 393224 | tf_op jit(solution)/shard_map/ppermute | solution.py:327
  113.3 13.1 %collective-permute-start.6 = (bf16[128,1536]{1,0:T(8,128)(2,1)S(1)}, bf16[128,1536]{1,0:T(8,128)(2,1)S(1)}, u32[]{:S(2)}, u32[]{:S(2)}) collective-permute-start(bf16[128,1536]{1,0:T(8,128)(2,1)S(1)} %collective-permute-done.1.refs_2_.g2), channel_id=1, source_target_pairs={{0,1},{1,0},{2,3},{3,2},{4,5},{5,4},{6,7},{7,6},{8,9},{9,8},{10,11... | collective-permute-start | bytes 1179656 | tf_op jit(solution)/shard_map/ppermute | solution.py:327
  120.5 5.9 %collective-permute-start.4 = (bf16[128,1024]{1,0:T(8,128)(2,1)S(1)}, bf16[128,1024]{1,0:T(8,128)(2,1)S(1)}, u32[]{:S(2)}, u32[]{:S(2)}) collective-permute-start(bf16[128,1024]{1,0:T(8,128)(2,1)S(1)} %copy-done.1), channel_id=1, source_target_pairs={{0,1},{1,0},{2,3},{3,2},{4,5},{5,4},{6,7},{7,6},{8,9},{9,8},{10,11... | collective-permute-start | bytes 786440 | tf_op jit(solution)/shard_map/ppermute | solution.py:327
  120.5 5.9 %collective-permute-start.11 = (bf16[2,2,128,128]{3,2,1,0:T(8,128)(2,1)S(1)}, bf16[2,2,128,128]{3,2,1,0:T(8,128)(2,1)S(1)}, u32[]{:S(2)}, u32[]{:S(2)}) collective-permute-start(bf16[2,2,128,128]{3,2,1,0:T(8,128)(2,1)S(1)} %get-tuple-element.48), channel_id=1, source_target_pairs={{0,12},{1,13},{2,14},{3,15},{4,0},{5,1},{6,2},{7,3},{8,4},{9,5},{1... | collective-permute-start | bytes 393224 | tf_op jit(solution)/shard_map/ppermute | solution.py:327
  126.4 16.4 %collective-permute-start.27 = (bf16[2,256,256]{2,1,0:T(8,128)(2,1)S(1)}, bf16[2,256,256]{2,1,0:T(8,128)(2,1)S(1)}, u32[]{:S(2)}, u32[]{:S(2)}) collective-permute-start(bf16[2,256,256]{2,1,0:T(8,128)(2,1)S(1)} %collective-permute-done.26.refs_1_), channel_id=1, source_target_pairs={{0,4},{1,5},{2,6},{3,7},{4,8},{5,9},{6,10},{7,11},{8,12},{9,13},{1... | collective-permute-start | bytes 786440 | tf_op jit(solution)/shard_map/ppermute | solution.py:327
  126.4 14.0 %copy-start.5 = (bf16[16,256,128]{2,1,0:T(8,128)(2,1)S(1)}, bf16[16,256,128]{2,1,0:T(8,128)(2,1)}, u32[]{:S(2)}) copy-start(bf16[16,256,128]{2,1,0:T(8,128)(2,1)} %constant.45.clone.refs_8_) | copy-start | bytes 3145732
  126.4 14.0 %copy-start.6 = (bf16[16,256,128]{2,1,0:T(8,128)(2,1)S(1)}, bf16[16,256,128]{2,1,0:T(8,128)(2,1)}, u32[]{:S(2)}) copy-start(bf16[16,256,128]{2,1,0:T(8,128)(2,1)} %constant.46.clone.refs_9_) | copy-start | bytes 3145732
  129.2 9.8 %collective-permute-start.18 = (bf16[256,128]{1,0:T(8,128)(2,1)S(1)}, bf16[256,128]{1,0:T(8,128)(2,1)S(1)}, u32[]{:S(2)}, u32[]{:S(2)}) collective-permute-start(bf16[256,128]{1,0:T(8,128)(2,1)S(1)} %get-tuple-element.52), channel_id=1, source_target_pairs={{0,4},{1,5},{2,6},{3,7},{4,8},{5,9},{6,10},{7,11},{8,12},{9,13},{1... | collective-permute-start | bytes 196616 | tf_op jit(solution)/shard_map/ppermute | solution.py:327
  129.2 11.2 %collective-permute-start.19 = (bf16[256,128]{1,0:T(8,128)(2,1)S(1)}, bf16[256,128]{1,0:T(8,128)(2,1)S(1)}, u32[]{:S(2)}, u32[]{:S(2)}) collective-permute-start(bf16[256,128]{1,0:T(8,128)(2,1)S(1)} %get-tuple-element.53), channel_id=1, source_target_pairs={{0,8},{1,9},{2,10},{3,11},{4,12},{5,13},{6,14},{7,15},{8,0},{9,1},... | collective-permute-start | bytes 196616 | tf_op jit(solution)/shard_map/ppermute | solution.py:327
  133.6 6.8 %collective-permute-start.20 = (bf16[256,128]{1,0:T(8,128)(2,1)S(1)}, bf16[256,128]{1,0:T(8,128)(2,1)S(1)}, u32[]{:S(2)}, u32[]{:S(2)}) collective-permute-start(bf16[256,128]{1,0:T(8,128)(2,1)S(1)} %get-tuple-element.54), channel_id=1, source_target_pairs={{0,12},{1,13},{2,14},{3,15},{4,0},{5,1},{6,2},{7,3},{8,4},{9,5},{1... | collective-permute-start | bytes 196616 | tf_op jit(solution)/shard_map/ppermute | solution.py:327
  142.8 14.3 %collective-permute-start.28 = (bf16[2,256,256]{2,1,0:T(8,128)(2,1)S(1)}, bf16[2,256,256]{2,1,0:T(8,128)(2,1)S(1)}, u32[]{:S(2)}, u32[]{:S(2)}) collective-permute-start(bf16[2,256,256]{2,1,0:T(8,128)(2,1)S(1)} %collective-permute-done.27.refs_2_), channel_id=1, source_target_pairs={{0,4},{1,5},{2,6},{3,7},{4,8},{5,9},{6,10},{7,11},{8,12},{9,13},{1... | collective-permute-start | bytes 786440 | tf_op jit(solution)/shard_map/ppermute | solution.py:327
  144.8 10.7 %collective-permute-start.21 = (bf16[256,128]{1,0:T(8,128)(2,1)S(1)}, bf16[256,128]{1,0:T(8,128)(2,1)S(1)}, u32[]{:S(2)}, u32[]{:S(2)}) collective-permute-start(bf16[256,128]{1,0:T(8,128)(2,1)S(1)} %get-tuple-element.56), channel_id=1, source_target_pairs={{0,4},{1,5},{2,6},{3,7},{4,8},{5,9},{6,10},{7,11},{8,12},{9,13},{1... | collective-permute-start | bytes 196616 | tf_op jit(solution)/shard_map/ppermute | solution.py:327
  144.8 12.3 %collective-permute-start.22 = (bf16[256,128]{1,0:T(8,128)(2,1)S(1)}, bf16[256,128]{1,0:T(8,128)(2,1)S(1)}, u32[]{:S(2)}, u32[]{:S(2)}) collective-permute-start(bf16[256,128]{1,0:T(8,128)(2,1)S(1)} %get-tuple-element.57), channel_id=1, source_target_pairs={{0,8},{1,9},{2,10},{3,11},{4,12},{5,13},{6,14},{7,15},{8,0},{9,1},... | collective-permute-start | bytes 196616 | tf_op jit(solution)/shard_map/ppermute | solution.py:327
  147.3 9.9 %collective-permute-start.23 = (bf16[256,128]{1,0:T(8,128)(2,1)S(1)}, bf16[256,128]{1,0:T(8,128)(2,1)S(1)}, u32[]{:S(2)}, u32[]{:S(2)}) collective-permute-start(bf16[256,128]{1,0:T(8,128)(2,1)S(1)} %get-tuple-element.58), channel_id=1, source_target_pairs={{0,12},{1,13},{2,14},{3,15},{4,0},{5,1},{6,2},{7,3},{8,4},{9,5},{1... | collective-permute-start | bytes 196616 | tf_op jit(solution)/shard_map/ppermute | solution.py:327
  158.7 3.3 %collective-permute-start.29 = (bf16[4,256,256]{2,1,0:T(8,128)(2,1)}, bf16[4,256,256]{2,1,0:T(8,128)(2,1)}, u32[]{:S(2)}, u32[]{:S(2)}) collective-permute-start(bf16[4,256,256]{2,1,0:T(8,128)(2,1)} %get-tuple-element.68), channel_id=1, source_target_pairs={{0,1},{1,0},{2,3},{3,2},{4,5},{5,4},{6,7},{7,6},{8,9},{9,8},{10,11... | collective-permute-start | bytes 1572872 | tf_op jit(solution)/shard_map/ppermute | solution.py:327
  160.2 1.7 collective-permute-start.24
  164.5 9.2 %collective-permute-start.32 = (bf16[128,1024]{1,0:T(8,128)(2,1)S(1)}, bf16[128,1024]{1,0:T(8,128)(2,1)S(1)}, u32[]{:S(2)}, u32[]{:S(2)}) collective-permute-start(bf16[128,1024]{1,0:T(8,128)(2,1)S(1)} %get-tuple-element.72), channel_id=1, source_target_pairs={{0,2},{1,3},{2,0},{3,1},{4,6},{5,7},{6,4},{7,5},{8,10},{9,11},{10,... | collective-permute-start | bytes 786440 | tf_op jit(solution)/shard_map/ppermute | solution.py:327
  165.8 13.9 %collective-permute-start.31 = (bf16[128,1024]{1,0:T(8,128)(2,1)S(1)}, bf16[128,1024]{1,0:T(8,128)(2,1)S(1)}, u32[]{:S(2)}, u32[]{:S(2)}) collective-permute-start(bf16[128,1024]{1,0:T(8,128)(2,1)S(1)} %get-tuple-element.71), channel_id=1, source_target_pairs={{0,16},{1,17},{2,18},{3,19},{4,20},{5,21},{6,22},{7,23},{8,24},{9,... | collective-permute-start | bytes 786440 | tf_op jit(solution)/shard_map/ppermute | solution.py:327
  166.3 13.4 %collective-permute-start.30 = (bf16[128,1024]{1,0:T(8,128)(2,1)S(1)}, bf16[128,1024]{1,0:T(8,128)(2,1)S(1)}, u32[]{:S(2)}, u32[]{:S(2)}) collective-permute-start(bf16[128,1024]{1,0:T(8,128)(2,1)S(1)} %get-tuple-element.70), channel_id=1, source_target_pairs={{0,18},{1,19},{2,16},{3,17},{4,22},{5,23},{6,20},{7,21},{8,26},{9,... | collective-permute-start | bytes 786440 | tf_op jit(solution)/shard_map/ppermute | solution.py:327

commit v4 on v3

--- a/solution.py
+++ b/solution.py
@@ -64,7 +64,7 @@
 
 
 def prologue(where, tokens, key, query, value, out, filt, *refs):
-    own_v, away_v, own_o, away_o, to_x, to_y, own, away_f, sem = refs
+    own_v, away_v, own_o, away_o, m1, m2, m3, own, away_f, sem = refs
     y, x = where[0], where[1]
 
     def lanes(p):
@@ -73,12 +73,13 @@
         return pl.ds(pl.multiple_of(row * 512 + column * 256, 256), 256)
 
     moves = [(value.at[:, lanes(0)], own_v), (value.at[:, lanes(1)], away_v)]
+    moves.append((filt.at[:, :, :, lanes(1)], away_f))
+    for p, message in enumerate((own, m1, m2, m3)):
+        moves.append((key.at[:, lanes(p)], message.at[:, pl.ds(0, 256)]))
+        moves.append((query.at[:, lanes(p)], message.at[:, pl.ds(256, 256)]))
+        if p:
+            moves.append((tokens, message.at[:, pl.ds(512, 1024)]))
     moves += [(out.at[:, lanes(0)], own_o), (out.at[:, lanes(1)], away_o)]
-    moves.append((filt.at[:, :, :, lanes(1)], away_f))
-    moves += [(tokens, m.at[:, pl.ds(512, 1024)]) for m in (to_x, to_y)]
-    for p, target, base in ((0, own, 0), (1, to_x, 0), (2, to_y, 0), (3, to_x, 1536)):
-        moves.append((key.at[:, lanes(p)], target.at[:, pl.ds(base, 256)]))
-        moves.append((query.at[:, lanes(p)], target.at[:, pl.ds(base + 256, 256)]))
     copies = [pltpu.make_async_copy(a, b, sem.at[i]) for i, (a, b) in enumerate(moves)]
     for copy in copies:
         copy.start()
@@ -133,7 +134,7 @@
 
     for p in range(4):
         rows = pl.ds(p * 128, 128)
-        gate = mine[p][:, 1536:1792] if p == 3 else (mine[p] if p else gates)[:, 0:256]
+        gate = (mine[p] if p else gates)[:, 0:256]
         value = acc[rows, :].astype(BF16).astype(F32)
         drive[rows, :] = (gate.astype(F32) * value).astype(BF16)
     low = low_lanes((256, 128))
@@ -270,7 +271,7 @@
             rows = pl.ds(p * 128, 128)
             own = parts[p // 2][(p % 2) * 128 : (p % 2) * 128 + 128]
             direct = skip[:, lanes] * drive[rows, lanes].astype(F32)
-            query = gate[:, pl.ds((1792 if p == 3 else 256) + j * 128, 128)].astype(F32)
+            query = gate[:, pl.ds(256 + j * 128, 128)].astype(F32)
             gated[rows, lanes] = (query * (own + direct)).astype(BF16)
 
 
@@ -344,21 +345,19 @@
     shape = jax.ShapeDtypeStruct
     block, square = shape((256, 128), BF16), shape((256, 256), BF16)
     inside = pl.BlockSpec(memory_space=pltpu.MemorySpace.HBM)
-    laid = [square] * 4 + [shape((128, w), BF16) for w in (2048, 1536, 512)]
+    laid = [square] * 4 + [shape((128, w), BF16) for w in (1536, 1536, 1536, 512)]
     laid.append(shape((2, 2, 128, 256), BF16))
-    own_v, away_v, own_o, away_o, message_x, message_y, gates, away_f = pl.pallas_call(
+    own_v, away_v, own_o, away_o, *messages, gates, away_f = pl.pallas_call(
         prologue,
         out_shape=laid,
         in_specs=[pl.BlockSpec(memory_space=pltpu.SMEM)] + [inside] * 6,
-        out_specs=[inside] * 8,
-        scratch_shapes=[pltpu.SemaphoreType.DMA((15,))],
-        compiler_params=pltpu.CompilerParams(vmem_limit_bytes=62 * 1024 * 1024),
+        out_specs=[pl.BlockSpec(memory_space=pltpu.VMEM)] * 9,
+        scratch_shapes=[pltpu.SemaphoreType.DMA((16,))],
+        compiler_params=pltpu.CompilerParams(vmem_limit_bytes=61 * 1024 * 1024),
     )(where, tokens, gate_k, gate_q, w_value, w_out, filter_spectrum)
     ring = [own_v, to_x(away_v)]
-    from_x = to_peer(message_x, 1)
-    from_y = to_peer(message_y, 2)
+    received = [to_peer(messages[p - 1], p) for p in (1, 2, 3)]
     ring += [to_z(ring[0], 1), to_z(ring[1], 1)]
-    received = [from_x, from_y, to_peer(after(from_x, from_y, ring[2]), 2)]
     got = to_x(away_f)
     filters = in_vmem(
         pack_filter,
@@ -370,9 +369,9 @@
     mine = [tokens] + received
     other = [to_core(m) for m in mine]
     ring += [to_z(ring[2], 1), to_z(ring[3], 1)]
-    ring += [to_z(ring[4], 1), to_z(ring[5], 1)]
+    ring += [to_z(after(ring[4], *received[:2]), 1), to_z(ring[5], 1)]
     pair = jnp.stack([own_o, to_x(after(away_o, got))])
-    hops = [after(pair, ring[4], ring[5])]
+    hops = [after(pair, ring[4], ring[5], received[2])]
     hops.append(to_z(hops[0], 1))
     hops.append(to_z(after(hops[1], ring[6], ring[7]), 1))
     gates = after(gates, *filters)

time: 181 us -> 112 us (0.62)
  Pallas kernels: 68.3 us -> 14.5 us
  waiting for transfers between devices: 73.5 us -> 53.7 us
  starting transfers between devices: 36.3 us -> 41.2 us
    pallas_call x1, Pallas kernels: 57.6 us -> 3.81 us  [planes(): pl.pallas_call(prologue, out_shape=laid, in_specs=[pl.BlockSpec(memory_sp...]
    ppermute x33, waiting for transfers between devices: 73.5 us -> 53.7 us  [permute(): return lax.ppermute(values, AXES, pairs)]
    ppermute x33, starting transfers between devices: 36.3 us -> 41.2 us  [permute(): return lax.ppermute(values, AXES, pairs)]
  transfers between devices with their start and end apart: 33 -> 33, of which waited for: 17 -> 13; matrix products, arithmetic and copies ran while one was open for 0% -> 1% of each run, Pallas kernels for 4% -> 6%
where the time goes in v4:
time: 112 us
  waiting for transfers between devices  53.7 us (48%)
  starting transfers between devices  41.2 us (37%)
  Pallas kernels  14.5 us (13%)
  other arithmetic  1.53 us (1%)
    ppermute x33, waiting for transfers between devices, permute(): return lax.ppermute(values, AXES, pairs)  53.7 us
    ppermute x33, starting transfers between devices, permute(): return lax.ppermute(values, AXES, pairs)  41.2 us
    pallas_call x6, Pallas kernels, call(): pl.pallas_call(kernel, out_shape=out_shape, in_specs=specs, out_specs=jax...  10.7 us
    pallas_call x1, Pallas kernels, planes(): pl.pallas_call(prologue, out_shape=laid, in_specs=[pl.BlockSpec(memory_sp...  3.81 us
  transfers between devices with their start and end apart: 33, of which 13 were waited for; matrix products, arithmetic and copies ran while one was open for 1% of the time, Pallas kernels for 6%

profile of v4, /device:TPU:0, one launch (start us, length us, event | category | flops | bytes accessed | tf_op | source)
XLA Modules:
  0.0 111.9 jit_solution(8435539888568528759)
XLA Ops:
  0.0 0.7 pad_add_fusion.where
  0.7 3.8 %shard_map.91 = (bf16[256,256]{1,0:T(8,128)(2,1)}, bf16[256,256]{1,0:T(8,128)(2,1)}, bf16[256,256]{1,0:T(8,128)(2,1)}, bf16[256,256]{1,0:T(8,128)(2,1)}, bf16[12...) custom-call(s32[4]{0:T(128)} %pad_add_fusion.where, ...), custom_call_target="tpu_custom_call" | custom-call | tf_op jit(solution)/shard_map/pallas_call | solution.py:350
  4.5 3.0 %collective-permute-start.7 = (bf16[2,2,128,256]{3,2,1,0:T(8,128)(2,1)}, bf16[2,2,128,256]{3,2,1,0:T(8,128)(2,1)S(1)}, u32[]{:S(2)}, u32[]{:S(2)}) collective-permute-start(bf16[2,2,128,256]{3,2,1,0:T(8,128)(2,1)} %get-tuple-element.44), channel_id=1, source_target_pairs={{0,2},{1,3},{2,0},{3,1},{4,6},{5,7},{6,4},{7,5},{8,10},{9,11},{10,... | collective-permute-start | bytes 786440 | tf_op jit(solution)/shard_map/ppermute | solution.py:328
  7.5 0.1 collective-permute-start.11
  7.6 1.9 %collective-permute-start = (bf16[128,1536]{1,0:T(8,128)(2,1)}, bf16[128,1536]{1,0:T(8,128)(2,1)S(1)}, u32[]{:S(2)}, u32[]{:S(2)}) collective-permute-start(bf16[128,1536]{1,0:T(8,128)(2,1)} %get-tuple-element.40), channel_id=1, source_target_pairs={{0,2},{1,3},{2,0},{3,1},{4,6},{5,7},{6,4},{7,5},{8,10},{9,11},{10,... | collective-permute-start | bytes 1179656 | tf_op jit(solution)/shard_map/ppermute | solution.py:328
  9.5 1.5 %collective-permute-start.1 = (bf16[128,1536]{1,0:T(8,128)(2,1)}, bf16[128,1536]{1,0:T(8,128)(2,1)S(1)}, u32[]{:S(2)}, u32[]{:S(2)}) collective-permute-start(bf16[128,1536]{1,0:T(8,128)(2,1)} %get-tuple-element.41), channel_id=1, source_target_pairs={{0,16},{1,17},{2,18},{3,19},{4,20},{5,21},{6,22},{7,23},{8,24},{9,... | collective-permute-start | bytes 1179656 | tf_op jit(solution)/shard_map/ppermute | solution.py:328
  11.1 1.6 %collective-permute-start.12 = (bf16[256,256]{1,0:T(8,128)(2,1)}, bf16[256,256]{1,0:T(8,128)(2,1)S(1)}, u32[]{:S(2)}, u32[]{:S(2)}) collective-permute-start(bf16[256,256]{1,0:T(8,128)(2,1)} %get-tuple-element.50.refs_9_), channel_id=1, source_target_pairs={{0,4},{1,5},{2,6},{3,7},{4,8},{5,9},{6,10},{7,11},{8,12},{9,13},{1... | collective-permute-start | bytes 393224 | tf_op jit(solution)/shard_map/ppermute | solution.py:328
  12.6 5.0 %collective-permute-done.11.refs_10_ = bf16[256,256]{1,0:T(8,128)(2,1)S(1)} collective-permute-done((bf16[256,256]{1,0:T(8,128)(2,1)}, bf16[256,256]{1,0:T(8,128)(2,1)S(1)}, u32[]{:S(2)}, u32[]{:S(2)}) %collective-permute-start.11) | collective-permute-done | bytes 131104 | tf_op jit(solution)/shard_map/ppermute | solution.py:328
  17.7 3.0 %collective-permute-start.2 = (bf16[128,1536]{1,0:T(8,128)(2,1)}, bf16[128,1536]{1,0:T(8,128)(2,1)S(1)}, u32[]{:S(2)}, u32[]{:S(2)}) collective-permute-start(bf16[128,1536]{1,0:T(8,128)(2,1)} %get-tuple-element.42), channel_id=1, source_target_pairs={{0,18},{1,19},{2,16},{3,17},{4,22},{5,23},{6,20},{7,21},{8,26},{9,... | collective-permute-start | bytes 1179656 | tf_op jit(solution)/shard_map/ppermute | solution.py:328
  20.7 1.6 %collective-permute-start.13 = (bf16[256,256]{1,0:T(8,128)(2,1)S(1)}, bf16[256,256]{1,0:T(8,128)(2,1)S(1)}, u32[]{:S(2)}, u32[]{:S(2)}) collective-permute-start(bf16[256,256]{1,0:T(8,128)(2,1)S(1)} %collective-permute-done.11.refs_10_), channel_id=1, source_target_pairs={{0,4},{1,5},{2,6},{3,7},{4,8},{5,9},{6,10},{7,11},{8,12},{9,13},{1... | collective-permute-start | bytes 393224 | tf_op jit(solution)/shard_map/ppermute | solution.py:328
  22.3 0.0 collective-permute-done.7.near
  22.3 1.6 %collective-permute-start.14 = (bf16[256,256]{1,0:T(8,128)(2,1)S(1)}, bf16[256,256]{1,0:T(8,128)(2,1)S(1)}, u32[]{:S(2)}, u32[]{:S(2)}) collective-permute-start(bf16[256,256]{1,0:T(8,128)(2,1)S(1)} %collective-permute-done.12.refs_11_), channel_id=1, source_target_pairs={{0,4},{1,5},{2,6},{3,7},{4,8},{5,9},{6,10},{7,11},{8,12},{9,13},{1... | collective-permute-start | bytes 393224 | tf_op jit(solution)/shard_map/ppermute | solution.py:328
  23.9 3.6 %collective-permute-done.13.refs_12_ = bf16[256,256]{1,0:T(8,128)(2,1)S(1)} collective-permute-done((bf16[256,256]{1,0:T(8,128)(2,1)S(1)}, bf16[256,256]{1,0:T(8,128)(2,1)S(1)}, u32[]{:S(2)}, u32[]{:S(2)}) %collective-permute-start.13) | collective-permute-done | bytes 131104 | tf_op jit(solution)/shard_map/ppermute | solution.py:328
  27.5 0.5 collective-permute-start.25
  28.0 1.0 collective-permute-done.14.refs_13_
  29.0 0.4 collective-permute-start.15
  29.5 0.9 shard_map.92
  30.4 1.9 %collective-permute-start.8 = (bf16[2,2,128,128]{3,2,1,0:T(8,128)(2,1)S(1)}, bf16[2,2,128,128]{3,2,1,0:T(8,128)(2,1)S(1)}, u32[]{:S(2)}, u32[]{:S(2)}) collective-permute-start(bf16[2,2,128,128]{3,2,1,0:T(8,128)(2,1)S(1)} %get-tuple-element.46), channel_id=1, source_target_pairs={{0,4},{1,5},{2,6},{3,7},{4,8},{5,9},{6,10},{7,11},{8,12},{9,13},{1... | collective-permute-start | bytes 393224 | tf_op jit(solution)/shard_map/ppermute | solution.py:328
  32.3 0.0 collective-permute-done.1.refs_2_.g2
  32.3 2.1 %collective-permute-start.9 = (bf16[2,2,128,128]{3,2,1,0:T(8,128)(2,1)S(1)}, bf16[2,2,128,128]{3,2,1,0:T(8,128)(2,1)S(1)}, u32[]{:S(2)}, u32[]{:S(2)}) collective-permute-start(bf16[2,2,128,128]{3,2,1,0:T(8,128)(2,1)S(1)} %get-tuple-element.47), channel_id=1, source_target_pairs={{0,8},{1,9},{2,10},{3,11},{4,12},{5,13},{6,14},{7,15},{8,0},{9,1},... | collective-permute-start | bytes 393224 | tf_op jit(solution)/shard_map/ppermute | solution.py:328
  34.4 2.1 %collective-permute-done.25 = bf16[256,256]{1,0:T(8,128)(2,1)S(1)} collective-permute-done((bf16[256,256]{1,0:T(8,128)(2,1)}, bf16[256,256]{1,0:T(8,128)(2,1)S(1)}, u32[]{:S(2)}, u32[]{:S(2)}) %collective-permute-start.25) | collective-permute-done | bytes 131104 | tf_op jit(solution)/shard_map/ppermute | solution.py:328
  36.5 1.8 %collective-permute-start.16 = (bf16[256,256]{1,0:T(8,128)(2,1)S(1)}, bf16[256,256]{1,0:T(8,128)(2,1)S(1)}, u32[]{:S(2)}, u32[]{:S(2)}) collective-permute-start(bf16[256,256]{1,0:T(8,128)(2,1)S(1)} %collective-permute-done.14.refs_13_), channel_id=1, source_target_pairs={{0,4},{1,5},{2,6},{3,7},{4,8},{5,9},{6,10},{7,11},{8,12},{9,13},{1... | collective-permute-start | bytes 393224 | tf_op jit(solution)/shard_map/ppermute | solution.py:328
  38.4 0.0 collective-permute-done.2.refs_3_.g3
  38.4 1.6 %collective-permute-start.26 = (bf16[2,256,256]{2,1,0:T(8,128)(2,1)S(1)}, bf16[2,256,256]{2,1,0:T(8,128)(2,1)S(1)}, u32[]{:S(2)}, u32[]{:S(2)}) collective-permute-start(bf16[2,256,256]{2,1,0:T(8,128)(2,1)S(1)} %pad_maximum_fusion.refs_0_), channel_id=1, source_target_pairs={{0,4},{1,5},{2,6},{3,7},{4,8},{5,9},{6,10},{7,11},{8,12},{9,13},{1... | collective-permute-start | bytes 786440 | tf_op jit(solution)/shard_map/ppermute | solution.py:328
  40.0 1.6 %collective-permute-start.17 = (bf16[256,256]{1,0:T(8,128)(2,1)S(1)}, bf16[256,256]{1,0:T(8,128)(2,1)S(1)}, u32[]{:S(2)}, u32[]{:S(2)}) collective-permute-start(bf16[256,256]{1,0:T(8,128)(2,1)S(1)} %collective-permute-done.15.refs_14_), channel_id=1, source_target_pairs={{0,4},{1,5},{2,6},{3,7},{4,8},{5,9},{6,10},{7,11},{8,12},{9,13},{1... | collective-permute-start | bytes 393224 | tf_op jit(solution)/shard_map/ppermute | solution.py:328
  41.6 10.6 %collective-permute-done.9.refs_6_ = bf16[2,2,128,128]{3,2,1,0:T(8,128)(2,1)S(1)} collective-permute-done((bf16[2,2,128,128]{3,2,1,0:T(8,128)(2,1)S(1)}, bf16[2,2,128,128]{3,2,1,0:T(8,128)(2,1)S(1)}, u32[]{:S(2)}, u32[]{:S(2)}) %collective-permute-start.9) | collective-permute-done | bytes 131104 | tf_op jit(solution)/shard_map/ppermute | solution.py:328
  52.2 0.0 collective-permute-start.5
  52.2 0.0 collective-permute-done.16.refs_15_
  52.2 0.5 collective-permute-start.6
  52.7 0.1 collective-permute-start.3
  52.8 0.0 collective-permute-done.26.refs_1_
  52.8 0.5 collective-permute-start.10
  53.3 5.3 %collective-permute-done.10.refs_7_ = bf16[2,2,128,128]{3,2,1,0:T(8,128)(2,1)S(1)} collective-permute-done((bf16[2,2,128,128]{3,2,1,0:T(8,128)(2,1)S(1)}, bf16[2,2,128,128]{3,2,1,0:T(8,128)(2,1)S(1)}, u32[]{:S(2)}, u32[]{:S(2)}) %collective-permute-start.10) | collective-permute-done | bytes 131104 | tf_op jit(solution)/shard_map/ppermute | solution.py:328
  58.6 0.0 collective-permute-done.3.refs_4_
  58.6 0.0 collective-permute-done.5.refs_6_
  58.7 0.0 collective-permute-done.6.refs_7_
  58.7 2.7 %shard_map.93 = (bf16[512,256]{1,0:T(8,128)(2,1)S(1)}, bf16[256,128]{1,0:T(8,128)(2,1)S(1)}, bf16[256,128]{1,0:T(8,128)(2,1)S(1)}, bf16[256,128]{1,0:T(8,128)(2,1)S(1)}, bf16[256,128]{1,0:T(8,128)(2,1)S(1)}) custom-call(s32[4]{0:T(128)S(1)} %copy-done.4, bf16[128,1024]{1,0:T(8,128)(2,1)S(1)} %copy-done.1, ...), custom_call_target="tpu_custom_call" | custom-call | flops 536870912 | bytes 4194304 | tf_op jit(solution)/shard_map/pallas_call | solution.py:38
  61.4 0.2 collective-permute-start.18
  61.6 4.2 %collective-permute-start.19 = (bf16[256,128]{1,0:T(8,128)(2,1)S(1)}, bf16[256,128]{1,0:T(8,128)(2,1)S(1)}, u32[]{:S(2)}, u32[]{:S(2)}) collective-permute-start(bf16[256,128]{1,0:T(8,128)(2,1)S(1)} %get-tuple-element.55), channel_id=1, source_target_pairs={{0,8},{1,9},{2,10},{3,11},{4,12},{5,13},{6,14},{7,15},{8,0},{9,1},... | collective-permute-start | bytes 196616 | tf_op jit(solution)/shard_map/ppermute | solution.py:328
  65.8 1.4 %collective-permute-start.20 = (bf16[256,128]{1,0:T(8,128)(2,1)S(1)}, bf16[256,128]{1,0:T(8,128)(2,1)S(1)}, u32[]{:S(2)}, u32[]{:S(2)}) collective-permute-start(bf16[256,128]{1,0:T(8,128)(2,1)S(1)} %get-tuple-element.56), channel_id=1, source_target_pairs={{0,12},{1,13},{2,14},{3,15},{4,0},{5,1},{6,2},{7,3},{8,4},{9,5},{1... | collective-permute-start | bytes 196616 | tf_op jit(solution)/shard_map/ppermute | solution.py:328
  67.2 3.9 %collective-permute-done.18.refs_1_ = bf16[256,128]{1,0:T(8,128)(2,1)S(1)} collective-permute-done((bf16[256,128]{1,0:T(8,128)(2,1)S(1)}, bf16[256,128]{1,0:T(8,128)(2,1)S(1)}, u32[]{:S(2)}, u32[]{:S(2)}) %collective-permute-start.18) | collective-permute-done | bytes 65568 | tf_op jit(solution)/shard_map/ppermute | solution.py:328
  71.1 1.5 %collective-permute-done.19.refs_2_ = bf16[256,128]{1,0:T(8,128)(2,1)S(1)} collective-permute-done((bf16[256,128]{1,0:T(8,128)(2,1)S(1)}, bf16[256,128]{1,0:T(8,128)(2,1)S(1)}, u32[]{:S(2)}, u32[]{:S(2)}) %collective-permute-start.19) | collective-permute-done | bytes 65568 | tf_op jit(solution)/shard_map/ppermute | solution.py:328
  72.6 0.0 collective-permute-done.20.refs_3_
  72.6 2.4 %shard_map.94 = (bf16[256,128]{1,0:T(8,128)(2,1)S(1)}, bf16[256,128]{1,0:T(8,128)(2,1)S(1)}, bf16[256,128]{1,0:T(8,128)(2,1)S(1)}, bf16[256,128]{1,0:T(8,128)(2,1)S(1)}) custom-call(s32[4]{0:T(128)S(1)} %copy-done.4, bf16[256,128]{1,0:T(8,128)(2,1)S(1)} %get-tuple-element.53.refs_0_, bf16[256,128]{1,0:T(8,128)(2,1)S(1)} %collective-permute-done.18.refs_1_, ...), custom_call_target="tpu_custom_call" | custom-call | flops 1073741824 | bytes 5242880 | tf_op jit(solution)/shard_map/pallas_call | solution.py:38
  75.0 0.0 collective-permute-done.27.refs_2_
  75.0 1.9 %collective-permute-start.28 = (bf16[2,256,256]{2,1,0:T(8,128)(2,1)S(1)}, bf16[2,256,256]{2,1,0:T(8,128)(2,1)S(1)}, u32[]{:S(2)}, u32[]{:S(2)}) collective-permute-start(bf16[2,256,256]{2,1,0:T(8,128)(2,1)S(1)} %collective-permute-done.27.refs_2_), channel_id=1, source_target_pairs={{0,4},{1,5},{2,6},{3,7},{4,8},{5,9},{6,10},{7,11},{8,12},{9,13},{1... | collective-permute-start | bytes 786440 | tf_op jit(solution)/shard_map/ppermute | solution.py:328
  77.0 0.1 collective-permute-start.21
  77.0 2.5 %collective-permute-start.22 = (bf16[256,128]{1,0:T(8,128)(2,1)S(1)}, bf16[256,128]{1,0:T(8,128)(2,1)S(1)}, u32[]{:S(2)}, u32[]{:S(2)}) collective-permute-start(bf16[256,128]{1,0:T(8,128)(2,1)S(1)} %get-tuple-element.59), channel_id=1, source_target_pairs={{0,8},{1,9},{2,10},{3,11},{4,12},{5,13},{6,14},{7,15},{8,0},{9,1},... | collective-permute-start | bytes 196616 | tf_op jit(solution)/shard_map/ppermute | solution.py:328
  79.5 1.3 %collective-permute-start.23 = (bf16[256,128]{1,0:T(8,128)(2,1)S(1)}, bf16[256,128]{1,0:T(8,128)(2,1)S(1)}, u32[]{:S(2)}, u32[]{:S(2)}) collective-permute-start(bf16[256,128]{1,0:T(8,128)(2,1)S(1)} %get-tuple-element.60), channel_id=1, source_target_pairs={{0,12},{1,13},{2,14},{3,15},{4,0},{5,1},{6,2},{7,3},{8,4},{9,5},{1... | collective-permute-start | bytes 196616 | tf_op jit(solution)/shard_map/ppermute | solution.py:328
  80.8 6.8 %collective-permute-done.21.e1 = bf16[256,128]{1,0:T(8,128)(2,1)S(1)} collective-permute-done((bf16[256,128]{1,0:T(8,128)(2,1)S(1)}, bf16[256,128]{1,0:T(8,128)(2,1)S(1)}, u32[]{:S(2)}, u32[]{:S(2)}) %collective-permute-start.21) | collective-permute-done | bytes 65568 | tf_op jit(solution)/shard_map/ppermute | solution.py:328
  87.6 1.8 %collective-permute-done.22.e2 = bf16[256,128]{1,0:T(8,128)(2,1)S(1)} collective-permute-done((bf16[256,128]{1,0:T(8,128)(2,1)S(1)}, bf16[256,128]{1,0:T(8,128)(2,1)S(1)}, u32[]{:S(2)}, u32[]{:S(2)}) %collective-permute-start.22) | collective-permute-done | bytes 65568 | tf_op jit(solution)/shard_map/ppermute | solution.py:328
  89.4 0.0 collective-permute-done.23.e3
  89.4 1.5 %shard_map.96 = (bf16[4,256,256]{2,1,0:T(8,128)(2,1)S(1)}, bf16[4,256,256]{2,1,0:T(8,128)(2,1)}) custom-call(s32[4]{0:T(128)S(1)} %copy-done.4, bf16[2,256,256]{2,1,0:T(8,128)(2,1)S(1)} %pad_maximum_fusion.refs_0_, bf16[2,256,256]{2,1,0:T(8,128)(2,1)S(1)} %collective-permute-done.26.refs_1_, bf16[2,256,256]{2,1,0:T(8,128)(2,1)S(1)} %collective-permute-done.27.refs_2_, ...), custom_call_target="tpu_custom_call" | custom-call | bytes 2097152 | tf_op jit(solution)/shard_map/pallas_call | solution.py:38
  90.9 0.8 dynamic_slice.3
  91.6 0.8 shard_map.95.gated
  92.4 0.6 collective-permute-start.24
  93.0 1.2 %collective-permute-done.24.other = bf16[512,256]{1,0:T(8,128)(2,1)S(1)} collective-permute-done((bf16[512,256]{1,0:T(8,128)(2,1)S(1)}, bf16[512,256]{1,0:T(8,128)(2,1)S(1)}, u32[]{:S(2)}, u32[]{:S(2)}) %collective-permute-start.24) | collective-permute-done | bytes 262176 | tf_op jit(solution)/shard_map/ppermute | solution.py:328
  94.1 2.5 %shard_map.97 = (f32[128,1024]{1,0:T(8,128)S(1)}, bf16[128,1024]{1,0:T(8,128)(2,1)S(1)}, bf16[128,1024]{1,0:T(8,128)(2,1)S(1)}, bf16[128,1024]{1,0:T(8,128)(2,1)S(1)}) custom-call(bf16[512,256]{1,0:T(8,128)(2,1)S(1)} %shard_map.95.gated, bf16[512,256]{1,0:T(8,128)(2,1)S(1)} %collective-permute-done.24.other, ...), custom_call_target="tpu_custom_call" | custom-call | flops 1073741824 | bytes 4194304 | tf_op jit(solution)/shard_map/pallas_call | solution.py:38
  96.7 0.3 collective-permute-start.32
  96.9 1.5 %collective-permute-start.31 = (bf16[128,1024]{1,0:T(8,128)(2,1)S(1)}, bf16[128,1024]{1,0:T(8,128)(2,1)S(1)}, u32[]{:S(2)}, u32[]{:S(2)}) collective-permute-start(bf16[128,1024]{1,0:T(8,128)(2,1)S(1)} %get-tuple-element.73), channel_id=1, source_target_pairs={{0,16},{1,17},{2,18},{3,19},{4,20},{5,21},{6,22},{7,23},{8,24},{9,... | collective-permute-start | bytes 786440 | tf_op jit(solution)/shard_map/ppermute | solution.py:328
  98.5 1.8 %collective-permute-start.30 = (bf16[128,1024]{1,0:T(8,128)(2,1)S(1)}, bf16[128,1024]{1,0:T(8,128)(2,1)S(1)}, u32[]{:S(2)}, u32[]{:S(2)}) collective-permute-start(bf16[128,1024]{1,0:T(8,128)(2,1)S(1)} %get-tuple-element.72), channel_id=1, source_target_pairs={{0,18},{1,19},{2,16},{3,17},{4,22},{5,23},{6,20},{7,21},{8,26},{9,... | collective-permute-start | bytes 786440 | tf_op jit(solution)/shard_map/ppermute | solution.py:328
  100.2 5.6 %collective-permute-done.32 = bf16[128,1024]{1,0:T(8,128)(2,1)S(1)} collective-permute-done((bf16[128,1024]{1,0:T(8,128)(2,1)S(1)}, bf16[128,1024]{1,0:T(8,128)(2,1)S(1)}, u32[]{:S(2)}, u32[]{:S(2)}) %collective-permute-start.32) | collective-permute-done | bytes 262176 | tf_op jit(solution)/shard_map/ppermute | solution.py:328
  105.9 5.1 %collective-permute-done.31 = bf16[128,1024]{1,0:T(8,128)(2,1)S(1)} collective-permute-done((bf16[128,1024]{1,0:T(8,128)(2,1)S(1)}, bf16[128,1024]{1,0:T(8,128)(2,1)S(1)}, u32[]{:S(2)}, u32[]{:S(2)}) %collective-permute-start.31) | collective-permute-done | bytes 262176 | tf_op jit(solution)/shard_map/ppermute | solution.py:328
  111.0 0.8 add_convert_fusion
  (29 shorter events, 0.1 us)
Async XLA Ops:
  0.7 28.8 %copy-start = (bf16[2,2,128,1024]{3,2,1,0:T(8,128)(2,1)S(1)}, bf16[2,2,128,1024]{3,2,1,0:T(8,128)(2,1)}, u32[]{:S(2)}) copy-start(bf16[2,2,128,1024]{3,2,1,0:T(8,128)(2,1)} %filt.3) | copy-start | bytes 3145732
  4.5 17.8 %collective-permute-start.7 = (bf16[2,2,128,256]{3,2,1,0:T(8,128)(2,1)}, bf16[2,2,128,256]{3,2,1,0:T(8,128)(2,1)S(1)}, u32[]{:S(2)}, u32[]{:S(2)}) collective-permute-start(bf16[2,2,128,256]{3,2,1,0:T(8,128)(2,1)} %get-tuple-element.44), channel_id=1, source_target_pairs={{0,2},{1,3},{2,0},{3,1},{4,6},{5,7},{6,4},{7,5},{8,10},{9,11},{10,... | collective-permute-start | bytes 786440 | tf_op jit(solution)/shard_map/ppermute | solution.py:328
  7.5 10.2 %collective-permute-start.11 = (bf16[256,256]{1,0:T(8,128)(2,1)}, bf16[256,256]{1,0:T(8,128)(2,1)S(1)}, u32[]{:S(2)}, u32[]{:S(2)}) collective-permute-start(bf16[256,256]{1,0:T(8,128)(2,1)} %get-tuple-element.51), channel_id=1, source_target_pairs={{0,2},{1,3},{2,0},{3,1},{4,6},{5,7},{6,4},{7,5},{8,10},{9,11},{10,... | collective-permute-start | bytes 393224 | tf_op jit(solution)/shard_map/ppermute | solution.py:328
  7.6 22.8 %collective-permute-start = (bf16[128,1536]{1,0:T(8,128)(2,1)}, bf16[128,1536]{1,0:T(8,128)(2,1)S(1)}, u32[]{:S(2)}, u32[]{:S(2)}) collective-permute-start(bf16[128,1536]{1,0:T(8,128)(2,1)} %get-tuple-element.40), channel_id=1, source_target_pairs={{0,2},{1,3},{2,0},{3,1},{4,6},{5,7},{6,4},{7,5},{8,10},{9,11},{10,... | collective-permute-start | bytes 1179656 | tf_op jit(solution)/shard_map/ppermute | solution.py:328
  9.5 22.8 %collective-permute-start.1 = (bf16[128,1536]{1,0:T(8,128)(2,1)}, bf16[128,1536]{1,0:T(8,128)(2,1)S(1)}, u32[]{:S(2)}, u32[]{:S(2)}) collective-permute-start(bf16[128,1536]{1,0:T(8,128)(2,1)} %get-tuple-element.41), channel_id=1, source_target_pairs={{0,16},{1,17},{2,18},{3,19},{4,20},{5,21},{6,22},{7,23},{8,24},{9,... | collective-permute-start | bytes 1179656 | tf_op jit(solution)/shard_map/ppermute | solution.py:328
  11.1 9.6 %collective-permute-start.12 = (bf16[256,256]{1,0:T(8,128)(2,1)}, bf16[256,256]{1,0:T(8,128)(2,1)S(1)}, u32[]{:S(2)}, u32[]{:S(2)}) collective-permute-start(bf16[256,256]{1,0:T(8,128)(2,1)} %get-tuple-element.50.refs_9_), channel_id=1, source_target_pairs={{0,4},{1,5},{2,6},{3,7},{4,8},{5,9},{6,10},{7,11},{8,12},{9,13},{1... | collective-permute-start | bytes 393224 | tf_op jit(solution)/shard_map/ppermute | solution.py:328
  17.7 11.8 %copy-start.4 = (s32[4]{0:T(128)S(1)}, s32[4]{0:T(128)}, u32[]{:S(2)}) copy-start(s32[4]{0:T(128)} %pad_add_fusion.where) | copy-start | bytes 52
  17.7 20.7 %collective-permute-start.2 = (bf16[128,1536]{1,0:T(8,128)(2,1)}, bf16[128,1536]{1,0:T(8,128)(2,1)S(1)}, u32[]{:S(2)}, u32[]{:S(2)}) collective-permute-start(bf16[128,1536]{1,0:T(8,128)(2,1)} %get-tuple-element.42), channel_id=1, source_target_pairs={{0,18},{1,19},{2,16},{3,17},{4,22},{5,23},{6,20},{7,21},{8,26},{9,... | collective-permute-start | bytes 1179656 | tf_op jit(solution)/shard_map/ppermute | solution.py:328
  20.7 6.8 %collective-permute-start.13 = (bf16[256,256]{1,0:T(8,128)(2,1)S(1)}, bf16[256,256]{1,0:T(8,128)(2,1)S(1)}, u32[]{:S(2)}, u32[]{:S(2)}) collective-permute-start(bf16[256,256]{1,0:T(8,128)(2,1)S(1)} %collective-permute-done.11.refs_10_), channel_id=1, source_target_pairs={{0,4},{1,5},{2,6},{3,7},{4,8},{5,9},{6,10},{7,11},{8,12},{9,13},{1... | collective-permute-start | bytes 393224 | tf_op jit(solution)/shard_map/ppermute | solution.py:328
  22.3 6.8 %collective-permute-start.14 = (bf16[256,256]{1,0:T(8,128)(2,1)S(1)}, bf16[256,256]{1,0:T(8,128)(2,1)S(1)}, u32[]{:S(2)}, u32[]{:S(2)}) collective-permute-start(bf16[256,256]{1,0:T(8,128)(2,1)S(1)} %collective-permute-done.12.refs_11_), channel_id=1, source_target_pairs={{0,4},{1,5},{2,6},{3,7},{4,8},{5,9},{6,10},{7,11},{8,12},{9,13},{1... | collective-permute-start | bytes 393224 | tf_op jit(solution)/shard_map/ppermute | solution.py:328
  23.8 14.5 %copy-start.7 = (bf16[256,256]{1,0:T(8,128)(2,1)S(1)}, bf16[256,256]{1,0:T(8,128)(2,1)}, u32[]{:S(2)}) copy-start(bf16[256,256]{1,0:T(8,128)(2,1)} %get-tuple-element.62) | copy-start | bytes 393220
  27.5 9.0 %collective-permute-start.25 = (bf16[256,256]{1,0:T(8,128)(2,1)}, bf16[256,256]{1,0:T(8,128)(2,1)S(1)}, u32[]{:S(2)}, u32[]{:S(2)}) collective-permute-start(bf16[256,256]{1,0:T(8,128)(2,1)} %get-tuple-element.64), channel_id=1, source_target_pairs={{0,2},{1,3},{2,0},{3,1},{4,6},{5,7},{6,4},{7,5},{8,10},{9,11},{10,... | collective-permute-start | bytes 393224 | tf_op jit(solution)/shard_map/ppermute | solution.py:328
  29.0 9.3 %collective-permute-start.15 = (bf16[256,256]{1,0:T(8,128)(2,1)S(1)}, bf16[256,256]{1,0:T(8,128)(2,1)S(1)}, u32[]{:S(2)}, u32[]{:S(2)}) collective-permute-start(bf16[256,256]{1,0:T(8,128)(2,1)S(1)} %collective-permute-done.13.refs_12_), channel_id=1, source_target_pairs={{0,4},{1,5},{2,6},{3,7},{4,8},{5,9},{6,10},{7,11},{8,12},{9,13},{1... | collective-permute-start | bytes 393224 | tf_op jit(solution)/shard_map/ppermute | solution.py:328
  30.4 11.2 %collective-permute-start.8 = (bf16[2,2,128,128]{3,2,1,0:T(8,128)(2,1)S(1)}, bf16[2,2,128,128]{3,2,1,0:T(8,128)(2,1)S(1)}, u32[]{:S(2)}, u32[]{:S(2)}) collective-permute-start(bf16[2,2,128,128]{3,2,1,0:T(8,128)(2,1)S(1)} %get-tuple-element.46), channel_id=1, source_target_pairs={{0,4},{1,5},{2,6},{3,7},{4,8},{5,9},{6,10},{7,11},{8,12},{9,13},{1... | collective-permute-start | bytes 393224 | tf_op jit(solution)/shard_map/ppermute | solution.py:328
  32.3 19.9 %collective-permute-start.9 = (bf16[2,2,128,128]{3,2,1,0:T(8,128)(2,1)S(1)}, bf16[2,2,128,128]{3,2,1,0:T(8,128)(2,1)S(1)}, u32[]{:S(2)}, u32[]{:S(2)}) collective-permute-start(bf16[2,2,128,128]{3,2,1,0:T(8,128)(2,1)S(1)} %get-tuple-element.47), channel_id=1, source_target_pairs={{0,8},{1,9},{2,10},{3,11},{4,12},{5,13},{6,14},{7,15},{8,0},{9,1},... | collective-permute-start | bytes 393224 | tf_op jit(solution)/shard_map/ppermute | solution.py:328
  36.5 15.7 %collective-permute-start.16 = (bf16[256,256]{1,0:T(8,128)(2,1)S(1)}, bf16[256,256]{1,0:T(8,128)(2,1)S(1)}, u32[]{:S(2)}, u32[]{:S(2)}) collective-permute-start(bf16[256,256]{1,0:T(8,128)(2,1)S(1)} %collective-permute-done.14.refs_13_), channel_id=1, source_target_pairs={{0,4},{1,5},{2,6},{3,7},{4,8},{5,9},{6,10},{7,11},{8,12},{9,13},{1... | collective-permute-start | bytes 393224 | tf_op jit(solution)/shard_map/ppermute | solution.py:328
  38.3 14.4 %copy-start.1 = (bf16[128,1024]{1,0:T(8,128)(2,1)S(1)}, bf16[128,1024]{1,0:T(8,128)(2,1)}, u32[]{:S(2)}) copy-start(bf16[128,1024]{1,0:T(8,128)(2,1)} %refs_0_.1) | copy-start | bytes 786436
  38.3 20.4 %copy-start.2 = (bf16[128,512]{1,0:T(8,128)(2,1)S(1)}, bf16[128,512]{1,0:T(8,128)(2,1)}, u32[]{:S(2)}) copy-start(bf16[128,512]{1,0:T(8,128)(2,1)} %get-tuple-element.49.refs_8_.gates) | copy-start | bytes 393220
  38.3 20.4 %copy-start.3 = (bf16[256,256]{1,0:T(8,128)(2,1)S(1)}, bf16[256,256]{1,0:T(8,128)(2,1)}, u32[]{:S(2)}) copy-start(bf16[256,256]{1,0:T(8,128)(2,1)} %get-tuple-element.50.refs_9_) | copy-start | bytes 393220
  38.4 14.4 %collective-permute-start.26 = (bf16[2,256,256]{2,1,0:T(8,128)(2,1)S(1)}, bf16[2,256,256]{2,1,0:T(8,128)(2,1)S(1)}, u32[]{:S(2)}, u32[]{:S(2)}) collective-permute-start(bf16[2,256,256]{2,1,0:T(8,128)(2,1)S(1)} %pad_maximum_fusion.refs_0_), channel_id=1, source_target_pairs={{0,4},{1,5},{2,6},{3,7},{4,8},{5,9},{6,10},{7,11},{8,12},{9,13},{1... | collective-permute-start | bytes 786440 | tf_op jit(solution)/shard_map/ppermute | solution.py:328
  40.0 12.7 %collective-permute-start.17 = (bf16[256,256]{1,0:T(8,128)(2,1)S(1)}, bf16[256,256]{1,0:T(8,128)(2,1)S(1)}, u32[]{:S(2)}, u32[]{:S(2)}) collective-permute-start(bf16[256,256]{1,0:T(8,128)(2,1)S(1)} %collective-permute-done.15.refs_14_), channel_id=1, source_target_pairs={{0,4},{1,5},{2,6},{3,7},{4,8},{5,9},{6,10},{7,11},{8,12},{9,13},{1... | collective-permute-start | bytes 393224 | tf_op jit(solution)/shard_map/ppermute | solution.py:328
  41.6 17.1 %collective-permute-start.4 = (bf16[128,1536]{1,0:T(8,128)(2,1)S(1)}, bf16[128,1536]{1,0:T(8,128)(2,1)S(1)}, u32[]{:S(2)}, u32[]{:S(2)}) collective-permute-start(bf16[128,1536]{1,0:T(8,128)(2,1)S(1)} %collective-permute-done.refs_1_.g1), channel_id=1, source_target_pairs={{0,1},{1,0},{2,3},{3,2},{4,5},{5,4},{6,7},{7,6},{8,9},{9,8},{10,11... | collective-permute-start | bytes 1179656 | tf_op jit(solution)/shard_map/ppermute | solution.py:328
  52.2 6.5 %collective-permute-start.5 = (bf16[128,1536]{1,0:T(8,128)(2,1)S(1)}, bf16[128,1536]{1,0:T(8,128)(2,1)S(1)}, u32[]{:S(2)}, u32[]{:S(2)}) collective-permute-start(bf16[128,1536]{1,0:T(8,128)(2,1)S(1)} %collective-permute-done.1.refs_2_.g2), channel_id=1, source_target_pairs={{0,1},{1,0},{2,3},{3,2},{4,5},{5,4},{6,7},{7,6},{8,9},{9,8},{10,11... | collective-permute-start | bytes 1179656 | tf_op jit(solution)/shard_map/ppermute | solution.py:328
  52.2 6.5 %collective-permute-start.6 = (bf16[128,1536]{1,0:T(8,128)(2,1)S(1)}, bf16[128,1536]{1,0:T(8,128)(2,1)S(1)}, u32[]{:S(2)}, u32[]{:S(2)}) collective-permute-start(bf16[128,1536]{1,0:T(8,128)(2,1)S(1)} %collective-permute-done.2.refs_3_.g3), channel_id=1, source_target_pairs={{0,1},{1,0},{2,3},{3,2},{4,5},{5,4},{6,7},{7,6},{8,9},{9,8},{10,11... | collective-permute-start | bytes 1179656 | tf_op jit(solution)/shard_map/ppermute | solution.py:328
  52.7 5.9 %collective-permute-start.3 = (bf16[128,1024]{1,0:T(8,128)(2,1)S(1)}, bf16[128,1024]{1,0:T(8,128)(2,1)S(1)}, u32[]{:S(2)}, u32[]{:S(2)}) collective-permute-start(bf16[128,1024]{1,0:T(8,128)(2,1)S(1)} %copy-done.1), channel_id=1, source_target_pairs={{0,1},{1,0},{2,3},{3,2},{4,5},{5,4},{6,7},{7,6},{8,9},{9,8},{10,11... | collective-permute-start | bytes 786440 | tf_op jit(solution)/shard_map/ppermute | solution.py:328
  52.8 5.9 %collective-permute-start.10 = (bf16[2,2,128,128]{3,2,1,0:T(8,128)(2,1)S(1)}, bf16[2,2,128,128]{3,2,1,0:T(8,128)(2,1)S(1)}, u32[]{:S(2)}, u32[]{:S(2)}) collective-permute-start(bf16[2,2,128,128]{3,2,1,0:T(8,128)(2,1)S(1)} %get-tuple-element.48), channel_id=1, source_target_pairs={{0,12},{1,13},{2,14},{3,15},{4,0},{5,1},{6,2},{7,3},{8,4},{9,5},{1... | collective-permute-start | bytes 393224 | tf_op jit(solution)/shard_map/ppermute | solution.py:328
  58.6 16.4 %collective-permute-start.27 = (bf16[2,256,256]{2,1,0:T(8,128)(2,1)S(1)}, bf16[2,256,256]{2,1,0:T(8,128)(2,1)S(1)}, u32[]{:S(2)}, u32[]{:S(2)}) collective-permute-start(bf16[2,256,256]{2,1,0:T(8,128)(2,1)S(1)} %collective-permute-done.26.refs_1_), channel_id=1, source_target_pairs={{0,4},{1,5},{2,6},{3,7},{4,8},{5,9},{6,10},{7,11},{8,12},{9,13},{1... | collective-permute-start | bytes 786440 | tf_op jit(solution)/shard_map/ppermute | solution.py:328
  58.6 14.0 %copy-start.5 = (bf16[16,256,128]{2,1,0:T(8,128)(2,1)S(1)}, bf16[16,256,128]{2,1,0:T(8,128)(2,1)}, u32[]{:S(2)}) copy-start(bf16[16,256,128]{2,1,0:T(8,128)(2,1)} %constant.45.clone.refs_8_) | copy-start | bytes 3145732
  58.6 14.0 %copy-start.6 = (bf16[16,256,128]{2,1,0:T(8,128)(2,1)S(1)}, bf16[16,256,128]{2,1,0:T(8,128)(2,1)}, u32[]{:S(2)}) copy-start(bf16[16,256,128]{2,1,0:T(8,128)(2,1)} %constant.46.clone.refs_9_) | copy-start | bytes 3145732
  61.4 9.8 %collective-permute-start.18 = (bf16[256,128]{1,0:T(8,128)(2,1)S(1)}, bf16[256,128]{1,0:T(8,128)(2,1)S(1)}, u32[]{:S(2)}, u32[]{:S(2)}) collective-permute-start(bf16[256,128]{1,0:T(8,128)(2,1)S(1)} %get-tuple-element.54), channel_id=1, source_target_pairs={{0,4},{1,5},{2,6},{3,7},{4,8},{5,9},{6,10},{7,11},{8,12},{9,13},{1... | collective-permute-start | bytes 196616 | tf_op jit(solution)/shard_map/ppermute | solution.py:328
  61.6 11.0 %collective-permute-start.19 = (bf16[256,128]{1,0:T(8,128)(2,1)S(1)}, bf16[256,128]{1,0:T(8,128)(2,1)S(1)}, u32[]{:S(2)}, u32[]{:S(2)}) collective-permute-start(bf16[256,128]{1,0:T(8,128)(2,1)S(1)} %get-tuple-element.55), channel_id=1, source_target_pairs={{0,8},{1,9},{2,10},{3,11},{4,12},{5,13},{6,14},{7,15},{8,0},{9,1},... | collective-permute-start | bytes 196616 | tf_op jit(solution)/shard_map/ppermute | solution.py:328
  65.8 6.8 %collective-permute-start.20 = (bf16[256,128]{1,0:T(8,128)(2,1)S(1)}, bf16[256,128]{1,0:T(8,128)(2,1)S(1)}, u32[]{:S(2)}, u32[]{:S(2)}) collective-permute-start(bf16[256,128]{1,0:T(8,128)(2,1)S(1)} %get-tuple-element.56), channel_id=1, source_target_pairs={{0,12},{1,13},{2,14},{3,15},{4,0},{5,1},{6,2},{7,3},{8,4},{9,5},{1... | collective-permute-start | bytes 196616 | tf_op jit(solution)/shard_map/ppermute | solution.py:328
  75.0 14.3 %collective-permute-start.28 = (bf16[2,256,256]{2,1,0:T(8,128)(2,1)S(1)}, bf16[2,256,256]{2,1,0:T(8,128)(2,1)S(1)}, u32[]{:S(2)}, u32[]{:S(2)}) collective-permute-start(bf16[2,256,256]{2,1,0:T(8,128)(2,1)S(1)} %collective-permute-done.27.refs_2_), channel_id=1, source_target_pairs={{0,4},{1,5},{2,6},{3,7},{4,8},{5,9},{6,10},{7,11},{8,12},{9,13},{1... | collective-permute-start | bytes 786440 | tf_op jit(solution)/shard_map/ppermute | solution.py:328
  77.0 10.7 %collective-permute-start.21 = (bf16[256,128]{1,0:T(8,128)(2,1)S(1)}, bf16[256,128]{1,0:T(8,128)(2,1)S(1)}, u32[]{:S(2)}, u32[]{:S(2)}) collective-permute-start(bf16[256,128]{1,0:T(8,128)(2,1)S(1)} %get-tuple-element.58), channel_id=1, source_target_pairs={{0,4},{1,5},{2,6},{3,7},{4,8},{5,9},{6,10},{7,11},{8,12},{9,13},{1... | collective-permute-start | bytes 196616 | tf_op jit(solution)/shard_map/ppermute | solution.py:328
  77.0 12.3 %collective-permute-start.22 = (bf16[256,128]{1,0:T(8,128)(2,1)S(1)}, bf16[256,128]{1,0:T(8,128)(2,1)S(1)}, u32[]{:S(2)}, u32[]{:S(2)}) collective-permute-start(bf16[256,128]{1,0:T(8,128)(2,1)S(1)} %get-tuple-element.59), channel_id=1, source_target_pairs={{0,8},{1,9},{2,10},{3,11},{4,12},{5,13},{6,14},{7,15},{8,0},{9,1},... | collective-permute-start | bytes 196616 | tf_op jit(solution)/shard_map/ppermute | solution.py:328
  79.5 9.9 %collective-permute-start.23 = (bf16[256,128]{1,0:T(8,128)(2,1)S(1)}, bf16[256,128]{1,0:T(8,128)(2,1)S(1)}, u32[]{:S(2)}, u32[]{:S(2)}) collective-permute-start(bf16[256,128]{1,0:T(8,128)(2,1)S(1)} %get-tuple-element.60), channel_id=1, source_target_pairs={{0,12},{1,13},{2,14},{3,15},{4,0},{5,1},{6,2},{7,3},{8,4},{9,5},{1... | collective-permute-start | bytes 196616 | tf_op jit(solution)/shard_map/ppermute | solution.py:328
  90.9 3.3 %collective-permute-start.29 = (bf16[4,256,256]{2,1,0:T(8,128)(2,1)}, bf16[4,256,256]{2,1,0:T(8,128)(2,1)}, u32[]{:S(2)}, u32[]{:S(2)}) collective-permute-start(bf16[4,256,256]{2,1,0:T(8,128)(2,1)} %get-tuple-element.70), channel_id=1, source_target_pairs={{0,1},{1,0},{2,3},{3,2},{4,5},{5,4},{6,7},{7,6},{8,9},{9,8},{10,11... | collective-permute-start | bytes 1572872 | tf_op jit(solution)/shard_map/ppermute | solution.py:328
  92.4 1.7 %collective-permute-start.24 = (bf16[512,256]{1,0:T(8,128)(2,1)S(1)}, bf16[512,256]{1,0:T(8,128)(2,1)S(1)}, u32[]{:S(2)}, u32[]{:S(2)}) collective-permute-start(bf16[512,256]{1,0:T(8,128)(2,1)S(1)} %shard_map.95.gated), channel_id=1, source_target_pairs={{0,1},{1,0},{2,3},{3,2},{4,5},{5,4},{6,7},{7,6},{8,9},{9,8},{10,11... | collective-permute-start | bytes 786440 | tf_op jit(solution)/shard_map/ppermute | solution.py:328
  96.7 9.2 %collective-permute-start.32 = (bf16[128,1024]{1,0:T(8,128)(2,1)S(1)}, bf16[128,1024]{1,0:T(8,128)(2,1)S(1)}, u32[]{:S(2)}, u32[]{:S(2)}) collective-permute-start(bf16[128,1024]{1,0:T(8,128)(2,1)S(1)} %get-tuple-element.74), channel_id=1, source_target_pairs={{0,2},{1,3},{2,0},{3,1},{4,6},{5,7},{6,4},{7,5},{8,10},{9,11},{10,... | collective-permute-start | bytes 786440 | tf_op jit(solution)/shard_map/ppermute | solution.py:328
  96.9 14.1 %collective-permute-start.31 = (bf16[128,1024]{1,0:T(8,128)(2,1)S(1)}, bf16[128,1024]{1,0:T(8,128)(2,1)S(1)}, u32[]{:S(2)}, u32[]{:S(2)}) collective-permute-start(bf16[128,1024]{1,0:T(8,128)(2,1)S(1)} %get-tuple-element.73), channel_id=1, source_target_pairs={{0,16},{1,17},{2,18},{3,19},{4,20},{5,21},{6,22},{7,23},{8,24},{9,... | collective-permute-start | bytes 786440 | tf_op jit(solution)/shard_map/ppermute | solution.py:328
  98.5 12.6 %collective-permute-start.30 = (bf16[128,1024]{1,0:T(8,128)(2,1)S(1)}, bf16[128,1024]{1,0:T(8,128)(2,1)S(1)}, u32[]{:S(2)}, u32[]{:S(2)}) collective-permute-start(bf16[128,1024]{1,0:T(8,128)(2,1)S(1)} %get-tuple-element.72), channel_id=1, source_target_pairs={{0,18},{1,19},{2,16},{3,17},{4,22},{5,23},{6,20},{7,21},{8,26},{9,... | collective-permute-start | bytes 786440 | tf_op jit(solution)/shard_map/ppermute | solution.py:328

commit v5 on v4

--- a/solution.py
+++ b/solution.py
@@ -31,21 +31,25 @@
     return lax.dot_general(a, b, (((1,), (1,)), ((), ())), preferred_element_type=F32)
 
 
-def in_vmem(kernel, out_shape, scratch=(), smem=1, flops=0, moved=0):
+def in_vmem(kernel, out_shape, scratch=(), flops=0, moved=0):
     def call(*operands):
-        specs = [pl.BlockSpec(memory_space=pltpu.SMEM)] * smem
-        specs += [pl.BlockSpec(memory_space=pltpu.VMEM)] * (len(operands) - smem)
+        specs = [pl.BlockSpec(memory_space=pltpu.VMEM)] * len(operands)
         return pl.pallas_call(
             kernel,
             out_shape=out_shape,
             in_specs=specs,
             out_specs=jax.tree.map(lambda _: pl.BlockSpec(memory_space=pltpu.VMEM), out_shape),
             scratch_shapes=list(scratch),
-            compiler_params=pltpu.CompilerParams(vmem_limit_bytes=48 * 1024 * 1024),
+            compiler_params=pltpu.CompilerParams(vmem_limit_bytes=20 * 1024 * 1024),
             cost_estimate=pl.CostEstimate(flops=flops, bytes_accessed=moved, transcendentals=0),
         )(*operands)
 
     return call
+
+
+def place():
+    y, s, c = (lax.axis_index(a) for a in AXES)
+    return y, lax.rem(s, 2), lax.div(s, 2), c
 
 
 def low_lanes(shape):
@@ -63,23 +67,14 @@
     )
 
 
-def prologue(where, tokens, key, query, value, out, filt, *refs):
-    own_v, away_v, own_o, away_o, m1, m2, m3, own, away_f, sem = refs
-    y, x = where[0], where[1]
-
-    def lanes(p):
-        row = 1 - y if p // 2 else y
-        column = 1 - x if p % 2 else x
-        return pl.ds(pl.multiple_of(row * 512 + column * 256, 256), 256)
-
-    moves = [(value.at[:, lanes(0)], own_v), (value.at[:, lanes(1)], away_v)]
-    moves.append((filt.at[:, :, :, lanes(1)], away_f))
-    for p, message in enumerate((own, m1, m2, m3)):
-        moves.append((key.at[:, lanes(p)], message.at[:, pl.ds(0, 256)]))
-        moves.append((query.at[:, lanes(p)], message.at[:, pl.ds(256, 256)]))
-        if p:
-            moves.append((tokens, message.at[:, pl.ds(512, 1024)]))
-    moves += [(out.at[:, lanes(0)], own_o), (out.at[:, lanes(1)], away_o)]
+def quarter(p):
+    y, x, _, _ = place()
+    row = 1 - y if p // 2 else y
+    column = 1 - x if p % 2 else x
+    return pl.ds(pl.multiple_of(row * 512 + column * 256, 256), 256)
+
+
+def copied(moves, sem):
     copies = [pltpu.make_async_copy(a, b, sem.at[i]) for i, (a, b) in enumerate(moves)]
     for copy in copies:
         copy.start()
@@ -87,18 +82,45 @@
         copy.wait()
 
 
-def pack_filter(where, filt, near, *outs):
-    y, x, z = where[0], where[1], where[2]
-    packed, outs = outs[4], outs[:4]
+def cut_weights(value, out, own_v, away_v, own_o, away_o, sem):
+    moves = [(value.at[:, quarter(0)], own_v), (value.at[:, quarter(1)], away_v)]
+    copied(moves + [(out.at[:, quarter(0)], own_o), (out.at[:, quarter(1)], away_o)], sem)
+
+
+def cut_messages(tokens, key, query, after, m1, m2, m3, own, sem):
+    moves = []
+    for p, message in enumerate((own, m1, m2, m3)):
+        moves.append((key.at[:, quarter(p)], message.at[:, pl.ds(0, 256)]))
+        moves.append((query.at[:, quarter(p)], message.at[:, pl.ds(256, 256)]))
+        if p:
+            moves.append((tokens, message.at[:, pl.ds(512, 1024)]))
+    copied(moves, sem)
+
+
+def copy_kernel(kernel, out_shape):
+    def call(*operands):
+        return pl.pallas_call(
+            kernel,
+            out_shape=out_shape,
+            in_specs=[pl.BlockSpec(memory_space=pltpu.MemorySpace.HBM)] * len(operands),
+            out_specs=[pl.BlockSpec(memory_space=pltpu.VMEM)] * len(out_shape),
+            scratch_shapes=[pltpu.SemaphoreType.DMA((12,))],
+            compiler_params=pltpu.CompilerParams(vmem_limit_bytes=61 * 1024 * 1024),
+        )(*operands)
+
+    return call
+
+
+def pack_filter(filt, *refs):
+    y, x, z, _ = place()
+    packed, outs = refs[4], refs[:4]
     low = low_lanes((128, 128))
     for k in range(2):
+        column = 1 - x if k else x
         for j in range(2):
-            base = pl.multiple_of(y * 512 + x * 256 + j * 128, 128)
+            base = pl.multiple_of(y * 512 + column * 256 + j * 128, 128)
             for part in range(2):
-                if k:
-                    pair = [near[part, i, :, pl.ds(j * 128, 128)].astype(F32) for i in range(2)]
-                else:
-                    pair = [filt[part, i, :, pl.ds(base, 128)].astype(F32) for i in range(2)]
+                pair = [filt[part, i, :, pl.ds(base, 128)].astype(F32) for i in range(2)]
                 one, two = both(*pair, low)
                 packed[2 * j, k, part] = one
                 packed[2 * j + 1, k, part] = two
@@ -106,16 +128,27 @@
         outs[r][...] = packed[lax.rem(z + r, 4)]
 
 
-def value_kernel(where, *refs):
-    mine, other, gates, pieces = refs[:4], refs[4:8], refs[8], refs[9:17]
-    drive, outs = refs[17], refs[18:22]
-    acc, packed = refs[22], refs[23]
-    x, z, c = where[1], where[2], where[3]
+def pass_filter(f0, f1, f2, f3, out):
+    for r, block in enumerate((f0, f1, f2, f3)):
+        out[r] = block[1]
+
+
+def join_tokens(m1, m2, m3, out):
+    for p, message in enumerate((m1, m2, m3)):
+        out[pl.ds(p * 128, 128), :] = message[:, pl.ds(512, 1024)]
+
+
+def value_kernel(*refs):
+    mine, other, gates, pieces = refs[:4], refs[4:6], refs[6], refs[7:15]
+    drive, outs = refs[15], refs[16:20]
+    acc, packed = refs[20], refs[21]
+    _, x, z, c = place()
     acc[...] = jnp.zeros_like(acc)
 
     def gather(blocks, base):
-        lanes = [pl.ds(pl.multiple_of(base + (512 if p else 0), 256), 256) for p in range(4)]
-        return jnp.concatenate([b[:, at] for b, at in zip(blocks, lanes)], axis=0)
+        near, far = pl.multiple_of(base, 256), pl.multiple_of(base + 512, 256)
+        lanes = [near] + [near if len(blocks) == 2 else far] * 3
+        return jnp.concatenate([b[:, pl.ds(at, 256)] for b, at in zip(blocks, lanes)], axis=0)
 
     for r in range(4):
         owner = lax.rem(z - r + 4, 4)
@@ -193,14 +226,14 @@
     return [cadd(at(even, k), cmul(at(odd, k), -2 * math.pi * k / count)) for k in range(rows)]
 
 
-def conv_kernel(where, *refs):
-    drives, filters, (table, table_t) = refs[:4], refs[4:8], refs[8:10]
-    outs, (data, filt, first, sums) = refs[10:14], refs[14:]
-    x, z = where[1], where[2]
+def conv_kernel(*refs):
+    drives, filters, (beside, table, table_t) = refs[:4], refs[4:8], refs[8:11]
+    outs, (data, filt, first, sums) = refs[11:15], refs[15:]
+    _, x, z, _ = place()
     for r, block in enumerate(drives):
         base = 2 * lax.rem(z - r + 4, 4)
         filt[base + x] = filters[r][0]
-        filt[base + 1 - x] = filters[r][1]
+        filt[base + 1 - x] = beside[r]
         data[base + x] = block[pl.ds(0, 128), :]
         data[base + 1 - x] = block[pl.ds(128, 128), :]
     for i in range(8):
@@ -258,8 +291,8 @@
         out[pl.ds(128, 128), :] = data[base + 1 - x]
 
 
-def gate_kernel(where, e0, e1, e2, e3, drive, skip, gates, g1, g2, g3, gated, conv):
-    z = where[2]
+def gate_kernel(e0, e1, e2, e3, drive, skip, gates, g1, g2, g3, gated, conv):
+    y, x, z, _ = place()
     for r, block in enumerate((e0, e1, e2, e3)):
         conv[lax.rem(z - r + 4, 4)] = block[...]
     low = low_lanes((256, 128))
@@ -270,14 +303,15 @@
         for p, gate in enumerate((gates, g1, g2, g3)):
             rows = pl.ds(p * 128, 128)
             own = parts[p // 2][(p % 2) * 128 : (p % 2) * 128 + 128]
-            direct = skip[:, lanes] * drive[rows, lanes].astype(F32)
+            at = pl.ds(pl.multiple_of(y * 512 + x * 256 + j * 128, 128), 128)
+            direct = skip[:, at] * drive[rows, lanes].astype(F32)
             query = gate[:, pl.ds(256 + j * 128, 128)].astype(F32)
             gated[rows, lanes] = (query * (own + direct)).astype(BF16)
 
 
-def sort_weight(where, *refs):
+def sort_weight(*refs):
     pieces, keep, give = refs[:4], refs[4], refs[5]
-    x, z, c = where[1], where[2], where[3]
+    _, x, z, c = place()
     for r in range(4):
         owner = lax.rem(z - r + 4, 4)
         for k in range(2):
@@ -313,10 +347,7 @@
 
 
 def planes(tokens, gate_q, gate_k, w_value, skip, filter_spectrum, w_out):
-    y, s, c = (lax.axis_index(a) for a in AXES)
-    x, z = s % 2, s // 2
     seq, deep = 8, 4
-    where = jnp.stack([y, x, z, c]).astype(jnp.int32)
 
     def permute(values, move):
         pairs = []
@@ -344,45 +375,47 @@
 
     shape = jax.ShapeDtypeStruct
     block, square = shape((256, 128), BF16), shape((256, 256), BF16)
-    inside = pl.BlockSpec(memory_space=pltpu.MemorySpace.HBM)
-    laid = [square] * 4 + [shape((128, w), BF16) for w in (1536, 1536, 1536, 512)]
-    laid.append(shape((2, 2, 128, 256), BF16))
-    own_v, away_v, own_o, away_o, *messages, gates, away_f = pl.pallas_call(
-        prologue,
-        out_shape=laid,
-        in_specs=[pl.BlockSpec(memory_space=pltpu.SMEM)] + [inside] * 6,
-        out_specs=[pl.BlockSpec(memory_space=pltpu.VMEM)] * 9,
-        scratch_shapes=[pltpu.SemaphoreType.DMA((16,))],
-        compiler_params=pltpu.CompilerParams(vmem_limit_bytes=61 * 1024 * 1024),
-    )(where, tokens, gate_k, gate_q, w_value, w_out, filter_spectrum)
-    ring = [own_v, to_x(away_v)]
-    received = [to_peer(messages[p - 1], p) for p in (1, 2, 3)]
-    ring += [to_z(ring[0], 1), to_z(ring[1], 1)]
-    got = to_x(away_f)
+    own_v, away_v, own_o, away_o = copy_kernel(cut_weights, [square] * 4)(w_value, w_out)
+    laid = [shape((128, w), BF16) for w in (1536, 1536, 1536, 512)]
+    *messages, gates = copy_kernel(cut_messages, laid)(tokens, gate_k, gate_q, own_v)
     filters = in_vmem(
         pack_filter,
         [shape((2, 2, 128, 128), BF16)] * 4,
         [pltpu.VMEM((4, 2, 2, 128, 128), BF16)],
         moved=1 << 20,
-    )(where, filter_spectrum, got)
+        )(after(filter_spectrum, messages[0]))
     filters = [filters[0]] + [to_z(filters[r], r) for r in (1, 2, 3)]
+    received = [to_peer(messages[p - 1], p) for p in (1, 2, 3)]
+    b0 = to_x(away_v)
+    a1 = to_z(own_v, 1)
+    b1 = to_z(b0, 1)
+    a2 = to_z(after(a1, b0), 1)
+    b2 = to_z(after(b1, a1, received[1]), 1)
+    a3 = to_z(after(a2, b1, received[2]), 1)
+    got_o = to_x(after(away_o, b0))
+    b3 = to_z(after(b2, a2, got_o, *filters[1:]), 1)
+    ring = [own_v, b0, a1, b1, a2, b2, a3, b3]
+    passed = in_vmem(pass_filter, shape((4, 2, 128, 128), BF16), moved=1 << 20)(
+        after(filters[0], b2), *filters[1:]
+    )
+    beside = to_x(passed)
     mine = [tokens] + received
-    other = [to_core(m) for m in mine]
-    ring += [to_z(ring[2], 1), to_z(ring[3], 1)]
-    ring += [to_z(after(ring[4], *received[:2]), 1), to_z(ring[5], 1)]
-    pair = jnp.stack([own_o, to_x(after(away_o, got))])
-    hops = [after(pair, ring[4], ring[5], received[2])]
-    hops.append(to_z(hops[0], 1))
-    hops.append(to_z(after(hops[1], ring[6], ring[7]), 1))
-    gates = after(gates, *filters)
+    first = after(received[0], a3, b3)
+    joined = in_vmem(join_tokens, shape((384, 1024), BF16), moved=2 << 20)(first, *received[1:])
+    other = [to_core(tokens), to_core(joined)]
+    pair = jnp.stack([own_o, got_o])
+    hops = [pair, to_z(after(pair, a3), 1)]
+    gates = after(gates, passed)
     drive, *sends = in_vmem(
         value_kernel,
         [shape((512, 256), BF16)] + [block] * 4,
         [pltpu.VMEM((512, 256), F32), pltpu.VMEM((4, 256, 128), BF16)],
         flops=1 << 29,
         moved=4 << 20,
-    )(where, *mine, *other, gates, *ring)
+    )(*mine, *other, gates, *ring)
     columns = [sends[0]] + [to_z(sends[r], r) for r in (1, 2, 3)]
+    hops.append(to_z(after(hops[1], drive), 1))
+    hops.append(to_z(after(hops[2], *columns[1:]), 1))
     table, table_t = tables()
     sends = in_vmem(
         conv_kernel,
@@ -395,23 +428,20 @@
         ],
         flops=1 << 30,
         moved=5 << 20,
-    )(where, *columns, *filters, table, table_t)
+    )(*columns, *filters, beside, table, table_t)
     rows = [sends[0]] + [to_z(sends[r], r) for r in (1, 2, 3)]
 
-    hops.append(to_z(after(hops[2], sends[0]), 1))
     hops[3] = after(hops[3], *rows[1:])
     quad = shape((4, 256, 256), BF16)
-    keep, give = in_vmem(sort_weight, [quad] * 2, moved=2 << 20)(where, *hops)
+    keep, give = in_vmem(sort_weight, [quad] * 2, moved=2 << 20)(*hops)
     theirs = to_core(give)
-    channels = lax.dynamic_slice_in_dim(skip, (y * 2 + x) * 256, 256)[None, :]
     gated = in_vmem(
         gate_kernel, shape((512, 256), BF16), [pltpu.VMEM((4, 256, 128), BF16)], moved=1 << 20
-    )(where, *rows, drive, channels, gates, *received)
+    )(*rows, drive, skip[None, :], gates, *received)
     gated_other = to_core(gated)
     own, *sends = in_vmem(
         out_kernel,
         [shape((128, 1024), F32)] + [shape((128, 1024), BF16)] * 3,
-        smem=0,
         flops=1 << 30,
         moved=4 << 20,
     )(gated, gated_other, keep, theirs)

time: 112 us -> 111 us (level)
  starting transfers between devices: 41.2 us -> 46.4 us
  Pallas kernels: 14.5 us -> 10.8 us
  waiting for transfers between devices: 53.7 us -> 50.7 us
    ppermute x33 -> x31, starting transfers between devices: 41.2 us -> 46.4 us  [permute(): return lax.ppermute(values, AXES, pairs)]
    pallas_call x6 -> x8, Pallas kernels: 10.7 us -> 6.16 us  [call(): pl.pallas_call(kernel, out_shape=out_shape, in_specs=specs, out_specs=jax...]
    ppermute x33 -> x31, waiting for transfers between devices: 53.7 us -> 50.7 us  [permute(): return lax.ppermute(values, AXES, pairs)]
    unnamed x16 -> x22, local copies, waits for them, and re-layouts: 0.03 us -> 1.48 us
    pallas_call x1 -> x2, Pallas kernels: 3.81 us -> 4.65 us  [call(): pl.pallas_call(kernel, out_shape=out_shape, in_specs=[pl.BlockSpec(memory...]
  transfers between devices with their start and end apart: 33 -> 31, of which waited for: 13 -> 14; matrix products, arithmetic and copies ran while one was open for 1% -> 0% of each run, Pallas kernels for 6% -> 4%
where the time goes in v5:
time: 111 us; the launch traced here: 110 us
  waiting for transfers between devices  50.7 us (46%)
  starting transfers between devices  46.4 us (42%)
  Pallas kernels  10.8 us (10%)
  local copies, waits for them, and re-layouts  1.48 us (1%)
    ppermute x31, waiting for transfers between devices, permute(): return lax.ppermute(values, AXES, pairs)  50.7 us
    ppermute x31, starting transfers between devices, permute(): return lax.ppermute(values, AXES, pairs)  46.4 us
    pallas_call x8, Pallas kernels, call(): pl.pallas_call(kernel, out_shape=out_shape, in_specs=specs, out_specs=jax...  6.16 us
    pallas_call x2, Pallas kernels, call(): pl.pallas_call(kernel, out_shape=out_shape, in_specs=[pl.BlockSpec(memory...  4.65 us
  transfers between devices with their start and end apart: 31, of which 14 were waited for; matrix products, arithmetic and copies ran while one was open for 0% of the time, Pallas kernels for 4%

profile of v5, /device:TPU:0, one launch (start us, length us, event | category | flops | bytes accessed | tf_op | source)
XLA Modules:
  0.0 110.4 jit_solution(4166848563391831751)
XLA Ops:
  0.0 2.1 %shard_map.91 = (bf16[256,256]{1,0:T(8,128)(2,1)}, bf16[256,256]{1,0:T(8,128)(2,1)}, bf16[256,256]{1,0:T(8,128)(2,1)}, bf16[256,256]{1,0:T(8,128)(2,1)}) custom-call(bf16[256,1024]{1,0:T(8,128)(2,1)} %value.1, bf16[256,1024]{1,0:T(8,128)(2,1)} %out.1), custom_call_target="tpu_custom_call" | custom-call | tf_op jit(solution)/shard_map/pallas_call | solution.py:102
  2.1 0.0 copy-start.3
  2.1 2.6 %shard_map.92 = (bf16[128,1536]{1,0:T(8,128)(2,1)}, bf16[128,1536]{1,0:T(8,128)(2,1)}, bf16[128,1536]{1,0:T(8,128)(2,1)}, bf16[128,512]{1,0:T(8,128)(2,1)}) custom-call(bf16[128,1024]{1,0:T(8,128)(2,1)} %refs_0_.1, bf16[128,1024]{1,0:T(8,128)(2,1)} %key.1, bf16[128,1024]{1,0:T(8,128)(2,1)} %query.1, bf16[256,256]{1,0:T(8,128)(2,1)} %get-tuple-element.45.after.refs_7_), custom_call_target="tpu_custom_call" | custom-call | tf_op jit(solution)/shard_map/pallas_call | solution.py:102
  4.7 3.0 %collective-permute-start.1 = (bf16[128,1536]{1,0:T(8,128)(2,1)}, bf16[128,1536]{1,0:T(8,128)(2,1)S(1)}, u32[]{:S(2)}, u32[]{:S(2)}) collective-permute-start(bf16[128,1536]{1,0:T(8,128)(2,1)} %get-tuple-element.47), channel_id=1, source_target_pairs={{0,16},{1,17},{2,18},{3,19},{4,20},{5,21},{6,22},{7,23},{8,24},{9,... | collective-permute-start | bytes 1179656 | tf_op jit(solution)/shard_map/ppermute | solution.py:359
  7.7 1.4 %collective-permute-start.2 = (bf16[128,1536]{1,0:T(8,128)(2,1)}, bf16[128,1536]{1,0:T(8,128)(2,1)S(1)}, u32[]{:S(2)}, u32[]{:S(2)}) collective-permute-start(bf16[128,1536]{1,0:T(8,128)(2,1)} %get-tuple-element.48), channel_id=1, source_target_pairs={{0,18},{1,19},{2,16},{3,17},{4,22},{5,23},{6,20},{7,21},{8,26},{9,... | collective-permute-start | bytes 1179656 | tf_op jit(solution)/shard_map/ppermute | solution.py:359
  9.2 0.1 collective-permute-start.5
  9.3 2.0 %collective-permute-start.4 = (bf16[256,256]{1,0:T(8,128)(2,1)S(1)}, bf16[256,256]{1,0:T(8,128)(2,1)S(1)}, u32[]{:S(2)}, u32[]{:S(2)}) collective-permute-start(bf16[256,256]{1,0:T(8,128)(2,1)S(1)} %copy-done.3), channel_id=1, source_target_pairs={{0,4},{1,5},{2,6},{3,7},{4,8},{5,9},{6,10},{7,11},{8,12},{9,13},{1... | collective-permute-start | bytes 393224 | tf_op jit(solution)/shard_map/ppermute | solution.py:359
  11.3 9.9 %collective-permute-done.5.refs_8_ = bf16[256,256]{1,0:T(8,128)(2,1)S(1)} collective-permute-done((bf16[256,256]{1,0:T(8,128)(2,1)S(1)}, bf16[256,256]{1,0:T(8,128)(2,1)S(1)}, u32[]{:S(2)}, u32[]{:S(2)}) %collective-permute-start.5) | collective-permute-done | bytes 131104 | tf_op jit(solution)/shard_map/ppermute | solution.py:359
  21.2 1.7 %collective-permute-start.7 = (bf16[256,256]{1,0:T(8,128)(2,1)S(1)}, bf16[256,256]{1,0:T(8,128)(2,1)S(1)}, u32[]{:S(2)}, u32[]{:S(2)}) collective-permute-start(bf16[256,256]{1,0:T(8,128)(2,1)S(1)} %collective-permute-done.5.refs_8_), channel_id=1, source_target_pairs={{0,4},{1,5},{2,6},{3,7},{4,8},{5,9},{6,10},{7,11},{8,12},{9,13},{1... | collective-permute-start | bytes 393224 | tf_op jit(solution)/shard_map/ppermute | solution.py:359
  22.9 0.3 shard_map.93
  23.2 1.6 %collective-permute-start.11 = (bf16[2,2,128,128]{3,2,1,0:T(8,128)(2,1)S(1)}, bf16[2,2,128,128]{3,2,1,0:T(8,128)(2,1)S(1)}, u32[]{:S(2)}, u32[]{:S(2)}) collective-permute-start(bf16[2,2,128,128]{3,2,1,0:T(8,128)(2,1)S(1)} %get-tuple-element.56), channel_id=1, source_target_pairs={{0,4},{1,5},{2,6},{3,7},{4,8},{5,9},{6,10},{7,11},{8,12},{9,13},{1... | collective-permute-start | bytes 393224 | tf_op jit(solution)/shard_map/ppermute | solution.py:359
  24.9 1.6 %collective-permute-start.6 = (bf16[256,256]{1,0:T(8,128)(2,1)S(1)}, bf16[256,256]{1,0:T(8,128)(2,1)S(1)}, u32[]{:S(2)}, u32[]{:S(2)}) collective-permute-start(bf16[256,256]{1,0:T(8,128)(2,1)S(1)} %collective-permute-done.4.refs_9_), channel_id=1, source_target_pairs={{0,4},{1,5},{2,6},{3,7},{4,8},{5,9},{6,10},{7,11},{8,12},{9,13},{1... | collective-permute-start | bytes 393224 | tf_op jit(solution)/shard_map/ppermute | solution.py:359
  26.4 2.8 %collective-permute-done.7.refs_10_ = bf16[256,256]{1,0:T(8,128)(2,1)S(1)} collective-permute-done((bf16[256,256]{1,0:T(8,128)(2,1)S(1)}, bf16[256,256]{1,0:T(8,128)(2,1)S(1)}, u32[]{:S(2)}, u32[]{:S(2)}) %collective-permute-start.7) | collective-permute-done | bytes 131104 | tf_op jit(solution)/shard_map/ppermute | solution.py:359
  29.3 1.7 %collective-permute-start = (bf16[128,1536]{1,0:T(8,128)(2,1)S(1)}, bf16[128,1536]{1,0:T(8,128)(2,1)S(1)}, u32[]{:S(2)}, u32[]{:S(2)}) collective-permute-start(bf16[128,1536]{1,0:T(8,128)(2,1)S(1)} %copy-done.8), channel_id=1, source_target_pairs={{0,2},{1,3},{2,0},{3,1},{4,6},{5,7},{6,4},{7,5},{8,10},{9,11},{10,... | collective-permute-start | bytes 1179656 | tf_op jit(solution)/shard_map/ppermute | solution.py:359
  30.9 0.8 collective-permute-start.12
  31.7 0.4 collective-permute-done.11.f1.refs_5_
  32.2 1.1 %collective-permute-start.13 = (bf16[2,2,128,128]{3,2,1,0:T(8,128)(2,1)S(1)}, bf16[2,2,128,128]{3,2,1,0:T(8,128)(2,1)S(1)}, u32[]{:S(2)}, u32[]{:S(2)}) collective-permute-start(bf16[2,2,128,128]{3,2,1,0:T(8,128)(2,1)S(1)} %get-tuple-element.58), channel_id=1, source_target_pairs={{0,12},{1,13},{2,14},{3,15},{4,0},{5,1},{6,2},{7,3},{8,4},{9,5},{1... | collective-permute-start | bytes 393224 | tf_op jit(solution)/shard_map/ppermute | solution.py:359
  33.3 1.6 %collective-permute-done.6.refs_11_ = bf16[256,256]{1,0:T(8,128)(2,1)S(1)} collective-permute-done((bf16[256,256]{1,0:T(8,128)(2,1)S(1)}, bf16[256,256]{1,0:T(8,128)(2,1)S(1)}, u32[]{:S(2)}, u32[]{:S(2)}) %collective-permute-start.6) | collective-permute-done | bytes 131104 | tf_op jit(solution)/shard_map/ppermute | solution.py:359
  34.9 1.7 %collective-permute-start.10 = (bf16[256,256]{1,0:T(8,128)(2,1)S(1)}, bf16[256,256]{1,0:T(8,128)(2,1)S(1)}, u32[]{:S(2)}, u32[]{:S(2)}) collective-permute-start(bf16[256,256]{1,0:T(8,128)(2,1)S(1)} %copy-done.9), channel_id=1, source_target_pairs={{0,2},{1,3},{2,0},{3,1},{4,6},{5,7},{6,4},{7,5},{8,10},{9,11},{10,... | collective-permute-start | bytes 393224 | tf_op jit(solution)/shard_map/ppermute | solution.py:359
  36.6 4.3 %collective-permute-start.9 = (bf16[256,256]{1,0:T(8,128)(2,1)S(1)}, bf16[256,256]{1,0:T(8,128)(2,1)S(1)}, u32[]{:S(2)}, u32[]{:S(2)}) collective-permute-start(bf16[256,256]{1,0:T(8,128)(2,1)S(1)} %collective-permute-done.7.refs_10_), channel_id=1, source_target_pairs={{0,4},{1,5},{2,6},{3,7},{4,8},{5,9},{6,10},{7,11},{8,12},{9,13},{1... | collective-permute-start | bytes 393224 | tf_op jit(solution)/shard_map/ppermute | solution.py:359
  40.9 2.6 %collective-permute-start.8 = (bf16[256,256]{1,0:T(8,128)(2,1)S(1)}, bf16[256,256]{1,0:T(8,128)(2,1)S(1)}, u32[]{:S(2)}, u32[]{:S(2)}) collective-permute-start(bf16[256,256]{1,0:T(8,128)(2,1)S(1)} %collective-permute-done.6.refs_11_), channel_id=1, source_target_pairs={{0,4},{1,5},{2,6},{3,7},{4,8},{5,9},{6,10},{7,11},{8,12},{9,13},{1... | collective-permute-start | bytes 393224 | tf_op jit(solution)/shard_map/ppermute | solution.py:359
  43.5 0.0 collective-permute-done.9.refs_12_
  43.5 5.6 %collective-permute-start.14 = (bf16[256,256]{1,0:T(8,128)(2,1)S(1)}, bf16[256,256]{1,0:T(8,128)(2,1)S(1)}, u32[]{:S(2)}, u32[]{:S(2)}) collective-permute-start(bf16[256,256]{1,0:T(8,128)(2,1)S(1)} %collective-permute-done.9.refs_12_), channel_id=1, source_target_pairs={{0,4},{1,5},{2,6},{3,7},{4,8},{5,9},{6,10},{7,11},{8,12},{9,13},{1... | collective-permute-start | bytes 393224 | tf_op jit(solution)/shard_map/ppermute | solution.py:359
  49.1 0.0 collective-permute-done.m1.refs_1_.g1
  49.1 0.0 collective-permute-done.8.refs_13_
  49.1 2.5 %collective-permute-done.14.refs_14_ = bf16[256,256]{1,0:T(8,128)(2,1)S(1)} collective-permute-done((bf16[256,256]{1,0:T(8,128)(2,1)S(1)}, bf16[256,256]{1,0:T(8,128)(2,1)S(1)}, u32[]{:S(2)}, u32[]{:S(2)}) %collective-permute-start.14) | collective-permute-done | bytes 131104 | tf_op jit(solution)/shard_map/ppermute | solution.py:359
  51.6 0.1 shard_map.94
  51.7 0.1 collective-permute-start.15
  51.8 0.5 collective-permute-start.3
  52.3 2.5 %collective-permute-start.24 = (bf16[2,256,256]{2,1,0:T(8,128)(2,1)S(1)}, bf16[2,256,256]{2,1,0:T(8,128)(2,1)S(1)}, u32[]{:S(2)}, u32[]{:S(2)}) collective-permute-start(bf16[2,256,256]{2,1,0:T(8,128)(2,1)S(1)} %pad_maximum_fusion.refs_0_), channel_id=1, source_target_pairs={{0,4},{1,5},{2,6},{3,7},{4,8},{5,9},{6,10},{7,11},{8,12},{9,13},{1... | collective-permute-start | bytes 786440 | tf_op jit(solution)/shard_map/ppermute | solution.py:359
  54.8 0.0 copy-start.5
  54.8 0.0 copy-start.6
  54.9 0.0 collective-permute-done.15.refs_5_
  54.9 0.8 copy-done.2
  55.7 2.1 %shard_map.96 = (bf16[512,256]{1,0:T(8,128)(2,1)S(1)}, bf16[256,128]{1,0:T(8,128)(2,1)S(1)}, bf16[256,128]{1,0:T(8,128)(2,1)S(1)}, bf16[256,128]{1,0:T(8,128)(2,1)S(1)}, bf16[256,128]{1,0:T(8,128)(2,1)S(1)}) custom-call(bf16[128,1024]{1,0:T(8,128)(2,1)S(1)} %copy-done, bf16[128,1536]{1,0:T(8,128)(2,1)S(1)} %collective-permute-done.m1.refs_1_.g1, ...), custom_call_target="tpu_custom_call" | custom-call | flops 536870912 | bytes 4194304 | tf_op jit(solution)/shard_map/pallas_call | solution.py:37
  57.8 4.6 %collective-permute-done.24.refs_1_ = bf16[2,256,256]{2,1,0:T(8,128)(2,1)S(1)} collective-permute-done((bf16[2,256,256]{2,1,0:T(8,128)(2,1)S(1)}, bf16[2,256,256]{2,1,0:T(8,128)(2,1)S(1)}, u32[]{:S(2)}, u32[]{:S(2)}) %collective-permute-start.24) | collective-permute-done | bytes 262176 | tf_op jit(solution)/shard_map/ppermute | solution.py:359
  62.4 0.6 collective-permute-start.25
  63.1 0.0 collective-permute-start.19
  63.1 0.3 collective-permute-start.16
  63.4 3.7 %collective-permute-start.17 = (bf16[256,128]{1,0:T(8,128)(2,1)S(1)}, bf16[256,128]{1,0:T(8,128)(2,1)S(1)}, u32[]{:S(2)}, u32[]{:S(2)}) collective-permute-start(bf16[256,128]{1,0:T(8,128)(2,1)S(1)} %get-tuple-element.67), channel_id=1, source_target_pairs={{0,8},{1,9},{2,10},{3,11},{4,12},{5,13},{6,14},{7,15},{8,0},{9,1},... | collective-permute-start | bytes 196616 | tf_op jit(solution)/shard_map/ppermute | solution.py:359
  67.0 7.6 %collective-permute-done.16.refs_1_ = bf16[256,128]{1,0:T(8,128)(2,1)S(1)} collective-permute-done((bf16[256,128]{1,0:T(8,128)(2,1)S(1)}, bf16[256,128]{1,0:T(8,128)(2,1)S(1)}, u32[]{:S(2)}, u32[]{:S(2)}) %collective-permute-start.16) | collective-permute-done | bytes 65568 | tf_op jit(solution)/shard_map/ppermute | solution.py:359
  74.6 1.4 %collective-permute-done.17.refs_2_ = bf16[256,128]{1,0:T(8,128)(2,1)S(1)} collective-permute-done((bf16[256,128]{1,0:T(8,128)(2,1)S(1)}, bf16[256,128]{1,0:T(8,128)(2,1)S(1)}, u32[]{:S(2)}, u32[]{:S(2)}) %collective-permute-start.17) | collective-permute-done | bytes 65568 | tf_op jit(solution)/shard_map/ppermute | solution.py:359
  76.1 1.9 %collective-permute-start.26 = (bf16[2,256,256]{2,1,0:T(8,128)(2,1)S(1)}, bf16[2,256,256]{2,1,0:T(8,128)(2,1)S(1)}, u32[]{:S(2)}, u32[]{:S(2)}) collective-permute-start(bf16[2,256,256]{2,1,0:T(8,128)(2,1)S(1)} %collective-permute-done.25.refs_2_), channel_id=1, source_target_pairs={{0,4},{1,5},{2,6},{3,7},{4,8},{5,9},{6,10},{7,11},{8,12},{9,13},{1... | collective-permute-start | bytes 786440 | tf_op jit(solution)/shard_map/ppermute | solution.py:359
  77.9 1.8 %shard_map.97 = (bf16[256,128]{1,0:T(8,128)(2,1)S(1)}, bf16[256,128]{1,0:T(8,128)(2,1)S(1)}, bf16[256,128]{1,0:T(8,128)(2,1)S(1)}, bf16[256,128]{1,0:T(8,128)(2,1)S(1)}) custom-call(bf16[256,128]{1,0:T(8,128)(2,1)S(1)} %get-tuple-element.65.refs_0_, bf16[256,128]{1,0:T(8,128)(2,1)S(1)} %collective-permute-done.16.refs_1_, ...), custom_call_target="tpu_custom_call" | custom-call | flops 1073741824 | bytes 5242880 | tf_op jit(solution)/shard_map/pallas_call | solution.py:37
  79.8 0.1 collective-permute-start.20
  79.8 2.5 %collective-permute-start.21 = (bf16[256,128]{1,0:T(8,128)(2,1)S(1)}, bf16[256,128]{1,0:T(8,128)(2,1)S(1)}, u32[]{:S(2)}, u32[]{:S(2)}) collective-permute-start(bf16[256,128]{1,0:T(8,128)(2,1)S(1)} %get-tuple-element.71), channel_id=1, source_target_pairs={{0,8},{1,9},{2,10},{3,11},{4,12},{5,13},{6,14},{7,15},{8,0},{9,1},... | collective-permute-start | bytes 196616 | tf_op jit(solution)/shard_map/ppermute | solution.py:359
  82.3 1.3 %collective-permute-start.22 = (bf16[256,128]{1,0:T(8,128)(2,1)S(1)}, bf16[256,128]{1,0:T(8,128)(2,1)S(1)}, u32[]{:S(2)}, u32[]{:S(2)}) collective-permute-start(bf16[256,128]{1,0:T(8,128)(2,1)S(1)} %get-tuple-element.72), channel_id=1, source_target_pairs={{0,12},{1,13},{2,14},{3,15},{4,0},{5,1},{6,2},{7,3},{8,4},{9,5},{1... | collective-permute-start | bytes 196616 | tf_op jit(solution)/shard_map/ppermute | solution.py:359
  83.6 4.9 %collective-permute-done.20.e1 = bf16[256,128]{1,0:T(8,128)(2,1)S(1)} collective-permute-done((bf16[256,128]{1,0:T(8,128)(2,1)S(1)}, bf16[256,128]{1,0:T(8,128)(2,1)S(1)}, u32[]{:S(2)}, u32[]{:S(2)}) %collective-permute-start.20) | collective-permute-done | bytes 65568 | tf_op jit(solution)/shard_map/ppermute | solution.py:359
  88.6 1.8 %collective-permute-done.21.e2 = bf16[256,128]{1,0:T(8,128)(2,1)S(1)} collective-permute-done((bf16[256,128]{1,0:T(8,128)(2,1)S(1)}, bf16[256,128]{1,0:T(8,128)(2,1)S(1)}, u32[]{:S(2)}, u32[]{:S(2)}) %collective-permute-start.21) | collective-permute-done | bytes 65568 | tf_op jit(solution)/shard_map/ppermute | solution.py:359
  90.3 0.1 shard_map.99
  90.5 0.0 copy-start.4
  90.5 0.1 collective-permute-start.27
  90.6 0.6 copy-done.4
  91.2 0.2 shard_map.98.gated
  91.4 0.1 collective-permute-start.23
  91.5 1.5 %collective-permute-done.23.other = bf16[512,256]{1,0:T(8,128)(2,1)S(1)} collective-permute-done((bf16[512,256]{1,0:T(8,128)(2,1)S(1)}, bf16[512,256]{1,0:T(8,128)(2,1)S(1)}, u32[]{:S(2)}, u32[]{:S(2)}) %collective-permute-start.23) | collective-permute-done | bytes 262176 | tf_op jit(solution)/shard_map/ppermute | solution.py:359
  93.0 1.5 %shard_map.100 = (f32[128,1024]{1,0:T(8,128)S(1)}, bf16[128,1024]{1,0:T(8,128)(2,1)S(1)}, bf16[128,1024]{1,0:T(8,128)(2,1)S(1)}, bf16[128,1024]{1,0:T(8,128)(2,1)S(1)}) custom-call(bf16[512,256]{1,0:T(8,128)(2,1)S(1)} %shard_map.98.gated, bf16[512,256]{1,0:T(8,128)(2,1)S(1)} %collective-permute-done.23.other, ...), custom_call_target="tpu_custom_call" | custom-call | flops 1073741824 | bytes 4194304 | tf_op jit(solution)/shard_map/pallas_call | solution.py:37
  94.5 1.3 %collective-permute-start.28 = (bf16[128,1024]{1,0:T(8,128)(2,1)S(1)}, bf16[128,1024]{1,0:T(8,128)(2,1)S(1)}, u32[]{:S(2)}, u32[]{:S(2)}) collective-permute-start(bf16[128,1024]{1,0:T(8,128)(2,1)S(1)} %get-tuple-element.82), channel_id=1, source_target_pairs={{0,18},{1,19},{2,16},{3,17},{4,22},{5,23},{6,20},{7,21},{8,26},{9,... | collective-permute-start | bytes 786440 | tf_op jit(solution)/shard_map/ppermute | solution.py:359
  95.8 0.4 collective-permute-start.29
  96.2 1.8 %collective-permute-start.30 = (bf16[128,1024]{1,0:T(8,128)(2,1)S(1)}, bf16[128,1024]{1,0:T(8,128)(2,1)S(1)}, u32[]{:S(2)}, u32[]{:S(2)}) collective-permute-start(bf16[128,1024]{1,0:T(8,128)(2,1)S(1)} %get-tuple-element.84), channel_id=1, source_target_pairs={{0,2},{1,3},{2,0},{3,1},{4,6},{5,7},{6,4},{7,5},{8,10},{9,11},{10,... | collective-permute-start | bytes 786440 | tf_op jit(solution)/shard_map/ppermute | solution.py:359
  98.1 6.6 %collective-permute-done.28 = bf16[128,1024]{1,0:T(8,128)(2,1)S(1)} collective-permute-done((bf16[128,1024]{1,0:T(8,128)(2,1)S(1)}, bf16[128,1024]{1,0:T(8,128)(2,1)S(1)}, u32[]{:S(2)}, u32[]{:S(2)}) %collective-permute-start.28) | collective-permute-done | bytes 262176 | tf_op jit(solution)/shard_map/ppermute | solution.py:359
  104.7 4.8 %collective-permute-done.29 = bf16[128,1024]{1,0:T(8,128)(2,1)S(1)} collective-permute-done((bf16[128,1024]{1,0:T(8,128)(2,1)S(1)}, bf16[128,1024]{1,0:T(8,128)(2,1)S(1)}, u32[]{:S(2)}, u32[]{:S(2)}) %collective-permute-start.29) | collective-permute-done | bytes 262176 | tf_op jit(solution)/shard_map/ppermute | solution.py:359
  109.4 0.1 collective-permute-done.30
  109.5 0.8 add_convert_fusion
  (32 shorter events, 0.1 us)
Async XLA Ops:
  0.0 22.9 %copy-start.1 = (bf16[2,2,128,1024]{3,2,1,0:T(8,128)(2,1)S(1)}, bf16[2,2,128,1024]{3,2,1,0:T(8,128)(2,1)}, u32[]{:S(2)}) copy-start(bf16[2,2,128,1024]{3,2,1,0:T(8,128)(2,1)} %filt) | copy-start | bytes 3145732
  2.1 7.1 %copy-start.10 = (bf16[256,256]{1,0:T(8,128)(2,1)S(1)}, bf16[256,256]{1,0:T(8,128)(2,1)}, u32[]{:S(2)}) copy-start(bf16[256,256]{1,0:T(8,128)(2,1)} %get-tuple-element.49) | copy-start | bytes 393220
  2.1 7.2 %copy-start.3 = (bf16[256,256]{1,0:T(8,128)(2,1)S(1)}, bf16[256,256]{1,0:T(8,128)(2,1)}, u32[]{:S(2)}) copy-start(bf16[256,256]{1,0:T(8,128)(2,1)} %get-tuple-element.45.after.refs_7_) | copy-start | bytes 393220
  4.7 26.2 %collective-permute-start.1 = (bf16[128,1536]{1,0:T(8,128)(2,1)}, bf16[128,1536]{1,0:T(8,128)(2,1)S(1)}, u32[]{:S(2)}, u32[]{:S(2)}) collective-permute-start(bf16[128,1536]{1,0:T(8,128)(2,1)} %get-tuple-element.47), channel_id=1, source_target_pairs={{0,16},{1,17},{2,18},{3,19},{4,20},{5,21},{6,22},{7,23},{8,24},{9,... | collective-permute-start | bytes 1179656 | tf_op jit(solution)/shard_map/ppermute | solution.py:359
  7.7 28.9 %collective-permute-start.2 = (bf16[128,1536]{1,0:T(8,128)(2,1)}, bf16[128,1536]{1,0:T(8,128)(2,1)S(1)}, u32[]{:S(2)}, u32[]{:S(2)}) collective-permute-start(bf16[128,1536]{1,0:T(8,128)(2,1)} %get-tuple-element.48), channel_id=1, source_target_pairs={{0,18},{1,19},{2,16},{3,17},{4,22},{5,23},{6,20},{7,21},{8,26},{9,... | collective-permute-start | bytes 1179656 | tf_op jit(solution)/shard_map/ppermute | solution.py:359
  9.2 12.0 %collective-permute-start.5 = (bf16[256,256]{1,0:T(8,128)(2,1)S(1)}, bf16[256,256]{1,0:T(8,128)(2,1)S(1)}, u32[]{:S(2)}, u32[]{:S(2)}) collective-permute-start(bf16[256,256]{1,0:T(8,128)(2,1)S(1)} %copy-done.10), channel_id=1, source_target_pairs={{0,2},{1,3},{2,0},{3,1},{4,6},{5,7},{6,4},{7,5},{8,10},{9,11},{10,... | collective-permute-start | bytes 393224 | tf_op jit(solution)/shard_map/ppermute | solution.py:359
  9.3 15.6 %collective-permute-start.4 = (bf16[256,256]{1,0:T(8,128)(2,1)S(1)}, bf16[256,256]{1,0:T(8,128)(2,1)S(1)}, u32[]{:S(2)}, u32[]{:S(2)}) collective-permute-start(bf16[256,256]{1,0:T(8,128)(2,1)S(1)} %copy-done.3), channel_id=1, source_target_pairs={{0,4},{1,5},{2,6},{3,7},{4,8},{5,9},{6,10},{7,11},{8,12},{9,13},{1... | collective-permute-start | bytes 393224 | tf_op jit(solution)/shard_map/ppermute | solution.py:359
  21.2 8.1 %collective-permute-start.7 = (bf16[256,256]{1,0:T(8,128)(2,1)S(1)}, bf16[256,256]{1,0:T(8,128)(2,1)S(1)}, u32[]{:S(2)}, u32[]{:S(2)}) collective-permute-start(bf16[256,256]{1,0:T(8,128)(2,1)S(1)} %collective-permute-done.5.refs_8_), channel_id=1, source_target_pairs={{0,4},{1,5},{2,6},{3,7},{4,8},{5,9},{6,10},{7,11},{8,12},{9,13},{1... | collective-permute-start | bytes 393224 | tf_op jit(solution)/shard_map/ppermute | solution.py:359
  22.9 6.4 %copy-start.8 = (bf16[128,1536]{1,0:T(8,128)(2,1)S(1)}, bf16[128,1536]{1,0:T(8,128)(2,1)}, u32[]{:S(2)}) copy-start(bf16[128,1536]{1,0:T(8,128)(2,1)} %get-tuple-element.46) | copy-start | bytes 1179652
  22.9 12.0 %copy-start.9 = (bf16[256,256]{1,0:T(8,128)(2,1)S(1)}, bf16[256,256]{1,0:T(8,128)(2,1)}, u32[]{:S(2)}) copy-start(bf16[256,256]{1,0:T(8,128)(2,1)} %get-tuple-element.54) | copy-start | bytes 393220
  23.2 8.9 %collective-permute-start.11 = (bf16[2,2,128,128]{3,2,1,0:T(8,128)(2,1)S(1)}, bf16[2,2,128,128]{3,2,1,0:T(8,128)(2,1)S(1)}, u32[]{:S(2)}, u32[]{:S(2)}) collective-permute-start(bf16[2,2,128,128]{3,2,1,0:T(8,128)(2,1)S(1)} %get-tuple-element.56), channel_id=1, source_target_pairs={{0,4},{1,5},{2,6},{3,7},{4,8},{5,9},{6,10},{7,11},{8,12},{9,13},{1... | collective-permute-start | bytes 393224 | tf_op jit(solution)/shard_map/ppermute | solution.py:359
  24.9 10.1 %collective-permute-start.6 = (bf16[256,256]{1,0:T(8,128)(2,1)S(1)}, bf16[256,256]{1,0:T(8,128)(2,1)S(1)}, u32[]{:S(2)}, u32[]{:S(2)}) collective-permute-start(bf16[256,256]{1,0:T(8,128)(2,1)S(1)} %collective-permute-done.4.refs_9_), channel_id=1, source_target_pairs={{0,4},{1,5},{2,6},{3,7},{4,8},{5,9},{6,10},{7,11},{8,12},{9,13},{1... | collective-permute-start | bytes 393224 | tf_op jit(solution)/shard_map/ppermute | solution.py:359
  29.3 19.9 %collective-permute-start = (bf16[128,1536]{1,0:T(8,128)(2,1)S(1)}, bf16[128,1536]{1,0:T(8,128)(2,1)S(1)}, u32[]{:S(2)}, u32[]{:S(2)}) collective-permute-start(bf16[128,1536]{1,0:T(8,128)(2,1)S(1)} %copy-done.8), channel_id=1, source_target_pairs={{0,2},{1,3},{2,0},{3,1},{4,6},{5,7},{6,4},{7,5},{8,10},{9,11},{10,... | collective-permute-start | bytes 1179656 | tf_op jit(solution)/shard_map/ppermute | solution.py:359
  30.9 10.0 %collective-permute-start.12 = (bf16[2,2,128,128]{3,2,1,0:T(8,128)(2,1)S(1)}, bf16[2,2,128,128]{3,2,1,0:T(8,128)(2,1)S(1)}, u32[]{:S(2)}, u32[]{:S(2)}) collective-permute-start(bf16[2,2,128,128]{3,2,1,0:T(8,128)(2,1)S(1)} %get-tuple-element.57), channel_id=1, source_target_pairs={{0,8},{1,9},{2,10},{3,11},{4,12},{5,13},{6,14},{7,15},{8,0},{9,1},... | collective-permute-start | bytes 393224 | tf_op jit(solution)/shard_map/ppermute | solution.py:359
  32.2 19.6 %copy-start = (bf16[128,1024]{1,0:T(8,128)(2,1)S(1)}, bf16[128,1024]{1,0:T(8,128)(2,1)}, u32[]{:S(2)}) copy-start(bf16[128,1024]{1,0:T(8,128)(2,1)} %refs_0_.1) | copy-start | bytes 786436
  32.2 20.1 %copy-start.7 = (bf16[256,256]{1,0:T(8,128)(2,1)S(1)}, bf16[256,256]{1,0:T(8,128)(2,1)}, u32[]{:S(2)}) copy-start(bf16[256,256]{1,0:T(8,128)(2,1)} %get-tuple-element.74) | copy-start | bytes 393220
  32.2 11.4 %collective-permute-start.13 = (bf16[2,2,128,128]{3,2,1,0:T(8,128)(2,1)S(1)}, bf16[2,2,128,128]{3,2,1,0:T(8,128)(2,1)S(1)}, u32[]{:S(2)}, u32[]{:S(2)}) collective-permute-start(bf16[2,2,128,128]{3,2,1,0:T(8,128)(2,1)S(1)} %get-tuple-element.58), channel_id=1, source_target_pairs={{0,12},{1,13},{2,14},{3,15},{4,0},{5,1},{6,2},{7,3},{8,4},{9,5},{1... | collective-permute-start | bytes 393224 | tf_op jit(solution)/shard_map/ppermute | solution.py:359
  34.9 8.6 %collective-permute-start.10 = (bf16[256,256]{1,0:T(8,128)(2,1)S(1)}, bf16[256,256]{1,0:T(8,128)(2,1)S(1)}, u32[]{:S(2)}, u32[]{:S(2)}) collective-permute-start(bf16[256,256]{1,0:T(8,128)(2,1)S(1)} %copy-done.9), channel_id=1, source_target_pairs={{0,2},{1,3},{2,0},{3,1},{4,6},{5,7},{6,4},{7,5},{8,10},{9,11},{10,... | collective-permute-start | bytes 393224 | tf_op jit(solution)/shard_map/ppermute | solution.py:359
  36.6 6.9 %collective-permute-start.9 = (bf16[256,256]{1,0:T(8,128)(2,1)S(1)}, bf16[256,256]{1,0:T(8,128)(2,1)S(1)}, u32[]{:S(2)}, u32[]{:S(2)}) collective-permute-start(bf16[256,256]{1,0:T(8,128)(2,1)S(1)} %collective-permute-done.7.refs_10_), channel_id=1, source_target_pairs={{0,4},{1,5},{2,6},{3,7},{4,8},{5,9},{6,10},{7,11},{8,12},{9,13},{1... | collective-permute-start | bytes 393224 | tf_op jit(solution)/shard_map/ppermute | solution.py:359
  40.9 8.2 %collective-permute-start.8 = (bf16[256,256]{1,0:T(8,128)(2,1)S(1)}, bf16[256,256]{1,0:T(8,128)(2,1)S(1)}, u32[]{:S(2)}, u32[]{:S(2)}) collective-permute-start(bf16[256,256]{1,0:T(8,128)(2,1)S(1)} %collective-permute-done.6.refs_11_), channel_id=1, source_target_pairs={{0,4},{1,5},{2,6},{3,7},{4,8},{5,9},{6,10},{7,11},{8,12},{9,13},{1... | collective-permute-start | bytes 393224 | tf_op jit(solution)/shard_map/ppermute | solution.py:359
  43.5 8.1 %collective-permute-start.14 = (bf16[256,256]{1,0:T(8,128)(2,1)S(1)}, bf16[256,256]{1,0:T(8,128)(2,1)S(1)}, u32[]{:S(2)}, u32[]{:S(2)}) collective-permute-start(bf16[256,256]{1,0:T(8,128)(2,1)S(1)} %collective-permute-done.9.refs_12_), channel_id=1, source_target_pairs={{0,4},{1,5},{2,6},{3,7},{4,8},{5,9},{6,10},{7,11},{8,12},{9,13},{1... | collective-permute-start | bytes 393224 | tf_op jit(solution)/shard_map/ppermute | solution.py:359
  51.7 3.2 %collective-permute-start.15 = (bf16[384,1024]{1,0:T(8,128)(2,1)S(1)}, bf16[384,1024]{1,0:T(8,128)(2,1)S(1)}, u32[]{:S(2)}, u32[]{:S(2)}) collective-permute-start(bf16[384,1024]{1,0:T(8,128)(2,1)S(1)} %shard_map.94), channel_id=1, source_target_pairs={{0,1},{1,0},{2,3},{3,2},{4,5},{5,4},{6,7},{7,6},{8,9},{9,8},{10,11... | collective-permute-start | bytes 2359304 | tf_op jit(solution)/shard_map/ppermute | solution.py:359
  51.8 3.1 %collective-permute-start.3 = (bf16[128,1024]{1,0:T(8,128)(2,1)S(1)}, bf16[128,1024]{1,0:T(8,128)(2,1)S(1)}, u32[]{:S(2)}, u32[]{:S(2)}) collective-permute-start(bf16[128,1024]{1,0:T(8,128)(2,1)S(1)} %copy-done), channel_id=1, source_target_pairs={{0,1},{1,0},{2,3},{3,2},{4,5},{5,4},{6,7},{7,6},{8,9},{9,8},{10,11... | collective-permute-start | bytes 786440 | tf_op jit(solution)/shard_map/ppermute | solution.py:359
  52.3 10.1 %collective-permute-start.24 = (bf16[2,256,256]{2,1,0:T(8,128)(2,1)S(1)}, bf16[2,256,256]{2,1,0:T(8,128)(2,1)S(1)}, u32[]{:S(2)}, u32[]{:S(2)}) collective-permute-start(bf16[2,256,256]{2,1,0:T(8,128)(2,1)S(1)} %pad_maximum_fusion.refs_0_), channel_id=1, source_target_pairs={{0,4},{1,5},{2,6},{3,7},{4,8},{5,9},{6,10},{7,11},{8,12},{9,13},{1... | collective-permute-start | bytes 786440 | tf_op jit(solution)/shard_map/ppermute | solution.py:359
  54.8 0.9 copy-start.2
  54.8 23.1 %copy-start.5 = (bf16[16,256,128]{2,1,0:T(8,128)(2,1)S(1)}, bf16[16,256,128]{2,1,0:T(8,128)(2,1)}, u32[]{:S(2)}) copy-start(bf16[16,256,128]{2,1,0:T(8,128)(2,1)} %constant.4.clone.refs_9_) | copy-start | bytes 3145732
  54.8 23.1 %copy-start.6 = (bf16[16,256,128]{2,1,0:T(8,128)(2,1)S(1)}, bf16[16,256,128]{2,1,0:T(8,128)(2,1)}, u32[]{:S(2)}) copy-start(bf16[16,256,128]{2,1,0:T(8,128)(2,1)} %constant.5.clone.refs_10_) | copy-start | bytes 3145732
  62.4 13.6 %collective-permute-start.25 = (bf16[2,256,256]{2,1,0:T(8,128)(2,1)S(1)}, bf16[2,256,256]{2,1,0:T(8,128)(2,1)S(1)}, u32[]{:S(2)}, u32[]{:S(2)}) collective-permute-start(bf16[2,256,256]{2,1,0:T(8,128)(2,1)S(1)} %collective-permute-done.24.refs_1_), channel_id=1, source_target_pairs={{0,4},{1,5},{2,6},{3,7},{4,8},{5,9},{6,10},{7,11},{8,12},{9,13},{1... | collective-permute-start | bytes 786440 | tf_op jit(solution)/shard_map/ppermute | solution.py:359
  63.1 14.8 %collective-permute-start.19 = (bf16[4,2,128,128]{3,2,1,0:T(8,128)(2,1)S(1)}, bf16[4,2,128,128]{3,2,1,0:T(8,128)(2,1)S(1)}, u32[]{:S(2)}, u32[]{:S(2)}) collective-permute-start(bf16[4,2,128,128]{3,2,1,0:T(8,128)(2,1)S(1)} %shard_map.95), channel_id=1, source_target_pairs={{0,2},{1,3},{2,0},{3,1},{4,6},{5,7},{6,4},{7,5},{8,10},{9,11},{10,... | collective-permute-start | bytes 786440 | tf_op jit(solution)/shard_map/ppermute | solution.py:359
  63.1 11.6 %collective-permute-start.16 = (bf16[256,128]{1,0:T(8,128)(2,1)S(1)}, bf16[256,128]{1,0:T(8,128)(2,1)S(1)}, u32[]{:S(2)}, u32[]{:S(2)}) collective-permute-start(bf16[256,128]{1,0:T(8,128)(2,1)S(1)} %get-tuple-element.66), channel_id=1, source_target_pairs={{0,4},{1,5},{2,6},{3,7},{4,8},{5,9},{6,10},{7,11},{8,12},{9,13},{1... | collective-permute-start | bytes 196616 | tf_op jit(solution)/shard_map/ppermute | solution.py:359
  63.4 12.7 %collective-permute-start.17 = (bf16[256,128]{1,0:T(8,128)(2,1)S(1)}, bf16[256,128]{1,0:T(8,128)(2,1)S(1)}, u32[]{:S(2)}, u32[]{:S(2)}) collective-permute-start(bf16[256,128]{1,0:T(8,128)(2,1)S(1)} %get-tuple-element.67), channel_id=1, source_target_pairs={{0,8},{1,9},{2,10},{3,11},{4,12},{5,13},{6,14},{7,15},{8,0},{9,1},... | collective-permute-start | bytes 196616 | tf_op jit(solution)/shard_map/ppermute | solution.py:359
  67.0 9.0 %collective-permute-start.18 = (bf16[256,128]{1,0:T(8,128)(2,1)S(1)}, bf16[256,128]{1,0:T(8,128)(2,1)S(1)}, u32[]{:S(2)}, u32[]{:S(2)}) collective-permute-start(bf16[256,128]{1,0:T(8,128)(2,1)S(1)} %get-tuple-element.68), channel_id=1, source_target_pairs={{0,12},{1,13},{2,14},{3,15},{4,0},{5,1},{6,2},{7,3},{8,4},{9,5},{1... | collective-permute-start | bytes 196616 | tf_op jit(solution)/shard_map/ppermute | solution.py:359
  76.1 14.3 %collective-permute-start.26 = (bf16[2,256,256]{2,1,0:T(8,128)(2,1)S(1)}, bf16[2,256,256]{2,1,0:T(8,128)(2,1)S(1)}, u32[]{:S(2)}, u32[]{:S(2)}) collective-permute-start(bf16[2,256,256]{2,1,0:T(8,128)(2,1)S(1)} %collective-permute-done.25.refs_2_), channel_id=1, source_target_pairs={{0,4},{1,5},{2,6},{3,7},{4,8},{5,9},{6,10},{7,11},{8,12},{9,13},{1... | collective-permute-start | bytes 786440 | tf_op jit(solution)/shard_map/ppermute | solution.py:359
  79.8 8.8 %collective-permute-start.20 = (bf16[256,128]{1,0:T(8,128)(2,1)S(1)}, bf16[256,128]{1,0:T(8,128)(2,1)S(1)}, u32[]{:S(2)}, u32[]{:S(2)}) collective-permute-start(bf16[256,128]{1,0:T(8,128)(2,1)S(1)} %get-tuple-element.70), channel_id=1, source_target_pairs={{0,4},{1,5},{2,6},{3,7},{4,8},{5,9},{6,10},{7,11},{8,12},{9,13},{1... | collective-permute-start | bytes 196616 | tf_op jit(solution)/shard_map/ppermute | solution.py:359
  79.8 10.5 %collective-permute-start.21 = (bf16[256,128]{1,0:T(8,128)(2,1)S(1)}, bf16[256,128]{1,0:T(8,128)(2,1)S(1)}, u32[]{:S(2)}, u32[]{:S(2)}) collective-permute-start(bf16[256,128]{1,0:T(8,128)(2,1)S(1)} %get-tuple-element.71), channel_id=1, source_target_pairs={{0,8},{1,9},{2,10},{3,11},{4,12},{5,13},{6,14},{7,15},{8,0},{9,1},... | collective-permute-start | bytes 196616 | tf_op jit(solution)/shard_map/ppermute | solution.py:359
  82.3 8.0 %collective-permute-start.22 = (bf16[256,128]{1,0:T(8,128)(2,1)S(1)}, bf16[256,128]{1,0:T(8,128)(2,1)S(1)}, u32[]{:S(2)}, u32[]{:S(2)}) collective-permute-start(bf16[256,128]{1,0:T(8,128)(2,1)S(1)} %get-tuple-element.72), channel_id=1, source_target_pairs={{0,12},{1,13},{2,14},{3,15},{4,0},{5,1},{6,2},{7,3},{8,4},{9,5},{1... | collective-permute-start | bytes 196616 | tf_op jit(solution)/shard_map/ppermute | solution.py:359
  90.5 0.7 copy-start.4
  90.5 2.5 %collective-permute-start.27 = (bf16[4,256,256]{2,1,0:T(8,128)(2,1)S(1)}, bf16[4,256,256]{2,1,0:T(8,128)(2,1)S(1)}, u32[]{:S(2)}, u32[]{:S(2)}) collective-permute-start(bf16[4,256,256]{2,1,0:T(8,128)(2,1)S(1)} %get-tuple-element.80), channel_id=1, source_target_pairs={{0,1},{1,0},{2,3},{3,2},{4,5},{5,4},{6,7},{7,6},{8,9},{9,8},{10,11... | collective-permute-start | bytes 1572872 | tf_op jit(solution)/shard_map/ppermute | solution.py:359
  91.4 1.6 %collective-permute-start.23 = (bf16[512,256]{1,0:T(8,128)(2,1)S(1)}, bf16[512,256]{1,0:T(8,128)(2,1)S(1)}, u32[]{:S(2)}, u32[]{:S(2)}) collective-permute-start(bf16[512,256]{1,0:T(8,128)(2,1)S(1)} %shard_map.98.gated), channel_id=1, source_target_pairs={{0,1},{1,0},{2,3},{3,2},{4,5},{5,4},{6,7},{7,6},{8,9},{9,8},{10,11... | collective-permute-start | bytes 786440 | tf_op jit(solution)/shard_map/ppermute | solution.py:359
  94.5 10.2 %collective-permute-start.28 = (bf16[128,1024]{1,0:T(8,128)(2,1)S(1)}, bf16[128,1024]{1,0:T(8,128)(2,1)S(1)}, u32[]{:S(2)}, u32[]{:S(2)}) collective-permute-start(bf16[128,1024]{1,0:T(8,128)(2,1)S(1)} %get-tuple-element.82), channel_id=1, source_target_pairs={{0,18},{1,19},{2,16},{3,17},{4,22},{5,23},{6,20},{7,21},{8,26},{9,... | collective-permute-start | bytes 786440 | tf_op jit(solution)/shard_map/ppermute | solution.py:359
  95.8 13.6 %collective-permute-start.29 = (bf16[128,1024]{1,0:T(8,128)(2,1)S(1)}, bf16[128,1024]{1,0:T(8,128)(2,1)S(1)}, u32[]{:S(2)}, u32[]{:S(2)}) collective-permute-start(bf16[128,1024]{1,0:T(8,128)(2,1)S(1)} %get-tuple-element.83), channel_id=1, source_target_pairs={{0,16},{1,17},{2,18},{3,19},{4,20},{5,21},{6,22},{7,23},{8,24},{9,... | collective-permute-start | bytes 786440 | tf_op jit(solution)/shard_map/ppermute | solution.py:359
  96.2 13.3 %collective-permute-start.30 = (bf16[128,1024]{1,0:T(8,128)(2,1)S(1)}, bf16[128,1024]{1,0:T(8,128)(2,1)S(1)}, u32[]{:S(2)}, u32[]{:S(2)}) collective-permute-start(bf16[128,1024]{1,0:T(8,128)(2,1)S(1)} %get-tuple-element.84), channel_id=1, source_target_pairs={{0,2},{1,3},{2,0},{3,1},{4,6},{5,7},{6,4},{7,5},{8,10},{9,11},{10,... | collective-permute-start | bytes 786440 | tf_op jit(solution)/shard_map/ppermute | solution.py:359

commit v6 on v5

--- a/solution.py
+++ b/solution.py
@@ -82,18 +82,22 @@
         copy.wait()
 
 
-def cut_weights(value, out, own_v, away_v, own_o, away_o, sem):
-    moves = [(value.at[:, quarter(0)], own_v), (value.at[:, quarter(1)], away_v)]
-    copied(moves + [(out.at[:, quarter(0)], own_o), (out.at[:, quarter(1)], away_o)], sem)
-
-
-def cut_messages(tokens, key, query, after, m1, m2, m3, own, sem):
-    moves = []
+def cut_first(value, own_v, sem):
+    y, _, _, _ = place()
+    copied([(value.at[:, pl.ds(pl.multiple_of(y * 512, 512), 512)], own_v)], sem)
+
+
+def cut_messages(tokens, key, query, out, filt, after, m1, m2, m3, own, own_o, away_o, away_f, sem):
+    _, x, _, _ = place()
+    moves = [(filt.at[:, :, :, quarter(1)], away_f)]
     for p, message in enumerate((own, m1, m2, m3)):
+        column = 1 - x if p % 2 else x
+        for i in range(2):
+            lanes = pl.ds(pl.multiple_of(i * 512 + column * 256, 256), 256)
+            moves.append((tokens.at[:, lanes], message.at[:, pl.ds(512 + i * 256, 256)]))
         moves.append((key.at[:, quarter(p)], message.at[:, pl.ds(0, 256)]))
         moves.append((query.at[:, quarter(p)], message.at[:, pl.ds(256, 256)]))
-        if p:
-            moves.append((tokens, message.at[:, pl.ds(512, 1024)]))
+    moves += [(out.at[:, quarter(0)], own_o), (out.at[:, quarter(1)], away_o)]
     copied(moves, sem)
 
 
@@ -104,23 +108,25 @@
             out_shape=out_shape,
             in_specs=[pl.BlockSpec(memory_space=pltpu.MemorySpace.HBM)] * len(operands),
             out_specs=[pl.BlockSpec(memory_space=pltpu.VMEM)] * len(out_shape),
-            scratch_shapes=[pltpu.SemaphoreType.DMA((12,))],
+            scratch_shapes=[pltpu.SemaphoreType.DMA((19,))],
             compiler_params=pltpu.CompilerParams(vmem_limit_bytes=61 * 1024 * 1024),
         )(*operands)
 
     return call
 
 
-def pack_filter(filt, *refs):
+def pack_filter(filt, near, *refs):
     y, x, z, _ = place()
     packed, outs = refs[4], refs[:4]
     low = low_lanes((128, 128))
     for k in range(2):
-        column = 1 - x if k else x
         for j in range(2):
-            base = pl.multiple_of(y * 512 + column * 256 + j * 128, 128)
+            base = pl.multiple_of(y * 512 + x * 256 + j * 128, 128)
             for part in range(2):
-                pair = [filt[part, i, :, pl.ds(base, 128)].astype(F32) for i in range(2)]
+                if k:
+                    pair = [near[part, i, :, pl.ds(j * 128, 128)].astype(F32) for i in range(2)]
+                else:
+                    pair = [filt[part, i, :, pl.ds(base, 128)].astype(F32) for i in range(2)]
                 one, two = both(*pair, low)
                 packed[2 * j, k, part] = one
                 packed[2 * j + 1, k, part] = two
@@ -128,56 +134,49 @@
         outs[r][...] = packed[lax.rem(z + r, 4)]
 
 
-def pass_filter(f0, f1, f2, f3, out):
-    for r, block in enumerate((f0, f1, f2, f3)):
-        out[r] = block[1]
-
-
-def join_tokens(m1, m2, m3, out):
-    for p, message in enumerate((m1, m2, m3)):
-        out[pl.ds(p * 128, 128), :] = message[:, pl.ds(512, 1024)]
-
-
-def value_kernel(*refs):
-    mine, other, gates, pieces = refs[:4], refs[4:6], refs[6], refs[7:15]
-    drive, outs = refs[15], refs[16:20]
-    acc, packed = refs[20], refs[21]
+def join_tokens(*refs):
+    for p, message in enumerate(refs[:4]):
+        refs[4][pl.ds(p * 128, 128), :] = message[:, pl.ds(512, 512)]
+
+
+def value_kernel(mine, other, w0, w1, w2, w3, keep, give, acc):
     _, x, z, c = place()
-    acc[...] = jnp.zeros_like(acc)
-
-    def gather(blocks, base):
-        near, far = pl.multiple_of(base, 256), pl.multiple_of(base + 512, 256)
-        lanes = [near] + [near if len(blocks) == 2 else far] * 3
-        return jnp.concatenate([b[:, pl.ds(at, 256)] for b, at in zip(blocks, lanes)], axis=0)
-
-    for r in range(4):
+    for r, piece in enumerate((w0, w1, w2, w3)):
         owner = lax.rem(z - r + 4, 4)
-        for k in range(2):
-            row = 1 - x if k else x
-            base = lax.rem(owner, 2) * 512 + row * 256
-            piece = pieces[2 * r + k]
-
-            @pl.when(owner // 2 == c)
-            def _():
-                acc[...] += dot(gather(mine, base), piece[...])
-
-            @pl.when(owner // 2 != c)
-            def _():
-                acc[...] += dot(gather(other, base), piece[...])
-
+        lanes = pl.ds(pl.multiple_of(lax.rem(owner, 2) * 256, 256), 256)
+
+        @pl.when(lax.div(owner, 2) == c)
+        def _():
+            term = dot(mine[:, lanes], piece[...])
+            acc[...] = acc[...] + term if r else term
+
+        @pl.when(lax.div(owner, 2) != c)
+        def _():
+            term = dot(other[:, lanes], piece[...])
+            acc[...] = acc[...] + term if r else term
+
+    keep[...] = acc[:, pl.ds(pl.multiple_of(x * 256, 256), 256)]
+    away = pl.ds(pl.multiple_of(256 - x * 256, 256), 256)
     for p in range(4):
+        give[pl.ds(p * 128, 128), :] = acc[pl.ds((p ^ 1) * 128, 128), away].astype(BF16)
+
+
+def drive_kernel(keep, taken, g0, g1, g2, g3, skip, direct, o0, o1, o2, o3, drive, packed):
+    _, _, z, _ = place()
+    for p, gate in enumerate((g0, g1, g2, g3)):
         rows = pl.ds(p * 128, 128)
-        gate = (mine[p] if p else gates)[:, 0:256]
-        value = acc[rows, :].astype(BF16).astype(F32)
-        drive[rows, :] = (gate.astype(F32) * value).astype(BF16)
+        value = (keep[rows, :] + taken[rows, :].astype(F32)).astype(BF16).astype(F32)
+        held = (gate[:, 0:256].astype(F32) * value).astype(BF16)
+        drive[rows, :] = held
+        direct[rows, :] = skip[:, quarter(0)] * held.astype(F32)
     low = low_lanes((256, 128))
     for j in range(2):
         lanes = pl.ds(j * 128, 128)
         first = drive[pl.ds(0, 256), lanes].astype(F32)
         second = drive[pl.ds(256, 256), lanes].astype(F32)
         packed[2 * j], packed[2 * j + 1] = both(first, second, low)
-    for r in range(4):
-        outs[r][...] = packed[lax.rem(z + r, 4)]
+    for r, out in enumerate((o0, o1, o2, o3)):
+        out[...] = packed[lax.rem(z + r, 4)]
 
 
 def add(a, b):
@@ -227,13 +226,13 @@
 
 
 def conv_kernel(*refs):
-    drives, filters, (beside, table, table_t) = refs[:4], refs[4:8], refs[8:11]
-    outs, (data, filt, first, sums) = refs[11:15], refs[15:]
+    drives, filters, (table, table_t) = refs[:4], refs[4:8], refs[8:10]
+    outs, (data, filt, first, sums) = refs[10:14], refs[14:]
     _, x, z, _ = place()
     for r, block in enumerate(drives):
         base = 2 * lax.rem(z - r + 4, 4)
         filt[base + x] = filters[r][0]
-        filt[base + 1 - x] = beside[r]
+        filt[base + 1 - x] = filters[r][1]
         data[base + x] = block[pl.ds(0, 128), :]
         data[base + 1 - x] = block[pl.ds(128, 128), :]
     for i in range(8):
@@ -291,8 +290,8 @@
         out[pl.ds(128, 128), :] = data[base + 1 - x]
 
 
-def gate_kernel(e0, e1, e2, e3, drive, skip, gates, g1, g2, g3, gated, conv):
-    y, x, z, _ = place()
+def gate_kernel(e0, e1, e2, e3, direct, g0, g1, g2, g3, gated, conv):
+    _, _, z, _ = place()
     for r, block in enumerate((e0, e1, e2, e3)):
         conv[lax.rem(z - r + 4, 4)] = block[...]
     low = low_lanes((256, 128))
@@ -300,13 +299,11 @@
         lanes = pl.ds(j * 128, 128)
         even, odd = conv[2 * j].astype(F32), conv[2 * j + 1].astype(F32)
         parts = (jnp.where(low, even, half_turn(odd)), jnp.where(low, half_turn(even), odd))
-        for p, gate in enumerate((gates, g1, g2, g3)):
+        for p, gate in enumerate((g0, g1, g2, g3)):
             rows = pl.ds(p * 128, 128)
             own = parts[p // 2][(p % 2) * 128 : (p % 2) * 128 + 128]
-            at = pl.ds(pl.multiple_of(y * 512 + x * 256 + j * 128, 128), 128)
-            direct = skip[:, at] * drive[rows, lanes].astype(F32)
             query = gate[:, pl.ds(256 + j * 128, 128)].astype(F32)
-            gated[rows, lanes] = (query * (own + direct)).astype(BF16)
+            gated[rows, lanes] = (query * (own + direct[rows, lanes])).astype(BF16)
 
 
 def sort_weight(*refs):
@@ -375,44 +372,42 @@
 
     shape = jax.ShapeDtypeStruct
     block, square = shape((256, 128), BF16), shape((256, 256), BF16)
-    own_v, away_v, own_o, away_o = copy_kernel(cut_weights, [square] * 4)(w_value, w_out)
-    laid = [shape((128, w), BF16) for w in (1536, 1536, 1536, 512)]
-    *messages, gates = copy_kernel(cut_messages, laid)(tokens, gate_k, gate_q, own_v)
+    (own_v,) = copy_kernel(cut_first, [shape((256, 512), BF16)])(w_value)
+    laid = [shape((128, 1024), BF16)] * 4 + [square] * 2 + [shape((2, 2, 128, 256), BF16)]
+    *messages, own, own_o, away_o, away_f = copy_kernel(cut_messages, laid)(
+        tokens, gate_k, gate_q, w_out, filter_spectrum, own_v
+    )
+    near = to_x(away_f)
+    received = [to_peer(messages[p - 1], p) for p in (1, 2, 3)]
+    plane = [own] + received
     filters = in_vmem(
         pack_filter,
         [shape((2, 2, 128, 128), BF16)] * 4,
         [pltpu.VMEM((4, 2, 2, 128, 128), BF16)],
         moved=1 << 20,
-        )(after(filter_spectrum, messages[0]))
+    )(filter_spectrum, near)
     filters = [filters[0]] + [to_z(filters[r], r) for r in (1, 2, 3)]
-    received = [to_peer(messages[p - 1], p) for p in (1, 2, 3)]
-    b0 = to_x(away_v)
-    a1 = to_z(own_v, 1)
-    b1 = to_z(b0, 1)
-    a2 = to_z(after(a1, b0), 1)
-    b2 = to_z(after(b1, a1, received[1]), 1)
-    a3 = to_z(after(a2, b1, received[2]), 1)
-    got_o = to_x(after(away_o, b0))
-    b3 = to_z(after(b2, a2, got_o, *filters[1:]), 1)
-    ring = [own_v, b0, a1, b1, a2, b2, a3, b3]
-    passed = in_vmem(pass_filter, shape((4, 2, 128, 128), BF16), moved=1 << 20)(
-        after(filters[0], b2), *filters[1:]
-    )
-    beside = to_x(passed)
-    mine = [tokens] + received
-    first = after(received[0], a3, b3)
-    joined = in_vmem(join_tokens, shape((384, 1024), BF16), moved=2 << 20)(first, *received[1:])
-    other = [to_core(tokens), to_core(joined)]
+    v1 = to_z(own_v, 1)
+    v2 = to_z(after(v1, received[0], received[1]), 1)
+    mine = in_vmem(join_tokens, shape((512, 512), BF16), moved=1 << 20)(after(own, v2), *received)
+    v3 = to_z(after(v2, mine), 1)
+    other = to_core(mine)
+    got_o = to_x(after(away_o, v2))
     pair = jnp.stack([own_o, got_o])
-    hops = [pair, to_z(after(pair, a3), 1)]
-    gates = after(gates, passed)
+    hops = [pair, to_z(after(pair, v3), 1)]
+    keep, give = in_vmem(
+        value_kernel,
+        [shape((512, 256), F32), shape((512, 256), BF16)],
+        [pltpu.VMEM((512, 512), F32)],
+        flops=1 << 29,
+        moved=2 << 20,
+    )(after(mine, *filters[1:]), other, own_v, v1, v2, v3)
     drive, *sends = in_vmem(
-        value_kernel,
-        [shape((512, 256), BF16)] + [block] * 4,
-        [pltpu.VMEM((512, 256), F32), pltpu.VMEM((4, 256, 128), BF16)],
-        flops=1 << 29,
-        moved=4 << 20,
-    )(*mine, *other, gates, *ring)
+        drive_kernel,
+        [shape((512, 256), F32)] + [block] * 4,
+        [pltpu.VMEM((512, 256), BF16), pltpu.VMEM((4, 256, 128), BF16)],
+        moved=2 << 20,
+    )(keep, to_x(give), *plane, skip[None, :])
     columns = [sends[0]] + [to_z(sends[r], r) for r in (1, 2, 3)]
     hops.append(to_z(after(hops[1], drive), 1))
     hops.append(to_z(after(hops[2], *columns[1:]), 1))
@@ -428,7 +423,7 @@
         ],
         flops=1 << 30,
         moved=5 << 20,
-    )(*columns, *filters, beside, table, table_t)
+    )(*columns, *filters, table, table_t)
     rows = [sends[0]] + [to_z(sends[r], r) for r in (1, 2, 3)]
 
     hops[3] = after(hops[3], *rows[1:])
@@ -437,7 +432,7 @@
     theirs = to_core(give)
     gated = in_vmem(
         gate_kernel, shape((512, 256), BF16), [pltpu.VMEM((4, 256, 128), BF16)], moved=1 << 20
-    )(*rows, drive, skip[None, :], gates, *received)
+    )(*rows, drive, *plane)
     gated_other = to_core(gated)
     own, *sends = in_vmem(
         out_kernel,

time: 111 us -> 107 us (0.964)
  starting transfers between devices: 46.4 us -> 35.6 us
  waiting for transfers between devices: 50.7 us -> 58.3 us
    ppermute x31 -> x27, starting transfers between devices: 46.4 us -> 35.6 us  [permute(): return lax.ppermute(values, AXES, pairs)]
    ppermute x31 -> x27, waiting for transfers between devices: 50.7 us -> 58.3 us  [permute(): return lax.ppermute(values, AXES, pairs)]
  transfers between devices with their start and end apart: 31 -> 27, of which waited for: 14 -> 17; matrix products, arithmetic and copies ran while one was open for 0% -> 0% of each run, Pallas kernels for 4% -> 6%
where the time goes in v6:
time: 107 us
  waiting for transfers between devices  58.3 us (54%)
  starting transfers between devices  35.6 us (33%)
  Pallas kernels  10.2 us (10%)
  local copies, waits for them, and re-layouts  1.82 us (2%)
    ppermute x27, waiting for transfers between devices, permute(): return lax.ppermute(values, AXES, pairs)  58.3 us
    ppermute x27, starting transfers between devices, permute(): return lax.ppermute(values, AXES, pairs)  35.6 us
    pallas_call x8, Pallas kernels, call(): pl.pallas_call(kernel, out_shape=out_shape, in_specs=specs, out_specs=jax...  5.62 us
    pallas_call x2, Pallas kernels, call(): pl.pallas_call(kernel, out_shape=out_shape, in_specs=[pl.BlockSpec(memory...  4.57 us
  transfers between devices with their start and end apart: 27, of which 17 were waited for; matrix products, arithmetic and copies ran while one was open for 0% of the time, Pallas kernels for 6%

profile of v6, /device:TPU:0, one launch (start us, length us, event | category | flops | bytes accessed | tf_op | source)
XLA Modules:
  0.0 107.0 jit_solution(9332915168089234437)
XLA Ops:
  0.0 1.8 %shard_map.91.after.w0 = bf16[256,512]{1,0:T(8,128)(2,1)} custom-call(bf16[256,1024]{1,0:T(8,128)(2,1)} %value.1), custom_call_target="tpu_custom_call" | custom-call | tf_op jit(solution)/shard_map/pallas_call | solution.py:106
  1.8 3.1 %collective-permute-start = (bf16[256,512]{1,0:T(8,128)(2,1)}, bf16[256,512]{1,0:T(8,128)(2,1)S(1)}, u32[]{:S(2)}, u32[]{:S(2)}) collective-permute-start(bf16[256,512]{1,0:T(8,128)(2,1)} %shard_map.91.after.w0), channel_id=1, source_target_pairs={{0,4},{1,5},{2,6},{3,7},{4,8},{5,9},{6,10},{7,11},{8,12},{9,13},{1... | collective-permute-start | bytes 786440 | tf_op jit(solution)/shard_map/ppermute | solution.py:356
  4.9 2.7 %shard_map.92 = (bf16[128,1024]{1,0:T(8,128)(2,1)}, bf16[128,1024]{1,0:T(8,128)(2,1)}, bf16[128,1024]{1,0:T(8,128)(2,1)}, bf16[128,1024]{1,0:T(8,128)(2,1)}, bf1...) custom-call(bf16[128,1024]{1,0:T(8,128)(2,1)} %tokens.1, bf16[128,1024]{1,0:T(8,128)(2,1)} %key.1, ...), custom_call_target="tpu_custom_call" | custom-call | tf_op jit(solution)/shard_map/pallas_call | solution.py:106
  7.7 0.0 copy-start
  7.7 1.6 %collective-permute-start.1 = (bf16[128,1024]{1,0:T(8,128)(2,1)}, bf16[128,1024]{1,0:T(8,128)(2,1)S(1)}, u32[]{:S(2)}, u32[]{:S(2)}) collective-permute-start(bf16[128,1024]{1,0:T(8,128)(2,1)} %get-tuple-element.43), channel_id=1, source_target_pairs={{0,2},{1,3},{2,0},{3,1},{4,6},{5,7},{6,4},{7,5},{8,10},{9,11},{10,... | collective-permute-start | bytes 786440 | tf_op jit(solution)/shard_map/ppermute | solution.py:356
  9.2 1.5 %collective-permute-start.2 = (bf16[128,1024]{1,0:T(8,128)(2,1)}, bf16[128,1024]{1,0:T(8,128)(2,1)S(1)}, u32[]{:S(2)}, u32[]{:S(2)}) collective-permute-start(bf16[128,1024]{1,0:T(8,128)(2,1)} %get-tuple-element.44), channel_id=1, source_target_pairs={{0,16},{1,17},{2,18},{3,19},{4,20},{5,21},{6,22},{7,23},{8,24},{9,... | collective-permute-start | bytes 786440 | tf_op jit(solution)/shard_map/ppermute | solution.py:356
  10.8 2.7 %collective-permute-done.w1 = bf16[256,512]{1,0:T(8,128)(2,1)S(1)} collective-permute-done((bf16[256,512]{1,0:T(8,128)(2,1)}, bf16[256,512]{1,0:T(8,128)(2,1)S(1)}, u32[]{:S(2)}, u32[]{:S(2)}) %collective-permute-start) | collective-permute-done | bytes 262176 | tf_op jit(solution)/shard_map/ppermute | solution.py:356
  13.4 2.3 %collective-permute-done.1.refs_1_.g1 = bf16[128,1024]{1,0:T(8,128)(2,1)S(1)} collective-permute-done((bf16[128,1024]{1,0:T(8,128)(2,1)}, bf16[128,1024]{1,0:T(8,128)(2,1)S(1)}, u32[]{:S(2)}, u32[]{:S(2)}) %collective-permute-start.1) | collective-permute-done | bytes 262176 | tf_op jit(solution)/shard_map/ppermute | solution.py:356
  15.7 1.2 %collective-permute-done.2.refs_2_.g2 = bf16[128,1024]{1,0:T(8,128)(2,1)S(1)} collective-permute-done((bf16[128,1024]{1,0:T(8,128)(2,1)}, bf16[128,1024]{1,0:T(8,128)(2,1)S(1)}, u32[]{:S(2)}, u32[]{:S(2)}) %collective-permute-start.2) | collective-permute-done | bytes 262176 | tf_op jit(solution)/shard_map/ppermute | solution.py:356
  16.9 1.6 %collective-permute-start.3 = (bf16[256,512]{1,0:T(8,128)(2,1)S(1)}, bf16[256,512]{1,0:T(8,128)(2,1)S(1)}, u32[]{:S(2)}, u32[]{:S(2)}) collective-permute-start(bf16[256,512]{1,0:T(8,128)(2,1)S(1)} %collective-permute-done.w1), channel_id=1, source_target_pairs={{0,4},{1,5},{2,6},{3,7},{4,8},{5,9},{6,10},{7,11},{8,12},{9,13},{1... | collective-permute-start | bytes 786440 | tf_op jit(solution)/shard_map/ppermute | solution.py:356
  18.5 1.5 %collective-permute-start.4 = (bf16[128,1024]{1,0:T(8,128)(2,1)}, bf16[128,1024]{1,0:T(8,128)(2,1)S(1)}, u32[]{:S(2)}, u32[]{:S(2)}) collective-permute-start(bf16[128,1024]{1,0:T(8,128)(2,1)} %get-tuple-element.47), channel_id=1, source_target_pairs={{0,18},{1,19},{2,16},{3,17},{4,22},{5,23},{6,20},{7,21},{8,26},{9,... | collective-permute-start | bytes 786440 | tf_op jit(solution)/shard_map/ppermute | solution.py:356
  20.0 5.3 %collective-permute-done.3.w2 = bf16[256,512]{1,0:T(8,128)(2,1)S(1)} collective-permute-done((bf16[256,512]{1,0:T(8,128)(2,1)S(1)}, bf16[256,512]{1,0:T(8,128)(2,1)S(1)}, u32[]{:S(2)}, u32[]{:S(2)}) %collective-permute-start.3) | collective-permute-done | bytes 262176 | tf_op jit(solution)/shard_map/ppermute | solution.py:356
  25.3 0.7 collective-permute-done.4.refs_3_.g3
  26.0 0.9 copy-done.2
  27.0 0.1 collective-permute-start.9
  27.1 0.8 copy-done.8
  27.9 0.5 collective-permute-start.5
  28.4 1.6 %collective-permute-start.10 = (bf16[256,512]{1,0:T(8,128)(2,1)S(1)}, bf16[256,512]{1,0:T(8,128)(2,1)S(1)}, u32[]{:S(2)}, u32[]{:S(2)}) collective-permute-start(bf16[256,512]{1,0:T(8,128)(2,1)S(1)} %collective-permute-done.3.w2), channel_id=1, source_target_pairs={{0,4},{1,5},{2,6},{3,7},{4,8},{5,9},{6,10},{7,11},{8,12},{9,13},{1... | collective-permute-start | bytes 786440 | tf_op jit(solution)/shard_map/ppermute | solution.py:356
  30.0 5.8 %collective-permute-done.5.near = bf16[2,2,128,256]{3,2,1,0:T(8,128)(2,1)S(1)} collective-permute-done((bf16[2,2,128,256]{3,2,1,0:T(8,128)(2,1)S(1)}, bf16[2,2,128,256]{3,2,1,0:T(8,128)(2,1)S(1)}, u32[]{:S(2)}, u32[]{:S(2)}) %collective-permute-start.5) | collective-permute-done | bytes 262176 | tf_op jit(solution)/shard_map/ppermute | solution.py:356
  35.8 0.3 shard_map.94
  36.1 1.6 %collective-permute-start.6 = (bf16[2,2,128,128]{3,2,1,0:T(8,128)(2,1)S(1)}, bf16[2,2,128,128]{3,2,1,0:T(8,128)(2,1)S(1)}, u32[]{:S(2)}, u32[]{:S(2)}) collective-permute-start(bf16[2,2,128,128]{3,2,1,0:T(8,128)(2,1)S(1)} %get-tuple-element.49), channel_id=1, source_target_pairs={{0,4},{1,5},{2,6},{3,7},{4,8},{5,9},{6,10},{7,11},{8,12},{9,13},{1... | collective-permute-start | bytes 393224 | tf_op jit(solution)/shard_map/ppermute | solution.py:356
  37.7 1.2 %collective-permute-start.7 = (bf16[2,2,128,128]{3,2,1,0:T(8,128)(2,1)S(1)}, bf16[2,2,128,128]{3,2,1,0:T(8,128)(2,1)S(1)}, u32[]{:S(2)}, u32[]{:S(2)}) collective-permute-start(bf16[2,2,128,128]{3,2,1,0:T(8,128)(2,1)S(1)} %get-tuple-element.50), channel_id=1, source_target_pairs={{0,8},{1,9},{2,10},{3,11},{4,12},{5,13},{6,14},{7,15},{8,0},{9,1},... | collective-permute-start | bytes 393224 | tf_op jit(solution)/shard_map/ppermute | solution.py:356
  39.0 1.4 %collective-permute-start.8 = (bf16[2,2,128,128]{3,2,1,0:T(8,128)(2,1)S(1)}, bf16[2,2,128,128]{3,2,1,0:T(8,128)(2,1)S(1)}, u32[]{:S(2)}, u32[]{:S(2)}) collective-permute-start(bf16[2,2,128,128]{3,2,1,0:T(8,128)(2,1)S(1)} %get-tuple-element.51), channel_id=1, source_target_pairs={{0,12},{1,13},{2,14},{3,15},{4,0},{5,1},{6,2},{7,3},{8,4},{9,5},{1... | collective-permute-start | bytes 393224 | tf_op jit(solution)/shard_map/ppermute | solution.py:356
  40.4 4.0 %collective-permute-done.6.refs_5_ = bf16[2,2,128,128]{3,2,1,0:T(8,128)(2,1)S(1)} collective-permute-done((bf16[2,2,128,128]{3,2,1,0:T(8,128)(2,1)S(1)}, bf16[2,2,128,128]{3,2,1,0:T(8,128)(2,1)S(1)}, u32[]{:S(2)}, u32[]{:S(2)}) %collective-permute-start.6) | collective-permute-done | bytes 131104 | tf_op jit(solution)/shard_map/ppermute | solution.py:356
  44.4 0.5 collective-permute-start.19
  45.0 2.9 %collective-permute-done.7.refs_6_ = bf16[2,2,128,128]{3,2,1,0:T(8,128)(2,1)S(1)} collective-permute-done((bf16[2,2,128,128]{3,2,1,0:T(8,128)(2,1)S(1)}, bf16[2,2,128,128]{3,2,1,0:T(8,128)(2,1)S(1)}, u32[]{:S(2)}, u32[]{:S(2)}) %collective-permute-start.7) | collective-permute-done | bytes 131104 | tf_op jit(solution)/shard_map/ppermute | solution.py:356
  47.9 0.0 collective-permute-done.8.refs_7_
  47.9 0.0 collective-permute-done.10.w3
  47.9 0.0 collective-permute-done.9.other
  47.9 1.3 %shard_map.95 = (f32[512,256]{1,0:T(8,128)S(1)}, bf16[512,256]{1,0:T(8,128)(2,1)S(1)}) custom-call(bf16[512,512]{1,0:T(8,128)(2,1)S(1)} %shard_map.93.mine, bf16[512,512]{1,0:T(8,128)(2,1)S(1)} %collective-permute-done.9.other, bf16[256,512]{1,0:T(8,128)(2,1)S(1)} %copy-done.1, bf16[256,512]{1,0:T(8,128)(2,1)S(1)} %collective-permute-done.w1, ...), custom_call_target="tpu_custom_call" | custom-call | flops 536870912 | bytes 2097152 | tf_op jit(solution)/shard_map/pallas_call | solution.py:37
  49.2 0.6 collective-permute-start.11
  49.8 0.0 collective-permute-done.19
  49.8 0.0 copy-start.6
  49.8 0.0 copy-start.5
  49.8 3.3 %collective-permute-start.20 = (bf16[2,256,256]{2,1,0:T(8,128)(2,1)S(1)}, bf16[2,256,256]{2,1,0:T(8,128)(2,1)S(1)}, u32[]{:S(2)}, u32[]{:S(2)}) collective-permute-start(bf16[2,256,256]{2,1,0:T(8,128)(2,1)S(1)} %pad_maximum_fusion.refs_0_), channel_id=1, source_target_pairs={{0,4},{1,5},{2,6},{3,7},{4,8},{5,9},{6,10},{7,11},{8,12},{9,13},{1... | collective-permute-start | bytes 786440 | tf_op jit(solution)/shard_map/ppermute | solution.py:356
  53.2 4.2 %collective-permute-done.11.taken = bf16[512,256]{1,0:T(8,128)(2,1)S(1)} collective-permute-done((bf16[512,256]{1,0:T(8,128)(2,1)S(1)}, bf16[512,256]{1,0:T(8,128)(2,1)S(1)}, u32[]{:S(2)}, u32[]{:S(2)}) %collective-permute-start.11) | collective-permute-done | bytes 262176 | tf_op jit(solution)/shard_map/ppermute | solution.py:356
  57.4 0.4 shard_map.96
  57.7 1.8 %collective-permute-done.20.refs_1_ = bf16[2,256,256]{2,1,0:T(8,128)(2,1)S(1)} collective-permute-done((bf16[2,256,256]{2,1,0:T(8,128)(2,1)S(1)}, bf16[2,256,256]{2,1,0:T(8,128)(2,1)S(1)}, u32[]{:S(2)}, u32[]{:S(2)}) %collective-permute-start.20) | collective-permute-done | bytes 262176 | tf_op jit(solution)/shard_map/ppermute | solution.py:356
  59.6 1.6 %collective-permute-start.21 = (bf16[2,256,256]{2,1,0:T(8,128)(2,1)S(1)}, bf16[2,256,256]{2,1,0:T(8,128)(2,1)S(1)}, u32[]{:S(2)}, u32[]{:S(2)}) collective-permute-start(bf16[2,256,256]{2,1,0:T(8,128)(2,1)S(1)} %collective-permute-done.20.refs_1_), channel_id=1, source_target_pairs={{0,4},{1,5},{2,6},{3,7},{4,8},{5,9},{6,10},{7,11},{8,12},{9,13},{1... | collective-permute-start | bytes 786440 | tf_op jit(solution)/shard_map/ppermute | solution.py:356
  61.2 0.6 collective-permute-start.12
  61.8 2.2 %collective-permute-start.13 = (bf16[256,128]{1,0:T(8,128)(2,1)S(1)}, bf16[256,128]{1,0:T(8,128)(2,1)S(1)}, u32[]{:S(2)}, u32[]{:S(2)}) collective-permute-start(bf16[256,128]{1,0:T(8,128)(2,1)S(1)} %get-tuple-element.58), channel_id=1, source_target_pairs={{0,8},{1,9},{2,10},{3,11},{4,12},{5,13},{6,14},{7,15},{8,0},{9,1},... | collective-permute-start | bytes 196616 | tf_op jit(solution)/shard_map/ppermute | solution.py:356
  64.0 1.0 collective-permute-start.14
  65.0 6.1 %collective-permute-done.12.refs_1_ = bf16[256,128]{1,0:T(8,128)(2,1)S(1)} collective-permute-done((bf16[256,128]{1,0:T(8,128)(2,1)S(1)}, bf16[256,128]{1,0:T(8,128)(2,1)S(1)}, u32[]{:S(2)}, u32[]{:S(2)}) %collective-permute-start.12) | collective-permute-done | bytes 65568 | tf_op jit(solution)/shard_map/ppermute | solution.py:356
  71.1 1.4 %collective-permute-done.13.refs_2_ = bf16[256,128]{1,0:T(8,128)(2,1)S(1)} collective-permute-done((bf16[256,128]{1,0:T(8,128)(2,1)S(1)}, bf16[256,128]{1,0:T(8,128)(2,1)S(1)}, u32[]{:S(2)}, u32[]{:S(2)}) %collective-permute-start.13) | collective-permute-done | bytes 65568 | tf_op jit(solution)/shard_map/ppermute | solution.py:356
  72.5 0.0 collective-permute-done.14.refs_3_
  72.5 1.9 %collective-permute-start.22 = (bf16[2,256,256]{2,1,0:T(8,128)(2,1)S(1)}, bf16[2,256,256]{2,1,0:T(8,128)(2,1)S(1)}, u32[]{:S(2)}, u32[]{:S(2)}) collective-permute-start(bf16[2,256,256]{2,1,0:T(8,128)(2,1)S(1)} %collective-permute-done.21.refs_2_), channel_id=1, source_target_pairs={{0,4},{1,5},{2,6},{3,7},{4,8},{5,9},{6,10},{7,11},{8,12},{9,13},{1... | collective-permute-start | bytes 786440 | tf_op jit(solution)/shard_map/ppermute | solution.py:356
  74.4 1.8 %shard_map.97 = (bf16[256,128]{1,0:T(8,128)(2,1)S(1)}, bf16[256,128]{1,0:T(8,128)(2,1)S(1)}, bf16[256,128]{1,0:T(8,128)(2,1)S(1)}, bf16[256,128]{1,0:T(8,128)(2,1)S(1)}) custom-call(bf16[256,128]{1,0:T(8,128)(2,1)S(1)} %get-tuple-element.56.refs_0_, bf16[256,128]{1,0:T(8,128)(2,1)S(1)} %collective-permute-done.12.refs_1_, ...), custom_call_target="tpu_custom_call" | custom-call | flops 1073741824 | bytes 5242880 | tf_op jit(solution)/shard_map/pallas_call | solution.py:37
  76.2 0.1 collective-permute-start.15
  76.3 2.5 %collective-permute-start.16 = (bf16[256,128]{1,0:T(8,128)(2,1)S(1)}, bf16[256,128]{1,0:T(8,128)(2,1)S(1)}, u32[]{:S(2)}, u32[]{:S(2)}) collective-permute-start(bf16[256,128]{1,0:T(8,128)(2,1)S(1)} %get-tuple-element.63), channel_id=1, source_target_pairs={{0,8},{1,9},{2,10},{3,11},{4,12},{5,13},{6,14},{7,15},{8,0},{9,1},... | collective-permute-start | bytes 196616 | tf_op jit(solution)/shard_map/ppermute | solution.py:356
  78.8 1.3 %collective-permute-start.17 = (bf16[256,128]{1,0:T(8,128)(2,1)S(1)}, bf16[256,128]{1,0:T(8,128)(2,1)S(1)}, u32[]{:S(2)}, u32[]{:S(2)}) collective-permute-start(bf16[256,128]{1,0:T(8,128)(2,1)S(1)} %get-tuple-element.64), channel_id=1, source_target_pairs={{0,12},{1,13},{2,14},{3,15},{4,0},{5,1},{6,2},{7,3},{8,4},{9,5},{1... | collective-permute-start | bytes 196616 | tf_op jit(solution)/shard_map/ppermute | solution.py:356
  80.2 4.9 %collective-permute-done.15.e1 = bf16[256,128]{1,0:T(8,128)(2,1)S(1)} collective-permute-done((bf16[256,128]{1,0:T(8,128)(2,1)S(1)}, bf16[256,128]{1,0:T(8,128)(2,1)S(1)}, u32[]{:S(2)}, u32[]{:S(2)}) %collective-permute-start.15) | collective-permute-done | bytes 65568 | tf_op jit(solution)/shard_map/ppermute | solution.py:356
  85.1 1.8 %collective-permute-done.16.e2 = bf16[256,128]{1,0:T(8,128)(2,1)S(1)} collective-permute-done((bf16[256,128]{1,0:T(8,128)(2,1)S(1)}, bf16[256,128]{1,0:T(8,128)(2,1)S(1)}, u32[]{:S(2)}, u32[]{:S(2)}) %collective-permute-start.16) | collective-permute-done | bytes 65568 | tf_op jit(solution)/shard_map/ppermute | solution.py:356
  86.8 0.1 shard_map.99
  87.0 0.1 collective-permute-start.23
  87.1 0.2 shard_map.98.gated
  87.3 0.6 collective-permute-start.18
  87.8 1.5 %collective-permute-done.18.other = bf16[512,256]{1,0:T(8,128)(2,1)S(1)} collective-permute-done((bf16[512,256]{1,0:T(8,128)(2,1)S(1)}, bf16[512,256]{1,0:T(8,128)(2,1)S(1)}, u32[]{:S(2)}, u32[]{:S(2)}) %collective-permute-start.18) | collective-permute-done | bytes 262176 | tf_op jit(solution)/shard_map/ppermute | solution.py:356
  89.3 1.5 %shard_map.100 = (f32[128,1024]{1,0:T(8,128)S(1)}, bf16[128,1024]{1,0:T(8,128)(2,1)S(1)}, bf16[128,1024]{1,0:T(8,128)(2,1)S(1)}, bf16[128,1024]{1,0:T(8,128)(2,1)S(1)}) custom-call(bf16[512,256]{1,0:T(8,128)(2,1)S(1)} %shard_map.98.gated, bf16[512,256]{1,0:T(8,128)(2,1)S(1)} %collective-permute-done.18.other, ...), custom_call_target="tpu_custom_call" | custom-call | flops 1073741824 | bytes 4194304 | tf_op jit(solution)/shard_map/pallas_call | solution.py:37
  90.8 1.6 %collective-permute-start.26 = (bf16[128,1024]{1,0:T(8,128)(2,1)S(1)}, bf16[128,1024]{1,0:T(8,128)(2,1)S(1)}, u32[]{:S(2)}, u32[]{:S(2)}) collective-permute-start(bf16[128,1024]{1,0:T(8,128)(2,1)S(1)} %get-tuple-element.78), channel_id=1, source_target_pairs={{0,2},{1,3},{2,0},{3,1},{4,6},{5,7},{6,4},{7,5},{8,10},{9,11},{10,... | collective-permute-start | bytes 786440 | tf_op jit(solution)/shard_map/ppermute | solution.py:356
  92.4 1.5 %collective-permute-start.25 = (bf16[128,1024]{1,0:T(8,128)(2,1)S(1)}, bf16[128,1024]{1,0:T(8,128)(2,1)S(1)}, u32[]{:S(2)}, u32[]{:S(2)}) collective-permute-start(bf16[128,1024]{1,0:T(8,128)(2,1)S(1)} %get-tuple-element.77), channel_id=1, source_target_pairs={{0,16},{1,17},{2,18},{3,19},{4,20},{5,21},{6,22},{7,23},{8,24},{9,... | collective-permute-start | bytes 786440 | tf_op jit(solution)/shard_map/ppermute | solution.py:356
  93.9 0.4 collective-permute-start.24
  94.4 5.7 %collective-permute-done.26 = bf16[128,1024]{1,0:T(8,128)(2,1)S(1)} collective-permute-done((bf16[128,1024]{1,0:T(8,128)(2,1)S(1)}, bf16[128,1024]{1,0:T(8,128)(2,1)S(1)}, u32[]{:S(2)}, u32[]{:S(2)}) %collective-permute-start.26) | collective-permute-done | bytes 262176 | tf_op jit(solution)/shard_map/ppermute | solution.py:356
  100.0 6.1 %collective-permute-done.25 = bf16[128,1024]{1,0:T(8,128)(2,1)S(1)} collective-permute-done((bf16[128,1024]{1,0:T(8,128)(2,1)S(1)}, bf16[128,1024]{1,0:T(8,128)(2,1)S(1)}, u32[]{:S(2)}, u32[]{:S(2)}) %collective-permute-start.25) | collective-permute-done | bytes 262176 | tf_op jit(solution)/shard_map/ppermute | solution.py:356
  106.1 0.8 add_convert_fusion
  (22 shorter events, 0.1 us)
Async XLA Ops:
  1.8 11.6 %collective-permute-start = (bf16[256,512]{1,0:T(8,128)(2,1)}, bf16[256,512]{1,0:T(8,128)(2,1)S(1)}, u32[]{:S(2)}, u32[]{:S(2)}) collective-permute-start(bf16[256,512]{1,0:T(8,128)(2,1)} %shard_map.91.after.w0), channel_id=1, source_target_pairs={{0,4},{1,5},{2,6},{3,7},{4,8},{5,9},{6,10},{7,11},{8,12},{9,13},{1... | collective-permute-start | bytes 786440 | tf_op jit(solution)/shard_map/ppermute | solution.py:356
  7.7 28.1 %copy-start = (bf16[2,2,128,1024]{3,2,1,0:T(8,128)(2,1)S(1)}, bf16[2,2,128,1024]{3,2,1,0:T(8,128)(2,1)}, u32[]{:S(2)}) copy-start(bf16[2,2,128,1024]{3,2,1,0:T(8,128)(2,1)} %filt.3) | copy-start | bytes 3145732
  7.7 8.0 %collective-permute-start.1 = (bf16[128,1024]{1,0:T(8,128)(2,1)}, bf16[128,1024]{1,0:T(8,128)(2,1)S(1)}, u32[]{:S(2)}, u32[]{:S(2)}) collective-permute-start(bf16[128,1024]{1,0:T(8,128)(2,1)} %get-tuple-element.43), channel_id=1, source_target_pairs={{0,2},{1,3},{2,0},{3,1},{4,6},{5,7},{6,4},{7,5},{8,10},{9,11},{10,... | collective-permute-start | bytes 786440 | tf_op jit(solution)/shard_map/ppermute | solution.py:356
  9.2 7.7 %collective-permute-start.2 = (bf16[128,1024]{1,0:T(8,128)(2,1)}, bf16[128,1024]{1,0:T(8,128)(2,1)S(1)}, u32[]{:S(2)}, u32[]{:S(2)}) collective-permute-start(bf16[128,1024]{1,0:T(8,128)(2,1)} %get-tuple-element.44), channel_id=1, source_target_pairs={{0,16},{1,17},{2,18},{3,19},{4,20},{5,21},{6,22},{7,23},{8,24},{9,... | collective-permute-start | bytes 786440 | tf_op jit(solution)/shard_map/ppermute | solution.py:356
  16.9 8.4 %collective-permute-start.3 = (bf16[256,512]{1,0:T(8,128)(2,1)S(1)}, bf16[256,512]{1,0:T(8,128)(2,1)S(1)}, u32[]{:S(2)}, u32[]{:S(2)}) collective-permute-start(bf16[256,512]{1,0:T(8,128)(2,1)S(1)} %collective-permute-done.w1), channel_id=1, source_target_pairs={{0,4},{1,5},{2,6},{3,7},{4,8},{5,9},{6,10},{7,11},{8,12},{9,13},{1... | collective-permute-start | bytes 786440 | tf_op jit(solution)/shard_map/ppermute | solution.py:356
  18.5 7.5 %collective-permute-start.4 = (bf16[128,1024]{1,0:T(8,128)(2,1)}, bf16[128,1024]{1,0:T(8,128)(2,1)S(1)}, u32[]{:S(2)}, u32[]{:S(2)}) collective-permute-start(bf16[128,1024]{1,0:T(8,128)(2,1)} %get-tuple-element.47), channel_id=1, source_target_pairs={{0,18},{1,19},{2,16},{3,17},{4,22},{5,23},{6,20},{7,21},{8,26},{9,... | collective-permute-start | bytes 786440 | tf_op jit(solution)/shard_map/ppermute | solution.py:356
  26.0 1.0 copy-start.2
  26.9 0.9 copy-start.8
  27.0 20.9 %collective-permute-start.9 = (bf16[512,512]{1,0:T(8,128)(2,1)S(1)}, bf16[512,512]{1,0:T(8,128)(2,1)S(1)}, u32[]{:S(2)}, u32[]{:S(2)}) collective-permute-start(bf16[512,512]{1,0:T(8,128)(2,1)S(1)} %shard_map.93.mine), channel_id=1, source_target_pairs={{0,1},{1,0},{2,3},{3,2},{4,5},{5,4},{6,7},{7,6},{8,9},{9,8},{10,11... | collective-permute-start | bytes 1572872 | tf_op jit(solution)/shard_map/ppermute | solution.py:356
  27.9 16.6 %copy-start.9 = (bf16[256,256]{1,0:T(8,128)(2,1)S(1)}, bf16[256,256]{1,0:T(8,128)(2,1)}, u32[]{:S(2)}) copy-start(bf16[256,256]{1,0:T(8,128)(2,1)} %get-tuple-element.68) | copy-start | bytes 393220
  27.9 20.0 %copy-start.1 = (bf16[256,512]{1,0:T(8,128)(2,1)S(1)}, bf16[256,512]{1,0:T(8,128)(2,1)}, u32[]{:S(2)}) copy-start(bf16[256,512]{1,0:T(8,128)(2,1)} %shard_map.91.after.w0) | copy-start | bytes 786436
  27.9 7.9 %collective-permute-start.5 = (bf16[2,2,128,256]{3,2,1,0:T(8,128)(2,1)S(1)}, bf16[2,2,128,256]{3,2,1,0:T(8,128)(2,1)S(1)}, u32[]{:S(2)}, u32[]{:S(2)}) collective-permute-start(bf16[2,2,128,256]{3,2,1,0:T(8,128)(2,1)S(1)} %copy-done.8), channel_id=1, source_target_pairs={{0,2},{1,3},{2,0},{3,1},{4,6},{5,7},{6,4},{7,5},{8,10},{9,11},{10,... | collective-permute-start | bytes 786440 | tf_op jit(solution)/shard_map/ppermute | solution.py:356
  28.4 19.4 %collective-permute-start.10 = (bf16[256,512]{1,0:T(8,128)(2,1)S(1)}, bf16[256,512]{1,0:T(8,128)(2,1)S(1)}, u32[]{:S(2)}, u32[]{:S(2)}) collective-permute-start(bf16[256,512]{1,0:T(8,128)(2,1)S(1)} %collective-permute-done.3.w2), channel_id=1, source_target_pairs={{0,4},{1,5},{2,6},{3,7},{4,8},{5,9},{6,10},{7,11},{8,12},{9,13},{1... | collective-permute-start | bytes 786440 | tf_op jit(solution)/shard_map/ppermute | solution.py:356
  36.1 8.3 %collective-permute-start.6 = (bf16[2,2,128,128]{3,2,1,0:T(8,128)(2,1)S(1)}, bf16[2,2,128,128]{3,2,1,0:T(8,128)(2,1)S(1)}, u32[]{:S(2)}, u32[]{:S(2)}) collective-permute-start(bf16[2,2,128,128]{3,2,1,0:T(8,128)(2,1)S(1)} %get-tuple-element.49), channel_id=1, source_target_pairs={{0,4},{1,5},{2,6},{3,7},{4,8},{5,9},{6,10},{7,11},{8,12},{9,13},{1... | collective-permute-start | bytes 393224 | tf_op jit(solution)/shard_map/ppermute | solution.py:356
  37.7 10.1 %collective-permute-start.7 = (bf16[2,2,128,128]{3,2,1,0:T(8,128)(2,1)S(1)}, bf16[2,2,128,128]{3,2,1,0:T(8,128)(2,1)S(1)}, u32[]{:S(2)}, u32[]{:S(2)}) collective-permute-start(bf16[2,2,128,128]{3,2,1,0:T(8,128)(2,1)S(1)} %get-tuple-element.50), channel_id=1, source_target_pairs={{0,8},{1,9},{2,10},{3,11},{4,12},{5,13},{6,14},{7,15},{8,0},{9,1},... | collective-permute-start | bytes 393224 | tf_op jit(solution)/shard_map/ppermute | solution.py:356
  39.0 8.9 %collective-permute-start.8 = (bf16[2,2,128,128]{3,2,1,0:T(8,128)(2,1)S(1)}, bf16[2,2,128,128]{3,2,1,0:T(8,128)(2,1)S(1)}, u32[]{:S(2)}, u32[]{:S(2)}) collective-permute-start(bf16[2,2,128,128]{3,2,1,0:T(8,128)(2,1)S(1)} %get-tuple-element.51), channel_id=1, source_target_pairs={{0,12},{1,13},{2,14},{3,15},{4,0},{5,1},{6,2},{7,3},{8,4},{9,5},{1... | collective-permute-start | bytes 393224 | tf_op jit(solution)/shard_map/ppermute | solution.py:356
  40.4 9.4 %copy-start.7 = (bf16[256,256]{1,0:T(8,128)(2,1)S(1)}, bf16[256,256]{1,0:T(8,128)(2,1)}, u32[]{:S(2)}) copy-start(bf16[256,256]{1,0:T(8,128)(2,1)} %get-tuple-element.66) | copy-start | bytes 393220
  44.4 5.3 %collective-permute-start.19 = (bf16[256,256]{1,0:T(8,128)(2,1)S(1)}, bf16[256,256]{1,0:T(8,128)(2,1)S(1)}, u32[]{:S(2)}, u32[]{:S(2)}) collective-permute-start(bf16[256,256]{1,0:T(8,128)(2,1)S(1)} %copy-done.9), channel_id=1, source_target_pairs={{0,2},{1,3},{2,0},{3,1},{4,6},{5,7},{6,4},{7,5},{8,10},{9,11},{10,... | collective-permute-start | bytes 393224 | tf_op jit(solution)/shard_map/ppermute | solution.py:356
  49.2 8.2 %collective-permute-start.11 = (bf16[512,256]{1,0:T(8,128)(2,1)S(1)}, bf16[512,256]{1,0:T(8,128)(2,1)S(1)}, u32[]{:S(2)}, u32[]{:S(2)}) collective-permute-start(bf16[512,256]{1,0:T(8,128)(2,1)S(1)} %get-tuple-element.55), channel_id=1, source_target_pairs={{0,2},{1,3},{2,0},{3,1},{4,6},{5,7},{6,4},{7,5},{8,10},{9,11},{10,... | collective-permute-start | bytes 786440 | tf_op jit(solution)/shard_map/ppermute | solution.py:356
  49.8 7.6 %copy-start.3 = (bf16[128,1024]{1,0:T(8,128)(2,1)S(1)}, bf16[128,1024]{1,0:T(8,128)(2,1)}, u32[]{:S(2)}) copy-start(bf16[128,1024]{1,0:T(8,128)(2,1)} %get-tuple-element.46.refs_0_.g0) | copy-start | bytes 786436
  49.8 7.6 %copy-start.4 = (f32[1024]{0:T(1024)S(1)}, f32[1024]{0:T(1024)}, u32[]{:S(2)}) copy-start(f32[1024]{0:T(1024)} %param.13) | copy-start | bytes 12292
  49.8 24.6 %copy-start.6 = (bf16[16,256,128]{2,1,0:T(8,128)(2,1)S(1)}, bf16[16,256,128]{2,1,0:T(8,128)(2,1)}, u32[]{:S(2)}) copy-start(bf16[16,256,128]{2,1,0:T(8,128)(2,1)} %constant.5.clone.refs_9_) | copy-start | bytes 3145732
  49.8 24.6 %copy-start.5 = (bf16[16,256,128]{2,1,0:T(8,128)(2,1)S(1)}, bf16[16,256,128]{2,1,0:T(8,128)(2,1)}, u32[]{:S(2)}) copy-start(bf16[16,256,128]{2,1,0:T(8,128)(2,1)} %constant.4.clone.refs_8_) | copy-start | bytes 3145732
  49.8 9.7 %collective-permute-start.20 = (bf16[2,256,256]{2,1,0:T(8,128)(2,1)S(1)}, bf16[2,256,256]{2,1,0:T(8,128)(2,1)S(1)}, u32[]{:S(2)}, u32[]{:S(2)}) collective-permute-start(bf16[2,256,256]{2,1,0:T(8,128)(2,1)S(1)} %pad_maximum_fusion.refs_0_), channel_id=1, source_target_pairs={{0,4},{1,5},{2,6},{3,7},{4,8},{5,9},{6,10},{7,11},{8,12},{9,13},{1... | collective-permute-start | bytes 786440 | tf_op jit(solution)/shard_map/ppermute | solution.py:356
  59.6 13.0 %collective-permute-start.21 = (bf16[2,256,256]{2,1,0:T(8,128)(2,1)S(1)}, bf16[2,256,256]{2,1,0:T(8,128)(2,1)S(1)}, u32[]{:S(2)}, u32[]{:S(2)}) collective-permute-start(bf16[2,256,256]{2,1,0:T(8,128)(2,1)S(1)} %collective-permute-done.20.refs_1_), channel_id=1, source_target_pairs={{0,4},{1,5},{2,6},{3,7},{4,8},{5,9},{6,10},{7,11},{8,12},{9,13},{1... | collective-permute-start | bytes 786440 | tf_op jit(solution)/shard_map/ppermute | solution.py:356
  61.2 10.0 %collective-permute-start.12 = (bf16[256,128]{1,0:T(8,128)(2,1)S(1)}, bf16[256,128]{1,0:T(8,128)(2,1)S(1)}, u32[]{:S(2)}, u32[]{:S(2)}) collective-permute-start(bf16[256,128]{1,0:T(8,128)(2,1)S(1)} %get-tuple-element.57), channel_id=1, source_target_pairs={{0,4},{1,5},{2,6},{3,7},{4,8},{5,9},{6,10},{7,11},{8,12},{9,13},{1... | collective-permute-start | bytes 196616 | tf_op jit(solution)/shard_map/ppermute | solution.py:356
  61.8 10.8 %collective-permute-start.13 = (bf16[256,128]{1,0:T(8,128)(2,1)S(1)}, bf16[256,128]{1,0:T(8,128)(2,1)S(1)}, u32[]{:S(2)}, u32[]{:S(2)}) collective-permute-start(bf16[256,128]{1,0:T(8,128)(2,1)S(1)} %get-tuple-element.58), channel_id=1, source_target_pairs={{0,8},{1,9},{2,10},{3,11},{4,12},{5,13},{6,14},{7,15},{8,0},{9,1},... | collective-permute-start | bytes 196616 | tf_op jit(solution)/shard_map/ppermute | solution.py:356
  64.0 8.6 %collective-permute-start.14 = (bf16[256,128]{1,0:T(8,128)(2,1)S(1)}, bf16[256,128]{1,0:T(8,128)(2,1)S(1)}, u32[]{:S(2)}, u32[]{:S(2)}) collective-permute-start(bf16[256,128]{1,0:T(8,128)(2,1)S(1)} %get-tuple-element.59), channel_id=1, source_target_pairs={{0,12},{1,13},{2,14},{3,15},{4,0},{5,1},{6,2},{7,3},{8,4},{9,5},{1... | collective-permute-start | bytes 196616 | tf_op jit(solution)/shard_map/ppermute | solution.py:356
  72.5 14.3 %collective-permute-start.22 = (bf16[2,256,256]{2,1,0:T(8,128)(2,1)S(1)}, bf16[2,256,256]{2,1,0:T(8,128)(2,1)S(1)}, u32[]{:S(2)}, u32[]{:S(2)}) collective-permute-start(bf16[2,256,256]{2,1,0:T(8,128)(2,1)S(1)} %collective-permute-done.21.refs_2_), channel_id=1, source_target_pairs={{0,4},{1,5},{2,6},{3,7},{4,8},{5,9},{6,10},{7,11},{8,12},{9,13},{1... | collective-permute-start | bytes 786440 | tf_op jit(solution)/shard_map/ppermute | solution.py:356
  76.2 8.8 %collective-permute-start.15 = (bf16[256,128]{1,0:T(8,128)(2,1)S(1)}, bf16[256,128]{1,0:T(8,128)(2,1)S(1)}, u32[]{:S(2)}, u32[]{:S(2)}) collective-permute-start(bf16[256,128]{1,0:T(8,128)(2,1)S(1)} %get-tuple-element.62), channel_id=1, source_target_pairs={{0,4},{1,5},{2,6},{3,7},{4,8},{5,9},{6,10},{7,11},{8,12},{9,13},{1... | collective-permute-start | bytes 196616 | tf_op jit(solution)/shard_map/ppermute | solution.py:356
  76.3 10.5 %collective-permute-start.16 = (bf16[256,128]{1,0:T(8,128)(2,1)S(1)}, bf16[256,128]{1,0:T(8,128)(2,1)S(1)}, u32[]{:S(2)}, u32[]{:S(2)}) collective-permute-start(bf16[256,128]{1,0:T(8,128)(2,1)S(1)} %get-tuple-element.63), channel_id=1, source_target_pairs={{0,8},{1,9},{2,10},{3,11},{4,12},{5,13},{6,14},{7,15},{8,0},{9,1},... | collective-permute-start | bytes 196616 | tf_op jit(solution)/shard_map/ppermute | solution.py:356
  78.8 8.0 %collective-permute-start.17 = (bf16[256,128]{1,0:T(8,128)(2,1)S(1)}, bf16[256,128]{1,0:T(8,128)(2,1)S(1)}, u32[]{:S(2)}, u32[]{:S(2)}) collective-permute-start(bf16[256,128]{1,0:T(8,128)(2,1)S(1)} %get-tuple-element.64), channel_id=1, source_target_pairs={{0,12},{1,13},{2,14},{3,15},{4,0},{5,1},{6,2},{7,3},{8,4},{9,5},{1... | collective-permute-start | bytes 196616 | tf_op jit(solution)/shard_map/ppermute | solution.py:356
  87.0 2.4 %collective-permute-start.23 = (bf16[4,256,256]{2,1,0:T(8,128)(2,1)S(1)}, bf16[4,256,256]{2,1,0:T(8,128)(2,1)S(1)}, u32[]{:S(2)}, u32[]{:S(2)}) collective-permute-start(bf16[4,256,256]{2,1,0:T(8,128)(2,1)S(1)} %get-tuple-element.74), channel_id=1, source_target_pairs={{0,1},{1,0},{2,3},{3,2},{4,5},{5,4},{6,7},{7,6},{8,9},{9,8},{10,11... | collective-permute-start | bytes 1572872 | tf_op jit(solution)/shard_map/ppermute | solution.py:356
  87.3 2.1 %collective-permute-start.18 = (bf16[512,256]{1,0:T(8,128)(2,1)S(1)}, bf16[512,256]{1,0:T(8,128)(2,1)S(1)}, u32[]{:S(2)}, u32[]{:S(2)}) collective-permute-start(bf16[512,256]{1,0:T(8,128)(2,1)S(1)} %shard_map.98.gated), channel_id=1, source_target_pairs={{0,1},{1,0},{2,3},{3,2},{4,5},{5,4},{6,7},{7,6},{8,9},{9,8},{10,11... | collective-permute-start | bytes 786440 | tf_op jit(solution)/shard_map/ppermute | solution.py:356
  90.8 9.2 %collective-permute-start.26 = (bf16[128,1024]{1,0:T(8,128)(2,1)S(1)}, bf16[128,1024]{1,0:T(8,128)(2,1)S(1)}, u32[]{:S(2)}, u32[]{:S(2)}) collective-permute-start(bf16[128,1024]{1,0:T(8,128)(2,1)S(1)} %get-tuple-element.78), channel_id=1, source_target_pairs={{0,2},{1,3},{2,0},{3,1},{4,6},{5,7},{6,4},{7,5},{8,10},{9,11},{10,... | collective-permute-start | bytes 786440 | tf_op jit(solution)/shard_map/ppermute | solution.py:356
  92.4 13.7 %collective-permute-start.25 = (bf16[128,1024]{1,0:T(8,128)(2,1)S(1)}, bf16[128,1024]{1,0:T(8,128)(2,1)S(1)}, u32[]{:S(2)}, u32[]{:S(2)}) collective-permute-start(bf16[128,1024]{1,0:T(8,128)(2,1)S(1)} %get-tuple-element.77), channel_id=1, source_target_pairs={{0,16},{1,17},{2,18},{3,19},{4,20},{5,21},{6,22},{7,23},{8,24},{9,... | collective-permute-start | bytes 786440 | tf_op jit(solution)/shard_map/ppermute | solution.py:356
  93.9 12.2 %collective-permute-start.24 = (bf16[128,1024]{1,0:T(8,128)(2,1)S(1)}, bf16[128,1024]{1,0:T(8,128)(2,1)S(1)}, u32[]{:S(2)}, u32[]{:S(2)}) collective-permute-start(bf16[128,1024]{1,0:T(8,128)(2,1)S(1)} %get-tuple-element.76), channel_id=1, source_target_pairs={{0,18},{1,19},{2,16},{3,17},{4,22},{5,23},{6,20},{7,21},{8,26},{9,... | collective-permute-start | bytes 786440 | tf_op jit(solution)/shard_map/ppermute | solution.py:356

commit v7 on v6

--- a/solution.py
+++ b/solution.py
@@ -307,7 +307,7 @@
 
 
 def sort_weight(*refs):
-    pieces, keep, give = refs[:4], refs[4], refs[5]
+    pieces, keep, give = refs[:8], refs[8], refs[9]
     _, x, z, c = place()
     for r in range(4):
         owner = lax.rem(z - r + 4, 4)
@@ -316,11 +316,11 @@
 
             @pl.when(owner // 2 == c)
             def _():
-                keep[to] = pieces[r][k]
+                keep[to] = pieces[2 * r + k][...]
 
             @pl.when(owner // 2 != c)
             def _():
-                give[to] = pieces[r][k]
+                give[to] = pieces[2 * r + k][...]
 
 
 def out_kernel(gated, other, keep, theirs, own, *sends):
@@ -388,20 +388,23 @@
     )(filter_spectrum, near)
     filters = [filters[0]] + [to_z(filters[r], r) for r in (1, 2, 3)]
     v1 = to_z(own_v, 1)
-    v2 = to_z(after(v1, received[0], received[1]), 1)
-    mine = in_vmem(join_tokens, shape((512, 512), BF16), moved=1 << 20)(after(own, v2), *received)
-    v3 = to_z(after(v2, mine), 1)
+    q1 = to_z(own_o, 1)
+    v2 = to_z(after(v1, near, received[1], q1), 1)
+    q2 = to_z(q1, 1)
+    mine = in_vmem(join_tokens, shape((512, 512), BF16), moved=1 << 20)(after(own, v2, q2, *filters[1:]), *received)
+    v3 = to_z(after(v2, filters[1]), 1)
+    q3 = to_z(q2, 1)
     other = to_core(mine)
     got_o = to_x(after(away_o, v2))
-    pair = jnp.stack([own_o, got_o])
-    hops = [pair, to_z(after(pair, v3), 1)]
+    r1 = to_z(after(got_o, v3), 1)
     keep, give = in_vmem(
         value_kernel,
         [shape((512, 256), F32), shape((512, 256), BF16)],
         [pltpu.VMEM((512, 512), F32)],
         flops=1 << 29,
         moved=2 << 20,
-    )(after(mine, *filters[1:]), other, own_v, v1, v2, v3)
+    )(after(mine, q3), other, own_v, v1, v2, v3)
+    r2 = to_z(after(r1, keep), 1)
     drive, *sends = in_vmem(
         drive_kernel,
         [shape((512, 256), F32)] + [block] * 4,
@@ -409,8 +412,7 @@
         moved=2 << 20,
     )(keep, to_x(give), *plane, skip[None, :])
     columns = [sends[0]] + [to_z(sends[r], r) for r in (1, 2, 3)]
-    hops.append(to_z(after(hops[1], drive), 1))
-    hops.append(to_z(after(hops[2], *columns[1:]), 1))
+    r3 = to_z(after(r2, *columns[1:]), 1)
     table, table_t = tables()
     sends = in_vmem(
         conv_kernel,
@@ -426,7 +428,7 @@
     )(*columns, *filters, table, table_t)
     rows = [sends[0]] + [to_z(sends[r], r) for r in (1, 2, 3)]
 
-    hops[3] = after(hops[3], *rows[1:])
+    hops = [own_o, got_o, q1, r1, q2, r2, q3, after(r3, *rows[1:])]
     quad = shape((4, 256, 256), BF16)
     keep, give = in_vmem(sort_weight, [quad] * 2, moved=2 << 20)(*hops)
     theirs = to_core(give)

time: 107 us -> 105 us (0.981)
  starting transfers between devices: 35.6 us -> 32.4 us
  waiting for transfers between devices: 58.3 us -> 60.9 us
  local copies, waits for them, and re-layouts: 1.82 us -> 0.05 us
    ppermute x27 -> x30, starting transfers between devices: 35.6 us -> 32.4 us  [permute(): return lax.ppermute(values, AXES, pairs)]
    ppermute x27 -> x30, waiting for transfers between devices: 58.3 us -> 60.9 us  [permute(): return lax.ppermute(values, AXES, pairs)]
    unnamed x20, local copies, waits for them, and re-layouts: 1.82 us -> 0.05 us
  transfers between devices with their start and end apart: 27 -> 30, of which waited for: 17 -> 16; matrix products, arithmetic and copies ran while one was open for 0% -> 0% of each run, Pallas kernels for 6% -> 4%
where the time goes in v7:
time: 105 us
  waiting for transfers between devices  60.9 us (58%)
  starting transfers between devices  32.4 us (31%)
  Pallas kernels  10.3 us (10%)
    ppermute x30, waiting for transfers between devices, permute(): return lax.ppermute(values, AXES, pairs)  60.9 us
    ppermute x30, starting transfers between devices, permute(): return lax.ppermute(values, AXES, pairs)  32.4 us
    pallas_call x8, Pallas kernels, call(): pl.pallas_call(kernel, out_shape=out_shape, in_specs=specs, out_specs=jax...  5.63 us
    pallas_call x2, Pallas kernels, call(): pl.pallas_call(kernel, out_shape=out_shape, in_specs=[pl.BlockSpec(memory...  4.72 us
  transfers between devices with their start and end apart: 30, of which 16 were waited for; matrix products, arithmetic and copies ran while one was open for 0% of the time, Pallas kernels for 4%

profile of v7, /device:TPU:0, one launch (start us, length us, event | category | flops | bytes accessed | tf_op | source)
XLA Modules:
  0.0 104.8 jit_solution(4883033137255263648)
XLA Ops:
  0.0 1.8 %shard_map.91.after.w0 = bf16[256,512]{1,0:T(8,128)(2,1)} custom-call(bf16[256,1024]{1,0:T(8,128)(2,1)} %value.1), custom_call_target="tpu_custom_call" | custom-call | tf_op jit(solution)/shard_map/pallas_call | solution.py:106
  1.8 0.0 copy-start.1
  1.8 0.0 copy-start
  1.9 2.9 %shard_map.92 = (bf16[128,1024]{1,0:T(8,128)(2,1)}, bf16[128,1024]{1,0:T(8,128)(2,1)}, bf16[128,1024]{1,0:T(8,128)(2,1)}, bf16[128,1024]{1,0:T(8,128)(2,1)}, bf1...) custom-call(bf16[128,1024]{1,0:T(8,128)(2,1)} %tokens.1, bf16[128,1024]{1,0:T(8,128)(2,1)} %key.1, ...), custom_call_target="tpu_custom_call" | custom-call | tf_op jit(solution)/shard_map/pallas_call | solution.py:106
  4.8 3.0 %collective-permute-start.1 = (bf16[2,2,128,256]{3,2,1,0:T(8,128)(2,1)}, bf16[2,2,128,256]{3,2,1,0:T(8,128)(2,1)S(1)}, u32[]{:S(2)}, u32[]{:S(2)}) collective-permute-start(bf16[2,2,128,256]{3,2,1,0:T(8,128)(2,1)} %get-tuple-element.43), channel_id=1, source_target_pairs={{0,2},{1,3},{2,0},{3,1},{4,6},{5,7},{6,4},{7,5},{8,10},{9,11},{10,... | collective-permute-start | bytes 786440 | tf_op jit(solution)/shard_map/ppermute | solution.py:356
  7.8 1.5 %collective-permute-start.2 = (bf16[128,1024]{1,0:T(8,128)(2,1)}, bf16[128,1024]{1,0:T(8,128)(2,1)S(1)}, u32[]{:S(2)}, u32[]{:S(2)}) collective-permute-start(bf16[128,1024]{1,0:T(8,128)(2,1)} %get-tuple-element.44), channel_id=1, source_target_pairs={{0,16},{1,17},{2,18},{3,19},{4,20},{5,21},{6,22},{7,23},{8,24},{9,... | collective-permute-start | bytes 786440 | tf_op jit(solution)/shard_map/ppermute | solution.py:356
  9.3 1.6 %collective-permute-start = (bf16[256,512]{1,0:T(8,128)(2,1)S(1)}, bf16[256,512]{1,0:T(8,128)(2,1)S(1)}, u32[]{:S(2)}, u32[]{:S(2)}) collective-permute-start(bf16[256,512]{1,0:T(8,128)(2,1)S(1)} %copy-done.1), channel_id=1, source_target_pairs={{0,4},{1,5},{2,6},{3,7},{4,8},{5,9},{6,10},{7,11},{8,12},{9,13},{1... | collective-permute-start | bytes 786440 | tf_op jit(solution)/shard_map/ppermute | solution.py:356
  10.9 1.6 %collective-permute-start.3 = (bf16[256,256]{1,0:T(8,128)(2,1)}, bf16[256,256]{1,0:T(8,128)(2,1)S(1)}, u32[]{:S(2)}, u32[]{:S(2)}) collective-permute-start(bf16[256,256]{1,0:T(8,128)(2,1)} %get-tuple-element.45.refs_0_), channel_id=1, source_target_pairs={{0,4},{1,5},{2,6},{3,7},{4,8},{5,9},{6,10},{7,11},{8,12},{9,13},{1... | collective-permute-start | bytes 393224 | tf_op jit(solution)/shard_map/ppermute | solution.py:356
  12.4 9.0 %collective-permute-done.3.refs_2_ = bf16[256,256]{1,0:T(8,128)(2,1)S(1)} collective-permute-done((bf16[256,256]{1,0:T(8,128)(2,1)}, bf16[256,256]{1,0:T(8,128)(2,1)S(1)}, u32[]{:S(2)}, u32[]{:S(2)}) %collective-permute-start.3) | collective-permute-done | bytes 131104 | tf_op jit(solution)/shard_map/ppermute | solution.py:356
  21.4 0.0 collective-permute-start.5
  21.4 0.0 collective-permute-done.1.near
  21.4 0.3 shard_map.93
  21.8 1.3 %collective-permute-start.6 = (bf16[2,2,128,128]{3,2,1,0:T(8,128)(2,1)S(1)}, bf16[2,2,128,128]{3,2,1,0:T(8,128)(2,1)S(1)}, u32[]{:S(2)}, u32[]{:S(2)}) collective-permute-start(bf16[2,2,128,128]{3,2,1,0:T(8,128)(2,1)S(1)} %get-tuple-element.47), channel_id=1, source_target_pairs={{0,4},{1,5},{2,6},{3,7},{4,8},{5,9},{6,10},{7,11},{8,12},{9,13},{1... | collective-permute-start | bytes 393224 | tf_op jit(solution)/shard_map/ppermute | solution.py:356
  23.1 0.0 collective-permute-done.2.refs_2_.g2
  23.1 0.0 collective-permute-done.w1
  23.1 1.6 %collective-permute-start.4 = (bf16[256,512]{1,0:T(8,128)(2,1)S(1)}, bf16[256,512]{1,0:T(8,128)(2,1)S(1)}, u32[]{:S(2)}, u32[]{:S(2)}) collective-permute-start(bf16[256,512]{1,0:T(8,128)(2,1)S(1)} %collective-permute-done.w1), channel_id=1, source_target_pairs={{0,4},{1,5},{2,6},{3,7},{4,8},{5,9},{6,10},{7,11},{8,12},{9,13},{1... | collective-permute-start | bytes 786440 | tf_op jit(solution)/shard_map/ppermute | solution.py:356
  24.7 0.5 collective-permute-start.10
  25.2 1.5 %collective-permute-start.9 = (bf16[128,1024]{1,0:T(8,128)(2,1)S(1)}, bf16[128,1024]{1,0:T(8,128)(2,1)S(1)}, u32[]{:S(2)}, u32[]{:S(2)}) collective-permute-start(bf16[128,1024]{1,0:T(8,128)(2,1)S(1)} %copy-done.7), channel_id=1, source_target_pairs={{0,2},{1,3},{2,0},{3,1},{4,6},{5,7},{6,4},{7,5},{8,10},{9,11},{10,... | collective-permute-start | bytes 786440 | tf_op jit(solution)/shard_map/ppermute | solution.py:356
  26.7 3.1 %collective-permute-done.5.refs_4_ = bf16[256,256]{1,0:T(8,128)(2,1)S(1)} collective-permute-done((bf16[256,256]{1,0:T(8,128)(2,1)S(1)}, bf16[256,256]{1,0:T(8,128)(2,1)S(1)}, u32[]{:S(2)}, u32[]{:S(2)}) %collective-permute-start.5) | collective-permute-done | bytes 131104 | tf_op jit(solution)/shard_map/ppermute | solution.py:356
  29.7 2.9 %collective-permute-done.6.refs_5_ = bf16[2,2,128,128]{3,2,1,0:T(8,128)(2,1)S(1)} collective-permute-done((bf16[2,2,128,128]{3,2,1,0:T(8,128)(2,1)S(1)}, bf16[2,2,128,128]{3,2,1,0:T(8,128)(2,1)S(1)}, u32[]{:S(2)}, u32[]{:S(2)}) %collective-permute-start.6) | collective-permute-done | bytes 131104 | tf_op jit(solution)/shard_map/ppermute | solution.py:356
  32.7 0.0 collective-permute-start.8
  32.7 8.6 %collective-permute-done.7.refs_6_ = bf16[2,2,128,128]{3,2,1,0:T(8,128)(2,1)S(1)} collective-permute-done((bf16[2,2,128,128]{3,2,1,0:T(8,128)(2,1)S(1)}, bf16[2,2,128,128]{3,2,1,0:T(8,128)(2,1)S(1)}, u32[]{:S(2)}, u32[]{:S(2)}) %collective-permute-start.7) | collective-permute-done | bytes 131104 | tf_op jit(solution)/shard_map/ppermute | solution.py:356
  41.2 0.0 collective-permute-done.10.refs_3_.g3
  41.3 0.1 collective-permute-start.12
  41.4 3.3 %collective-permute-start.13 = (bf16[256,512]{1,0:T(8,128)(2,1)S(1)}, bf16[256,512]{1,0:T(8,128)(2,1)S(1)}, u32[]{:S(2)}, u32[]{:S(2)}) collective-permute-start(bf16[256,512]{1,0:T(8,128)(2,1)S(1)} %collective-permute-done.4.w2), channel_id=1, source_target_pairs={{0,4},{1,5},{2,6},{3,7},{4,8},{5,9},{6,10},{7,11},{8,12},{9,13},{1... | collective-permute-start | bytes 786440 | tf_op jit(solution)/shard_map/ppermute | solution.py:356
  44.7 0.1 collective-permute-start.11
  44.8 0.5 collective-permute-start.22
  45.4 9.4 %collective-permute-done.11.refs_6_ = bf16[256,256]{1,0:T(8,128)(2,1)S(1)} collective-permute-done((bf16[256,256]{1,0:T(8,128)(2,1)S(1)}, bf16[256,256]{1,0:T(8,128)(2,1)S(1)}, u32[]{:S(2)}, u32[]{:S(2)}) %collective-permute-start.11) | collective-permute-done | bytes 131104 | tf_op jit(solution)/shard_map/ppermute | solution.py:356
  54.7 0.0 collective-permute-done.13.w3
  54.7 0.0 collective-permute-done.12.other
  54.7 1.3 %shard_map.95 = (f32[512,256]{1,0:T(8,128)S(1)}, bf16[512,256]{1,0:T(8,128)(2,1)S(1)}) custom-call(bf16[512,512]{1,0:T(8,128)(2,1)S(1)} %shard_map.94.mine, bf16[512,512]{1,0:T(8,128)(2,1)S(1)} %collective-permute-done.12.other, bf16[256,512]{1,0:T(8,128)(2,1)S(1)} %copy-done.1, bf16[256,512]{1,0:T(8,128)(2,1)S(1)} %collective-permute-done.w1, ...), custom_call_target="tpu_custom_call" | custom-call | flops 536870912 | bytes 2097152 | tf_op jit(solution)/shard_map/pallas_call | solution.py:37
  56.0 0.0 copy-start.4
  56.0 0.0 copy-start.5
  56.0 0.6 collective-permute-start.14
  56.6 1.5 %collective-permute-start.23 = (bf16[256,256]{1,0:T(8,128)(2,1)S(1)}, bf16[256,256]{1,0:T(8,128)(2,1)S(1)}, u32[]{:S(2)}, u32[]{:S(2)}) collective-permute-start(bf16[256,256]{1,0:T(8,128)(2,1)S(1)} %collective-permute-done.22.refs_1_), channel_id=1, source_target_pairs={{0,4},{1,5},{2,6},{3,7},{4,8},{5,9},{6,10},{7,11},{8,12},{9,13},{1... | collective-permute-start | bytes 393224 | tf_op jit(solution)/shard_map/ppermute | solution.py:356
  58.1 5.3 %collective-permute-done.23.refs_3_ = bf16[256,256]{1,0:T(8,128)(2,1)S(1)} collective-permute-done((bf16[256,256]{1,0:T(8,128)(2,1)S(1)}, bf16[256,256]{1,0:T(8,128)(2,1)S(1)}, u32[]{:S(2)}, u32[]{:S(2)}) %collective-permute-start.23) | collective-permute-done | bytes 131104 | tf_op jit(solution)/shard_map/ppermute | solution.py:356
  63.4 0.6 collective-permute-done.14.taken
  64.0 0.4 shard_map.96
  64.3 1.5 %collective-permute-start.15 = (bf16[256,128]{1,0:T(8,128)(2,1)S(1)}, bf16[256,128]{1,0:T(8,128)(2,1)S(1)}, u32[]{:S(2)}, u32[]{:S(2)}) collective-permute-start(bf16[256,128]{1,0:T(8,128)(2,1)S(1)} %get-tuple-element.58), channel_id=1, source_target_pairs={{0,4},{1,5},{2,6},{3,7},{4,8},{5,9},{6,10},{7,11},{8,12},{9,13},{1... | collective-permute-start | bytes 196616 | tf_op jit(solution)/shard_map/ppermute | solution.py:356
  65.9 2.4 %collective-permute-start.16 = (bf16[256,128]{1,0:T(8,128)(2,1)S(1)}, bf16[256,128]{1,0:T(8,128)(2,1)S(1)}, u32[]{:S(2)}, u32[]{:S(2)}) collective-permute-start(bf16[256,128]{1,0:T(8,128)(2,1)S(1)} %get-tuple-element.59), channel_id=1, source_target_pairs={{0,8},{1,9},{2,10},{3,11},{4,12},{5,13},{6,14},{7,15},{8,0},{9,1},... | collective-permute-start | bytes 196616 | tf_op jit(solution)/shard_map/ppermute | solution.py:356
  68.2 0.5 collective-permute-start.17
  68.7 2.4 %collective-permute-done.24.refs_5_ = bf16[256,256]{1,0:T(8,128)(2,1)S(1)} collective-permute-done((bf16[256,256]{1,0:T(8,128)(2,1)S(1)}, bf16[256,256]{1,0:T(8,128)(2,1)S(1)}, u32[]{:S(2)}, u32[]{:S(2)}) %collective-permute-start.24) | collective-permute-done | bytes 131104 | tf_op jit(solution)/shard_map/ppermute | solution.py:356
  71.1 0.7 collective-permute-done.15.refs_1_
  71.8 2.1 %collective-permute-done.16.refs_2_ = bf16[256,128]{1,0:T(8,128)(2,1)S(1)} collective-permute-done((bf16[256,128]{1,0:T(8,128)(2,1)S(1)}, bf16[256,128]{1,0:T(8,128)(2,1)S(1)}, u32[]{:S(2)}, u32[]{:S(2)}) %collective-permute-start.16) | collective-permute-done | bytes 65568 | tf_op jit(solution)/shard_map/ppermute | solution.py:356
  73.8 1.3 %collective-permute-start.25 = (bf16[256,256]{1,0:T(8,128)(2,1)S(1)}, bf16[256,256]{1,0:T(8,128)(2,1)S(1)}, u32[]{:S(2)}, u32[]{:S(2)}) collective-permute-start(bf16[256,256]{1,0:T(8,128)(2,1)S(1)} %collective-permute-done.24.refs_5_), channel_id=1, source_target_pairs={{0,4},{1,5},{2,6},{3,7},{4,8},{5,9},{6,10},{7,11},{8,12},{9,13},{1... | collective-permute-start | bytes 393224 | tf_op jit(solution)/shard_map/ppermute | solution.py:356
  75.2 1.8 %shard_map.97 = (bf16[256,128]{1,0:T(8,128)(2,1)S(1)}, bf16[256,128]{1,0:T(8,128)(2,1)S(1)}, bf16[256,128]{1,0:T(8,128)(2,1)S(1)}, bf16[256,128]{1,0:T(8,128)(2,1)S(1)}) custom-call(bf16[256,128]{1,0:T(8,128)(2,1)S(1)} %get-tuple-element.57.refs_0_, bf16[256,128]{1,0:T(8,128)(2,1)S(1)} %collective-permute-done.15.refs_1_, ...), custom_call_target="tpu_custom_call" | custom-call | flops 1073741824 | bytes 5242880 | tf_op jit(solution)/shard_map/pallas_call | solution.py:37
  77.0 0.1 collective-permute-start.18
  77.1 3.1 %collective-permute-start.19 = (bf16[256,128]{1,0:T(8,128)(2,1)S(1)}, bf16[256,128]{1,0:T(8,128)(2,1)S(1)}, u32[]{:S(2)}, u32[]{:S(2)}) collective-permute-start(bf16[256,128]{1,0:T(8,128)(2,1)S(1)} %get-tuple-element.64), channel_id=1, source_target_pairs={{0,8},{1,9},{2,10},{3,11},{4,12},{5,13},{6,14},{7,15},{8,0},{9,1},... | collective-permute-start | bytes 196616 | tf_op jit(solution)/shard_map/ppermute | solution.py:356
  80.1 0.8 collective-permute-start.20
  80.9 2.6 %collective-permute-done.18.e1 = bf16[256,128]{1,0:T(8,128)(2,1)S(1)} collective-permute-done((bf16[256,128]{1,0:T(8,128)(2,1)S(1)}, bf16[256,128]{1,0:T(8,128)(2,1)S(1)}, u32[]{:S(2)}, u32[]{:S(2)}) %collective-permute-start.18) | collective-permute-done | bytes 65568 | tf_op jit(solution)/shard_map/ppermute | solution.py:356
  83.5 1.5 %collective-permute-done.19.e2 = bf16[256,128]{1,0:T(8,128)(2,1)S(1)} collective-permute-done((bf16[256,128]{1,0:T(8,128)(2,1)S(1)}, bf16[256,128]{1,0:T(8,128)(2,1)S(1)}, u32[]{:S(2)}, u32[]{:S(2)}) %collective-permute-start.19) | collective-permute-done | bytes 65568 | tf_op jit(solution)/shard_map/ppermute | solution.py:356
  84.9 0.1 collective-permute-done.20.e3
  85.0 0.1 shard_map.99
  85.2 0.1 collective-permute-start.26
  85.3 0.2 shard_map.98.gated
  85.5 0.6 collective-permute-start.21
  86.0 1.5 %collective-permute-done.21.other = bf16[512,256]{1,0:T(8,128)(2,1)S(1)} collective-permute-done((bf16[512,256]{1,0:T(8,128)(2,1)S(1)}, bf16[512,256]{1,0:T(8,128)(2,1)S(1)}, u32[]{:S(2)}, u32[]{:S(2)}) %collective-permute-start.21) | collective-permute-done | bytes 262176 | tf_op jit(solution)/shard_map/ppermute | solution.py:356
  87.5 1.5 %shard_map.100 = (f32[128,1024]{1,0:T(8,128)S(1)}, bf16[128,1024]{1,0:T(8,128)(2,1)S(1)}, bf16[128,1024]{1,0:T(8,128)(2,1)S(1)}, bf16[128,1024]{1,0:T(8,128)(2,1)S(1)}) custom-call(bf16[512,256]{1,0:T(8,128)(2,1)S(1)} %shard_map.98.gated, bf16[512,256]{1,0:T(8,128)(2,1)S(1)} %collective-permute-done.21.other, ...), custom_call_target="tpu_custom_call" | custom-call | flops 1073741824 | bytes 4194304 | tf_op jit(solution)/shard_map/pallas_call | solution.py:37
  89.0 1.3 %collective-permute-start.27 = (bf16[128,1024]{1,0:T(8,128)(2,1)S(1)}, bf16[128,1024]{1,0:T(8,128)(2,1)S(1)}, u32[]{:S(2)}, u32[]{:S(2)}) collective-permute-start(bf16[128,1024]{1,0:T(8,128)(2,1)S(1)} %get-tuple-element.76), channel_id=1, source_target_pairs={{0,18},{1,19},{2,16},{3,17},{4,22},{5,23},{6,20},{7,21},{8,26},{9,... | collective-permute-start | bytes 786440 | tf_op jit(solution)/shard_map/ppermute | solution.py:356
  90.4 1.5 %collective-permute-start.28 = (bf16[128,1024]{1,0:T(8,128)(2,1)S(1)}, bf16[128,1024]{1,0:T(8,128)(2,1)S(1)}, u32[]{:S(2)}, u32[]{:S(2)}) collective-permute-start(bf16[128,1024]{1,0:T(8,128)(2,1)S(1)} %get-tuple-element.77), channel_id=1, source_target_pairs={{0,16},{1,17},{2,18},{3,19},{4,20},{5,21},{6,22},{7,23},{8,24},{9,... | collective-permute-start | bytes 786440 | tf_op jit(solution)/shard_map/ppermute | solution.py:356
  91.9 0.7 collective-permute-start.29
  92.6 6.6 %collective-permute-done.27 = bf16[128,1024]{1,0:T(8,128)(2,1)S(1)} collective-permute-done((bf16[128,1024]{1,0:T(8,128)(2,1)S(1)}, bf16[128,1024]{1,0:T(8,128)(2,1)S(1)}, u32[]{:S(2)}, u32[]{:S(2)}) %collective-permute-start.27) | collective-permute-done | bytes 262176 | tf_op jit(solution)/shard_map/ppermute | solution.py:356
  99.2 4.7 %collective-permute-done.28 = bf16[128,1024]{1,0:T(8,128)(2,1)S(1)} collective-permute-done((bf16[128,1024]{1,0:T(8,128)(2,1)S(1)}, bf16[128,1024]{1,0:T(8,128)(2,1)S(1)}, u32[]{:S(2)}, u32[]{:S(2)}) %collective-permute-start.28) | collective-permute-done | bytes 262176 | tf_op jit(solution)/shard_map/ppermute | solution.py:356
  103.9 0.8 add_convert_fusion
  (27 shorter events, 0.1 us)
Async XLA Ops:
  1.8 7.5 %copy-start.1 = (bf16[256,512]{1,0:T(8,128)(2,1)S(1)}, bf16[256,512]{1,0:T(8,128)(2,1)}, u32[]{:S(2)}) copy-start(bf16[256,512]{1,0:T(8,128)(2,1)} %shard_map.91.after.w0) | copy-start | bytes 786436
  1.8 19.6 %copy-start = (bf16[2,2,128,1024]{3,2,1,0:T(8,128)(2,1)S(1)}, bf16[2,2,128,1024]{3,2,1,0:T(8,128)(2,1)}, u32[]{:S(2)}) copy-start(bf16[2,2,128,1024]{3,2,1,0:T(8,128)(2,1)} %filt.3) | copy-start | bytes 3145732
  4.8 16.7 %collective-permute-start.1 = (bf16[2,2,128,256]{3,2,1,0:T(8,128)(2,1)}, bf16[2,2,128,256]{3,2,1,0:T(8,128)(2,1)S(1)}, u32[]{:S(2)}, u32[]{:S(2)}) collective-permute-start(bf16[2,2,128,256]{3,2,1,0:T(8,128)(2,1)} %get-tuple-element.43), channel_id=1, source_target_pairs={{0,2},{1,3},{2,0},{3,1},{4,6},{5,7},{6,4},{7,5},{8,10},{9,11},{10,... | collective-permute-start | bytes 786440 | tf_op jit(solution)/shard_map/ppermute | solution.py:356
  7.8 15.3 %collective-permute-start.2 = (bf16[128,1024]{1,0:T(8,128)(2,1)}, bf16[128,1024]{1,0:T(8,128)(2,1)S(1)}, u32[]{:S(2)}, u32[]{:S(2)}) collective-permute-start(bf16[128,1024]{1,0:T(8,128)(2,1)} %get-tuple-element.44), channel_id=1, source_target_pairs={{0,16},{1,17},{2,18},{3,19},{4,20},{5,21},{6,22},{7,23},{8,24},{9,... | collective-permute-start | bytes 786440 | tf_op jit(solution)/shard_map/ppermute | solution.py:356
  9.3 13.8 %collective-permute-start = (bf16[256,512]{1,0:T(8,128)(2,1)S(1)}, bf16[256,512]{1,0:T(8,128)(2,1)S(1)}, u32[]{:S(2)}, u32[]{:S(2)}) collective-permute-start(bf16[256,512]{1,0:T(8,128)(2,1)S(1)} %copy-done.1), channel_id=1, source_target_pairs={{0,4},{1,5},{2,6},{3,7},{4,8},{5,9},{6,10},{7,11},{8,12},{9,13},{1... | collective-permute-start | bytes 786440 | tf_op jit(solution)/shard_map/ppermute | solution.py:356
  10.9 13.8 %copy-start.8 = (bf16[128,1024]{1,0:T(8,128)(2,1)S(1)}, bf16[128,1024]{1,0:T(8,128)(2,1)}, u32[]{:S(2)}) copy-start(bf16[128,1024]{1,0:T(8,128)(2,1)} %get-tuple-element.52) | copy-start | bytes 786436
  10.9 14.3 %copy-start.7 = (bf16[128,1024]{1,0:T(8,128)(2,1)S(1)}, bf16[128,1024]{1,0:T(8,128)(2,1)}, u32[]{:S(2)}) copy-start(bf16[128,1024]{1,0:T(8,128)(2,1)} %get-tuple-element.51) | copy-start | bytes 786436
  10.9 30.4 %copy-start.2 = (bf16[128,1024]{1,0:T(8,128)(2,1)S(1)}, bf16[128,1024]{1,0:T(8,128)(2,1)}, u32[]{:S(2)}) copy-start(bf16[128,1024]{1,0:T(8,128)(2,1)} %get-tuple-element.50.refs_0_.g0) | copy-start | bytes 786436
  10.9 10.6 %collective-permute-start.3 = (bf16[256,256]{1,0:T(8,128)(2,1)}, bf16[256,256]{1,0:T(8,128)(2,1)S(1)}, u32[]{:S(2)}, u32[]{:S(2)}) collective-permute-start(bf16[256,256]{1,0:T(8,128)(2,1)} %get-tuple-element.45.refs_0_), channel_id=1, source_target_pairs={{0,4},{1,5},{2,6},{3,7},{4,8},{5,9},{6,10},{7,11},{8,12},{9,13},{1... | collective-permute-start | bytes 393224 | tf_op jit(solution)/shard_map/ppermute | solution.py:356
  21.4 8.3 %collective-permute-start.5 = (bf16[256,256]{1,0:T(8,128)(2,1)S(1)}, bf16[256,256]{1,0:T(8,128)(2,1)S(1)}, u32[]{:S(2)}, u32[]{:S(2)}) collective-permute-start(bf16[256,256]{1,0:T(8,128)(2,1)S(1)} %collective-permute-done.3.refs_2_), channel_id=1, source_target_pairs={{0,4},{1,5},{2,6},{3,7},{4,8},{5,9},{6,10},{7,11},{8,12},{9,13},{1... | collective-permute-start | bytes 393224 | tf_op jit(solution)/shard_map/ppermute | solution.py:356
  21.8 10.9 %collective-permute-start.6 = (bf16[2,2,128,128]{3,2,1,0:T(8,128)(2,1)S(1)}, bf16[2,2,128,128]{3,2,1,0:T(8,128)(2,1)S(1)}, u32[]{:S(2)}, u32[]{:S(2)}) collective-permute-start(bf16[2,2,128,128]{3,2,1,0:T(8,128)(2,1)S(1)} %get-tuple-element.47), channel_id=1, source_target_pairs={{0,4},{1,5},{2,6},{3,7},{4,8},{5,9},{6,10},{7,11},{8,12},{9,13},{1... | collective-permute-start | bytes 393224 | tf_op jit(solution)/shard_map/ppermute | solution.py:356
  23.1 18.1 %collective-permute-start.4 = (bf16[256,512]{1,0:T(8,128)(2,1)S(1)}, bf16[256,512]{1,0:T(8,128)(2,1)S(1)}, u32[]{:S(2)}, u32[]{:S(2)}) collective-permute-start(bf16[256,512]{1,0:T(8,128)(2,1)S(1)} %collective-permute-done.w1), channel_id=1, source_target_pairs={{0,4},{1,5},{2,6},{3,7},{4,8},{5,9},{6,10},{7,11},{8,12},{9,13},{1... | collective-permute-start | bytes 786440 | tf_op jit(solution)/shard_map/ppermute | solution.py:356
  24.7 16.6 %collective-permute-start.10 = (bf16[128,1024]{1,0:T(8,128)(2,1)S(1)}, bf16[128,1024]{1,0:T(8,128)(2,1)S(1)}, u32[]{:S(2)}, u32[]{:S(2)}) collective-permute-start(bf16[128,1024]{1,0:T(8,128)(2,1)S(1)} %copy-done.8), channel_id=1, source_target_pairs={{0,18},{1,19},{2,16},{3,17},{4,22},{5,23},{6,20},{7,21},{8,26},{9,... | collective-permute-start | bytes 786440 | tf_op jit(solution)/shard_map/ppermute | solution.py:356
  25.2 16.1 %collective-permute-start.9 = (bf16[128,1024]{1,0:T(8,128)(2,1)S(1)}, bf16[128,1024]{1,0:T(8,128)(2,1)S(1)}, u32[]{:S(2)}, u32[]{:S(2)}) collective-permute-start(bf16[128,1024]{1,0:T(8,128)(2,1)S(1)} %copy-done.7), channel_id=1, source_target_pairs={{0,2},{1,3},{2,0},{3,1},{4,6},{5,7},{6,4},{7,5},{8,10},{9,11},{10,... | collective-permute-start | bytes 786440 | tf_op jit(solution)/shard_map/ppermute | solution.py:356
  29.7 11.5 %collective-permute-start.7 = (bf16[2,2,128,128]{3,2,1,0:T(8,128)(2,1)S(1)}, bf16[2,2,128,128]{3,2,1,0:T(8,128)(2,1)S(1)}, u32[]{:S(2)}, u32[]{:S(2)}) collective-permute-start(bf16[2,2,128,128]{3,2,1,0:T(8,128)(2,1)S(1)} %get-tuple-element.48), channel_id=1, source_target_pairs={{0,8},{1,9},{2,10},{3,11},{4,12},{5,13},{6,14},{7,15},{8,0},{9,1},... | collective-permute-start | bytes 393224 | tf_op jit(solution)/shard_map/ppermute | solution.py:356
  32.7 8.6 %collective-permute-start.8 = (bf16[2,2,128,128]{3,2,1,0:T(8,128)(2,1)S(1)}, bf16[2,2,128,128]{3,2,1,0:T(8,128)(2,1)S(1)}, u32[]{:S(2)}, u32[]{:S(2)}) collective-permute-start(bf16[2,2,128,128]{3,2,1,0:T(8,128)(2,1)S(1)} %get-tuple-element.49), channel_id=1, source_target_pairs={{0,12},{1,13},{2,14},{3,15},{4,0},{5,1},{6,2},{7,3},{8,4},{9,5},{1... | collective-permute-start | bytes 393224 | tf_op jit(solution)/shard_map/ppermute | solution.py:356
  41.2 3.6 %copy-start.9 = (bf16[256,256]{1,0:T(8,128)(2,1)S(1)}, bf16[256,256]{1,0:T(8,128)(2,1)}, u32[]{:S(2)}) copy-start(bf16[256,256]{1,0:T(8,128)(2,1)} %get-tuple-element.68) | copy-start | bytes 393220
  41.3 13.4 %collective-permute-start.12 = (bf16[512,512]{1,0:T(8,128)(2,1)S(1)}, bf16[512,512]{1,0:T(8,128)(2,1)S(1)}, u32[]{:S(2)}, u32[]{:S(2)}) collective-permute-start(bf16[512,512]{1,0:T(8,128)(2,1)S(1)} %shard_map.94.mine), channel_id=1, source_target_pairs={{0,1},{1,0},{2,3},{3,2},{4,5},{5,4},{6,7},{7,6},{8,9},{9,8},{10,11... | collective-permute-start | bytes 1572872 | tf_op jit(solution)/shard_map/ppermute | solution.py:356
  41.4 13.3 %collective-permute-start.13 = (bf16[256,512]{1,0:T(8,128)(2,1)S(1)}, bf16[256,512]{1,0:T(8,128)(2,1)S(1)}, u32[]{:S(2)}, u32[]{:S(2)}) collective-permute-start(bf16[256,512]{1,0:T(8,128)(2,1)S(1)} %collective-permute-done.4.w2), channel_id=1, source_target_pairs={{0,4},{1,5},{2,6},{3,7},{4,8},{5,9},{6,10},{7,11},{8,12},{9,13},{1... | collective-permute-start | bytes 786440 | tf_op jit(solution)/shard_map/ppermute | solution.py:356
  44.7 10.0 %collective-permute-start.11 = (bf16[256,256]{1,0:T(8,128)(2,1)S(1)}, bf16[256,256]{1,0:T(8,128)(2,1)S(1)}, u32[]{:S(2)}, u32[]{:S(2)}) collective-permute-start(bf16[256,256]{1,0:T(8,128)(2,1)S(1)} %collective-permute-done.5.refs_4_), channel_id=1, source_target_pairs={{0,4},{1,5},{2,6},{3,7},{4,8},{5,9},{6,10},{7,11},{8,12},{9,13},{1... | collective-permute-start | bytes 393224 | tf_op jit(solution)/shard_map/ppermute | solution.py:356
  44.8 11.8 %collective-permute-start.22 = (bf16[256,256]{1,0:T(8,128)(2,1)S(1)}, bf16[256,256]{1,0:T(8,128)(2,1)S(1)}, u32[]{:S(2)}, u32[]{:S(2)}) collective-permute-start(bf16[256,256]{1,0:T(8,128)(2,1)S(1)} %copy-done.9), channel_id=1, source_target_pairs={{0,2},{1,3},{2,0},{3,1},{4,6},{5,7},{6,4},{7,5},{8,10},{9,11},{10,... | collective-permute-start | bytes 393224 | tf_op jit(solution)/shard_map/ppermute | solution.py:356
  54.7 20.4 %copy-start.6 = (bf16[16,256,128]{2,1,0:T(8,128)(2,1)S(1)}, bf16[16,256,128]{2,1,0:T(8,128)(2,1)}, u32[]{:S(2)}) copy-start(bf16[16,256,128]{2,1,0:T(8,128)(2,1)} %constant.5.clone.refs_9_) | copy-start | bytes 3145732
  56.0 8.0 %copy-start.4 = (f32[1024]{0:T(1024)S(1)}, f32[1024]{0:T(1024)}, u32[]{:S(2)}) copy-start(f32[1024]{0:T(1024)} %param.13) | copy-start | bytes 12292
  56.0 19.1 %copy-start.5 = (bf16[16,256,128]{2,1,0:T(8,128)(2,1)S(1)}, bf16[16,256,128]{2,1,0:T(8,128)(2,1)}, u32[]{:S(2)}) copy-start(bf16[16,256,128]{2,1,0:T(8,128)(2,1)} %constant.4.clone.refs_8_) | copy-start | bytes 3145732
  56.0 8.0 %collective-permute-start.14 = (bf16[512,256]{1,0:T(8,128)(2,1)S(1)}, bf16[512,256]{1,0:T(8,128)(2,1)S(1)}, u32[]{:S(2)}, u32[]{:S(2)}) collective-permute-start(bf16[512,256]{1,0:T(8,128)(2,1)S(1)} %get-tuple-element.56), channel_id=1, source_target_pairs={{0,2},{1,3},{2,0},{3,1},{4,6},{5,7},{6,4},{7,5},{8,10},{9,11},{10,... | collective-permute-start | bytes 786440 | tf_op jit(solution)/shard_map/ppermute | solution.py:356
  56.6 6.8 %collective-permute-start.23 = (bf16[256,256]{1,0:T(8,128)(2,1)S(1)}, bf16[256,256]{1,0:T(8,128)(2,1)S(1)}, u32[]{:S(2)}, u32[]{:S(2)}) collective-permute-start(bf16[256,256]{1,0:T(8,128)(2,1)S(1)} %collective-permute-done.22.refs_1_), channel_id=1, source_target_pairs={{0,4},{1,5},{2,6},{3,7},{4,8},{5,9},{6,10},{7,11},{8,12},{9,13},{1... | collective-permute-start | bytes 393224 | tf_op jit(solution)/shard_map/ppermute | solution.py:356
  63.4 7.7 %collective-permute-start.24 = (bf16[256,256]{1,0:T(8,128)(2,1)S(1)}, bf16[256,256]{1,0:T(8,128)(2,1)S(1)}, u32[]{:S(2)}, u32[]{:S(2)}) collective-permute-start(bf16[256,256]{1,0:T(8,128)(2,1)S(1)} %collective-permute-done.23.refs_3_), channel_id=1, source_target_pairs={{0,4},{1,5},{2,6},{3,7},{4,8},{5,9},{6,10},{7,11},{8,12},{9,13},{1... | collective-permute-start | bytes 393224 | tf_op jit(solution)/shard_map/ppermute | solution.py:356
  64.3 7.4 %collective-permute-start.15 = (bf16[256,128]{1,0:T(8,128)(2,1)S(1)}, bf16[256,128]{1,0:T(8,128)(2,1)S(1)}, u32[]{:S(2)}, u32[]{:S(2)}) collective-permute-start(bf16[256,128]{1,0:T(8,128)(2,1)S(1)} %get-tuple-element.58), channel_id=1, source_target_pairs={{0,4},{1,5},{2,6},{3,7},{4,8},{5,9},{6,10},{7,11},{8,12},{9,13},{1... | collective-permute-start | bytes 196616 | tf_op jit(solution)/shard_map/ppermute | solution.py:356
  65.9 8.0 %collective-permute-start.16 = (bf16[256,128]{1,0:T(8,128)(2,1)S(1)}, bf16[256,128]{1,0:T(8,128)(2,1)S(1)}, u32[]{:S(2)}, u32[]{:S(2)}) collective-permute-start(bf16[256,128]{1,0:T(8,128)(2,1)S(1)} %get-tuple-element.59), channel_id=1, source_target_pairs={{0,8},{1,9},{2,10},{3,11},{4,12},{5,13},{6,14},{7,15},{8,0},{9,1},... | collective-permute-start | bytes 196616 | tf_op jit(solution)/shard_map/ppermute | solution.py:356
  68.2 5.6 %collective-permute-start.17 = (bf16[256,128]{1,0:T(8,128)(2,1)S(1)}, bf16[256,128]{1,0:T(8,128)(2,1)S(1)}, u32[]{:S(2)}, u32[]{:S(2)}) collective-permute-start(bf16[256,128]{1,0:T(8,128)(2,1)S(1)} %get-tuple-element.60), channel_id=1, source_target_pairs={{0,12},{1,13},{2,14},{3,15},{4,0},{5,1},{6,2},{7,3},{8,4},{9,5},{1... | collective-permute-start | bytes 196616 | tf_op jit(solution)/shard_map/ppermute | solution.py:356
  73.8 11.2 %collective-permute-start.25 = (bf16[256,256]{1,0:T(8,128)(2,1)S(1)}, bf16[256,256]{1,0:T(8,128)(2,1)S(1)}, u32[]{:S(2)}, u32[]{:S(2)}) collective-permute-start(bf16[256,256]{1,0:T(8,128)(2,1)S(1)} %collective-permute-done.24.refs_5_), channel_id=1, source_target_pairs={{0,4},{1,5},{2,6},{3,7},{4,8},{5,9},{6,10},{7,11},{8,12},{9,13},{1... | collective-permute-start | bytes 393224 | tf_op jit(solution)/shard_map/ppermute | solution.py:356
  75.2 9.9 %copy-start.3 = (bf16[256,256]{1,0:T(8,128)(2,1)S(1)}, bf16[256,256]{1,0:T(8,128)(2,1)}, u32[]{:S(2)}) copy-start(bf16[256,256]{1,0:T(8,128)(2,1)} %get-tuple-element.45.refs_0_) | copy-start | bytes 393220
  77.0 6.5 %collective-permute-start.18 = (bf16[256,128]{1,0:T(8,128)(2,1)S(1)}, bf16[256,128]{1,0:T(8,128)(2,1)S(1)}, u32[]{:S(2)}, u32[]{:S(2)}) collective-permute-start(bf16[256,128]{1,0:T(8,128)(2,1)S(1)} %get-tuple-element.63), channel_id=1, source_target_pairs={{0,4},{1,5},{2,6},{3,7},{4,8},{5,9},{6,10},{7,11},{8,12},{9,13},{1... | collective-permute-start | bytes 196616 | tf_op jit(solution)/shard_map/ppermute | solution.py:356
  77.1 7.9 %collective-permute-start.19 = (bf16[256,128]{1,0:T(8,128)(2,1)S(1)}, bf16[256,128]{1,0:T(8,128)(2,1)S(1)}, u32[]{:S(2)}, u32[]{:S(2)}) collective-permute-start(bf16[256,128]{1,0:T(8,128)(2,1)S(1)} %get-tuple-element.64), channel_id=1, source_target_pairs={{0,8},{1,9},{2,10},{3,11},{4,12},{5,13},{6,14},{7,15},{8,0},{9,1},... | collective-permute-start | bytes 196616 | tf_op jit(solution)/shard_map/ppermute | solution.py:356
  80.1 4.9 %collective-permute-start.20 = (bf16[256,128]{1,0:T(8,128)(2,1)S(1)}, bf16[256,128]{1,0:T(8,128)(2,1)S(1)}, u32[]{:S(2)}, u32[]{:S(2)}) collective-permute-start(bf16[256,128]{1,0:T(8,128)(2,1)S(1)} %get-tuple-element.65), channel_id=1, source_target_pairs={{0,12},{1,13},{2,14},{3,15},{4,0},{5,1},{6,2},{7,3},{8,4},{9,5},{1... | collective-permute-start | bytes 196616 | tf_op jit(solution)/shard_map/ppermute | solution.py:356
  85.2 2.4 %collective-permute-start.26 = (bf16[4,256,256]{2,1,0:T(8,128)(2,1)S(1)}, bf16[4,256,256]{2,1,0:T(8,128)(2,1)S(1)}, u32[]{:S(2)}, u32[]{:S(2)}) collective-permute-start(bf16[4,256,256]{2,1,0:T(8,128)(2,1)S(1)} %get-tuple-element.74), channel_id=1, source_target_pairs={{0,1},{1,0},{2,3},{3,2},{4,5},{5,4},{6,7},{7,6},{8,9},{9,8},{10,11... | collective-permute-start | bytes 1572872 | tf_op jit(solution)/shard_map/ppermute | solution.py:356
  85.5 2.1 %collective-permute-start.21 = (bf16[512,256]{1,0:T(8,128)(2,1)S(1)}, bf16[512,256]{1,0:T(8,128)(2,1)S(1)}, u32[]{:S(2)}, u32[]{:S(2)}) collective-permute-start(bf16[512,256]{1,0:T(8,128)(2,1)S(1)} %shard_map.98.gated), channel_id=1, source_target_pairs={{0,1},{1,0},{2,3},{3,2},{4,5},{5,4},{6,7},{7,6},{8,9},{9,8},{10,11... | collective-permute-start | bytes 786440 | tf_op jit(solution)/shard_map/ppermute | solution.py:356
  89.0 10.2 %collective-permute-start.27 = (bf16[128,1024]{1,0:T(8,128)(2,1)S(1)}, bf16[128,1024]{1,0:T(8,128)(2,1)S(1)}, u32[]{:S(2)}, u32[]{:S(2)}) collective-permute-start(bf16[128,1024]{1,0:T(8,128)(2,1)S(1)} %get-tuple-element.76), channel_id=1, source_target_pairs={{0,18},{1,19},{2,16},{3,17},{4,22},{5,23},{6,20},{7,21},{8,26},{9,... | collective-permute-start | bytes 786440 | tf_op jit(solution)/shard_map/ppermute | solution.py:356
  90.4 13.6 %collective-permute-start.28 = (bf16[128,1024]{1,0:T(8,128)(2,1)S(1)}, bf16[128,1024]{1,0:T(8,128)(2,1)S(1)}, u32[]{:S(2)}, u32[]{:S(2)}) collective-permute-start(bf16[128,1024]{1,0:T(8,128)(2,1)S(1)} %get-tuple-element.77), channel_id=1, source_target_pairs={{0,16},{1,17},{2,18},{3,19},{4,20},{5,21},{6,22},{7,23},{8,24},{9,... | collective-permute-start | bytes 786440 | tf_op jit(solution)/shard_map/ppermute | solution.py:356
  91.9 12.1 %collective-permute-start.29 = (bf16[128,1024]{1,0:T(8,128)(2,1)S(1)}, bf16[128,1024]{1,0:T(8,128)(2,1)S(1)}, u32[]{:S(2)}, u32[]{:S(2)}) collective-permute-start(bf16[128,1024]{1,0:T(8,128)(2,1)S(1)} %get-tuple-element.78), channel_id=1, source_target_pairs={{0,2},{1,3},{2,0},{3,1},{4,6},{5,7},{6,4},{7,5},{8,10},{9,11},{10,... | collective-permute-start | bytes 786440 | tf_op jit(solution)/shard_map/ppermute | solution.py:356

commit v8 on v7

--- a/solution.py
+++ b/solution.py
@@ -389,10 +389,10 @@
     filters = [filters[0]] + [to_z(filters[r], r) for r in (1, 2, 3)]
     v1 = to_z(own_v, 1)
     q1 = to_z(own_o, 1)
-    v2 = to_z(after(v1, near, received[1], q1), 1)
-    q2 = to_z(q1, 1)
-    mine = in_vmem(join_tokens, shape((512, 512), BF16), moved=1 << 20)(after(own, v2, q2, *filters[1:]), *received)
-    v3 = to_z(after(v2, filters[1]), 1)
+    v2 = to_z(after(v1, received[0], received[1]), 1)
+    q2 = to_z(after(q1, v1), 1)
+    mine = in_vmem(join_tokens, shape((512, 512), BF16), moved=1 << 20)(after(own, v2, q2), *received)
+    v3 = to_z(after(v2, mine), 1)
     q3 = to_z(q2, 1)
     other = to_core(mine)
     got_o = to_x(after(away_o, v2))
@@ -403,14 +403,14 @@
         [pltpu.VMEM((512, 512), F32)],
         flops=1 << 29,
         moved=2 << 20,
-    )(after(mine, q3), other, own_v, v1, v2, v3)
+    )(after(mine, q3, near, got_o), other, own_v, v1, v2, v3)
     r2 = to_z(after(r1, keep), 1)
     drive, *sends = in_vmem(
         drive_kernel,
         [shape((512, 256), F32)] + [block] * 4,
         [pltpu.VMEM((512, 256), BF16), pltpu.VMEM((4, 256, 128), BF16)],
         moved=2 << 20,
-    )(keep, to_x(give), *plane, skip[None, :])
+    )(after(keep, filters[1], filters[2]), to_x(give), *plane, skip[None, :])
     columns = [sends[0]] + [to_z(sends[r], r) for r in (1, 2, 3)]
     r3 = to_z(after(r2, *columns[1:]), 1)
     table, table_t = tables()

time: 105 us -> 102 us (0.971)
  waiting for transfers between devices: 60.9 us -> 50.2 us
  starting transfers between devices: 32.4 us -> 39 us
  local copies, waits for them, and re-layouts: 0.05 us -> 1.85 us
    ppermute x30, waiting for transfers between devices: 60.9 us -> 50.2 us  [permute(): return lax.ppermute(values, AXES, pairs)]
    ppermute x30, starting transfers between devices: 32.4 us -> 39 us  [permute(): return lax.ppermute(values, AXES, pairs)]
    unnamed x20, local copies, waits for them, and re-layouts: 0.05 us -> 1.85 us
  transfers between devices with their start and end apart: 30 -> 30, of which waited for: 16 -> 17; matrix products, arithmetic and copies ran while one was open for 0% -> 0% of each run, Pallas kernels for 4% -> 5%
where the time goes in v8:
time: 102 us
  waiting for transfers between devices  50.2 us (49%)
  starting transfers between devices  39 us (38%)
  Pallas kernels  10.2 us (10%)
  local copies, waits for them, and re-layouts  1.85 us (2%)
    ppermute x30, waiting for transfers between devices, permute(): return lax.ppermute(values, AXES, pairs)  50.2 us
    ppermute x30, starting transfers between devices, permute(): return lax.ppermute(values, AXES, pairs)  39 us
    pallas_call x8, Pallas kernels, call(): pl.pallas_call(kernel, out_shape=out_shape, in_specs=specs, out_specs=jax...  5.62 us
    pallas_call x2, Pallas kernels, call(): pl.pallas_call(kernel, out_shape=out_shape, in_specs=[pl.BlockSpec(memory...  4.6 us
  transfers between devices with their start and end apart: 30, of which 17 were waited for; matrix products, arithmetic and copies ran while one was open for 0% of the time, Pallas kernels for 5%

profile of v8, /device:TPU:0, one launch (start us, length us, event | category | flops | bytes accessed | tf_op | source)
XLA Modules:
  0.0 102.3 jit_solution(310494808047411949)
XLA Ops:
  0.0 1.8 %shard_map.91.after.w0 = bf16[256,512]{1,0:T(8,128)(2,1)} custom-call(bf16[256,1024]{1,0:T(8,128)(2,1)} %value.1), custom_call_target="tpu_custom_call" | custom-call | tf_op jit(solution)/shard_map/pallas_call | solution.py:106
  1.8 3.1 %collective-permute-start = (bf16[256,512]{1,0:T(8,128)(2,1)}, bf16[256,512]{1,0:T(8,128)(2,1)S(1)}, u32[]{:S(2)}, u32[]{:S(2)}) collective-permute-start(bf16[256,512]{1,0:T(8,128)(2,1)} %shard_map.91.after.w0), channel_id=1, source_target_pairs={{0,4},{1,5},{2,6},{3,7},{4,8},{5,9},{6,10},{7,11},{8,12},{9,13},{1... | collective-permute-start | bytes 786440 | tf_op jit(solution)/shard_map/ppermute | solution.py:356
  4.9 2.8 %shard_map.92 = (bf16[128,1024]{1,0:T(8,128)(2,1)}, bf16[128,1024]{1,0:T(8,128)(2,1)}, bf16[128,1024]{1,0:T(8,128)(2,1)}, bf16[128,1024]{1,0:T(8,128)(2,1)}, bf1...) custom-call(bf16[128,1024]{1,0:T(8,128)(2,1)} %tokens.1, bf16[128,1024]{1,0:T(8,128)(2,1)} %key.1, ...), custom_call_target="tpu_custom_call" | custom-call | tf_op jit(solution)/shard_map/pallas_call | solution.py:106
  7.7 1.6 %collective-permute-start.1 = (bf16[128,1024]{1,0:T(8,128)(2,1)}, bf16[128,1024]{1,0:T(8,128)(2,1)S(1)}, u32[]{:S(2)}, u32[]{:S(2)}) collective-permute-start(bf16[128,1024]{1,0:T(8,128)(2,1)} %get-tuple-element.45), channel_id=1, source_target_pairs={{0,2},{1,3},{2,0},{3,1},{4,6},{5,7},{6,4},{7,5},{8,10},{9,11},{10,... | collective-permute-start | bytes 786440 | tf_op jit(solution)/shard_map/ppermute | solution.py:356
  9.2 1.5 %collective-permute-start.2 = (bf16[128,1024]{1,0:T(8,128)(2,1)}, bf16[128,1024]{1,0:T(8,128)(2,1)S(1)}, u32[]{:S(2)}, u32[]{:S(2)}) collective-permute-start(bf16[128,1024]{1,0:T(8,128)(2,1)} %get-tuple-element.46), channel_id=1, source_target_pairs={{0,16},{1,17},{2,18},{3,19},{4,20},{5,21},{6,22},{7,23},{8,24},{9,... | collective-permute-start | bytes 786440 | tf_op jit(solution)/shard_map/ppermute | solution.py:356
  10.8 1.6 %collective-permute-start.4 = (bf16[256,256]{1,0:T(8,128)(2,1)}, bf16[256,256]{1,0:T(8,128)(2,1)S(1)}, u32[]{:S(2)}, u32[]{:S(2)}) collective-permute-start(bf16[256,256]{1,0:T(8,128)(2,1)} %get-tuple-element.48.refs_0_), channel_id=1, source_target_pairs={{0,4},{1,5},{2,6},{3,7},{4,8},{5,9},{6,10},{7,11},{8,12},{9,13},{1... | collective-permute-start | bytes 393224 | tf_op jit(solution)/shard_map/ppermute | solution.py:356
  12.3 1.1 %collective-permute-done.w1 = bf16[256,512]{1,0:T(8,128)(2,1)S(1)} collective-permute-done((bf16[256,512]{1,0:T(8,128)(2,1)}, bf16[256,512]{1,0:T(8,128)(2,1)S(1)}, u32[]{:S(2)}, u32[]{:S(2)}) %collective-permute-start) | collective-permute-done | bytes 262176 | tf_op jit(solution)/shard_map/ppermute | solution.py:356
  13.4 2.3 %collective-permute-done.1.refs_1_.g1 = bf16[128,1024]{1,0:T(8,128)(2,1)S(1)} collective-permute-done((bf16[128,1024]{1,0:T(8,128)(2,1)}, bf16[128,1024]{1,0:T(8,128)(2,1)S(1)}, u32[]{:S(2)}, u32[]{:S(2)}) %collective-permute-start.1) | collective-permute-done | bytes 262176 | tf_op jit(solution)/shard_map/ppermute | solution.py:356
  15.7 1.2 %collective-permute-done.2.refs_2_.g2 = bf16[128,1024]{1,0:T(8,128)(2,1)S(1)} collective-permute-done((bf16[128,1024]{1,0:T(8,128)(2,1)}, bf16[128,1024]{1,0:T(8,128)(2,1)S(1)}, u32[]{:S(2)}, u32[]{:S(2)}) %collective-permute-start.2) | collective-permute-done | bytes 262176 | tf_op jit(solution)/shard_map/ppermute | solution.py:356
  16.9 1.6 %collective-permute-start.3 = (bf16[256,512]{1,0:T(8,128)(2,1)S(1)}, bf16[256,512]{1,0:T(8,128)(2,1)S(1)}, u32[]{:S(2)}, u32[]{:S(2)}) collective-permute-start(bf16[256,512]{1,0:T(8,128)(2,1)S(1)} %collective-permute-done.w1), channel_id=1, source_target_pairs={{0,4},{1,5},{2,6},{3,7},{4,8},{5,9},{6,10},{7,11},{8,12},{9,13},{1... | collective-permute-start | bytes 786440 | tf_op jit(solution)/shard_map/ppermute | solution.py:356
  18.5 1.5 %collective-permute-start.6 = (bf16[128,1024]{1,0:T(8,128)(2,1)}, bf16[128,1024]{1,0:T(8,128)(2,1)S(1)}, u32[]{:S(2)}, u32[]{:S(2)}) collective-permute-start(bf16[128,1024]{1,0:T(8,128)(2,1)} %get-tuple-element.51), channel_id=1, source_target_pairs={{0,18},{1,19},{2,16},{3,17},{4,22},{5,23},{6,20},{7,21},{8,26},{9,... | collective-permute-start | bytes 786440 | tf_op jit(solution)/shard_map/ppermute | solution.py:356
  20.0 1.6 %collective-permute-start.5 = (bf16[256,256]{1,0:T(8,128)(2,1)S(1)}, bf16[256,256]{1,0:T(8,128)(2,1)S(1)}, u32[]{:S(2)}, u32[]{:S(2)}) collective-permute-start(bf16[256,256]{1,0:T(8,128)(2,1)S(1)} %collective-permute-done.4.refs_2_), channel_id=1, source_target_pairs={{0,4},{1,5},{2,6},{3,7},{4,8},{5,9},{6,10},{7,11},{8,12},{9,13},{1... | collective-permute-start | bytes 393224 | tf_op jit(solution)/shard_map/ppermute | solution.py:356
  21.6 6.5 %collective-permute-done.5.refs_4_ = bf16[256,256]{1,0:T(8,128)(2,1)S(1)} collective-permute-done((bf16[256,256]{1,0:T(8,128)(2,1)S(1)}, bf16[256,256]{1,0:T(8,128)(2,1)S(1)}, u32[]{:S(2)}, u32[]{:S(2)}) %collective-permute-start.5) | collective-permute-done | bytes 131104 | tf_op jit(solution)/shard_map/ppermute | solution.py:356
  28.1 0.0 collective-permute-done.3.w2
  28.1 1.0 copy-done.2
  29.2 0.1 collective-permute-start.10
  29.2 0.8 copy-done.8
  30.1 0.6 collective-permute-start.8
  30.7 0.0 collective-permute-start.11
  30.7 1.4 %collective-permute-start.7 = (bf16[256,256]{1,0:T(8,128)(2,1)S(1)}, bf16[256,256]{1,0:T(8,128)(2,1)S(1)}, u32[]{:S(2)}, u32[]{:S(2)}) collective-permute-start(bf16[256,256]{1,0:T(8,128)(2,1)S(1)} %collective-permute-done.5.refs_4_), channel_id=1, source_target_pairs={{0,4},{1,5},{2,6},{3,7},{4,8},{5,9},{6,10},{7,11},{8,12},{9,13},{1... | collective-permute-start | bytes 393224 | tf_op jit(solution)/shard_map/ppermute | solution.py:356
  32.0 1.4 %collective-permute-start.9 = (bf16[256,256]{1,0:T(8,128)(2,1)S(1)}, bf16[256,256]{1,0:T(8,128)(2,1)S(1)}, u32[]{:S(2)}, u32[]{:S(2)}) collective-permute-start(bf16[256,256]{1,0:T(8,128)(2,1)S(1)} %copy-done.9), channel_id=1, source_target_pairs={{0,2},{1,3},{2,0},{3,1},{4,6},{5,7},{6,4},{7,5},{8,10},{9,11},{10,... | collective-permute-start | bytes 393224 | tf_op jit(solution)/shard_map/ppermute | solution.py:356
  33.5 5.8 %collective-permute-done.8.near = bf16[2,2,128,256]{3,2,1,0:T(8,128)(2,1)S(1)} collective-permute-done((bf16[2,2,128,256]{3,2,1,0:T(8,128)(2,1)S(1)}, bf16[2,2,128,256]{3,2,1,0:T(8,128)(2,1)S(1)}, u32[]{:S(2)}, u32[]{:S(2)}) %collective-permute-start.8) | collective-permute-done | bytes 262176 | tf_op jit(solution)/shard_map/ppermute | solution.py:356
  39.3 3.6 %collective-permute-done.7.refs_6_ = bf16[256,256]{1,0:T(8,128)(2,1)S(1)} collective-permute-done((bf16[256,256]{1,0:T(8,128)(2,1)S(1)}, bf16[256,256]{1,0:T(8,128)(2,1)S(1)}, u32[]{:S(2)}, u32[]{:S(2)}) %collective-permute-start.7) | collective-permute-done | bytes 131104 | tf_op jit(solution)/shard_map/ppermute | solution.py:356
  42.9 0.0 collective-permute-done.9.refs_1_
  42.9 0.0 collective-permute-done.11.w3
  42.9 0.0 collective-permute-done.10.other
  42.9 1.3 %shard_map.94 = (f32[512,256]{1,0:T(8,128)S(1)}, bf16[512,256]{1,0:T(8,128)(2,1)S(1)}) custom-call(bf16[512,512]{1,0:T(8,128)(2,1)S(1)} %shard_map.93.mine, bf16[512,512]{1,0:T(8,128)(2,1)S(1)} %collective-permute-done.10.other, bf16[256,512]{1,0:T(8,128)(2,1)S(1)} %copy-done.1, bf16[256,512]{1,0:T(8,128)(2,1)S(1)} %collective-permute-done.w1, ...), custom_call_target="tpu_custom_call" | custom-call | flops 536870912 | bytes 2097152 | tf_op jit(solution)/shard_map/pallas_call | solution.py:37
  44.2 1.5 %collective-permute-start.14 = (bf16[512,256]{1,0:T(8,128)(2,1)S(1)}, bf16[512,256]{1,0:T(8,128)(2,1)S(1)}, u32[]{:S(2)}, u32[]{:S(2)}) collective-permute-start(bf16[512,256]{1,0:T(8,128)(2,1)S(1)} %get-tuple-element.61), channel_id=1, source_target_pairs={{0,2},{1,3},{2,0},{3,1},{4,6},{5,7},{6,4},{7,5},{8,10},{9,11},{10,... | collective-permute-start | bytes 786440 | tf_op jit(solution)/shard_map/ppermute | solution.py:356
  45.7 0.3 shard_map.95
  46.0 0.0 copy-start.5
  46.0 0.0 copy-start.6
  46.1 0.1 collective-permute-start.12
  46.1 4.4 %collective-permute-start.13 = (bf16[2,2,128,128]{3,2,1,0:T(8,128)(2,1)S(1)}, bf16[2,2,128,128]{3,2,1,0:T(8,128)(2,1)S(1)}, u32[]{:S(2)}, u32[]{:S(2)}) collective-permute-start(bf16[2,2,128,128]{3,2,1,0:T(8,128)(2,1)S(1)} %get-tuple-element.59), channel_id=1, source_target_pairs={{0,8},{1,9},{2,10},{3,11},{4,12},{5,13},{6,14},{7,15},{8,0},{9,1},... | collective-permute-start | bytes 393224 | tf_op jit(solution)/shard_map/ppermute | solution.py:356
  50.5 3.5 %collective-permute-done.23.refs_3_ = bf16[256,256]{1,0:T(8,128)(2,1)S(1)} collective-permute-done((bf16[256,256]{1,0:T(8,128)(2,1)S(1)}, bf16[256,256]{1,0:T(8,128)(2,1)S(1)}, u32[]{:S(2)}, u32[]{:S(2)}) %collective-permute-start.23) | collective-permute-done | bytes 131104 | tf_op jit(solution)/shard_map/ppermute | solution.py:356
  54.0 0.0 collective-permute-start.24
  54.0 3.8 %collective-permute-start.18 = (bf16[2,2,128,128]{3,2,1,0:T(8,128)(2,1)S(1)}, bf16[2,2,128,128]{3,2,1,0:T(8,128)(2,1)S(1)}, u32[]{:S(2)}, u32[]{:S(2)}) collective-permute-start(bf16[2,2,128,128]{3,2,1,0:T(8,128)(2,1)S(1)} %get-tuple-element.67), channel_id=1, source_target_pairs={{0,12},{1,13},{2,14},{3,15},{4,0},{5,1},{6,2},{7,3},{8,4},{9,5},{1... | collective-permute-start | bytes 393224 | tf_op jit(solution)/shard_map/ppermute | solution.py:356
  57.8 4.6 %collective-permute-done.13.refs_6_ = bf16[2,2,128,128]{3,2,1,0:T(8,128)(2,1)S(1)} collective-permute-done((bf16[2,2,128,128]{3,2,1,0:T(8,128)(2,1)S(1)}, bf16[2,2,128,128]{3,2,1,0:T(8,128)(2,1)S(1)}, u32[]{:S(2)}, u32[]{:S(2)}) %collective-permute-start.13) | collective-permute-done | bytes 131104 | tf_op jit(solution)/shard_map/ppermute | solution.py:356
  62.5 0.3 shard_map.96
  62.8 0.1 collective-permute-start.15
  62.9 0.1 collective-permute-start.16
  63.0 3.7 %collective-permute-start.17 = (bf16[256,128]{1,0:T(8,128)(2,1)S(1)}, bf16[256,128]{1,0:T(8,128)(2,1)S(1)}, u32[]{:S(2)}, u32[]{:S(2)}) collective-permute-start(bf16[256,128]{1,0:T(8,128)(2,1)S(1)} %get-tuple-element.65), channel_id=1, source_target_pairs={{0,12},{1,13},{2,14},{3,15},{4,0},{5,1},{6,2},{7,3},{8,4},{9,5},{1... | collective-permute-start | bytes 196616 | tf_op jit(solution)/shard_map/ppermute | solution.py:356
  66.7 2.9 %collective-permute-done.15.refs_1_ = bf16[256,128]{1,0:T(8,128)(2,1)S(1)} collective-permute-done((bf16[256,128]{1,0:T(8,128)(2,1)S(1)}, bf16[256,128]{1,0:T(8,128)(2,1)S(1)}, u32[]{:S(2)}, u32[]{:S(2)}) %collective-permute-start.15) | collective-permute-done | bytes 65568 | tf_op jit(solution)/shard_map/ppermute | solution.py:356
  69.6 1.7 %collective-permute-done.16.refs_2_ = bf16[256,128]{1,0:T(8,128)(2,1)S(1)} collective-permute-done((bf16[256,128]{1,0:T(8,128)(2,1)S(1)}, bf16[256,128]{1,0:T(8,128)(2,1)S(1)}, u32[]{:S(2)}, u32[]{:S(2)}) %collective-permute-start.16) | collective-permute-done | bytes 65568 | tf_op jit(solution)/shard_map/ppermute | solution.py:356
  71.3 1.4 %collective-permute-start.25 = (bf16[256,256]{1,0:T(8,128)(2,1)S(1)}, bf16[256,256]{1,0:T(8,128)(2,1)S(1)}, u32[]{:S(2)}, u32[]{:S(2)}) collective-permute-start(bf16[256,256]{1,0:T(8,128)(2,1)S(1)} %collective-permute-done.24.refs_5_), channel_id=1, source_target_pairs={{0,4},{1,5},{2,6},{3,7},{4,8},{5,9},{6,10},{7,11},{8,12},{9,13},{1... | collective-permute-start | bytes 393224 | tf_op jit(solution)/shard_map/ppermute | solution.py:356
  72.7 1.8 %shard_map.97 = (bf16[256,128]{1,0:T(8,128)(2,1)S(1)}, bf16[256,128]{1,0:T(8,128)(2,1)S(1)}, bf16[256,128]{1,0:T(8,128)(2,1)S(1)}, bf16[256,128]{1,0:T(8,128)(2,1)S(1)}) custom-call(bf16[256,128]{1,0:T(8,128)(2,1)S(1)} %get-tuple-element.62.refs_0_, bf16[256,128]{1,0:T(8,128)(2,1)S(1)} %collective-permute-done.15.refs_1_, ...), custom_call_target="tpu_custom_call" | custom-call | flops 1073741824 | bytes 5242880 | tf_op jit(solution)/shard_map/pallas_call | solution.py:37
  74.5 0.1 collective-permute-start.19
  74.6 3.0 %collective-permute-start.20 = (bf16[256,128]{1,0:T(8,128)(2,1)S(1)}, bf16[256,128]{1,0:T(8,128)(2,1)S(1)}, u32[]{:S(2)}, u32[]{:S(2)}) collective-permute-start(bf16[256,128]{1,0:T(8,128)(2,1)S(1)} %get-tuple-element.70), channel_id=1, source_target_pairs={{0,8},{1,9},{2,10},{3,11},{4,12},{5,13},{6,14},{7,15},{8,0},{9,1},... | collective-permute-start | bytes 196616 | tf_op jit(solution)/shard_map/ppermute | solution.py:356
  77.6 0.9 collective-permute-start.21
  78.5 2.5 %collective-permute-done.19.e1 = bf16[256,128]{1,0:T(8,128)(2,1)S(1)} collective-permute-done((bf16[256,128]{1,0:T(8,128)(2,1)S(1)}, bf16[256,128]{1,0:T(8,128)(2,1)S(1)}, u32[]{:S(2)}, u32[]{:S(2)}) %collective-permute-start.19) | collective-permute-done | bytes 65568 | tf_op jit(solution)/shard_map/ppermute | solution.py:356
  81.0 1.4 %collective-permute-done.20.e2 = bf16[256,128]{1,0:T(8,128)(2,1)S(1)} collective-permute-done((bf16[256,128]{1,0:T(8,128)(2,1)S(1)}, bf16[256,128]{1,0:T(8,128)(2,1)S(1)}, u32[]{:S(2)}, u32[]{:S(2)}) %collective-permute-start.20) | collective-permute-done | bytes 65568 | tf_op jit(solution)/shard_map/ppermute | solution.py:356
  82.4 0.1 collective-permute-done.21.e3
  82.5 0.1 shard_map.99
  82.6 0.1 collective-permute-start.26
  82.7 0.2 shard_map.98.gated
  82.9 0.6 collective-permute-start.22
  83.5 1.5 %collective-permute-done.22.other = bf16[512,256]{1,0:T(8,128)(2,1)S(1)} collective-permute-done((bf16[512,256]{1,0:T(8,128)(2,1)S(1)}, bf16[512,256]{1,0:T(8,128)(2,1)S(1)}, u32[]{:S(2)}, u32[]{:S(2)}) %collective-permute-start.22) | collective-permute-done | bytes 262176 | tf_op jit(solution)/shard_map/ppermute | solution.py:356
  85.0 1.5 %shard_map.100 = (f32[128,1024]{1,0:T(8,128)S(1)}, bf16[128,1024]{1,0:T(8,128)(2,1)S(1)}, bf16[128,1024]{1,0:T(8,128)(2,1)S(1)}, bf16[128,1024]{1,0:T(8,128)(2,1)S(1)}) custom-call(bf16[512,256]{1,0:T(8,128)(2,1)S(1)} %shard_map.98.gated, bf16[512,256]{1,0:T(8,128)(2,1)S(1)} %collective-permute-done.22.other, ...), custom_call_target="tpu_custom_call" | custom-call | flops 1073741824 | bytes 4194304 | tf_op jit(solution)/shard_map/pallas_call | solution.py:37
  86.4 0.6 collective-permute-start.29
  87.1 1.5 %collective-permute-start.28 = (bf16[128,1024]{1,0:T(8,128)(2,1)S(1)}, bf16[128,1024]{1,0:T(8,128)(2,1)S(1)}, u32[]{:S(2)}, u32[]{:S(2)}) collective-permute-start(bf16[128,1024]{1,0:T(8,128)(2,1)S(1)} %get-tuple-element.81), channel_id=1, source_target_pairs={{0,16},{1,17},{2,18},{3,19},{4,20},{5,21},{6,22},{7,23},{8,24},{9,... | collective-permute-start | bytes 786440 | tf_op jit(solution)/shard_map/ppermute | solution.py:356
  88.6 1.4 %collective-permute-start.27 = (bf16[128,1024]{1,0:T(8,128)(2,1)S(1)}, bf16[128,1024]{1,0:T(8,128)(2,1)S(1)}, u32[]{:S(2)}, u32[]{:S(2)}) collective-permute-start(bf16[128,1024]{1,0:T(8,128)(2,1)S(1)} %get-tuple-element.80), channel_id=1, source_target_pairs={{0,18},{1,19},{2,16},{3,17},{4,22},{5,23},{6,20},{7,21},{8,26},{9,... | collective-permute-start | bytes 786440 | tf_op jit(solution)/shard_map/ppermute | solution.py:356
  90.0 5.7 %collective-permute-done.29 = bf16[128,1024]{1,0:T(8,128)(2,1)S(1)} collective-permute-done((bf16[128,1024]{1,0:T(8,128)(2,1)S(1)}, bf16[128,1024]{1,0:T(8,128)(2,1)S(1)}, u32[]{:S(2)}, u32[]{:S(2)}) %collective-permute-start.29) | collective-permute-done | bytes 262176 | tf_op jit(solution)/shard_map/ppermute | solution.py:356
  95.7 4.2 %collective-permute-done.28 = bf16[128,1024]{1,0:T(8,128)(2,1)S(1)} collective-permute-done((bf16[128,1024]{1,0:T(8,128)(2,1)S(1)}, bf16[128,1024]{1,0:T(8,128)(2,1)S(1)}, u32[]{:S(2)}, u32[]{:S(2)}) %collective-permute-start.28) | collective-permute-done | bytes 262176 | tf_op jit(solution)/shard_map/ppermute | solution.py:356
  99.9 1.6 %collective-permute-done.27 = bf16[128,1024]{1,0:T(8,128)(2,1)S(1)} collective-permute-done((bf16[128,1024]{1,0:T(8,128)(2,1)S(1)}, bf16[128,1024]{1,0:T(8,128)(2,1)S(1)}, u32[]{:S(2)}, u32[]{:S(2)}) %collective-permute-start.27) | collective-permute-done | bytes 262176 | tf_op jit(solution)/shard_map/ppermute | solution.py:356
  101.4 0.8 add_convert_fusion
  (27 shorter events, 0.1 us)
Async XLA Ops:
  1.8 11.6 %collective-permute-start = (bf16[256,512]{1,0:T(8,128)(2,1)}, bf16[256,512]{1,0:T(8,128)(2,1)S(1)}, u32[]{:S(2)}, u32[]{:S(2)}) collective-permute-start(bf16[256,512]{1,0:T(8,128)(2,1)} %shard_map.91.after.w0), channel_id=1, source_target_pairs={{0,4},{1,5},{2,6},{3,7},{4,8},{5,9},{6,10},{7,11},{8,12},{9,13},{1... | collective-permute-start | bytes 786440 | tf_op jit(solution)/shard_map/ppermute | solution.py:356
  7.7 8.0 %collective-permute-start.1 = (bf16[128,1024]{1,0:T(8,128)(2,1)}, bf16[128,1024]{1,0:T(8,128)(2,1)S(1)}, u32[]{:S(2)}, u32[]{:S(2)}) collective-permute-start(bf16[128,1024]{1,0:T(8,128)(2,1)} %get-tuple-element.45), channel_id=1, source_target_pairs={{0,2},{1,3},{2,0},{3,1},{4,6},{5,7},{6,4},{7,5},{8,10},{9,11},{10,... | collective-permute-start | bytes 786440 | tf_op jit(solution)/shard_map/ppermute | solution.py:356
  9.2 7.7 %collective-permute-start.2 = (bf16[128,1024]{1,0:T(8,128)(2,1)}, bf16[128,1024]{1,0:T(8,128)(2,1)S(1)}, u32[]{:S(2)}, u32[]{:S(2)}) collective-permute-start(bf16[128,1024]{1,0:T(8,128)(2,1)} %get-tuple-element.46), channel_id=1, source_target_pairs={{0,16},{1,17},{2,18},{3,19},{4,20},{5,21},{6,22},{7,23},{8,24},{9,... | collective-permute-start | bytes 786440 | tf_op jit(solution)/shard_map/ppermute | solution.py:356
  10.8 9.2 %collective-permute-start.4 = (bf16[256,256]{1,0:T(8,128)(2,1)}, bf16[256,256]{1,0:T(8,128)(2,1)S(1)}, u32[]{:S(2)}, u32[]{:S(2)}) collective-permute-start(bf16[256,256]{1,0:T(8,128)(2,1)} %get-tuple-element.48.refs_0_), channel_id=1, source_target_pairs={{0,4},{1,5},{2,6},{3,7},{4,8},{5,9},{6,10},{7,11},{8,12},{9,13},{1... | collective-permute-start | bytes 393224 | tf_op jit(solution)/shard_map/ppermute | solution.py:356
  16.9 11.2 %collective-permute-start.3 = (bf16[256,512]{1,0:T(8,128)(2,1)S(1)}, bf16[256,512]{1,0:T(8,128)(2,1)S(1)}, u32[]{:S(2)}, u32[]{:S(2)}) collective-permute-start(bf16[256,512]{1,0:T(8,128)(2,1)S(1)} %collective-permute-done.w1), channel_id=1, source_target_pairs={{0,4},{1,5},{2,6},{3,7},{4,8},{5,9},{6,10},{7,11},{8,12},{9,13},{1... | collective-permute-start | bytes 786440 | tf_op jit(solution)/shard_map/ppermute | solution.py:356
  18.5 9.6 %collective-permute-start.6 = (bf16[128,1024]{1,0:T(8,128)(2,1)}, bf16[128,1024]{1,0:T(8,128)(2,1)S(1)}, u32[]{:S(2)}, u32[]{:S(2)}) collective-permute-start(bf16[128,1024]{1,0:T(8,128)(2,1)} %get-tuple-element.51), channel_id=1, source_target_pairs={{0,18},{1,19},{2,16},{3,17},{4,22},{5,23},{6,20},{7,21},{8,26},{9,... | collective-permute-start | bytes 786440 | tf_op jit(solution)/shard_map/ppermute | solution.py:356
  20.0 8.1 %collective-permute-start.5 = (bf16[256,256]{1,0:T(8,128)(2,1)S(1)}, bf16[256,256]{1,0:T(8,128)(2,1)S(1)}, u32[]{:S(2)}, u32[]{:S(2)}) collective-permute-start(bf16[256,256]{1,0:T(8,128)(2,1)S(1)} %collective-permute-done.4.refs_2_), channel_id=1, source_target_pairs={{0,4},{1,5},{2,6},{3,7},{4,8},{5,9},{6,10},{7,11},{8,12},{9,13},{1... | collective-permute-start | bytes 393224 | tf_op jit(solution)/shard_map/ppermute | solution.py:356
  28.1 14.8 %copy-start.1 = (bf16[256,512]{1,0:T(8,128)(2,1)S(1)}, bf16[256,512]{1,0:T(8,128)(2,1)}, u32[]{:S(2)}) copy-start(bf16[256,512]{1,0:T(8,128)(2,1)} %shard_map.91.after.w0) | copy-start | bytes 786436
  28.1 1.0 copy-start.2
  29.1 0.9 copy-start.8
  29.1 2.9 %copy-start.9 = (bf16[256,256]{1,0:T(8,128)(2,1)S(1)}, bf16[256,256]{1,0:T(8,128)(2,1)}, u32[]{:S(2)}) copy-start(bf16[256,256]{1,0:T(8,128)(2,1)} %get-tuple-element.54) | copy-start | bytes 393220
  29.2 13.7 %collective-permute-start.10 = (bf16[512,512]{1,0:T(8,128)(2,1)S(1)}, bf16[512,512]{1,0:T(8,128)(2,1)S(1)}, u32[]{:S(2)}, u32[]{:S(2)}) collective-permute-start(bf16[512,512]{1,0:T(8,128)(2,1)S(1)} %shard_map.93.mine), channel_id=1, source_target_pairs={{0,1},{1,0},{2,3},{3,2},{4,5},{5,4},{6,7},{7,6},{8,9},{9,8},{10,11... | collective-permute-start | bytes 1572872 | tf_op jit(solution)/shard_map/ppermute | solution.py:356
  30.1 9.2 %collective-permute-start.8 = (bf16[2,2,128,256]{3,2,1,0:T(8,128)(2,1)S(1)}, bf16[2,2,128,256]{3,2,1,0:T(8,128)(2,1)S(1)}, u32[]{:S(2)}, u32[]{:S(2)}) collective-permute-start(bf16[2,2,128,256]{3,2,1,0:T(8,128)(2,1)S(1)} %copy-done.8), channel_id=1, source_target_pairs={{0,2},{1,3},{2,0},{3,1},{4,6},{5,7},{6,4},{7,5},{8,10},{9,11},{10,... | collective-permute-start | bytes 786440 | tf_op jit(solution)/shard_map/ppermute | solution.py:356
  30.7 12.2 %collective-permute-start.11 = (bf16[256,512]{1,0:T(8,128)(2,1)S(1)}, bf16[256,512]{1,0:T(8,128)(2,1)S(1)}, u32[]{:S(2)}, u32[]{:S(2)}) collective-permute-start(bf16[256,512]{1,0:T(8,128)(2,1)S(1)} %collective-permute-done.3.w2), channel_id=1, source_target_pairs={{0,4},{1,5},{2,6},{3,7},{4,8},{5,9},{6,10},{7,11},{8,12},{9,13},{1... | collective-permute-start | bytes 786440 | tf_op jit(solution)/shard_map/ppermute | solution.py:356
  30.7 12.2 %collective-permute-start.7 = (bf16[256,256]{1,0:T(8,128)(2,1)S(1)}, bf16[256,256]{1,0:T(8,128)(2,1)S(1)}, u32[]{:S(2)}, u32[]{:S(2)}) collective-permute-start(bf16[256,256]{1,0:T(8,128)(2,1)S(1)} %collective-permute-done.5.refs_4_), channel_id=1, source_target_pairs={{0,4},{1,5},{2,6},{3,7},{4,8},{5,9},{6,10},{7,11},{8,12},{9,13},{1... | collective-permute-start | bytes 393224 | tf_op jit(solution)/shard_map/ppermute | solution.py:356
  32.0 13.7 %copy-start = (bf16[2,2,128,1024]{3,2,1,0:T(8,128)(2,1)S(1)}, bf16[2,2,128,1024]{3,2,1,0:T(8,128)(2,1)}, u32[]{:S(2)}) copy-start(bf16[2,2,128,1024]{3,2,1,0:T(8,128)(2,1)} %filt.3) | copy-start | bytes 3145732
  32.0 10.9 %collective-permute-start.9 = (bf16[256,256]{1,0:T(8,128)(2,1)S(1)}, bf16[256,256]{1,0:T(8,128)(2,1)S(1)}, u32[]{:S(2)}, u32[]{:S(2)}) collective-permute-start(bf16[256,256]{1,0:T(8,128)(2,1)S(1)} %copy-done.9), channel_id=1, source_target_pairs={{0,2},{1,3},{2,0},{3,1},{4,6},{5,7},{6,4},{7,5},{8,10},{9,11},{10,... | collective-permute-start | bytes 393224 | tf_op jit(solution)/shard_map/ppermute | solution.py:356
  44.2 18.3 %copy-start.3 = (bf16[128,1024]{1,0:T(8,128)(2,1)S(1)}, bf16[128,1024]{1,0:T(8,128)(2,1)}, u32[]{:S(2)}) copy-start(bf16[128,1024]{1,0:T(8,128)(2,1)} %get-tuple-element.50.refs_0_.g0) | copy-start | bytes 786436
  44.2 18.3 %collective-permute-start.14 = (bf16[512,256]{1,0:T(8,128)(2,1)S(1)}, bf16[512,256]{1,0:T(8,128)(2,1)S(1)}, u32[]{:S(2)}, u32[]{:S(2)}) collective-permute-start(bf16[512,256]{1,0:T(8,128)(2,1)S(1)} %get-tuple-element.61), channel_id=1, source_target_pairs={{0,2},{1,3},{2,0},{3,1},{4,6},{5,7},{6,4},{7,5},{8,10},{9,11},{10,... | collective-permute-start | bytes 786440 | tf_op jit(solution)/shard_map/ppermute | solution.py:356
  45.7 8.3 %collective-permute-start.23 = (bf16[256,256]{1,0:T(8,128)(2,1)S(1)}, bf16[256,256]{1,0:T(8,128)(2,1)S(1)}, u32[]{:S(2)}, u32[]{:S(2)}) collective-permute-start(bf16[256,256]{1,0:T(8,128)(2,1)S(1)} %collective-permute-done.9.refs_1_), channel_id=1, source_target_pairs={{0,4},{1,5},{2,6},{3,7},{4,8},{5,9},{6,10},{7,11},{8,12},{9,13},{1... | collective-permute-start | bytes 393224 | tf_op jit(solution)/shard_map/ppermute | solution.py:356
  45.7 27.0 %copy-start.7 = (bf16[16,256,128]{2,1,0:T(8,128)(2,1)S(1)}, bf16[16,256,128]{2,1,0:T(8,128)(2,1)}, u32[]{:S(2)}) copy-start(bf16[16,256,128]{2,1,0:T(8,128)(2,1)} %constant.5.clone.refs_9_) | copy-start | bytes 3145732
  46.0 16.4 %copy-start.5 = (f32[1024]{0:T(1024)S(1)}, f32[1024]{0:T(1024)}, u32[]{:S(2)}) copy-start(f32[1024]{0:T(1024)} %param.13) | copy-start | bytes 12292
  46.0 26.6 %copy-start.6 = (bf16[16,256,128]{2,1,0:T(8,128)(2,1)S(1)}, bf16[16,256,128]{2,1,0:T(8,128)(2,1)}, u32[]{:S(2)}) copy-start(bf16[16,256,128]{2,1,0:T(8,128)(2,1)} %constant.4.clone.refs_8_) | copy-start | bytes 3145732
  46.1 11.8 %collective-permute-start.12 = (bf16[2,2,128,128]{3,2,1,0:T(8,128)(2,1)S(1)}, bf16[2,2,128,128]{3,2,1,0:T(8,128)(2,1)S(1)}, u32[]{:S(2)}, u32[]{:S(2)}) collective-permute-start(bf16[2,2,128,128]{3,2,1,0:T(8,128)(2,1)S(1)} %get-tuple-element.58), channel_id=1, source_target_pairs={{0,4},{1,5},{2,6},{3,7},{4,8},{5,9},{6,10},{7,11},{8,12},{9,13},{1... | collective-permute-start | bytes 393224 | tf_op jit(solution)/shard_map/ppermute | solution.py:356
  46.1 16.3 %collective-permute-start.13 = (bf16[2,2,128,128]{3,2,1,0:T(8,128)(2,1)S(1)}, bf16[2,2,128,128]{3,2,1,0:T(8,128)(2,1)S(1)}, u32[]{:S(2)}, u32[]{:S(2)}) collective-permute-start(bf16[2,2,128,128]{3,2,1,0:T(8,128)(2,1)S(1)} %get-tuple-element.59), channel_id=1, source_target_pairs={{0,8},{1,9},{2,10},{3,11},{4,12},{5,13},{6,14},{7,15},{8,0},{9,1},... | collective-permute-start | bytes 393224 | tf_op jit(solution)/shard_map/ppermute | solution.py:356
  54.0 12.7 %collective-permute-start.24 = (bf16[256,256]{1,0:T(8,128)(2,1)S(1)}, bf16[256,256]{1,0:T(8,128)(2,1)S(1)}, u32[]{:S(2)}, u32[]{:S(2)}) collective-permute-start(bf16[256,256]{1,0:T(8,128)(2,1)S(1)} %collective-permute-done.23.refs_3_), channel_id=1, source_target_pairs={{0,4},{1,5},{2,6},{3,7},{4,8},{5,9},{6,10},{7,11},{8,12},{9,13},{1... | collective-permute-start | bytes 393224 | tf_op jit(solution)/shard_map/ppermute | solution.py:356
  54.0 18.7 %collective-permute-start.18 = (bf16[2,2,128,128]{3,2,1,0:T(8,128)(2,1)S(1)}, bf16[2,2,128,128]{3,2,1,0:T(8,128)(2,1)S(1)}, u32[]{:S(2)}, u32[]{:S(2)}) collective-permute-start(bf16[2,2,128,128]{3,2,1,0:T(8,128)(2,1)S(1)} %get-tuple-element.67), channel_id=1, source_target_pairs={{0,12},{1,13},{2,14},{3,15},{4,0},{5,1},{6,2},{7,3},{8,4},{9,5},{1... | collective-permute-start | bytes 393224 | tf_op jit(solution)/shard_map/ppermute | solution.py:356
  62.8 6.8 %collective-permute-start.15 = (bf16[256,128]{1,0:T(8,128)(2,1)S(1)}, bf16[256,128]{1,0:T(8,128)(2,1)S(1)}, u32[]{:S(2)}, u32[]{:S(2)}) collective-permute-start(bf16[256,128]{1,0:T(8,128)(2,1)S(1)} %get-tuple-element.63), channel_id=1, source_target_pairs={{0,4},{1,5},{2,6},{3,7},{4,8},{5,9},{6,10},{7,11},{8,12},{9,13},{1... | collective-permute-start | bytes 196616 | tf_op jit(solution)/shard_map/ppermute | solution.py:356
  62.9 8.4 %collective-permute-start.16 = (bf16[256,128]{1,0:T(8,128)(2,1)S(1)}, bf16[256,128]{1,0:T(8,128)(2,1)S(1)}, u32[]{:S(2)}, u32[]{:S(2)}) collective-permute-start(bf16[256,128]{1,0:T(8,128)(2,1)S(1)} %get-tuple-element.64), channel_id=1, source_target_pairs={{0,8},{1,9},{2,10},{3,11},{4,12},{5,13},{6,14},{7,15},{8,0},{9,1},... | collective-permute-start | bytes 196616 | tf_op jit(solution)/shard_map/ppermute | solution.py:356
  63.0 8.3 %collective-permute-start.17 = (bf16[256,128]{1,0:T(8,128)(2,1)S(1)}, bf16[256,128]{1,0:T(8,128)(2,1)S(1)}, u32[]{:S(2)}, u32[]{:S(2)}) collective-permute-start(bf16[256,128]{1,0:T(8,128)(2,1)S(1)} %get-tuple-element.65), channel_id=1, source_target_pairs={{0,12},{1,13},{2,14},{3,15},{4,0},{5,1},{6,2},{7,3},{8,4},{9,5},{1... | collective-permute-start | bytes 196616 | tf_op jit(solution)/shard_map/ppermute | solution.py:356
  71.3 11.1 %collective-permute-start.25 = (bf16[256,256]{1,0:T(8,128)(2,1)S(1)}, bf16[256,256]{1,0:T(8,128)(2,1)S(1)}, u32[]{:S(2)}, u32[]{:S(2)}) collective-permute-start(bf16[256,256]{1,0:T(8,128)(2,1)S(1)} %collective-permute-done.24.refs_5_), channel_id=1, source_target_pairs={{0,4},{1,5},{2,6},{3,7},{4,8},{5,9},{6,10},{7,11},{8,12},{9,13},{1... | collective-permute-start | bytes 393224 | tf_op jit(solution)/shard_map/ppermute | solution.py:356
  72.7 9.8 %copy-start.4 = (bf16[256,256]{1,0:T(8,128)(2,1)S(1)}, bf16[256,256]{1,0:T(8,128)(2,1)}, u32[]{:S(2)}) copy-start(bf16[256,256]{1,0:T(8,128)(2,1)} %get-tuple-element.48.refs_0_) | copy-start | bytes 393220
  74.5 6.5 %collective-permute-start.19 = (bf16[256,128]{1,0:T(8,128)(2,1)S(1)}, bf16[256,128]{1,0:T(8,128)(2,1)S(1)}, u32[]{:S(2)}, u32[]{:S(2)}) collective-permute-start(bf16[256,128]{1,0:T(8,128)(2,1)S(1)} %get-tuple-element.69), channel_id=1, source_target_pairs={{0,4},{1,5},{2,6},{3,7},{4,8},{5,9},{6,10},{7,11},{8,12},{9,13},{1... | collective-permute-start | bytes 196616 | tf_op jit(solution)/shard_map/ppermute | solution.py:356
  74.6 7.8 %collective-permute-start.20 = (bf16[256,128]{1,0:T(8,128)(2,1)S(1)}, bf16[256,128]{1,0:T(8,128)(2,1)S(1)}, u32[]{:S(2)}, u32[]{:S(2)}) collective-permute-start(bf16[256,128]{1,0:T(8,128)(2,1)S(1)} %get-tuple-element.70), channel_id=1, source_target_pairs={{0,8},{1,9},{2,10},{3,11},{4,12},{5,13},{6,14},{7,15},{8,0},{9,1},... | collective-permute-start | bytes 196616 | tf_op jit(solution)/shard_map/ppermute | solution.py:356
  77.6 4.9 %collective-permute-start.21 = (bf16[256,128]{1,0:T(8,128)(2,1)S(1)}, bf16[256,128]{1,0:T(8,128)(2,1)S(1)}, u32[]{:S(2)}, u32[]{:S(2)}) collective-permute-start(bf16[256,128]{1,0:T(8,128)(2,1)S(1)} %get-tuple-element.71), channel_id=1, source_target_pairs={{0,12},{1,13},{2,14},{3,15},{4,0},{5,1},{6,2},{7,3},{8,4},{9,5},{1... | collective-permute-start | bytes 196616 | tf_op jit(solution)/shard_map/ppermute | solution.py:356
  82.6 2.4 %collective-permute-start.26 = (bf16[4,256,256]{2,1,0:T(8,128)(2,1)S(1)}, bf16[4,256,256]{2,1,0:T(8,128)(2,1)S(1)}, u32[]{:S(2)}, u32[]{:S(2)}) collective-permute-start(bf16[4,256,256]{2,1,0:T(8,128)(2,1)S(1)} %get-tuple-element.78), channel_id=1, source_target_pairs={{0,1},{1,0},{2,3},{3,2},{4,5},{5,4},{6,7},{7,6},{8,9},{9,8},{10,11... | collective-permute-start | bytes 1572872 | tf_op jit(solution)/shard_map/ppermute | solution.py:356
  82.9 2.1 %collective-permute-start.22 = (bf16[512,256]{1,0:T(8,128)(2,1)S(1)}, bf16[512,256]{1,0:T(8,128)(2,1)S(1)}, u32[]{:S(2)}, u32[]{:S(2)}) collective-permute-start(bf16[512,256]{1,0:T(8,128)(2,1)S(1)} %shard_map.98.gated), channel_id=1, source_target_pairs={{0,1},{1,0},{2,3},{3,2},{4,5},{5,4},{6,7},{7,6},{8,9},{9,8},{10,11... | collective-permute-start | bytes 786440 | tf_op jit(solution)/shard_map/ppermute | solution.py:356
  86.4 9.2 %collective-permute-start.29 = (bf16[128,1024]{1,0:T(8,128)(2,1)S(1)}, bf16[128,1024]{1,0:T(8,128)(2,1)S(1)}, u32[]{:S(2)}, u32[]{:S(2)}) collective-permute-start(bf16[128,1024]{1,0:T(8,128)(2,1)S(1)} %get-tuple-element.82), channel_id=1, source_target_pairs={{0,2},{1,3},{2,0},{3,1},{4,6},{5,7},{6,4},{7,5},{8,10},{9,11},{10,... | collective-permute-start | bytes 786440 | tf_op jit(solution)/shard_map/ppermute | solution.py:356
  87.1 12.8 %collective-permute-start.28 = (bf16[128,1024]{1,0:T(8,128)(2,1)S(1)}, bf16[128,1024]{1,0:T(8,128)(2,1)S(1)}, u32[]{:S(2)}, u32[]{:S(2)}) collective-permute-start(bf16[128,1024]{1,0:T(8,128)(2,1)S(1)} %get-tuple-element.81), channel_id=1, source_target_pairs={{0,16},{1,17},{2,18},{3,19},{4,20},{5,21},{6,22},{7,23},{8,24},{9,... | collective-permute-start | bytes 786440 | tf_op jit(solution)/shard_map/ppermute | solution.py:356
  88.6 12.8 %collective-permute-start.27 = (bf16[128,1024]{1,0:T(8,128)(2,1)S(1)}, bf16[128,1024]{1,0:T(8,128)(2,1)S(1)}, u32[]{:S(2)}, u32[]{:S(2)}) collective-permute-start(bf16[128,1024]{1,0:T(8,128)(2,1)S(1)} %get-tuple-element.80), channel_id=1, source_target_pairs={{0,18},{1,19},{2,16},{3,17},{4,22},{5,23},{6,20},{7,21},{8,26},{9,... | collective-permute-start | bytes 786440 | tf_op jit(solution)/shard_map/ppermute | solution.py:356

commit v9 on v8

--- a/solution.py
+++ b/solution.py
@@ -82,15 +82,10 @@
         copy.wait()
 
 
-def cut_first(value, own_v, sem):
-    y, _, _, _ = place()
-    copied([(value.at[:, pl.ds(pl.multiple_of(y * 512, 512), 512)], own_v)], sem)
-
-
-def cut_messages(tokens, key, query, out, filt, after, m1, m2, m3, own, own_o, away_o, away_f, sem):
+def cut_messages(tokens, key, query, out, filt, after, m1, m2, m3, own_o, away_o, away_f, sem):
     _, x, _, _ = place()
     moves = [(filt.at[:, :, :, quarter(1)], away_f)]
-    for p, message in enumerate((own, m1, m2, m3)):
+    for p, message in enumerate((m1, m2, m3), 1):
         column = 1 - x if p % 2 else x
         for i in range(2):
             lanes = pl.ds(pl.multiple_of(i * 512 + column * 256, 256), 256)
@@ -135,8 +130,12 @@
 
 
 def join_tokens(*refs):
-    for p, message in enumerate(refs[:4]):
-        refs[4][pl.ds(p * 128, 128), :] = message[:, pl.ds(512, 512)]
+    _, x, _, _ = place()
+    for i in range(2):
+        lanes = pl.ds(pl.multiple_of(i * 512 + x * 256, 256), 256)
+        refs[4][pl.ds(0, 128), pl.ds(i * 256, 256)] = refs[0][:, lanes]
+    for p in (1, 2, 3):
+        refs[4][pl.ds(p * 128, 128), :] = refs[p][:, pl.ds(512, 512)]
 
 
 def value_kernel(mine, other, w0, w1, w2, w3, keep, give, acc):
@@ -166,7 +165,7 @@
     for p, gate in enumerate((g0, g1, g2, g3)):
         rows = pl.ds(p * 128, 128)
         value = (keep[rows, :] + taken[rows, :].astype(F32)).astype(BF16).astype(F32)
-        held = (gate[:, 0:256].astype(F32) * value).astype(BF16)
+        held = ((gate[:, 0:256] if p else gate[:, quarter(0)]).astype(F32) * value).astype(BF16)
         drive[rows, :] = held
         direct[rows, :] = skip[:, quarter(0)] * held.astype(F32)
     low = low_lanes((256, 128))
@@ -302,7 +301,9 @@
         for p, gate in enumerate((g0, g1, g2, g3)):
             rows = pl.ds(p * 128, 128)
             own = parts[p // 2][(p % 2) * 128 : (p % 2) * 128 + 128]
-            query = gate[:, pl.ds(256 + j * 128, 128)].astype(F32)
+            y, x, _, _ = place()
+            base = y * 512 + x * 256 if p == 0 else 256
+            query = gate[:, pl.ds(pl.multiple_of(base + j * 128, 128), 128)].astype(F32)
             gated[rows, lanes] = (query * (own + direct[rows, lanes])).astype(BF16)
 
 
@@ -372,14 +373,13 @@
 
     shape = jax.ShapeDtypeStruct
     block, square = shape((256, 128), BF16), shape((256, 256), BF16)
-    (own_v,) = copy_kernel(cut_first, [shape((256, 512), BF16)])(w_value)
-    laid = [shape((128, 1024), BF16)] * 4 + [square] * 2 + [shape((2, 2, 128, 256), BF16)]
-    *messages, own, own_o, away_o, away_f = copy_kernel(cut_messages, laid)(
+    own_v = lax.dynamic_slice_in_dim(w_value, lax.axis_index("grp") * 512, 512, axis=1)
+    laid = [shape((128, 1024), BF16)] * 3 + [square] * 2 + [shape((2, 2, 128, 256), BF16)]
+    *messages, own_o, away_o, away_f = copy_kernel(cut_messages, laid)(
         tokens, gate_k, gate_q, w_out, filter_spectrum, own_v
     )
     near = to_x(away_f)
     received = [to_peer(messages[p - 1], p) for p in (1, 2, 3)]
-    plane = [own] + received
     filters = in_vmem(
         pack_filter,
         [shape((2, 2, 128, 128), BF16)] * 4,
@@ -389,10 +389,10 @@
     filters = [filters[0]] + [to_z(filters[r], r) for r in (1, 2, 3)]
     v1 = to_z(own_v, 1)
     q1 = to_z(own_o, 1)
-    v2 = to_z(after(v1, received[0], received[1]), 1)
+    v2 = to_z(v1, 1)
     q2 = to_z(after(q1, v1), 1)
-    mine = in_vmem(join_tokens, shape((512, 512), BF16), moved=1 << 20)(after(own, v2, q2), *received)
-    v3 = to_z(after(v2, mine), 1)
+    mine = in_vmem(join_tokens, shape((512, 512), BF16), moved=1 << 20)(tokens, after(received[0], q2), *received[1:])
+    v3 = to_z(v2, 1)
     q3 = to_z(q2, 1)
     other = to_core(mine)
     got_o = to_x(after(away_o, v2))
@@ -410,7 +410,7 @@
         [shape((512, 256), F32)] + [block] * 4,
         [pltpu.VMEM((512, 256), BF16), pltpu.VMEM((4, 256, 128), BF16)],
         moved=2 << 20,
-    )(after(keep, filters[1], filters[2]), to_x(give), *plane, skip[None, :])
+    )(after(keep, filters[1], filters[2]), to_x(give), gate_k, *received, skip[None, :])
     columns = [sends[0]] + [to_z(sends[r], r) for r in (1, 2, 3)]
     r3 = to_z(after(r2, *columns[1:]), 1)
     table, table_t = tables()
@@ -434,7 +434,7 @@
     theirs = to_core(give)
     gated = in_vmem(
         gate_kernel, shape((512, 256), BF16), [pltpu.VMEM((4, 256, 128), BF16)], moved=1 << 20
-    )(*rows, drive, *plane)
+    )(*rows, drive, gate_q, *received)
     gated_other = to_core(gated)
     own, *sends = in_vmem(
         out_kernel,

time: 102 us -> 96.5 us (0.946)
  starting transfers between devices: 39 us -> 35.1 us
  Pallas kernels: 10.2 us -> 8.22 us
    ppermute x30, starting transfers between devices: 39 us -> 35.1 us  [permute(): return lax.ppermute(values, AXES, pairs)]
    pallas_call x2 -> x1, Pallas kernels: 4.6 us -> 2.58 us  [call(): pl.pallas_call(kernel, out_shape=out_shape, in_specs=[pl.BlockSpec(memory...]
  transfers between devices with their start and end apart: 30 -> 30, of which waited for: 17 -> 17; matrix products, arithmetic and copies ran while one was open for 0% -> 0% of each run, Pallas kernels for 5% -> 6%
where the time goes in v9:
time: 96.5 us; the launch traced here: 96.3 us
  waiting for transfers between devices  50.8 us (53%)
  starting transfers between devices  35.1 us (36%)
  Pallas kernels  8.22 us (9%)
  local copies, waits for them, and re-layouts  1.12 us (1%)
    ppermute x30, waiting for transfers between devices, permute(): return lax.ppermute(values, AXES, pairs)  50.8 us
    ppermute x30, starting transfers between devices, permute(): return lax.ppermute(values, AXES, pairs)  35.1 us
    pallas_call x8, Pallas kernels, call(): pl.pallas_call(kernel, out_shape=out_shape, in_specs=specs, out_specs=jax...  5.64 us
    pallas_call x1, Pallas kernels, call(): pl.pallas_call(kernel, out_shape=out_shape, in_specs=[pl.BlockSpec(memory...  2.58 us
  transfers between devices with their start and end apart: 30, of which 17 were waited for; matrix products, arithmetic and copies ran while one was open for 0% of the time, Pallas kernels for 6%

profile of v9, /device:TPU:0, one launch (start us, length us, event | category | flops | bytes accessed | tf_op | source)
XLA Modules:
  0.0 96.3 jit_solution(14309991231449388930)
XLA Ops:
  0.0 1.0 %copy-done = bf16[256,1024]{1,0:T(8,128)(2,1)S(1)} copy-done((bf16[256,1024]{1,0:T(8,128)(2,1)S(1)}, bf16[256,1024]{1,0:T(8,128)(2,1)}, u32[]{:S(2)}) %copy-start) | copy-done | bytes 524312
  1.1 0.0 copy-start.2
  1.1 0.0 copy-start.5
  1.1 3.1 %collective-permute-start.2 = (bf16[256,512]{1,0:T(8,128)(2,1)S(1)}, bf16[256,512]{1,0:T(8,128)(2,1)S(1)}, u32[]{:S(2)}, u32[]{:S(2)}) collective-permute-start(bf16[256,512]{1,0:T(8,128)(2,1)S(1)} %constant_dynamic-slice_fusion.after.w0), channel_id=1, source_target_pairs={{0,4},{1,5},{2,6},{3,7},{4,8},{5,9},{6,10},{7,11},{8,12},{9,13},{1... | collective-permute-start | bytes 786440 | tf_op jit(solution)/shard_map/ppermute | solution.py:357
  4.2 2.6 %shard_map.91 = (bf16[128,1024]{1,0:T(8,128)(2,1)}, bf16[128,1024]{1,0:T(8,128)(2,1)}, bf16[128,1024]{1,0:T(8,128)(2,1)}, bf16[256,256]{1,0:T(8,128)(2,1)}, bf16...) custom-call(bf16[128,1024]{1,0:T(8,128)(2,1)} %refs_0_.1, bf16[128,1024]{1,0:T(8,128)(2,1)} %g0.2, ...), custom_call_target="tpu_custom_call" | custom-call | tf_op jit(solution)/shard_map/pallas_call | solution.py:101
  6.8 1.6 %collective-permute-start.1 = (bf16[256,256]{1,0:T(8,128)(2,1)}, bf16[256,256]{1,0:T(8,128)(2,1)S(1)}, u32[]{:S(2)}, u32[]{:S(2)}) collective-permute-start(bf16[256,256]{1,0:T(8,128)(2,1)} %get-tuple-element.42.refs_0_), channel_id=1, source_target_pairs={{0,4},{1,5},{2,6},{3,7},{4,8},{5,9},{6,10},{7,11},{8,12},{9,13},{1... | collective-permute-start | bytes 393224 | tf_op jit(solution)/shard_map/ppermute | solution.py:357
  8.4 1.5 %collective-permute-start = (bf16[128,1024]{1,0:T(8,128)(2,1)}, bf16[128,1024]{1,0:T(8,128)(2,1)S(1)}, u32[]{:S(2)}, u32[]{:S(2)}) collective-permute-start(bf16[128,1024]{1,0:T(8,128)(2,1)} %get-tuple-element.41), channel_id=1, source_target_pairs={{0,2},{1,3},{2,0},{3,1},{4,6},{5,7},{6,4},{7,5},{8,10},{9,11},{10,... | collective-permute-start | bytes 786440 | tf_op jit(solution)/shard_map/ppermute | solution.py:357
  9.9 1.5 %collective-permute-start.4 = (bf16[128,1024]{1,0:T(8,128)(2,1)}, bf16[128,1024]{1,0:T(8,128)(2,1)S(1)}, u32[]{:S(2)}, u32[]{:S(2)}) collective-permute-start(bf16[128,1024]{1,0:T(8,128)(2,1)} %get-tuple-element.45), channel_id=1, source_target_pairs={{0,16},{1,17},{2,18},{3,19},{4,20},{5,21},{6,22},{7,23},{8,24},{9,... | collective-permute-start | bytes 786440 | tf_op jit(solution)/shard_map/ppermute | solution.py:357
  11.4 0.5 collective-permute-start.5
  11.9 3.4 %collective-permute-done.1.refs_2_ = bf16[256,256]{1,0:T(8,128)(2,1)S(1)} collective-permute-done((bf16[256,256]{1,0:T(8,128)(2,1)}, bf16[256,256]{1,0:T(8,128)(2,1)S(1)}, u32[]{:S(2)}, u32[]{:S(2)}) %collective-permute-start.1) | collective-permute-done | bytes 131104 | tf_op jit(solution)/shard_map/ppermute | solution.py:357
  15.3 1.3 %collective-permute-start.8 = (bf16[256,512]{1,0:T(8,128)(2,1)S(1)}, bf16[256,512]{1,0:T(8,128)(2,1)S(1)}, u32[]{:S(2)}, u32[]{:S(2)}) collective-permute-start(bf16[256,512]{1,0:T(8,128)(2,1)S(1)} %collective-permute-done.2.w1), channel_id=1, source_target_pairs={{0,4},{1,5},{2,6},{3,7},{4,8},{5,9},{6,10},{7,11},{8,12},{9,13},{1... | collective-permute-start | bytes 786440 | tf_op jit(solution)/shard_map/ppermute | solution.py:357
  16.6 1.2 %collective-permute-done.refs_1_.g1 = bf16[128,1024]{1,0:T(8,128)(2,1)S(1)} collective-permute-done((bf16[128,1024]{1,0:T(8,128)(2,1)}, bf16[128,1024]{1,0:T(8,128)(2,1)S(1)}, u32[]{:S(2)}, u32[]{:S(2)}) %collective-permute-start) | collective-permute-done | bytes 262176 | tf_op jit(solution)/shard_map/ppermute | solution.py:357
  17.8 5.7 %collective-permute-done.3.refs_4_ = bf16[256,256]{1,0:T(8,128)(2,1)S(1)} collective-permute-done((bf16[256,256]{1,0:T(8,128)(2,1)S(1)}, bf16[256,256]{1,0:T(8,128)(2,1)S(1)}, u32[]{:S(2)}, u32[]{:S(2)}) %collective-permute-start.3) | collective-permute-done | bytes 131104 | tf_op jit(solution)/shard_map/ppermute | solution.py:357
  23.5 0.0 collective-permute-done.4.refs_2_.g2
  23.5 0.0 collective-permute-done.5.refs_3_.g3
  23.6 0.1 collective-permute-start.10
  23.7 1.6 %collective-permute-start.7 = (bf16[2,2,128,256]{3,2,1,0:T(8,128)(2,1)S(1)}, bf16[2,2,128,256]{3,2,1,0:T(8,128)(2,1)S(1)}, u32[]{:S(2)}, u32[]{:S(2)}) collective-permute-start(bf16[2,2,128,256]{3,2,1,0:T(8,128)(2,1)S(1)} %copy-done.11), channel_id=1, source_target_pairs={{0,2},{1,3},{2,0},{3,1},{4,6},{5,7},{6,4},{7,5},{8,10},{9,11},{10,... | collective-permute-start | bytes 786440 | tf_op jit(solution)/shard_map/ppermute | solution.py:357
  25.2 2.2 %collective-permute-done.8.w2 = bf16[256,512]{1,0:T(8,128)(2,1)S(1)} collective-permute-done((bf16[256,512]{1,0:T(8,128)(2,1)S(1)}, bf16[256,512]{1,0:T(8,128)(2,1)S(1)}, u32[]{:S(2)}, u32[]{:S(2)}) %collective-permute-start.8) | collective-permute-done | bytes 262176 | tf_op jit(solution)/shard_map/ppermute | solution.py:357
  27.4 0.0 collective-permute-start.11
  27.4 0.0 collective-permute-start.6
  27.4 0.0 copy-start.1
  27.4 1.3 %collective-permute-start.9 = (bf16[256,256]{1,0:T(8,128)(2,1)S(1)}, bf16[256,256]{1,0:T(8,128)(2,1)S(1)}, u32[]{:S(2)}, u32[]{:S(2)}) collective-permute-start(bf16[256,256]{1,0:T(8,128)(2,1)S(1)} %copy-done.12), channel_id=1, source_target_pairs={{0,2},{1,3},{2,0},{3,1},{4,6},{5,7},{6,4},{7,5},{8,10},{9,11},{10,... | collective-permute-start | bytes 393224 | tf_op jit(solution)/shard_map/ppermute | solution.py:357
  28.7 4.1 %collective-permute-done.7.near = bf16[2,2,128,256]{3,2,1,0:T(8,128)(2,1)S(1)} collective-permute-done((bf16[2,2,128,256]{3,2,1,0:T(8,128)(2,1)S(1)}, bf16[2,2,128,256]{3,2,1,0:T(8,128)(2,1)S(1)}, u32[]{:S(2)}, u32[]{:S(2)}) %collective-permute-start.7) | collective-permute-done | bytes 262176 | tf_op jit(solution)/shard_map/ppermute | solution.py:357
  32.9 5.7 %collective-permute-done.6.refs_6_ = bf16[256,256]{1,0:T(8,128)(2,1)S(1)} collective-permute-done((bf16[256,256]{1,0:T(8,128)(2,1)S(1)}, bf16[256,256]{1,0:T(8,128)(2,1)S(1)}, u32[]{:S(2)}, u32[]{:S(2)}) %collective-permute-start.6) | collective-permute-done | bytes 131104 | tf_op jit(solution)/shard_map/ppermute | solution.py:357
  38.6 0.0 collective-permute-done.9.refs_1_
  38.6 1.3 %shard_map.93 = (f32[512,256]{1,0:T(8,128)S(1)}, bf16[512,256]{1,0:T(8,128)(2,1)S(1)}) custom-call(bf16[512,512]{1,0:T(8,128)(2,1)S(1)} %shard_map.92.mine, bf16[512,512]{1,0:T(8,128)(2,1)S(1)} %collective-permute-done.10.other, bf16[256,512]{1,0:T(8,128)(2,1)S(1)} %copy-done.3, bf16[256,512]{1,0:T(8,128)(2,1)S(1)} %collective-permute-done.2.w1, ...), custom_call_target="tpu_custom_call" | custom-call | flops 536870912 | bytes 2097152 | tf_op jit(solution)/shard_map/pallas_call | solution.py:37
  39.9 0.0 copy-start.4
  39.9 1.1 %collective-permute-start.14 = (bf16[512,256]{1,0:T(8,128)(2,1)S(1)}, bf16[512,256]{1,0:T(8,128)(2,1)S(1)}, u32[]{:S(2)}, u32[]{:S(2)}) collective-permute-start(bf16[512,256]{1,0:T(8,128)(2,1)S(1)} %get-tuple-element.55), channel_id=1, source_target_pairs={{0,2},{1,3},{2,0},{3,1},{4,6},{5,7},{6,4},{7,5},{8,10},{9,11},{10,... | collective-permute-start | bytes 786440 | tf_op jit(solution)/shard_map/ppermute | solution.py:357
  41.0 0.3 shard_map.94
  41.3 0.0 copy-start.8
  41.3 0.0 copy-start.9
  41.3 0.1 collective-permute-start.12
  41.4 4.4 %collective-permute-start.13 = (bf16[2,2,128,128]{3,2,1,0:T(8,128)(2,1)S(1)}, bf16[2,2,128,128]{3,2,1,0:T(8,128)(2,1)S(1)}, u32[]{:S(2)}, u32[]{:S(2)}) collective-permute-start(bf16[2,2,128,128]{3,2,1,0:T(8,128)(2,1)S(1)} %get-tuple-element.53), channel_id=1, source_target_pairs={{0,8},{1,9},{2,10},{3,11},{4,12},{5,13},{6,14},{7,15},{8,0},{9,1},... | collective-permute-start | bytes 393224 | tf_op jit(solution)/shard_map/ppermute | solution.py:357
  45.8 2.3 %collective-permute-done.23.refs_3_ = bf16[256,256]{1,0:T(8,128)(2,1)S(1)} collective-permute-done((bf16[256,256]{1,0:T(8,128)(2,1)S(1)}, bf16[256,256]{1,0:T(8,128)(2,1)S(1)}, u32[]{:S(2)}, u32[]{:S(2)}) %collective-permute-start.23) | collective-permute-done | bytes 131104 | tf_op jit(solution)/shard_map/ppermute | solution.py:357
  48.1 3.8 %collective-permute-start.18 = (bf16[2,2,128,128]{3,2,1,0:T(8,128)(2,1)S(1)}, bf16[2,2,128,128]{3,2,1,0:T(8,128)(2,1)S(1)}, u32[]{:S(2)}, u32[]{:S(2)}) collective-permute-start(bf16[2,2,128,128]{3,2,1,0:T(8,128)(2,1)S(1)} %get-tuple-element.61), channel_id=1, source_target_pairs={{0,12},{1,13},{2,14},{3,15},{4,0},{5,1},{6,2},{7,3},{8,4},{9,5},{1... | collective-permute-start | bytes 393224 | tf_op jit(solution)/shard_map/ppermute | solution.py:357
  51.9 4.5 %collective-permute-done.13.refs_6_ = bf16[2,2,128,128]{3,2,1,0:T(8,128)(2,1)S(1)} collective-permute-done((bf16[2,2,128,128]{3,2,1,0:T(8,128)(2,1)S(1)}, bf16[2,2,128,128]{3,2,1,0:T(8,128)(2,1)S(1)}, u32[]{:S(2)}, u32[]{:S(2)}) %collective-permute-start.13) | collective-permute-done | bytes 131104 | tf_op jit(solution)/shard_map/ppermute | solution.py:357
  56.5 0.0 collective-permute-done.14.taken
  56.5 0.3 shard_map.95
  56.8 0.1 collective-permute-start.15
  56.9 0.1 collective-permute-start.16
  57.0 3.7 %collective-permute-start.17 = (bf16[256,128]{1,0:T(8,128)(2,1)S(1)}, bf16[256,128]{1,0:T(8,128)(2,1)S(1)}, u32[]{:S(2)}, u32[]{:S(2)}) collective-permute-start(bf16[256,128]{1,0:T(8,128)(2,1)S(1)} %get-tuple-element.59), channel_id=1, source_target_pairs={{0,12},{1,13},{2,14},{3,15},{4,0},{5,1},{6,2},{7,3},{8,4},{9,5},{1... | collective-permute-start | bytes 196616 | tf_op jit(solution)/shard_map/ppermute | solution.py:357
  60.7 2.9 %collective-permute-done.15.refs_1_ = bf16[256,128]{1,0:T(8,128)(2,1)S(1)} collective-permute-done((bf16[256,128]{1,0:T(8,128)(2,1)S(1)}, bf16[256,128]{1,0:T(8,128)(2,1)S(1)}, u32[]{:S(2)}, u32[]{:S(2)}) %collective-permute-start.15) | collective-permute-done | bytes 65568 | tf_op jit(solution)/shard_map/ppermute | solution.py:357
  63.7 1.7 %collective-permute-done.16.refs_2_ = bf16[256,128]{1,0:T(8,128)(2,1)S(1)} collective-permute-done((bf16[256,128]{1,0:T(8,128)(2,1)S(1)}, bf16[256,128]{1,0:T(8,128)(2,1)S(1)}, u32[]{:S(2)}, u32[]{:S(2)}) %collective-permute-start.16) | collective-permute-done | bytes 65568 | tf_op jit(solution)/shard_map/ppermute | solution.py:357
  65.3 1.4 %collective-permute-start.25 = (bf16[256,256]{1,0:T(8,128)(2,1)S(1)}, bf16[256,256]{1,0:T(8,128)(2,1)S(1)}, u32[]{:S(2)}, u32[]{:S(2)}) collective-permute-start(bf16[256,256]{1,0:T(8,128)(2,1)S(1)} %collective-permute-done.24.refs_5_), channel_id=1, source_target_pairs={{0,4},{1,5},{2,6},{3,7},{4,8},{5,9},{6,10},{7,11},{8,12},{9,13},{1... | collective-permute-start | bytes 393224 | tf_op jit(solution)/shard_map/ppermute | solution.py:357
  66.7 1.8 %shard_map.96 = (bf16[256,128]{1,0:T(8,128)(2,1)S(1)}, bf16[256,128]{1,0:T(8,128)(2,1)S(1)}, bf16[256,128]{1,0:T(8,128)(2,1)S(1)}, bf16[256,128]{1,0:T(8,128)(2,1)S(1)}) custom-call(bf16[256,128]{1,0:T(8,128)(2,1)S(1)} %get-tuple-element.56.refs_0_, bf16[256,128]{1,0:T(8,128)(2,1)S(1)} %collective-permute-done.15.refs_1_, ...), custom_call_target="tpu_custom_call" | custom-call | flops 1073741824 | bytes 5242880 | tf_op jit(solution)/shard_map/pallas_call | solution.py:37
  68.5 0.1 collective-permute-start.19
  68.6 3.0 %collective-permute-start.20 = (bf16[256,128]{1,0:T(8,128)(2,1)S(1)}, bf16[256,128]{1,0:T(8,128)(2,1)S(1)}, u32[]{:S(2)}, u32[]{:S(2)}) collective-permute-start(bf16[256,128]{1,0:T(8,128)(2,1)S(1)} %get-tuple-element.64), channel_id=1, source_target_pairs={{0,8},{1,9},{2,10},{3,11},{4,12},{5,13},{6,14},{7,15},{8,0},{9,1},... | collective-permute-start | bytes 196616 | tf_op jit(solution)/shard_map/ppermute | solution.py:357
  71.6 0.9 collective-permute-start.21
  72.5 2.5 %collective-permute-done.19.e1 = bf16[256,128]{1,0:T(8,128)(2,1)S(1)} collective-permute-done((bf16[256,128]{1,0:T(8,128)(2,1)S(1)}, bf16[256,128]{1,0:T(8,128)(2,1)S(1)}, u32[]{:S(2)}, u32[]{:S(2)}) %collective-permute-start.19) | collective-permute-done | bytes 65568 | tf_op jit(solution)/shard_map/ppermute | solution.py:357
  75.0 1.4 %collective-permute-done.20.e2 = bf16[256,128]{1,0:T(8,128)(2,1)S(1)} collective-permute-done((bf16[256,128]{1,0:T(8,128)(2,1)S(1)}, bf16[256,128]{1,0:T(8,128)(2,1)S(1)}, u32[]{:S(2)}, u32[]{:S(2)}) %collective-permute-start.20) | collective-permute-done | bytes 65568 | tf_op jit(solution)/shard_map/ppermute | solution.py:357
  76.4 0.1 collective-permute-done.21.e3
  76.5 0.1 shard_map.98
  76.6 0.1 collective-permute-start.26
  76.7 0.2 shard_map.97.gated
  76.9 0.5 collective-permute-start.22
  77.5 1.5 %collective-permute-done.22.other = bf16[512,256]{1,0:T(8,128)(2,1)S(1)} collective-permute-done((bf16[512,256]{1,0:T(8,128)(2,1)S(1)}, bf16[512,256]{1,0:T(8,128)(2,1)S(1)}, u32[]{:S(2)}, u32[]{:S(2)}) %collective-permute-start.22) | collective-permute-done | bytes 262176 | tf_op jit(solution)/shard_map/ppermute | solution.py:357
  79.0 1.5 %shard_map.99 = (f32[128,1024]{1,0:T(8,128)S(1)}, bf16[128,1024]{1,0:T(8,128)(2,1)S(1)}, bf16[128,1024]{1,0:T(8,128)(2,1)S(1)}, bf16[128,1024]{1,0:T(8,128)(2,1)S(1)}) custom-call(bf16[512,256]{1,0:T(8,128)(2,1)S(1)} %shard_map.97.gated, bf16[512,256]{1,0:T(8,128)(2,1)S(1)} %collective-permute-done.22.other, ...), custom_call_target="tpu_custom_call" | custom-call | flops 1073741824 | bytes 4194304 | tf_op jit(solution)/shard_map/pallas_call | solution.py:37
  80.4 1.8 %collective-permute-start.27 = (bf16[128,1024]{1,0:T(8,128)(2,1)S(1)}, bf16[128,1024]{1,0:T(8,128)(2,1)S(1)}, u32[]{:S(2)}, u32[]{:S(2)}) collective-permute-start(bf16[128,1024]{1,0:T(8,128)(2,1)S(1)} %get-tuple-element.74), channel_id=1, source_target_pairs={{0,18},{1,19},{2,16},{3,17},{4,22},{5,23},{6,20},{7,21},{8,26},{9,... | collective-permute-start | bytes 786440 | tf_op jit(solution)/shard_map/ppermute | solution.py:357
  82.3 1.0 %collective-permute-start.28 = (bf16[128,1024]{1,0:T(8,128)(2,1)S(1)}, bf16[128,1024]{1,0:T(8,128)(2,1)S(1)}, u32[]{:S(2)}, u32[]{:S(2)}) collective-permute-start(bf16[128,1024]{1,0:T(8,128)(2,1)S(1)} %get-tuple-element.75), channel_id=1, source_target_pairs={{0,16},{1,17},{2,18},{3,19},{4,20},{5,21},{6,22},{7,23},{8,24},{9,... | collective-permute-start | bytes 786440 | tf_op jit(solution)/shard_map/ppermute | solution.py:357
  83.3 0.7 collective-permute-start.29
  84.0 6.6 %collective-permute-done.27 = bf16[128,1024]{1,0:T(8,128)(2,1)S(1)} collective-permute-done((bf16[128,1024]{1,0:T(8,128)(2,1)S(1)}, bf16[128,1024]{1,0:T(8,128)(2,1)S(1)}, u32[]{:S(2)}, u32[]{:S(2)}) %collective-permute-start.27) | collective-permute-done | bytes 262176 | tf_op jit(solution)/shard_map/ppermute | solution.py:357
  90.6 4.8 %collective-permute-done.28 = bf16[128,1024]{1,0:T(8,128)(2,1)S(1)} collective-permute-done((bf16[128,1024]{1,0:T(8,128)(2,1)S(1)}, bf16[128,1024]{1,0:T(8,128)(2,1)S(1)}, u32[]{:S(2)}, u32[]{:S(2)}) %collective-permute-start.28) | collective-permute-done | bytes 262176 | tf_op jit(solution)/shard_map/ppermute | solution.py:357
  95.4 0.1 collective-permute-done.29
  95.5 0.8 add_convert_fusion
  (33 shorter events, 0.1 us)
Async XLA Ops:
  0.0 1.0 %copy-start = (bf16[256,1024]{1,0:T(8,128)(2,1)S(1)}, bf16[256,1024]{1,0:T(8,128)(2,1)}, u32[]{:S(2)}) copy-start(bf16[256,1024]{1,0:T(8,128)(2,1)} %param.12) | copy-start | bytes 1572868
  1.1 3.1 %copy-start.2 = (bf16[256,512]{1,0:T(8,128)(2,1)}, bf16[256,512]{1,0:T(8,128)(2,1)S(1)}, u32[]{:S(2)}) copy-start(bf16[256,512]{1,0:T(8,128)(2,1)S(1)} %constant_dynamic-slice_fusion.after.w0) | copy-start | bytes 786436
  1.1 22.5 %copy-start.5 = (bf16[128,1024]{1,0:T(8,128)(2,1)S(1)}, bf16[128,1024]{1,0:T(8,128)(2,1)}, u32[]{:S(2)}) copy-start(bf16[128,1024]{1,0:T(8,128)(2,1)} %refs_0_.1) | copy-start | bytes 786436
  1.1 14.2 %collective-permute-start.2 = (bf16[256,512]{1,0:T(8,128)(2,1)S(1)}, bf16[256,512]{1,0:T(8,128)(2,1)S(1)}, u32[]{:S(2)}, u32[]{:S(2)}) collective-permute-start(bf16[256,512]{1,0:T(8,128)(2,1)S(1)} %constant_dynamic-slice_fusion.after.w0), channel_id=1, source_target_pairs={{0,4},{1,5},{2,6},{3,7},{4,8},{5,9},{6,10},{7,11},{8,12},{9,13},{1... | collective-permute-start | bytes 786440 | tf_op jit(solution)/shard_map/ppermute | solution.py:357
  6.8 8.5 %collective-permute-start.1 = (bf16[256,256]{1,0:T(8,128)(2,1)}, bf16[256,256]{1,0:T(8,128)(2,1)S(1)}, u32[]{:S(2)}, u32[]{:S(2)}) collective-permute-start(bf16[256,256]{1,0:T(8,128)(2,1)} %get-tuple-element.42.refs_0_), channel_id=1, source_target_pairs={{0,4},{1,5},{2,6},{3,7},{4,8},{5,9},{6,10},{7,11},{8,12},{9,13},{1... | collective-permute-start | bytes 393224 | tf_op jit(solution)/shard_map/ppermute | solution.py:357
  8.4 9.5 %collective-permute-start = (bf16[128,1024]{1,0:T(8,128)(2,1)}, bf16[128,1024]{1,0:T(8,128)(2,1)S(1)}, u32[]{:S(2)}, u32[]{:S(2)}) collective-permute-start(bf16[128,1024]{1,0:T(8,128)(2,1)} %get-tuple-element.41), channel_id=1, source_target_pairs={{0,2},{1,3},{2,0},{3,1},{4,6},{5,7},{6,4},{7,5},{8,10},{9,11},{10,... | collective-permute-start | bytes 786440 | tf_op jit(solution)/shard_map/ppermute | solution.py:357
  9.9 13.7 %collective-permute-start.4 = (bf16[128,1024]{1,0:T(8,128)(2,1)}, bf16[128,1024]{1,0:T(8,128)(2,1)S(1)}, u32[]{:S(2)}, u32[]{:S(2)}) collective-permute-start(bf16[128,1024]{1,0:T(8,128)(2,1)} %get-tuple-element.45), channel_id=1, source_target_pairs={{0,16},{1,17},{2,18},{3,19},{4,20},{5,21},{6,22},{7,23},{8,24},{9,... | collective-permute-start | bytes 786440 | tf_op jit(solution)/shard_map/ppermute | solution.py:357
  11.4 12.3 %copy-start.11 = (bf16[2,2,128,256]{3,2,1,0:T(8,128)(2,1)S(1)}, bf16[2,2,128,256]{3,2,1,0:T(8,128)(2,1)}, u32[]{:S(2)}) copy-start(bf16[2,2,128,256]{3,2,1,0:T(8,128)(2,1)} %get-tuple-element.47) | copy-start | bytes 786436
  11.4 16.0 %copy-start.12 = (bf16[256,256]{1,0:T(8,128)(2,1)S(1)}, bf16[256,256]{1,0:T(8,128)(2,1)}, u32[]{:S(2)}) copy-start(bf16[256,256]{1,0:T(8,128)(2,1)} %get-tuple-element.49) | copy-start | bytes 393220
  11.4 27.2 %copy-start.3 = (bf16[256,512]{1,0:T(8,128)(2,1)S(1)}, bf16[256,512]{1,0:T(8,128)(2,1)}, u32[]{:S(2)}) copy-start(bf16[256,512]{1,0:T(8,128)(2,1)} %copy-done.2) | copy-start | bytes 786436
  11.4 12.1 %collective-permute-start.5 = (bf16[128,1024]{1,0:T(8,128)(2,1)}, bf16[128,1024]{1,0:T(8,128)(2,1)S(1)}, u32[]{:S(2)}, u32[]{:S(2)}) collective-permute-start(bf16[128,1024]{1,0:T(8,128)(2,1)} %get-tuple-element.46), channel_id=1, source_target_pairs={{0,18},{1,19},{2,16},{3,17},{4,22},{5,23},{6,20},{7,21},{8,26},{9,... | collective-permute-start | bytes 786440 | tf_op jit(solution)/shard_map/ppermute | solution.py:357
  15.3 8.2 %collective-permute-start.3 = (bf16[256,256]{1,0:T(8,128)(2,1)S(1)}, bf16[256,256]{1,0:T(8,128)(2,1)S(1)}, u32[]{:S(2)}, u32[]{:S(2)}) collective-permute-start(bf16[256,256]{1,0:T(8,128)(2,1)S(1)} %collective-permute-done.1.refs_2_), channel_id=1, source_target_pairs={{0,4},{1,5},{2,6},{3,7},{4,8},{5,9},{6,10},{7,11},{8,12},{9,13},{1... | collective-permute-start | bytes 393224 | tf_op jit(solution)/shard_map/ppermute | solution.py:357
  15.3 12.1 %collective-permute-start.8 = (bf16[256,512]{1,0:T(8,128)(2,1)S(1)}, bf16[256,512]{1,0:T(8,128)(2,1)S(1)}, u32[]{:S(2)}, u32[]{:S(2)}) collective-permute-start(bf16[256,512]{1,0:T(8,128)(2,1)S(1)} %collective-permute-done.2.w1), channel_id=1, source_target_pairs={{0,4},{1,5},{2,6},{3,7},{4,8},{5,9},{6,10},{7,11},{8,12},{9,13},{1... | collective-permute-start | bytes 786440 | tf_op jit(solution)/shard_map/ppermute | solution.py:357
  23.6 15.0 %collective-permute-start.10 = (bf16[512,512]{1,0:T(8,128)(2,1)S(1)}, bf16[512,512]{1,0:T(8,128)(2,1)S(1)}, u32[]{:S(2)}, u32[]{:S(2)}) collective-permute-start(bf16[512,512]{1,0:T(8,128)(2,1)S(1)} %shard_map.92.mine), channel_id=1, source_target_pairs={{0,1},{1,0},{2,3},{3,2},{4,5},{5,4},{6,7},{7,6},{8,9},{9,8},{10,11... | collective-permute-start | bytes 1572872 | tf_op jit(solution)/shard_map/ppermute | solution.py:357
  23.7 9.2 %collective-permute-start.7 = (bf16[2,2,128,256]{3,2,1,0:T(8,128)(2,1)S(1)}, bf16[2,2,128,256]{3,2,1,0:T(8,128)(2,1)S(1)}, u32[]{:S(2)}, u32[]{:S(2)}) collective-permute-start(bf16[2,2,128,256]{3,2,1,0:T(8,128)(2,1)S(1)} %copy-done.11), channel_id=1, source_target_pairs={{0,2},{1,3},{2,0},{3,1},{4,6},{5,7},{6,4},{7,5},{8,10},{9,11},{10,... | collective-permute-start | bytes 786440 | tf_op jit(solution)/shard_map/ppermute | solution.py:357
  27.4 11.2 %collective-permute-start.11 = (bf16[256,512]{1,0:T(8,128)(2,1)S(1)}, bf16[256,512]{1,0:T(8,128)(2,1)S(1)}, u32[]{:S(2)}, u32[]{:S(2)}) collective-permute-start(bf16[256,512]{1,0:T(8,128)(2,1)S(1)} %collective-permute-done.8.w2), channel_id=1, source_target_pairs={{0,4},{1,5},{2,6},{3,7},{4,8},{5,9},{6,10},{7,11},{8,12},{9,13},{1... | collective-permute-start | bytes 786440 | tf_op jit(solution)/shard_map/ppermute | solution.py:357
  27.4 11.2 %collective-permute-start.6 = (bf16[256,256]{1,0:T(8,128)(2,1)S(1)}, bf16[256,256]{1,0:T(8,128)(2,1)S(1)}, u32[]{:S(2)}, u32[]{:S(2)}) collective-permute-start(bf16[256,256]{1,0:T(8,128)(2,1)S(1)} %collective-permute-done.3.refs_4_), channel_id=1, source_target_pairs={{0,4},{1,5},{2,6},{3,7},{4,8},{5,9},{6,10},{7,11},{8,12},{9,13},{1... | collective-permute-start | bytes 393224 | tf_op jit(solution)/shard_map/ppermute | solution.py:357
  27.4 13.6 %copy-start.1 = (bf16[2,2,128,1024]{3,2,1,0:T(8,128)(2,1)S(1)}, bf16[2,2,128,1024]{3,2,1,0:T(8,128)(2,1)}, u32[]{:S(2)}) copy-start(bf16[2,2,128,1024]{3,2,1,0:T(8,128)(2,1)} %filt.3) | copy-start | bytes 3145732
  27.4 11.2 %collective-permute-start.9 = (bf16[256,256]{1,0:T(8,128)(2,1)S(1)}, bf16[256,256]{1,0:T(8,128)(2,1)S(1)}, u32[]{:S(2)}, u32[]{:S(2)}) collective-permute-start(bf16[256,256]{1,0:T(8,128)(2,1)S(1)} %copy-done.12), channel_id=1, source_target_pairs={{0,2},{1,3},{2,0},{3,1},{4,6},{5,7},{6,4},{7,5},{8,10},{9,11},{10,... | collective-permute-start | bytes 393224 | tf_op jit(solution)/shard_map/ppermute | solution.py:357
  39.9 16.6 %copy-start.4 = (bf16[128,1024]{1,0:T(8,128)(2,1)S(1)}, bf16[128,1024]{1,0:T(8,128)(2,1)}, u32[]{:S(2)}) copy-start(bf16[128,1024]{1,0:T(8,128)(2,1)} %g0.2) | copy-start | bytes 786436
  39.9 16.5 %collective-permute-start.14 = (bf16[512,256]{1,0:T(8,128)(2,1)S(1)}, bf16[512,256]{1,0:T(8,128)(2,1)S(1)}, u32[]{:S(2)}, u32[]{:S(2)}) collective-permute-start(bf16[512,256]{1,0:T(8,128)(2,1)S(1)} %get-tuple-element.55), channel_id=1, source_target_pairs={{0,2},{1,3},{2,0},{3,1},{4,6},{5,7},{6,4},{7,5},{8,10},{9,11},{10,... | collective-permute-start | bytes 786440 | tf_op jit(solution)/shard_map/ppermute | solution.py:357
  41.0 7.1 %collective-permute-start.23 = (bf16[256,256]{1,0:T(8,128)(2,1)S(1)}, bf16[256,256]{1,0:T(8,128)(2,1)S(1)}, u32[]{:S(2)}, u32[]{:S(2)}) collective-permute-start(bf16[256,256]{1,0:T(8,128)(2,1)S(1)} %collective-permute-done.9.refs_1_), channel_id=1, source_target_pairs={{0,4},{1,5},{2,6},{3,7},{4,8},{5,9},{6,10},{7,11},{8,12},{9,13},{1... | collective-permute-start | bytes 393224 | tf_op jit(solution)/shard_map/ppermute | solution.py:357
  41.0 25.7 %copy-start.10 = (bf16[16,256,128]{2,1,0:T(8,128)(2,1)S(1)}, bf16[16,256,128]{2,1,0:T(8,128)(2,1)}, u32[]{:S(2)}) copy-start(bf16[16,256,128]{2,1,0:T(8,128)(2,1)} %constant.17.clone.refs_9_) | copy-start | bytes 3145732
  41.3 15.2 %copy-start.8 = (f32[1024]{0:T(1024)S(1)}, f32[1024]{0:T(1024)}, u32[]{:S(2)}) copy-start(f32[1024]{0:T(1024)} %param.13) | copy-start | bytes 12292
  41.3 25.4 %copy-start.9 = (bf16[16,256,128]{2,1,0:T(8,128)(2,1)S(1)}, bf16[16,256,128]{2,1,0:T(8,128)(2,1)}, u32[]{:S(2)}) copy-start(bf16[16,256,128]{2,1,0:T(8,128)(2,1)} %constant.16.clone.refs_8_) | copy-start | bytes 3145732
  41.3 10.6 %collective-permute-start.12 = (bf16[2,2,128,128]{3,2,1,0:T(8,128)(2,1)S(1)}, bf16[2,2,128,128]{3,2,1,0:T(8,128)(2,1)S(1)}, u32[]{:S(2)}, u32[]{:S(2)}) collective-permute-start(bf16[2,2,128,128]{3,2,1,0:T(8,128)(2,1)S(1)} %get-tuple-element.52), channel_id=1, source_target_pairs={{0,4},{1,5},{2,6},{3,7},{4,8},{5,9},{6,10},{7,11},{8,12},{9,13},{1... | collective-permute-start | bytes 393224 | tf_op jit(solution)/shard_map/ppermute | solution.py:357
  41.4 15.1 %collective-permute-start.13 = (bf16[2,2,128,128]{3,2,1,0:T(8,128)(2,1)S(1)}, bf16[2,2,128,128]{3,2,1,0:T(8,128)(2,1)S(1)}, u32[]{:S(2)}, u32[]{:S(2)}) collective-permute-start(bf16[2,2,128,128]{3,2,1,0:T(8,128)(2,1)S(1)} %get-tuple-element.53), channel_id=1, source_target_pairs={{0,8},{1,9},{2,10},{3,11},{4,12},{5,13},{6,14},{7,15},{8,0},{9,1},... | collective-permute-start | bytes 393224 | tf_op jit(solution)/shard_map/ppermute | solution.py:357
  48.1 12.6 %collective-permute-start.24 = (bf16[256,256]{1,0:T(8,128)(2,1)S(1)}, bf16[256,256]{1,0:T(8,128)(2,1)S(1)}, u32[]{:S(2)}, u32[]{:S(2)}) collective-permute-start(bf16[256,256]{1,0:T(8,128)(2,1)S(1)} %collective-permute-done.23.refs_3_), channel_id=1, source_target_pairs={{0,4},{1,5},{2,6},{3,7},{4,8},{5,9},{6,10},{7,11},{8,12},{9,13},{1... | collective-permute-start | bytes 393224 | tf_op jit(solution)/shard_map/ppermute | solution.py:357
  48.1 18.6 %collective-permute-start.18 = (bf16[2,2,128,128]{3,2,1,0:T(8,128)(2,1)S(1)}, bf16[2,2,128,128]{3,2,1,0:T(8,128)(2,1)S(1)}, u32[]{:S(2)}, u32[]{:S(2)}) collective-permute-start(bf16[2,2,128,128]{3,2,1,0:T(8,128)(2,1)S(1)} %get-tuple-element.61), channel_id=1, source_target_pairs={{0,12},{1,13},{2,14},{3,15},{4,0},{5,1},{6,2},{7,3},{8,4},{9,5},{1... | collective-permute-start | bytes 393224 | tf_op jit(solution)/shard_map/ppermute | solution.py:357
  56.8 6.8 %collective-permute-start.15 = (bf16[256,128]{1,0:T(8,128)(2,1)S(1)}, bf16[256,128]{1,0:T(8,128)(2,1)S(1)}, u32[]{:S(2)}, u32[]{:S(2)}) collective-permute-start(bf16[256,128]{1,0:T(8,128)(2,1)S(1)} %get-tuple-element.57), channel_id=1, source_target_pairs={{0,4},{1,5},{2,6},{3,7},{4,8},{5,9},{6,10},{7,11},{8,12},{9,13},{1... | collective-permute-start | bytes 196616 | tf_op jit(solution)/shard_map/ppermute | solution.py:357
  56.9 8.4 %collective-permute-start.16 = (bf16[256,128]{1,0:T(8,128)(2,1)S(1)}, bf16[256,128]{1,0:T(8,128)(2,1)S(1)}, u32[]{:S(2)}, u32[]{:S(2)}) collective-permute-start(bf16[256,128]{1,0:T(8,128)(2,1)S(1)} %get-tuple-element.58), channel_id=1, source_target_pairs={{0,8},{1,9},{2,10},{3,11},{4,12},{5,13},{6,14},{7,15},{8,0},{9,1},... | collective-permute-start | bytes 196616 | tf_op jit(solution)/shard_map/ppermute | solution.py:357
  57.0 8.3 %collective-permute-start.17 = (bf16[256,128]{1,0:T(8,128)(2,1)S(1)}, bf16[256,128]{1,0:T(8,128)(2,1)S(1)}, u32[]{:S(2)}, u32[]{:S(2)}) collective-permute-start(bf16[256,128]{1,0:T(8,128)(2,1)S(1)} %get-tuple-element.59), channel_id=1, source_target_pairs={{0,12},{1,13},{2,14},{3,15},{4,0},{5,1},{6,2},{7,3},{8,4},{9,5},{1... | collective-permute-start | bytes 196616 | tf_op jit(solution)/shard_map/ppermute | solution.py:357
  65.3 11.2 %collective-permute-start.25 = (bf16[256,256]{1,0:T(8,128)(2,1)S(1)}, bf16[256,256]{1,0:T(8,128)(2,1)S(1)}, u32[]{:S(2)}, u32[]{:S(2)}) collective-permute-start(bf16[256,256]{1,0:T(8,128)(2,1)S(1)} %collective-permute-done.24.refs_5_), channel_id=1, source_target_pairs={{0,4},{1,5},{2,6},{3,7},{4,8},{5,9},{6,10},{7,11},{8,12},{9,13},{1... | collective-permute-start | bytes 393224 | tf_op jit(solution)/shard_map/ppermute | solution.py:357
  66.7 9.8 %copy-start.7 = (bf16[256,256]{1,0:T(8,128)(2,1)S(1)}, bf16[256,256]{1,0:T(8,128)(2,1)}, u32[]{:S(2)}) copy-start(bf16[256,256]{1,0:T(8,128)(2,1)} %get-tuple-element.42.refs_0_) | copy-start | bytes 393220
  68.5 6.5 %collective-permute-start.19 = (bf16[256,128]{1,0:T(8,128)(2,1)S(1)}, bf16[256,128]{1,0:T(8,128)(2,1)S(1)}, u32[]{:S(2)}, u32[]{:S(2)}) collective-permute-start(bf16[256,128]{1,0:T(8,128)(2,1)S(1)} %get-tuple-element.63), channel_id=1, source_target_pairs={{0,4},{1,5},{2,6},{3,7},{4,8},{5,9},{6,10},{7,11},{8,12},{9,13},{1... | collective-permute-start | bytes 196616 | tf_op jit(solution)/shard_map/ppermute | solution.py:357
  68.6 7.8 %collective-permute-start.20 = (bf16[256,128]{1,0:T(8,128)(2,1)S(1)}, bf16[256,128]{1,0:T(8,128)(2,1)S(1)}, u32[]{:S(2)}, u32[]{:S(2)}) collective-permute-start(bf16[256,128]{1,0:T(8,128)(2,1)S(1)} %get-tuple-element.64), channel_id=1, source_target_pairs={{0,8},{1,9},{2,10},{3,11},{4,12},{5,13},{6,14},{7,15},{8,0},{9,1},... | collective-permute-start | bytes 196616 | tf_op jit(solution)/shard_map/ppermute | solution.py:357
  71.6 5.1 %copy-start.6 = (bf16[128,1024]{1,0:T(8,128)(2,1)S(1)}, bf16[128,1024]{1,0:T(8,128)(2,1)}, u32[]{:S(2)}) copy-start(bf16[128,1024]{1,0:T(8,128)(2,1)} %g0.3) | copy-start | bytes 786436
  71.6 4.9 %collective-permute-start.21 = (bf16[256,128]{1,0:T(8,128)(2,1)S(1)}, bf16[256,128]{1,0:T(8,128)(2,1)S(1)}, u32[]{:S(2)}, u32[]{:S(2)}) collective-permute-start(bf16[256,128]{1,0:T(8,128)(2,1)S(1)} %get-tuple-element.65), channel_id=1, source_target_pairs={{0,12},{1,13},{2,14},{3,15},{4,0},{5,1},{6,2},{7,3},{8,4},{9,5},{1... | collective-permute-start | bytes 196616 | tf_op jit(solution)/shard_map/ppermute | solution.py:357
  76.6 2.4 %collective-permute-start.26 = (bf16[4,256,256]{2,1,0:T(8,128)(2,1)S(1)}, bf16[4,256,256]{2,1,0:T(8,128)(2,1)S(1)}, u32[]{:S(2)}, u32[]{:S(2)}) collective-permute-start(bf16[4,256,256]{2,1,0:T(8,128)(2,1)S(1)} %get-tuple-element.72), channel_id=1, source_target_pairs={{0,1},{1,0},{2,3},{3,2},{4,5},{5,4},{6,7},{7,6},{8,9},{9,8},{10,11... | collective-permute-start | bytes 1572872 | tf_op jit(solution)/shard_map/ppermute | solution.py:357
  76.9 2.0 %collective-permute-start.22 = (bf16[512,256]{1,0:T(8,128)(2,1)S(1)}, bf16[512,256]{1,0:T(8,128)(2,1)S(1)}, u32[]{:S(2)}, u32[]{:S(2)}) collective-permute-start(bf16[512,256]{1,0:T(8,128)(2,1)S(1)} %shard_map.97.gated), channel_id=1, source_target_pairs={{0,1},{1,0},{2,3},{3,2},{4,5},{5,4},{6,7},{7,6},{8,9},{9,8},{10,11... | collective-permute-start | bytes 786440 | tf_op jit(solution)/shard_map/ppermute | solution.py:357
  80.4 10.2 %collective-permute-start.27 = (bf16[128,1024]{1,0:T(8,128)(2,1)S(1)}, bf16[128,1024]{1,0:T(8,128)(2,1)S(1)}, u32[]{:S(2)}, u32[]{:S(2)}) collective-permute-start(bf16[128,1024]{1,0:T(8,128)(2,1)S(1)} %get-tuple-element.74), channel_id=1, source_target_pairs={{0,18},{1,19},{2,16},{3,17},{4,22},{5,23},{6,20},{7,21},{8,26},{9,... | collective-permute-start | bytes 786440 | tf_op jit(solution)/shard_map/ppermute | solution.py:357
  82.3 13.1 %collective-permute-start.28 = (bf16[128,1024]{1,0:T(8,128)(2,1)S(1)}, bf16[128,1024]{1,0:T(8,128)(2,1)S(1)}, u32[]{:S(2)}, u32[]{:S(2)}) collective-permute-start(bf16[128,1024]{1,0:T(8,128)(2,1)S(1)} %get-tuple-element.75), channel_id=1, source_target_pairs={{0,16},{1,17},{2,18},{3,19},{4,20},{5,21},{6,22},{7,23},{8,24},{9,... | collective-permute-start | bytes 786440 | tf_op jit(solution)/shard_map/ppermute | solution.py:357
  83.3 12.2 %collective-permute-start.29 = (bf16[128,1024]{1,0:T(8,128)(2,1)S(1)}, bf16[128,1024]{1,0:T(8,128)(2,1)S(1)}, u32[]{:S(2)}, u32[]{:S(2)}) collective-permute-start(bf16[128,1024]{1,0:T(8,128)(2,1)S(1)} %get-tuple-element.76), channel_id=1, source_target_pairs={{0,2},{1,3},{2,0},{3,1},{4,6},{5,7},{6,4},{7,5},{8,10},{9,11},{10,... | collective-permute-start | bytes 786440 | tf_op jit(solution)/shard_map/ppermute | solution.py:357

commit v10 on v9

--- a/solution.py
+++ b/solution.py
@@ -324,16 +324,12 @@
                 give[to] = pieces[2 * r + k][...]
 
 
-def out_kernel(gated, other, keep, theirs, own, *sends):
-    for p in (3, 2, 1, 0):
+def out_kernel(blocks, gated, other, keep, theirs, *outs):
+    for p, out in zip(blocks, outs):
         rows = pl.ds(p * 128, 128)
         for i in range(4):
             total = dot_t(gated[rows, :], keep[i]) + dot_t(other[rows, :], theirs[i])
-            lanes = pl.ds(i * 256, 256)
-            if p == 0:
-                own[:, lanes] = total
-            else:
-                sends[p - 1][:, lanes] = total.astype(BF16)
+            out[:, pl.ds(i * 256, 256)] = total.astype(out.dtype)
 
 
 def tables():
@@ -393,7 +389,6 @@
     q2 = to_z(after(q1, v1), 1)
     mine = in_vmem(join_tokens, shape((512, 512), BF16), moved=1 << 20)(tokens, after(received[0], q2), *received[1:])
     v3 = to_z(v2, 1)
-    q3 = to_z(q2, 1)
     other = to_core(mine)
     got_o = to_x(after(away_o, v2))
     r1 = to_z(after(got_o, v3), 1)
@@ -403,7 +398,7 @@
         [pltpu.VMEM((512, 512), F32)],
         flops=1 << 29,
         moved=2 << 20,
-    )(after(mine, q3, near, got_o), other, own_v, v1, v2, v3)
+    )(after(mine, filters[1], got_o), other, own_v, v1, v2, v3)
     r2 = to_z(after(r1, keep), 1)
     drive, *sends = in_vmem(
         drive_kernel,
@@ -412,6 +407,7 @@
         moved=2 << 20,
     )(after(keep, filters[1], filters[2]), to_x(give), gate_k, *received, skip[None, :])
     columns = [sends[0]] + [to_z(sends[r], r) for r in (1, 2, 3)]
+    q3 = to_z(after(q2, columns[1]), 1)
     r3 = to_z(after(r2, *columns[1:]), 1)
     table, table_t = tables()
     sends = in_vmem(
@@ -436,15 +432,21 @@
         gate_kernel, shape((512, 256), BF16), [pltpu.VMEM((4, 256, 128), BF16)], moved=1 << 20
     )(*rows, drive, gate_q, *received)
     gated_other = to_core(gated)
-    own, *sends = in_vmem(
-        out_kernel,
-        [shape((128, 1024), F32)] + [shape((128, 1024), BF16)] * 3,
-        flops=1 << 30,
-        moved=4 << 20,
-    )(gated, gated_other, keep, theirs)
-    total = own
-    for p in (3, 2, 1):
-        total = total + to_peer(sends[p - 1], p).astype(F32)
+    summed = (gated, gated_other, keep, theirs)
+    send = shape((128, 1024), BF16)
+    far = in_vmem(functools.partial(out_kernel, (3, 1)), [send] * 2, flops=1 << 29, moved=2 << 20)
+    close = in_vmem(
+        functools.partial(out_kernel, (2, 0)),
+        [send, shape((128, 1024), F32)],
+        flops=1 << 29,
+        moved=2 << 20,
+    )
+    to_xy, to_row = far(*summed)
+    parts = [to_peer(to_xy, 3), to_peer(to_row, 1)]
+    to_column, total = close(*summed)
+    parts.append(to_peer(to_column, 2))
+    for part in parts:
+        total = total + part.astype(F32)
     return total.astype(BF16)
 
 

time: 96.5 us -> 99.3 us (1.029)
  starting transfers between devices: 35.1 us -> 39.2 us
  waiting for transfers between devices: 50.8 us -> 49.4 us
    ppermute x30, starting transfers between devices: 35.1 us -> 39.2 us  [permute(): return lax.ppermute(values, AXES, pairs)]
    ppermute x30, waiting for transfers between devices: 50.8 us -> 49.4 us  [permute(): return lax.ppermute(values, AXES, pairs)]
    pallas_call x8 -> x9, Pallas kernels: 5.64 us -> 5.78 us  [call(): pl.pallas_call(kernel, out_shape=out_shape, in_specs=specs, out_specs=jax...]
  transfers between devices with their start and end apart: 30 -> 30, of which waited for: 17 -> 16; matrix products, arithmetic and copies ran while one was open for 0% -> 0% of each run, Pallas kernels for 6% -> 6%
where the time goes in v10:
time: 99.3 us; the launch traced here: 99.2 us
  waiting for transfers between devices  49.4 us (50%)
  starting transfers between devices  39.2 us (39%)
  Pallas kernels  8.36 us (8%)
  local copies, waits for them, and re-layouts  1.12 us (1%)
    ppermute x30, waiting for transfers between devices, permute(): return lax.ppermute(values, AXES, pairs)  49.4 us
    ppermute x30, starting transfers between devices, permute(): return lax.ppermute(values, AXES, pairs)  39.2 us
    pallas_call x9, Pallas kernels, call(): pl.pallas_call(kernel, out_shape=out_shape, in_specs=specs, out_specs=jax...  5.78 us
    pallas_call x1, Pallas kernels, call(): pl.pallas_call(kernel, out_shape=out_shape, in_specs=[pl.BlockSpec(memory...  2.58 us
  transfers between devices with their start and end apart: 30, of which 16 were waited for; matrix products, arithmetic and copies ran while one was open for 0% of the time, Pallas kernels for 6%

profile of v10, /device:TPU:0, one launch (start us, length us, event | category | flops | bytes accessed | tf_op | source)
XLA Modules:
  0.0 99.2 jit_solution(16064071061115005273)
XLA Ops:
  0.0 1.0 %copy-done = bf16[256,1024]{1,0:T(8,128)(2,1)S(1)} copy-done((bf16[256,1024]{1,0:T(8,128)(2,1)S(1)}, bf16[256,1024]{1,0:T(8,128)(2,1)}, u32[]{:S(2)}) %copy-start) | copy-done | bytes 524312
  1.1 0.0 copy-start.2
  1.1 0.0 copy-start.5
  1.1 3.1 %collective-permute-start.2 = (bf16[256,512]{1,0:T(8,128)(2,1)S(1)}, bf16[256,512]{1,0:T(8,128)(2,1)S(1)}, u32[]{:S(2)}, u32[]{:S(2)}) collective-permute-start(bf16[256,512]{1,0:T(8,128)(2,1)S(1)} %constant_dynamic-slice_fusion.after.w0), channel_id=1, source_target_pairs={{0,4},{1,5},{2,6},{3,7},{4,8},{5,9},{6,10},{7,11},{8,12},{9,13},{1... | collective-permute-start | bytes 786440 | tf_op jit(solution)/shard_map/ppermute | solution.py:353
  4.2 2.6 %shard_map.91 = (bf16[128,1024]{1,0:T(8,128)(2,1)}, bf16[128,1024]{1,0:T(8,128)(2,1)}, bf16[128,1024]{1,0:T(8,128)(2,1)}, bf16[256,256]{1,0:T(8,128)(2,1)}, bf16...) custom-call(bf16[128,1024]{1,0:T(8,128)(2,1)} %refs_0_.1, bf16[128,1024]{1,0:T(8,128)(2,1)} %g0.2, ...), custom_call_target="tpu_custom_call" | custom-call | tf_op jit(solution)/shard_map/pallas_call | solution.py:101
  6.8 0.0 copy-start.1
  6.8 1.6 %collective-permute-start.1 = (bf16[256,256]{1,0:T(8,128)(2,1)}, bf16[256,256]{1,0:T(8,128)(2,1)S(1)}, u32[]{:S(2)}, u32[]{:S(2)}) collective-permute-start(bf16[256,256]{1,0:T(8,128)(2,1)} %get-tuple-element.43.refs_0_), channel_id=1, source_target_pairs={{0,4},{1,5},{2,6},{3,7},{4,8},{5,9},{6,10},{7,11},{8,12},{9,13},{1... | collective-permute-start | bytes 393224 | tf_op jit(solution)/shard_map/ppermute | solution.py:353
  8.4 1.5 %collective-permute-start = (bf16[128,1024]{1,0:T(8,128)(2,1)}, bf16[128,1024]{1,0:T(8,128)(2,1)S(1)}, u32[]{:S(2)}, u32[]{:S(2)}) collective-permute-start(bf16[128,1024]{1,0:T(8,128)(2,1)} %get-tuple-element.42), channel_id=1, source_target_pairs={{0,2},{1,3},{2,0},{3,1},{4,6},{5,7},{6,4},{7,5},{8,10},{9,11},{10,... | collective-permute-start | bytes 786440 | tf_op jit(solution)/shard_map/ppermute | solution.py:353
  9.9 1.5 %collective-permute-start.4 = (bf16[128,1024]{1,0:T(8,128)(2,1)}, bf16[128,1024]{1,0:T(8,128)(2,1)S(1)}, u32[]{:S(2)}, u32[]{:S(2)}) collective-permute-start(bf16[128,1024]{1,0:T(8,128)(2,1)} %get-tuple-element.46), channel_id=1, source_target_pairs={{0,16},{1,17},{2,18},{3,19},{4,20},{5,21},{6,22},{7,23},{8,24},{9,... | collective-permute-start | bytes 786440 | tf_op jit(solution)/shard_map/ppermute | solution.py:353
  11.4 0.5 collective-permute-start.5
  11.9 3.4 %collective-permute-done.1.refs_2_ = bf16[256,256]{1,0:T(8,128)(2,1)S(1)} collective-permute-done((bf16[256,256]{1,0:T(8,128)(2,1)}, bf16[256,256]{1,0:T(8,128)(2,1)S(1)}, u32[]{:S(2)}, u32[]{:S(2)}) %collective-permute-start.1) | collective-permute-done | bytes 131104 | tf_op jit(solution)/shard_map/ppermute | solution.py:353
  15.3 0.0 collective-permute-start.3
  15.3 1.3 %collective-permute-start.8 = (bf16[256,512]{1,0:T(8,128)(2,1)S(1)}, bf16[256,512]{1,0:T(8,128)(2,1)S(1)}, u32[]{:S(2)}, u32[]{:S(2)}) collective-permute-start(bf16[256,512]{1,0:T(8,128)(2,1)S(1)} %collective-permute-done.2.w1), channel_id=1, source_target_pairs={{0,4},{1,5},{2,6},{3,7},{4,8},{5,9},{6,10},{7,11},{8,12},{9,13},{1... | collective-permute-start | bytes 786440 | tf_op jit(solution)/shard_map/ppermute | solution.py:353
  16.6 1.2 %collective-permute-done.refs_1_.g1 = bf16[128,1024]{1,0:T(8,128)(2,1)S(1)} collective-permute-done((bf16[128,1024]{1,0:T(8,128)(2,1)}, bf16[128,1024]{1,0:T(8,128)(2,1)S(1)}, u32[]{:S(2)}, u32[]{:S(2)}) %collective-permute-start) | collective-permute-done | bytes 262176 | tf_op jit(solution)/shard_map/ppermute | solution.py:353
  17.9 5.7 %collective-permute-done.3.refs_4_ = bf16[256,256]{1,0:T(8,128)(2,1)S(1)} collective-permute-done((bf16[256,256]{1,0:T(8,128)(2,1)S(1)}, bf16[256,256]{1,0:T(8,128)(2,1)S(1)}, u32[]{:S(2)}, u32[]{:S(2)}) %collective-permute-start.3) | collective-permute-done | bytes 131104 | tf_op jit(solution)/shard_map/ppermute | solution.py:353
  23.5 0.0 collective-permute-done.4.refs_2_.g2
  23.5 0.0 collective-permute-done.5.refs_3_.g3
  23.6 0.1 collective-permute-start.10
  23.7 0.0 copy-start.3
  23.7 1.6 %collective-permute-start.6 = (bf16[2,2,128,256]{3,2,1,0:T(8,128)(2,1)S(1)}, bf16[2,2,128,256]{3,2,1,0:T(8,128)(2,1)S(1)}, u32[]{:S(2)}, u32[]{:S(2)}) collective-permute-start(bf16[2,2,128,256]{3,2,1,0:T(8,128)(2,1)S(1)} %copy-done.11), channel_id=1, source_target_pairs={{0,2},{1,3},{2,0},{3,1},{4,6},{5,7},{6,4},{7,5},{8,10},{9,11},{10,... | collective-permute-start | bytes 786440 | tf_op jit(solution)/shard_map/ppermute | solution.py:353
  25.3 2.1 %collective-permute-done.8.w2 = bf16[256,512]{1,0:T(8,128)(2,1)S(1)} collective-permute-done((bf16[256,512]{1,0:T(8,128)(2,1)S(1)}, bf16[256,512]{1,0:T(8,128)(2,1)S(1)}, u32[]{:S(2)}, u32[]{:S(2)}) %collective-permute-start.8) | collective-permute-done | bytes 262176 | tf_op jit(solution)/shard_map/ppermute | solution.py:353
  27.4 0.0 collective-permute-start.11
  27.4 5.0 %collective-permute-done.6.near = bf16[2,2,128,256]{3,2,1,0:T(8,128)(2,1)S(1)} collective-permute-done((bf16[2,2,128,256]{3,2,1,0:T(8,128)(2,1)S(1)}, bf16[2,2,128,256]{3,2,1,0:T(8,128)(2,1)S(1)}, u32[]{:S(2)}, u32[]{:S(2)}) %collective-permute-start.6) | collective-permute-done | bytes 262176 | tf_op jit(solution)/shard_map/ppermute | solution.py:353
  32.4 0.3 shard_map.93
  32.7 1.0 %collective-permute-start.7 = (bf16[2,2,128,128]{3,2,1,0:T(8,128)(2,1)S(1)}, bf16[2,2,128,128]{3,2,1,0:T(8,128)(2,1)S(1)}, u32[]{:S(2)}, u32[]{:S(2)}) collective-permute-start(bf16[2,2,128,128]{3,2,1,0:T(8,128)(2,1)S(1)} %get-tuple-element.49), channel_id=1, source_target_pairs={{0,4},{1,5},{2,6},{3,7},{4,8},{5,9},{6,10},{7,11},{8,12},{9,13},{1... | collective-permute-start | bytes 393224 | tf_op jit(solution)/shard_map/ppermute | solution.py:353
  33.7 1.2 %collective-permute-start.9 = (bf16[256,256]{1,0:T(8,128)(2,1)S(1)}, bf16[256,256]{1,0:T(8,128)(2,1)S(1)}, u32[]{:S(2)}, u32[]{:S(2)}) collective-permute-start(bf16[256,256]{1,0:T(8,128)(2,1)S(1)} %copy-done.12), channel_id=1, source_target_pairs={{0,2},{1,3},{2,0},{3,1},{4,6},{5,7},{6,4},{7,5},{8,10},{9,11},{10,... | collective-permute-start | bytes 393224 | tf_op jit(solution)/shard_map/ppermute | solution.py:353
  35.0 4.7 %collective-permute-done.7.refs_5_ = bf16[2,2,128,128]{3,2,1,0:T(8,128)(2,1)S(1)} collective-permute-done((bf16[2,2,128,128]{3,2,1,0:T(8,128)(2,1)S(1)}, bf16[2,2,128,128]{3,2,1,0:T(8,128)(2,1)S(1)}, u32[]{:S(2)}, u32[]{:S(2)}) %collective-permute-start.7) | collective-permute-done | bytes 131104 | tf_op jit(solution)/shard_map/ppermute | solution.py:353
  39.6 0.0 collective-permute-done.9.refs_1_
  39.7 0.0 copy-start.10
  39.7 1.3 %shard_map.94 = (f32[512,256]{1,0:T(8,128)S(1)}, bf16[512,256]{1,0:T(8,128)(2,1)S(1)}) custom-call(bf16[512,512]{1,0:T(8,128)(2,1)S(1)} %shard_map.92.mine, bf16[512,512]{1,0:T(8,128)(2,1)S(1)} %collective-permute-done.10.other, bf16[256,512]{1,0:T(8,128)(2,1)S(1)} %copy-done.3, bf16[256,512]{1,0:T(8,128)(2,1)S(1)} %collective-permute-done.2.w1, ...), custom_call_target="tpu_custom_call" | custom-call | flops 536870912 | bytes 2097152 | tf_op jit(solution)/shard_map/pallas_call | solution.py:37
  41.0 0.0 copy-start.8
  41.0 0.0 copy-start.9
  41.0 1.6 %collective-permute-start.13 = (bf16[512,256]{1,0:T(8,128)(2,1)S(1)}, bf16[512,256]{1,0:T(8,128)(2,1)S(1)}, u32[]{:S(2)}, u32[]{:S(2)}) collective-permute-start(bf16[512,256]{1,0:T(8,128)(2,1)S(1)} %get-tuple-element.56), channel_id=1, source_target_pairs={{0,2},{1,3},{2,0},{3,1},{4,6},{5,7},{6,4},{7,5},{8,10},{9,11},{10,... | collective-permute-start | bytes 786440 | tf_op jit(solution)/shard_map/ppermute | solution.py:353
  42.5 2.5 %collective-permute-start.12 = (bf16[2,2,128,128]{3,2,1,0:T(8,128)(2,1)S(1)}, bf16[2,2,128,128]{3,2,1,0:T(8,128)(2,1)S(1)}, u32[]{:S(2)}, u32[]{:S(2)}) collective-permute-start(bf16[2,2,128,128]{3,2,1,0:T(8,128)(2,1)S(1)} %get-tuple-element.54), channel_id=1, source_target_pairs={{0,8},{1,9},{2,10},{3,11},{4,12},{5,13},{6,14},{7,15},{8,0},{9,1},... | collective-permute-start | bytes 393224 | tf_op jit(solution)/shard_map/ppermute | solution.py:353
  45.1 4.7 %collective-permute-done.22.refs_3_ = bf16[256,256]{1,0:T(8,128)(2,1)S(1)} collective-permute-done((bf16[256,256]{1,0:T(8,128)(2,1)S(1)}, bf16[256,256]{1,0:T(8,128)(2,1)S(1)}, u32[]{:S(2)}, u32[]{:S(2)}) %collective-permute-start.22) | collective-permute-done | bytes 131104 | tf_op jit(solution)/shard_map/ppermute | solution.py:353
  49.8 3.8 %collective-permute-start.17 = (bf16[2,2,128,128]{3,2,1,0:T(8,128)(2,1)S(1)}, bf16[2,2,128,128]{3,2,1,0:T(8,128)(2,1)S(1)}, u32[]{:S(2)}, u32[]{:S(2)}) collective-permute-start(bf16[2,2,128,128]{3,2,1,0:T(8,128)(2,1)S(1)} %get-tuple-element.62), channel_id=1, source_target_pairs={{0,12},{1,13},{2,14},{3,15},{4,0},{5,1},{6,2},{7,3},{8,4},{9,5},{1... | collective-permute-start | bytes 393224 | tf_op jit(solution)/shard_map/ppermute | solution.py:353
  53.6 3.2 %collective-permute-done.12.refs_6_ = bf16[2,2,128,128]{3,2,1,0:T(8,128)(2,1)S(1)} collective-permute-done((bf16[2,2,128,128]{3,2,1,0:T(8,128)(2,1)S(1)}, bf16[2,2,128,128]{3,2,1,0:T(8,128)(2,1)S(1)}, u32[]{:S(2)}, u32[]{:S(2)}) %collective-permute-start.12) | collective-permute-done | bytes 131104 | tf_op jit(solution)/shard_map/ppermute | solution.py:353
  56.8 0.3 shard_map.95
  57.2 0.1 collective-permute-start.14
  57.2 0.1 collective-permute-start.15
  57.3 3.7 %collective-permute-start.16 = (bf16[256,128]{1,0:T(8,128)(2,1)S(1)}, bf16[256,128]{1,0:T(8,128)(2,1)S(1)}, u32[]{:S(2)}, u32[]{:S(2)}) collective-permute-start(bf16[256,128]{1,0:T(8,128)(2,1)S(1)} %get-tuple-element.60), channel_id=1, source_target_pairs={{0,12},{1,13},{2,14},{3,15},{4,0},{5,1},{6,2},{7,3},{8,4},{9,5},{1... | collective-permute-start | bytes 196616 | tf_op jit(solution)/shard_map/ppermute | solution.py:353
  61.0 2.2 %collective-permute-done.14.refs_1_ = bf16[256,128]{1,0:T(8,128)(2,1)S(1)} collective-permute-done((bf16[256,128]{1,0:T(8,128)(2,1)S(1)}, bf16[256,128]{1,0:T(8,128)(2,1)S(1)}, u32[]{:S(2)}, u32[]{:S(2)}) %collective-permute-start.14) | collective-permute-done | bytes 65568 | tf_op jit(solution)/shard_map/ppermute | solution.py:353
  63.3 0.7 collective-permute-done.16.refs_3_
  64.0 5.4 %collective-permute-start.25 = (bf16[256,256]{1,0:T(8,128)(2,1)S(1)}, bf16[256,256]{1,0:T(8,128)(2,1)S(1)}, u32[]{:S(2)}, u32[]{:S(2)}) collective-permute-start(bf16[256,256]{1,0:T(8,128)(2,1)S(1)} %collective-permute-done.23.refs_5_), channel_id=1, source_target_pairs={{0,4},{1,5},{2,6},{3,7},{4,8},{5,9},{6,10},{7,11},{8,12},{9,13},{1... | collective-permute-start | bytes 393224 | tf_op jit(solution)/shard_map/ppermute | solution.py:353
  69.4 0.0 collective-permute-start.24
  69.4 1.8 %shard_map.96 = (bf16[256,128]{1,0:T(8,128)(2,1)S(1)}, bf16[256,128]{1,0:T(8,128)(2,1)S(1)}, bf16[256,128]{1,0:T(8,128)(2,1)S(1)}, bf16[256,128]{1,0:T(8,128)(2,1)S(1)}) custom-call(bf16[256,128]{1,0:T(8,128)(2,1)S(1)} %get-tuple-element.57.refs_0_, bf16[256,128]{1,0:T(8,128)(2,1)S(1)} %collective-permute-done.14.refs_1_, ...), custom_call_target="tpu_custom_call" | custom-call | flops 1073741824 | bytes 5242880 | tf_op jit(solution)/shard_map/pallas_call | solution.py:37
  71.2 0.1 collective-permute-start.18
  71.3 4.3 %collective-permute-start.19 = (bf16[256,128]{1,0:T(8,128)(2,1)S(1)}, bf16[256,128]{1,0:T(8,128)(2,1)S(1)}, u32[]{:S(2)}, u32[]{:S(2)}) collective-permute-start(bf16[256,128]{1,0:T(8,128)(2,1)S(1)} %get-tuple-element.65), channel_id=1, source_target_pairs={{0,8},{1,9},{2,10},{3,11},{4,12},{5,13},{6,14},{7,15},{8,0},{9,1},... | collective-permute-start | bytes 196616 | tf_op jit(solution)/shard_map/ppermute | solution.py:353
  75.7 1.7 %collective-permute-done.18.e1 = bf16[256,128]{1,0:T(8,128)(2,1)S(1)} collective-permute-done((bf16[256,128]{1,0:T(8,128)(2,1)S(1)}, bf16[256,128]{1,0:T(8,128)(2,1)S(1)}, u32[]{:S(2)}, u32[]{:S(2)}) %collective-permute-start.18) | collective-permute-done | bytes 65568 | tf_op jit(solution)/shard_map/ppermute | solution.py:353
  77.4 1.4 %collective-permute-done.19.e2 = bf16[256,128]{1,0:T(8,128)(2,1)S(1)} collective-permute-done((bf16[256,128]{1,0:T(8,128)(2,1)S(1)}, bf16[256,128]{1,0:T(8,128)(2,1)S(1)}, u32[]{:S(2)}, u32[]{:S(2)}) %collective-permute-start.19) | collective-permute-done | bytes 65568 | tf_op jit(solution)/shard_map/ppermute | solution.py:353
  78.8 1.2 %collective-permute-done.20.e3 = bf16[256,128]{1,0:T(8,128)(2,1)S(1)} collective-permute-done((bf16[256,128]{1,0:T(8,128)(2,1)S(1)}, bf16[256,128]{1,0:T(8,128)(2,1)S(1)}, u32[]{:S(2)}, u32[]{:S(2)}) %collective-permute-start.20) | collective-permute-done | bytes 65568 | tf_op jit(solution)/shard_map/ppermute | solution.py:353
  79.9 0.2 shard_map.98
  80.1 0.1 collective-permute-start.26
  80.2 0.2 shard_map.97.gated
  80.4 0.5 collective-permute-start.21
  81.0 1.5 %collective-permute-done.21.other = bf16[512,256]{1,0:T(8,128)(2,1)S(1)} collective-permute-done((bf16[512,256]{1,0:T(8,128)(2,1)S(1)}, bf16[512,256]{1,0:T(8,128)(2,1)S(1)}, u32[]{:S(2)}, u32[]{:S(2)}) %collective-permute-start.21) | collective-permute-done | bytes 262176 | tf_op jit(solution)/shard_map/ppermute | solution.py:353
  82.5 0.8 shard_map.100
  83.3 1.5 %collective-permute-start.27 = (bf16[128,1024]{1,0:T(8,128)(2,1)S(1)}, bf16[128,1024]{1,0:T(8,128)(2,1)S(1)}, u32[]{:S(2)}, u32[]{:S(2)}) collective-permute-start(bf16[128,1024]{1,0:T(8,128)(2,1)S(1)} %get-tuple-element.76), channel_id=1, source_target_pairs={{0,18},{1,19},{2,16},{3,17},{4,22},{5,23},{6,20},{7,21},{8,26},{9,... | collective-permute-start | bytes 786440 | tf_op jit(solution)/shard_map/ppermute | solution.py:353
  84.8 1.5 %collective-permute-start.28 = (bf16[128,1024]{1,0:T(8,128)(2,1)S(1)}, bf16[128,1024]{1,0:T(8,128)(2,1)S(1)}, u32[]{:S(2)}, u32[]{:S(2)}) collective-permute-start(bf16[128,1024]{1,0:T(8,128)(2,1)S(1)} %get-tuple-element.77), channel_id=1, source_target_pairs={{0,2},{1,3},{2,0},{3,1},{4,6},{5,7},{6,4},{7,5},{8,10},{9,11},{10,... | collective-permute-start | bytes 786440 | tf_op jit(solution)/shard_map/ppermute | solution.py:353
  86.3 0.8 shard_map.99
  87.1 0.6 collective-permute-start.29
  87.7 5.7 %collective-permute-done.27 = bf16[128,1024]{1,0:T(8,128)(2,1)S(1)} collective-permute-done((bf16[128,1024]{1,0:T(8,128)(2,1)S(1)}, bf16[128,1024]{1,0:T(8,128)(2,1)S(1)}, u32[]{:S(2)}, u32[]{:S(2)}) %collective-permute-start.27) | collective-permute-done | bytes 262176 | tf_op jit(solution)/shard_map/ppermute | solution.py:353
  93.5 4.9 %collective-permute-done.28 = bf16[128,1024]{1,0:T(8,128)(2,1)S(1)} collective-permute-done((bf16[128,1024]{1,0:T(8,128)(2,1)S(1)}, bf16[128,1024]{1,0:T(8,128)(2,1)S(1)}, u32[]{:S(2)}, u32[]{:S(2)}) %collective-permute-start.28) | collective-permute-done | bytes 262176 | tf_op jit(solution)/shard_map/ppermute | solution.py:353
  98.3 0.8 add_convert_fusion
  (34 shorter events, 0.1 us)
Async XLA Ops:
  0.0 1.0 %copy-start = (bf16[256,1024]{1,0:T(8,128)(2,1)S(1)}, bf16[256,1024]{1,0:T(8,128)(2,1)}, u32[]{:S(2)}) copy-start(bf16[256,1024]{1,0:T(8,128)(2,1)} %param.12) | copy-start | bytes 1572868
  1.1 3.1 %copy-start.2 = (bf16[256,512]{1,0:T(8,128)(2,1)}, bf16[256,512]{1,0:T(8,128)(2,1)S(1)}, u32[]{:S(2)}) copy-start(bf16[256,512]{1,0:T(8,128)(2,1)S(1)} %constant_dynamic-slice_fusion.after.w0) | copy-start | bytes 786436
  1.1 22.5 %copy-start.5 = (bf16[128,1024]{1,0:T(8,128)(2,1)S(1)}, bf16[128,1024]{1,0:T(8,128)(2,1)}, u32[]{:S(2)}) copy-start(bf16[128,1024]{1,0:T(8,128)(2,1)} %refs_0_.1) | copy-start | bytes 786436
  1.1 14.2 %collective-permute-start.2 = (bf16[256,512]{1,0:T(8,128)(2,1)S(1)}, bf16[256,512]{1,0:T(8,128)(2,1)S(1)}, u32[]{:S(2)}, u32[]{:S(2)}) collective-permute-start(bf16[256,512]{1,0:T(8,128)(2,1)S(1)} %constant_dynamic-slice_fusion.after.w0), channel_id=1, source_target_pairs={{0,4},{1,5},{2,6},{3,7},{4,8},{5,9},{6,10},{7,11},{8,12},{9,13},{1... | collective-permute-start | bytes 786440 | tf_op jit(solution)/shard_map/ppermute | solution.py:353
  6.8 25.7 %copy-start.1 = (bf16[2,2,128,1024]{3,2,1,0:T(8,128)(2,1)S(1)}, bf16[2,2,128,1024]{3,2,1,0:T(8,128)(2,1)}, u32[]{:S(2)}) copy-start(bf16[2,2,128,1024]{3,2,1,0:T(8,128)(2,1)} %filt.3) | copy-start | bytes 3145732
  6.8 8.5 %collective-permute-start.1 = (bf16[256,256]{1,0:T(8,128)(2,1)}, bf16[256,256]{1,0:T(8,128)(2,1)S(1)}, u32[]{:S(2)}, u32[]{:S(2)}) collective-permute-start(bf16[256,256]{1,0:T(8,128)(2,1)} %get-tuple-element.43.refs_0_), channel_id=1, source_target_pairs={{0,4},{1,5},{2,6},{3,7},{4,8},{5,9},{6,10},{7,11},{8,12},{9,13},{1... | collective-permute-start | bytes 393224 | tf_op jit(solution)/shard_map/ppermute | solution.py:353
  8.4 9.5 %collective-permute-start = (bf16[128,1024]{1,0:T(8,128)(2,1)}, bf16[128,1024]{1,0:T(8,128)(2,1)S(1)}, u32[]{:S(2)}, u32[]{:S(2)}) collective-permute-start(bf16[128,1024]{1,0:T(8,128)(2,1)} %get-tuple-element.42), channel_id=1, source_target_pairs={{0,2},{1,3},{2,0},{3,1},{4,6},{5,7},{6,4},{7,5},{8,10},{9,11},{10,... | collective-permute-start | bytes 786440 | tf_op jit(solution)/shard_map/ppermute | solution.py:353
  9.9 13.7 %collective-permute-start.4 = (bf16[128,1024]{1,0:T(8,128)(2,1)}, bf16[128,1024]{1,0:T(8,128)(2,1)S(1)}, u32[]{:S(2)}, u32[]{:S(2)}) collective-permute-start(bf16[128,1024]{1,0:T(8,128)(2,1)} %get-tuple-element.46), channel_id=1, source_target_pairs={{0,16},{1,17},{2,18},{3,19},{4,20},{5,21},{6,22},{7,23},{8,24},{9,... | collective-permute-start | bytes 786440 | tf_op jit(solution)/shard_map/ppermute | solution.py:353
  11.4 12.3 %copy-start.11 = (bf16[2,2,128,256]{3,2,1,0:T(8,128)(2,1)S(1)}, bf16[2,2,128,256]{3,2,1,0:T(8,128)(2,1)}, u32[]{:S(2)}) copy-start(bf16[2,2,128,256]{3,2,1,0:T(8,128)(2,1)} %get-tuple-element.48) | copy-start | bytes 786436
  11.4 12.1 %collective-permute-start.5 = (bf16[128,1024]{1,0:T(8,128)(2,1)}, bf16[128,1024]{1,0:T(8,128)(2,1)S(1)}, u32[]{:S(2)}, u32[]{:S(2)}) collective-permute-start(bf16[128,1024]{1,0:T(8,128)(2,1)} %get-tuple-element.47), channel_id=1, source_target_pairs={{0,18},{1,19},{2,16},{3,17},{4,22},{5,23},{6,20},{7,21},{8,26},{9,... | collective-permute-start | bytes 786440 | tf_op jit(solution)/shard_map/ppermute | solution.py:353
  15.3 8.2 %collective-permute-start.3 = (bf16[256,256]{1,0:T(8,128)(2,1)S(1)}, bf16[256,256]{1,0:T(8,128)(2,1)S(1)}, u32[]{:S(2)}, u32[]{:S(2)}) collective-permute-start(bf16[256,256]{1,0:T(8,128)(2,1)S(1)} %collective-permute-done.1.refs_2_), channel_id=1, source_target_pairs={{0,4},{1,5},{2,6},{3,7},{4,8},{5,9},{6,10},{7,11},{8,12},{9,13},{1... | collective-permute-start | bytes 393224 | tf_op jit(solution)/shard_map/ppermute | solution.py:353
  15.3 12.1 %collective-permute-start.8 = (bf16[256,512]{1,0:T(8,128)(2,1)S(1)}, bf16[256,512]{1,0:T(8,128)(2,1)S(1)}, u32[]{:S(2)}, u32[]{:S(2)}) collective-permute-start(bf16[256,512]{1,0:T(8,128)(2,1)S(1)} %collective-permute-done.2.w1), channel_id=1, source_target_pairs={{0,4},{1,5},{2,6},{3,7},{4,8},{5,9},{6,10},{7,11},{8,12},{9,13},{1... | collective-permute-start | bytes 786440 | tf_op jit(solution)/shard_map/ppermute | solution.py:353
  23.6 16.0 %collective-permute-start.10 = (bf16[512,512]{1,0:T(8,128)(2,1)S(1)}, bf16[512,512]{1,0:T(8,128)(2,1)S(1)}, u32[]{:S(2)}, u32[]{:S(2)}) collective-permute-start(bf16[512,512]{1,0:T(8,128)(2,1)S(1)} %shard_map.92.mine), channel_id=1, source_target_pairs={{0,1},{1,0},{2,3},{3,2},{4,5},{5,4},{6,7},{7,6},{8,9},{9,8},{10,11... | collective-permute-start | bytes 1572872 | tf_op jit(solution)/shard_map/ppermute | solution.py:353
  23.7 10.0 %copy-start.12 = (bf16[256,256]{1,0:T(8,128)(2,1)S(1)}, bf16[256,256]{1,0:T(8,128)(2,1)}, u32[]{:S(2)}) copy-start(bf16[256,256]{1,0:T(8,128)(2,1)} %get-tuple-element.51) | copy-start | bytes 393220
  23.7 15.9 %copy-start.3 = (bf16[256,512]{1,0:T(8,128)(2,1)S(1)}, bf16[256,512]{1,0:T(8,128)(2,1)}, u32[]{:S(2)}) copy-start(bf16[256,512]{1,0:T(8,128)(2,1)} %copy-done.2) | copy-start | bytes 786436
  23.7 8.7 %collective-permute-start.6 = (bf16[2,2,128,256]{3,2,1,0:T(8,128)(2,1)S(1)}, bf16[2,2,128,256]{3,2,1,0:T(8,128)(2,1)S(1)}, u32[]{:S(2)}, u32[]{:S(2)}) collective-permute-start(bf16[2,2,128,256]{3,2,1,0:T(8,128)(2,1)S(1)} %copy-done.11), channel_id=1, source_target_pairs={{0,2},{1,3},{2,0},{3,1},{4,6},{5,7},{6,4},{7,5},{8,10},{9,11},{10,... | collective-permute-start | bytes 786440 | tf_op jit(solution)/shard_map/ppermute | solution.py:353
  27.4 12.2 %collective-permute-start.11 = (bf16[256,512]{1,0:T(8,128)(2,1)S(1)}, bf16[256,512]{1,0:T(8,128)(2,1)S(1)}, u32[]{:S(2)}, u32[]{:S(2)}) collective-permute-start(bf16[256,512]{1,0:T(8,128)(2,1)S(1)} %collective-permute-done.8.w2), channel_id=1, source_target_pairs={{0,4},{1,5},{2,6},{3,7},{4,8},{5,9},{6,10},{7,11},{8,12},{9,13},{1... | collective-permute-start | bytes 786440 | tf_op jit(solution)/shard_map/ppermute | solution.py:353
  32.7 6.9 %collective-permute-start.7 = (bf16[2,2,128,128]{3,2,1,0:T(8,128)(2,1)S(1)}, bf16[2,2,128,128]{3,2,1,0:T(8,128)(2,1)S(1)}, u32[]{:S(2)}, u32[]{:S(2)}) collective-permute-start(bf16[2,2,128,128]{3,2,1,0:T(8,128)(2,1)S(1)} %get-tuple-element.49), channel_id=1, source_target_pairs={{0,4},{1,5},{2,6},{3,7},{4,8},{5,9},{6,10},{7,11},{8,12},{9,13},{1... | collective-permute-start | bytes 393224 | tf_op jit(solution)/shard_map/ppermute | solution.py:353
  33.7 23.1 %copy-start.4 = (bf16[128,1024]{1,0:T(8,128)(2,1)S(1)}, bf16[128,1024]{1,0:T(8,128)(2,1)}, u32[]{:S(2)}) copy-start(bf16[128,1024]{1,0:T(8,128)(2,1)} %g0.2) | copy-start | bytes 786436
  33.7 5.9 %collective-permute-start.9 = (bf16[256,256]{1,0:T(8,128)(2,1)S(1)}, bf16[256,256]{1,0:T(8,128)(2,1)S(1)}, u32[]{:S(2)}, u32[]{:S(2)}) collective-permute-start(bf16[256,256]{1,0:T(8,128)(2,1)S(1)} %copy-done.12), channel_id=1, source_target_pairs={{0,2},{1,3},{2,0},{3,1},{4,6},{5,7},{6,4},{7,5},{8,10},{9,11},{10,... | collective-permute-start | bytes 393224 | tf_op jit(solution)/shard_map/ppermute | solution.py:353
  39.7 29.8 %copy-start.10 = (bf16[16,256,128]{2,1,0:T(8,128)(2,1)S(1)}, bf16[16,256,128]{2,1,0:T(8,128)(2,1)}, u32[]{:S(2)}) copy-start(bf16[16,256,128]{2,1,0:T(8,128)(2,1)} %constant.17.clone.refs_9_) | copy-start | bytes 3145732
  41.0 15.8 %copy-start.8 = (f32[1024]{0:T(1024)S(1)}, f32[1024]{0:T(1024)}, u32[]{:S(2)}) copy-start(f32[1024]{0:T(1024)} %param.13) | copy-start | bytes 12292
  41.0 28.5 %copy-start.9 = (bf16[16,256,128]{2,1,0:T(8,128)(2,1)S(1)}, bf16[16,256,128]{2,1,0:T(8,128)(2,1)}, u32[]{:S(2)}) copy-start(bf16[16,256,128]{2,1,0:T(8,128)(2,1)} %constant.16.clone.refs_8_) | copy-start | bytes 3145732
  41.0 15.8 %collective-permute-start.13 = (bf16[512,256]{1,0:T(8,128)(2,1)S(1)}, bf16[512,256]{1,0:T(8,128)(2,1)S(1)}, u32[]{:S(2)}, u32[]{:S(2)}) collective-permute-start(bf16[512,256]{1,0:T(8,128)(2,1)S(1)} %get-tuple-element.56), channel_id=1, source_target_pairs={{0,2},{1,3},{2,0},{3,1},{4,6},{5,7},{6,4},{7,5},{8,10},{9,11},{10,... | collective-permute-start | bytes 786440 | tf_op jit(solution)/shard_map/ppermute | solution.py:353
  42.5 7.2 %collective-permute-start.22 = (bf16[256,256]{1,0:T(8,128)(2,1)S(1)}, bf16[256,256]{1,0:T(8,128)(2,1)S(1)}, u32[]{:S(2)}, u32[]{:S(2)}) collective-permute-start(bf16[256,256]{1,0:T(8,128)(2,1)S(1)} %collective-permute-done.9.refs_1_), channel_id=1, source_target_pairs={{0,4},{1,5},{2,6},{3,7},{4,8},{5,9},{6,10},{7,11},{8,12},{9,13},{1... | collective-permute-start | bytes 393224 | tf_op jit(solution)/shard_map/ppermute | solution.py:353
  42.5 14.3 %collective-permute-start.12 = (bf16[2,2,128,128]{3,2,1,0:T(8,128)(2,1)S(1)}, bf16[2,2,128,128]{3,2,1,0:T(8,128)(2,1)S(1)}, u32[]{:S(2)}, u32[]{:S(2)}) collective-permute-start(bf16[2,2,128,128]{3,2,1,0:T(8,128)(2,1)S(1)} %get-tuple-element.54), channel_id=1, source_target_pairs={{0,8},{1,9},{2,10},{3,11},{4,12},{5,13},{6,14},{7,15},{8,0},{9,1},... | collective-permute-start | bytes 393224 | tf_op jit(solution)/shard_map/ppermute | solution.py:353
  49.7 11.3 %collective-permute-start.23 = (bf16[256,256]{1,0:T(8,128)(2,1)S(1)}, bf16[256,256]{1,0:T(8,128)(2,1)S(1)}, u32[]{:S(2)}, u32[]{:S(2)}) collective-permute-start(bf16[256,256]{1,0:T(8,128)(2,1)S(1)} %collective-permute-done.22.refs_3_), channel_id=1, source_target_pairs={{0,4},{1,5},{2,6},{3,7},{4,8},{5,9},{6,10},{7,11},{8,12},{9,13},{1... | collective-permute-start | bytes 393224 | tf_op jit(solution)/shard_map/ppermute | solution.py:353
  49.8 19.7 %collective-permute-start.17 = (bf16[2,2,128,128]{3,2,1,0:T(8,128)(2,1)S(1)}, bf16[2,2,128,128]{3,2,1,0:T(8,128)(2,1)S(1)}, u32[]{:S(2)}, u32[]{:S(2)}) collective-permute-start(bf16[2,2,128,128]{3,2,1,0:T(8,128)(2,1)S(1)} %get-tuple-element.62), channel_id=1, source_target_pairs={{0,12},{1,13},{2,14},{3,15},{4,0},{5,1},{6,2},{7,3},{8,4},{9,5},{1... | collective-permute-start | bytes 393224 | tf_op jit(solution)/shard_map/ppermute | solution.py:353
  57.2 6.1 %collective-permute-start.14 = (bf16[256,128]{1,0:T(8,128)(2,1)S(1)}, bf16[256,128]{1,0:T(8,128)(2,1)S(1)}, u32[]{:S(2)}, u32[]{:S(2)}) collective-permute-start(bf16[256,128]{1,0:T(8,128)(2,1)S(1)} %get-tuple-element.58), channel_id=1, source_target_pairs={{0,4},{1,5},{2,6},{3,7},{4,8},{5,9},{6,10},{7,11},{8,12},{9,13},{1... | collective-permute-start | bytes 196616 | tf_op jit(solution)/shard_map/ppermute | solution.py:353
  57.2 6.1 %collective-permute-start.15 = (bf16[256,128]{1,0:T(8,128)(2,1)S(1)}, bf16[256,128]{1,0:T(8,128)(2,1)S(1)}, u32[]{:S(2)}, u32[]{:S(2)}) collective-permute-start(bf16[256,128]{1,0:T(8,128)(2,1)S(1)} %get-tuple-element.59), channel_id=1, source_target_pairs={{0,8},{1,9},{2,10},{3,11},{4,12},{5,13},{6,14},{7,15},{8,0},{9,1},... | collective-permute-start | bytes 196616 | tf_op jit(solution)/shard_map/ppermute | solution.py:353
  57.3 6.7 %collective-permute-start.16 = (bf16[256,128]{1,0:T(8,128)(2,1)S(1)}, bf16[256,128]{1,0:T(8,128)(2,1)S(1)}, u32[]{:S(2)}, u32[]{:S(2)}) collective-permute-start(bf16[256,128]{1,0:T(8,128)(2,1)S(1)} %get-tuple-element.60), channel_id=1, source_target_pairs={{0,12},{1,13},{2,14},{3,15},{4,0},{5,1},{6,2},{7,3},{8,4},{9,5},{1... | collective-permute-start | bytes 196616 | tf_op jit(solution)/shard_map/ppermute | solution.py:353
  64.0 16.0 %collective-permute-start.25 = (bf16[256,256]{1,0:T(8,128)(2,1)S(1)}, bf16[256,256]{1,0:T(8,128)(2,1)S(1)}, u32[]{:S(2)}, u32[]{:S(2)}) collective-permute-start(bf16[256,256]{1,0:T(8,128)(2,1)S(1)} %collective-permute-done.23.refs_5_), channel_id=1, source_target_pairs={{0,4},{1,5},{2,6},{3,7},{4,8},{5,9},{6,10},{7,11},{8,12},{9,13},{1... | collective-permute-start | bytes 393224 | tf_op jit(solution)/shard_map/ppermute | solution.py:353
  69.4 10.6 %collective-permute-start.24 = (bf16[256,256]{1,0:T(8,128)(2,1)S(1)}, bf16[256,256]{1,0:T(8,128)(2,1)S(1)}, u32[]{:S(2)}, u32[]{:S(2)}) collective-permute-start(bf16[256,256]{1,0:T(8,128)(2,1)S(1)} %collective-permute-done.3.refs_4_), channel_id=1, source_target_pairs={{0,4},{1,5},{2,6},{3,7},{4,8},{5,9},{6,10},{7,11},{8,12},{9,13},{1... | collective-permute-start | bytes 393224 | tf_op jit(solution)/shard_map/ppermute | solution.py:353
  69.4 10.5 %copy-start.7 = (bf16[256,256]{1,0:T(8,128)(2,1)S(1)}, bf16[256,256]{1,0:T(8,128)(2,1)}, u32[]{:S(2)}) copy-start(bf16[256,256]{1,0:T(8,128)(2,1)} %get-tuple-element.43.refs_0_) | copy-start | bytes 393220
  71.2 6.1 %collective-permute-start.18 = (bf16[256,128]{1,0:T(8,128)(2,1)S(1)}, bf16[256,128]{1,0:T(8,128)(2,1)S(1)}, u32[]{:S(2)}, u32[]{:S(2)}) collective-permute-start(bf16[256,128]{1,0:T(8,128)(2,1)S(1)} %get-tuple-element.64), channel_id=1, source_target_pairs={{0,4},{1,5},{2,6},{3,7},{4,8},{5,9},{6,10},{7,11},{8,12},{9,13},{1... | collective-permute-start | bytes 196616 | tf_op jit(solution)/shard_map/ppermute | solution.py:353
  71.3 7.5 %collective-permute-start.19 = (bf16[256,128]{1,0:T(8,128)(2,1)S(1)}, bf16[256,128]{1,0:T(8,128)(2,1)S(1)}, u32[]{:S(2)}, u32[]{:S(2)}) collective-permute-start(bf16[256,128]{1,0:T(8,128)(2,1)S(1)} %get-tuple-element.65), channel_id=1, source_target_pairs={{0,8},{1,9},{2,10},{3,11},{4,12},{5,13},{6,14},{7,15},{8,0},{9,1},... | collective-permute-start | bytes 196616 | tf_op jit(solution)/shard_map/ppermute | solution.py:353
  75.7 4.5 %copy-start.6 = (bf16[128,1024]{1,0:T(8,128)(2,1)S(1)}, bf16[128,1024]{1,0:T(8,128)(2,1)}, u32[]{:S(2)}) copy-start(bf16[128,1024]{1,0:T(8,128)(2,1)} %g0.3) | copy-start | bytes 786436
  75.7 4.3 %collective-permute-start.20 = (bf16[256,128]{1,0:T(8,128)(2,1)S(1)}, bf16[256,128]{1,0:T(8,128)(2,1)S(1)}, u32[]{:S(2)}, u32[]{:S(2)}) collective-permute-start(bf16[256,128]{1,0:T(8,128)(2,1)S(1)} %get-tuple-element.66), channel_id=1, source_target_pairs={{0,12},{1,13},{2,14},{3,15},{4,0},{5,1},{6,2},{7,3},{8,4},{9,5},{1... | collective-permute-start | bytes 196616 | tf_op jit(solution)/shard_map/ppermute | solution.py:353
  80.1 2.4 %collective-permute-start.26 = (bf16[4,256,256]{2,1,0:T(8,128)(2,1)S(1)}, bf16[4,256,256]{2,1,0:T(8,128)(2,1)S(1)}, u32[]{:S(2)}, u32[]{:S(2)}) collective-permute-start(bf16[4,256,256]{2,1,0:T(8,128)(2,1)S(1)} %get-tuple-element.74), channel_id=1, source_target_pairs={{0,1},{1,0},{2,3},{3,2},{4,5},{5,4},{6,7},{7,6},{8,9},{9,8},{10,11... | collective-permute-start | bytes 1572872 | tf_op jit(solution)/shard_map/ppermute | solution.py:353
  80.4 2.0 %collective-permute-start.21 = (bf16[512,256]{1,0:T(8,128)(2,1)S(1)}, bf16[512,256]{1,0:T(8,128)(2,1)S(1)}, u32[]{:S(2)}, u32[]{:S(2)}) collective-permute-start(bf16[512,256]{1,0:T(8,128)(2,1)S(1)} %shard_map.97.gated), channel_id=1, source_target_pairs={{0,1},{1,0},{2,3},{3,2},{4,5},{5,4},{6,7},{7,6},{8,9},{9,8},{10,11... | collective-permute-start | bytes 786440 | tf_op jit(solution)/shard_map/ppermute | solution.py:353
  83.3 10.2 %collective-permute-start.27 = (bf16[128,1024]{1,0:T(8,128)(2,1)S(1)}, bf16[128,1024]{1,0:T(8,128)(2,1)S(1)}, u32[]{:S(2)}, u32[]{:S(2)}) collective-permute-start(bf16[128,1024]{1,0:T(8,128)(2,1)S(1)} %get-tuple-element.76), channel_id=1, source_target_pairs={{0,18},{1,19},{2,16},{3,17},{4,22},{5,23},{6,20},{7,21},{8,26},{9,... | collective-permute-start | bytes 786440 | tf_op jit(solution)/shard_map/ppermute | solution.py:353
  84.8 13.5 %collective-permute-start.28 = (bf16[128,1024]{1,0:T(8,128)(2,1)S(1)}, bf16[128,1024]{1,0:T(8,128)(2,1)S(1)}, u32[]{:S(2)}, u32[]{:S(2)}) collective-permute-start(bf16[128,1024]{1,0:T(8,128)(2,1)S(1)} %get-tuple-element.77), channel_id=1, source_target_pairs={{0,2},{1,3},{2,0},{3,1},{4,6},{5,7},{6,4},{7,5},{8,10},{9,11},{10,... | collective-permute-start | bytes 786440 | tf_op jit(solution)/shard_map/ppermute | solution.py:353
  87.1 11.2 %collective-permute-start.29 = (bf16[128,1024]{1,0:T(8,128)(2,1)S(1)}, bf16[128,1024]{1,0:T(8,128)(2,1)S(1)}, u32[]{:S(2)}, u32[]{:S(2)}) collective-permute-start(bf16[128,1024]{1,0:T(8,128)(2,1)S(1)} %get-tuple-element.78), channel_id=1, source_target_pairs={{0,16},{1,17},{2,18},{3,19},{4,20},{5,21},{6,22},{7,23},{8,24},{9,... | collective-permute-start | bytes 786440 | tf_op jit(solution)/shard_map/ppermute | solution.py:353

commit v11 on v10

--- a/solution.py
+++ b/solution.py
@@ -126,7 +126,7 @@
                 packed[2 * j, k, part] = one
                 packed[2 * j + 1, k, part] = two
     for r in range(4):
-        outs[r][...] = packed[lax.rem(z + r, 4)]
+        outs[r][...] = packed[z ^ r]
 
 
 def join_tokens(*refs):
@@ -175,7 +175,7 @@
         second = drive[pl.ds(256, 256), lanes].astype(F32)
         packed[2 * j], packed[2 * j + 1] = both(first, second, low)
     for r, out in enumerate((o0, o1, o2, o3)):
-        out[...] = packed[lax.rem(z + r, 4)]
+        out[...] = packed[z ^ r]
 
 
 def add(a, b):
@@ -229,7 +229,7 @@
     outs, (data, filt, first, sums) = refs[10:14], refs[14:]
     _, x, z, _ = place()
     for r, block in enumerate(drives):
-        base = 2 * lax.rem(z - r + 4, 4)
+        base = 2 * (z ^ r)
         filt[base + x] = filters[r][0]
         filt[base + 1 - x] = filters[r][1]
         data[base + x] = block[pl.ds(0, 128), :]
@@ -284,7 +284,7 @@
             if 0 < a < 4:
                 data[8 - a, rows, :] = sub(sub(add(ec, os), oc), es).astype(BF16)
     for r, out in enumerate(outs):
-        base = 2 * lax.rem(z + r, 4)
+        base = 2 * (z ^ r)
         out[pl.ds(0, 128), :] = data[base + x]
         out[pl.ds(128, 128), :] = data[base + 1 - x]
 
@@ -292,7 +292,7 @@
 def gate_kernel(e0, e1, e2, e3, direct, g0, g1, g2, g3, gated, conv):
     _, _, z, _ = place()
     for r, block in enumerate((e0, e1, e2, e3)):
-        conv[lax.rem(z - r + 4, 4)] = block[...]
+        conv[z ^ r] = block[...]
     low = low_lanes((256, 128))
     for j in range(2):
         lanes = pl.ds(j * 128, 128)
@@ -358,6 +358,9 @@
     def to_core(values):
         return permute(values, lambda g, z, x, k: (g, z, x, 1 - k))
 
+    def with_z(values, r):
+        return permute(values, lambda g, z, x, k: (g, z ^ r, x, k))
+
     def to_z(values, r):
         return permute(values, lambda g, z, x, k: (g, (z + r) % deep, x, k))
 
@@ -382,13 +385,14 @@
         [pltpu.VMEM((4, 2, 2, 128, 128), BF16)],
         moved=1 << 20,
     )(filter_spectrum, near)
-    filters = [filters[0]] + [to_z(filters[r], r) for r in (1, 2, 3)]
+    filters = [filters[0]] + [with_z(filters[r], r) for r in (1, 2, 3)]
     v1 = to_z(own_v, 1)
     q1 = to_z(own_o, 1)
     v2 = to_z(v1, 1)
     q2 = to_z(after(q1, v1), 1)
     mine = in_vmem(join_tokens, shape((512, 512), BF16), moved=1 << 20)(tokens, after(received[0], q2), *received[1:])
     v3 = to_z(v2, 1)
+    q3 = to_z(q2, 1)
     other = to_core(mine)
     got_o = to_x(after(away_o, v2))
     r1 = to_z(after(got_o, v3), 1)
@@ -398,7 +402,7 @@
         [pltpu.VMEM((512, 512), F32)],
         flops=1 << 29,
         moved=2 << 20,
-    )(after(mine, filters[1], got_o), other, own_v, v1, v2, v3)
+    )(after(mine, q3, near, got_o), other, own_v, v1, v2, v3)
     r2 = to_z(after(r1, keep), 1)
     drive, *sends = in_vmem(
         drive_kernel,
@@ -406,8 +410,7 @@
         [pltpu.VMEM((512, 256), BF16), pltpu.VMEM((4, 256, 128), BF16)],
         moved=2 << 20,
     )(after(keep, filters[1], filters[2]), to_x(give), gate_k, *received, skip[None, :])
-    columns = [sends[0]] + [to_z(sends[r], r) for r in (1, 2, 3)]
-    q3 = to_z(after(q2, columns[1]), 1)
+    columns = [sends[0]] + [with_z(sends[r], r) for r in (1, 2, 3)]
     r3 = to_z(after(r2, *columns[1:]), 1)
     table, table_t = tables()
     sends = in_vmem(
@@ -422,7 +425,7 @@
         flops=1 << 30,
         moved=5 << 20,
     )(*columns, *filters, table, table_t)
-    rows = [sends[0]] + [to_z(sends[r], r) for r in (1, 2, 3)]
+    rows = [sends[0]] + [with_z(sends[r], r) for r in (1, 2, 3)]
 
     hops = [own_o, got_o, q1, r1, q2, r2, q3, after(r3, *rows[1:])]
     quad = shape((4, 256, 256), BF16)

time: 99.3 us -> 99.9 us (level)
  waiting for transfers between devices: 49.4 us -> 53.1 us
  starting transfers between devices: 39.2 us -> 36.1 us
    ppermute x30, waiting for transfers between devices: 49.4 us -> 53.1 us  [permute(): return lax.ppermute(values, AXES, pairs)]
    ppermute x30, starting transfers between devices: 39.2 us -> 36.1 us  [permute(): return lax.ppermute(values, AXES, pairs)]
  transfers between devices with their start and end apart: 30 -> 30, of which waited for: 16 -> 15; matrix products, arithmetic and copies ran while one was open for 0% -> 0% of each run, Pallas kernels for 6% -> 6%
where the time goes in v11:
time: 99.9 us; the launch traced here: 99.7 us
  waiting for transfers between devices  53.1 us (53%)
  starting transfers between devices  36.1 us (36%)
  Pallas kernels  8.3 us (8%)
  local copies, waits for them, and re-layouts  1.12 us (1%)
    ppermute x30, waiting for transfers between devices, permute(): return lax.ppermute(values, AXES, pairs)  53.1 us
    ppermute x30, starting transfers between devices, permute(): return lax.ppermute(values, AXES, pairs)  36.1 us
    pallas_call x9, Pallas kernels, call(): pl.pallas_call(kernel, out_shape=out_shape, in_specs=specs, out_specs=jax...  5.73 us
    pallas_call x1, Pallas kernels, call(): pl.pallas_call(kernel, out_shape=out_shape, in_specs=[pl.BlockSpec(memory...  2.58 us
  transfers between devices with their start and end apart: 30, of which 15 were waited for; matrix products, arithmetic and copies ran while one was open for 0% of the time, Pallas kernels for 6%

profile of v11, /device:TPU:0, one launch (start us, length us, event | category | flops | bytes accessed | tf_op | source)
XLA Modules:
  0.0 99.7 jit_solution(8693938845552187124)
XLA Ops:
  0.0 1.0 %copy-done = bf16[256,1024]{1,0:T(8,128)(2,1)S(1)} copy-done((bf16[256,1024]{1,0:T(8,128)(2,1)S(1)}, bf16[256,1024]{1,0:T(8,128)(2,1)}, u32[]{:S(2)}) %copy-start) | copy-done | bytes 524312
  1.1 0.0 copy-start.2
  1.1 0.0 copy-start.5
  1.1 3.1 %collective-permute-start.2 = (bf16[256,512]{1,0:T(8,128)(2,1)S(1)}, bf16[256,512]{1,0:T(8,128)(2,1)S(1)}, u32[]{:S(2)}, u32[]{:S(2)}) collective-permute-start(bf16[256,512]{1,0:T(8,128)(2,1)S(1)} %constant_dynamic-slice_fusion.after.w0), channel_id=1, source_target_pairs={{0,4},{1,5},{2,6},{3,7},{4,8},{5,9},{6,10},{7,11},{8,12},{9,13},{1... | collective-permute-start | bytes 786440 | tf_op jit(solution)/shard_map/ppermute | solution.py:353
  4.2 2.6 %shard_map.91 = (bf16[128,1024]{1,0:T(8,128)(2,1)}, bf16[128,1024]{1,0:T(8,128)(2,1)}, bf16[128,1024]{1,0:T(8,128)(2,1)}, bf16[256,256]{1,0:T(8,128)(2,1)}, bf16...) custom-call(bf16[128,1024]{1,0:T(8,128)(2,1)} %refs_0_.1, bf16[128,1024]{1,0:T(8,128)(2,1)} %g0.2, ...), custom_call_target="tpu_custom_call" | custom-call | tf_op jit(solution)/shard_map/pallas_call | solution.py:101
  6.8 1.6 %collective-permute-start.1 = (bf16[256,256]{1,0:T(8,128)(2,1)}, bf16[256,256]{1,0:T(8,128)(2,1)S(1)}, u32[]{:S(2)}, u32[]{:S(2)}) collective-permute-start(bf16[256,256]{1,0:T(8,128)(2,1)} %get-tuple-element.42.refs_0_), channel_id=1, source_target_pairs={{0,4},{1,5},{2,6},{3,7},{4,8},{5,9},{6,10},{7,11},{8,12},{9,13},{1... | collective-permute-start | bytes 393224 | tf_op jit(solution)/shard_map/ppermute | solution.py:353
  8.4 1.5 %collective-permute-start = (bf16[128,1024]{1,0:T(8,128)(2,1)}, bf16[128,1024]{1,0:T(8,128)(2,1)S(1)}, u32[]{:S(2)}, u32[]{:S(2)}) collective-permute-start(bf16[128,1024]{1,0:T(8,128)(2,1)} %get-tuple-element.41), channel_id=1, source_target_pairs={{0,2},{1,3},{2,0},{3,1},{4,6},{5,7},{6,4},{7,5},{8,10},{9,11},{10,... | collective-permute-start | bytes 786440 | tf_op jit(solution)/shard_map/ppermute | solution.py:353
  9.9 1.5 %collective-permute-start.4 = (bf16[128,1024]{1,0:T(8,128)(2,1)}, bf16[128,1024]{1,0:T(8,128)(2,1)S(1)}, u32[]{:S(2)}, u32[]{:S(2)}) collective-permute-start(bf16[128,1024]{1,0:T(8,128)(2,1)} %get-tuple-element.45), channel_id=1, source_target_pairs={{0,16},{1,17},{2,18},{3,19},{4,20},{5,21},{6,22},{7,23},{8,24},{9,... | collective-permute-start | bytes 786440 | tf_op jit(solution)/shard_map/ppermute | solution.py:353
  11.4 0.5 collective-permute-start.5
  11.9 3.4 %collective-permute-done.1.refs_2_ = bf16[256,256]{1,0:T(8,128)(2,1)S(1)} collective-permute-done((bf16[256,256]{1,0:T(8,128)(2,1)}, bf16[256,256]{1,0:T(8,128)(2,1)S(1)}, u32[]{:S(2)}, u32[]{:S(2)}) %collective-permute-start.1) | collective-permute-done | bytes 131104 | tf_op jit(solution)/shard_map/ppermute | solution.py:353
  15.3 0.0 collective-permute-done.2.w1
  15.3 0.0 collective-permute-start.3
  15.3 1.3 %collective-permute-start.8 = (bf16[256,512]{1,0:T(8,128)(2,1)S(1)}, bf16[256,512]{1,0:T(8,128)(2,1)S(1)}, u32[]{:S(2)}, u32[]{:S(2)}) collective-permute-start(bf16[256,512]{1,0:T(8,128)(2,1)S(1)} %collective-permute-done.2.w1), channel_id=1, source_target_pairs={{0,4},{1,5},{2,6},{3,7},{4,8},{5,9},{6,10},{7,11},{8,12},{9,13},{1... | collective-permute-start | bytes 786440 | tf_op jit(solution)/shard_map/ppermute | solution.py:353
  16.6 1.2 %collective-permute-done.refs_1_.g1 = bf16[128,1024]{1,0:T(8,128)(2,1)S(1)} collective-permute-done((bf16[128,1024]{1,0:T(8,128)(2,1)}, bf16[128,1024]{1,0:T(8,128)(2,1)S(1)}, u32[]{:S(2)}, u32[]{:S(2)}) %collective-permute-start) | collective-permute-done | bytes 262176 | tf_op jit(solution)/shard_map/ppermute | solution.py:353
  17.8 5.7 %collective-permute-done.3.refs_4_ = bf16[256,256]{1,0:T(8,128)(2,1)S(1)} collective-permute-done((bf16[256,256]{1,0:T(8,128)(2,1)S(1)}, bf16[256,256]{1,0:T(8,128)(2,1)S(1)}, u32[]{:S(2)}, u32[]{:S(2)}) %collective-permute-start.3) | collective-permute-done | bytes 131104 | tf_op jit(solution)/shard_map/ppermute | solution.py:353
  23.5 0.0 collective-permute-done.4.refs_2_.g2
  23.5 0.0 collective-permute-done.5.refs_3_.g3
  23.6 0.1 collective-permute-start.10
  23.7 1.6 %collective-permute-start.7 = (bf16[2,2,128,256]{3,2,1,0:T(8,128)(2,1)S(1)}, bf16[2,2,128,256]{3,2,1,0:T(8,128)(2,1)S(1)}, u32[]{:S(2)}, u32[]{:S(2)}) collective-permute-start(bf16[2,2,128,256]{3,2,1,0:T(8,128)(2,1)S(1)} %copy-done.11), channel_id=1, source_target_pairs={{0,2},{1,3},{2,0},{3,1},{4,6},{5,7},{6,4},{7,5},{8,10},{9,11},{10,... | collective-permute-start | bytes 786440 | tf_op jit(solution)/shard_map/ppermute | solution.py:353
  25.2 2.2 %collective-permute-done.8.w2 = bf16[256,512]{1,0:T(8,128)(2,1)S(1)} collective-permute-done((bf16[256,512]{1,0:T(8,128)(2,1)S(1)}, bf16[256,512]{1,0:T(8,128)(2,1)S(1)}, u32[]{:S(2)}, u32[]{:S(2)}) %collective-permute-start.8) | collective-permute-done | bytes 262176 | tf_op jit(solution)/shard_map/ppermute | solution.py:353
  27.4 0.0 copy-start.1
  27.4 1.3 %collective-permute-start.9 = (bf16[256,256]{1,0:T(8,128)(2,1)S(1)}, bf16[256,256]{1,0:T(8,128)(2,1)S(1)}, u32[]{:S(2)}, u32[]{:S(2)}) collective-permute-start(bf16[256,256]{1,0:T(8,128)(2,1)S(1)} %copy-done.12), channel_id=1, source_target_pairs={{0,2},{1,3},{2,0},{3,1},{4,6},{5,7},{6,4},{7,5},{8,10},{9,11},{10,... | collective-permute-start | bytes 393224 | tf_op jit(solution)/shard_map/ppermute | solution.py:353
  28.7 4.1 %collective-permute-done.7.near = bf16[2,2,128,256]{3,2,1,0:T(8,128)(2,1)S(1)} collective-permute-done((bf16[2,2,128,256]{3,2,1,0:T(8,128)(2,1)S(1)}, bf16[2,2,128,256]{3,2,1,0:T(8,128)(2,1)S(1)}, u32[]{:S(2)}, u32[]{:S(2)}) %collective-permute-start.7) | collective-permute-done | bytes 262176 | tf_op jit(solution)/shard_map/ppermute | solution.py:353
  32.9 5.7 %collective-permute-done.6.refs_6_ = bf16[256,256]{1,0:T(8,128)(2,1)S(1)} collective-permute-done((bf16[256,256]{1,0:T(8,128)(2,1)S(1)}, bf16[256,256]{1,0:T(8,128)(2,1)S(1)}, u32[]{:S(2)}, u32[]{:S(2)}) %collective-permute-start.6) | collective-permute-done | bytes 131104 | tf_op jit(solution)/shard_map/ppermute | solution.py:353
  38.6 0.0 collective-permute-done.11.w3
  38.6 0.0 collective-permute-done.10.other
  38.6 1.3 %shard_map.93 = (f32[512,256]{1,0:T(8,128)S(1)}, bf16[512,256]{1,0:T(8,128)(2,1)S(1)}) custom-call(bf16[512,512]{1,0:T(8,128)(2,1)S(1)} %shard_map.92.mine, bf16[512,512]{1,0:T(8,128)(2,1)S(1)} %collective-permute-done.10.other, bf16[256,512]{1,0:T(8,128)(2,1)S(1)} %copy-done.3, bf16[256,512]{1,0:T(8,128)(2,1)S(1)} %collective-permute-done.2.w1, ...), custom_call_target="tpu_custom_call" | custom-call | flops 536870912 | bytes 2097152 | tf_op jit(solution)/shard_map/pallas_call | solution.py:37
  39.9 0.0 copy-start.4
  39.9 1.1 %collective-permute-start.14 = (bf16[512,256]{1,0:T(8,128)(2,1)S(1)}, bf16[512,256]{1,0:T(8,128)(2,1)S(1)}, u32[]{:S(2)}, u32[]{:S(2)}) collective-permute-start(bf16[512,256]{1,0:T(8,128)(2,1)S(1)} %get-tuple-element.55), channel_id=1, source_target_pairs={{0,2},{1,3},{2,0},{3,1},{4,6},{5,7},{6,4},{7,5},{8,10},{9,11},{10,... | collective-permute-start | bytes 786440 | tf_op jit(solution)/shard_map/ppermute | solution.py:353
  41.0 0.0 collective-permute-start.23
  41.0 0.3 shard_map.94
  41.3 0.0 copy-start.8
  41.3 0.0 copy-start.9
  41.3 0.1 collective-permute-start.12
  41.4 4.4 %collective-permute-start.13 = (bf16[2,2,128,128]{3,2,1,0:T(8,128)(2,1)S(1)}, bf16[2,2,128,128]{3,2,1,0:T(8,128)(2,1)S(1)}, u32[]{:S(2)}, u32[]{:S(2)}) collective-permute-start(bf16[2,2,128,128]{3,2,1,0:T(8,128)(2,1)S(1)} %get-tuple-element.53), channel_id=1, source_target_pairs={{0,8},{1,9},{2,10},{3,11},{4,12},{5,13},{6,14},{7,15},{8,0},{9,1},... | collective-permute-start | bytes 393224 | tf_op jit(solution)/shard_map/ppermute | solution.py:353
  45.7 2.3 %collective-permute-done.23.refs_3_ = bf16[256,256]{1,0:T(8,128)(2,1)S(1)} collective-permute-done((bf16[256,256]{1,0:T(8,128)(2,1)S(1)}, bf16[256,256]{1,0:T(8,128)(2,1)S(1)}, u32[]{:S(2)}, u32[]{:S(2)}) %collective-permute-start.23) | collective-permute-done | bytes 131104 | tf_op jit(solution)/shard_map/ppermute | solution.py:353
  48.0 3.8 %collective-permute-start.18 = (bf16[2,2,128,128]{3,2,1,0:T(8,128)(2,1)S(1)}, bf16[2,2,128,128]{3,2,1,0:T(8,128)(2,1)S(1)}, u32[]{:S(2)}, u32[]{:S(2)}) collective-permute-start(bf16[2,2,128,128]{3,2,1,0:T(8,128)(2,1)S(1)} %get-tuple-element.61), channel_id=1, source_target_pairs={{0,12},{1,13},{2,14},{3,15},{4,8},{5,9},{6,10},{7,11},{8,4},{9,5},... | collective-permute-start | bytes 393224 | tf_op jit(solution)/shard_map/ppermute | solution.py:353
  51.8 7.5 %collective-permute-done.13.refs_6_ = bf16[2,2,128,128]{3,2,1,0:T(8,128)(2,1)S(1)} collective-permute-done((bf16[2,2,128,128]{3,2,1,0:T(8,128)(2,1)S(1)}, bf16[2,2,128,128]{3,2,1,0:T(8,128)(2,1)S(1)}, u32[]{:S(2)}, u32[]{:S(2)}) %collective-permute-start.13) | collective-permute-done | bytes 131104 | tf_op jit(solution)/shard_map/ppermute | solution.py:353
  59.3 0.3 shard_map.95
  59.7 0.1 collective-permute-start.15
  59.7 0.1 collective-permute-start.16
  59.8 4.3 %collective-permute-start.17 = (bf16[256,128]{1,0:T(8,128)(2,1)S(1)}, bf16[256,128]{1,0:T(8,128)(2,1)S(1)}, u32[]{:S(2)}, u32[]{:S(2)}) collective-permute-start(bf16[256,128]{1,0:T(8,128)(2,1)S(1)} %get-tuple-element.59), channel_id=1, source_target_pairs={{0,12},{1,13},{2,14},{3,15},{4,8},{5,9},{6,10},{7,11},{8,4},{9,5},... | collective-permute-start | bytes 196616 | tf_op jit(solution)/shard_map/ppermute | solution.py:353
  64.1 3.1 %collective-permute-done.16.refs_2_ = bf16[256,128]{1,0:T(8,128)(2,1)S(1)} collective-permute-done((bf16[256,128]{1,0:T(8,128)(2,1)S(1)}, bf16[256,128]{1,0:T(8,128)(2,1)S(1)}, u32[]{:S(2)}, u32[]{:S(2)}) %collective-permute-start.16) | collective-permute-done | bytes 65568 | tf_op jit(solution)/shard_map/ppermute | solution.py:353
  67.2 0.9 collective-permute-done.17.refs_3_
  68.2 1.2 %collective-permute-start.25 = (bf16[256,256]{1,0:T(8,128)(2,1)S(1)}, bf16[256,256]{1,0:T(8,128)(2,1)S(1)}, u32[]{:S(2)}, u32[]{:S(2)}) collective-permute-start(bf16[256,256]{1,0:T(8,128)(2,1)S(1)} %collective-permute-done.24.refs_5_), channel_id=1, source_target_pairs={{0,4},{1,5},{2,6},{3,7},{4,8},{5,9},{6,10},{7,11},{8,12},{9,13},{1... | collective-permute-start | bytes 393224 | tf_op jit(solution)/shard_map/ppermute | solution.py:353
  69.4 1.8 %shard_map.96 = (bf16[256,128]{1,0:T(8,128)(2,1)S(1)}, bf16[256,128]{1,0:T(8,128)(2,1)S(1)}, bf16[256,128]{1,0:T(8,128)(2,1)S(1)}, bf16[256,128]{1,0:T(8,128)(2,1)S(1)}) custom-call(bf16[256,128]{1,0:T(8,128)(2,1)S(1)} %get-tuple-element.56.refs_0_, bf16[256,128]{1,0:T(8,128)(2,1)S(1)} %collective-permute-done.15.refs_1_, ...), custom_call_target="tpu_custom_call" | custom-call | flops 1073741824 | bytes 5242880 | tf_op jit(solution)/shard_map/pallas_call | solution.py:37
  71.3 0.1 collective-permute-start.19
  71.3 3.1 %collective-permute-start.20 = (bf16[256,128]{1,0:T(8,128)(2,1)S(1)}, bf16[256,128]{1,0:T(8,128)(2,1)S(1)}, u32[]{:S(2)}, u32[]{:S(2)}) collective-permute-start(bf16[256,128]{1,0:T(8,128)(2,1)S(1)} %get-tuple-element.64), channel_id=1, source_target_pairs={{0,8},{1,9},{2,10},{3,11},{4,12},{5,13},{6,14},{7,15},{8,0},{9,1},... | collective-permute-start | bytes 196616 | tf_op jit(solution)/shard_map/ppermute | solution.py:353
  74.5 1.2 %collective-permute-start.21 = (bf16[256,128]{1,0:T(8,128)(2,1)S(1)}, bf16[256,128]{1,0:T(8,128)(2,1)S(1)}, u32[]{:S(2)}, u32[]{:S(2)}) collective-permute-start(bf16[256,128]{1,0:T(8,128)(2,1)S(1)} %get-tuple-element.65), channel_id=1, source_target_pairs={{0,12},{1,13},{2,14},{3,15},{4,8},{5,9},{6,10},{7,11},{8,4},{9,5},... | collective-permute-start | bytes 196616 | tf_op jit(solution)/shard_map/ppermute | solution.py:353
  75.7 1.0 collective-permute-done.20.e2
  76.7 3.8 %collective-permute-done.21.e3 = bf16[256,128]{1,0:T(8,128)(2,1)S(1)} collective-permute-done((bf16[256,128]{1,0:T(8,128)(2,1)S(1)}, bf16[256,128]{1,0:T(8,128)(2,1)S(1)}, u32[]{:S(2)}, u32[]{:S(2)}) %collective-permute-start.21) | collective-permute-done | bytes 65568 | tf_op jit(solution)/shard_map/ppermute | solution.py:353
  80.5 0.1 shard_map.98
  80.7 0.1 collective-permute-start.26
  80.8 0.2 shard_map.97.gated
  81.0 0.5 collective-permute-start.22
  81.5 1.5 %collective-permute-done.22.other = bf16[512,256]{1,0:T(8,128)(2,1)S(1)} collective-permute-done((bf16[512,256]{1,0:T(8,128)(2,1)S(1)}, bf16[512,256]{1,0:T(8,128)(2,1)S(1)}, u32[]{:S(2)}, u32[]{:S(2)}) %collective-permute-start.22) | collective-permute-done | bytes 262176 | tf_op jit(solution)/shard_map/ppermute | solution.py:353
  83.0 0.8 shard_map.100
  83.9 1.8 %collective-permute-start.27 = (bf16[128,1024]{1,0:T(8,128)(2,1)S(1)}, bf16[128,1024]{1,0:T(8,128)(2,1)S(1)}, u32[]{:S(2)}, u32[]{:S(2)}) collective-permute-start(bf16[128,1024]{1,0:T(8,128)(2,1)S(1)} %get-tuple-element.74), channel_id=1, source_target_pairs={{0,18},{1,19},{2,16},{3,17},{4,22},{5,23},{6,20},{7,21},{8,26},{9,... | collective-permute-start | bytes 786440 | tf_op jit(solution)/shard_map/ppermute | solution.py:353
  85.7 1.2 %collective-permute-start.28 = (bf16[128,1024]{1,0:T(8,128)(2,1)S(1)}, bf16[128,1024]{1,0:T(8,128)(2,1)S(1)}, u32[]{:S(2)}, u32[]{:S(2)}) collective-permute-start(bf16[128,1024]{1,0:T(8,128)(2,1)S(1)} %get-tuple-element.75), channel_id=1, source_target_pairs={{0,2},{1,3},{2,0},{3,1},{4,6},{5,7},{6,4},{7,5},{8,10},{9,11},{10,... | collective-permute-start | bytes 786440 | tf_op jit(solution)/shard_map/ppermute | solution.py:353
  86.9 0.8 shard_map.99
  87.7 0.6 collective-permute-start.29
  88.3 5.7 %collective-permute-done.27 = bf16[128,1024]{1,0:T(8,128)(2,1)S(1)} collective-permute-done((bf16[128,1024]{1,0:T(8,128)(2,1)S(1)}, bf16[128,1024]{1,0:T(8,128)(2,1)S(1)}, u32[]{:S(2)}, u32[]{:S(2)}) %collective-permute-start.27) | collective-permute-done | bytes 262176 | tf_op jit(solution)/shard_map/ppermute | solution.py:353
  94.0 4.9 %collective-permute-done.28 = bf16[128,1024]{1,0:T(8,128)(2,1)S(1)} collective-permute-done((bf16[128,1024]{1,0:T(8,128)(2,1)S(1)}, bf16[128,1024]{1,0:T(8,128)(2,1)S(1)}, u32[]{:S(2)}, u32[]{:S(2)}) %collective-permute-start.28) | collective-permute-done | bytes 262176 | tf_op jit(solution)/shard_map/ppermute | solution.py:353
  98.9 0.8 add_convert_fusion
  (34 shorter events, 0.1 us)
Async XLA Ops:
  0.0 1.0 %copy-start = (bf16[256,1024]{1,0:T(8,128)(2,1)S(1)}, bf16[256,1024]{1,0:T(8,128)(2,1)}, u32[]{:S(2)}) copy-start(bf16[256,1024]{1,0:T(8,128)(2,1)} %param.12) | copy-start | bytes 1572868
  1.1 3.1 %copy-start.2 = (bf16[256,512]{1,0:T(8,128)(2,1)}, bf16[256,512]{1,0:T(8,128)(2,1)S(1)}, u32[]{:S(2)}) copy-start(bf16[256,512]{1,0:T(8,128)(2,1)S(1)} %constant_dynamic-slice_fusion.after.w0) | copy-start | bytes 786436
  1.1 22.5 %copy-start.5 = (bf16[128,1024]{1,0:T(8,128)(2,1)S(1)}, bf16[128,1024]{1,0:T(8,128)(2,1)}, u32[]{:S(2)}) copy-start(bf16[128,1024]{1,0:T(8,128)(2,1)} %refs_0_.1) | copy-start | bytes 786436
  1.1 14.2 %collective-permute-start.2 = (bf16[256,512]{1,0:T(8,128)(2,1)S(1)}, bf16[256,512]{1,0:T(8,128)(2,1)S(1)}, u32[]{:S(2)}, u32[]{:S(2)}) collective-permute-start(bf16[256,512]{1,0:T(8,128)(2,1)S(1)} %constant_dynamic-slice_fusion.after.w0), channel_id=1, source_target_pairs={{0,4},{1,5},{2,6},{3,7},{4,8},{5,9},{6,10},{7,11},{8,12},{9,13},{1... | collective-permute-start | bytes 786440 | tf_op jit(solution)/shard_map/ppermute | solution.py:353
  6.8 8.6 %collective-permute-start.1 = (bf16[256,256]{1,0:T(8,128)(2,1)}, bf16[256,256]{1,0:T(8,128)(2,1)S(1)}, u32[]{:S(2)}, u32[]{:S(2)}) collective-permute-start(bf16[256,256]{1,0:T(8,128)(2,1)} %get-tuple-element.42.refs_0_), channel_id=1, source_target_pairs={{0,4},{1,5},{2,6},{3,7},{4,8},{5,9},{6,10},{7,11},{8,12},{9,13},{1... | collective-permute-start | bytes 393224 | tf_op jit(solution)/shard_map/ppermute | solution.py:353
  8.4 9.5 %collective-permute-start = (bf16[128,1024]{1,0:T(8,128)(2,1)}, bf16[128,1024]{1,0:T(8,128)(2,1)S(1)}, u32[]{:S(2)}, u32[]{:S(2)}) collective-permute-start(bf16[128,1024]{1,0:T(8,128)(2,1)} %get-tuple-element.41), channel_id=1, source_target_pairs={{0,2},{1,3},{2,0},{3,1},{4,6},{5,7},{6,4},{7,5},{8,10},{9,11},{10,... | collective-permute-start | bytes 786440 | tf_op jit(solution)/shard_map/ppermute | solution.py:353
  9.9 13.7 %collective-permute-start.4 = (bf16[128,1024]{1,0:T(8,128)(2,1)}, bf16[128,1024]{1,0:T(8,128)(2,1)S(1)}, u32[]{:S(2)}, u32[]{:S(2)}) collective-permute-start(bf16[128,1024]{1,0:T(8,128)(2,1)} %get-tuple-element.45), channel_id=1, source_target_pairs={{0,16},{1,17},{2,18},{3,19},{4,20},{5,21},{6,22},{7,23},{8,24},{9,... | collective-permute-start | bytes 786440 | tf_op jit(solution)/shard_map/ppermute | solution.py:353
  11.4 12.3 %copy-start.11 = (bf16[2,2,128,256]{3,2,1,0:T(8,128)(2,1)S(1)}, bf16[2,2,128,256]{3,2,1,0:T(8,128)(2,1)}, u32[]{:S(2)}) copy-start(bf16[2,2,128,256]{3,2,1,0:T(8,128)(2,1)} %get-tuple-element.47) | copy-start | bytes 786436
  11.4 16.0 %copy-start.12 = (bf16[256,256]{1,0:T(8,128)(2,1)S(1)}, bf16[256,256]{1,0:T(8,128)(2,1)}, u32[]{:S(2)}) copy-start(bf16[256,256]{1,0:T(8,128)(2,1)} %get-tuple-element.49) | copy-start | bytes 393220
  11.4 27.2 %copy-start.3 = (bf16[256,512]{1,0:T(8,128)(2,1)S(1)}, bf16[256,512]{1,0:T(8,128)(2,1)}, u32[]{:S(2)}) copy-start(bf16[256,512]{1,0:T(8,128)(2,1)} %copy-done.2) | copy-start | bytes 786436
  11.4 12.1 %collective-permute-start.5 = (bf16[128,1024]{1,0:T(8,128)(2,1)}, bf16[128,1024]{1,0:T(8,128)(2,1)S(1)}, u32[]{:S(2)}, u32[]{:S(2)}) collective-permute-start(bf16[128,1024]{1,0:T(8,128)(2,1)} %get-tuple-element.46), channel_id=1, source_target_pairs={{0,18},{1,19},{2,16},{3,17},{4,22},{5,23},{6,20},{7,21},{8,26},{9,... | collective-permute-start | bytes 786440 | tf_op jit(solution)/shard_map/ppermute | solution.py:353
  15.3 8.2 %collective-permute-start.3 = (bf16[256,256]{1,0:T(8,128)(2,1)S(1)}, bf16[256,256]{1,0:T(8,128)(2,1)S(1)}, u32[]{:S(2)}, u32[]{:S(2)}) collective-permute-start(bf16[256,256]{1,0:T(8,128)(2,1)S(1)} %collective-permute-done.1.refs_2_), channel_id=1, source_target_pairs={{0,4},{1,5},{2,6},{3,7},{4,8},{5,9},{6,10},{7,11},{8,12},{9,13},{1... | collective-permute-start | bytes 393224 | tf_op jit(solution)/shard_map/ppermute | solution.py:353
  15.3 12.1 %collective-permute-start.8 = (bf16[256,512]{1,0:T(8,128)(2,1)S(1)}, bf16[256,512]{1,0:T(8,128)(2,1)S(1)}, u32[]{:S(2)}, u32[]{:S(2)}) collective-permute-start(bf16[256,512]{1,0:T(8,128)(2,1)S(1)} %collective-permute-done.2.w1), channel_id=1, source_target_pairs={{0,4},{1,5},{2,6},{3,7},{4,8},{5,9},{6,10},{7,11},{8,12},{9,13},{1... | collective-permute-start | bytes 786440 | tf_op jit(solution)/shard_map/ppermute | solution.py:353
  23.6 15.0 %collective-permute-start.10 = (bf16[512,512]{1,0:T(8,128)(2,1)S(1)}, bf16[512,512]{1,0:T(8,128)(2,1)S(1)}, u32[]{:S(2)}, u32[]{:S(2)}) collective-permute-start(bf16[512,512]{1,0:T(8,128)(2,1)S(1)} %shard_map.92.mine), channel_id=1, source_target_pairs={{0,1},{1,0},{2,3},{3,2},{4,5},{5,4},{6,7},{7,6},{8,9},{9,8},{10,11... | collective-permute-start | bytes 1572872 | tf_op jit(solution)/shard_map/ppermute | solution.py:353
  23.7 9.2 %collective-permute-start.7 = (bf16[2,2,128,256]{3,2,1,0:T(8,128)(2,1)S(1)}, bf16[2,2,128,256]{3,2,1,0:T(8,128)(2,1)S(1)}, u32[]{:S(2)}, u32[]{:S(2)}) collective-permute-start(bf16[2,2,128,256]{3,2,1,0:T(8,128)(2,1)S(1)} %copy-done.11), channel_id=1, source_target_pairs={{0,2},{1,3},{2,0},{3,1},{4,6},{5,7},{6,4},{7,5},{8,10},{9,11},{10,... | collective-permute-start | bytes 786440 | tf_op jit(solution)/shard_map/ppermute | solution.py:353
  27.4 11.2 %collective-permute-start.11 = (bf16[256,512]{1,0:T(8,128)(2,1)S(1)}, bf16[256,512]{1,0:T(8,128)(2,1)S(1)}, u32[]{:S(2)}, u32[]{:S(2)}) collective-permute-start(bf16[256,512]{1,0:T(8,128)(2,1)S(1)} %collective-permute-done.8.w2), channel_id=1, source_target_pairs={{0,4},{1,5},{2,6},{3,7},{4,8},{5,9},{6,10},{7,11},{8,12},{9,13},{1... | collective-permute-start | bytes 786440 | tf_op jit(solution)/shard_map/ppermute | solution.py:353
  27.4 11.2 %collective-permute-start.6 = (bf16[256,256]{1,0:T(8,128)(2,1)S(1)}, bf16[256,256]{1,0:T(8,128)(2,1)S(1)}, u32[]{:S(2)}, u32[]{:S(2)}) collective-permute-start(bf16[256,256]{1,0:T(8,128)(2,1)S(1)} %collective-permute-done.3.refs_4_), channel_id=1, source_target_pairs={{0,4},{1,5},{2,6},{3,7},{4,8},{5,9},{6,10},{7,11},{8,12},{9,13},{1... | collective-permute-start | bytes 393224 | tf_op jit(solution)/shard_map/ppermute | solution.py:353
  27.4 13.6 %copy-start.1 = (bf16[2,2,128,1024]{3,2,1,0:T(8,128)(2,1)S(1)}, bf16[2,2,128,1024]{3,2,1,0:T(8,128)(2,1)}, u32[]{:S(2)}) copy-start(bf16[2,2,128,1024]{3,2,1,0:T(8,128)(2,1)} %filt.3) | copy-start | bytes 3145732
  27.4 11.2 %collective-permute-start.9 = (bf16[256,256]{1,0:T(8,128)(2,1)S(1)}, bf16[256,256]{1,0:T(8,128)(2,1)S(1)}, u32[]{:S(2)}, u32[]{:S(2)}) collective-permute-start(bf16[256,256]{1,0:T(8,128)(2,1)S(1)} %copy-done.12), channel_id=1, source_target_pairs={{0,2},{1,3},{2,0},{3,1},{4,6},{5,7},{6,4},{7,5},{8,10},{9,11},{10,... | collective-permute-start | bytes 393224 | tf_op jit(solution)/shard_map/ppermute | solution.py:353
  39.9 19.4 %copy-start.4 = (bf16[128,1024]{1,0:T(8,128)(2,1)S(1)}, bf16[128,1024]{1,0:T(8,128)(2,1)}, u32[]{:S(2)}) copy-start(bf16[128,1024]{1,0:T(8,128)(2,1)} %g0.2) | copy-start | bytes 786436
  39.9 19.4 %collective-permute-start.14 = (bf16[512,256]{1,0:T(8,128)(2,1)S(1)}, bf16[512,256]{1,0:T(8,128)(2,1)S(1)}, u32[]{:S(2)}, u32[]{:S(2)}) collective-permute-start(bf16[512,256]{1,0:T(8,128)(2,1)S(1)} %get-tuple-element.55), channel_id=1, source_target_pairs={{0,2},{1,3},{2,0},{3,1},{4,6},{5,7},{6,4},{7,5},{8,10},{9,11},{10,... | collective-permute-start | bytes 786440 | tf_op jit(solution)/shard_map/ppermute | solution.py:353
  41.0 7.0 %collective-permute-start.23 = (bf16[256,256]{1,0:T(8,128)(2,1)S(1)}, bf16[256,256]{1,0:T(8,128)(2,1)S(1)}, u32[]{:S(2)}, u32[]{:S(2)}) collective-permute-start(bf16[256,256]{1,0:T(8,128)(2,1)S(1)} %collective-permute-done.9.refs_1_), channel_id=1, source_target_pairs={{0,4},{1,5},{2,6},{3,7},{4,8},{5,9},{6,10},{7,11},{8,12},{9,13},{1... | collective-permute-start | bytes 393224 | tf_op jit(solution)/shard_map/ppermute | solution.py:353
  41.0 28.4 %copy-start.10 = (bf16[16,256,128]{2,1,0:T(8,128)(2,1)S(1)}, bf16[16,256,128]{2,1,0:T(8,128)(2,1)}, u32[]{:S(2)}) copy-start(bf16[16,256,128]{2,1,0:T(8,128)(2,1)} %constant.17.clone.refs_9_) | copy-start | bytes 3145732
  41.3 18.0 %copy-start.8 = (f32[1024]{0:T(1024)S(1)}, f32[1024]{0:T(1024)}, u32[]{:S(2)}) copy-start(f32[1024]{0:T(1024)} %param.13) | copy-start | bytes 12292
  41.3 28.1 %copy-start.9 = (bf16[16,256,128]{2,1,0:T(8,128)(2,1)S(1)}, bf16[16,256,128]{2,1,0:T(8,128)(2,1)}, u32[]{:S(2)}) copy-start(bf16[16,256,128]{2,1,0:T(8,128)(2,1)} %constant.16.clone.refs_8_) | copy-start | bytes 3145732
  41.3 10.5 %collective-permute-start.12 = (bf16[2,2,128,128]{3,2,1,0:T(8,128)(2,1)S(1)}, bf16[2,2,128,128]{3,2,1,0:T(8,128)(2,1)S(1)}, u32[]{:S(2)}, u32[]{:S(2)}) collective-permute-start(bf16[2,2,128,128]{3,2,1,0:T(8,128)(2,1)S(1)} %get-tuple-element.52), channel_id=1, source_target_pairs={{0,4},{1,5},{2,6},{3,7},{4,0},{5,1},{6,2},{7,3},{8,12},{9,13},{10,... | collective-permute-start | bytes 393224 | tf_op jit(solution)/shard_map/ppermute | solution.py:353
  41.4 17.9 %collective-permute-start.13 = (bf16[2,2,128,128]{3,2,1,0:T(8,128)(2,1)S(1)}, bf16[2,2,128,128]{3,2,1,0:T(8,128)(2,1)S(1)}, u32[]{:S(2)}, u32[]{:S(2)}) collective-permute-start(bf16[2,2,128,128]{3,2,1,0:T(8,128)(2,1)S(1)} %get-tuple-element.53), channel_id=1, source_target_pairs={{0,8},{1,9},{2,10},{3,11},{4,12},{5,13},{6,14},{7,15},{8,0},{9,1},... | collective-permute-start | bytes 393224 | tf_op jit(solution)/shard_map/ppermute | solution.py:353
  48.0 16.1 %collective-permute-start.24 = (bf16[256,256]{1,0:T(8,128)(2,1)S(1)}, bf16[256,256]{1,0:T(8,128)(2,1)S(1)}, u32[]{:S(2)}, u32[]{:S(2)}) collective-permute-start(bf16[256,256]{1,0:T(8,128)(2,1)S(1)} %collective-permute-done.23.refs_3_), channel_id=1, source_target_pairs={{0,4},{1,5},{2,6},{3,7},{4,8},{5,9},{6,10},{7,11},{8,12},{9,13},{1... | collective-permute-start | bytes 393224 | tf_op jit(solution)/shard_map/ppermute | solution.py:353
  48.0 21.4 %collective-permute-start.18 = (bf16[2,2,128,128]{3,2,1,0:T(8,128)(2,1)S(1)}, bf16[2,2,128,128]{3,2,1,0:T(8,128)(2,1)S(1)}, u32[]{:S(2)}, u32[]{:S(2)}) collective-permute-start(bf16[2,2,128,128]{3,2,1,0:T(8,128)(2,1)S(1)} %get-tuple-element.61), channel_id=1, source_target_pairs={{0,12},{1,13},{2,14},{3,15},{4,8},{5,9},{6,10},{7,11},{8,4},{9,5},... | collective-permute-start | bytes 393224 | tf_op jit(solution)/shard_map/ppermute | solution.py:353
  59.7 4.5 %collective-permute-start.15 = (bf16[256,128]{1,0:T(8,128)(2,1)S(1)}, bf16[256,128]{1,0:T(8,128)(2,1)S(1)}, u32[]{:S(2)}, u32[]{:S(2)}) collective-permute-start(bf16[256,128]{1,0:T(8,128)(2,1)S(1)} %get-tuple-element.57), channel_id=1, source_target_pairs={{0,4},{1,5},{2,6},{3,7},{4,0},{5,1},{6,2},{7,3},{8,12},{9,13},{10,... | collective-permute-start | bytes 196616 | tf_op jit(solution)/shard_map/ppermute | solution.py:353
  59.7 7.5 %collective-permute-start.16 = (bf16[256,128]{1,0:T(8,128)(2,1)S(1)}, bf16[256,128]{1,0:T(8,128)(2,1)S(1)}, u32[]{:S(2)}, u32[]{:S(2)}) collective-permute-start(bf16[256,128]{1,0:T(8,128)(2,1)S(1)} %get-tuple-element.58), channel_id=1, source_target_pairs={{0,8},{1,9},{2,10},{3,11},{4,12},{5,13},{6,14},{7,15},{8,0},{9,1},... | collective-permute-start | bytes 196616 | tf_op jit(solution)/shard_map/ppermute | solution.py:353
  59.8 8.4 %collective-permute-start.17 = (bf16[256,128]{1,0:T(8,128)(2,1)S(1)}, bf16[256,128]{1,0:T(8,128)(2,1)S(1)}, u32[]{:S(2)}, u32[]{:S(2)}) collective-permute-start(bf16[256,128]{1,0:T(8,128)(2,1)S(1)} %get-tuple-element.59), channel_id=1, source_target_pairs={{0,12},{1,13},{2,14},{3,15},{4,8},{5,9},{6,10},{7,11},{8,4},{9,5},... | collective-permute-start | bytes 196616 | tf_op jit(solution)/shard_map/ppermute | solution.py:353
  68.2 12.4 %collective-permute-start.25 = (bf16[256,256]{1,0:T(8,128)(2,1)S(1)}, bf16[256,256]{1,0:T(8,128)(2,1)S(1)}, u32[]{:S(2)}, u32[]{:S(2)}) collective-permute-start(bf16[256,256]{1,0:T(8,128)(2,1)S(1)} %collective-permute-done.24.refs_5_), channel_id=1, source_target_pairs={{0,4},{1,5},{2,6},{3,7},{4,8},{5,9},{6,10},{7,11},{8,12},{9,13},{1... | collective-permute-start | bytes 393224 | tf_op jit(solution)/shard_map/ppermute | solution.py:353
  69.4 11.1 %copy-start.7 = (bf16[256,256]{1,0:T(8,128)(2,1)S(1)}, bf16[256,256]{1,0:T(8,128)(2,1)}, u32[]{:S(2)}) copy-start(bf16[256,256]{1,0:T(8,128)(2,1)} %get-tuple-element.42.refs_0_) | copy-start | bytes 393220
  71.3 4.5 %collective-permute-start.19 = (bf16[256,128]{1,0:T(8,128)(2,1)S(1)}, bf16[256,128]{1,0:T(8,128)(2,1)S(1)}, u32[]{:S(2)}, u32[]{:S(2)}) collective-permute-start(bf16[256,128]{1,0:T(8,128)(2,1)S(1)} %get-tuple-element.63), channel_id=1, source_target_pairs={{0,4},{1,5},{2,6},{3,7},{4,0},{5,1},{6,2},{7,3},{8,12},{9,13},{10,... | collective-permute-start | bytes 196616 | tf_op jit(solution)/shard_map/ppermute | solution.py:353
  71.3 5.4 %collective-permute-start.20 = (bf16[256,128]{1,0:T(8,128)(2,1)S(1)}, bf16[256,128]{1,0:T(8,128)(2,1)S(1)}, u32[]{:S(2)}, u32[]{:S(2)}) collective-permute-start(bf16[256,128]{1,0:T(8,128)(2,1)S(1)} %get-tuple-element.64), channel_id=1, source_target_pairs={{0,8},{1,9},{2,10},{3,11},{4,12},{5,13},{6,14},{7,15},{8,0},{9,1},... | collective-permute-start | bytes 196616 | tf_op jit(solution)/shard_map/ppermute | solution.py:353
  74.5 6.3 %copy-start.6 = (bf16[128,1024]{1,0:T(8,128)(2,1)S(1)}, bf16[128,1024]{1,0:T(8,128)(2,1)}, u32[]{:S(2)}) copy-start(bf16[128,1024]{1,0:T(8,128)(2,1)} %g0.3) | copy-start | bytes 786436
  74.5 6.1 %collective-permute-start.21 = (bf16[256,128]{1,0:T(8,128)(2,1)S(1)}, bf16[256,128]{1,0:T(8,128)(2,1)S(1)}, u32[]{:S(2)}, u32[]{:S(2)}) collective-permute-start(bf16[256,128]{1,0:T(8,128)(2,1)S(1)} %get-tuple-element.65), channel_id=1, source_target_pairs={{0,12},{1,13},{2,14},{3,15},{4,8},{5,9},{6,10},{7,11},{8,4},{9,5},... | collective-permute-start | bytes 196616 | tf_op jit(solution)/shard_map/ppermute | solution.py:353
  80.7 2.4 %collective-permute-start.26 = (bf16[4,256,256]{2,1,0:T(8,128)(2,1)S(1)}, bf16[4,256,256]{2,1,0:T(8,128)(2,1)S(1)}, u32[]{:S(2)}, u32[]{:S(2)}) collective-permute-start(bf16[4,256,256]{2,1,0:T(8,128)(2,1)S(1)} %get-tuple-element.72), channel_id=1, source_target_pairs={{0,1},{1,0},{2,3},{3,2},{4,5},{5,4},{6,7},{7,6},{8,9},{9,8},{10,11... | collective-permute-start | bytes 1572872 | tf_op jit(solution)/shard_map/ppermute | solution.py:353
  81.0 2.0 %collective-permute-start.22 = (bf16[512,256]{1,0:T(8,128)(2,1)S(1)}, bf16[512,256]{1,0:T(8,128)(2,1)S(1)}, u32[]{:S(2)}, u32[]{:S(2)}) collective-permute-start(bf16[512,256]{1,0:T(8,128)(2,1)S(1)} %shard_map.97.gated), channel_id=1, source_target_pairs={{0,1},{1,0},{2,3},{3,2},{4,5},{5,4},{6,7},{7,6},{8,9},{9,8},{10,11... | collective-permute-start | bytes 786440 | tf_op jit(solution)/shard_map/ppermute | solution.py:353
  83.9 10.2 %collective-permute-start.27 = (bf16[128,1024]{1,0:T(8,128)(2,1)S(1)}, bf16[128,1024]{1,0:T(8,128)(2,1)S(1)}, u32[]{:S(2)}, u32[]{:S(2)}) collective-permute-start(bf16[128,1024]{1,0:T(8,128)(2,1)S(1)} %get-tuple-element.74), channel_id=1, source_target_pairs={{0,18},{1,19},{2,16},{3,17},{4,22},{5,23},{6,20},{7,21},{8,26},{9,... | collective-permute-start | bytes 786440 | tf_op jit(solution)/shard_map/ppermute | solution.py:353
  85.7 13.2 %collective-permute-start.28 = (bf16[128,1024]{1,0:T(8,128)(2,1)S(1)}, bf16[128,1024]{1,0:T(8,128)(2,1)S(1)}, u32[]{:S(2)}, u32[]{:S(2)}) collective-permute-start(bf16[128,1024]{1,0:T(8,128)(2,1)S(1)} %get-tuple-element.75), channel_id=1, source_target_pairs={{0,2},{1,3},{2,0},{3,1},{4,6},{5,7},{6,4},{7,5},{8,10},{9,11},{10,... | collective-permute-start | bytes 786440 | tf_op jit(solution)/shard_map/ppermute | solution.py:353
  87.7 11.2 %collective-permute-start.29 = (bf16[128,1024]{1,0:T(8,128)(2,1)S(1)}, bf16[128,1024]{1,0:T(8,128)(2,1)S(1)}, u32[]{:S(2)}, u32[]{:S(2)}) collective-permute-start(bf16[128,1024]{1,0:T(8,128)(2,1)S(1)} %get-tuple-element.76), channel_id=1, source_target_pairs={{0,16},{1,17},{2,18},{3,19},{4,20},{5,21},{6,22},{7,23},{8,24},{9,... | collective-permute-start | bytes 786440 | tf_op jit(solution)/shard_map/ppermute | solution.py:353

commit v12 on v10

--- a/solution.py
+++ b/solution.py
@@ -390,25 +390,25 @@
     mine = in_vmem(join_tokens, shape((512, 512), BF16), moved=1 << 20)(tokens, after(received[0], q2), *received[1:])
     v3 = to_z(v2, 1)
     other = to_core(mine)
-    got_o = to_x(after(away_o, v2))
-    r1 = to_z(after(got_o, v3), 1)
+    got_o = to_x(after(away_o, v1))
+    r1 = to_z(after(got_o, v2), 1)
     keep, give = in_vmem(
         value_kernel,
         [shape((512, 256), F32), shape((512, 256), BF16)],
         [pltpu.VMEM((512, 512), F32)],
         flops=1 << 29,
         moved=2 << 20,
-    )(after(mine, filters[1], got_o), other, own_v, v1, v2, v3)
+    )(after(mine, r1, near), other, own_v, v1, v2, v3)
     r2 = to_z(after(r1, keep), 1)
     drive, *sends = in_vmem(
         drive_kernel,
         [shape((512, 256), F32)] + [block] * 4,
         [pltpu.VMEM((512, 256), BF16), pltpu.VMEM((4, 256, 128), BF16)],
         moved=2 << 20,
-    )(after(keep, filters[1], filters[2]), to_x(give), gate_k, *received, skip[None, :])
+    )(after(keep, filters[1]), to_x(give), gate_k, *received, skip[None, :])
     columns = [sends[0]] + [to_z(sends[r], r) for r in (1, 2, 3)]
-    q3 = to_z(after(q2, columns[1]), 1)
-    r3 = to_z(after(r2, *columns[1:]), 1)
+    r3 = to_z(after(r2, *filters[2:], columns[1]), 1)
+    q3 = to_z(after(q2, *columns[1:]), 1)
     table, table_t = tables()
     sends = in_vmem(
         conv_kernel,

time: 99.3 us -> 94.5 us (0.952)
  starting transfers between devices: 39.2 us -> 36.5 us
  waiting for transfers between devices: 49.4 us -> 47.3 us
    ppermute x30, starting transfers between devices: 39.2 us -> 36.5 us  [permute(): return lax.ppermute(values, AXES, pairs)]
    ppermute x30, waiting for transfers between devices: 49.4 us -> 47.3 us  [permute(): return lax.ppermute(values, AXES, pairs)]
  transfers between devices with their start and end apart: 30 -> 30, of which waited for: 16 -> 17; matrix products, arithmetic and copies ran while one was open for 0% -> 0% of each run, Pallas kernels for 6% -> 6%
where the time goes in v12:
time: 94.5 us; the launch traced here: 94.3 us
  waiting for transfers between devices  47.3 us (50%)
  starting transfers between devices  36.5 us (39%)
  Pallas kernels  8.37 us (9%)
  local copies, waits for them, and re-layouts  1.12 us (1%)
    ppermute x30, waiting for transfers between devices, permute(): return lax.ppermute(values, AXES, pairs)  47.3 us
    ppermute x30, starting transfers between devices, permute(): return lax.ppermute(values, AXES, pairs)  36.5 us
    pallas_call x9, Pallas kernels, call(): pl.pallas_call(kernel, out_shape=out_shape, in_specs=specs, out_specs=jax...  5.79 us
    pallas_call x1, Pallas kernels, call(): pl.pallas_call(kernel, out_shape=out_shape, in_specs=[pl.BlockSpec(memory...  2.58 us
  transfers between devices with their start and end apart: 30, of which 17 were waited for; matrix products, arithmetic and copies ran while one was open for 0% of the time, Pallas kernels for 6%

profile of v12, /device:TPU:0, one launch (start us, length us, event | category | flops | bytes accessed | tf_op | source)
XLA Modules:
  0.0 94.3 jit_solution(16016293755628176648)
XLA Ops:
  0.0 1.0 %copy-done = bf16[256,1024]{1,0:T(8,128)(2,1)S(1)} copy-done((bf16[256,1024]{1,0:T(8,128)(2,1)S(1)}, bf16[256,1024]{1,0:T(8,128)(2,1)}, u32[]{:S(2)}) %copy-start) | copy-done | bytes 524312
  1.1 0.0 copy-start.2
  1.1 0.0 copy-start.5
  1.1 3.1 %collective-permute-start.2 = (bf16[256,512]{1,0:T(8,128)(2,1)S(1)}, bf16[256,512]{1,0:T(8,128)(2,1)S(1)}, u32[]{:S(2)}, u32[]{:S(2)}) collective-permute-start(bf16[256,512]{1,0:T(8,128)(2,1)S(1)} %constant_dynamic-slice_fusion.after.w0), channel_id=1, source_target_pairs={{0,4},{1,5},{2,6},{3,7},{4,8},{5,9},{6,10},{7,11},{8,12},{9,13},{1... | collective-permute-start | bytes 786440 | tf_op jit(solution)/shard_map/ppermute | solution.py:353
  4.2 2.6 %shard_map.91 = (bf16[128,1024]{1,0:T(8,128)(2,1)}, bf16[128,1024]{1,0:T(8,128)(2,1)}, bf16[128,1024]{1,0:T(8,128)(2,1)}, bf16[256,256]{1,0:T(8,128)(2,1)}, bf16...) custom-call(bf16[128,1024]{1,0:T(8,128)(2,1)} %refs_0_.1, bf16[128,1024]{1,0:T(8,128)(2,1)} %g0.2, ...), custom_call_target="tpu_custom_call" | custom-call | tf_op jit(solution)/shard_map/pallas_call | solution.py:101
  6.8 1.6 %collective-permute-start.1 = (bf16[256,256]{1,0:T(8,128)(2,1)}, bf16[256,256]{1,0:T(8,128)(2,1)S(1)}, u32[]{:S(2)}, u32[]{:S(2)}) collective-permute-start(bf16[256,256]{1,0:T(8,128)(2,1)} %get-tuple-element.43.refs_0_), channel_id=1, source_target_pairs={{0,4},{1,5},{2,6},{3,7},{4,8},{5,9},{6,10},{7,11},{8,12},{9,13},{1... | collective-permute-start | bytes 393224 | tf_op jit(solution)/shard_map/ppermute | solution.py:353
  8.4 1.5 %collective-permute-start = (bf16[128,1024]{1,0:T(8,128)(2,1)}, bf16[128,1024]{1,0:T(8,128)(2,1)S(1)}, u32[]{:S(2)}, u32[]{:S(2)}) collective-permute-start(bf16[128,1024]{1,0:T(8,128)(2,1)} %get-tuple-element.42), channel_id=1, source_target_pairs={{0,2},{1,3},{2,0},{3,1},{4,6},{5,7},{6,4},{7,5},{8,10},{9,11},{10,... | collective-permute-start | bytes 786440 | tf_op jit(solution)/shard_map/ppermute | solution.py:353
  9.9 1.5 %collective-permute-start.4 = (bf16[128,1024]{1,0:T(8,128)(2,1)}, bf16[128,1024]{1,0:T(8,128)(2,1)S(1)}, u32[]{:S(2)}, u32[]{:S(2)}) collective-permute-start(bf16[128,1024]{1,0:T(8,128)(2,1)} %get-tuple-element.46), channel_id=1, source_target_pairs={{0,16},{1,17},{2,18},{3,19},{4,20},{5,21},{6,22},{7,23},{8,24},{9,... | collective-permute-start | bytes 786440 | tf_op jit(solution)/shard_map/ppermute | solution.py:353
  11.4 0.5 collective-permute-start.5
  11.9 3.4 %collective-permute-done.1.refs_2_ = bf16[256,256]{1,0:T(8,128)(2,1)S(1)} collective-permute-done((bf16[256,256]{1,0:T(8,128)(2,1)}, bf16[256,256]{1,0:T(8,128)(2,1)S(1)}, u32[]{:S(2)}, u32[]{:S(2)}) %collective-permute-start.1) | collective-permute-done | bytes 131104 | tf_op jit(solution)/shard_map/ppermute | solution.py:353
  15.3 0.0 collective-permute-done.2.w1
  15.3 0.0 collective-permute-start.3
  15.3 1.3 %collective-permute-start.7 = (bf16[256,512]{1,0:T(8,128)(2,1)S(1)}, bf16[256,512]{1,0:T(8,128)(2,1)S(1)}, u32[]{:S(2)}, u32[]{:S(2)}) collective-permute-start(bf16[256,512]{1,0:T(8,128)(2,1)S(1)} %collective-permute-done.2.w1), channel_id=1, source_target_pairs={{0,4},{1,5},{2,6},{3,7},{4,8},{5,9},{6,10},{7,11},{8,12},{9,13},{1... | collective-permute-start | bytes 786440 | tf_op jit(solution)/shard_map/ppermute | solution.py:353
  16.6 1.2 %collective-permute-done.refs_1_.g1 = bf16[128,1024]{1,0:T(8,128)(2,1)S(1)} collective-permute-done((bf16[128,1024]{1,0:T(8,128)(2,1)}, bf16[128,1024]{1,0:T(8,128)(2,1)S(1)}, u32[]{:S(2)}, u32[]{:S(2)}) %collective-permute-start) | collective-permute-done | bytes 262176 | tf_op jit(solution)/shard_map/ppermute | solution.py:353
  17.8 5.7 %collective-permute-done.3.refs_4_ = bf16[256,256]{1,0:T(8,128)(2,1)S(1)} collective-permute-done((bf16[256,256]{1,0:T(8,128)(2,1)S(1)}, bf16[256,256]{1,0:T(8,128)(2,1)S(1)}, u32[]{:S(2)}, u32[]{:S(2)}) %collective-permute-start.3) | collective-permute-done | bytes 131104 | tf_op jit(solution)/shard_map/ppermute | solution.py:353
  23.5 0.0 collective-permute-done.4.refs_2_.g2
  23.6 0.1 collective-permute-start.10
  23.7 1.6 %collective-permute-start.6 = (bf16[256,256]{1,0:T(8,128)(2,1)S(1)}, bf16[256,256]{1,0:T(8,128)(2,1)S(1)}, u32[]{:S(2)}, u32[]{:S(2)}) collective-permute-start(bf16[256,256]{1,0:T(8,128)(2,1)S(1)} %copy-done.12), channel_id=1, source_target_pairs={{0,2},{1,3},{2,0},{3,1},{4,6},{5,7},{6,4},{7,5},{8,10},{9,11},{10,... | collective-permute-start | bytes 393224 | tf_op jit(solution)/shard_map/ppermute | solution.py:353
  25.3 0.5 collective-permute-start.9
  25.8 1.6 %collective-permute-done.7.w2 = bf16[256,512]{1,0:T(8,128)(2,1)S(1)} collective-permute-done((bf16[256,512]{1,0:T(8,128)(2,1)S(1)}, bf16[256,512]{1,0:T(8,128)(2,1)S(1)}, u32[]{:S(2)}, u32[]{:S(2)}) %collective-permute-start.7) | collective-permute-done | bytes 262176 | tf_op jit(solution)/shard_map/ppermute | solution.py:353
  27.4 2.6 %collective-permute-done.6.refs_1_ = bf16[256,256]{1,0:T(8,128)(2,1)S(1)} collective-permute-done((bf16[256,256]{1,0:T(8,128)(2,1)S(1)}, bf16[256,256]{1,0:T(8,128)(2,1)S(1)}, u32[]{:S(2)}, u32[]{:S(2)}) %collective-permute-start.6) | collective-permute-done | bytes 131104 | tf_op jit(solution)/shard_map/ppermute | solution.py:353
  30.1 0.9 collective-permute-start.8
  31.0 4.2 %collective-permute-done.9.near = bf16[2,2,128,256]{3,2,1,0:T(8,128)(2,1)S(1)} collective-permute-done((bf16[2,2,128,256]{3,2,1,0:T(8,128)(2,1)S(1)}, bf16[2,2,128,256]{3,2,1,0:T(8,128)(2,1)S(1)}, u32[]{:S(2)}, u32[]{:S(2)}) %collective-permute-start.9) | collective-permute-done | bytes 262176 | tf_op jit(solution)/shard_map/ppermute | solution.py:353
  35.2 3.4 %collective-permute-done.8.refs_3_ = bf16[256,256]{1,0:T(8,128)(2,1)S(1)} collective-permute-done((bf16[256,256]{1,0:T(8,128)(2,1)S(1)}, bf16[256,256]{1,0:T(8,128)(2,1)S(1)}, u32[]{:S(2)}, u32[]{:S(2)}) %collective-permute-start.8) | collective-permute-done | bytes 131104 | tf_op jit(solution)/shard_map/ppermute | solution.py:353
  38.6 1.3 %shard_map.93 = (f32[512,256]{1,0:T(8,128)S(1)}, bf16[512,256]{1,0:T(8,128)(2,1)S(1)}) custom-call(bf16[512,512]{1,0:T(8,128)(2,1)S(1)} %shard_map.92.mine, bf16[512,512]{1,0:T(8,128)(2,1)S(1)} %collective-permute-done.10.other, bf16[256,512]{1,0:T(8,128)(2,1)S(1)} %copy-done.3, bf16[256,512]{1,0:T(8,128)(2,1)S(1)} %collective-permute-done.2.w1, ...), custom_call_target="tpu_custom_call" | custom-call | flops 536870912 | bytes 2097152 | tf_op jit(solution)/shard_map/pallas_call | solution.py:37
  39.9 0.0 copy-start.4
  39.9 1.5 %collective-permute-start.13 = (bf16[512,256]{1,0:T(8,128)(2,1)S(1)}, bf16[512,256]{1,0:T(8,128)(2,1)S(1)}, u32[]{:S(2)}, u32[]{:S(2)}) collective-permute-start(bf16[512,256]{1,0:T(8,128)(2,1)S(1)} %get-tuple-element.56), channel_id=1, source_target_pairs={{0,2},{1,3},{2,0},{3,1},{4,6},{5,7},{6,4},{7,5},{8,10},{9,11},{10,... | collective-permute-start | bytes 786440 | tf_op jit(solution)/shard_map/ppermute | solution.py:353
  41.4 0.3 shard_map.94
  41.7 0.0 copy-start.8
  41.7 0.0 copy-start.9
  41.7 0.1 collective-permute-start.12
  41.8 0.1 collective-permute-start.17
  41.9 3.7 %collective-permute-start.18 = (bf16[2,2,128,128]{3,2,1,0:T(8,128)(2,1)S(1)}, bf16[2,2,128,128]{3,2,1,0:T(8,128)(2,1)S(1)}, u32[]{:S(2)}, u32[]{:S(2)}) collective-permute-start(bf16[2,2,128,128]{3,2,1,0:T(8,128)(2,1)S(1)} %get-tuple-element.63), channel_id=1, source_target_pairs={{0,12},{1,13},{2,14},{3,15},{4,0},{5,1},{6,2},{7,3},{8,4},{9,5},{1... | collective-permute-start | bytes 393224 | tf_op jit(solution)/shard_map/ppermute | solution.py:353
  45.6 0.6 collective-permute-start.23
  46.1 3.9 %collective-permute-done.12.refs_5_ = bf16[2,2,128,128]{3,2,1,0:T(8,128)(2,1)S(1)} collective-permute-done((bf16[2,2,128,128]{3,2,1,0:T(8,128)(2,1)S(1)}, bf16[2,2,128,128]{3,2,1,0:T(8,128)(2,1)S(1)}, u32[]{:S(2)}, u32[]{:S(2)}) %collective-permute-start.12) | collective-permute-done | bytes 131104 | tf_op jit(solution)/shard_map/ppermute | solution.py:353
  50.1 0.3 shard_map.95
  50.4 0.1 collective-permute-start.14
  50.5 1.0 %collective-permute-start.15 = (bf16[256,128]{1,0:T(8,128)(2,1)S(1)}, bf16[256,128]{1,0:T(8,128)(2,1)S(1)}, u32[]{:S(2)}, u32[]{:S(2)}) collective-permute-start(bf16[256,128]{1,0:T(8,128)(2,1)S(1)} %get-tuple-element.59), channel_id=1, source_target_pairs={{0,8},{1,9},{2,10},{3,11},{4,12},{5,13},{6,14},{7,15},{8,0},{9,1},... | collective-permute-start | bytes 196616 | tf_op jit(solution)/shard_map/ppermute | solution.py:353
  51.5 3.9 %collective-permute-done.17.refs_6_ = bf16[2,2,128,128]{3,2,1,0:T(8,128)(2,1)S(1)} collective-permute-done((bf16[2,2,128,128]{3,2,1,0:T(8,128)(2,1)S(1)}, bf16[2,2,128,128]{3,2,1,0:T(8,128)(2,1)S(1)}, u32[]{:S(2)}, u32[]{:S(2)}) %collective-permute-start.17) | collective-permute-done | bytes 131104 | tf_op jit(solution)/shard_map/ppermute | solution.py:353
  55.4 1.7 %collective-permute-start.16 = (bf16[256,128]{1,0:T(8,128)(2,1)S(1)}, bf16[256,128]{1,0:T(8,128)(2,1)S(1)}, u32[]{:S(2)}, u32[]{:S(2)}) collective-permute-start(bf16[256,128]{1,0:T(8,128)(2,1)S(1)} %get-tuple-element.60), channel_id=1, source_target_pairs={{0,12},{1,13},{2,14},{3,15},{4,0},{5,1},{6,2},{7,3},{8,4},{9,5},{1... | collective-permute-start | bytes 196616 | tf_op jit(solution)/shard_map/ppermute | solution.py:353
  57.1 0.4 collective-permute-done.23.refs_5_
  57.5 1.0 %collective-permute-done.14.refs_1_ = bf16[256,128]{1,0:T(8,128)(2,1)S(1)} collective-permute-done((bf16[256,128]{1,0:T(8,128)(2,1)S(1)}, bf16[256,128]{1,0:T(8,128)(2,1)S(1)}, u32[]{:S(2)}, u32[]{:S(2)}) %collective-permute-start.14) | collective-permute-done | bytes 65568 | tf_op jit(solution)/shard_map/ppermute | solution.py:353
  58.5 4.5 %collective-permute-start.25 = (bf16[256,256]{1,0:T(8,128)(2,1)S(1)}, bf16[256,256]{1,0:T(8,128)(2,1)S(1)}, u32[]{:S(2)}, u32[]{:S(2)}) collective-permute-start(bf16[256,256]{1,0:T(8,128)(2,1)S(1)} %collective-permute-done.23.refs_5_), channel_id=1, source_target_pairs={{0,4},{1,5},{2,6},{3,7},{4,8},{5,9},{6,10},{7,11},{8,12},{9,13},{1... | collective-permute-start | bytes 393224 | tf_op jit(solution)/shard_map/ppermute | solution.py:353
  63.0 0.6 collective-permute-done.15.refs_2_
  63.5 2.7 %collective-permute-start.24 = (bf16[256,256]{1,0:T(8,128)(2,1)S(1)}, bf16[256,256]{1,0:T(8,128)(2,1)S(1)}, u32[]{:S(2)}, u32[]{:S(2)}) collective-permute-start(bf16[256,256]{1,0:T(8,128)(2,1)S(1)} %collective-permute-done.3.refs_4_), channel_id=1, source_target_pairs={{0,4},{1,5},{2,6},{3,7},{4,8},{5,9},{6,10},{7,11},{8,12},{9,13},{1... | collective-permute-start | bytes 393224 | tf_op jit(solution)/shard_map/ppermute | solution.py:353
  66.2 1.8 %shard_map.96 = (bf16[256,128]{1,0:T(8,128)(2,1)S(1)}, bf16[256,128]{1,0:T(8,128)(2,1)S(1)}, bf16[256,128]{1,0:T(8,128)(2,1)S(1)}, bf16[256,128]{1,0:T(8,128)(2,1)S(1)}) custom-call(bf16[256,128]{1,0:T(8,128)(2,1)S(1)} %get-tuple-element.57.refs_0_, bf16[256,128]{1,0:T(8,128)(2,1)S(1)} %collective-permute-done.14.refs_1_, ...), custom_call_target="tpu_custom_call" | custom-call | flops 1073741824 | bytes 5242880 | tf_op jit(solution)/shard_map/pallas_call | solution.py:37
  68.0 0.1 collective-permute-start.19
  68.1 1.7 %collective-permute-start.20 = (bf16[256,128]{1,0:T(8,128)(2,1)S(1)}, bf16[256,128]{1,0:T(8,128)(2,1)S(1)}, u32[]{:S(2)}, u32[]{:S(2)}) collective-permute-start(bf16[256,128]{1,0:T(8,128)(2,1)S(1)} %get-tuple-element.66), channel_id=1, source_target_pairs={{0,8},{1,9},{2,10},{3,11},{4,12},{5,13},{6,14},{7,15},{8,0},{9,1},... | collective-permute-start | bytes 196616 | tf_op jit(solution)/shard_map/ppermute | solution.py:353
  69.8 2.1 %collective-permute-start.21 = (bf16[256,128]{1,0:T(8,128)(2,1)S(1)}, bf16[256,128]{1,0:T(8,128)(2,1)S(1)}, u32[]{:S(2)}, u32[]{:S(2)}) collective-permute-start(bf16[256,128]{1,0:T(8,128)(2,1)S(1)} %get-tuple-element.67), channel_id=1, source_target_pairs={{0,12},{1,13},{2,14},{3,15},{4,0},{5,1},{6,2},{7,3},{8,4},{9,5},{1... | collective-permute-start | bytes 196616 | tf_op jit(solution)/shard_map/ppermute | solution.py:353
  71.9 2.4 %collective-permute-done.19.e1 = bf16[256,128]{1,0:T(8,128)(2,1)S(1)} collective-permute-done((bf16[256,128]{1,0:T(8,128)(2,1)S(1)}, bf16[256,128]{1,0:T(8,128)(2,1)S(1)}, u32[]{:S(2)}, u32[]{:S(2)}) %collective-permute-start.19) | collective-permute-done | bytes 65568 | tf_op jit(solution)/shard_map/ppermute | solution.py:353
  74.2 0.9 collective-permute-done.20.e2
  75.1 0.2 shard_map.98
  75.3 0.1 collective-permute-start.26
  75.4 0.2 shard_map.97.gated
  75.6 0.5 collective-permute-start.22
  76.2 1.5 %collective-permute-done.22.other = bf16[512,256]{1,0:T(8,128)(2,1)S(1)} collective-permute-done((bf16[512,256]{1,0:T(8,128)(2,1)S(1)}, bf16[512,256]{1,0:T(8,128)(2,1)S(1)}, u32[]{:S(2)}, u32[]{:S(2)}) %collective-permute-start.22) | collective-permute-done | bytes 262176 | tf_op jit(solution)/shard_map/ppermute | solution.py:353
  77.7 0.8 shard_map.100
  78.5 1.6 %collective-permute-start.27 = (bf16[128,1024]{1,0:T(8,128)(2,1)S(1)}, bf16[128,1024]{1,0:T(8,128)(2,1)S(1)}, u32[]{:S(2)}, u32[]{:S(2)}) collective-permute-start(bf16[128,1024]{1,0:T(8,128)(2,1)S(1)} %get-tuple-element.76), channel_id=1, source_target_pairs={{0,18},{1,19},{2,16},{3,17},{4,22},{5,23},{6,20},{7,21},{8,26},{9,... | collective-permute-start | bytes 786440 | tf_op jit(solution)/shard_map/ppermute | solution.py:353
  80.0 1.5 %collective-permute-start.28 = (bf16[128,1024]{1,0:T(8,128)(2,1)S(1)}, bf16[128,1024]{1,0:T(8,128)(2,1)S(1)}, u32[]{:S(2)}, u32[]{:S(2)}) collective-permute-start(bf16[128,1024]{1,0:T(8,128)(2,1)S(1)} %get-tuple-element.77), channel_id=1, source_target_pairs={{0,2},{1,3},{2,0},{3,1},{4,6},{5,7},{6,4},{7,5},{8,10},{9,11},{10,... | collective-permute-start | bytes 786440 | tf_op jit(solution)/shard_map/ppermute | solution.py:353
  81.5 0.8 shard_map.99
  82.3 0.6 collective-permute-start.29
  82.9 5.7 %collective-permute-done.27 = bf16[128,1024]{1,0:T(8,128)(2,1)S(1)} collective-permute-done((bf16[128,1024]{1,0:T(8,128)(2,1)S(1)}, bf16[128,1024]{1,0:T(8,128)(2,1)S(1)}, u32[]{:S(2)}, u32[]{:S(2)}) %collective-permute-start.27) | collective-permute-done | bytes 262176 | tf_op jit(solution)/shard_map/ppermute | solution.py:353
  88.6 4.9 %collective-permute-done.28 = bf16[128,1024]{1,0:T(8,128)(2,1)S(1)} collective-permute-done((bf16[128,1024]{1,0:T(8,128)(2,1)S(1)}, bf16[128,1024]{1,0:T(8,128)(2,1)S(1)}, u32[]{:S(2)}, u32[]{:S(2)}) %collective-permute-start.28) | collective-permute-done | bytes 262176 | tf_op jit(solution)/shard_map/ppermute | solution.py:353
  93.5 0.8 add_convert_fusion
  (34 shorter events, 0.1 us)
Async XLA Ops:
  0.0 1.0 %copy-start = (bf16[256,1024]{1,0:T(8,128)(2,1)S(1)}, bf16[256,1024]{1,0:T(8,128)(2,1)}, u32[]{:S(2)}) copy-start(bf16[256,1024]{1,0:T(8,128)(2,1)} %param.12) | copy-start | bytes 1572868
  1.1 3.1 %copy-start.2 = (bf16[256,512]{1,0:T(8,128)(2,1)}, bf16[256,512]{1,0:T(8,128)(2,1)S(1)}, u32[]{:S(2)}) copy-start(bf16[256,512]{1,0:T(8,128)(2,1)S(1)} %constant_dynamic-slice_fusion.after.w0) | copy-start | bytes 786436
  1.1 22.5 %copy-start.5 = (bf16[128,1024]{1,0:T(8,128)(2,1)S(1)}, bf16[128,1024]{1,0:T(8,128)(2,1)}, u32[]{:S(2)}) copy-start(bf16[128,1024]{1,0:T(8,128)(2,1)} %refs_0_.1) | copy-start | bytes 786436
  1.1 14.2 %collective-permute-start.2 = (bf16[256,512]{1,0:T(8,128)(2,1)S(1)}, bf16[256,512]{1,0:T(8,128)(2,1)S(1)}, u32[]{:S(2)}, u32[]{:S(2)}) collective-permute-start(bf16[256,512]{1,0:T(8,128)(2,1)S(1)} %constant_dynamic-slice_fusion.after.w0), channel_id=1, source_target_pairs={{0,4},{1,5},{2,6},{3,7},{4,8},{5,9},{6,10},{7,11},{8,12},{9,13},{1... | collective-permute-start | bytes 786440 | tf_op jit(solution)/shard_map/ppermute | solution.py:353
  6.8 8.6 %collective-permute-start.1 = (bf16[256,256]{1,0:T(8,128)(2,1)}, bf16[256,256]{1,0:T(8,128)(2,1)S(1)}, u32[]{:S(2)}, u32[]{:S(2)}) collective-permute-start(bf16[256,256]{1,0:T(8,128)(2,1)} %get-tuple-element.43.refs_0_), channel_id=1, source_target_pairs={{0,4},{1,5},{2,6},{3,7},{4,8},{5,9},{6,10},{7,11},{8,12},{9,13},{1... | collective-permute-start | bytes 393224 | tf_op jit(solution)/shard_map/ppermute | solution.py:353
  8.4 9.5 %collective-permute-start = (bf16[128,1024]{1,0:T(8,128)(2,1)}, bf16[128,1024]{1,0:T(8,128)(2,1)S(1)}, u32[]{:S(2)}, u32[]{:S(2)}) collective-permute-start(bf16[128,1024]{1,0:T(8,128)(2,1)} %get-tuple-element.42), channel_id=1, source_target_pairs={{0,2},{1,3},{2,0},{3,1},{4,6},{5,7},{6,4},{7,5},{8,10},{9,11},{10,... | collective-permute-start | bytes 786440 | tf_op jit(solution)/shard_map/ppermute | solution.py:353
  9.9 13.7 %collective-permute-start.4 = (bf16[128,1024]{1,0:T(8,128)(2,1)}, bf16[128,1024]{1,0:T(8,128)(2,1)S(1)}, u32[]{:S(2)}, u32[]{:S(2)}) collective-permute-start(bf16[128,1024]{1,0:T(8,128)(2,1)} %get-tuple-element.46), channel_id=1, source_target_pairs={{0,16},{1,17},{2,18},{3,19},{4,20},{5,21},{6,22},{7,23},{8,24},{9,... | collective-permute-start | bytes 786440 | tf_op jit(solution)/shard_map/ppermute | solution.py:353
  11.4 12.3 %copy-start.12 = (bf16[256,256]{1,0:T(8,128)(2,1)S(1)}, bf16[256,256]{1,0:T(8,128)(2,1)}, u32[]{:S(2)}) copy-start(bf16[256,256]{1,0:T(8,128)(2,1)} %get-tuple-element.49) | copy-start | bytes 393220
  11.4 13.9 %copy-start.11 = (bf16[2,2,128,256]{3,2,1,0:T(8,128)(2,1)S(1)}, bf16[2,2,128,256]{3,2,1,0:T(8,128)(2,1)}, u32[]{:S(2)}) copy-start(bf16[2,2,128,256]{3,2,1,0:T(8,128)(2,1)} %get-tuple-element.51) | copy-start | bytes 786436
  11.4 27.2 %copy-start.3 = (bf16[256,512]{1,0:T(8,128)(2,1)S(1)}, bf16[256,512]{1,0:T(8,128)(2,1)}, u32[]{:S(2)}) copy-start(bf16[256,512]{1,0:T(8,128)(2,1)} %copy-done.2) | copy-start | bytes 786436
  11.4 12.1 %collective-permute-start.5 = (bf16[128,1024]{1,0:T(8,128)(2,1)}, bf16[128,1024]{1,0:T(8,128)(2,1)S(1)}, u32[]{:S(2)}, u32[]{:S(2)}) collective-permute-start(bf16[128,1024]{1,0:T(8,128)(2,1)} %get-tuple-element.47), channel_id=1, source_target_pairs={{0,18},{1,19},{2,16},{3,17},{4,22},{5,23},{6,20},{7,21},{8,26},{9,... | collective-permute-start | bytes 786440 | tf_op jit(solution)/shard_map/ppermute | solution.py:353
  15.3 8.2 %collective-permute-start.3 = (bf16[256,256]{1,0:T(8,128)(2,1)S(1)}, bf16[256,256]{1,0:T(8,128)(2,1)S(1)}, u32[]{:S(2)}, u32[]{:S(2)}) collective-permute-start(bf16[256,256]{1,0:T(8,128)(2,1)S(1)} %collective-permute-done.1.refs_2_), channel_id=1, source_target_pairs={{0,4},{1,5},{2,6},{3,7},{4,8},{5,9},{6,10},{7,11},{8,12},{9,13},{1... | collective-permute-start | bytes 393224 | tf_op jit(solution)/shard_map/ppermute | solution.py:353
  15.3 12.1 %collective-permute-start.7 = (bf16[256,512]{1,0:T(8,128)(2,1)S(1)}, bf16[256,512]{1,0:T(8,128)(2,1)S(1)}, u32[]{:S(2)}, u32[]{:S(2)}) collective-permute-start(bf16[256,512]{1,0:T(8,128)(2,1)S(1)} %collective-permute-done.2.w1), channel_id=1, source_target_pairs={{0,4},{1,5},{2,6},{3,7},{4,8},{5,9},{6,10},{7,11},{8,12},{9,13},{1... | collective-permute-start | bytes 786440 | tf_op jit(solution)/shard_map/ppermute | solution.py:353
  23.6 15.0 %collective-permute-start.10 = (bf16[512,512]{1,0:T(8,128)(2,1)S(1)}, bf16[512,512]{1,0:T(8,128)(2,1)S(1)}, u32[]{:S(2)}, u32[]{:S(2)}) collective-permute-start(bf16[512,512]{1,0:T(8,128)(2,1)S(1)} %shard_map.92.mine), channel_id=1, source_target_pairs={{0,1},{1,0},{2,3},{3,2},{4,5},{5,4},{6,7},{7,6},{8,9},{9,8},{10,11... | collective-permute-start | bytes 1572872 | tf_op jit(solution)/shard_map/ppermute | solution.py:353
  23.7 6.4 %collective-permute-start.6 = (bf16[256,256]{1,0:T(8,128)(2,1)S(1)}, bf16[256,256]{1,0:T(8,128)(2,1)S(1)}, u32[]{:S(2)}, u32[]{:S(2)}) collective-permute-start(bf16[256,256]{1,0:T(8,128)(2,1)S(1)} %copy-done.12), channel_id=1, source_target_pairs={{0,2},{1,3},{2,0},{3,1},{4,6},{5,7},{6,4},{7,5},{8,10},{9,11},{10,... | collective-permute-start | bytes 393224 | tf_op jit(solution)/shard_map/ppermute | solution.py:353
  25.3 16.1 %copy-start.1 = (bf16[2,2,128,1024]{3,2,1,0:T(8,128)(2,1)S(1)}, bf16[2,2,128,1024]{3,2,1,0:T(8,128)(2,1)}, u32[]{:S(2)}) copy-start(bf16[2,2,128,1024]{3,2,1,0:T(8,128)(2,1)} %filt.3) | copy-start | bytes 3145732
  25.3 10.0 %collective-permute-start.9 = (bf16[2,2,128,256]{3,2,1,0:T(8,128)(2,1)S(1)}, bf16[2,2,128,256]{3,2,1,0:T(8,128)(2,1)S(1)}, u32[]{:S(2)}, u32[]{:S(2)}) collective-permute-start(bf16[2,2,128,256]{3,2,1,0:T(8,128)(2,1)S(1)} %copy-done.11), channel_id=1, source_target_pairs={{0,2},{1,3},{2,0},{3,1},{4,6},{5,7},{6,4},{7,5},{8,10},{9,11},{10,... | collective-permute-start | bytes 786440 | tf_op jit(solution)/shard_map/ppermute | solution.py:353
  27.4 11.2 %collective-permute-start.11 = (bf16[256,512]{1,0:T(8,128)(2,1)S(1)}, bf16[256,512]{1,0:T(8,128)(2,1)S(1)}, u32[]{:S(2)}, u32[]{:S(2)}) collective-permute-start(bf16[256,512]{1,0:T(8,128)(2,1)S(1)} %collective-permute-done.7.w2), channel_id=1, source_target_pairs={{0,4},{1,5},{2,6},{3,7},{4,8},{5,9},{6,10},{7,11},{8,12},{9,13},{1... | collective-permute-start | bytes 786440 | tf_op jit(solution)/shard_map/ppermute | solution.py:353
  30.1 8.5 %collective-permute-start.8 = (bf16[256,256]{1,0:T(8,128)(2,1)S(1)}, bf16[256,256]{1,0:T(8,128)(2,1)S(1)}, u32[]{:S(2)}, u32[]{:S(2)}) collective-permute-start(bf16[256,256]{1,0:T(8,128)(2,1)S(1)} %collective-permute-done.6.refs_1_), channel_id=1, source_target_pairs={{0,4},{1,5},{2,6},{3,7},{4,8},{5,9},{6,10},{7,11},{8,12},{9,13},{1... | collective-permute-start | bytes 393224 | tf_op jit(solution)/shard_map/ppermute | solution.py:353
  39.9 10.2 %copy-start.4 = (bf16[128,1024]{1,0:T(8,128)(2,1)S(1)}, bf16[128,1024]{1,0:T(8,128)(2,1)}, u32[]{:S(2)}) copy-start(bf16[128,1024]{1,0:T(8,128)(2,1)} %g0.2) | copy-start | bytes 786436
  39.9 10.1 %collective-permute-start.13 = (bf16[512,256]{1,0:T(8,128)(2,1)S(1)}, bf16[512,256]{1,0:T(8,128)(2,1)S(1)}, u32[]{:S(2)}, u32[]{:S(2)}) collective-permute-start(bf16[512,256]{1,0:T(8,128)(2,1)S(1)} %get-tuple-element.56), channel_id=1, source_target_pairs={{0,2},{1,3},{2,0},{3,1},{4,6},{5,7},{6,4},{7,5},{8,10},{9,11},{10,... | collective-permute-start | bytes 786440 | tf_op jit(solution)/shard_map/ppermute | solution.py:353
  41.4 24.8 %copy-start.10 = (bf16[16,256,128]{2,1,0:T(8,128)(2,1)S(1)}, bf16[16,256,128]{2,1,0:T(8,128)(2,1)}, u32[]{:S(2)}) copy-start(bf16[16,256,128]{2,1,0:T(8,128)(2,1)} %constant.17.clone.refs_9_) | copy-start | bytes 3145732
  41.7 8.4 %copy-start.8 = (f32[1024]{0:T(1024)S(1)}, f32[1024]{0:T(1024)}, u32[]{:S(2)}) copy-start(f32[1024]{0:T(1024)} %param.13) | copy-start | bytes 12292
  41.7 24.5 %copy-start.9 = (bf16[16,256,128]{2,1,0:T(8,128)(2,1)S(1)}, bf16[16,256,128]{2,1,0:T(8,128)(2,1)}, u32[]{:S(2)}) copy-start(bf16[16,256,128]{2,1,0:T(8,128)(2,1)} %constant.16.clone.refs_8_) | copy-start | bytes 3145732
  41.7 8.3 %collective-permute-start.12 = (bf16[2,2,128,128]{3,2,1,0:T(8,128)(2,1)S(1)}, bf16[2,2,128,128]{3,2,1,0:T(8,128)(2,1)S(1)}, u32[]{:S(2)}, u32[]{:S(2)}) collective-permute-start(bf16[2,2,128,128]{3,2,1,0:T(8,128)(2,1)S(1)} %get-tuple-element.54), channel_id=1, source_target_pairs={{0,4},{1,5},{2,6},{3,7},{4,8},{5,9},{6,10},{7,11},{8,12},{9,13},{1... | collective-permute-start | bytes 393224 | tf_op jit(solution)/shard_map/ppermute | solution.py:353
  41.8 13.6 %collective-permute-start.17 = (bf16[2,2,128,128]{3,2,1,0:T(8,128)(2,1)S(1)}, bf16[2,2,128,128]{3,2,1,0:T(8,128)(2,1)S(1)}, u32[]{:S(2)}, u32[]{:S(2)}) collective-permute-start(bf16[2,2,128,128]{3,2,1,0:T(8,128)(2,1)S(1)} %get-tuple-element.62), channel_id=1, source_target_pairs={{0,8},{1,9},{2,10},{3,11},{4,12},{5,13},{6,14},{7,15},{8,0},{9,1},... | collective-permute-start | bytes 393224 | tf_op jit(solution)/shard_map/ppermute | solution.py:353
  41.9 15.2 %collective-permute-start.18 = (bf16[2,2,128,128]{3,2,1,0:T(8,128)(2,1)S(1)}, bf16[2,2,128,128]{3,2,1,0:T(8,128)(2,1)S(1)}, u32[]{:S(2)}, u32[]{:S(2)}) collective-permute-start(bf16[2,2,128,128]{3,2,1,0:T(8,128)(2,1)S(1)} %get-tuple-element.63), channel_id=1, source_target_pairs={{0,12},{1,13},{2,14},{3,15},{4,0},{5,1},{6,2},{7,3},{8,4},{9,5},{1... | collective-permute-start | bytes 393224 | tf_op jit(solution)/shard_map/ppermute | solution.py:353
  45.6 11.9 %collective-permute-start.23 = (bf16[256,256]{1,0:T(8,128)(2,1)S(1)}, bf16[256,256]{1,0:T(8,128)(2,1)S(1)}, u32[]{:S(2)}, u32[]{:S(2)}) collective-permute-start(bf16[256,256]{1,0:T(8,128)(2,1)S(1)} %collective-permute-done.8.refs_3_), channel_id=1, source_target_pairs={{0,4},{1,5},{2,6},{3,7},{4,8},{5,9},{6,10},{7,11},{8,12},{9,13},{1... | collective-permute-start | bytes 393224 | tf_op jit(solution)/shard_map/ppermute | solution.py:353
  50.4 8.1 %collective-permute-start.14 = (bf16[256,128]{1,0:T(8,128)(2,1)S(1)}, bf16[256,128]{1,0:T(8,128)(2,1)S(1)}, u32[]{:S(2)}, u32[]{:S(2)}) collective-permute-start(bf16[256,128]{1,0:T(8,128)(2,1)S(1)} %get-tuple-element.58), channel_id=1, source_target_pairs={{0,4},{1,5},{2,6},{3,7},{4,8},{5,9},{6,10},{7,11},{8,12},{9,13},{1... | collective-permute-start | bytes 196616 | tf_op jit(solution)/shard_map/ppermute | solution.py:353
  50.5 13.0 %collective-permute-start.15 = (bf16[256,128]{1,0:T(8,128)(2,1)S(1)}, bf16[256,128]{1,0:T(8,128)(2,1)S(1)}, u32[]{:S(2)}, u32[]{:S(2)}) collective-permute-start(bf16[256,128]{1,0:T(8,128)(2,1)S(1)} %get-tuple-element.59), channel_id=1, source_target_pairs={{0,8},{1,9},{2,10},{3,11},{4,12},{5,13},{6,14},{7,15},{8,0},{9,1},... | collective-permute-start | bytes 196616 | tf_op jit(solution)/shard_map/ppermute | solution.py:353
  55.4 8.1 %collective-permute-start.16 = (bf16[256,128]{1,0:T(8,128)(2,1)S(1)}, bf16[256,128]{1,0:T(8,128)(2,1)S(1)}, u32[]{:S(2)}, u32[]{:S(2)}) collective-permute-start(bf16[256,128]{1,0:T(8,128)(2,1)S(1)} %get-tuple-element.60), channel_id=1, source_target_pairs={{0,12},{1,13},{2,14},{3,15},{4,0},{5,1},{6,2},{7,3},{8,4},{9,5},{1... | collective-permute-start | bytes 196616 | tf_op jit(solution)/shard_map/ppermute | solution.py:353
  58.5 16.6 %collective-permute-start.25 = (bf16[256,256]{1,0:T(8,128)(2,1)S(1)}, bf16[256,256]{1,0:T(8,128)(2,1)S(1)}, u32[]{:S(2)}, u32[]{:S(2)}) collective-permute-start(bf16[256,256]{1,0:T(8,128)(2,1)S(1)} %collective-permute-done.23.refs_5_), channel_id=1, source_target_pairs={{0,4},{1,5},{2,6},{3,7},{4,8},{5,9},{6,10},{7,11},{8,12},{9,13},{1... | collective-permute-start | bytes 393224 | tf_op jit(solution)/shard_map/ppermute | solution.py:353
  63.5 11.6 %collective-permute-start.24 = (bf16[256,256]{1,0:T(8,128)(2,1)S(1)}, bf16[256,256]{1,0:T(8,128)(2,1)S(1)}, u32[]{:S(2)}, u32[]{:S(2)}) collective-permute-start(bf16[256,256]{1,0:T(8,128)(2,1)S(1)} %collective-permute-done.3.refs_4_), channel_id=1, source_target_pairs={{0,4},{1,5},{2,6},{3,7},{4,8},{5,9},{6,10},{7,11},{8,12},{9,13},{1... | collective-permute-start | bytes 393224 | tf_op jit(solution)/shard_map/ppermute | solution.py:353
  66.2 8.9 %copy-start.7 = (bf16[256,256]{1,0:T(8,128)(2,1)S(1)}, bf16[256,256]{1,0:T(8,128)(2,1)}, u32[]{:S(2)}) copy-start(bf16[256,256]{1,0:T(8,128)(2,1)} %get-tuple-element.43.refs_0_) | copy-start | bytes 393220
  68.0 6.2 %collective-permute-start.19 = (bf16[256,128]{1,0:T(8,128)(2,1)S(1)}, bf16[256,128]{1,0:T(8,128)(2,1)S(1)}, u32[]{:S(2)}, u32[]{:S(2)}) collective-permute-start(bf16[256,128]{1,0:T(8,128)(2,1)S(1)} %get-tuple-element.65), channel_id=1, source_target_pairs={{0,4},{1,5},{2,6},{3,7},{4,8},{5,9},{6,10},{7,11},{8,12},{9,13},{1... | collective-permute-start | bytes 196616 | tf_op jit(solution)/shard_map/ppermute | solution.py:353
  68.1 7.0 %collective-permute-start.20 = (bf16[256,128]{1,0:T(8,128)(2,1)S(1)}, bf16[256,128]{1,0:T(8,128)(2,1)S(1)}, u32[]{:S(2)}, u32[]{:S(2)}) collective-permute-start(bf16[256,128]{1,0:T(8,128)(2,1)S(1)} %get-tuple-element.66), channel_id=1, source_target_pairs={{0,8},{1,9},{2,10},{3,11},{4,12},{5,13},{6,14},{7,15},{8,0},{9,1},... | collective-permute-start | bytes 196616 | tf_op jit(solution)/shard_map/ppermute | solution.py:353
  69.8 5.6 %copy-start.6 = (bf16[128,1024]{1,0:T(8,128)(2,1)S(1)}, bf16[128,1024]{1,0:T(8,128)(2,1)}, u32[]{:S(2)}) copy-start(bf16[128,1024]{1,0:T(8,128)(2,1)} %g0.3) | copy-start | bytes 786436
  69.8 5.3 %collective-permute-start.21 = (bf16[256,128]{1,0:T(8,128)(2,1)S(1)}, bf16[256,128]{1,0:T(8,128)(2,1)S(1)}, u32[]{:S(2)}, u32[]{:S(2)}) collective-permute-start(bf16[256,128]{1,0:T(8,128)(2,1)S(1)} %get-tuple-element.67), channel_id=1, source_target_pairs={{0,12},{1,13},{2,14},{3,15},{4,0},{5,1},{6,2},{7,3},{8,4},{9,5},{1... | collective-permute-start | bytes 196616 | tf_op jit(solution)/shard_map/ppermute | solution.py:353
  75.3 2.4 %collective-permute-start.26 = (bf16[4,256,256]{2,1,0:T(8,128)(2,1)S(1)}, bf16[4,256,256]{2,1,0:T(8,128)(2,1)S(1)}, u32[]{:S(2)}, u32[]{:S(2)}) collective-permute-start(bf16[4,256,256]{2,1,0:T(8,128)(2,1)S(1)} %get-tuple-element.74), channel_id=1, source_target_pairs={{0,1},{1,0},{2,3},{3,2},{4,5},{5,4},{6,7},{7,6},{8,9},{9,8},{10,11... | collective-permute-start | bytes 1572872 | tf_op jit(solution)/shard_map/ppermute | solution.py:353
  75.6 2.0 %collective-permute-start.22 = (bf16[512,256]{1,0:T(8,128)(2,1)S(1)}, bf16[512,256]{1,0:T(8,128)(2,1)S(1)}, u32[]{:S(2)}, u32[]{:S(2)}) collective-permute-start(bf16[512,256]{1,0:T(8,128)(2,1)S(1)} %shard_map.97.gated), channel_id=1, source_target_pairs={{0,1},{1,0},{2,3},{3,2},{4,5},{5,4},{6,7},{7,6},{8,9},{9,8},{10,11... | collective-permute-start | bytes 786440 | tf_op jit(solution)/shard_map/ppermute | solution.py:353
  78.5 10.2 %collective-permute-start.27 = (bf16[128,1024]{1,0:T(8,128)(2,1)S(1)}, bf16[128,1024]{1,0:T(8,128)(2,1)S(1)}, u32[]{:S(2)}, u32[]{:S(2)}) collective-permute-start(bf16[128,1024]{1,0:T(8,128)(2,1)S(1)} %get-tuple-element.76), channel_id=1, source_target_pairs={{0,18},{1,19},{2,16},{3,17},{4,22},{5,23},{6,20},{7,21},{8,26},{9,... | collective-permute-start | bytes 786440 | tf_op jit(solution)/shard_map/ppermute | solution.py:353
  80.0 13.5 %collective-permute-start.28 = (bf16[128,1024]{1,0:T(8,128)(2,1)S(1)}, bf16[128,1024]{1,0:T(8,128)(2,1)S(1)}, u32[]{:S(2)}, u32[]{:S(2)}) collective-permute-start(bf16[128,1024]{1,0:T(8,128)(2,1)S(1)} %get-tuple-element.77), channel_id=1, source_target_pairs={{0,2},{1,3},{2,0},{3,1},{4,6},{5,7},{6,4},{7,5},{8,10},{9,11},{10,... | collective-permute-start | bytes 786440 | tf_op jit(solution)/shard_map/ppermute | solution.py:353
  82.3 11.2 %collective-permute-start.29 = (bf16[128,1024]{1,0:T(8,128)(2,1)S(1)}, bf16[128,1024]{1,0:T(8,128)(2,1)S(1)}, u32[]{:S(2)}, u32[]{:S(2)}) collective-permute-start(bf16[128,1024]{1,0:T(8,128)(2,1)S(1)} %get-tuple-element.78), channel_id=1, source_target_pairs={{0,16},{1,17},{2,18},{3,19},{4,20},{5,21},{6,22},{7,23},{8,24},{9,... | collective-permute-start | bytes 786440 | tf_op jit(solution)/shard_map/ppermute | solution.py:353

commit v13 on v12

--- a/solution.py
+++ b/solution.py
@@ -384,10 +384,10 @@
     )(filter_spectrum, near)
     filters = [filters[0]] + [to_z(filters[r], r) for r in (1, 2, 3)]
     v1 = to_z(own_v, 1)
-    q1 = to_z(own_o, 1)
+    q1 = to_z(after(own_o, v1), 1)
     v2 = to_z(v1, 1)
-    q2 = to_z(after(q1, v1), 1)
-    mine = in_vmem(join_tokens, shape((512, 512), BF16), moved=1 << 20)(tokens, after(received[0], q2), *received[1:])
+    q2 = to_z(after(q1, v2), 1)
+    mine = in_vmem(join_tokens, shape((512, 512), BF16), moved=1 << 20)(tokens, after(received[0], q1), *received[1:])
     v3 = to_z(v2, 1)
     other = to_core(mine)
     got_o = to_x(after(away_o, v1))
@@ -398,7 +398,7 @@
         [pltpu.VMEM((512, 512), F32)],
         flops=1 << 29,
         moved=2 << 20,
-    )(after(mine, r1, near), other, own_v, v1, v2, v3)
+    )(after(mine, q2, r1, near), other, own_v, v1, v2, v3)
     r2 = to_z(after(r1, keep), 1)
     drive, *sends = in_vmem(
         drive_kernel,
@@ -408,7 +408,7 @@
     )(after(keep, filters[1]), to_x(give), gate_k, *received, skip[None, :])
     columns = [sends[0]] + [to_z(sends[r], r) for r in (1, 2, 3)]
     r3 = to_z(after(r2, *filters[2:], columns[1]), 1)
-    q3 = to_z(after(q2, *columns[1:]), 1)
+    q3 = to_z(after(q2, columns[1]), 1)
     table, table_t = tables()
     sends = in_vmem(
         conv_kernel,

time: 94.5 us -> 94.7 us (level)
  starting transfers between devices: 36.5 us -> 39.9 us
  waiting for transfers between devices: 47.3 us -> 44.1 us
    ppermute x30, starting transfers between devices: 36.5 us -> 39.9 us  [permute(): return lax.ppermute(values, AXES, pairs)]
    ppermute x30, waiting for transfers between devices: 47.3 us -> 44.1 us  [permute(): return lax.ppermute(values, AXES, pairs)]
  transfers between devices with their start and end apart: 30 -> 30, of which waited for: 17 -> 18; matrix products, arithmetic and copies ran while one was open for 0% -> 0% of each run, Pallas kernels for 6% -> 6%
where the time goes in v13:
time: 94.7 us; the launch traced here: 94.5 us
  waiting for transfers between devices  44.1 us (47%)
  starting transfers between devices  39.9 us (42%)
  Pallas kernels  8.36 us (9%)
  local copies, waits for them, and re-layouts  1.12 us (1%)
    ppermute x30, waiting for transfers between devices, permute(): return lax.ppermute(values, AXES, pairs)  44.1 us
    ppermute x30, starting transfers between devices, permute(): return lax.ppermute(values, AXES, pairs)  39.9 us
    pallas_call x9, Pallas kernels, call(): pl.pallas_call(kernel, out_shape=out_shape, in_specs=specs, out_specs=jax...  5.79 us
    pallas_call x1, Pallas kernels, call(): pl.pallas_call(kernel, out_shape=out_shape, in_specs=[pl.BlockSpec(memory...  2.58 us
  transfers between devices with their start and end apart: 30, of which 18 were waited for; matrix products, arithmetic and copies ran while one was open for 0% of the time, Pallas kernels for 6%

profile of v13, /device:TPU:0, one launch (start us, length us, event | category | flops | bytes accessed | tf_op | source)
XLA Modules:
  0.0 94.5 jit_solution(4265377859863992441)
XLA Ops:
  0.0 1.0 %copy-done = bf16[256,1024]{1,0:T(8,128)(2,1)S(1)} copy-done((bf16[256,1024]{1,0:T(8,128)(2,1)S(1)}, bf16[256,1024]{1,0:T(8,128)(2,1)}, u32[]{:S(2)}) %copy-start) | copy-done | bytes 524312
  1.1 0.0 copy-start.2
  1.1 0.0 copy-start.5
  1.1 3.1 %collective-permute-start.1 = (bf16[256,512]{1,0:T(8,128)(2,1)S(1)}, bf16[256,512]{1,0:T(8,128)(2,1)S(1)}, u32[]{:S(2)}, u32[]{:S(2)}) collective-permute-start(bf16[256,512]{1,0:T(8,128)(2,1)S(1)} %constant_dynamic-slice_fusion.after.w0), channel_id=1, source_target_pairs={{0,4},{1,5},{2,6},{3,7},{4,8},{5,9},{6,10},{7,11},{8,12},{9,13},{1... | collective-permute-start | bytes 786440 | tf_op jit(solution)/shard_map/ppermute | solution.py:353
  4.2 2.6 %shard_map.91 = (bf16[128,1024]{1,0:T(8,128)(2,1)}, bf16[128,1024]{1,0:T(8,128)(2,1)}, bf16[128,1024]{1,0:T(8,128)(2,1)}, bf16[256,256]{1,0:T(8,128)(2,1)}, bf16...) custom-call(bf16[128,1024]{1,0:T(8,128)(2,1)} %refs_0_.1, bf16[128,1024]{1,0:T(8,128)(2,1)} %g0.2, ...), custom_call_target="tpu_custom_call" | custom-call | tf_op jit(solution)/shard_map/pallas_call | solution.py:101
  6.8 1.6 %collective-permute-start = (bf16[128,1024]{1,0:T(8,128)(2,1)}, bf16[128,1024]{1,0:T(8,128)(2,1)S(1)}, u32[]{:S(2)}, u32[]{:S(2)}) collective-permute-start(bf16[128,1024]{1,0:T(8,128)(2,1)} %get-tuple-element.43), channel_id=1, source_target_pairs={{0,2},{1,3},{2,0},{3,1},{4,6},{5,7},{6,4},{7,5},{8,10},{9,11},{10,... | collective-permute-start | bytes 786440 | tf_op jit(solution)/shard_map/ppermute | solution.py:353
  8.3 1.5 %collective-permute-start.3 = (bf16[128,1024]{1,0:T(8,128)(2,1)}, bf16[128,1024]{1,0:T(8,128)(2,1)S(1)}, u32[]{:S(2)}, u32[]{:S(2)}) collective-permute-start(bf16[128,1024]{1,0:T(8,128)(2,1)} %get-tuple-element.47), channel_id=1, source_target_pairs={{0,16},{1,17},{2,18},{3,19},{4,20},{5,21},{6,22},{7,23},{8,24},{9,... | collective-permute-start | bytes 786440 | tf_op jit(solution)/shard_map/ppermute | solution.py:353
  9.8 0.5 collective-permute-start.4
  10.3 2.2 %collective-permute-done.1.w1 = bf16[256,512]{1,0:T(8,128)(2,1)S(1)} collective-permute-done((bf16[256,512]{1,0:T(8,128)(2,1)S(1)}, bf16[256,512]{1,0:T(8,128)(2,1)S(1)}, u32[]{:S(2)}, u32[]{:S(2)}) %collective-permute-start.1) | collective-permute-done | bytes 262176 | tf_op jit(solution)/shard_map/ppermute | solution.py:353
  12.5 0.0 collective-permute-start.2
  12.5 1.3 %collective-permute-start.5 = (bf16[256,512]{1,0:T(8,128)(2,1)S(1)}, bf16[256,512]{1,0:T(8,128)(2,1)S(1)}, u32[]{:S(2)}, u32[]{:S(2)}) collective-permute-start(bf16[256,512]{1,0:T(8,128)(2,1)S(1)} %collective-permute-done.1.w1), channel_id=1, source_target_pairs={{0,4},{1,5},{2,6},{3,7},{4,8},{5,9},{6,10},{7,11},{8,12},{9,13},{1... | collective-permute-start | bytes 786440 | tf_op jit(solution)/shard_map/ppermute | solution.py:353
  13.8 2.5 %collective-permute-done.refs_1_.g1 = bf16[128,1024]{1,0:T(8,128)(2,1)S(1)} collective-permute-done((bf16[128,1024]{1,0:T(8,128)(2,1)}, bf16[128,1024]{1,0:T(8,128)(2,1)S(1)}, u32[]{:S(2)}, u32[]{:S(2)}) %collective-permute-start) | collective-permute-done | bytes 262176 | tf_op jit(solution)/shard_map/ppermute | solution.py:353
  16.3 4.7 %collective-permute-done.2.refs_2_ = bf16[256,256]{1,0:T(8,128)(2,1)S(1)} collective-permute-done((bf16[256,256]{1,0:T(8,128)(2,1)}, bf16[256,256]{1,0:T(8,128)(2,1)S(1)}, u32[]{:S(2)}, u32[]{:S(2)}) %collective-permute-start.2) | collective-permute-done | bytes 131104 | tf_op jit(solution)/shard_map/ppermute | solution.py:353
  20.9 0.7 collective-permute-done.3.refs_2_.g2
  21.7 0.1 collective-permute-start.10
  21.8 1.3 %collective-permute-start.7 = (bf16[256,256]{1,0:T(8,128)(2,1)S(1)}, bf16[256,256]{1,0:T(8,128)(2,1)S(1)}, u32[]{:S(2)}, u32[]{:S(2)}) collective-permute-start(bf16[256,256]{1,0:T(8,128)(2,1)S(1)} %copy-done.12), channel_id=1, source_target_pairs={{0,2},{1,3},{2,0},{3,1},{4,6},{5,7},{6,4},{7,5},{8,10},{9,11},{10,... | collective-permute-start | bytes 393224 | tf_op jit(solution)/shard_map/ppermute | solution.py:353
  23.1 0.8 collective-permute-start.9
  23.9 1.0 %collective-permute-done.5.w2 = bf16[256,512]{1,0:T(8,128)(2,1)S(1)} collective-permute-done((bf16[256,512]{1,0:T(8,128)(2,1)S(1)}, bf16[256,512]{1,0:T(8,128)(2,1)S(1)}, u32[]{:S(2)}, u32[]{:S(2)}) %collective-permute-start.5) | collective-permute-done | bytes 262176 | tf_op jit(solution)/shard_map/ppermute | solution.py:353
  24.8 0.6 collective-permute-start.11
  25.4 1.6 %collective-permute-start.6 = (bf16[256,256]{1,0:T(8,128)(2,1)S(1)}, bf16[256,256]{1,0:T(8,128)(2,1)S(1)}, u32[]{:S(2)}, u32[]{:S(2)}) collective-permute-start(bf16[256,256]{1,0:T(8,128)(2,1)S(1)} %collective-permute-done.2.refs_2_), channel_id=1, source_target_pairs={{0,4},{1,5},{2,6},{3,7},{4,8},{5,9},{6,10},{7,11},{8,12},{9,13},{1... | collective-permute-start | bytes 393224 | tf_op jit(solution)/shard_map/ppermute | solution.py:353
  27.0 1.1 %collective-permute-done.7.refs_1_ = bf16[256,256]{1,0:T(8,128)(2,1)S(1)} collective-permute-done((bf16[256,256]{1,0:T(8,128)(2,1)S(1)}, bf16[256,256]{1,0:T(8,128)(2,1)S(1)}, u32[]{:S(2)}, u32[]{:S(2)}) %collective-permute-start.7) | collective-permute-done | bytes 131104 | tf_op jit(solution)/shard_map/ppermute | solution.py:353
  28.1 1.6 %collective-permute-start.8 = (bf16[256,256]{1,0:T(8,128)(2,1)S(1)}, bf16[256,256]{1,0:T(8,128)(2,1)S(1)}, u32[]{:S(2)}, u32[]{:S(2)}) collective-permute-start(bf16[256,256]{1,0:T(8,128)(2,1)S(1)} %collective-permute-done.7.refs_1_), channel_id=1, source_target_pairs={{0,4},{1,5},{2,6},{3,7},{4,8},{5,9},{6,10},{7,11},{8,12},{9,13},{1... | collective-permute-start | bytes 393224 | tf_op jit(solution)/shard_map/ppermute | solution.py:353
  29.7 3.6 %collective-permute-done.9.near = bf16[2,2,128,256]{3,2,1,0:T(8,128)(2,1)S(1)} collective-permute-done((bf16[2,2,128,256]{3,2,1,0:T(8,128)(2,1)S(1)}, bf16[2,2,128,256]{3,2,1,0:T(8,128)(2,1)S(1)}, u32[]{:S(2)}, u32[]{:S(2)}) %collective-permute-start.9) | collective-permute-done | bytes 262176 | tf_op jit(solution)/shard_map/ppermute | solution.py:353
  33.3 4.7 %collective-permute-done.6.refs_4_ = bf16[256,256]{1,0:T(8,128)(2,1)S(1)} collective-permute-done((bf16[256,256]{1,0:T(8,128)(2,1)S(1)}, bf16[256,256]{1,0:T(8,128)(2,1)S(1)}, u32[]{:S(2)}, u32[]{:S(2)}) %collective-permute-start.6) | collective-permute-done | bytes 131104 | tf_op jit(solution)/shard_map/ppermute | solution.py:353
  38.0 1.4 %collective-permute-done.8.refs_3_ = bf16[256,256]{1,0:T(8,128)(2,1)S(1)} collective-permute-done((bf16[256,256]{1,0:T(8,128)(2,1)S(1)}, bf16[256,256]{1,0:T(8,128)(2,1)S(1)}, u32[]{:S(2)}, u32[]{:S(2)}) %collective-permute-start.8) | collective-permute-done | bytes 131104 | tf_op jit(solution)/shard_map/ppermute | solution.py:353
  39.4 1.3 %shard_map.93 = (f32[512,256]{1,0:T(8,128)S(1)}, bf16[512,256]{1,0:T(8,128)(2,1)S(1)}) custom-call(bf16[512,512]{1,0:T(8,128)(2,1)S(1)} %shard_map.92.mine, bf16[512,512]{1,0:T(8,128)(2,1)S(1)} %collective-permute-done.10.other, bf16[256,512]{1,0:T(8,128)(2,1)S(1)} %copy-done.3, bf16[256,512]{1,0:T(8,128)(2,1)S(1)} %collective-permute-done.1.w1, ...), custom_call_target="tpu_custom_call" | custom-call | flops 536870912 | bytes 2097152 | tf_op jit(solution)/shard_map/pallas_call | solution.py:37
  40.7 0.0 copy-start.4
  40.7 1.3 %collective-permute-start.13 = (bf16[512,256]{1,0:T(8,128)(2,1)S(1)}, bf16[512,256]{1,0:T(8,128)(2,1)S(1)}, u32[]{:S(2)}, u32[]{:S(2)}) collective-permute-start(bf16[512,256]{1,0:T(8,128)(2,1)S(1)} %get-tuple-element.58), channel_id=1, source_target_pairs={{0,2},{1,3},{2,0},{3,1},{4,6},{5,7},{6,4},{7,5},{8,10},{9,11},{10,... | collective-permute-start | bytes 786440 | tf_op jit(solution)/shard_map/ppermute | solution.py:353
  42.0 0.3 shard_map.94
  42.3 0.0 copy-start.8
  42.3 0.0 copy-start.9
  42.3 0.1 collective-permute-start.12
  42.4 1.7 %collective-permute-start.17 = (bf16[2,2,128,128]{3,2,1,0:T(8,128)(2,1)S(1)}, bf16[2,2,128,128]{3,2,1,0:T(8,128)(2,1)S(1)}, u32[]{:S(2)}, u32[]{:S(2)}) collective-permute-start(bf16[2,2,128,128]{3,2,1,0:T(8,128)(2,1)S(1)} %get-tuple-element.64), channel_id=1, source_target_pairs={{0,8},{1,9},{2,10},{3,11},{4,12},{5,13},{6,14},{7,15},{8,0},{9,1},... | collective-permute-start | bytes 393224 | tf_op jit(solution)/shard_map/ppermute | solution.py:353
  44.1 2.1 %collective-permute-start.18 = (bf16[2,2,128,128]{3,2,1,0:T(8,128)(2,1)S(1)}, bf16[2,2,128,128]{3,2,1,0:T(8,128)(2,1)S(1)}, u32[]{:S(2)}, u32[]{:S(2)}) collective-permute-start(bf16[2,2,128,128]{3,2,1,0:T(8,128)(2,1)S(1)} %get-tuple-element.65), channel_id=1, source_target_pairs={{0,12},{1,13},{2,14},{3,15},{4,0},{5,1},{6,2},{7,3},{8,4},{9,5},{1... | collective-permute-start | bytes 393224 | tf_op jit(solution)/shard_map/ppermute | solution.py:353
  46.2 0.6 collective-permute-start.23
  46.8 3.9 %collective-permute-done.12.refs_5_ = bf16[2,2,128,128]{3,2,1,0:T(8,128)(2,1)S(1)} collective-permute-done((bf16[2,2,128,128]{3,2,1,0:T(8,128)(2,1)S(1)}, bf16[2,2,128,128]{3,2,1,0:T(8,128)(2,1)S(1)}, u32[]{:S(2)}, u32[]{:S(2)}) %collective-permute-start.12) | collective-permute-done | bytes 131104 | tf_op jit(solution)/shard_map/ppermute | solution.py:353
  50.7 0.3 shard_map.95
  51.1 0.9 collective-permute-start.14
  52.0 2.2 %collective-permute-start.15 = (bf16[256,128]{1,0:T(8,128)(2,1)S(1)}, bf16[256,128]{1,0:T(8,128)(2,1)S(1)}, u32[]{:S(2)}, u32[]{:S(2)}) collective-permute-start(bf16[256,128]{1,0:T(8,128)(2,1)S(1)} %get-tuple-element.61), channel_id=1, source_target_pairs={{0,8},{1,9},{2,10},{3,11},{4,12},{5,13},{6,14},{7,15},{8,0},{9,1},... | collective-permute-start | bytes 196616 | tf_op jit(solution)/shard_map/ppermute | solution.py:353
  54.2 1.7 %collective-permute-done.17.refs_6_ = bf16[2,2,128,128]{3,2,1,0:T(8,128)(2,1)S(1)} collective-permute-done((bf16[2,2,128,128]{3,2,1,0:T(8,128)(2,1)S(1)}, bf16[2,2,128,128]{3,2,1,0:T(8,128)(2,1)S(1)}, u32[]{:S(2)}, u32[]{:S(2)}) %collective-permute-start.17) | collective-permute-done | bytes 131104 | tf_op jit(solution)/shard_map/ppermute | solution.py:353
  56.0 2.9 %collective-permute-start.16 = (bf16[256,128]{1,0:T(8,128)(2,1)S(1)}, bf16[256,128]{1,0:T(8,128)(2,1)S(1)}, u32[]{:S(2)}, u32[]{:S(2)}) collective-permute-start(bf16[256,128]{1,0:T(8,128)(2,1)S(1)} %get-tuple-element.62), channel_id=1, source_target_pairs={{0,12},{1,13},{2,14},{3,15},{4,0},{5,1},{6,2},{7,3},{8,4},{9,5},{1... | collective-permute-start | bytes 196616 | tf_op jit(solution)/shard_map/ppermute | solution.py:353
  58.9 4.6 %collective-permute-start.25 = (bf16[256,256]{1,0:T(8,128)(2,1)S(1)}, bf16[256,256]{1,0:T(8,128)(2,1)S(1)}, u32[]{:S(2)}, u32[]{:S(2)}) collective-permute-start(bf16[256,256]{1,0:T(8,128)(2,1)S(1)} %collective-permute-done.23.refs_5_), channel_id=1, source_target_pairs={{0,4},{1,5},{2,6},{3,7},{4,8},{5,9},{6,10},{7,11},{8,12},{9,13},{1... | collective-permute-start | bytes 393224 | tf_op jit(solution)/shard_map/ppermute | solution.py:353
  63.5 0.1 collective-permute-start.24
  63.6 0.8 collective-permute-done.15.refs_2_
  64.4 1.8 %shard_map.96 = (bf16[256,128]{1,0:T(8,128)(2,1)S(1)}, bf16[256,128]{1,0:T(8,128)(2,1)S(1)}, bf16[256,128]{1,0:T(8,128)(2,1)S(1)}, bf16[256,128]{1,0:T(8,128)(2,1)S(1)}) custom-call(bf16[256,128]{1,0:T(8,128)(2,1)S(1)} %get-tuple-element.59.refs_0_, bf16[256,128]{1,0:T(8,128)(2,1)S(1)} %collective-permute-done.14.refs_1_, ...), custom_call_target="tpu_custom_call" | custom-call | flops 1073741824 | bytes 5242880 | tf_op jit(solution)/shard_map/pallas_call | solution.py:37
  66.2 2.9 %collective-permute-start.19 = (bf16[256,128]{1,0:T(8,128)(2,1)S(1)}, bf16[256,128]{1,0:T(8,128)(2,1)S(1)}, u32[]{:S(2)}, u32[]{:S(2)}) collective-permute-start(bf16[256,128]{1,0:T(8,128)(2,1)S(1)} %get-tuple-element.67), channel_id=1, source_target_pairs={{0,4},{1,5},{2,6},{3,7},{4,8},{5,9},{6,10},{7,11},{8,12},{9,13},{1... | collective-permute-start | bytes 196616 | tf_op jit(solution)/shard_map/ppermute | solution.py:353
  69.1 0.7 collective-permute-start.20
  69.8 1.7 %collective-permute-start.21 = (bf16[256,128]{1,0:T(8,128)(2,1)S(1)}, bf16[256,128]{1,0:T(8,128)(2,1)S(1)}, u32[]{:S(2)}, u32[]{:S(2)}) collective-permute-start(bf16[256,128]{1,0:T(8,128)(2,1)S(1)} %get-tuple-element.69), channel_id=1, source_target_pairs={{0,12},{1,13},{2,14},{3,15},{4,0},{5,1},{6,2},{7,3},{8,4},{9,5},{1... | collective-permute-start | bytes 196616 | tf_op jit(solution)/shard_map/ppermute | solution.py:353
  71.5 1.6 %collective-permute-done.19.e1 = bf16[256,128]{1,0:T(8,128)(2,1)S(1)} collective-permute-done((bf16[256,128]{1,0:T(8,128)(2,1)S(1)}, bf16[256,128]{1,0:T(8,128)(2,1)S(1)}, u32[]{:S(2)}, u32[]{:S(2)}) %collective-permute-start.19) | collective-permute-done | bytes 65568 | tf_op jit(solution)/shard_map/ppermute | solution.py:353
  73.1 2.3 %collective-permute-done.20.e2 = bf16[256,128]{1,0:T(8,128)(2,1)S(1)} collective-permute-done((bf16[256,128]{1,0:T(8,128)(2,1)S(1)}, bf16[256,128]{1,0:T(8,128)(2,1)S(1)}, u32[]{:S(2)}, u32[]{:S(2)}) %collective-permute-start.20) | collective-permute-done | bytes 65568 | tf_op jit(solution)/shard_map/ppermute | solution.py:353
  75.4 0.2 shard_map.98
  75.6 0.1 collective-permute-start.26
  75.7 0.2 shard_map.97.gated
  75.9 0.5 collective-permute-start.22
  76.5 1.5 %collective-permute-done.22.other = bf16[512,256]{1,0:T(8,128)(2,1)S(1)} collective-permute-done((bf16[512,256]{1,0:T(8,128)(2,1)S(1)}, bf16[512,256]{1,0:T(8,128)(2,1)S(1)}, u32[]{:S(2)}, u32[]{:S(2)}) %collective-permute-start.22) | collective-permute-done | bytes 262176 | tf_op jit(solution)/shard_map/ppermute | solution.py:353
  77.9 0.8 shard_map.100
  78.8 2.3 %collective-permute-start.27 = (bf16[128,1024]{1,0:T(8,128)(2,1)S(1)}, bf16[128,1024]{1,0:T(8,128)(2,1)S(1)}, u32[]{:S(2)}, u32[]{:S(2)}) collective-permute-start(bf16[128,1024]{1,0:T(8,128)(2,1)S(1)} %get-tuple-element.78), channel_id=1, source_target_pairs={{0,18},{1,19},{2,16},{3,17},{4,22},{5,23},{6,20},{7,21},{8,26},{9,... | collective-permute-start | bytes 786440 | tf_op jit(solution)/shard_map/ppermute | solution.py:353
  81.1 0.4 collective-permute-start.28
  81.5 0.8 shard_map.99
  82.3 0.9 collective-permute-start.29
  83.2 5.7 %collective-permute-done.27 = bf16[128,1024]{1,0:T(8,128)(2,1)S(1)} collective-permute-done((bf16[128,1024]{1,0:T(8,128)(2,1)S(1)}, bf16[128,1024]{1,0:T(8,128)(2,1)S(1)}, u32[]{:S(2)}, u32[]{:S(2)}) %collective-permute-start.27) | collective-permute-done | bytes 262176 | tf_op jit(solution)/shard_map/ppermute | solution.py:353
  88.9 4.5 %collective-permute-done.28 = bf16[128,1024]{1,0:T(8,128)(2,1)S(1)} collective-permute-done((bf16[128,1024]{1,0:T(8,128)(2,1)S(1)}, bf16[128,1024]{1,0:T(8,128)(2,1)S(1)}, u32[]{:S(2)}, u32[]{:S(2)}) %collective-permute-start.28) | collective-permute-done | bytes 262176 | tf_op jit(solution)/shard_map/ppermute | solution.py:353
  93.5 0.2 collective-permute-done.29
  93.7 0.8 add_convert_fusion
  (34 shorter events, 0.1 us)
Async XLA Ops:
  0.0 1.0 %copy-start = (bf16[256,1024]{1,0:T(8,128)(2,1)S(1)}, bf16[256,1024]{1,0:T(8,128)(2,1)}, u32[]{:S(2)}) copy-start(bf16[256,1024]{1,0:T(8,128)(2,1)} %param.12) | copy-start | bytes 1572868
  1.1 3.1 %copy-start.2 = (bf16[256,512]{1,0:T(8,128)(2,1)}, bf16[256,512]{1,0:T(8,128)(2,1)S(1)}, u32[]{:S(2)}) copy-start(bf16[256,512]{1,0:T(8,128)(2,1)S(1)} %constant_dynamic-slice_fusion.after.w0) | copy-start | bytes 786436
  1.1 20.6 %copy-start.5 = (bf16[128,1024]{1,0:T(8,128)(2,1)S(1)}, bf16[128,1024]{1,0:T(8,128)(2,1)}, u32[]{:S(2)}) copy-start(bf16[128,1024]{1,0:T(8,128)(2,1)} %refs_0_.1) | copy-start | bytes 786436
  1.1 11.4 %collective-permute-start.1 = (bf16[256,512]{1,0:T(8,128)(2,1)S(1)}, bf16[256,512]{1,0:T(8,128)(2,1)S(1)}, u32[]{:S(2)}, u32[]{:S(2)}) collective-permute-start(bf16[256,512]{1,0:T(8,128)(2,1)S(1)} %constant_dynamic-slice_fusion.after.w0), channel_id=1, source_target_pairs={{0,4},{1,5},{2,6},{3,7},{4,8},{5,9},{6,10},{7,11},{8,12},{9,13},{1... | collective-permute-start | bytes 786440 | tf_op jit(solution)/shard_map/ppermute | solution.py:353
  6.8 9.5 %collective-permute-start = (bf16[128,1024]{1,0:T(8,128)(2,1)}, bf16[128,1024]{1,0:T(8,128)(2,1)S(1)}, u32[]{:S(2)}, u32[]{:S(2)}) collective-permute-start(bf16[128,1024]{1,0:T(8,128)(2,1)} %get-tuple-element.43), channel_id=1, source_target_pairs={{0,2},{1,3},{2,0},{3,1},{4,6},{5,7},{6,4},{7,5},{8,10},{9,11},{10,... | collective-permute-start | bytes 786440 | tf_op jit(solution)/shard_map/ppermute | solution.py:353
  8.3 13.3 %collective-permute-start.3 = (bf16[128,1024]{1,0:T(8,128)(2,1)}, bf16[128,1024]{1,0:T(8,128)(2,1)S(1)}, u32[]{:S(2)}, u32[]{:S(2)}) collective-permute-start(bf16[128,1024]{1,0:T(8,128)(2,1)} %get-tuple-element.47), channel_id=1, source_target_pairs={{0,16},{1,17},{2,18},{3,19},{4,20},{5,21},{6,22},{7,23},{8,24},{9,... | collective-permute-start | bytes 786440 | tf_op jit(solution)/shard_map/ppermute | solution.py:353
  9.8 11.8 %collective-permute-start.4 = (bf16[128,1024]{1,0:T(8,128)(2,1)}, bf16[128,1024]{1,0:T(8,128)(2,1)S(1)}, u32[]{:S(2)}, u32[]{:S(2)}) collective-permute-start(bf16[128,1024]{1,0:T(8,128)(2,1)} %get-tuple-element.48), channel_id=1, source_target_pairs={{0,18},{1,19},{2,16},{3,17},{4,22},{5,23},{6,20},{7,21},{8,26},{9,... | collective-permute-start | bytes 786440 | tf_op jit(solution)/shard_map/ppermute | solution.py:353
  12.5 9.3 %copy-start.12 = (bf16[256,256]{1,0:T(8,128)(2,1)S(1)}, bf16[256,256]{1,0:T(8,128)(2,1)}, u32[]{:S(2)}) copy-start(bf16[256,256]{1,0:T(8,128)(2,1)} %get-tuple-element.51) | copy-start | bytes 393220
  12.5 10.6 %copy-start.11 = (bf16[2,2,128,256]{3,2,1,0:T(8,128)(2,1)S(1)}, bf16[2,2,128,256]{3,2,1,0:T(8,128)(2,1)}, u32[]{:S(2)}) copy-start(bf16[2,2,128,256]{3,2,1,0:T(8,128)(2,1)} %get-tuple-element.53) | copy-start | bytes 786436
  12.5 26.9 %copy-start.3 = (bf16[256,512]{1,0:T(8,128)(2,1)S(1)}, bf16[256,512]{1,0:T(8,128)(2,1)}, u32[]{:S(2)}) copy-start(bf16[256,512]{1,0:T(8,128)(2,1)} %copy-done.2) | copy-start | bytes 786436
  12.5 8.4 %collective-permute-start.2 = (bf16[256,256]{1,0:T(8,128)(2,1)}, bf16[256,256]{1,0:T(8,128)(2,1)S(1)}, u32[]{:S(2)}, u32[]{:S(2)}) collective-permute-start(bf16[256,256]{1,0:T(8,128)(2,1)} %get-tuple-element.45.refs_0_), channel_id=1, source_target_pairs={{0,4},{1,5},{2,6},{3,7},{4,8},{5,9},{6,10},{7,11},{8,12},{9,13},{1... | collective-permute-start | bytes 393224 | tf_op jit(solution)/shard_map/ppermute | solution.py:353
  12.5 12.3 %collective-permute-start.5 = (bf16[256,512]{1,0:T(8,128)(2,1)S(1)}, bf16[256,512]{1,0:T(8,128)(2,1)S(1)}, u32[]{:S(2)}, u32[]{:S(2)}) collective-permute-start(bf16[256,512]{1,0:T(8,128)(2,1)S(1)} %collective-permute-done.1.w1), channel_id=1, source_target_pairs={{0,4},{1,5},{2,6},{3,7},{4,8},{5,9},{6,10},{7,11},{8,12},{9,13},{1... | collective-permute-start | bytes 786440 | tf_op jit(solution)/shard_map/ppermute | solution.py:353
  21.7 17.7 %collective-permute-start.10 = (bf16[512,512]{1,0:T(8,128)(2,1)S(1)}, bf16[512,512]{1,0:T(8,128)(2,1)S(1)}, u32[]{:S(2)}, u32[]{:S(2)}) collective-permute-start(bf16[512,512]{1,0:T(8,128)(2,1)S(1)} %shard_map.92.mine), channel_id=1, source_target_pairs={{0,1},{1,0},{2,3},{3,2},{4,5},{5,4},{6,7},{7,6},{8,9},{9,8},{10,11... | collective-permute-start | bytes 1572872 | tf_op jit(solution)/shard_map/ppermute | solution.py:353
  21.8 6.4 %collective-permute-start.7 = (bf16[256,256]{1,0:T(8,128)(2,1)S(1)}, bf16[256,256]{1,0:T(8,128)(2,1)S(1)}, u32[]{:S(2)}, u32[]{:S(2)}) collective-permute-start(bf16[256,256]{1,0:T(8,128)(2,1)S(1)} %copy-done.12), channel_id=1, source_target_pairs={{0,2},{1,3},{2,0},{3,1},{4,6},{5,7},{6,4},{7,5},{8,10},{9,11},{10,... | collective-permute-start | bytes 393224 | tf_op jit(solution)/shard_map/ppermute | solution.py:353
  23.1 18.9 %copy-start.1 = (bf16[2,2,128,1024]{3,2,1,0:T(8,128)(2,1)S(1)}, bf16[2,2,128,1024]{3,2,1,0:T(8,128)(2,1)}, u32[]{:S(2)}) copy-start(bf16[2,2,128,1024]{3,2,1,0:T(8,128)(2,1)} %filt.3) | copy-start | bytes 3145732
  23.1 10.2 %collective-permute-start.9 = (bf16[2,2,128,256]{3,2,1,0:T(8,128)(2,1)S(1)}, bf16[2,2,128,256]{3,2,1,0:T(8,128)(2,1)S(1)}, u32[]{:S(2)}, u32[]{:S(2)}) collective-permute-start(bf16[2,2,128,256]{3,2,1,0:T(8,128)(2,1)S(1)} %copy-done.11), channel_id=1, source_target_pairs={{0,2},{1,3},{2,0},{3,1},{4,6},{5,7},{6,4},{7,5},{8,10},{9,11},{10,... | collective-permute-start | bytes 786440 | tf_op jit(solution)/shard_map/ppermute | solution.py:353
  24.8 14.6 %collective-permute-start.11 = (bf16[256,512]{1,0:T(8,128)(2,1)S(1)}, bf16[256,512]{1,0:T(8,128)(2,1)S(1)}, u32[]{:S(2)}, u32[]{:S(2)}) collective-permute-start(bf16[256,512]{1,0:T(8,128)(2,1)S(1)} %collective-permute-done.5.w2), channel_id=1, source_target_pairs={{0,4},{1,5},{2,6},{3,7},{4,8},{5,9},{6,10},{7,11},{8,12},{9,13},{1... | collective-permute-start | bytes 786440 | tf_op jit(solution)/shard_map/ppermute | solution.py:353
  25.4 12.5 %collective-permute-start.6 = (bf16[256,256]{1,0:T(8,128)(2,1)S(1)}, bf16[256,256]{1,0:T(8,128)(2,1)S(1)}, u32[]{:S(2)}, u32[]{:S(2)}) collective-permute-start(bf16[256,256]{1,0:T(8,128)(2,1)S(1)} %collective-permute-done.2.refs_2_), channel_id=1, source_target_pairs={{0,4},{1,5},{2,6},{3,7},{4,8},{5,9},{6,10},{7,11},{8,12},{9,13},{1... | collective-permute-start | bytes 393224 | tf_op jit(solution)/shard_map/ppermute | solution.py:353
  28.1 11.2 %collective-permute-start.8 = (bf16[256,256]{1,0:T(8,128)(2,1)S(1)}, bf16[256,256]{1,0:T(8,128)(2,1)S(1)}, u32[]{:S(2)}, u32[]{:S(2)}) collective-permute-start(bf16[256,256]{1,0:T(8,128)(2,1)S(1)} %collective-permute-done.7.refs_1_), channel_id=1, source_target_pairs={{0,4},{1,5},{2,6},{3,7},{4,8},{5,9},{6,10},{7,11},{8,12},{9,13},{1... | collective-permute-start | bytes 393224 | tf_op jit(solution)/shard_map/ppermute | solution.py:353
  40.7 10.0 %copy-start.4 = (bf16[128,1024]{1,0:T(8,128)(2,1)S(1)}, bf16[128,1024]{1,0:T(8,128)(2,1)}, u32[]{:S(2)}) copy-start(bf16[128,1024]{1,0:T(8,128)(2,1)} %g0.2) | copy-start | bytes 786436
  40.7 10.0 %collective-permute-start.13 = (bf16[512,256]{1,0:T(8,128)(2,1)S(1)}, bf16[512,256]{1,0:T(8,128)(2,1)S(1)}, u32[]{:S(2)}, u32[]{:S(2)}) collective-permute-start(bf16[512,256]{1,0:T(8,128)(2,1)S(1)} %get-tuple-element.58), channel_id=1, source_target_pairs={{0,2},{1,3},{2,0},{3,1},{4,6},{5,7},{6,4},{7,5},{8,10},{9,11},{10,... | collective-permute-start | bytes 786440 | tf_op jit(solution)/shard_map/ppermute | solution.py:353
  42.0 22.4 %copy-start.10 = (bf16[16,256,128]{2,1,0:T(8,128)(2,1)S(1)}, bf16[16,256,128]{2,1,0:T(8,128)(2,1)}, u32[]{:S(2)}) copy-start(bf16[16,256,128]{2,1,0:T(8,128)(2,1)} %constant.17.clone.refs_9_) | copy-start | bytes 3145732
  42.3 8.4 %copy-start.8 = (f32[1024]{0:T(1024)S(1)}, f32[1024]{0:T(1024)}, u32[]{:S(2)}) copy-start(f32[1024]{0:T(1024)} %param.13) | copy-start | bytes 12292
  42.3 22.1 %copy-start.9 = (bf16[16,256,128]{2,1,0:T(8,128)(2,1)S(1)}, bf16[16,256,128]{2,1,0:T(8,128)(2,1)}, u32[]{:S(2)}) copy-start(bf16[16,256,128]{2,1,0:T(8,128)(2,1)} %constant.16.clone.refs_8_) | copy-start | bytes 3145732
  42.3 8.4 %collective-permute-start.12 = (bf16[2,2,128,128]{3,2,1,0:T(8,128)(2,1)S(1)}, bf16[2,2,128,128]{3,2,1,0:T(8,128)(2,1)S(1)}, u32[]{:S(2)}, u32[]{:S(2)}) collective-permute-start(bf16[2,2,128,128]{3,2,1,0:T(8,128)(2,1)S(1)} %get-tuple-element.56), channel_id=1, source_target_pairs={{0,4},{1,5},{2,6},{3,7},{4,8},{5,9},{6,10},{7,11},{8,12},{9,13},{1... | collective-permute-start | bytes 393224 | tf_op jit(solution)/shard_map/ppermute | solution.py:353
  42.4 13.6 %collective-permute-start.17 = (bf16[2,2,128,128]{3,2,1,0:T(8,128)(2,1)S(1)}, bf16[2,2,128,128]{3,2,1,0:T(8,128)(2,1)S(1)}, u32[]{:S(2)}, u32[]{:S(2)}) collective-permute-start(bf16[2,2,128,128]{3,2,1,0:T(8,128)(2,1)S(1)} %get-tuple-element.64), channel_id=1, source_target_pairs={{0,8},{1,9},{2,10},{3,11},{4,12},{5,13},{6,14},{7,15},{8,0},{9,1},... | collective-permute-start | bytes 393224 | tf_op jit(solution)/shard_map/ppermute | solution.py:353
  44.1 14.8 %collective-permute-start.18 = (bf16[2,2,128,128]{3,2,1,0:T(8,128)(2,1)S(1)}, bf16[2,2,128,128]{3,2,1,0:T(8,128)(2,1)S(1)}, u32[]{:S(2)}, u32[]{:S(2)}) collective-permute-start(bf16[2,2,128,128]{3,2,1,0:T(8,128)(2,1)S(1)} %get-tuple-element.65), channel_id=1, source_target_pairs={{0,12},{1,13},{2,14},{3,15},{4,0},{5,1},{6,2},{7,3},{8,4},{9,5},{1... | collective-permute-start | bytes 393224 | tf_op jit(solution)/shard_map/ppermute | solution.py:353
  46.2 12.7 %collective-permute-start.23 = (bf16[256,256]{1,0:T(8,128)(2,1)S(1)}, bf16[256,256]{1,0:T(8,128)(2,1)S(1)}, u32[]{:S(2)}, u32[]{:S(2)}) collective-permute-start(bf16[256,256]{1,0:T(8,128)(2,1)S(1)} %collective-permute-done.8.refs_3_), channel_id=1, source_target_pairs={{0,4},{1,5},{2,6},{3,7},{4,8},{5,9},{6,10},{7,11},{8,12},{9,13},{1... | collective-permute-start | bytes 393224 | tf_op jit(solution)/shard_map/ppermute | solution.py:353
  51.1 7.8 %collective-permute-start.14 = (bf16[256,128]{1,0:T(8,128)(2,1)S(1)}, bf16[256,128]{1,0:T(8,128)(2,1)S(1)}, u32[]{:S(2)}, u32[]{:S(2)}) collective-permute-start(bf16[256,128]{1,0:T(8,128)(2,1)S(1)} %get-tuple-element.60), channel_id=1, source_target_pairs={{0,4},{1,5},{2,6},{3,7},{4,8},{5,9},{6,10},{7,11},{8,12},{9,13},{1... | collective-permute-start | bytes 196616 | tf_op jit(solution)/shard_map/ppermute | solution.py:353
  52.0 12.4 %collective-permute-start.15 = (bf16[256,128]{1,0:T(8,128)(2,1)S(1)}, bf16[256,128]{1,0:T(8,128)(2,1)S(1)}, u32[]{:S(2)}, u32[]{:S(2)}) collective-permute-start(bf16[256,128]{1,0:T(8,128)(2,1)S(1)} %get-tuple-element.61), channel_id=1, source_target_pairs={{0,8},{1,9},{2,10},{3,11},{4,12},{5,13},{6,14},{7,15},{8,0},{9,1},... | collective-permute-start | bytes 196616 | tf_op jit(solution)/shard_map/ppermute | solution.py:353
  56.0 8.4 %collective-permute-start.16 = (bf16[256,128]{1,0:T(8,128)(2,1)S(1)}, bf16[256,128]{1,0:T(8,128)(2,1)S(1)}, u32[]{:S(2)}, u32[]{:S(2)}) collective-permute-start(bf16[256,128]{1,0:T(8,128)(2,1)S(1)} %get-tuple-element.62), channel_id=1, source_target_pairs={{0,12},{1,13},{2,14},{3,15},{4,0},{5,1},{6,2},{7,3},{8,4},{9,5},{1... | collective-permute-start | bytes 196616 | tf_op jit(solution)/shard_map/ppermute | solution.py:353
  58.9 16.5 %collective-permute-start.25 = (bf16[256,256]{1,0:T(8,128)(2,1)S(1)}, bf16[256,256]{1,0:T(8,128)(2,1)S(1)}, u32[]{:S(2)}, u32[]{:S(2)}) collective-permute-start(bf16[256,256]{1,0:T(8,128)(2,1)S(1)} %collective-permute-done.23.refs_5_), channel_id=1, source_target_pairs={{0,4},{1,5},{2,6},{3,7},{4,8},{5,9},{6,10},{7,11},{8,12},{9,13},{1... | collective-permute-start | bytes 393224 | tf_op jit(solution)/shard_map/ppermute | solution.py:353
  63.5 11.9 %collective-permute-start.24 = (bf16[256,256]{1,0:T(8,128)(2,1)S(1)}, bf16[256,256]{1,0:T(8,128)(2,1)S(1)}, u32[]{:S(2)}, u32[]{:S(2)}) collective-permute-start(bf16[256,256]{1,0:T(8,128)(2,1)S(1)} %collective-permute-done.6.refs_4_), channel_id=1, source_target_pairs={{0,4},{1,5},{2,6},{3,7},{4,8},{5,9},{6,10},{7,11},{8,12},{9,13},{1... | collective-permute-start | bytes 393224 | tf_op jit(solution)/shard_map/ppermute | solution.py:353
  64.4 11.0 %copy-start.7 = (bf16[256,256]{1,0:T(8,128)(2,1)S(1)}, bf16[256,256]{1,0:T(8,128)(2,1)}, u32[]{:S(2)}) copy-start(bf16[256,256]{1,0:T(8,128)(2,1)} %get-tuple-element.45.refs_0_) | copy-start | bytes 393220
  66.2 6.9 %collective-permute-start.19 = (bf16[256,128]{1,0:T(8,128)(2,1)S(1)}, bf16[256,128]{1,0:T(8,128)(2,1)S(1)}, u32[]{:S(2)}, u32[]{:S(2)}) collective-permute-start(bf16[256,128]{1,0:T(8,128)(2,1)S(1)} %get-tuple-element.67), channel_id=1, source_target_pairs={{0,4},{1,5},{2,6},{3,7},{4,8},{5,9},{6,10},{7,11},{8,12},{9,13},{1... | collective-permute-start | bytes 196616 | tf_op jit(solution)/shard_map/ppermute | solution.py:353
  69.1 6.3 %collective-permute-start.20 = (bf16[256,128]{1,0:T(8,128)(2,1)S(1)}, bf16[256,128]{1,0:T(8,128)(2,1)S(1)}, u32[]{:S(2)}, u32[]{:S(2)}) collective-permute-start(bf16[256,128]{1,0:T(8,128)(2,1)S(1)} %get-tuple-element.68), channel_id=1, source_target_pairs={{0,8},{1,9},{2,10},{3,11},{4,12},{5,13},{6,14},{7,15},{8,0},{9,1},... | collective-permute-start | bytes 196616 | tf_op jit(solution)/shard_map/ppermute | solution.py:353
  69.8 5.9 %copy-start.6 = (bf16[128,1024]{1,0:T(8,128)(2,1)S(1)}, bf16[128,1024]{1,0:T(8,128)(2,1)}, u32[]{:S(2)}) copy-start(bf16[128,1024]{1,0:T(8,128)(2,1)} %g0.3) | copy-start | bytes 786436
  69.8 5.6 %collective-permute-start.21 = (bf16[256,128]{1,0:T(8,128)(2,1)S(1)}, bf16[256,128]{1,0:T(8,128)(2,1)S(1)}, u32[]{:S(2)}, u32[]{:S(2)}) collective-permute-start(bf16[256,128]{1,0:T(8,128)(2,1)S(1)} %get-tuple-element.69), channel_id=1, source_target_pairs={{0,12},{1,13},{2,14},{3,15},{4,0},{5,1},{6,2},{7,3},{8,4},{9,5},{1... | collective-permute-start | bytes 196616 | tf_op jit(solution)/shard_map/ppermute | solution.py:353
  75.6 2.4 %collective-permute-start.26 = (bf16[4,256,256]{2,1,0:T(8,128)(2,1)S(1)}, bf16[4,256,256]{2,1,0:T(8,128)(2,1)S(1)}, u32[]{:S(2)}, u32[]{:S(2)}) collective-permute-start(bf16[4,256,256]{2,1,0:T(8,128)(2,1)S(1)} %get-tuple-element.76), channel_id=1, source_target_pairs={{0,1},{1,0},{2,3},{3,2},{4,5},{5,4},{6,7},{7,6},{8,9},{9,8},{10,11... | collective-permute-start | bytes 1572872 | tf_op jit(solution)/shard_map/ppermute | solution.py:353
  75.9 2.0 %collective-permute-start.22 = (bf16[512,256]{1,0:T(8,128)(2,1)S(1)}, bf16[512,256]{1,0:T(8,128)(2,1)S(1)}, u32[]{:S(2)}, u32[]{:S(2)}) collective-permute-start(bf16[512,256]{1,0:T(8,128)(2,1)S(1)} %shard_map.97.gated), channel_id=1, source_target_pairs={{0,1},{1,0},{2,3},{3,2},{4,5},{5,4},{6,7},{7,6},{8,9},{9,8},{10,11... | collective-permute-start | bytes 786440 | tf_op jit(solution)/shard_map/ppermute | solution.py:353
  78.8 10.2 %collective-permute-start.27 = (bf16[128,1024]{1,0:T(8,128)(2,1)S(1)}, bf16[128,1024]{1,0:T(8,128)(2,1)S(1)}, u32[]{:S(2)}, u32[]{:S(2)}) collective-permute-start(bf16[128,1024]{1,0:T(8,128)(2,1)S(1)} %get-tuple-element.78), channel_id=1, source_target_pairs={{0,18},{1,19},{2,16},{3,17},{4,22},{5,23},{6,20},{7,21},{8,26},{9,... | collective-permute-start | bytes 786440 | tf_op jit(solution)/shard_map/ppermute | solution.py:353
  81.1 12.4 %collective-permute-start.28 = (bf16[128,1024]{1,0:T(8,128)(2,1)S(1)}, bf16[128,1024]{1,0:T(8,128)(2,1)S(1)}, u32[]{:S(2)}, u32[]{:S(2)}) collective-permute-start(bf16[128,1024]{1,0:T(8,128)(2,1)S(1)} %get-tuple-element.79), channel_id=1, source_target_pairs={{0,2},{1,3},{2,0},{3,1},{4,6},{5,7},{6,4},{7,5},{8,10},{9,11},{10,... | collective-permute-start | bytes 786440 | tf_op jit(solution)/shard_map/ppermute | solution.py:353
  82.3 11.4 %collective-permute-start.29 = (bf16[128,1024]{1,0:T(8,128)(2,1)S(1)}, bf16[128,1024]{1,0:T(8,128)(2,1)S(1)}, u32[]{:S(2)}, u32[]{:S(2)}) collective-permute-start(bf16[128,1024]{1,0:T(8,128)(2,1)S(1)} %get-tuple-element.80), channel_id=1, source_target_pairs={{0,16},{1,17},{2,18},{3,19},{4,20},{5,21},{6,22},{7,23},{8,24},{9,... | collective-permute-start | bytes 786440 | tf_op jit(solution)/shard_map/ppermute | solution.py:353

commit v14 on v12

--- a/solution.py
+++ b/solution.py
@@ -50,6 +50,11 @@
 def place():
     y, s, c = (lax.axis_index(a) for a in AXES)
     return y, lax.rem(s, 2), lax.div(s, 2), c
+
+
+def before(z, r):
+    at = lax.rem((z ^ lax.div(z, 2)) - r + 4, 4)
+    return at ^ lax.div(at, 2)
 
 
 def low_lanes(shape):
@@ -141,7 +146,7 @@
 def value_kernel(mine, other, w0, w1, w2, w3, keep, give, acc):
     _, x, z, c = place()
     for r, piece in enumerate((w0, w1, w2, w3)):
-        owner = lax.rem(z - r + 4, 4)
+        owner = before(z, r)
         lanes = pl.ds(pl.multiple_of(lax.rem(owner, 2) * 256, 256), 256)
 
         @pl.when(lax.div(owner, 2) == c)
@@ -311,7 +316,7 @@
     pieces, keep, give = refs[:8], refs[8], refs[9]
     _, x, z, c = place()
     for r in range(4):
-        owner = lax.rem(z - r + 4, 4)
+        owner = before(z, r)
         for k in range(2):
             to = 2 * lax.rem(owner, 2) + (1 - x if k else x)
 
@@ -357,6 +362,10 @@
 
     def to_core(values):
         return permute(values, lambda g, z, x, k: (g, z, x, 1 - k))
+
+    def onward(values):
+        ring = (1, 3, 0, 2)
+        return permute(values, lambda g, z, x, k: (g, ring[z], x, k))
 
     def to_z(values, r):
         return permute(values, lambda g, z, x, k: (g, (z + r) % deep, x, k))
@@ -383,15 +392,15 @@
         moved=1 << 20,
     )(filter_spectrum, near)
     filters = [filters[0]] + [to_z(filters[r], r) for r in (1, 2, 3)]
-    v1 = to_z(own_v, 1)
-    q1 = to_z(own_o, 1)
-    v2 = to_z(v1, 1)
-    q2 = to_z(after(q1, v1), 1)
+    v1 = onward(own_v)
+    q1 = onward(own_o)
+    v2 = onward(v1)
+    q2 = onward(after(q1, v1))
     mine = in_vmem(join_tokens, shape((512, 512), BF16), moved=1 << 20)(tokens, after(received[0], q2), *received[1:])
-    v3 = to_z(v2, 1)
+    v3 = onward(v2)
     other = to_core(mine)
     got_o = to_x(after(away_o, v1))
-    r1 = to_z(after(got_o, v2), 1)
+    r1 = onward(after(got_o, v2))
     keep, give = in_vmem(
         value_kernel,
         [shape((512, 256), F32), shape((512, 256), BF16)],
@@ -399,7 +408,7 @@
         flops=1 << 29,
         moved=2 << 20,
     )(after(mine, r1, near), other, own_v, v1, v2, v3)
-    r2 = to_z(after(r1, keep), 1)
+    r2 = onward(after(r1, keep))
     drive, *sends = in_vmem(
         drive_kernel,
         [shape((512, 256), F32)] + [block] * 4,
@@ -407,8 +416,8 @@
         moved=2 << 20,
     )(after(keep, filters[1]), to_x(give), gate_k, *received, skip[None, :])
     columns = [sends[0]] + [to_z(sends[r], r) for r in (1, 2, 3)]
-    r3 = to_z(after(r2, *filters[2:], columns[1]), 1)
-    q3 = to_z(after(q2, *columns[1:]), 1)
+    r3 = onward(after(r2, *filters[2:], columns[1]))
+    q3 = onward(after(q2, *columns[1:]))
     table, table_t = tables()
     sends = in_vmem(
         conv_kernel,

time: 94.5 us -> 92.9 us (0.983)
  waiting for transfers between devices: 47.3 us -> 45.1 us
    ppermute x30, waiting for transfers between devices: 47.3 us -> 45.1 us  [permute(): return lax.ppermute(values, AXES, pairs)]
  transfers between devices with their start and end apart: 30 -> 30, of which waited for: 17 -> 17; matrix products, arithmetic and copies ran while one was open for 0% -> 0% of each run, Pallas kernels for 6% -> 7%
where the time goes in v14:
time: 92.9 us; the launch traced here: 92.7 us
  waiting for transfers between devices  45.1 us (49%)
  starting transfers between devices  37 us (40%)
  Pallas kernels  8.4 us (9%)
  local copies, waits for them, and re-layouts  1.12 us (1%)
    ppermute x30, waiting for transfers between devices, permute(): return lax.ppermute(values, AXES, pairs)  45.1 us
    ppermute x30, starting transfers between devices, permute(): return lax.ppermute(values, AXES, pairs)  37 us
    pallas_call x9, Pallas kernels, call(): pl.pallas_call(kernel, out_shape=out_shape, in_specs=specs, out_specs=jax...  5.83 us
    pallas_call x1, Pallas kernels, call(): pl.pallas_call(kernel, out_shape=out_shape, in_specs=[pl.BlockSpec(memory...  2.58 us
  transfers between devices with their start and end apart: 30, of which 17 were waited for; matrix products, arithmetic and copies ran while one was open for 0% of the time, Pallas kernels for 7%

profile of v14, /device:TPU:0, one launch (start us, length us, event | category | flops | bytes accessed | tf_op | source)
XLA Modules:
  0.0 92.7 jit_solution(3212823948889829241)
XLA Ops:
  0.0 1.0 %copy-done = bf16[256,1024]{1,0:T(8,128)(2,1)S(1)} copy-done((bf16[256,1024]{1,0:T(8,128)(2,1)S(1)}, bf16[256,1024]{1,0:T(8,128)(2,1)}, u32[]{:S(2)}) %copy-start) | copy-done | bytes 524312
  1.1 0.0 copy-start.2
  1.1 0.0 copy-start.5
  1.1 3.1 %collective-permute-start.2 = (bf16[256,512]{1,0:T(8,128)(2,1)S(1)}, bf16[256,512]{1,0:T(8,128)(2,1)S(1)}, u32[]{:S(2)}, u32[]{:S(2)}) collective-permute-start(bf16[256,512]{1,0:T(8,128)(2,1)S(1)} %constant_dynamic-slice_fusion.after.w0), channel_id=1, source_target_pairs={{0,4},{1,5},{2,6},{3,7},{4,12},{5,13},{6,14},{7,15},{8,0},{9,1},{1... | collective-permute-start | bytes 786440 | tf_op jit(solution)/shard_map/ppermute | solution.py:358
  4.2 2.6 %shard_map.91 = (bf16[128,1024]{1,0:T(8,128)(2,1)}, bf16[128,1024]{1,0:T(8,128)(2,1)}, bf16[128,1024]{1,0:T(8,128)(2,1)}, bf16[256,256]{1,0:T(8,128)(2,1)}, bf16...) custom-call(bf16[128,1024]{1,0:T(8,128)(2,1)} %refs_0_.1, bf16[128,1024]{1,0:T(8,128)(2,1)} %g0.2, ...), custom_call_target="tpu_custom_call" | custom-call | tf_op jit(solution)/shard_map/pallas_call | solution.py:106
  6.8 2.6 %collective-permute-start.1 = (bf16[256,256]{1,0:T(8,128)(2,1)}, bf16[256,256]{1,0:T(8,128)(2,1)S(1)}, u32[]{:S(2)}, u32[]{:S(2)}) collective-permute-start(bf16[256,256]{1,0:T(8,128)(2,1)} %get-tuple-element.43.refs_0_), channel_id=1, source_target_pairs={{0,4},{1,5},{2,6},{3,7},{4,12},{5,13},{6,14},{7,15},{8,0},{9,1},{1... | collective-permute-start | bytes 393224 | tf_op jit(solution)/shard_map/ppermute | solution.py:358
  9.4 1.5 %collective-permute-start = (bf16[128,1024]{1,0:T(8,128)(2,1)}, bf16[128,1024]{1,0:T(8,128)(2,1)S(1)}, u32[]{:S(2)}, u32[]{:S(2)}) collective-permute-start(bf16[128,1024]{1,0:T(8,128)(2,1)} %get-tuple-element.42), channel_id=1, source_target_pairs={{0,2},{1,3},{2,0},{3,1},{4,6},{5,7},{6,4},{7,5},{8,10},{9,11},{10,... | collective-permute-start | bytes 786440 | tf_op jit(solution)/shard_map/ppermute | solution.py:358
  10.9 1.5 %collective-permute-start.4 = (bf16[128,1024]{1,0:T(8,128)(2,1)}, bf16[128,1024]{1,0:T(8,128)(2,1)S(1)}, u32[]{:S(2)}, u32[]{:S(2)}) collective-permute-start(bf16[128,1024]{1,0:T(8,128)(2,1)} %get-tuple-element.46), channel_id=1, source_target_pairs={{0,16},{1,17},{2,18},{3,19},{4,20},{5,21},{6,22},{7,23},{8,24},{9,... | collective-permute-start | bytes 786440 | tf_op jit(solution)/shard_map/ppermute | solution.py:358
  12.4 0.5 collective-permute-start.5
  12.9 1.4 %collective-permute-done.1.refs_2_ = bf16[256,256]{1,0:T(8,128)(2,1)S(1)} collective-permute-done((bf16[256,256]{1,0:T(8,128)(2,1)}, bf16[256,256]{1,0:T(8,128)(2,1)S(1)}, u32[]{:S(2)}, u32[]{:S(2)}) %collective-permute-start.1) | collective-permute-done | bytes 131104 | tf_op jit(solution)/shard_map/ppermute | solution.py:358
  14.3 0.9 %collective-permute-start.3 = (bf16[256,256]{1,0:T(8,128)(2,1)S(1)}, bf16[256,256]{1,0:T(8,128)(2,1)S(1)}, u32[]{:S(2)}, u32[]{:S(2)}) collective-permute-start(bf16[256,256]{1,0:T(8,128)(2,1)S(1)} %collective-permute-done.1.refs_2_), channel_id=1, source_target_pairs={{0,4},{1,5},{2,6},{3,7},{4,12},{5,13},{6,14},{7,15},{8,0},{9,1},{1... | collective-permute-start | bytes 393224 | tf_op jit(solution)/shard_map/ppermute | solution.py:358
  15.2 3.3 %collective-permute-start.7 = (bf16[256,512]{1,0:T(8,128)(2,1)S(1)}, bf16[256,512]{1,0:T(8,128)(2,1)S(1)}, u32[]{:S(2)}, u32[]{:S(2)}) collective-permute-start(bf16[256,512]{1,0:T(8,128)(2,1)S(1)} %collective-permute-done.2.w1), channel_id=1, source_target_pairs={{0,4},{1,5},{2,6},{3,7},{4,12},{5,13},{6,14},{7,15},{8,0},{9,1},{1... | collective-permute-start | bytes 786440 | tf_op jit(solution)/shard_map/ppermute | solution.py:358
  18.5 0.3 collective-permute-done.refs_1_.g1
  18.9 2.8 %collective-permute-done.3.refs_4_ = bf16[256,256]{1,0:T(8,128)(2,1)S(1)} collective-permute-done((bf16[256,256]{1,0:T(8,128)(2,1)S(1)}, bf16[256,256]{1,0:T(8,128)(2,1)S(1)}, u32[]{:S(2)}, u32[]{:S(2)}) %collective-permute-start.3) | collective-permute-done | bytes 131104 | tf_op jit(solution)/shard_map/ppermute | solution.py:358
  21.6 2.3 %collective-permute-done.4.refs_2_.g2 = bf16[128,1024]{1,0:T(8,128)(2,1)S(1)} collective-permute-done((bf16[128,1024]{1,0:T(8,128)(2,1)}, bf16[128,1024]{1,0:T(8,128)(2,1)S(1)}, u32[]{:S(2)}, u32[]{:S(2)}) %collective-permute-start.4) | collective-permute-done | bytes 262176 | tf_op jit(solution)/shard_map/ppermute | solution.py:358
  24.0 0.1 collective-permute-start.10
  24.1 1.3 %collective-permute-start.6 = (bf16[256,256]{1,0:T(8,128)(2,1)S(1)}, bf16[256,256]{1,0:T(8,128)(2,1)S(1)}, u32[]{:S(2)}, u32[]{:S(2)}) collective-permute-start(bf16[256,256]{1,0:T(8,128)(2,1)S(1)} %copy-done.12), channel_id=1, source_target_pairs={{0,2},{1,3},{2,0},{3,1},{4,6},{5,7},{6,4},{7,5},{8,10},{9,11},{10,... | collective-permute-start | bytes 393224 | tf_op jit(solution)/shard_map/ppermute | solution.py:358
  25.4 0.8 collective-permute-start.9
  26.2 0.0 collective-permute-done.7.w2
  26.2 0.9 collective-permute-start.11
  27.1 3.4 %collective-permute-done.6.refs_1_ = bf16[256,256]{1,0:T(8,128)(2,1)S(1)} collective-permute-done((bf16[256,256]{1,0:T(8,128)(2,1)S(1)}, bf16[256,256]{1,0:T(8,128)(2,1)S(1)}, u32[]{:S(2)}, u32[]{:S(2)}) %collective-permute-start.6) | collective-permute-done | bytes 131104 | tf_op jit(solution)/shard_map/ppermute | solution.py:358
  30.4 0.9 collective-permute-start.8
  31.3 4.3 %collective-permute-done.9.near = bf16[2,2,128,256]{3,2,1,0:T(8,128)(2,1)S(1)} collective-permute-done((bf16[2,2,128,256]{3,2,1,0:T(8,128)(2,1)S(1)}, bf16[2,2,128,256]{3,2,1,0:T(8,128)(2,1)S(1)}, u32[]{:S(2)}, u32[]{:S(2)}) %collective-permute-start.9) | collective-permute-done | bytes 262176 | tf_op jit(solution)/shard_map/ppermute | solution.py:358
  35.6 2.4 %collective-permute-done.8.refs_3_ = bf16[256,256]{1,0:T(8,128)(2,1)S(1)} collective-permute-done((bf16[256,256]{1,0:T(8,128)(2,1)S(1)}, bf16[256,256]{1,0:T(8,128)(2,1)S(1)}, u32[]{:S(2)}, u32[]{:S(2)}) %collective-permute-start.8) | collective-permute-done | bytes 131104 | tf_op jit(solution)/shard_map/ppermute | solution.py:358
  38.0 1.3 %shard_map.93 = (f32[512,256]{1,0:T(8,128)S(1)}, bf16[512,256]{1,0:T(8,128)(2,1)S(1)}) custom-call(bf16[512,512]{1,0:T(8,128)(2,1)S(1)} %shard_map.92.mine, bf16[512,512]{1,0:T(8,128)(2,1)S(1)} %collective-permute-done.10.other, bf16[256,512]{1,0:T(8,128)(2,1)S(1)} %copy-done.3, bf16[256,512]{1,0:T(8,128)(2,1)S(1)} %collective-permute-done.2.w1, ...), custom_call_target="tpu_custom_call" | custom-call | flops 536870912 | bytes 2097152 | tf_op jit(solution)/shard_map/pallas_call | solution.py:37
  39.3 0.0 copy-start.4
  39.3 1.3 %collective-permute-start.13 = (bf16[512,256]{1,0:T(8,128)(2,1)S(1)}, bf16[512,256]{1,0:T(8,128)(2,1)S(1)}, u32[]{:S(2)}, u32[]{:S(2)}) collective-permute-start(bf16[512,256]{1,0:T(8,128)(2,1)S(1)} %get-tuple-element.56), channel_id=1, source_target_pairs={{0,2},{1,3},{2,0},{3,1},{4,6},{5,7},{6,4},{7,5},{8,10},{9,11},{10,... | collective-permute-start | bytes 786440 | tf_op jit(solution)/shard_map/ppermute | solution.py:358
  40.6 0.3 shard_map.94
  40.9 0.0 copy-start.8
  40.9 0.0 copy-start.9
  40.9 0.1 collective-permute-start.12
  41.0 2.2 %collective-permute-start.17 = (bf16[2,2,128,128]{3,2,1,0:T(8,128)(2,1)S(1)}, bf16[2,2,128,128]{3,2,1,0:T(8,128)(2,1)S(1)}, u32[]{:S(2)}, u32[]{:S(2)}) collective-permute-start(bf16[2,2,128,128]{3,2,1,0:T(8,128)(2,1)S(1)} %get-tuple-element.62), channel_id=1, source_target_pairs={{0,8},{1,9},{2,10},{3,11},{4,12},{5,13},{6,14},{7,15},{8,0},{9,1},... | collective-permute-start | bytes 393224 | tf_op jit(solution)/shard_map/ppermute | solution.py:358
  43.2 1.6 %collective-permute-start.18 = (bf16[2,2,128,128]{3,2,1,0:T(8,128)(2,1)S(1)}, bf16[2,2,128,128]{3,2,1,0:T(8,128)(2,1)S(1)}, u32[]{:S(2)}, u32[]{:S(2)}) collective-permute-start(bf16[2,2,128,128]{3,2,1,0:T(8,128)(2,1)S(1)} %get-tuple-element.63), channel_id=1, source_target_pairs={{0,12},{1,13},{2,14},{3,15},{4,0},{5,1},{6,2},{7,3},{8,4},{9,5},{1... | collective-permute-start | bytes 393224 | tf_op jit(solution)/shard_map/ppermute | solution.py:358
  44.8 0.6 collective-permute-start.23
  45.4 3.9 %collective-permute-done.12.refs_5_ = bf16[2,2,128,128]{3,2,1,0:T(8,128)(2,1)S(1)} collective-permute-done((bf16[2,2,128,128]{3,2,1,0:T(8,128)(2,1)S(1)}, bf16[2,2,128,128]{3,2,1,0:T(8,128)(2,1)S(1)}, u32[]{:S(2)}, u32[]{:S(2)}) %collective-permute-start.12) | collective-permute-done | bytes 131104 | tf_op jit(solution)/shard_map/ppermute | solution.py:358
  49.3 0.3 shard_map.95
  49.6 0.1 collective-permute-start.14
  49.7 0.1 collective-permute-start.15
  49.8 3.0 %collective-permute-done.17.refs_6_ = bf16[2,2,128,128]{3,2,1,0:T(8,128)(2,1)S(1)} collective-permute-done((bf16[2,2,128,128]{3,2,1,0:T(8,128)(2,1)S(1)}, bf16[2,2,128,128]{3,2,1,0:T(8,128)(2,1)S(1)}, u32[]{:S(2)}, u32[]{:S(2)}) %collective-permute-start.17) | collective-permute-done | bytes 131104 | tf_op jit(solution)/shard_map/ppermute | solution.py:358
  52.8 3.6 %collective-permute-start.16 = (bf16[256,128]{1,0:T(8,128)(2,1)S(1)}, bf16[256,128]{1,0:T(8,128)(2,1)S(1)}, u32[]{:S(2)}, u32[]{:S(2)}) collective-permute-start(bf16[256,128]{1,0:T(8,128)(2,1)S(1)} %get-tuple-element.60), channel_id=1, source_target_pairs={{0,12},{1,13},{2,14},{3,15},{4,0},{5,1},{6,2},{7,3},{8,4},{9,5},{1... | collective-permute-start | bytes 196616 | tf_op jit(solution)/shard_map/ppermute | solution.py:358
  56.4 0.0 collective-permute-done.18.refs_7_
  56.4 4.8 %collective-permute-done.23.refs_5_ = bf16[256,256]{1,0:T(8,128)(2,1)S(1)} collective-permute-done((bf16[256,256]{1,0:T(8,128)(2,1)S(1)}, bf16[256,256]{1,0:T(8,128)(2,1)S(1)}, u32[]{:S(2)}, u32[]{:S(2)}) %collective-permute-start.23) | collective-permute-done | bytes 131104 | tf_op jit(solution)/shard_map/ppermute | solution.py:358
  61.2 1.1 %collective-permute-done.15.refs_2_ = bf16[256,128]{1,0:T(8,128)(2,1)S(1)} collective-permute-done((bf16[256,128]{1,0:T(8,128)(2,1)S(1)}, bf16[256,128]{1,0:T(8,128)(2,1)S(1)}, u32[]{:S(2)}, u32[]{:S(2)}) %collective-permute-start.15) | collective-permute-done | bytes 65568 | tf_op jit(solution)/shard_map/ppermute | solution.py:358
  62.3 1.4 %collective-permute-start.24 = (bf16[256,256]{1,0:T(8,128)(2,1)S(1)}, bf16[256,256]{1,0:T(8,128)(2,1)S(1)}, u32[]{:S(2)}, u32[]{:S(2)}) collective-permute-start(bf16[256,256]{1,0:T(8,128)(2,1)S(1)} %collective-permute-done.3.refs_4_), channel_id=1, source_target_pairs={{0,4},{1,5},{2,6},{3,7},{4,12},{5,13},{6,14},{7,15},{8,0},{9,1},{1... | collective-permute-start | bytes 393224 | tf_op jit(solution)/shard_map/ppermute | solution.py:358
  63.7 1.8 %shard_map.96 = (bf16[256,128]{1,0:T(8,128)(2,1)S(1)}, bf16[256,128]{1,0:T(8,128)(2,1)S(1)}, bf16[256,128]{1,0:T(8,128)(2,1)S(1)}, bf16[256,128]{1,0:T(8,128)(2,1)S(1)}) custom-call(bf16[256,128]{1,0:T(8,128)(2,1)S(1)} %get-tuple-element.57.refs_0_, bf16[256,128]{1,0:T(8,128)(2,1)S(1)} %collective-permute-done.14.refs_1_, ...), custom_call_target="tpu_custom_call" | custom-call | flops 1073741824 | bytes 5242880 | tf_op jit(solution)/shard_map/pallas_call | solution.py:37
  65.5 1.1 %collective-permute-start.19 = (bf16[256,128]{1,0:T(8,128)(2,1)S(1)}, bf16[256,128]{1,0:T(8,128)(2,1)S(1)}, u32[]{:S(2)}, u32[]{:S(2)}) collective-permute-start(bf16[256,128]{1,0:T(8,128)(2,1)S(1)} %get-tuple-element.65), channel_id=1, source_target_pairs={{0,4},{1,5},{2,6},{3,7},{4,8},{5,9},{6,10},{7,11},{8,12},{9,13},{1... | collective-permute-start | bytes 196616 | tf_op jit(solution)/shard_map/ppermute | solution.py:358
  66.6 1.4 %collective-permute-start.20 = (bf16[256,128]{1,0:T(8,128)(2,1)S(1)}, bf16[256,128]{1,0:T(8,128)(2,1)S(1)}, u32[]{:S(2)}, u32[]{:S(2)}) collective-permute-start(bf16[256,128]{1,0:T(8,128)(2,1)S(1)} %get-tuple-element.66), channel_id=1, source_target_pairs={{0,8},{1,9},{2,10},{3,11},{4,12},{5,13},{6,14},{7,15},{8,0},{9,1},... | collective-permute-start | bytes 196616 | tf_op jit(solution)/shard_map/ppermute | solution.py:358
  68.0 2.0 %collective-permute-start.21 = (bf16[256,128]{1,0:T(8,128)(2,1)S(1)}, bf16[256,128]{1,0:T(8,128)(2,1)S(1)}, u32[]{:S(2)}, u32[]{:S(2)}) collective-permute-start(bf16[256,128]{1,0:T(8,128)(2,1)S(1)} %get-tuple-element.67), channel_id=1, source_target_pairs={{0,12},{1,13},{2,14},{3,15},{4,0},{5,1},{6,2},{7,3},{8,4},{9,5},{1... | collective-permute-start | bytes 196616 | tf_op jit(solution)/shard_map/ppermute | solution.py:358
  70.0 1.7 %collective-permute-done.19.e1 = bf16[256,128]{1,0:T(8,128)(2,1)S(1)} collective-permute-done((bf16[256,128]{1,0:T(8,128)(2,1)S(1)}, bf16[256,128]{1,0:T(8,128)(2,1)S(1)}, u32[]{:S(2)}, u32[]{:S(2)}) %collective-permute-start.19) | collective-permute-done | bytes 65568 | tf_op jit(solution)/shard_map/ppermute | solution.py:358
  71.7 1.8 %collective-permute-done.20.e2 = bf16[256,128]{1,0:T(8,128)(2,1)S(1)} collective-permute-done((bf16[256,128]{1,0:T(8,128)(2,1)S(1)}, bf16[256,128]{1,0:T(8,128)(2,1)S(1)}, u32[]{:S(2)}, u32[]{:S(2)}) %collective-permute-start.20) | collective-permute-done | bytes 65568 | tf_op jit(solution)/shard_map/ppermute | solution.py:358
  73.6 0.2 shard_map.98
  73.8 0.1 collective-permute-start.26
  73.8 0.2 shard_map.97.gated
  74.1 0.5 collective-permute-start.22
  74.6 1.5 %collective-permute-done.22.other = bf16[512,256]{1,0:T(8,128)(2,1)S(1)} collective-permute-done((bf16[512,256]{1,0:T(8,128)(2,1)S(1)}, bf16[512,256]{1,0:T(8,128)(2,1)S(1)}, u32[]{:S(2)}, u32[]{:S(2)}) %collective-permute-start.22) | collective-permute-done | bytes 262176 | tf_op jit(solution)/shard_map/ppermute | solution.py:358
  76.1 0.8 shard_map.100
  76.9 1.8 %collective-permute-start.27 = (bf16[128,1024]{1,0:T(8,128)(2,1)S(1)}, bf16[128,1024]{1,0:T(8,128)(2,1)S(1)}, u32[]{:S(2)}, u32[]{:S(2)}) collective-permute-start(bf16[128,1024]{1,0:T(8,128)(2,1)S(1)} %get-tuple-element.76), channel_id=1, source_target_pairs={{0,18},{1,19},{2,16},{3,17},{4,22},{5,23},{6,20},{7,21},{8,26},{9,... | collective-permute-start | bytes 786440 | tf_op jit(solution)/shard_map/ppermute | solution.py:358
  78.7 0.5 collective-permute-start.28
  79.2 0.8 shard_map.99
  80.0 1.3 %collective-permute-start.29 = (bf16[128,1024]{1,0:T(8,128)(2,1)S(1)}, bf16[128,1024]{1,0:T(8,128)(2,1)S(1)}, u32[]{:S(2)}, u32[]{:S(2)}) collective-permute-start(bf16[128,1024]{1,0:T(8,128)(2,1)S(1)} %get-tuple-element.78), channel_id=1, source_target_pairs={{0,16},{1,17},{2,18},{3,19},{4,20},{5,21},{6,22},{7,23},{8,24},{9,... | collective-permute-start | bytes 786440 | tf_op jit(solution)/shard_map/ppermute | solution.py:358
  81.4 5.7 %collective-permute-done.27 = bf16[128,1024]{1,0:T(8,128)(2,1)S(1)} collective-permute-done((bf16[128,1024]{1,0:T(8,128)(2,1)S(1)}, bf16[128,1024]{1,0:T(8,128)(2,1)S(1)}, u32[]{:S(2)}, u32[]{:S(2)}) %collective-permute-start.27) | collective-permute-done | bytes 262176 | tf_op jit(solution)/shard_map/ppermute | solution.py:358
  87.1 4.1 %collective-permute-done.28 = bf16[128,1024]{1,0:T(8,128)(2,1)S(1)} collective-permute-done((bf16[128,1024]{1,0:T(8,128)(2,1)S(1)}, bf16[128,1024]{1,0:T(8,128)(2,1)S(1)}, u32[]{:S(2)}, u32[]{:S(2)}) %collective-permute-start.28) | collective-permute-done | bytes 262176 | tf_op jit(solution)/shard_map/ppermute | solution.py:358
  91.2 0.7 collective-permute-done.29
  91.9 0.8 add_convert_fusion
  (34 shorter events, 0.1 us)
Async XLA Ops:
  0.0 1.0 %copy-start = (bf16[256,1024]{1,0:T(8,128)(2,1)S(1)}, bf16[256,1024]{1,0:T(8,128)(2,1)}, u32[]{:S(2)}) copy-start(bf16[256,1024]{1,0:T(8,128)(2,1)} %param.12) | copy-start | bytes 1572868
  1.1 3.1 %copy-start.2 = (bf16[256,512]{1,0:T(8,128)(2,1)}, bf16[256,512]{1,0:T(8,128)(2,1)S(1)}, u32[]{:S(2)}) copy-start(bf16[256,512]{1,0:T(8,128)(2,1)S(1)} %constant_dynamic-slice_fusion.after.w0) | copy-start | bytes 786436
  1.1 22.8 %copy-start.5 = (bf16[128,1024]{1,0:T(8,128)(2,1)S(1)}, bf16[128,1024]{1,0:T(8,128)(2,1)}, u32[]{:S(2)}) copy-start(bf16[128,1024]{1,0:T(8,128)(2,1)} %refs_0_.1) | copy-start | bytes 786436
  1.1 13.2 %collective-permute-start.2 = (bf16[256,512]{1,0:T(8,128)(2,1)S(1)}, bf16[256,512]{1,0:T(8,128)(2,1)S(1)}, u32[]{:S(2)}, u32[]{:S(2)}) collective-permute-start(bf16[256,512]{1,0:T(8,128)(2,1)S(1)} %constant_dynamic-slice_fusion.after.w0), channel_id=1, source_target_pairs={{0,4},{1,5},{2,6},{3,7},{4,12},{5,13},{6,14},{7,15},{8,0},{9,1},{1... | collective-permute-start | bytes 786440 | tf_op jit(solution)/shard_map/ppermute | solution.py:358
  6.8 7.5 %collective-permute-start.1 = (bf16[256,256]{1,0:T(8,128)(2,1)}, bf16[256,256]{1,0:T(8,128)(2,1)S(1)}, u32[]{:S(2)}, u32[]{:S(2)}) collective-permute-start(bf16[256,256]{1,0:T(8,128)(2,1)} %get-tuple-element.43.refs_0_), channel_id=1, source_target_pairs={{0,4},{1,5},{2,6},{3,7},{4,12},{5,13},{6,14},{7,15},{8,0},{9,1},{1... | collective-permute-start | bytes 393224 | tf_op jit(solution)/shard_map/ppermute | solution.py:358
  9.4 9.5 %collective-permute-start = (bf16[128,1024]{1,0:T(8,128)(2,1)}, bf16[128,1024]{1,0:T(8,128)(2,1)S(1)}, u32[]{:S(2)}, u32[]{:S(2)}) collective-permute-start(bf16[128,1024]{1,0:T(8,128)(2,1)} %get-tuple-element.42), channel_id=1, source_target_pairs={{0,2},{1,3},{2,0},{3,1},{4,6},{5,7},{6,4},{7,5},{8,10},{9,11},{10,... | collective-permute-start | bytes 786440 | tf_op jit(solution)/shard_map/ppermute | solution.py:358
  10.9 13.0 %collective-permute-start.4 = (bf16[128,1024]{1,0:T(8,128)(2,1)}, bf16[128,1024]{1,0:T(8,128)(2,1)S(1)}, u32[]{:S(2)}, u32[]{:S(2)}) collective-permute-start(bf16[128,1024]{1,0:T(8,128)(2,1)} %get-tuple-element.46), channel_id=1, source_target_pairs={{0,16},{1,17},{2,18},{3,19},{4,20},{5,21},{6,22},{7,23},{8,24},{9,... | collective-permute-start | bytes 786440 | tf_op jit(solution)/shard_map/ppermute | solution.py:358
  12.4 11.6 %copy-start.12 = (bf16[256,256]{1,0:T(8,128)(2,1)S(1)}, bf16[256,256]{1,0:T(8,128)(2,1)}, u32[]{:S(2)}) copy-start(bf16[256,256]{1,0:T(8,128)(2,1)} %get-tuple-element.49) | copy-start | bytes 393220
  12.4 13.0 %copy-start.11 = (bf16[2,2,128,256]{3,2,1,0:T(8,128)(2,1)S(1)}, bf16[2,2,128,256]{3,2,1,0:T(8,128)(2,1)}, u32[]{:S(2)}) copy-start(bf16[2,2,128,256]{3,2,1,0:T(8,128)(2,1)} %get-tuple-element.51) | copy-start | bytes 786436
  12.4 25.6 %copy-start.3 = (bf16[256,512]{1,0:T(8,128)(2,1)S(1)}, bf16[256,512]{1,0:T(8,128)(2,1)}, u32[]{:S(2)}) copy-start(bf16[256,512]{1,0:T(8,128)(2,1)} %copy-done.2) | copy-start | bytes 786436
  12.4 11.5 %collective-permute-start.5 = (bf16[128,1024]{1,0:T(8,128)(2,1)}, bf16[128,1024]{1,0:T(8,128)(2,1)S(1)}, u32[]{:S(2)}, u32[]{:S(2)}) collective-permute-start(bf16[128,1024]{1,0:T(8,128)(2,1)} %get-tuple-element.47), channel_id=1, source_target_pairs={{0,18},{1,19},{2,16},{3,17},{4,22},{5,23},{6,20},{7,21},{8,26},{9,... | collective-permute-start | bytes 786440 | tf_op jit(solution)/shard_map/ppermute | solution.py:358
  14.3 7.3 %collective-permute-start.3 = (bf16[256,256]{1,0:T(8,128)(2,1)S(1)}, bf16[256,256]{1,0:T(8,128)(2,1)S(1)}, u32[]{:S(2)}, u32[]{:S(2)}) collective-permute-start(bf16[256,256]{1,0:T(8,128)(2,1)S(1)} %collective-permute-done.1.refs_2_), channel_id=1, source_target_pairs={{0,4},{1,5},{2,6},{3,7},{4,12},{5,13},{6,14},{7,15},{8,0},{9,1},{1... | collective-permute-start | bytes 393224 | tf_op jit(solution)/shard_map/ppermute | solution.py:358
  15.2 10.9 %collective-permute-start.7 = (bf16[256,512]{1,0:T(8,128)(2,1)S(1)}, bf16[256,512]{1,0:T(8,128)(2,1)S(1)}, u32[]{:S(2)}, u32[]{:S(2)}) collective-permute-start(bf16[256,512]{1,0:T(8,128)(2,1)S(1)} %collective-permute-done.2.w1), channel_id=1, source_target_pairs={{0,4},{1,5},{2,6},{3,7},{4,12},{5,13},{6,14},{7,15},{8,0},{9,1},{1... | collective-permute-start | bytes 786440 | tf_op jit(solution)/shard_map/ppermute | solution.py:358
  24.0 14.0 %collective-permute-start.10 = (bf16[512,512]{1,0:T(8,128)(2,1)S(1)}, bf16[512,512]{1,0:T(8,128)(2,1)S(1)}, u32[]{:S(2)}, u32[]{:S(2)}) collective-permute-start(bf16[512,512]{1,0:T(8,128)(2,1)S(1)} %shard_map.92.mine), channel_id=1, source_target_pairs={{0,1},{1,0},{2,3},{3,2},{4,5},{5,4},{6,7},{7,6},{8,9},{9,8},{10,11... | collective-permute-start | bytes 1572872 | tf_op jit(solution)/shard_map/ppermute | solution.py:358
  24.1 6.4 %collective-permute-start.6 = (bf16[256,256]{1,0:T(8,128)(2,1)S(1)}, bf16[256,256]{1,0:T(8,128)(2,1)S(1)}, u32[]{:S(2)}, u32[]{:S(2)}) collective-permute-start(bf16[256,256]{1,0:T(8,128)(2,1)S(1)} %copy-done.12), channel_id=1, source_target_pairs={{0,2},{1,3},{2,0},{3,1},{4,6},{5,7},{6,4},{7,5},{8,10},{9,11},{10,... | collective-permute-start | bytes 393224 | tf_op jit(solution)/shard_map/ppermute | solution.py:358
  25.4 15.2 %copy-start.1 = (bf16[2,2,128,1024]{3,2,1,0:T(8,128)(2,1)S(1)}, bf16[2,2,128,1024]{3,2,1,0:T(8,128)(2,1)}, u32[]{:S(2)}) copy-start(bf16[2,2,128,1024]{3,2,1,0:T(8,128)(2,1)} %filt.3) | copy-start | bytes 3145732
  25.4 10.2 %collective-permute-start.9 = (bf16[2,2,128,256]{3,2,1,0:T(8,128)(2,1)S(1)}, bf16[2,2,128,256]{3,2,1,0:T(8,128)(2,1)S(1)}, u32[]{:S(2)}, u32[]{:S(2)}) collective-permute-start(bf16[2,2,128,256]{3,2,1,0:T(8,128)(2,1)S(1)} %copy-done.11), channel_id=1, source_target_pairs={{0,2},{1,3},{2,0},{3,1},{4,6},{5,7},{6,4},{7,5},{8,10},{9,11},{10,... | collective-permute-start | bytes 786440 | tf_op jit(solution)/shard_map/ppermute | solution.py:358
  26.2 11.8 %collective-permute-start.11 = (bf16[256,512]{1,0:T(8,128)(2,1)S(1)}, bf16[256,512]{1,0:T(8,128)(2,1)S(1)}, u32[]{:S(2)}, u32[]{:S(2)}) collective-permute-start(bf16[256,512]{1,0:T(8,128)(2,1)S(1)} %collective-permute-done.7.w2), channel_id=1, source_target_pairs={{0,4},{1,5},{2,6},{3,7},{4,12},{5,13},{6,14},{7,15},{8,0},{9,1},{1... | collective-permute-start | bytes 786440 | tf_op jit(solution)/shard_map/ppermute | solution.py:358
  30.4 7.5 %collective-permute-start.8 = (bf16[256,256]{1,0:T(8,128)(2,1)S(1)}, bf16[256,256]{1,0:T(8,128)(2,1)S(1)}, u32[]{:S(2)}, u32[]{:S(2)}) collective-permute-start(bf16[256,256]{1,0:T(8,128)(2,1)S(1)} %collective-permute-done.6.refs_1_), channel_id=1, source_target_pairs={{0,4},{1,5},{2,6},{3,7},{4,12},{5,13},{6,14},{7,15},{8,0},{9,1},{1... | collective-permute-start | bytes 393224 | tf_op jit(solution)/shard_map/ppermute | solution.py:358
  39.3 10.0 %copy-start.4 = (bf16[128,1024]{1,0:T(8,128)(2,1)S(1)}, bf16[128,1024]{1,0:T(8,128)(2,1)}, u32[]{:S(2)}) copy-start(bf16[128,1024]{1,0:T(8,128)(2,1)} %g0.2) | copy-start | bytes 786436
  39.3 10.0 %collective-permute-start.13 = (bf16[512,256]{1,0:T(8,128)(2,1)S(1)}, bf16[512,256]{1,0:T(8,128)(2,1)S(1)}, u32[]{:S(2)}, u32[]{:S(2)}) collective-permute-start(bf16[512,256]{1,0:T(8,128)(2,1)S(1)} %get-tuple-element.56), channel_id=1, source_target_pairs={{0,2},{1,3},{2,0},{3,1},{4,6},{5,7},{6,4},{7,5},{8,10},{9,11},{10,... | collective-permute-start | bytes 786440 | tf_op jit(solution)/shard_map/ppermute | solution.py:358
  40.6 23.1 %copy-start.10 = (bf16[16,256,128]{2,1,0:T(8,128)(2,1)S(1)}, bf16[16,256,128]{2,1,0:T(8,128)(2,1)}, u32[]{:S(2)}) copy-start(bf16[16,256,128]{2,1,0:T(8,128)(2,1)} %constant.17.clone.refs_9_) | copy-start | bytes 3145732
  40.9 8.4 %copy-start.8 = (f32[1024]{0:T(1024)S(1)}, f32[1024]{0:T(1024)}, u32[]{:S(2)}) copy-start(f32[1024]{0:T(1024)} %param.13) | copy-start | bytes 12292
  40.9 22.8 %copy-start.9 = (bf16[16,256,128]{2,1,0:T(8,128)(2,1)S(1)}, bf16[16,256,128]{2,1,0:T(8,128)(2,1)}, u32[]{:S(2)}) copy-start(bf16[16,256,128]{2,1,0:T(8,128)(2,1)} %constant.16.clone.refs_8_) | copy-start | bytes 3145732
  40.9 8.3 %collective-permute-start.12 = (bf16[2,2,128,128]{3,2,1,0:T(8,128)(2,1)S(1)}, bf16[2,2,128,128]{3,2,1,0:T(8,128)(2,1)S(1)}, u32[]{:S(2)}, u32[]{:S(2)}) collective-permute-start(bf16[2,2,128,128]{3,2,1,0:T(8,128)(2,1)S(1)} %get-tuple-element.54), channel_id=1, source_target_pairs={{0,4},{1,5},{2,6},{3,7},{4,8},{5,9},{6,10},{7,11},{8,12},{9,13},{1... | collective-permute-start | bytes 393224 | tf_op jit(solution)/shard_map/ppermute | solution.py:358
  41.0 11.7 %collective-permute-start.17 = (bf16[2,2,128,128]{3,2,1,0:T(8,128)(2,1)S(1)}, bf16[2,2,128,128]{3,2,1,0:T(8,128)(2,1)S(1)}, u32[]{:S(2)}, u32[]{:S(2)}) collective-permute-start(bf16[2,2,128,128]{3,2,1,0:T(8,128)(2,1)S(1)} %get-tuple-element.62), channel_id=1, source_target_pairs={{0,8},{1,9},{2,10},{3,11},{4,12},{5,13},{6,14},{7,15},{8,0},{9,1},... | collective-permute-start | bytes 393224 | tf_op jit(solution)/shard_map/ppermute | solution.py:358
  43.2 13.2 %collective-permute-start.18 = (bf16[2,2,128,128]{3,2,1,0:T(8,128)(2,1)S(1)}, bf16[2,2,128,128]{3,2,1,0:T(8,128)(2,1)S(1)}, u32[]{:S(2)}, u32[]{:S(2)}) collective-permute-start(bf16[2,2,128,128]{3,2,1,0:T(8,128)(2,1)S(1)} %get-tuple-element.63), channel_id=1, source_target_pairs={{0,12},{1,13},{2,14},{3,15},{4,0},{5,1},{6,2},{7,3},{8,4},{9,5},{1... | collective-permute-start | bytes 393224 | tf_op jit(solution)/shard_map/ppermute | solution.py:358
  44.8 16.4 %collective-permute-start.23 = (bf16[256,256]{1,0:T(8,128)(2,1)S(1)}, bf16[256,256]{1,0:T(8,128)(2,1)S(1)}, u32[]{:S(2)}, u32[]{:S(2)}) collective-permute-start(bf16[256,256]{1,0:T(8,128)(2,1)S(1)} %collective-permute-done.8.refs_3_), channel_id=1, source_target_pairs={{0,4},{1,5},{2,6},{3,7},{4,12},{5,13},{6,14},{7,15},{8,0},{9,1},{1... | collective-permute-start | bytes 393224 | tf_op jit(solution)/shard_map/ppermute | solution.py:358
  49.6 11.5 %collective-permute-start.14 = (bf16[256,128]{1,0:T(8,128)(2,1)S(1)}, bf16[256,128]{1,0:T(8,128)(2,1)S(1)}, u32[]{:S(2)}, u32[]{:S(2)}) collective-permute-start(bf16[256,128]{1,0:T(8,128)(2,1)S(1)} %get-tuple-element.58), channel_id=1, source_target_pairs={{0,4},{1,5},{2,6},{3,7},{4,8},{5,9},{6,10},{7,11},{8,12},{9,13},{1... | collective-permute-start | bytes 196616 | tf_op jit(solution)/shard_map/ppermute | solution.py:358
  49.7 12.6 %collective-permute-start.15 = (bf16[256,128]{1,0:T(8,128)(2,1)S(1)}, bf16[256,128]{1,0:T(8,128)(2,1)S(1)}, u32[]{:S(2)}, u32[]{:S(2)}) collective-permute-start(bf16[256,128]{1,0:T(8,128)(2,1)S(1)} %get-tuple-element.59), channel_id=1, source_target_pairs={{0,8},{1,9},{2,10},{3,11},{4,12},{5,13},{6,14},{7,15},{8,0},{9,1},... | collective-permute-start | bytes 196616 | tf_op jit(solution)/shard_map/ppermute | solution.py:358
  52.8 9.6 %collective-permute-start.16 = (bf16[256,128]{1,0:T(8,128)(2,1)S(1)}, bf16[256,128]{1,0:T(8,128)(2,1)S(1)}, u32[]{:S(2)}, u32[]{:S(2)}) collective-permute-start(bf16[256,128]{1,0:T(8,128)(2,1)S(1)} %get-tuple-element.60), channel_id=1, source_target_pairs={{0,12},{1,13},{2,14},{3,15},{4,0},{5,1},{6,2},{7,3},{8,4},{9,5},{1... | collective-permute-start | bytes 196616 | tf_op jit(solution)/shard_map/ppermute | solution.py:358
  61.2 12.4 %collective-permute-start.25 = (bf16[256,256]{1,0:T(8,128)(2,1)S(1)}, bf16[256,256]{1,0:T(8,128)(2,1)S(1)}, u32[]{:S(2)}, u32[]{:S(2)}) collective-permute-start(bf16[256,256]{1,0:T(8,128)(2,1)S(1)} %collective-permute-done.23.refs_5_), channel_id=1, source_target_pairs={{0,4},{1,5},{2,6},{3,7},{4,12},{5,13},{6,14},{7,15},{8,0},{9,1},{1... | collective-permute-start | bytes 393224 | tf_op jit(solution)/shard_map/ppermute | solution.py:358
  62.3 11.2 %collective-permute-start.24 = (bf16[256,256]{1,0:T(8,128)(2,1)S(1)}, bf16[256,256]{1,0:T(8,128)(2,1)S(1)}, u32[]{:S(2)}, u32[]{:S(2)}) collective-permute-start(bf16[256,256]{1,0:T(8,128)(2,1)S(1)} %collective-permute-done.3.refs_4_), channel_id=1, source_target_pairs={{0,4},{1,5},{2,6},{3,7},{4,12},{5,13},{6,14},{7,15},{8,0},{9,1},{1... | collective-permute-start | bytes 393224 | tf_op jit(solution)/shard_map/ppermute | solution.py:358
  63.7 9.9 %copy-start.7 = (bf16[256,256]{1,0:T(8,128)(2,1)S(1)}, bf16[256,256]{1,0:T(8,128)(2,1)}, u32[]{:S(2)}) copy-start(bf16[256,256]{1,0:T(8,128)(2,1)} %get-tuple-element.43.refs_0_) | copy-start | bytes 393220
  65.5 6.2 %collective-permute-start.19 = (bf16[256,128]{1,0:T(8,128)(2,1)S(1)}, bf16[256,128]{1,0:T(8,128)(2,1)S(1)}, u32[]{:S(2)}, u32[]{:S(2)}) collective-permute-start(bf16[256,128]{1,0:T(8,128)(2,1)S(1)} %get-tuple-element.65), channel_id=1, source_target_pairs={{0,4},{1,5},{2,6},{3,7},{4,8},{5,9},{6,10},{7,11},{8,12},{9,13},{1... | collective-permute-start | bytes 196616 | tf_op jit(solution)/shard_map/ppermute | solution.py:358
  66.6 7.0 %collective-permute-start.20 = (bf16[256,128]{1,0:T(8,128)(2,1)S(1)}, bf16[256,128]{1,0:T(8,128)(2,1)S(1)}, u32[]{:S(2)}, u32[]{:S(2)}) collective-permute-start(bf16[256,128]{1,0:T(8,128)(2,1)S(1)} %get-tuple-element.66), channel_id=1, source_target_pairs={{0,8},{1,9},{2,10},{3,11},{4,12},{5,13},{6,14},{7,15},{8,0},{9,1},... | collective-permute-start | bytes 196616 | tf_op jit(solution)/shard_map/ppermute | solution.py:358
  68.0 5.8 %copy-start.6 = (bf16[128,1024]{1,0:T(8,128)(2,1)S(1)}, bf16[128,1024]{1,0:T(8,128)(2,1)}, u32[]{:S(2)}) copy-start(bf16[128,1024]{1,0:T(8,128)(2,1)} %g0.3) | copy-start | bytes 786436
  68.0 5.5 %collective-permute-start.21 = (bf16[256,128]{1,0:T(8,128)(2,1)S(1)}, bf16[256,128]{1,0:T(8,128)(2,1)S(1)}, u32[]{:S(2)}, u32[]{:S(2)}) collective-permute-start(bf16[256,128]{1,0:T(8,128)(2,1)S(1)} %get-tuple-element.67), channel_id=1, source_target_pairs={{0,12},{1,13},{2,14},{3,15},{4,0},{5,1},{6,2},{7,3},{8,4},{9,5},{1... | collective-permute-start | bytes 196616 | tf_op jit(solution)/shard_map/ppermute | solution.py:358
  73.8 2.4 %collective-permute-start.26 = (bf16[4,256,256]{2,1,0:T(8,128)(2,1)S(1)}, bf16[4,256,256]{2,1,0:T(8,128)(2,1)S(1)}, u32[]{:S(2)}, u32[]{:S(2)}) collective-permute-start(bf16[4,256,256]{2,1,0:T(8,128)(2,1)S(1)} %get-tuple-element.74), channel_id=1, source_target_pairs={{0,1},{1,0},{2,3},{3,2},{4,5},{5,4},{6,7},{7,6},{8,9},{9,8},{10,11... | collective-permute-start | bytes 1572872 | tf_op jit(solution)/shard_map/ppermute | solution.py:358
  74.1 2.0 %collective-permute-start.22 = (bf16[512,256]{1,0:T(8,128)(2,1)S(1)}, bf16[512,256]{1,0:T(8,128)(2,1)S(1)}, u32[]{:S(2)}, u32[]{:S(2)}) collective-permute-start(bf16[512,256]{1,0:T(8,128)(2,1)S(1)} %shard_map.97.gated), channel_id=1, source_target_pairs={{0,1},{1,0},{2,3},{3,2},{4,5},{5,4},{6,7},{7,6},{8,9},{9,8},{10,11... | collective-permute-start | bytes 786440 | tf_op jit(solution)/shard_map/ppermute | solution.py:358
  76.9 10.2 %collective-permute-start.27 = (bf16[128,1024]{1,0:T(8,128)(2,1)S(1)}, bf16[128,1024]{1,0:T(8,128)(2,1)S(1)}, u32[]{:S(2)}, u32[]{:S(2)}) collective-permute-start(bf16[128,1024]{1,0:T(8,128)(2,1)S(1)} %get-tuple-element.76), channel_id=1, source_target_pairs={{0,18},{1,19},{2,16},{3,17},{4,22},{5,23},{6,20},{7,21},{8,26},{9,... | collective-permute-start | bytes 786440 | tf_op jit(solution)/shard_map/ppermute | solution.py:358
  78.7 12.5 %collective-permute-start.28 = (bf16[128,1024]{1,0:T(8,128)(2,1)S(1)}, bf16[128,1024]{1,0:T(8,128)(2,1)S(1)}, u32[]{:S(2)}, u32[]{:S(2)}) collective-permute-start(bf16[128,1024]{1,0:T(8,128)(2,1)S(1)} %get-tuple-element.77), channel_id=1, source_target_pairs={{0,2},{1,3},{2,0},{3,1},{4,6},{5,7},{6,4},{7,5},{8,10},{9,11},{10,... | collective-permute-start | bytes 786440 | tf_op jit(solution)/shard_map/ppermute | solution.py:358
  80.0 11.8 %collective-permute-start.29 = (bf16[128,1024]{1,0:T(8,128)(2,1)S(1)}, bf16[128,1024]{1,0:T(8,128)(2,1)S(1)}, u32[]{:S(2)}, u32[]{:S(2)}) collective-permute-start(bf16[128,1024]{1,0:T(8,128)(2,1)S(1)} %get-tuple-element.78), channel_id=1, source_target_pairs={{0,16},{1,17},{2,18},{3,19},{4,20},{5,21},{6,22},{7,23},{8,24},{9,... | collective-permute-start | bytes 786440 | tf_op jit(solution)/shard_map/ppermute | solution.py:358

commit v15 on v13

--- a/solution.py
+++ b/solution.py
@@ -141,7 +141,7 @@
 def value_kernel(mine, other, w0, w1, w2, w3, keep, give, acc):
     _, x, z, c = place()
     for r, piece in enumerate((w0, w1, w2, w3)):
-        owner = lax.rem(z - r + 4, 4)
+        owner = z ^ (0, 1, 3, 2)[r]
         lanes = pl.ds(pl.multiple_of(lax.rem(owner, 2) * 256, 256), 256)
 
         @pl.when(lax.div(owner, 2) == c)
@@ -311,7 +311,7 @@
     pieces, keep, give = refs[:8], refs[8], refs[9]
     _, x, z, c = place()
     for r in range(4):
-        owner = lax.rem(z - r + 4, 4)
+        owner = z ^ (0, 1, 3, 2)[r]
         for k in range(2):
             to = 2 * lax.rem(owner, 2) + (1 - x if k else x)
 
@@ -357,6 +357,9 @@
 
     def to_core(values):
         return permute(values, lambda g, z, x, k: (g, z, x, 1 - k))
+
+    def with_z(values, r):
+        return permute(values, lambda g, z, x, k: (g, z ^ r, x, k))
 
     def to_z(values, r):
         return permute(values, lambda g, z, x, k: (g, (z + r) % deep, x, k))
@@ -383,23 +386,26 @@
         moved=1 << 20,
     )(filter_spectrum, near)
     filters = [filters[0]] + [to_z(filters[r], r) for r in (1, 2, 3)]
-    v1 = to_z(own_v, 1)
-    q1 = to_z(after(own_o, v1), 1)
-    v2 = to_z(v1, 1)
-    q2 = to_z(after(q1, v2), 1)
-    mine = in_vmem(join_tokens, shape((512, 512), BF16), moved=1 << 20)(tokens, after(received[0], q1), *received[1:])
-    v3 = to_z(v2, 1)
+    v2 = with_z(own_v, 3)
+    v1 = with_z(own_v, 1)
+    q2 = with_z(after(own_o, v2), 3)
+    v3 = with_z(after(v2, v1), 1)
+    q3 = with_z(q2, 1)
+    q1 = with_z(after(own_o, v2), 1)
+    mine = in_vmem(join_tokens, shape((512, 512), BF16), moved=1 << 20)(
+        tokens, after(received[0], q2), *received[1:]
+    )
     other = to_core(mine)
-    got_o = to_x(after(away_o, v1))
-    r1 = to_z(after(got_o, v2), 1)
+    got_o = to_x(after(away_o, v2))
     keep, give = in_vmem(
         value_kernel,
         [shape((512, 256), F32), shape((512, 256), BF16)],
         [pltpu.VMEM((512, 512), F32)],
         flops=1 << 29,
         moved=2 << 20,
-    )(after(mine, q2, r1, near), other, own_v, v1, v2, v3)
-    r2 = to_z(after(r1, keep), 1)
+    )(after(mine, q1, q3, near, got_o), other, own_v, v1, v2, v3)
+    r2 = with_z(after(got_o, keep), 3)
+    r1 = with_z(after(got_o, keep), 1)
     drive, *sends = in_vmem(
         drive_kernel,
         [shape((512, 256), F32)] + [block] * 4,
@@ -407,8 +413,7 @@
         moved=2 << 20,
     )(after(keep, filters[1]), to_x(give), gate_k, *received, skip[None, :])
     columns = [sends[0]] + [to_z(sends[r], r) for r in (1, 2, 3)]
-    r3 = to_z(after(r2, *filters[2:], columns[1]), 1)
-    q3 = to_z(after(q2, columns[1]), 1)
+    r3 = with_z(after(r2, r1, *filters[2:], columns[1]), 1)
     table, table_t = tables()
     sends = in_vmem(
         conv_kernel,

time: 94.7 us -> 97.1 us (1.025)
  starting transfers between devices: 39.9 us -> 50.4 us
  waiting for transfers between devices: 44.1 us -> 36 us
    ppermute x30, starting transfers between devices: 39.9 us -> 50.4 us  [permute(): return lax.ppermute(values, AXES, pairs)]
    ppermute x30, waiting for transfers between devices: 44.1 us -> 36 us  [permute(): return lax.ppermute(values, AXES, pairs)]
  transfers between devices with their start and end apart: 30 -> 30, of which waited for: 18 -> 16; matrix products, arithmetic and copies ran while one was open for 0% -> 0% of each run, Pallas kernels for 6% -> 6%
where the time goes in v15:
time: 97.1 us; the launch traced here: 96.9 us
  starting transfers between devices  50.4 us (52%)
  waiting for transfers between devices  36 us (37%)
  Pallas kernels  8.32 us (9%)
  local copies, waits for them, and re-layouts  1.12 us (1%)
    ppermute x30, starting transfers between devices, permute(): return lax.ppermute(values, AXES, pairs)  50.4 us
    ppermute x30, waiting for transfers between devices, permute(): return lax.ppermute(values, AXES, pairs)  36 us
    pallas_call x9, Pallas kernels, call(): pl.pallas_call(kernel, out_shape=out_shape, in_specs=specs, out_specs=jax...  5.74 us
    pallas_call x1, Pallas kernels, call(): pl.pallas_call(kernel, out_shape=out_shape, in_specs=[pl.BlockSpec(memory...  2.58 us
  transfers between devices with their start and end apart: 30, of which 16 were waited for; matrix products, arithmetic and copies ran while one was open for 0% of the time, Pallas kernels for 6%

profile of v15, /device:TPU:0, one launch (start us, length us, event | category | flops | bytes accessed | tf_op | source)
XLA Modules:
  0.0 96.9 jit_solution(16682737433867097531)
XLA Ops:
  0.0 1.0 %copy-done = bf16[256,1024]{1,0:T(8,128)(2,1)S(1)} copy-done((bf16[256,1024]{1,0:T(8,128)(2,1)S(1)}, bf16[256,1024]{1,0:T(8,128)(2,1)}, u32[]{:S(2)}) %copy-start) | copy-done | bytes 524312
  1.1 0.0 copy-start.2
  1.1 0.0 copy-start.5
  1.1 5.1 %collective-permute-start.1 = (bf16[256,512]{1,0:T(8,128)(2,1)S(1)}, bf16[256,512]{1,0:T(8,128)(2,1)S(1)}, u32[]{:S(2)}, u32[]{:S(2)}) collective-permute-start(bf16[256,512]{1,0:T(8,128)(2,1)S(1)} %constant_dynamic-slice_fusion.after.w0), channel_id=1, source_target_pairs={{0,12},{1,13},{2,14},{3,15},{4,8},{5,9},{6,10},{7,11},{8,4},{9,5},... | collective-permute-start | bytes 786440 | tf_op jit(solution)/shard_map/ppermute | solution.py:353
  6.2 2.6 %shard_map.91 = (bf16[128,1024]{1,0:T(8,128)(2,1)}, bf16[128,1024]{1,0:T(8,128)(2,1)}, bf16[128,1024]{1,0:T(8,128)(2,1)}, bf16[256,256]{1,0:T(8,128)(2,1)}, bf16...) custom-call(bf16[128,1024]{1,0:T(8,128)(2,1)} %refs_0_.1, bf16[128,1024]{1,0:T(8,128)(2,1)} %g0.2, ...), custom_call_target="tpu_custom_call" | custom-call | tf_op jit(solution)/shard_map/pallas_call | solution.py:101
  8.8 1.6 %collective-permute-start = (bf16[128,1024]{1,0:T(8,128)(2,1)}, bf16[128,1024]{1,0:T(8,128)(2,1)S(1)}, u32[]{:S(2)}, u32[]{:S(2)}) collective-permute-start(bf16[128,1024]{1,0:T(8,128)(2,1)} %get-tuple-element.41), channel_id=1, source_target_pairs={{0,2},{1,3},{2,0},{3,1},{4,6},{5,7},{6,4},{7,5},{8,10},{9,11},{10,... | collective-permute-start | bytes 786440 | tf_op jit(solution)/shard_map/ppermute | solution.py:353
  10.3 1.5 %collective-permute-start.3 = (bf16[128,1024]{1,0:T(8,128)(2,1)}, bf16[128,1024]{1,0:T(8,128)(2,1)S(1)}, u32[]{:S(2)}, u32[]{:S(2)}) collective-permute-start(bf16[128,1024]{1,0:T(8,128)(2,1)} %get-tuple-element.45), channel_id=1, source_target_pairs={{0,16},{1,17},{2,18},{3,19},{4,20},{5,21},{6,22},{7,23},{8,24},{9,... | collective-permute-start | bytes 786440 | tf_op jit(solution)/shard_map/ppermute | solution.py:353
  11.9 0.5 collective-permute-start.4
  12.3 0.3 collective-permute-done.1.w2
  12.6 3.6 %collective-permute-start.2 = (bf16[256,256]{1,0:T(8,128)(2,1)}, bf16[256,256]{1,0:T(8,128)(2,1)S(1)}, u32[]{:S(2)}, u32[]{:S(2)}) collective-permute-start(bf16[256,256]{1,0:T(8,128)(2,1)} %get-tuple-element.43.refs_0_), channel_id=1, source_target_pairs={{0,12},{1,13},{2,14},{3,15},{4,8},{5,9},{6,10},{7,11},{8,4},{9,5},... | collective-permute-start | bytes 393224 | tf_op jit(solution)/shard_map/ppermute | solution.py:353
  16.2 4.9 %collective-permute-start.10 = (bf16[256,512]{1,0:T(8,128)(2,1)}, bf16[256,512]{1,0:T(8,128)(2,1)S(1)}, u32[]{:S(2)}, u32[]{:S(2)}) collective-permute-start(bf16[256,512]{1,0:T(8,128)(2,1)} %copy-done.2), channel_id=1, source_target_pairs={{0,4},{1,5},{2,6},{3,7},{4,0},{5,1},{6,2},{7,3},{8,12},{9,13},{10,... | collective-permute-start | bytes 786440 | tf_op jit(solution)/shard_map/ppermute | solution.py:353
  21.1 0.0 collective-permute-done.refs_1_.g1
  21.1 0.0 collective-permute-done.2.refs_4_
  21.1 2.5 %collective-permute-done.3.refs_2_.g2 = bf16[128,1024]{1,0:T(8,128)(2,1)S(1)} collective-permute-done((bf16[128,1024]{1,0:T(8,128)(2,1)}, bf16[128,1024]{1,0:T(8,128)(2,1)S(1)}, u32[]{:S(2)}, u32[]{:S(2)}) %collective-permute-start.3) | collective-permute-done | bytes 262176 | tf_op jit(solution)/shard_map/ppermute | solution.py:353
  23.7 0.0 collective-permute-done.4.refs_3_.g3
  23.7 0.1 collective-permute-start.9
  23.8 1.3 %collective-permute-start.7 = (bf16[2,2,128,256]{3,2,1,0:T(8,128)(2,1)S(1)}, bf16[2,2,128,256]{3,2,1,0:T(8,128)(2,1)S(1)}, u32[]{:S(2)}, u32[]{:S(2)}) collective-permute-start(bf16[2,2,128,256]{3,2,1,0:T(8,128)(2,1)S(1)} %copy-done.11), channel_id=1, source_target_pairs={{0,2},{1,3},{2,0},{3,1},{4,6},{5,7},{6,4},{7,5},{8,10},{9,11},{10,... | collective-permute-start | bytes 786440 | tf_op jit(solution)/shard_map/ppermute | solution.py:353
  25.1 0.6 collective-permute-done.10.w1
  25.7 2.2 %collective-permute-start.11 = (bf16[256,512]{1,0:T(8,128)(2,1)S(1)}, bf16[256,512]{1,0:T(8,128)(2,1)S(1)}, u32[]{:S(2)}, u32[]{:S(2)}) collective-permute-start(bf16[256,512]{1,0:T(8,128)(2,1)S(1)} %collective-permute-done.1.w2), channel_id=1, source_target_pairs={{0,4},{1,5},{2,6},{3,7},{4,0},{5,1},{6,2},{7,3},{8,12},{9,13},{10,... | collective-permute-start | bytes 786440 | tf_op jit(solution)/shard_map/ppermute | solution.py:353
  27.9 0.1 collective-permute-start.5
  28.0 1.3 %collective-permute-start.8 = (bf16[256,256]{1,0:T(8,128)(2,1)S(1)}, bf16[256,256]{1,0:T(8,128)(2,1)S(1)}, u32[]{:S(2)}, u32[]{:S(2)}) collective-permute-start(bf16[256,256]{1,0:T(8,128)(2,1)S(1)} %copy-done.12), channel_id=1, source_target_pairs={{0,2},{1,3},{2,0},{3,1},{4,6},{5,7},{6,4},{7,5},{8,10},{9,11},{10,... | collective-permute-start | bytes 393224 | tf_op jit(solution)/shard_map/ppermute | solution.py:353
  29.3 3.7 %collective-permute-done.7.near = bf16[2,2,128,256]{3,2,1,0:T(8,128)(2,1)S(1)} collective-permute-done((bf16[2,2,128,256]{3,2,1,0:T(8,128)(2,1)S(1)}, bf16[2,2,128,256]{3,2,1,0:T(8,128)(2,1)S(1)}, u32[]{:S(2)}, u32[]{:S(2)}) %collective-permute-start.7) | collective-permute-done | bytes 262176 | tf_op jit(solution)/shard_map/ppermute | solution.py:353
  33.0 2.6 %collective-permute-start.6 = (bf16[256,256]{1,0:T(8,128)(2,1)S(1)}, bf16[256,256]{1,0:T(8,128)(2,1)S(1)}, u32[]{:S(2)}, u32[]{:S(2)}) collective-permute-start(bf16[256,256]{1,0:T(8,128)(2,1)S(1)} %collective-permute-done.2.refs_4_), channel_id=1, source_target_pairs={{0,4},{1,5},{2,6},{3,7},{4,0},{5,1},{6,2},{7,3},{8,12},{9,13},{10,... | collective-permute-start | bytes 393224 | tf_op jit(solution)/shard_map/ppermute | solution.py:353
  35.5 2.3 %collective-permute-done.5.refs_2_ = bf16[256,256]{1,0:T(8,128)(2,1)S(1)} collective-permute-done((bf16[256,256]{1,0:T(8,128)(2,1)S(1)}, bf16[256,256]{1,0:T(8,128)(2,1)S(1)}, u32[]{:S(2)}, u32[]{:S(2)}) %collective-permute-start.5) | collective-permute-done | bytes 131104 | tf_op jit(solution)/shard_map/ppermute | solution.py:353
  37.8 2.3 %collective-permute-done.6.refs_6_ = bf16[256,256]{1,0:T(8,128)(2,1)S(1)} collective-permute-done((bf16[256,256]{1,0:T(8,128)(2,1)S(1)}, bf16[256,256]{1,0:T(8,128)(2,1)S(1)}, u32[]{:S(2)}, u32[]{:S(2)}) %collective-permute-start.6) | collective-permute-done | bytes 131104 | tf_op jit(solution)/shard_map/ppermute | solution.py:353
  40.2 1.3 %shard_map.93 = (f32[512,256]{1,0:T(8,128)S(1)}, bf16[512,256]{1,0:T(8,128)(2,1)S(1)}) custom-call(bf16[512,512]{1,0:T(8,128)(2,1)S(1)} %shard_map.92.mine, bf16[512,512]{1,0:T(8,128)(2,1)S(1)} %collective-permute-done.9.other, bf16[256,512]{1,0:T(8,128)(2,1)S(1)} %copy-done.3, bf16[256,512]{1,0:T(8,128)(2,1)S(1)} %collective-permute-done.10.w1, ...), custom_call_target="tpu_custom_call" | custom-call | flops 536870912 | bytes 2097152 | tf_op jit(solution)/shard_map/pallas_call | solution.py:37
  41.5 0.0 copy-start.4
  41.5 0.6 collective-permute-start.13
  42.1 0.3 shard_map.94
  42.4 0.0 copy-start.8
  42.4 0.0 copy-start.9
  42.4 1.8 %collective-permute-start.12 = (bf16[2,2,128,128]{3,2,1,0:T(8,128)(2,1)S(1)}, bf16[2,2,128,128]{3,2,1,0:T(8,128)(2,1)S(1)}, u32[]{:S(2)}, u32[]{:S(2)}) collective-permute-start(bf16[2,2,128,128]{3,2,1,0:T(8,128)(2,1)S(1)} %get-tuple-element.53), channel_id=1, source_target_pairs={{0,4},{1,5},{2,6},{3,7},{4,8},{5,9},{6,10},{7,11},{8,12},{9,13},{1... | collective-permute-start | bytes 393224 | tf_op jit(solution)/shard_map/ppermute | solution.py:353
  44.2 2.4 %collective-permute-start.18 = (bf16[2,2,128,128]{3,2,1,0:T(8,128)(2,1)S(1)}, bf16[2,2,128,128]{3,2,1,0:T(8,128)(2,1)S(1)}, u32[]{:S(2)}, u32[]{:S(2)}) collective-permute-start(bf16[2,2,128,128]{3,2,1,0:T(8,128)(2,1)S(1)} %get-tuple-element.62), channel_id=1, source_target_pairs={{0,12},{1,13},{2,14},{3,15},{4,0},{5,1},{6,2},{7,3},{8,4},{9,5},{1... | collective-permute-start | bytes 393224 | tf_op jit(solution)/shard_map/ppermute | solution.py:353
  46.7 0.2 collective-permute-start.23
  46.9 3.9 %collective-permute-done.12.refs_5_ = bf16[2,2,128,128]{3,2,1,0:T(8,128)(2,1)S(1)} collective-permute-done((bf16[2,2,128,128]{3,2,1,0:T(8,128)(2,1)S(1)}, bf16[2,2,128,128]{3,2,1,0:T(8,128)(2,1)S(1)}, u32[]{:S(2)}, u32[]{:S(2)}) %collective-permute-start.12) | collective-permute-done | bytes 131104 | tf_op jit(solution)/shard_map/ppermute | solution.py:353
  50.8 0.0 collective-permute-start.24
  50.8 0.3 shard_map.95
  51.2 3.0 %collective-permute-start.14 = (bf16[256,128]{1,0:T(8,128)(2,1)S(1)}, bf16[256,128]{1,0:T(8,128)(2,1)S(1)}, u32[]{:S(2)}, u32[]{:S(2)}) collective-permute-start(bf16[256,128]{1,0:T(8,128)(2,1)S(1)} %get-tuple-element.57), channel_id=1, source_target_pairs={{0,4},{1,5},{2,6},{3,7},{4,8},{5,9},{6,10},{7,11},{8,12},{9,13},{1... | collective-permute-start | bytes 196616 | tf_op jit(solution)/shard_map/ppermute | solution.py:353
  54.2 0.4 collective-permute-done.17.refs_6_
  54.5 1.1 %collective-permute-start.15 = (bf16[256,128]{1,0:T(8,128)(2,1)S(1)}, bf16[256,128]{1,0:T(8,128)(2,1)S(1)}, u32[]{:S(2)}, u32[]{:S(2)}) collective-permute-start(bf16[256,128]{1,0:T(8,128)(2,1)S(1)} %get-tuple-element.58), channel_id=1, source_target_pairs={{0,8},{1,9},{2,10},{3,11},{4,12},{5,13},{6,14},{7,15},{8,0},{9,1},... | collective-permute-start | bytes 196616 | tf_op jit(solution)/shard_map/ppermute | solution.py:353
  55.6 4.7 %collective-permute-start.16 = (bf16[256,128]{1,0:T(8,128)(2,1)S(1)}, bf16[256,128]{1,0:T(8,128)(2,1)S(1)}, u32[]{:S(2)}, u32[]{:S(2)}) collective-permute-start(bf16[256,128]{1,0:T(8,128)(2,1)S(1)} %get-tuple-element.59), channel_id=1, source_target_pairs={{0,12},{1,13},{2,14},{3,15},{4,0},{5,1},{6,2},{7,3},{8,4},{9,5},{1... | collective-permute-start | bytes 196616 | tf_op jit(solution)/shard_map/ppermute | solution.py:353
  60.3 1.7 %collective-permute-done.24.refs_5_ = bf16[256,256]{1,0:T(8,128)(2,1)S(1)} collective-permute-done((bf16[256,256]{1,0:T(8,128)(2,1)S(1)}, bf16[256,256]{1,0:T(8,128)(2,1)S(1)}, u32[]{:S(2)}, u32[]{:S(2)}) %collective-permute-start.24) | collective-permute-done | bytes 131104 | tf_op jit(solution)/shard_map/ppermute | solution.py:353
  62.0 1.0 %collective-permute-done.14.refs_1_ = bf16[256,128]{1,0:T(8,128)(2,1)S(1)} collective-permute-done((bf16[256,128]{1,0:T(8,128)(2,1)S(1)}, bf16[256,128]{1,0:T(8,128)(2,1)S(1)}, u32[]{:S(2)}, u32[]{:S(2)}) %collective-permute-start.14) | collective-permute-done | bytes 65568 | tf_op jit(solution)/shard_map/ppermute | solution.py:353
  63.0 3.3 %collective-permute-start.25 = (bf16[256,256]{1,0:T(8,128)(2,1)S(1)}, bf16[256,256]{1,0:T(8,128)(2,1)S(1)}, u32[]{:S(2)}, u32[]{:S(2)}) collective-permute-start(bf16[256,256]{1,0:T(8,128)(2,1)S(1)} %collective-permute-done.24.refs_5_), channel_id=1, source_target_pairs={{0,4},{1,5},{2,6},{3,7},{4,0},{5,1},{6,2},{7,3},{8,12},{9,13},{10,... | collective-permute-start | bytes 393224 | tf_op jit(solution)/shard_map/ppermute | solution.py:353
  66.4 0.8 collective-permute-done.15.refs_2_
  67.2 1.8 %shard_map.96 = (bf16[256,128]{1,0:T(8,128)(2,1)S(1)}, bf16[256,128]{1,0:T(8,128)(2,1)S(1)}, bf16[256,128]{1,0:T(8,128)(2,1)S(1)}, bf16[256,128]{1,0:T(8,128)(2,1)S(1)}) custom-call(bf16[256,128]{1,0:T(8,128)(2,1)S(1)} %get-tuple-element.56.refs_0_, bf16[256,128]{1,0:T(8,128)(2,1)S(1)} %collective-permute-done.14.refs_1_, ...), custom_call_target="tpu_custom_call" | custom-call | flops 1073741824 | bytes 5242880 | tf_op jit(solution)/shard_map/pallas_call | solution.py:37
  69.0 1.9 %collective-permute-start.19 = (bf16[256,128]{1,0:T(8,128)(2,1)S(1)}, bf16[256,128]{1,0:T(8,128)(2,1)S(1)}, u32[]{:S(2)}, u32[]{:S(2)}) collective-permute-start(bf16[256,128]{1,0:T(8,128)(2,1)S(1)} %get-tuple-element.64), channel_id=1, source_target_pairs={{0,4},{1,5},{2,6},{3,7},{4,8},{5,9},{6,10},{7,11},{8,12},{9,13},{1... | collective-permute-start | bytes 196616 | tf_op jit(solution)/shard_map/ppermute | solution.py:353
  70.9 0.8 collective-permute-start.20
  71.8 1.6 %collective-permute-start.21 = (bf16[256,128]{1,0:T(8,128)(2,1)S(1)}, bf16[256,128]{1,0:T(8,128)(2,1)S(1)}, u32[]{:S(2)}, u32[]{:S(2)}) collective-permute-start(bf16[256,128]{1,0:T(8,128)(2,1)S(1)} %get-tuple-element.66), channel_id=1, source_target_pairs={{0,12},{1,13},{2,14},{3,15},{4,0},{5,1},{6,2},{7,3},{8,4},{9,5},{1... | collective-permute-start | bytes 196616 | tf_op jit(solution)/shard_map/ppermute | solution.py:353
  73.4 2.3 %collective-permute-done.19.e1 = bf16[256,128]{1,0:T(8,128)(2,1)S(1)} collective-permute-done((bf16[256,128]{1,0:T(8,128)(2,1)S(1)}, bf16[256,128]{1,0:T(8,128)(2,1)S(1)}, u32[]{:S(2)}, u32[]{:S(2)}) %collective-permute-start.19) | collective-permute-done | bytes 65568 | tf_op jit(solution)/shard_map/ppermute | solution.py:353
  75.7 2.0 %collective-permute-done.20.e2 = bf16[256,128]{1,0:T(8,128)(2,1)S(1)} collective-permute-done((bf16[256,128]{1,0:T(8,128)(2,1)S(1)}, bf16[256,128]{1,0:T(8,128)(2,1)S(1)}, u32[]{:S(2)}, u32[]{:S(2)}) %collective-permute-start.20) | collective-permute-done | bytes 65568 | tf_op jit(solution)/shard_map/ppermute | solution.py:353
  77.7 0.1 shard_map.98
  77.8 0.1 collective-permute-start.26
  77.9 0.2 shard_map.97.gated
  78.2 0.5 collective-permute-start.22
  78.7 1.5 %collective-permute-done.22.other = bf16[512,256]{1,0:T(8,128)(2,1)S(1)} collective-permute-done((bf16[512,256]{1,0:T(8,128)(2,1)S(1)}, bf16[512,256]{1,0:T(8,128)(2,1)S(1)}, u32[]{:S(2)}, u32[]{:S(2)}) %collective-permute-start.22) | collective-permute-done | bytes 262176 | tf_op jit(solution)/shard_map/ppermute | solution.py:353
  80.2 0.8 shard_map.100
  81.0 2.7 %collective-permute-start.27 = (bf16[128,1024]{1,0:T(8,128)(2,1)S(1)}, bf16[128,1024]{1,0:T(8,128)(2,1)S(1)}, u32[]{:S(2)}, u32[]{:S(2)}) collective-permute-start(bf16[128,1024]{1,0:T(8,128)(2,1)S(1)} %get-tuple-element.74), channel_id=1, source_target_pairs={{0,18},{1,19},{2,16},{3,17},{4,22},{5,23},{6,20},{7,21},{8,26},{9,... | collective-permute-start | bytes 786440 | tf_op jit(solution)/shard_map/ppermute | solution.py:353
  83.7 0.3 collective-permute-start.28
  84.1 0.8 shard_map.99
  84.9 0.6 collective-permute-start.29
  85.4 5.7 %collective-permute-done.27 = bf16[128,1024]{1,0:T(8,128)(2,1)S(1)} collective-permute-done((bf16[128,1024]{1,0:T(8,128)(2,1)S(1)}, bf16[128,1024]{1,0:T(8,128)(2,1)S(1)}, u32[]{:S(2)}, u32[]{:S(2)}) %collective-permute-start.27) | collective-permute-done | bytes 262176 | tf_op jit(solution)/shard_map/ppermute | solution.py:353
  91.2 4.9 %collective-permute-done.28 = bf16[128,1024]{1,0:T(8,128)(2,1)S(1)} collective-permute-done((bf16[128,1024]{1,0:T(8,128)(2,1)S(1)}, bf16[128,1024]{1,0:T(8,128)(2,1)S(1)}, u32[]{:S(2)}, u32[]{:S(2)}) %collective-permute-start.28) | collective-permute-done | bytes 262176 | tf_op jit(solution)/shard_map/ppermute | solution.py:353
  96.1 0.8 add_convert_fusion
  (34 shorter events, 0.1 us)
Async XLA Ops:
  0.0 1.0 %copy-start = (bf16[256,1024]{1,0:T(8,128)(2,1)S(1)}, bf16[256,1024]{1,0:T(8,128)(2,1)}, u32[]{:S(2)}) copy-start(bf16[256,1024]{1,0:T(8,128)(2,1)} %param.12) | copy-start | bytes 1572868
  1.1 5.1 %copy-start.2 = (bf16[256,512]{1,0:T(8,128)(2,1)}, bf16[256,512]{1,0:T(8,128)(2,1)S(1)}, u32[]{:S(2)}) copy-start(bf16[256,512]{1,0:T(8,128)(2,1)S(1)} %constant_dynamic-slice_fusion.after.w0) | copy-start | bytes 786436
  1.1 22.6 %copy-start.5 = (bf16[128,1024]{1,0:T(8,128)(2,1)S(1)}, bf16[128,1024]{1,0:T(8,128)(2,1)}, u32[]{:S(2)}) copy-start(bf16[128,1024]{1,0:T(8,128)(2,1)} %refs_0_.1) | copy-start | bytes 786436
  1.1 11.5 %collective-permute-start.1 = (bf16[256,512]{1,0:T(8,128)(2,1)S(1)}, bf16[256,512]{1,0:T(8,128)(2,1)S(1)}, u32[]{:S(2)}, u32[]{:S(2)}) collective-permute-start(bf16[256,512]{1,0:T(8,128)(2,1)S(1)} %constant_dynamic-slice_fusion.after.w0), channel_id=1, source_target_pairs={{0,12},{1,13},{2,14},{3,15},{4,8},{5,9},{6,10},{7,11},{8,4},{9,5},... | collective-permute-start | bytes 786440 | tf_op jit(solution)/shard_map/ppermute | solution.py:353
  8.8 12.3 %collective-permute-start = (bf16[128,1024]{1,0:T(8,128)(2,1)}, bf16[128,1024]{1,0:T(8,128)(2,1)S(1)}, u32[]{:S(2)}, u32[]{:S(2)}) collective-permute-start(bf16[128,1024]{1,0:T(8,128)(2,1)} %get-tuple-element.41), channel_id=1, source_target_pairs={{0,2},{1,3},{2,0},{3,1},{4,6},{5,7},{6,4},{7,5},{8,10},{9,11},{10,... | collective-permute-start | bytes 786440 | tf_op jit(solution)/shard_map/ppermute | solution.py:353
  10.3 13.3 %collective-permute-start.3 = (bf16[128,1024]{1,0:T(8,128)(2,1)}, bf16[128,1024]{1,0:T(8,128)(2,1)S(1)}, u32[]{:S(2)}, u32[]{:S(2)}) collective-permute-start(bf16[128,1024]{1,0:T(8,128)(2,1)} %get-tuple-element.45), channel_id=1, source_target_pairs={{0,16},{1,17},{2,18},{3,19},{4,20},{5,21},{6,22},{7,23},{8,24},{9,... | collective-permute-start | bytes 786440 | tf_op jit(solution)/shard_map/ppermute | solution.py:353
  11.9 11.8 %collective-permute-start.4 = (bf16[128,1024]{1,0:T(8,128)(2,1)}, bf16[128,1024]{1,0:T(8,128)(2,1)S(1)}, u32[]{:S(2)}, u32[]{:S(2)}) collective-permute-start(bf16[128,1024]{1,0:T(8,128)(2,1)} %get-tuple-element.46), channel_id=1, source_target_pairs={{0,18},{1,19},{2,16},{3,17},{4,22},{5,23},{6,20},{7,21},{8,26},{9,... | collective-permute-start | bytes 786440 | tf_op jit(solution)/shard_map/ppermute | solution.py:353
  12.6 11.2 %copy-start.11 = (bf16[2,2,128,256]{3,2,1,0:T(8,128)(2,1)S(1)}, bf16[2,2,128,256]{3,2,1,0:T(8,128)(2,1)}, u32[]{:S(2)}) copy-start(bf16[2,2,128,256]{3,2,1,0:T(8,128)(2,1)} %get-tuple-element.47) | copy-start | bytes 786436
  12.6 15.3 %copy-start.7 = (bf16[256,256]{1,0:T(8,128)(2,1)S(1)}, bf16[256,256]{1,0:T(8,128)(2,1)}, u32[]{:S(2)}) copy-start(bf16[256,256]{1,0:T(8,128)(2,1)} %get-tuple-element.43.refs_0_) | copy-start | bytes 393220
  12.6 15.4 %copy-start.12 = (bf16[256,256]{1,0:T(8,128)(2,1)S(1)}, bf16[256,256]{1,0:T(8,128)(2,1)}, u32[]{:S(2)}) copy-start(bf16[256,256]{1,0:T(8,128)(2,1)} %get-tuple-element.49) | copy-start | bytes 393220
  12.6 27.6 %copy-start.3 = (bf16[256,512]{1,0:T(8,128)(2,1)S(1)}, bf16[256,512]{1,0:T(8,128)(2,1)}, u32[]{:S(2)}) copy-start(bf16[256,512]{1,0:T(8,128)(2,1)} %copy-done.2) | copy-start | bytes 786436
  12.6 8.5 %collective-permute-start.2 = (bf16[256,256]{1,0:T(8,128)(2,1)}, bf16[256,256]{1,0:T(8,128)(2,1)S(1)}, u32[]{:S(2)}, u32[]{:S(2)}) collective-permute-start(bf16[256,256]{1,0:T(8,128)(2,1)} %get-tuple-element.43.refs_0_), channel_id=1, source_target_pairs={{0,12},{1,13},{2,14},{3,15},{4,8},{5,9},{6,10},{7,11},{8,4},{9,5},... | collective-permute-start | bytes 393224 | tf_op jit(solution)/shard_map/ppermute | solution.py:353
  16.2 9.4 %collective-permute-start.10 = (bf16[256,512]{1,0:T(8,128)(2,1)}, bf16[256,512]{1,0:T(8,128)(2,1)S(1)}, u32[]{:S(2)}, u32[]{:S(2)}) collective-permute-start(bf16[256,512]{1,0:T(8,128)(2,1)} %copy-done.2), channel_id=1, source_target_pairs={{0,4},{1,5},{2,6},{3,7},{4,0},{5,1},{6,2},{7,3},{8,12},{9,13},{10,... | collective-permute-start | bytes 786440 | tf_op jit(solution)/shard_map/ppermute | solution.py:353
  23.7 16.5 %collective-permute-start.9 = (bf16[512,512]{1,0:T(8,128)(2,1)S(1)}, bf16[512,512]{1,0:T(8,128)(2,1)S(1)}, u32[]{:S(2)}, u32[]{:S(2)}) collective-permute-start(bf16[512,512]{1,0:T(8,128)(2,1)S(1)} %shard_map.92.mine), channel_id=1, source_target_pairs={{0,1},{1,0},{2,3},{3,2},{4,5},{5,4},{6,7},{7,6},{8,9},{9,8},{10,11... | collective-permute-start | bytes 1572872 | tf_op jit(solution)/shard_map/ppermute | solution.py:353
  23.8 9.2 %collective-permute-start.7 = (bf16[2,2,128,256]{3,2,1,0:T(8,128)(2,1)S(1)}, bf16[2,2,128,256]{3,2,1,0:T(8,128)(2,1)S(1)}, u32[]{:S(2)}, u32[]{:S(2)}) collective-permute-start(bf16[2,2,128,256]{3,2,1,0:T(8,128)(2,1)S(1)} %copy-done.11), channel_id=1, source_target_pairs={{0,2},{1,3},{2,0},{3,1},{4,6},{5,7},{6,4},{7,5},{8,10},{9,11},{10,... | collective-permute-start | bytes 786440 | tf_op jit(solution)/shard_map/ppermute | solution.py:353
  25.7 14.5 %collective-permute-start.11 = (bf16[256,512]{1,0:T(8,128)(2,1)S(1)}, bf16[256,512]{1,0:T(8,128)(2,1)S(1)}, u32[]{:S(2)}, u32[]{:S(2)}) collective-permute-start(bf16[256,512]{1,0:T(8,128)(2,1)S(1)} %collective-permute-done.1.w2), channel_id=1, source_target_pairs={{0,4},{1,5},{2,6},{3,7},{4,0},{5,1},{6,2},{7,3},{8,12},{9,13},{10,... | collective-permute-start | bytes 786440 | tf_op jit(solution)/shard_map/ppermute | solution.py:353
  27.9 9.9 %collective-permute-start.5 = (bf16[256,256]{1,0:T(8,128)(2,1)S(1)}, bf16[256,256]{1,0:T(8,128)(2,1)S(1)}, u32[]{:S(2)}, u32[]{:S(2)}) collective-permute-start(bf16[256,256]{1,0:T(8,128)(2,1)S(1)} %copy-done.7), channel_id=1, source_target_pairs={{0,4},{1,5},{2,6},{3,7},{4,0},{5,1},{6,2},{7,3},{8,12},{9,13},{10,... | collective-permute-start | bytes 393224 | tf_op jit(solution)/shard_map/ppermute | solution.py:353
  28.0 14.1 %copy-start.1 = (bf16[2,2,128,1024]{3,2,1,0:T(8,128)(2,1)S(1)}, bf16[2,2,128,1024]{3,2,1,0:T(8,128)(2,1)}, u32[]{:S(2)}) copy-start(bf16[2,2,128,1024]{3,2,1,0:T(8,128)(2,1)} %filt.3) | copy-start | bytes 3145732
  28.0 9.8 %collective-permute-start.8 = (bf16[256,256]{1,0:T(8,128)(2,1)S(1)}, bf16[256,256]{1,0:T(8,128)(2,1)S(1)}, u32[]{:S(2)}, u32[]{:S(2)}) collective-permute-start(bf16[256,256]{1,0:T(8,128)(2,1)S(1)} %copy-done.12), channel_id=1, source_target_pairs={{0,2},{1,3},{2,0},{3,1},{4,6},{5,7},{6,4},{7,5},{8,10},{9,11},{10,... | collective-permute-start | bytes 393224 | tf_op jit(solution)/shard_map/ppermute | solution.py:353
  33.0 7.2 %collective-permute-start.6 = (bf16[256,256]{1,0:T(8,128)(2,1)S(1)}, bf16[256,256]{1,0:T(8,128)(2,1)S(1)}, u32[]{:S(2)}, u32[]{:S(2)}) collective-permute-start(bf16[256,256]{1,0:T(8,128)(2,1)S(1)} %collective-permute-done.2.refs_4_), channel_id=1, source_target_pairs={{0,4},{1,5},{2,6},{3,7},{4,0},{5,1},{6,2},{7,3},{8,12},{9,13},{10,... | collective-permute-start | bytes 393224 | tf_op jit(solution)/shard_map/ppermute | solution.py:353
  41.5 9.3 %copy-start.4 = (bf16[128,1024]{1,0:T(8,128)(2,1)S(1)}, bf16[128,1024]{1,0:T(8,128)(2,1)}, u32[]{:S(2)}) copy-start(bf16[128,1024]{1,0:T(8,128)(2,1)} %g0.2) | copy-start | bytes 786436
  41.5 9.3 %collective-permute-start.13 = (bf16[512,256]{1,0:T(8,128)(2,1)S(1)}, bf16[512,256]{1,0:T(8,128)(2,1)S(1)}, u32[]{:S(2)}, u32[]{:S(2)}) collective-permute-start(bf16[512,256]{1,0:T(8,128)(2,1)S(1)} %get-tuple-element.55), channel_id=1, source_target_pairs={{0,2},{1,3},{2,0},{3,1},{4,6},{5,7},{6,4},{7,5},{8,10},{9,11},{10,... | collective-permute-start | bytes 786440 | tf_op jit(solution)/shard_map/ppermute | solution.py:353
  42.1 25.1 %copy-start.10 = (bf16[16,256,128]{2,1,0:T(8,128)(2,1)S(1)}, bf16[16,256,128]{2,1,0:T(8,128)(2,1)}, u32[]{:S(2)}) copy-start(bf16[16,256,128]{2,1,0:T(8,128)(2,1)} %constant.17.clone.refs_9_) | copy-start | bytes 3145732
  42.4 8.4 %copy-start.8 = (f32[1024]{0:T(1024)S(1)}, f32[1024]{0:T(1024)}, u32[]{:S(2)}) copy-start(f32[1024]{0:T(1024)} %param.13) | copy-start | bytes 12292
  42.4 24.8 %copy-start.9 = (bf16[16,256,128]{2,1,0:T(8,128)(2,1)S(1)}, bf16[16,256,128]{2,1,0:T(8,128)(2,1)}, u32[]{:S(2)}) copy-start(bf16[16,256,128]{2,1,0:T(8,128)(2,1)} %constant.16.clone.refs_8_) | copy-start | bytes 3145732
  42.4 8.4 %collective-permute-start.12 = (bf16[2,2,128,128]{3,2,1,0:T(8,128)(2,1)S(1)}, bf16[2,2,128,128]{3,2,1,0:T(8,128)(2,1)S(1)}, u32[]{:S(2)}, u32[]{:S(2)}) collective-permute-start(bf16[2,2,128,128]{3,2,1,0:T(8,128)(2,1)S(1)} %get-tuple-element.53), channel_id=1, source_target_pairs={{0,4},{1,5},{2,6},{3,7},{4,8},{5,9},{6,10},{7,11},{8,12},{9,13},{1... | collective-permute-start | bytes 393224 | tf_op jit(solution)/shard_map/ppermute | solution.py:353
  44.2 10.3 %collective-permute-start.17 = (bf16[2,2,128,128]{3,2,1,0:T(8,128)(2,1)S(1)}, bf16[2,2,128,128]{3,2,1,0:T(8,128)(2,1)S(1)}, u32[]{:S(2)}, u32[]{:S(2)}) collective-permute-start(bf16[2,2,128,128]{3,2,1,0:T(8,128)(2,1)S(1)} %get-tuple-element.61), channel_id=1, source_target_pairs={{0,8},{1,9},{2,10},{3,11},{4,12},{5,13},{6,14},{7,15},{8,0},{9,1},... | collective-permute-start | bytes 393224 | tf_op jit(solution)/shard_map/ppermute | solution.py:353
  44.2 11.4 %collective-permute-start.18 = (bf16[2,2,128,128]{3,2,1,0:T(8,128)(2,1)S(1)}, bf16[2,2,128,128]{3,2,1,0:T(8,128)(2,1)S(1)}, u32[]{:S(2)}, u32[]{:S(2)}) collective-permute-start(bf16[2,2,128,128]{3,2,1,0:T(8,128)(2,1)S(1)} %get-tuple-element.62), channel_id=1, source_target_pairs={{0,12},{1,13},{2,14},{3,15},{4,0},{5,1},{6,2},{7,3},{8,4},{9,5},{1... | collective-permute-start | bytes 393224 | tf_op jit(solution)/shard_map/ppermute | solution.py:353
  46.7 13.7 %collective-permute-start.23 = (bf16[256,256]{1,0:T(8,128)(2,1)S(1)}, bf16[256,256]{1,0:T(8,128)(2,1)S(1)}, u32[]{:S(2)}, u32[]{:S(2)}) collective-permute-start(bf16[256,256]{1,0:T(8,128)(2,1)S(1)} %collective-permute-done.8.refs_1_), channel_id=1, source_target_pairs={{0,4},{1,5},{2,6},{3,7},{4,0},{5,1},{6,2},{7,3},{8,12},{9,13},{10,... | collective-permute-start | bytes 393224 | tf_op jit(solution)/shard_map/ppermute | solution.py:353
  50.8 11.2 %collective-permute-start.24 = (bf16[256,256]{1,0:T(8,128)(2,1)S(1)}, bf16[256,256]{1,0:T(8,128)(2,1)S(1)}, u32[]{:S(2)}, u32[]{:S(2)}) collective-permute-start(bf16[256,256]{1,0:T(8,128)(2,1)S(1)} %collective-permute-done.8.refs_1_), channel_id=1, source_target_pairs={{0,12},{1,13},{2,14},{3,15},{4,8},{5,9},{6,10},{7,11},{8,4},{9,5},... | collective-permute-start | bytes 393224 | tf_op jit(solution)/shard_map/ppermute | solution.py:353
  51.2 11.9 %collective-permute-start.14 = (bf16[256,128]{1,0:T(8,128)(2,1)S(1)}, bf16[256,128]{1,0:T(8,128)(2,1)S(1)}, u32[]{:S(2)}, u32[]{:S(2)}) collective-permute-start(bf16[256,128]{1,0:T(8,128)(2,1)S(1)} %get-tuple-element.57), channel_id=1, source_target_pairs={{0,4},{1,5},{2,6},{3,7},{4,8},{5,9},{6,10},{7,11},{8,12},{9,13},{1... | collective-permute-start | bytes 196616 | tf_op jit(solution)/shard_map/ppermute | solution.py:353
  54.5 12.6 %collective-permute-start.15 = (bf16[256,128]{1,0:T(8,128)(2,1)S(1)}, bf16[256,128]{1,0:T(8,128)(2,1)S(1)}, u32[]{:S(2)}, u32[]{:S(2)}) collective-permute-start(bf16[256,128]{1,0:T(8,128)(2,1)S(1)} %get-tuple-element.58), channel_id=1, source_target_pairs={{0,8},{1,9},{2,10},{3,11},{4,12},{5,13},{6,14},{7,15},{8,0},{9,1},... | collective-permute-start | bytes 196616 | tf_op jit(solution)/shard_map/ppermute | solution.py:353
  55.6 11.6 %collective-permute-start.16 = (bf16[256,128]{1,0:T(8,128)(2,1)S(1)}, bf16[256,128]{1,0:T(8,128)(2,1)S(1)}, u32[]{:S(2)}, u32[]{:S(2)}) collective-permute-start(bf16[256,128]{1,0:T(8,128)(2,1)S(1)} %get-tuple-element.59), channel_id=1, source_target_pairs={{0,12},{1,13},{2,14},{3,15},{4,0},{5,1},{6,2},{7,3},{8,4},{9,5},{1... | collective-permute-start | bytes 196616 | tf_op jit(solution)/shard_map/ppermute | solution.py:353
  63.0 14.7 %collective-permute-start.25 = (bf16[256,256]{1,0:T(8,128)(2,1)S(1)}, bf16[256,256]{1,0:T(8,128)(2,1)S(1)}, u32[]{:S(2)}, u32[]{:S(2)}) collective-permute-start(bf16[256,256]{1,0:T(8,128)(2,1)S(1)} %collective-permute-done.24.refs_5_), channel_id=1, source_target_pairs={{0,4},{1,5},{2,6},{3,7},{4,0},{5,1},{6,2},{7,3},{8,12},{9,13},{10,... | collective-permute-start | bytes 393224 | tf_op jit(solution)/shard_map/ppermute | solution.py:353
  69.0 6.7 %collective-permute-start.19 = (bf16[256,128]{1,0:T(8,128)(2,1)S(1)}, bf16[256,128]{1,0:T(8,128)(2,1)S(1)}, u32[]{:S(2)}, u32[]{:S(2)}) collective-permute-start(bf16[256,128]{1,0:T(8,128)(2,1)S(1)} %get-tuple-element.64), channel_id=1, source_target_pairs={{0,4},{1,5},{2,6},{3,7},{4,8},{5,9},{6,10},{7,11},{8,12},{9,13},{1... | collective-permute-start | bytes 196616 | tf_op jit(solution)/shard_map/ppermute | solution.py:353
  70.9 6.8 %collective-permute-start.20 = (bf16[256,128]{1,0:T(8,128)(2,1)S(1)}, bf16[256,128]{1,0:T(8,128)(2,1)S(1)}, u32[]{:S(2)}, u32[]{:S(2)}) collective-permute-start(bf16[256,128]{1,0:T(8,128)(2,1)S(1)} %get-tuple-element.65), channel_id=1, source_target_pairs={{0,8},{1,9},{2,10},{3,11},{4,12},{5,13},{6,14},{7,15},{8,0},{9,1},... | collective-permute-start | bytes 196616 | tf_op jit(solution)/shard_map/ppermute | solution.py:353
  71.8 6.2 %copy-start.6 = (bf16[128,1024]{1,0:T(8,128)(2,1)S(1)}, bf16[128,1024]{1,0:T(8,128)(2,1)}, u32[]{:S(2)}) copy-start(bf16[128,1024]{1,0:T(8,128)(2,1)} %g0.3) | copy-start | bytes 786436
  71.8 5.9 %collective-permute-start.21 = (bf16[256,128]{1,0:T(8,128)(2,1)S(1)}, bf16[256,128]{1,0:T(8,128)(2,1)S(1)}, u32[]{:S(2)}, u32[]{:S(2)}) collective-permute-start(bf16[256,128]{1,0:T(8,128)(2,1)S(1)} %get-tuple-element.66), channel_id=1, source_target_pairs={{0,12},{1,13},{2,14},{3,15},{4,0},{5,1},{6,2},{7,3},{8,4},{9,5},{1... | collective-permute-start | bytes 196616 | tf_op jit(solution)/shard_map/ppermute | solution.py:353
  77.8 2.4 %collective-permute-start.26 = (bf16[4,256,256]{2,1,0:T(8,128)(2,1)S(1)}, bf16[4,256,256]{2,1,0:T(8,128)(2,1)S(1)}, u32[]{:S(2)}, u32[]{:S(2)}) collective-permute-start(bf16[4,256,256]{2,1,0:T(8,128)(2,1)S(1)} %get-tuple-element.72), channel_id=1, source_target_pairs={{0,1},{1,0},{2,3},{3,2},{4,5},{5,4},{6,7},{7,6},{8,9},{9,8},{10,11... | collective-permute-start | bytes 1572872 | tf_op jit(solution)/shard_map/ppermute | solution.py:353
  78.2 2.0 %collective-permute-start.22 = (bf16[512,256]{1,0:T(8,128)(2,1)S(1)}, bf16[512,256]{1,0:T(8,128)(2,1)S(1)}, u32[]{:S(2)}, u32[]{:S(2)}) collective-permute-start(bf16[512,256]{1,0:T(8,128)(2,1)S(1)} %shard_map.97.gated), channel_id=1, source_target_pairs={{0,1},{1,0},{2,3},{3,2},{4,5},{5,4},{6,7},{7,6},{8,9},{9,8},{10,11... | collective-permute-start | bytes 786440 | tf_op jit(solution)/shard_map/ppermute | solution.py:353
  81.0 10.2 %collective-permute-start.27 = (bf16[128,1024]{1,0:T(8,128)(2,1)S(1)}, bf16[128,1024]{1,0:T(8,128)(2,1)S(1)}, u32[]{:S(2)}, u32[]{:S(2)}) collective-permute-start(bf16[128,1024]{1,0:T(8,128)(2,1)S(1)} %get-tuple-element.74), channel_id=1, source_target_pairs={{0,18},{1,19},{2,16},{3,17},{4,22},{5,23},{6,20},{7,21},{8,26},{9,... | collective-permute-start | bytes 786440 | tf_op jit(solution)/shard_map/ppermute | solution.py:353
  83.7 12.3 %collective-permute-start.28 = (bf16[128,1024]{1,0:T(8,128)(2,1)S(1)}, bf16[128,1024]{1,0:T(8,128)(2,1)S(1)}, u32[]{:S(2)}, u32[]{:S(2)}) collective-permute-start(bf16[128,1024]{1,0:T(8,128)(2,1)S(1)} %get-tuple-element.75), channel_id=1, source_target_pairs={{0,2},{1,3},{2,0},{3,1},{4,6},{5,7},{6,4},{7,5},{8,10},{9,11},{10,... | collective-permute-start | bytes 786440 | tf_op jit(solution)/shard_map/ppermute | solution.py:353
  84.9 11.2 %collective-permute-start.29 = (bf16[128,1024]{1,0:T(8,128)(2,1)S(1)}, bf16[128,1024]{1,0:T(8,128)(2,1)S(1)}, u32[]{:S(2)}, u32[]{:S(2)}) collective-permute-start(bf16[128,1024]{1,0:T(8,128)(2,1)S(1)} %get-tuple-element.76), channel_id=1, source_target_pairs={{0,16},{1,17},{2,18},{3,19},{4,20},{5,21},{6,22},{7,23},{8,24},{9,... | collective-permute-start | bytes 786440 | tf_op jit(solution)/shard_map/ppermute | solution.py:353

commit v16 on v14

--- a/solution.py
+++ b/solution.py
@@ -52,8 +52,8 @@
     return y, lax.rem(s, 2), lax.div(s, 2), c
 
 
-def before(z, r):
-    at = lax.rem((z ^ lax.div(z, 2)) - r + 4, 4)
+def around(z, r):
+    at = lax.rem((z ^ lax.div(z, 2)) + r + 4, 4)
     return at ^ lax.div(at, 2)
 
 
@@ -131,7 +131,7 @@
                 packed[2 * j, k, part] = one
                 packed[2 * j + 1, k, part] = two
     for r in range(4):
-        outs[r][...] = packed[lax.rem(z + r, 4)]
+        outs[r][...] = packed[around(z, r)]
 
 
 def join_tokens(*refs):
@@ -146,7 +146,7 @@
 def value_kernel(mine, other, w0, w1, w2, w3, keep, give, acc):
     _, x, z, c = place()
     for r, piece in enumerate((w0, w1, w2, w3)):
-        owner = before(z, r)
+        owner = around(z, -r)
         lanes = pl.ds(pl.multiple_of(lax.rem(owner, 2) * 256, 256), 256)
 
         @pl.when(lax.div(owner, 2) == c)
@@ -180,7 +180,7 @@
         second = drive[pl.ds(256, 256), lanes].astype(F32)
         packed[2 * j], packed[2 * j + 1] = both(first, second, low)
     for r, out in enumerate((o0, o1, o2, o3)):
-        out[...] = packed[lax.rem(z + r, 4)]
+        out[...] = packed[around(z, r)]
 
 
 def add(a, b):
@@ -234,7 +234,7 @@
     outs, (data, filt, first, sums) = refs[10:14], refs[14:]
     _, x, z, _ = place()
     for r, block in enumerate(drives):
-        base = 2 * lax.rem(z - r + 4, 4)
+        base = 2 * around(z, -r)
         filt[base + x] = filters[r][0]
         filt[base + 1 - x] = filters[r][1]
         data[base + x] = block[pl.ds(0, 128), :]
@@ -289,7 +289,7 @@
             if 0 < a < 4:
                 data[8 - a, rows, :] = sub(sub(add(ec, os), oc), es).astype(BF16)
     for r, out in enumerate(outs):
-        base = 2 * lax.rem(z + r, 4)
+        base = 2 * around(z, r)
         out[pl.ds(0, 128), :] = data[base + x]
         out[pl.ds(128, 128), :] = data[base + 1 - x]
 
@@ -297,7 +297,7 @@
 def gate_kernel(e0, e1, e2, e3, direct, g0, g1, g2, g3, gated, conv):
     _, _, z, _ = place()
     for r, block in enumerate((e0, e1, e2, e3)):
-        conv[lax.rem(z - r + 4, 4)] = block[...]
+        conv[around(z, -r)] = block[...]
     low = low_lanes((256, 128))
     for j in range(2):
         lanes = pl.ds(j * 128, 128)
@@ -316,7 +316,7 @@
     pieces, keep, give = refs[:8], refs[8], refs[9]
     _, x, z, c = place()
     for r in range(4):
-        owner = before(z, r)
+        owner = around(z, -r)
         for k in range(2):
             to = 2 * lax.rem(owner, 2) + (1 - x if k else x)
 
@@ -363,12 +363,13 @@
     def to_core(values):
         return permute(values, lambda g, z, x, k: (g, z, x, 1 - k))
 
+    def to_z(values, r):
+        ring = (0, 1, 3, 2)
+        at = [ring.index(z) for z in range(deep)]
+        return permute(values, lambda g, z, x, k: (g, ring[(at[z] + r) % deep], x, k))
+
     def onward(values):
-        ring = (1, 3, 0, 2)
-        return permute(values, lambda g, z, x, k: (g, ring[z], x, k))
-
-    def to_z(values, r):
-        return permute(values, lambda g, z, x, k: (g, (z + r) % deep, x, k))
+        return to_z(values, 1)
 
     def to_peer(values, p):
         return permute(values, lambda g, z, x, k: (g ^ (p // 2), z, x ^ (p % 2), k))
@@ -407,7 +408,7 @@
         [pltpu.VMEM((512, 512), F32)],
         flops=1 << 29,
         moved=2 << 20,
-    )(after(mine, r1, near), other, own_v, v1, v2, v3)
+    )(after(mine, r1, filters[0]), other, own_v, v1, v2, v3)
     r2 = onward(after(r1, keep))
     drive, *sends = in_vmem(
         drive_kernel,

time: 92.9 us -> 93.5 us (level)
  transfers between devices with their start and end apart: 30 -> 30, of which waited for: 17 -> 18; matrix products, arithmetic and copies ran while one was open for 0% -> 0% of each run, Pallas kernels for 7% -> 6%
where the time goes in v16:
time: 93.5 us; the launch traced here: 93.3 us
  waiting for transfers between devices  45.4 us (49%)
  starting transfers between devices  37.4 us (40%)
  Pallas kernels  8.36 us (9%)
  local copies, waits for them, and re-layouts  1.11 us (1%)
    ppermute x30, waiting for transfers between devices, permute(): return lax.ppermute(values, AXES, pairs)  45.4 us
    ppermute x30, starting transfers between devices, permute(): return lax.ppermute(values, AXES, pairs)  37.4 us
    pallas_call x9, Pallas kernels, call(): pl.pallas_call(kernel, out_shape=out_shape, in_specs=specs, out_specs=jax...  5.78 us
    pallas_call x1, Pallas kernels, call(): pl.pallas_call(kernel, out_shape=out_shape, in_specs=[pl.BlockSpec(memory...  2.58 us
  transfers between devices with their start and end apart: 30, of which 18 were waited for; matrix products, arithmetic and copies ran while one was open for 0% of the time, Pallas kernels for 6%

profile of v16, /device:TPU:0, one launch (start us, length us, event | category | flops | bytes accessed | tf_op | source)
XLA Modules:
  0.0 93.3 jit_solution(3966888598879421017)
XLA Ops:
  0.0 1.0 %copy-done = bf16[256,1024]{1,0:T(8,128)(2,1)S(1)} copy-done((bf16[256,1024]{1,0:T(8,128)(2,1)S(1)}, bf16[256,1024]{1,0:T(8,128)(2,1)}, u32[]{:S(2)}) %copy-start) | copy-done | bytes 524312
  1.1 0.0 copy-start.2
  1.1 0.0 copy-start.5
  1.1 3.1 %collective-permute-start.2 = (bf16[256,512]{1,0:T(8,128)(2,1)S(1)}, bf16[256,512]{1,0:T(8,128)(2,1)S(1)}, u32[]{:S(2)}, u32[]{:S(2)}) collective-permute-start(bf16[256,512]{1,0:T(8,128)(2,1)S(1)} %constant_dynamic-slice_fusion.after.w0), channel_id=1, source_target_pairs={{0,4},{1,5},{2,6},{3,7},{4,12},{5,13},{6,14},{7,15},{8,0},{9,1},{1... | collective-permute-start | bytes 786440 | tf_op jit(solution)/shard_map/ppermute | solution.py:358
  4.2 2.6 %shard_map.91 = (bf16[128,1024]{1,0:T(8,128)(2,1)}, bf16[128,1024]{1,0:T(8,128)(2,1)}, bf16[128,1024]{1,0:T(8,128)(2,1)}, bf16[256,256]{1,0:T(8,128)(2,1)}, bf16...) custom-call(bf16[128,1024]{1,0:T(8,128)(2,1)} %refs_0_.1, bf16[128,1024]{1,0:T(8,128)(2,1)} %g0.2, ...), custom_call_target="tpu_custom_call" | custom-call | tf_op jit(solution)/shard_map/pallas_call | solution.py:106
  6.8 0.0 copy-start.1
  6.8 2.6 %collective-permute-start.1 = (bf16[256,256]{1,0:T(8,128)(2,1)}, bf16[256,256]{1,0:T(8,128)(2,1)S(1)}, u32[]{:S(2)}, u32[]{:S(2)}) collective-permute-start(bf16[256,256]{1,0:T(8,128)(2,1)} %get-tuple-element.43.refs_0_), channel_id=1, source_target_pairs={{0,4},{1,5},{2,6},{3,7},{4,12},{5,13},{6,14},{7,15},{8,0},{9,1},{1... | collective-permute-start | bytes 393224 | tf_op jit(solution)/shard_map/ppermute | solution.py:358
  9.4 1.5 %collective-permute-start = (bf16[128,1024]{1,0:T(8,128)(2,1)}, bf16[128,1024]{1,0:T(8,128)(2,1)S(1)}, u32[]{:S(2)}, u32[]{:S(2)}) collective-permute-start(bf16[128,1024]{1,0:T(8,128)(2,1)} %get-tuple-element.42), channel_id=1, source_target_pairs={{0,2},{1,3},{2,0},{3,1},{4,6},{5,7},{6,4},{7,5},{8,10},{9,11},{10,... | collective-permute-start | bytes 786440 | tf_op jit(solution)/shard_map/ppermute | solution.py:358
  10.9 1.5 %collective-permute-start.4 = (bf16[128,1024]{1,0:T(8,128)(2,1)}, bf16[128,1024]{1,0:T(8,128)(2,1)S(1)}, u32[]{:S(2)}, u32[]{:S(2)}) collective-permute-start(bf16[128,1024]{1,0:T(8,128)(2,1)} %get-tuple-element.46), channel_id=1, source_target_pairs={{0,16},{1,17},{2,18},{3,19},{4,20},{5,21},{6,22},{7,23},{8,24},{9,... | collective-permute-start | bytes 786440 | tf_op jit(solution)/shard_map/ppermute | solution.py:358
  12.4 0.5 collective-permute-start.5
  12.9 1.4 %collective-permute-done.1.refs_2_ = bf16[256,256]{1,0:T(8,128)(2,1)S(1)} collective-permute-done((bf16[256,256]{1,0:T(8,128)(2,1)}, bf16[256,256]{1,0:T(8,128)(2,1)S(1)}, u32[]{:S(2)}, u32[]{:S(2)}) %collective-permute-start.1) | collective-permute-done | bytes 131104 | tf_op jit(solution)/shard_map/ppermute | solution.py:358
  14.3 0.0 collective-permute-done.2.w1
  14.3 0.9 %collective-permute-start.3 = (bf16[256,256]{1,0:T(8,128)(2,1)S(1)}, bf16[256,256]{1,0:T(8,128)(2,1)S(1)}, u32[]{:S(2)}, u32[]{:S(2)}) collective-permute-start(bf16[256,256]{1,0:T(8,128)(2,1)S(1)} %collective-permute-done.1.refs_2_), channel_id=1, source_target_pairs={{0,4},{1,5},{2,6},{3,7},{4,12},{5,13},{6,14},{7,15},{8,0},{9,1},{1... | collective-permute-start | bytes 393224 | tf_op jit(solution)/shard_map/ppermute | solution.py:358
  15.2 3.3 %collective-permute-start.7 = (bf16[256,512]{1,0:T(8,128)(2,1)S(1)}, bf16[256,512]{1,0:T(8,128)(2,1)S(1)}, u32[]{:S(2)}, u32[]{:S(2)}) collective-permute-start(bf16[256,512]{1,0:T(8,128)(2,1)S(1)} %collective-permute-done.2.w1), channel_id=1, source_target_pairs={{0,4},{1,5},{2,6},{3,7},{4,12},{5,13},{6,14},{7,15},{8,0},{9,1},{1... | collective-permute-start | bytes 786440 | tf_op jit(solution)/shard_map/ppermute | solution.py:358
  18.5 0.4 collective-permute-done.refs_1_.g1
  18.9 2.8 %collective-permute-done.3.refs_4_ = bf16[256,256]{1,0:T(8,128)(2,1)S(1)} collective-permute-done((bf16[256,256]{1,0:T(8,128)(2,1)S(1)}, bf16[256,256]{1,0:T(8,128)(2,1)S(1)}, u32[]{:S(2)}, u32[]{:S(2)}) %collective-permute-start.3) | collective-permute-done | bytes 131104 | tf_op jit(solution)/shard_map/ppermute | solution.py:358
  21.6 2.3 %collective-permute-done.4.refs_2_.g2 = bf16[128,1024]{1,0:T(8,128)(2,1)S(1)} collective-permute-done((bf16[128,1024]{1,0:T(8,128)(2,1)}, bf16[128,1024]{1,0:T(8,128)(2,1)S(1)}, u32[]{:S(2)}, u32[]{:S(2)}) %collective-permute-start.4) | collective-permute-done | bytes 262176 | tf_op jit(solution)/shard_map/ppermute | solution.py:358
  23.9 0.0 collective-permute-done.5.refs_3_.g3
  24.0 0.1 collective-permute-start.10
  24.1 1.3 %collective-permute-start.6 = (bf16[256,256]{1,0:T(8,128)(2,1)S(1)}, bf16[256,256]{1,0:T(8,128)(2,1)S(1)}, u32[]{:S(2)}, u32[]{:S(2)}) collective-permute-start(bf16[256,256]{1,0:T(8,128)(2,1)S(1)} %copy-done.12), channel_id=1, source_target_pairs={{0,2},{1,3},{2,0},{3,1},{4,6},{5,7},{6,4},{7,5},{8,10},{9,11},{10,... | collective-permute-start | bytes 393224 | tf_op jit(solution)/shard_map/ppermute | solution.py:358
  25.4 0.8 collective-permute-start.9
  26.2 0.9 collective-permute-start.11
  27.1 3.4 %collective-permute-done.6.refs_1_ = bf16[256,256]{1,0:T(8,128)(2,1)S(1)} collective-permute-done((bf16[256,256]{1,0:T(8,128)(2,1)S(1)}, bf16[256,256]{1,0:T(8,128)(2,1)S(1)}, u32[]{:S(2)}, u32[]{:S(2)}) %collective-permute-start.6) | collective-permute-done | bytes 131104 | tf_op jit(solution)/shard_map/ppermute | solution.py:358
  30.4 0.9 collective-permute-start.8
  31.3 4.3 %collective-permute-done.9.near = bf16[2,2,128,256]{3,2,1,0:T(8,128)(2,1)S(1)} collective-permute-done((bf16[2,2,128,256]{3,2,1,0:T(8,128)(2,1)S(1)}, bf16[2,2,128,256]{3,2,1,0:T(8,128)(2,1)S(1)}, u32[]{:S(2)}, u32[]{:S(2)}) %collective-permute-start.9) | collective-permute-done | bytes 262176 | tf_op jit(solution)/shard_map/ppermute | solution.py:358
  35.6 0.3 shard_map.93
  35.9 2.1 %collective-permute-done.8.refs_3_ = bf16[256,256]{1,0:T(8,128)(2,1)S(1)} collective-permute-done((bf16[256,256]{1,0:T(8,128)(2,1)S(1)}, bf16[256,256]{1,0:T(8,128)(2,1)S(1)}, u32[]{:S(2)}, u32[]{:S(2)}) %collective-permute-start.8) | collective-permute-done | bytes 131104 | tf_op jit(solution)/shard_map/ppermute | solution.py:358
  38.0 0.0 copy-start.9
  38.0 1.3 %shard_map.94 = (f32[512,256]{1,0:T(8,128)S(1)}, bf16[512,256]{1,0:T(8,128)(2,1)S(1)}) custom-call(bf16[512,512]{1,0:T(8,128)(2,1)S(1)} %shard_map.92.mine, bf16[512,512]{1,0:T(8,128)(2,1)S(1)} %collective-permute-done.10.other, bf16[256,512]{1,0:T(8,128)(2,1)S(1)} %copy-done.3, bf16[256,512]{1,0:T(8,128)(2,1)S(1)} %collective-permute-done.2.w1, ...), custom_call_target="tpu_custom_call" | custom-call | flops 536870912 | bytes 2097152 | tf_op jit(solution)/shard_map/pallas_call | solution.py:37
  39.3 1.3 %collective-permute-start.13 = (bf16[512,256]{1,0:T(8,128)(2,1)S(1)}, bf16[512,256]{1,0:T(8,128)(2,1)S(1)}, u32[]{:S(2)}, u32[]{:S(2)}) collective-permute-start(bf16[512,256]{1,0:T(8,128)(2,1)S(1)} %get-tuple-element.57), channel_id=1, source_target_pairs={{0,2},{1,3},{2,0},{3,1},{4,6},{5,7},{6,4},{7,5},{8,10},{9,11},{10,... | collective-permute-start | bytes 786440 | tf_op jit(solution)/shard_map/ppermute | solution.py:358
  40.6 0.0 collective-permute-start.12
  40.6 1.6 %collective-permute-start.17 = (bf16[2,2,128,128]{3,2,1,0:T(8,128)(2,1)S(1)}, bf16[2,2,128,128]{3,2,1,0:T(8,128)(2,1)S(1)}, u32[]{:S(2)}, u32[]{:S(2)}) collective-permute-start(bf16[2,2,128,128]{3,2,1,0:T(8,128)(2,1)S(1)} %get-tuple-element.62), channel_id=1, source_target_pairs={{0,12},{1,13},{2,14},{3,15},{4,8},{5,9},{6,10},{7,11},{8,4},{9,5},... | collective-permute-start | bytes 393224 | tf_op jit(solution)/shard_map/ppermute | solution.py:358
  42.2 2.0 %collective-permute-start.18 = (bf16[2,2,128,128]{3,2,1,0:T(8,128)(2,1)S(1)}, bf16[2,2,128,128]{3,2,1,0:T(8,128)(2,1)S(1)}, u32[]{:S(2)}, u32[]{:S(2)}) collective-permute-start(bf16[2,2,128,128]{3,2,1,0:T(8,128)(2,1)S(1)} %get-tuple-element.63), channel_id=1, source_target_pairs={{0,8},{1,9},{2,10},{3,11},{4,0},{5,1},{6,2},{7,3},{8,12},{9,13},{1... | collective-permute-start | bytes 393224 | tf_op jit(solution)/shard_map/ppermute | solution.py:358
  44.3 8.6 %collective-permute-done.12.refs_5_ = bf16[2,2,128,128]{3,2,1,0:T(8,128)(2,1)S(1)} collective-permute-done((bf16[2,2,128,128]{3,2,1,0:T(8,128)(2,1)S(1)}, bf16[2,2,128,128]{3,2,1,0:T(8,128)(2,1)S(1)}, u32[]{:S(2)}, u32[]{:S(2)}) %collective-permute-start.12) | collective-permute-done | bytes 131104 | tf_op jit(solution)/shard_map/ppermute | solution.py:358
  52.9 0.3 shard_map.95
  53.2 0.1 collective-permute-start.14
  53.3 1.1 %collective-permute-start.15 = (bf16[256,128]{1,0:T(8,128)(2,1)S(1)}, bf16[256,128]{1,0:T(8,128)(2,1)S(1)}, u32[]{:S(2)}, u32[]{:S(2)}) collective-permute-start(bf16[256,128]{1,0:T(8,128)(2,1)S(1)} %get-tuple-element.60), channel_id=1, source_target_pairs={{0,12},{1,13},{2,14},{3,15},{4,8},{5,9},{6,10},{7,11},{8,4},{9,5},... | collective-permute-start | bytes 196616 | tf_op jit(solution)/shard_map/ppermute | solution.py:358
  54.4 0.0 collective-permute-done.17.refs_6_
  54.4 3.1 %collective-permute-start.16 = (bf16[256,128]{1,0:T(8,128)(2,1)S(1)}, bf16[256,128]{1,0:T(8,128)(2,1)S(1)}, u32[]{:S(2)}, u32[]{:S(2)}) collective-permute-start(bf16[256,128]{1,0:T(8,128)(2,1)S(1)} %get-tuple-element.61), channel_id=1, source_target_pairs={{0,8},{1,9},{2,10},{3,11},{4,0},{5,1},{6,2},{7,3},{8,12},{9,13},{1... | collective-permute-start | bytes 196616 | tf_op jit(solution)/shard_map/ppermute | solution.py:358
  57.5 2.9 %collective-permute-done.23.refs_5_ = bf16[256,256]{1,0:T(8,128)(2,1)S(1)} collective-permute-done((bf16[256,256]{1,0:T(8,128)(2,1)S(1)}, bf16[256,256]{1,0:T(8,128)(2,1)S(1)}, u32[]{:S(2)}, u32[]{:S(2)}) %collective-permute-start.23) | collective-permute-done | bytes 131104 | tf_op jit(solution)/shard_map/ppermute | solution.py:358
  60.4 0.7 collective-permute-done.14.refs_1_
  61.2 0.3 collective-permute-done.16.refs_3_
  61.5 2.2 %collective-permute-start.24 = (bf16[256,256]{1,0:T(8,128)(2,1)S(1)}, bf16[256,256]{1,0:T(8,128)(2,1)S(1)}, u32[]{:S(2)}, u32[]{:S(2)}) collective-permute-start(bf16[256,256]{1,0:T(8,128)(2,1)S(1)} %collective-permute-done.3.refs_4_), channel_id=1, source_target_pairs={{0,4},{1,5},{2,6},{3,7},{4,12},{5,13},{6,14},{7,15},{8,0},{9,1},{1... | collective-permute-start | bytes 393224 | tf_op jit(solution)/shard_map/ppermute | solution.py:358
  63.6 0.0 collective-permute-start.25
  63.7 1.8 %shard_map.96 = (bf16[256,128]{1,0:T(8,128)(2,1)S(1)}, bf16[256,128]{1,0:T(8,128)(2,1)S(1)}, bf16[256,128]{1,0:T(8,128)(2,1)S(1)}, bf16[256,128]{1,0:T(8,128)(2,1)S(1)}) custom-call(bf16[256,128]{1,0:T(8,128)(2,1)S(1)} %get-tuple-element.58.refs_0_, bf16[256,128]{1,0:T(8,128)(2,1)S(1)} %collective-permute-done.14.refs_1_, ...), custom_call_target="tpu_custom_call" | custom-call | flops 1073741824 | bytes 5242880 | tf_op jit(solution)/shard_map/pallas_call | solution.py:37
  65.5 1.3 %collective-permute-start.19 = (bf16[256,128]{1,0:T(8,128)(2,1)S(1)}, bf16[256,128]{1,0:T(8,128)(2,1)S(1)}, u32[]{:S(2)}, u32[]{:S(2)}) collective-permute-start(bf16[256,128]{1,0:T(8,128)(2,1)S(1)} %get-tuple-element.65), channel_id=1, source_target_pairs={{0,4},{1,5},{2,6},{3,7},{4,12},{5,13},{6,14},{7,15},{8,0},{9,1},{1... | collective-permute-start | bytes 196616 | tf_op jit(solution)/shard_map/ppermute | solution.py:358
  66.8 3.1 %collective-permute-start.20 = (bf16[256,128]{1,0:T(8,128)(2,1)S(1)}, bf16[256,128]{1,0:T(8,128)(2,1)S(1)}, u32[]{:S(2)}, u32[]{:S(2)}) collective-permute-start(bf16[256,128]{1,0:T(8,128)(2,1)S(1)} %get-tuple-element.66), channel_id=1, source_target_pairs={{0,12},{1,13},{2,14},{3,15},{4,8},{5,9},{6,10},{7,11},{8,4},{9,5},... | collective-permute-start | bytes 196616 | tf_op jit(solution)/shard_map/ppermute | solution.py:358
  69.9 2.2 %collective-permute-done.19.e1 = bf16[256,128]{1,0:T(8,128)(2,1)S(1)} collective-permute-done((bf16[256,128]{1,0:T(8,128)(2,1)S(1)}, bf16[256,128]{1,0:T(8,128)(2,1)S(1)}, u32[]{:S(2)}, u32[]{:S(2)}) %collective-permute-start.19) | collective-permute-done | bytes 65568 | tf_op jit(solution)/shard_map/ppermute | solution.py:358
  72.1 0.9 collective-permute-done.20.e2
  73.0 1.2 %collective-permute-done.21.e3 = bf16[256,128]{1,0:T(8,128)(2,1)S(1)} collective-permute-done((bf16[256,128]{1,0:T(8,128)(2,1)S(1)}, bf16[256,128]{1,0:T(8,128)(2,1)S(1)}, u32[]{:S(2)}, u32[]{:S(2)}) %collective-permute-start.21) | collective-permute-done | bytes 65568 | tf_op jit(solution)/shard_map/ppermute | solution.py:358
  74.2 0.2 shard_map.98
  74.4 0.1 collective-permute-start.26
  74.5 0.2 shard_map.97.gated
  74.7 0.5 collective-permute-start.22
  75.2 1.5 %collective-permute-done.22.other = bf16[512,256]{1,0:T(8,128)(2,1)S(1)} collective-permute-done((bf16[512,256]{1,0:T(8,128)(2,1)S(1)}, bf16[512,256]{1,0:T(8,128)(2,1)S(1)}, u32[]{:S(2)}, u32[]{:S(2)}) %collective-permute-start.22) | collective-permute-done | bytes 262176 | tf_op jit(solution)/shard_map/ppermute | solution.py:358
  76.7 0.8 shard_map.100
  77.5 1.7 %collective-permute-start.27 = (bf16[128,1024]{1,0:T(8,128)(2,1)S(1)}, bf16[128,1024]{1,0:T(8,128)(2,1)S(1)}, u32[]{:S(2)}, u32[]{:S(2)}) collective-permute-start(bf16[128,1024]{1,0:T(8,128)(2,1)S(1)} %get-tuple-element.76), channel_id=1, source_target_pairs={{0,18},{1,19},{2,16},{3,17},{4,22},{5,23},{6,20},{7,21},{8,26},{9,... | collective-permute-start | bytes 786440 | tf_op jit(solution)/shard_map/ppermute | solution.py:358
  79.2 0.5 collective-permute-start.28
  79.8 0.8 shard_map.99
  80.6 1.4 %collective-permute-start.29 = (bf16[128,1024]{1,0:T(8,128)(2,1)S(1)}, bf16[128,1024]{1,0:T(8,128)(2,1)S(1)}, u32[]{:S(2)}, u32[]{:S(2)}) collective-permute-start(bf16[128,1024]{1,0:T(8,128)(2,1)S(1)} %get-tuple-element.78), channel_id=1, source_target_pairs={{0,16},{1,17},{2,18},{3,19},{4,20},{5,21},{6,22},{7,23},{8,24},{9,... | collective-permute-start | bytes 786440 | tf_op jit(solution)/shard_map/ppermute | solution.py:358
  82.0 5.7 %collective-permute-done.27 = bf16[128,1024]{1,0:T(8,128)(2,1)S(1)} collective-permute-done((bf16[128,1024]{1,0:T(8,128)(2,1)S(1)}, bf16[128,1024]{1,0:T(8,128)(2,1)S(1)}, u32[]{:S(2)}, u32[]{:S(2)}) %collective-permute-start.27) | collective-permute-done | bytes 262176 | tf_op jit(solution)/shard_map/ppermute | solution.py:358
  87.7 4.0 %collective-permute-done.28 = bf16[128,1024]{1,0:T(8,128)(2,1)S(1)} collective-permute-done((bf16[128,1024]{1,0:T(8,128)(2,1)S(1)}, bf16[128,1024]{1,0:T(8,128)(2,1)S(1)}, u32[]{:S(2)}, u32[]{:S(2)}) %collective-permute-start.28) | collective-permute-done | bytes 262176 | tf_op jit(solution)/shard_map/ppermute | solution.py:358
  91.8 0.7 collective-permute-done.29
  92.5 0.8 add_convert_fusion
  (34 shorter events, 0.1 us)
Async XLA Ops:
  0.0 1.0 %copy-start = (bf16[256,1024]{1,0:T(8,128)(2,1)S(1)}, bf16[256,1024]{1,0:T(8,128)(2,1)}, u32[]{:S(2)}) copy-start(bf16[256,1024]{1,0:T(8,128)(2,1)} %param.12) | copy-start | bytes 1572868
  1.1 3.1 %copy-start.2 = (bf16[256,512]{1,0:T(8,128)(2,1)}, bf16[256,512]{1,0:T(8,128)(2,1)S(1)}, u32[]{:S(2)}) copy-start(bf16[256,512]{1,0:T(8,128)(2,1)S(1)} %constant_dynamic-slice_fusion.after.w0) | copy-start | bytes 786436
  1.1 22.9 %copy-start.5 = (bf16[128,1024]{1,0:T(8,128)(2,1)S(1)}, bf16[128,1024]{1,0:T(8,128)(2,1)}, u32[]{:S(2)}) copy-start(bf16[128,1024]{1,0:T(8,128)(2,1)} %refs_0_.1) | copy-start | bytes 786436
  1.1 13.2 %collective-permute-start.2 = (bf16[256,512]{1,0:T(8,128)(2,1)S(1)}, bf16[256,512]{1,0:T(8,128)(2,1)S(1)}, u32[]{:S(2)}, u32[]{:S(2)}) collective-permute-start(bf16[256,512]{1,0:T(8,128)(2,1)S(1)} %constant_dynamic-slice_fusion.after.w0), channel_id=1, source_target_pairs={{0,4},{1,5},{2,6},{3,7},{4,12},{5,13},{6,14},{7,15},{8,0},{9,1},{1... | collective-permute-start | bytes 786440 | tf_op jit(solution)/shard_map/ppermute | solution.py:358
  6.8 28.8 %copy-start.1 = (bf16[2,2,128,1024]{3,2,1,0:T(8,128)(2,1)S(1)}, bf16[2,2,128,1024]{3,2,1,0:T(8,128)(2,1)}, u32[]{:S(2)}) copy-start(bf16[2,2,128,1024]{3,2,1,0:T(8,128)(2,1)} %filt.3) | copy-start | bytes 3145732
  6.8 7.5 %collective-permute-start.1 = (bf16[256,256]{1,0:T(8,128)(2,1)}, bf16[256,256]{1,0:T(8,128)(2,1)S(1)}, u32[]{:S(2)}, u32[]{:S(2)}) collective-permute-start(bf16[256,256]{1,0:T(8,128)(2,1)} %get-tuple-element.43.refs_0_), channel_id=1, source_target_pairs={{0,4},{1,5},{2,6},{3,7},{4,12},{5,13},{6,14},{7,15},{8,0},{9,1},{1... | collective-permute-start | bytes 393224 | tf_op jit(solution)/shard_map/ppermute | solution.py:358
  9.4 9.5 %collective-permute-start = (bf16[128,1024]{1,0:T(8,128)(2,1)}, bf16[128,1024]{1,0:T(8,128)(2,1)S(1)}, u32[]{:S(2)}, u32[]{:S(2)}) collective-permute-start(bf16[128,1024]{1,0:T(8,128)(2,1)} %get-tuple-element.42), channel_id=1, source_target_pairs={{0,2},{1,3},{2,0},{3,1},{4,6},{5,7},{6,4},{7,5},{8,10},{9,11},{10,... | collective-permute-start | bytes 786440 | tf_op jit(solution)/shard_map/ppermute | solution.py:358
  10.9 13.0 %collective-permute-start.4 = (bf16[128,1024]{1,0:T(8,128)(2,1)}, bf16[128,1024]{1,0:T(8,128)(2,1)S(1)}, u32[]{:S(2)}, u32[]{:S(2)}) collective-permute-start(bf16[128,1024]{1,0:T(8,128)(2,1)} %get-tuple-element.46), channel_id=1, source_target_pairs={{0,16},{1,17},{2,18},{3,19},{4,20},{5,21},{6,22},{7,23},{8,24},{9,... | collective-permute-start | bytes 786440 | tf_op jit(solution)/shard_map/ppermute | solution.py:358
  12.4 11.6 %copy-start.12 = (bf16[256,256]{1,0:T(8,128)(2,1)S(1)}, bf16[256,256]{1,0:T(8,128)(2,1)}, u32[]{:S(2)}) copy-start(bf16[256,256]{1,0:T(8,128)(2,1)} %get-tuple-element.49) | copy-start | bytes 393220
  12.4 13.0 %copy-start.11 = (bf16[2,2,128,256]{3,2,1,0:T(8,128)(2,1)S(1)}, bf16[2,2,128,256]{3,2,1,0:T(8,128)(2,1)}, u32[]{:S(2)}) copy-start(bf16[2,2,128,256]{3,2,1,0:T(8,128)(2,1)} %get-tuple-element.51) | copy-start | bytes 786436
  12.4 11.5 %collective-permute-start.5 = (bf16[128,1024]{1,0:T(8,128)(2,1)}, bf16[128,1024]{1,0:T(8,128)(2,1)S(1)}, u32[]{:S(2)}, u32[]{:S(2)}) collective-permute-start(bf16[128,1024]{1,0:T(8,128)(2,1)} %get-tuple-element.47), channel_id=1, source_target_pairs={{0,18},{1,19},{2,16},{3,17},{4,22},{5,23},{6,20},{7,21},{8,26},{9,... | collective-permute-start | bytes 786440 | tf_op jit(solution)/shard_map/ppermute | solution.py:358
  14.3 7.3 %collective-permute-start.3 = (bf16[256,256]{1,0:T(8,128)(2,1)S(1)}, bf16[256,256]{1,0:T(8,128)(2,1)S(1)}, u32[]{:S(2)}, u32[]{:S(2)}) collective-permute-start(bf16[256,256]{1,0:T(8,128)(2,1)S(1)} %collective-permute-done.1.refs_2_), channel_id=1, source_target_pairs={{0,4},{1,5},{2,6},{3,7},{4,12},{5,13},{6,14},{7,15},{8,0},{9,1},{1... | collective-permute-start | bytes 393224 | tf_op jit(solution)/shard_map/ppermute | solution.py:358
  15.2 10.9 %collective-permute-start.7 = (bf16[256,512]{1,0:T(8,128)(2,1)S(1)}, bf16[256,512]{1,0:T(8,128)(2,1)S(1)}, u32[]{:S(2)}, u32[]{:S(2)}) collective-permute-start(bf16[256,512]{1,0:T(8,128)(2,1)S(1)} %collective-permute-done.2.w1), channel_id=1, source_target_pairs={{0,4},{1,5},{2,6},{3,7},{4,12},{5,13},{6,14},{7,15},{8,0},{9,1},{1... | collective-permute-start | bytes 786440 | tf_op jit(solution)/shard_map/ppermute | solution.py:358
  24.0 14.0 %collective-permute-start.10 = (bf16[512,512]{1,0:T(8,128)(2,1)S(1)}, bf16[512,512]{1,0:T(8,128)(2,1)S(1)}, u32[]{:S(2)}, u32[]{:S(2)}) collective-permute-start(bf16[512,512]{1,0:T(8,128)(2,1)S(1)} %shard_map.92.mine), channel_id=1, source_target_pairs={{0,1},{1,0},{2,3},{3,2},{4,5},{5,4},{6,7},{7,6},{8,9},{9,8},{10,11... | collective-permute-start | bytes 1572872 | tf_op jit(solution)/shard_map/ppermute | solution.py:358
  24.1 6.4 %collective-permute-start.6 = (bf16[256,256]{1,0:T(8,128)(2,1)S(1)}, bf16[256,256]{1,0:T(8,128)(2,1)S(1)}, u32[]{:S(2)}, u32[]{:S(2)}) collective-permute-start(bf16[256,256]{1,0:T(8,128)(2,1)S(1)} %copy-done.12), channel_id=1, source_target_pairs={{0,2},{1,3},{2,0},{3,1},{4,6},{5,7},{6,4},{7,5},{8,10},{9,11},{10,... | collective-permute-start | bytes 393224 | tf_op jit(solution)/shard_map/ppermute | solution.py:358
  25.4 12.6 %copy-start.3 = (bf16[256,512]{1,0:T(8,128)(2,1)S(1)}, bf16[256,512]{1,0:T(8,128)(2,1)}, u32[]{:S(2)}) copy-start(bf16[256,512]{1,0:T(8,128)(2,1)} %copy-done.2) | copy-start | bytes 786436
  25.4 10.2 %collective-permute-start.9 = (bf16[2,2,128,256]{3,2,1,0:T(8,128)(2,1)S(1)}, bf16[2,2,128,256]{3,2,1,0:T(8,128)(2,1)S(1)}, u32[]{:S(2)}, u32[]{:S(2)}) collective-permute-start(bf16[2,2,128,256]{3,2,1,0:T(8,128)(2,1)S(1)} %copy-done.11), channel_id=1, source_target_pairs={{0,2},{1,3},{2,0},{3,1},{4,6},{5,7},{6,4},{7,5},{8,10},{9,11},{10,... | collective-permute-start | bytes 786440 | tf_op jit(solution)/shard_map/ppermute | solution.py:358
  26.2 11.8 %collective-permute-start.11 = (bf16[256,512]{1,0:T(8,128)(2,1)S(1)}, bf16[256,512]{1,0:T(8,128)(2,1)S(1)}, u32[]{:S(2)}, u32[]{:S(2)}) collective-permute-start(bf16[256,512]{1,0:T(8,128)(2,1)S(1)} %collective-permute-done.7.w2), channel_id=1, source_target_pairs={{0,4},{1,5},{2,6},{3,7},{4,12},{5,13},{6,14},{7,15},{8,0},{9,1},{1... | collective-permute-start | bytes 786440 | tf_op jit(solution)/shard_map/ppermute | solution.py:358
  30.4 7.5 %collective-permute-start.8 = (bf16[256,256]{1,0:T(8,128)(2,1)S(1)}, bf16[256,256]{1,0:T(8,128)(2,1)S(1)}, u32[]{:S(2)}, u32[]{:S(2)}) collective-permute-start(bf16[256,256]{1,0:T(8,128)(2,1)S(1)} %collective-permute-done.6.refs_1_), channel_id=1, source_target_pairs={{0,4},{1,5},{2,6},{3,7},{4,12},{5,13},{6,14},{7,15},{8,0},{9,1},{1... | collective-permute-start | bytes 393224 | tf_op jit(solution)/shard_map/ppermute | solution.py:358
  38.0 14.9 %copy-start.4 = (bf16[128,1024]{1,0:T(8,128)(2,1)S(1)}, bf16[128,1024]{1,0:T(8,128)(2,1)}, u32[]{:S(2)}) copy-start(bf16[128,1024]{1,0:T(8,128)(2,1)} %g0.2) | copy-start | bytes 786436
  38.0 25.7 %copy-start.9 = (bf16[16,256,128]{2,1,0:T(8,128)(2,1)S(1)}, bf16[16,256,128]{2,1,0:T(8,128)(2,1)}, u32[]{:S(2)}) copy-start(bf16[16,256,128]{2,1,0:T(8,128)(2,1)} %constant.17.clone.refs_9_) | copy-start | bytes 3145732
  39.3 13.6 %collective-permute-start.13 = (bf16[512,256]{1,0:T(8,128)(2,1)S(1)}, bf16[512,256]{1,0:T(8,128)(2,1)S(1)}, u32[]{:S(2)}, u32[]{:S(2)}) collective-permute-start(bf16[512,256]{1,0:T(8,128)(2,1)S(1)} %get-tuple-element.57), channel_id=1, source_target_pairs={{0,2},{1,3},{2,0},{3,1},{4,6},{5,7},{6,4},{7,5},{8,10},{9,11},{10,... | collective-permute-start | bytes 786440 | tf_op jit(solution)/shard_map/ppermute | solution.py:358
  40.6 12.3 %copy-start.8 = (f32[1024]{0:T(1024)S(1)}, f32[1024]{0:T(1024)}, u32[]{:S(2)}) copy-start(f32[1024]{0:T(1024)} %param.13) | copy-start | bytes 12292
  40.6 23.0 %copy-start.10 = (bf16[16,256,128]{2,1,0:T(8,128)(2,1)S(1)}, bf16[16,256,128]{2,1,0:T(8,128)(2,1)}, u32[]{:S(2)}) copy-start(bf16[16,256,128]{2,1,0:T(8,128)(2,1)} %constant.16.clone.refs_8_) | copy-start | bytes 3145732
  40.6 12.3 %collective-permute-start.12 = (bf16[2,2,128,128]{3,2,1,0:T(8,128)(2,1)S(1)}, bf16[2,2,128,128]{3,2,1,0:T(8,128)(2,1)S(1)}, u32[]{:S(2)}, u32[]{:S(2)}) collective-permute-start(bf16[2,2,128,128]{3,2,1,0:T(8,128)(2,1)S(1)} %get-tuple-element.55), channel_id=1, source_target_pairs={{0,4},{1,5},{2,6},{3,7},{4,12},{5,13},{6,14},{7,15},{8,0},{9,1},{1... | collective-permute-start | bytes 393224 | tf_op jit(solution)/shard_map/ppermute | solution.py:358
  40.6 13.7 %collective-permute-start.17 = (bf16[2,2,128,128]{3,2,1,0:T(8,128)(2,1)S(1)}, bf16[2,2,128,128]{3,2,1,0:T(8,128)(2,1)S(1)}, u32[]{:S(2)}, u32[]{:S(2)}) collective-permute-start(bf16[2,2,128,128]{3,2,1,0:T(8,128)(2,1)S(1)} %get-tuple-element.62), channel_id=1, source_target_pairs={{0,12},{1,13},{2,14},{3,15},{4,8},{5,9},{6,10},{7,11},{8,4},{9,5},... | collective-permute-start | bytes 393224 | tf_op jit(solution)/shard_map/ppermute | solution.py:358
  42.2 15.3 %collective-permute-start.18 = (bf16[2,2,128,128]{3,2,1,0:T(8,128)(2,1)S(1)}, bf16[2,2,128,128]{3,2,1,0:T(8,128)(2,1)S(1)}, u32[]{:S(2)}, u32[]{:S(2)}) collective-permute-start(bf16[2,2,128,128]{3,2,1,0:T(8,128)(2,1)S(1)} %get-tuple-element.63), channel_id=1, source_target_pairs={{0,8},{1,9},{2,10},{3,11},{4,0},{5,1},{6,2},{7,3},{8,12},{9,13},{1... | collective-permute-start | bytes 393224 | tf_op jit(solution)/shard_map/ppermute | solution.py:358
  44.3 16.2 %collective-permute-start.23 = (bf16[256,256]{1,0:T(8,128)(2,1)S(1)}, bf16[256,256]{1,0:T(8,128)(2,1)S(1)}, u32[]{:S(2)}, u32[]{:S(2)}) collective-permute-start(bf16[256,256]{1,0:T(8,128)(2,1)S(1)} %collective-permute-done.8.refs_3_), channel_id=1, source_target_pairs={{0,4},{1,5},{2,6},{3,7},{4,12},{5,13},{6,14},{7,15},{8,0},{9,1},{1... | collective-permute-start | bytes 393224 | tf_op jit(solution)/shard_map/ppermute | solution.py:358
  53.2 7.9 %collective-permute-start.14 = (bf16[256,128]{1,0:T(8,128)(2,1)S(1)}, bf16[256,128]{1,0:T(8,128)(2,1)S(1)}, u32[]{:S(2)}, u32[]{:S(2)}) collective-permute-start(bf16[256,128]{1,0:T(8,128)(2,1)S(1)} %get-tuple-element.59), channel_id=1, source_target_pairs={{0,4},{1,5},{2,6},{3,7},{4,12},{5,13},{6,14},{7,15},{8,0},{9,1},{1... | collective-permute-start | bytes 196616 | tf_op jit(solution)/shard_map/ppermute | solution.py:358
  53.3 7.9 %collective-permute-start.15 = (bf16[256,128]{1,0:T(8,128)(2,1)S(1)}, bf16[256,128]{1,0:T(8,128)(2,1)S(1)}, u32[]{:S(2)}, u32[]{:S(2)}) collective-permute-start(bf16[256,128]{1,0:T(8,128)(2,1)S(1)} %get-tuple-element.60), channel_id=1, source_target_pairs={{0,12},{1,13},{2,14},{3,15},{4,8},{5,9},{6,10},{7,11},{8,4},{9,5},... | collective-permute-start | bytes 196616 | tf_op jit(solution)/shard_map/ppermute | solution.py:358
  54.4 7.1 %collective-permute-start.16 = (bf16[256,128]{1,0:T(8,128)(2,1)S(1)}, bf16[256,128]{1,0:T(8,128)(2,1)S(1)}, u32[]{:S(2)}, u32[]{:S(2)}) collective-permute-start(bf16[256,128]{1,0:T(8,128)(2,1)S(1)} %get-tuple-element.61), channel_id=1, source_target_pairs={{0,8},{1,9},{2,10},{3,11},{4,0},{5,1},{6,2},{7,3},{8,12},{9,13},{1... | collective-permute-start | bytes 196616 | tf_op jit(solution)/shard_map/ppermute | solution.py:358
  61.5 12.7 %collective-permute-start.24 = (bf16[256,256]{1,0:T(8,128)(2,1)S(1)}, bf16[256,256]{1,0:T(8,128)(2,1)S(1)}, u32[]{:S(2)}, u32[]{:S(2)}) collective-permute-start(bf16[256,256]{1,0:T(8,128)(2,1)S(1)} %collective-permute-done.3.refs_4_), channel_id=1, source_target_pairs={{0,4},{1,5},{2,6},{3,7},{4,12},{5,13},{6,14},{7,15},{8,0},{9,1},{1... | collective-permute-start | bytes 393224 | tf_op jit(solution)/shard_map/ppermute | solution.py:358
  63.6 10.5 %collective-permute-start.25 = (bf16[256,256]{1,0:T(8,128)(2,1)S(1)}, bf16[256,256]{1,0:T(8,128)(2,1)S(1)}, u32[]{:S(2)}, u32[]{:S(2)}) collective-permute-start(bf16[256,256]{1,0:T(8,128)(2,1)S(1)} %collective-permute-done.23.refs_5_), channel_id=1, source_target_pairs={{0,4},{1,5},{2,6},{3,7},{4,12},{5,13},{6,14},{7,15},{8,0},{9,1},{1... | collective-permute-start | bytes 393224 | tf_op jit(solution)/shard_map/ppermute | solution.py:358
  63.7 10.5 %copy-start.7 = (bf16[256,256]{1,0:T(8,128)(2,1)S(1)}, bf16[256,256]{1,0:T(8,128)(2,1)}, u32[]{:S(2)}) copy-start(bf16[256,256]{1,0:T(8,128)(2,1)} %get-tuple-element.43.refs_0_) | copy-start | bytes 393220
  65.5 6.6 %collective-permute-start.19 = (bf16[256,128]{1,0:T(8,128)(2,1)S(1)}, bf16[256,128]{1,0:T(8,128)(2,1)S(1)}, u32[]{:S(2)}, u32[]{:S(2)}) collective-permute-start(bf16[256,128]{1,0:T(8,128)(2,1)S(1)} %get-tuple-element.65), channel_id=1, source_target_pairs={{0,4},{1,5},{2,6},{3,7},{4,12},{5,13},{6,14},{7,15},{8,0},{9,1},{1... | collective-permute-start | bytes 196616 | tf_op jit(solution)/shard_map/ppermute | solution.py:358
  66.8 6.2 %collective-permute-start.20 = (bf16[256,128]{1,0:T(8,128)(2,1)S(1)}, bf16[256,128]{1,0:T(8,128)(2,1)S(1)}, u32[]{:S(2)}, u32[]{:S(2)}) collective-permute-start(bf16[256,128]{1,0:T(8,128)(2,1)S(1)} %get-tuple-element.66), channel_id=1, source_target_pairs={{0,12},{1,13},{2,14},{3,15},{4,8},{5,9},{6,10},{7,11},{8,4},{9,5},... | collective-permute-start | bytes 196616 | tf_op jit(solution)/shard_map/ppermute | solution.py:358
  69.9 4.6 %copy-start.6 = (bf16[128,1024]{1,0:T(8,128)(2,1)S(1)}, bf16[128,1024]{1,0:T(8,128)(2,1)}, u32[]{:S(2)}) copy-start(bf16[128,1024]{1,0:T(8,128)(2,1)} %g0.3) | copy-start | bytes 786436
  69.9 4.3 %collective-permute-start.21 = (bf16[256,128]{1,0:T(8,128)(2,1)S(1)}, bf16[256,128]{1,0:T(8,128)(2,1)S(1)}, u32[]{:S(2)}, u32[]{:S(2)}) collective-permute-start(bf16[256,128]{1,0:T(8,128)(2,1)S(1)} %get-tuple-element.67), channel_id=1, source_target_pairs={{0,8},{1,9},{2,10},{3,11},{4,0},{5,1},{6,2},{7,3},{8,12},{9,13},{1... | collective-permute-start | bytes 196616 | tf_op jit(solution)/shard_map/ppermute | solution.py:358
  74.4 2.4 %collective-permute-start.26 = (bf16[4,256,256]{2,1,0:T(8,128)(2,1)S(1)}, bf16[4,256,256]{2,1,0:T(8,128)(2,1)S(1)}, u32[]{:S(2)}, u32[]{:S(2)}) collective-permute-start(bf16[4,256,256]{2,1,0:T(8,128)(2,1)S(1)} %get-tuple-element.74), channel_id=1, source_target_pairs={{0,1},{1,0},{2,3},{3,2},{4,5},{5,4},{6,7},{7,6},{8,9},{9,8},{10,11... | collective-permute-start | bytes 1572872 | tf_op jit(solution)/shard_map/ppermute | solution.py:358
  74.7 2.0 %collective-permute-start.22 = (bf16[512,256]{1,0:T(8,128)(2,1)S(1)}, bf16[512,256]{1,0:T(8,128)(2,1)S(1)}, u32[]{:S(2)}, u32[]{:S(2)}) collective-permute-start(bf16[512,256]{1,0:T(8,128)(2,1)S(1)} %shard_map.97.gated), channel_id=1, source_target_pairs={{0,1},{1,0},{2,3},{3,2},{4,5},{5,4},{6,7},{7,6},{8,9},{9,8},{10,11... | collective-permute-start | bytes 786440 | tf_op jit(solution)/shard_map/ppermute | solution.py:358
  77.5 10.2 %collective-permute-start.27 = (bf16[128,1024]{1,0:T(8,128)(2,1)S(1)}, bf16[128,1024]{1,0:T(8,128)(2,1)S(1)}, u32[]{:S(2)}, u32[]{:S(2)}) collective-permute-start(bf16[128,1024]{1,0:T(8,128)(2,1)S(1)} %get-tuple-element.76), channel_id=1, source_target_pairs={{0,18},{1,19},{2,16},{3,17},{4,22},{5,23},{6,20},{7,21},{8,26},{9,... | collective-permute-start | bytes 786440 | tf_op jit(solution)/shard_map/ppermute | solution.py:358
  79.2 12.5 %collective-permute-start.28 = (bf16[128,1024]{1,0:T(8,128)(2,1)S(1)}, bf16[128,1024]{1,0:T(8,128)(2,1)S(1)}, u32[]{:S(2)}, u32[]{:S(2)}) collective-permute-start(bf16[128,1024]{1,0:T(8,128)(2,1)S(1)} %get-tuple-element.77), channel_id=1, source_target_pairs={{0,2},{1,3},{2,0},{3,1},{4,6},{5,7},{6,4},{7,5},{8,10},{9,11},{10,... | collective-permute-start | bytes 786440 | tf_op jit(solution)/shard_map/ppermute | solution.py:358
  80.6 11.9 %collective-permute-start.29 = (bf16[128,1024]{1,0:T(8,128)(2,1)S(1)}, bf16[128,1024]{1,0:T(8,128)(2,1)S(1)}, u32[]{:S(2)}, u32[]{:S(2)}) collective-permute-start(bf16[128,1024]{1,0:T(8,128)(2,1)S(1)} %get-tuple-element.78), channel_id=1, source_target_pairs={{0,16},{1,17},{2,18},{3,19},{4,20},{5,21},{6,22},{7,23},{8,24},{9,... | collective-permute-start | bytes 786440 | tf_op jit(solution)/shard_map/ppermute | solution.py:358

commit v17 on v16

--- a/solution.py
+++ b/solution.py
@@ -415,9 +415,9 @@
         [shape((512, 256), F32)] + [block] * 4,
         [pltpu.VMEM((512, 256), BF16), pltpu.VMEM((4, 256, 128), BF16)],
         moved=2 << 20,
-    )(after(keep, filters[1]), to_x(give), gate_k, *received, skip[None, :])
+    )(keep, to_x(give), gate_k, *received, skip[None, :])
     columns = [sends[0]] + [to_z(sends[r], r) for r in (1, 2, 3)]
-    r3 = onward(after(r2, *filters[2:], columns[1]))
+    r3 = onward(after(r2, filters[3], columns[1]))
     q3 = onward(after(q2, *columns[1:]))
     table, table_t = tables()
     sends = in_vmem(

time: 93.5 us -> 92.9 us (level)
  starting transfers between devices: 37.4 us -> 36 us
    ppermute x30, starting transfers between devices: 37.4 us -> 36 us  [permute(): return lax.ppermute(values, AXES, pairs)]
  transfers between devices with their start and end apart: 30 -> 30, of which waited for: 18 -> 18; matrix products, arithmetic and copies ran while one was open for 0% -> 0% of each run, Pallas kernels for 6% -> 7%
where the time goes in v17:
time: 92.9 us; the launch traced here: 92.7 us
  waiting for transfers between devices  46.1 us (50%)
  starting transfers between devices  36 us (39%)
  Pallas kernels  8.36 us (9%)
  local copies, waits for them, and re-layouts  1.12 us (1%)
    ppermute x30, waiting for transfers between devices, permute(): return lax.ppermute(values, AXES, pairs)  46.1 us
    ppermute x30, starting transfers between devices, permute(): return lax.ppermute(values, AXES, pairs)  36 us
    pallas_call x9, Pallas kernels, call(): pl.pallas_call(kernel, out_shape=out_shape, in_specs=specs, out_specs=jax...  5.79 us
    pallas_call x1, Pallas kernels, call(): pl.pallas_call(kernel, out_shape=out_shape, in_specs=[pl.BlockSpec(memory...  2.58 us
  transfers between devices with their start and end apart: 30, of which 18 were waited for; matrix products, arithmetic and copies ran while one was open for 0% of the time, Pallas kernels for 7%

profile of v17, /device:TPU:0, one launch (start us, length us, event | category | flops | bytes accessed | tf_op | source)
XLA Modules:
  0.0 92.7 jit_solution(3757646738243576828)
XLA Ops:
  0.0 1.0 %copy-done = bf16[256,1024]{1,0:T(8,128)(2,1)S(1)} copy-done((bf16[256,1024]{1,0:T(8,128)(2,1)S(1)}, bf16[256,1024]{1,0:T(8,128)(2,1)}, u32[]{:S(2)}) %copy-start) | copy-done | bytes 524312
  1.1 0.0 copy-start.2
  1.1 0.0 copy-start.5
  1.1 3.1 %collective-permute-start.2 = (bf16[256,512]{1,0:T(8,128)(2,1)S(1)}, bf16[256,512]{1,0:T(8,128)(2,1)S(1)}, u32[]{:S(2)}, u32[]{:S(2)}) collective-permute-start(bf16[256,512]{1,0:T(8,128)(2,1)S(1)} %constant_dynamic-slice_fusion.after.w0), channel_id=1, source_target_pairs={{0,4},{1,5},{2,6},{3,7},{4,12},{5,13},{6,14},{7,15},{8,0},{9,1},{1... | collective-permute-start | bytes 786440 | tf_op jit(solution)/shard_map/ppermute | solution.py:358
  4.2 2.6 %shard_map.91 = (bf16[128,1024]{1,0:T(8,128)(2,1)}, bf16[128,1024]{1,0:T(8,128)(2,1)}, bf16[128,1024]{1,0:T(8,128)(2,1)}, bf16[256,256]{1,0:T(8,128)(2,1)}, bf16...) custom-call(bf16[128,1024]{1,0:T(8,128)(2,1)} %refs_0_.1, bf16[128,1024]{1,0:T(8,128)(2,1)} %g0.2, ...), custom_call_target="tpu_custom_call" | custom-call | tf_op jit(solution)/shard_map/pallas_call | solution.py:106
  6.8 0.0 copy-start.1
  6.8 2.6 %collective-permute-start.1 = (bf16[256,256]{1,0:T(8,128)(2,1)}, bf16[256,256]{1,0:T(8,128)(2,1)S(1)}, u32[]{:S(2)}, u32[]{:S(2)}) collective-permute-start(bf16[256,256]{1,0:T(8,128)(2,1)} %get-tuple-element.42.refs_0_), channel_id=1, source_target_pairs={{0,4},{1,5},{2,6},{3,7},{4,12},{5,13},{6,14},{7,15},{8,0},{9,1},{1... | collective-permute-start | bytes 393224 | tf_op jit(solution)/shard_map/ppermute | solution.py:358
  9.4 1.5 %collective-permute-start = (bf16[128,1024]{1,0:T(8,128)(2,1)}, bf16[128,1024]{1,0:T(8,128)(2,1)S(1)}, u32[]{:S(2)}, u32[]{:S(2)}) collective-permute-start(bf16[128,1024]{1,0:T(8,128)(2,1)} %get-tuple-element.41), channel_id=1, source_target_pairs={{0,2},{1,3},{2,0},{3,1},{4,6},{5,7},{6,4},{7,5},{8,10},{9,11},{10,... | collective-permute-start | bytes 786440 | tf_op jit(solution)/shard_map/ppermute | solution.py:358
  10.9 1.5 %collective-permute-start.4 = (bf16[128,1024]{1,0:T(8,128)(2,1)}, bf16[128,1024]{1,0:T(8,128)(2,1)S(1)}, u32[]{:S(2)}, u32[]{:S(2)}) collective-permute-start(bf16[128,1024]{1,0:T(8,128)(2,1)} %get-tuple-element.45), channel_id=1, source_target_pairs={{0,16},{1,17},{2,18},{3,19},{4,20},{5,21},{6,22},{7,23},{8,24},{9,... | collective-permute-start | bytes 786440 | tf_op jit(solution)/shard_map/ppermute | solution.py:358
  12.4 0.5 collective-permute-start.5
  12.9 1.4 %collective-permute-done.1.refs_2_ = bf16[256,256]{1,0:T(8,128)(2,1)S(1)} collective-permute-done((bf16[256,256]{1,0:T(8,128)(2,1)}, bf16[256,256]{1,0:T(8,128)(2,1)S(1)}, u32[]{:S(2)}, u32[]{:S(2)}) %collective-permute-start.1) | collective-permute-done | bytes 131104 | tf_op jit(solution)/shard_map/ppermute | solution.py:358
  14.3 0.0 collective-permute-done.2.w1
  14.3 0.9 %collective-permute-start.3 = (bf16[256,256]{1,0:T(8,128)(2,1)S(1)}, bf16[256,256]{1,0:T(8,128)(2,1)S(1)}, u32[]{:S(2)}, u32[]{:S(2)}) collective-permute-start(bf16[256,256]{1,0:T(8,128)(2,1)S(1)} %collective-permute-done.1.refs_2_), channel_id=1, source_target_pairs={{0,4},{1,5},{2,6},{3,7},{4,12},{5,13},{6,14},{7,15},{8,0},{9,1},{1... | collective-permute-start | bytes 393224 | tf_op jit(solution)/shard_map/ppermute | solution.py:358
  15.2 3.3 %collective-permute-start.7 = (bf16[256,512]{1,0:T(8,128)(2,1)S(1)}, bf16[256,512]{1,0:T(8,128)(2,1)S(1)}, u32[]{:S(2)}, u32[]{:S(2)}) collective-permute-start(bf16[256,512]{1,0:T(8,128)(2,1)S(1)} %collective-permute-done.2.w1), channel_id=1, source_target_pairs={{0,4},{1,5},{2,6},{3,7},{4,12},{5,13},{6,14},{7,15},{8,0},{9,1},{1... | collective-permute-start | bytes 786440 | tf_op jit(solution)/shard_map/ppermute | solution.py:358
  18.5 0.4 collective-permute-done.refs_1_.g1
  18.9 2.8 %collective-permute-done.3.refs_4_ = bf16[256,256]{1,0:T(8,128)(2,1)S(1)} collective-permute-done((bf16[256,256]{1,0:T(8,128)(2,1)S(1)}, bf16[256,256]{1,0:T(8,128)(2,1)S(1)}, u32[]{:S(2)}, u32[]{:S(2)}) %collective-permute-start.3) | collective-permute-done | bytes 131104 | tf_op jit(solution)/shard_map/ppermute | solution.py:358
  21.6 2.3 %collective-permute-done.4.refs_2_.g2 = bf16[128,1024]{1,0:T(8,128)(2,1)S(1)} collective-permute-done((bf16[128,1024]{1,0:T(8,128)(2,1)}, bf16[128,1024]{1,0:T(8,128)(2,1)S(1)}, u32[]{:S(2)}, u32[]{:S(2)}) %collective-permute-start.4) | collective-permute-done | bytes 262176 | tf_op jit(solution)/shard_map/ppermute | solution.py:358
  23.9 0.0 collective-permute-done.5.refs_3_.g3
  24.0 0.1 collective-permute-start.10
  24.1 1.3 %collective-permute-start.6 = (bf16[256,256]{1,0:T(8,128)(2,1)S(1)}, bf16[256,256]{1,0:T(8,128)(2,1)S(1)}, u32[]{:S(2)}, u32[]{:S(2)}) collective-permute-start(bf16[256,256]{1,0:T(8,128)(2,1)S(1)} %copy-done.12), channel_id=1, source_target_pairs={{0,2},{1,3},{2,0},{3,1},{4,6},{5,7},{6,4},{7,5},{8,10},{9,11},{10,... | collective-permute-start | bytes 393224 | tf_op jit(solution)/shard_map/ppermute | solution.py:358
  25.4 0.8 collective-permute-start.9
  26.2 0.9 collective-permute-start.11
  27.1 3.4 %collective-permute-done.6.refs_1_ = bf16[256,256]{1,0:T(8,128)(2,1)S(1)} collective-permute-done((bf16[256,256]{1,0:T(8,128)(2,1)S(1)}, bf16[256,256]{1,0:T(8,128)(2,1)S(1)}, u32[]{:S(2)}, u32[]{:S(2)}) %collective-permute-start.6) | collective-permute-done | bytes 131104 | tf_op jit(solution)/shard_map/ppermute | solution.py:358
  30.4 0.9 collective-permute-start.8
  31.3 4.3 %collective-permute-done.9.near = bf16[2,2,128,256]{3,2,1,0:T(8,128)(2,1)S(1)} collective-permute-done((bf16[2,2,128,256]{3,2,1,0:T(8,128)(2,1)S(1)}, bf16[2,2,128,256]{3,2,1,0:T(8,128)(2,1)S(1)}, u32[]{:S(2)}, u32[]{:S(2)}) %collective-permute-start.9) | collective-permute-done | bytes 262176 | tf_op jit(solution)/shard_map/ppermute | solution.py:358
  35.6 0.3 shard_map.93
  35.9 2.1 %collective-permute-done.8.refs_3_ = bf16[256,256]{1,0:T(8,128)(2,1)S(1)} collective-permute-done((bf16[256,256]{1,0:T(8,128)(2,1)S(1)}, bf16[256,256]{1,0:T(8,128)(2,1)S(1)}, u32[]{:S(2)}, u32[]{:S(2)}) %collective-permute-start.8) | collective-permute-done | bytes 131104 | tf_op jit(solution)/shard_map/ppermute | solution.py:358
  38.0 0.0 copy-start.9
  38.0 1.3 %shard_map.94 = (f32[512,256]{1,0:T(8,128)S(1)}, bf16[512,256]{1,0:T(8,128)(2,1)S(1)}) custom-call(bf16[512,512]{1,0:T(8,128)(2,1)S(1)} %shard_map.92.mine, bf16[512,512]{1,0:T(8,128)(2,1)S(1)} %collective-permute-done.10.other, bf16[256,512]{1,0:T(8,128)(2,1)S(1)} %copy-done.3, bf16[256,512]{1,0:T(8,128)(2,1)S(1)} %collective-permute-done.2.w1, ...), custom_call_target="tpu_custom_call" | custom-call | flops 536870912 | bytes 2097152 | tf_op jit(solution)/shard_map/pallas_call | solution.py:37
  39.3 1.3 %collective-permute-start.12 = (bf16[512,256]{1,0:T(8,128)(2,1)S(1)}, bf16[512,256]{1,0:T(8,128)(2,1)S(1)}, u32[]{:S(2)}, u32[]{:S(2)}) collective-permute-start(bf16[512,256]{1,0:T(8,128)(2,1)S(1)} %get-tuple-element.54), channel_id=1, source_target_pairs={{0,2},{1,3},{2,0},{3,1},{4,6},{5,7},{6,4},{7,5},{8,10},{9,11},{10,... | collective-permute-start | bytes 786440 | tf_op jit(solution)/shard_map/ppermute | solution.py:358
  40.6 2.0 %collective-permute-start.23 = (bf16[256,256]{1,0:T(8,128)(2,1)S(1)}, bf16[256,256]{1,0:T(8,128)(2,1)S(1)}, u32[]{:S(2)}, u32[]{:S(2)}) collective-permute-start(bf16[256,256]{1,0:T(8,128)(2,1)S(1)} %collective-permute-done.8.refs_3_), channel_id=1, source_target_pairs={{0,4},{1,5},{2,6},{3,7},{4,12},{5,13},{6,14},{7,15},{8,0},{9,1},{1... | collective-permute-start | bytes 393224 | tf_op jit(solution)/shard_map/ppermute | solution.py:358
  42.6 0.9 collective-permute-start.16
  43.6 1.5 %collective-permute-start.17 = (bf16[2,2,128,128]{3,2,1,0:T(8,128)(2,1)S(1)}, bf16[2,2,128,128]{3,2,1,0:T(8,128)(2,1)S(1)}, u32[]{:S(2)}, u32[]{:S(2)}) collective-permute-start(bf16[2,2,128,128]{3,2,1,0:T(8,128)(2,1)S(1)} %get-tuple-element.60), channel_id=1, source_target_pairs={{0,12},{1,13},{2,14},{3,15},{4,8},{5,9},{6,10},{7,11},{8,4},{9,5},... | collective-permute-start | bytes 393224 | tf_op jit(solution)/shard_map/ppermute | solution.py:358
  45.0 1.6 %collective-permute-done.12.taken = bf16[512,256]{1,0:T(8,128)(2,1)S(1)} collective-permute-done((bf16[512,256]{1,0:T(8,128)(2,1)S(1)}, bf16[512,256]{1,0:T(8,128)(2,1)S(1)}, u32[]{:S(2)}, u32[]{:S(2)}) %collective-permute-start.12) | collective-permute-done | bytes 262176 | tf_op jit(solution)/shard_map/ppermute | solution.py:358
  46.6 0.3 shard_map.95
  46.9 0.1 collective-permute-start.13
  47.0 0.4 collective-permute-done.18.refs_7_
  47.4 1.3 %collective-permute-start.14 = (bf16[256,128]{1,0:T(8,128)(2,1)S(1)}, bf16[256,128]{1,0:T(8,128)(2,1)S(1)}, u32[]{:S(2)}, u32[]{:S(2)}) collective-permute-start(bf16[256,128]{1,0:T(8,128)(2,1)S(1)} %get-tuple-element.57), channel_id=1, source_target_pairs={{0,12},{1,13},{2,14},{3,15},{4,8},{5,9},{6,10},{7,11},{8,4},{9,5},... | collective-permute-start | bytes 196616 | tf_op jit(solution)/shard_map/ppermute | solution.py:358
  48.7 1.2 %collective-permute-done.23.refs_5_ = bf16[256,256]{1,0:T(8,128)(2,1)S(1)} collective-permute-done((bf16[256,256]{1,0:T(8,128)(2,1)S(1)}, bf16[256,256]{1,0:T(8,128)(2,1)S(1)}, u32[]{:S(2)}, u32[]{:S(2)}) %collective-permute-start.23) | collective-permute-done | bytes 131104 | tf_op jit(solution)/shard_map/ppermute | solution.py:358
  49.9 0.9 collective-permute-start.15
  50.8 10.5 %collective-permute-done.13.refs_1_ = bf16[256,128]{1,0:T(8,128)(2,1)S(1)} collective-permute-done((bf16[256,128]{1,0:T(8,128)(2,1)S(1)}, bf16[256,128]{1,0:T(8,128)(2,1)S(1)}, u32[]{:S(2)}, u32[]{:S(2)}) %collective-permute-start.13) | collective-permute-done | bytes 65568 | tf_op jit(solution)/shard_map/ppermute | solution.py:358
  61.2 1.3 %collective-permute-start.24 = (bf16[256,256]{1,0:T(8,128)(2,1)S(1)}, bf16[256,256]{1,0:T(8,128)(2,1)S(1)}, u32[]{:S(2)}, u32[]{:S(2)}) collective-permute-start(bf16[256,256]{1,0:T(8,128)(2,1)S(1)} %collective-permute-done.3.refs_4_), channel_id=1, source_target_pairs={{0,4},{1,5},{2,6},{3,7},{4,12},{5,13},{6,14},{7,15},{8,0},{9,1},{1... | collective-permute-start | bytes 393224 | tf_op jit(solution)/shard_map/ppermute | solution.py:358
  62.5 1.1 %collective-permute-start.25 = (bf16[256,256]{1,0:T(8,128)(2,1)S(1)}, bf16[256,256]{1,0:T(8,128)(2,1)S(1)}, u32[]{:S(2)}, u32[]{:S(2)}) collective-permute-start(bf16[256,256]{1,0:T(8,128)(2,1)S(1)} %collective-permute-done.23.refs_5_), channel_id=1, source_target_pairs={{0,4},{1,5},{2,6},{3,7},{4,12},{5,13},{6,14},{7,15},{8,0},{9,1},{1... | collective-permute-start | bytes 393224 | tf_op jit(solution)/shard_map/ppermute | solution.py:358
  63.6 1.8 %shard_map.96 = (bf16[256,128]{1,0:T(8,128)(2,1)S(1)}, bf16[256,128]{1,0:T(8,128)(2,1)S(1)}, bf16[256,128]{1,0:T(8,128)(2,1)S(1)}, bf16[256,128]{1,0:T(8,128)(2,1)S(1)}) custom-call(bf16[256,128]{1,0:T(8,128)(2,1)S(1)} %get-tuple-element.55.refs_0_, bf16[256,128]{1,0:T(8,128)(2,1)S(1)} %collective-permute-done.13.refs_1_, ...), custom_call_target="tpu_custom_call" | custom-call | flops 1073741824 | bytes 5242880 | tf_op jit(solution)/shard_map/pallas_call | solution.py:37
  65.4 1.3 %collective-permute-start.19 = (bf16[256,128]{1,0:T(8,128)(2,1)S(1)}, bf16[256,128]{1,0:T(8,128)(2,1)S(1)}, u32[]{:S(2)}, u32[]{:S(2)}) collective-permute-start(bf16[256,128]{1,0:T(8,128)(2,1)S(1)} %get-tuple-element.63), channel_id=1, source_target_pairs={{0,4},{1,5},{2,6},{3,7},{4,12},{5,13},{6,14},{7,15},{8,0},{9,1},{1... | collective-permute-start | bytes 196616 | tf_op jit(solution)/shard_map/ppermute | solution.py:358
  66.7 2.1 %collective-permute-start.20 = (bf16[256,128]{1,0:T(8,128)(2,1)S(1)}, bf16[256,128]{1,0:T(8,128)(2,1)S(1)}, u32[]{:S(2)}, u32[]{:S(2)}) collective-permute-start(bf16[256,128]{1,0:T(8,128)(2,1)S(1)} %get-tuple-element.64), channel_id=1, source_target_pairs={{0,12},{1,13},{2,14},{3,15},{4,8},{5,9},{6,10},{7,11},{8,4},{9,5},... | collective-permute-start | bytes 196616 | tf_op jit(solution)/shard_map/ppermute | solution.py:358
  68.8 0.8 collective-permute-start.21
  69.6 2.5 %collective-permute-done.19.e1 = bf16[256,128]{1,0:T(8,128)(2,1)S(1)} collective-permute-done((bf16[256,128]{1,0:T(8,128)(2,1)S(1)}, bf16[256,128]{1,0:T(8,128)(2,1)S(1)}, u32[]{:S(2)}, u32[]{:S(2)}) %collective-permute-start.19) | collective-permute-done | bytes 65568 | tf_op jit(solution)/shard_map/ppermute | solution.py:358
  72.1 0.8 collective-permute-done.20.e2
  72.9 0.6 collective-permute-done.21.e3
  73.5 0.2 shard_map.98
  73.7 0.1 collective-permute-start.26
  73.8 0.2 shard_map.97.gated
  74.1 0.5 collective-permute-start.22
  74.6 1.5 %collective-permute-done.22.other = bf16[512,256]{1,0:T(8,128)(2,1)S(1)} collective-permute-done((bf16[512,256]{1,0:T(8,128)(2,1)S(1)}, bf16[512,256]{1,0:T(8,128)(2,1)S(1)}, u32[]{:S(2)}, u32[]{:S(2)}) %collective-permute-start.22) | collective-permute-done | bytes 262176 | tf_op jit(solution)/shard_map/ppermute | solution.py:358
  76.1 0.8 shard_map.100
  76.9 1.9 %collective-permute-start.27 = (bf16[128,1024]{1,0:T(8,128)(2,1)S(1)}, bf16[128,1024]{1,0:T(8,128)(2,1)S(1)}, u32[]{:S(2)}, u32[]{:S(2)}) collective-permute-start(bf16[128,1024]{1,0:T(8,128)(2,1)S(1)} %get-tuple-element.74), channel_id=1, source_target_pairs={{0,18},{1,19},{2,16},{3,17},{4,22},{5,23},{6,20},{7,21},{8,26},{9,... | collective-permute-start | bytes 786440 | tf_op jit(solution)/shard_map/ppermute | solution.py:358
  78.8 0.5 collective-permute-start.28
  79.3 0.8 shard_map.99
  80.1 1.2 %collective-permute-start.29 = (bf16[128,1024]{1,0:T(8,128)(2,1)S(1)}, bf16[128,1024]{1,0:T(8,128)(2,1)S(1)}, u32[]{:S(2)}, u32[]{:S(2)}) collective-permute-start(bf16[128,1024]{1,0:T(8,128)(2,1)S(1)} %get-tuple-element.76), channel_id=1, source_target_pairs={{0,16},{1,17},{2,18},{3,19},{4,20},{5,21},{6,22},{7,23},{8,24},{9,... | collective-permute-start | bytes 786440 | tf_op jit(solution)/shard_map/ppermute | solution.py:358
  81.3 5.7 %collective-permute-done.27 = bf16[128,1024]{1,0:T(8,128)(2,1)S(1)} collective-permute-done((bf16[128,1024]{1,0:T(8,128)(2,1)S(1)}, bf16[128,1024]{1,0:T(8,128)(2,1)S(1)}, u32[]{:S(2)}, u32[]{:S(2)}) %collective-permute-start.27) | collective-permute-done | bytes 262176 | tf_op jit(solution)/shard_map/ppermute | solution.py:358
  87.1 4.2 %collective-permute-done.28 = bf16[128,1024]{1,0:T(8,128)(2,1)S(1)} collective-permute-done((bf16[128,1024]{1,0:T(8,128)(2,1)S(1)}, bf16[128,1024]{1,0:T(8,128)(2,1)S(1)}, u32[]{:S(2)}, u32[]{:S(2)}) %collective-permute-start.28) | collective-permute-done | bytes 262176 | tf_op jit(solution)/shard_map/ppermute | solution.py:358
  91.3 0.6 collective-permute-done.29
  91.8 0.8 add_convert_fusion
  (34 shorter events, 0.1 us)
Async XLA Ops:
  0.0 1.0 %copy-start = (bf16[256,1024]{1,0:T(8,128)(2,1)S(1)}, bf16[256,1024]{1,0:T(8,128)(2,1)}, u32[]{:S(2)}) copy-start(bf16[256,1024]{1,0:T(8,128)(2,1)} %param.12) | copy-start | bytes 1572868
  1.1 3.1 %copy-start.2 = (bf16[256,512]{1,0:T(8,128)(2,1)}, bf16[256,512]{1,0:T(8,128)(2,1)S(1)}, u32[]{:S(2)}) copy-start(bf16[256,512]{1,0:T(8,128)(2,1)S(1)} %constant_dynamic-slice_fusion.after.w0) | copy-start | bytes 786436
  1.1 22.9 %copy-start.5 = (bf16[128,1024]{1,0:T(8,128)(2,1)S(1)}, bf16[128,1024]{1,0:T(8,128)(2,1)}, u32[]{:S(2)}) copy-start(bf16[128,1024]{1,0:T(8,128)(2,1)} %refs_0_.1) | copy-start | bytes 786436
  1.1 13.2 %collective-permute-start.2 = (bf16[256,512]{1,0:T(8,128)(2,1)S(1)}, bf16[256,512]{1,0:T(8,128)(2,1)S(1)}, u32[]{:S(2)}, u32[]{:S(2)}) collective-permute-start(bf16[256,512]{1,0:T(8,128)(2,1)S(1)} %constant_dynamic-slice_fusion.after.w0), channel_id=1, source_target_pairs={{0,4},{1,5},{2,6},{3,7},{4,12},{5,13},{6,14},{7,15},{8,0},{9,1},{1... | collective-permute-start | bytes 786440 | tf_op jit(solution)/shard_map/ppermute | solution.py:358
  6.8 28.8 %copy-start.1 = (bf16[2,2,128,1024]{3,2,1,0:T(8,128)(2,1)S(1)}, bf16[2,2,128,1024]{3,2,1,0:T(8,128)(2,1)}, u32[]{:S(2)}) copy-start(bf16[2,2,128,1024]{3,2,1,0:T(8,128)(2,1)} %filt.3) | copy-start | bytes 3145732
  6.8 7.5 %collective-permute-start.1 = (bf16[256,256]{1,0:T(8,128)(2,1)}, bf16[256,256]{1,0:T(8,128)(2,1)S(1)}, u32[]{:S(2)}, u32[]{:S(2)}) collective-permute-start(bf16[256,256]{1,0:T(8,128)(2,1)} %get-tuple-element.42.refs_0_), channel_id=1, source_target_pairs={{0,4},{1,5},{2,6},{3,7},{4,12},{5,13},{6,14},{7,15},{8,0},{9,1},{1... | collective-permute-start | bytes 393224 | tf_op jit(solution)/shard_map/ppermute | solution.py:358
  9.4 9.5 %collective-permute-start = (bf16[128,1024]{1,0:T(8,128)(2,1)}, bf16[128,1024]{1,0:T(8,128)(2,1)S(1)}, u32[]{:S(2)}, u32[]{:S(2)}) collective-permute-start(bf16[128,1024]{1,0:T(8,128)(2,1)} %get-tuple-element.41), channel_id=1, source_target_pairs={{0,2},{1,3},{2,0},{3,1},{4,6},{5,7},{6,4},{7,5},{8,10},{9,11},{10,... | collective-permute-start | bytes 786440 | tf_op jit(solution)/shard_map/ppermute | solution.py:358
  10.9 13.0 %collective-permute-start.4 = (bf16[128,1024]{1,0:T(8,128)(2,1)}, bf16[128,1024]{1,0:T(8,128)(2,1)S(1)}, u32[]{:S(2)}, u32[]{:S(2)}) collective-permute-start(bf16[128,1024]{1,0:T(8,128)(2,1)} %get-tuple-element.45), channel_id=1, source_target_pairs={{0,16},{1,17},{2,18},{3,19},{4,20},{5,21},{6,22},{7,23},{8,24},{9,... | collective-permute-start | bytes 786440 | tf_op jit(solution)/shard_map/ppermute | solution.py:358
  12.4 11.6 %copy-start.12 = (bf16[256,256]{1,0:T(8,128)(2,1)S(1)}, bf16[256,256]{1,0:T(8,128)(2,1)}, u32[]{:S(2)}) copy-start(bf16[256,256]{1,0:T(8,128)(2,1)} %get-tuple-element.48) | copy-start | bytes 393220
  12.4 13.0 %copy-start.11 = (bf16[2,2,128,256]{3,2,1,0:T(8,128)(2,1)S(1)}, bf16[2,2,128,256]{3,2,1,0:T(8,128)(2,1)}, u32[]{:S(2)}) copy-start(bf16[2,2,128,256]{3,2,1,0:T(8,128)(2,1)} %get-tuple-element.50) | copy-start | bytes 786436
  12.4 11.5 %collective-permute-start.5 = (bf16[128,1024]{1,0:T(8,128)(2,1)}, bf16[128,1024]{1,0:T(8,128)(2,1)S(1)}, u32[]{:S(2)}, u32[]{:S(2)}) collective-permute-start(bf16[128,1024]{1,0:T(8,128)(2,1)} %get-tuple-element.46), channel_id=1, source_target_pairs={{0,18},{1,19},{2,16},{3,17},{4,22},{5,23},{6,20},{7,21},{8,26},{9,... | collective-permute-start | bytes 786440 | tf_op jit(solution)/shard_map/ppermute | solution.py:358
  14.3 7.3 %collective-permute-start.3 = (bf16[256,256]{1,0:T(8,128)(2,1)S(1)}, bf16[256,256]{1,0:T(8,128)(2,1)S(1)}, u32[]{:S(2)}, u32[]{:S(2)}) collective-permute-start(bf16[256,256]{1,0:T(8,128)(2,1)S(1)} %collective-permute-done.1.refs_2_), channel_id=1, source_target_pairs={{0,4},{1,5},{2,6},{3,7},{4,12},{5,13},{6,14},{7,15},{8,0},{9,1},{1... | collective-permute-start | bytes 393224 | tf_op jit(solution)/shard_map/ppermute | solution.py:358
  15.2 10.9 %collective-permute-start.7 = (bf16[256,512]{1,0:T(8,128)(2,1)S(1)}, bf16[256,512]{1,0:T(8,128)(2,1)S(1)}, u32[]{:S(2)}, u32[]{:S(2)}) collective-permute-start(bf16[256,512]{1,0:T(8,128)(2,1)S(1)} %collective-permute-done.2.w1), channel_id=1, source_target_pairs={{0,4},{1,5},{2,6},{3,7},{4,12},{5,13},{6,14},{7,15},{8,0},{9,1},{1... | collective-permute-start | bytes 786440 | tf_op jit(solution)/shard_map/ppermute | solution.py:358
  24.0 14.0 %collective-permute-start.10 = (bf16[512,512]{1,0:T(8,128)(2,1)S(1)}, bf16[512,512]{1,0:T(8,128)(2,1)S(1)}, u32[]{:S(2)}, u32[]{:S(2)}) collective-permute-start(bf16[512,512]{1,0:T(8,128)(2,1)S(1)} %shard_map.92.mine), channel_id=1, source_target_pairs={{0,1},{1,0},{2,3},{3,2},{4,5},{5,4},{6,7},{7,6},{8,9},{9,8},{10,11... | collective-permute-start | bytes 1572872 | tf_op jit(solution)/shard_map/ppermute | solution.py:358
  24.1 6.4 %collective-permute-start.6 = (bf16[256,256]{1,0:T(8,128)(2,1)S(1)}, bf16[256,256]{1,0:T(8,128)(2,1)S(1)}, u32[]{:S(2)}, u32[]{:S(2)}) collective-permute-start(bf16[256,256]{1,0:T(8,128)(2,1)S(1)} %copy-done.12), channel_id=1, source_target_pairs={{0,2},{1,3},{2,0},{3,1},{4,6},{5,7},{6,4},{7,5},{8,10},{9,11},{10,... | collective-permute-start | bytes 393224 | tf_op jit(solution)/shard_map/ppermute | solution.py:358
  25.4 12.6 %copy-start.3 = (bf16[256,512]{1,0:T(8,128)(2,1)S(1)}, bf16[256,512]{1,0:T(8,128)(2,1)}, u32[]{:S(2)}) copy-start(bf16[256,512]{1,0:T(8,128)(2,1)} %copy-done.2) | copy-start | bytes 786436
  25.4 10.2 %collective-permute-start.9 = (bf16[2,2,128,256]{3,2,1,0:T(8,128)(2,1)S(1)}, bf16[2,2,128,256]{3,2,1,0:T(8,128)(2,1)S(1)}, u32[]{:S(2)}, u32[]{:S(2)}) collective-permute-start(bf16[2,2,128,256]{3,2,1,0:T(8,128)(2,1)S(1)} %copy-done.11), channel_id=1, source_target_pairs={{0,2},{1,3},{2,0},{3,1},{4,6},{5,7},{6,4},{7,5},{8,10},{9,11},{10,... | collective-permute-start | bytes 786440 | tf_op jit(solution)/shard_map/ppermute | solution.py:358
  26.2 11.8 %collective-permute-start.11 = (bf16[256,512]{1,0:T(8,128)(2,1)S(1)}, bf16[256,512]{1,0:T(8,128)(2,1)S(1)}, u32[]{:S(2)}, u32[]{:S(2)}) collective-permute-start(bf16[256,512]{1,0:T(8,128)(2,1)S(1)} %collective-permute-done.7.w2), channel_id=1, source_target_pairs={{0,4},{1,5},{2,6},{3,7},{4,12},{5,13},{6,14},{7,15},{8,0},{9,1},{1... | collective-permute-start | bytes 786440 | tf_op jit(solution)/shard_map/ppermute | solution.py:358
  30.4 7.5 %collective-permute-start.8 = (bf16[256,256]{1,0:T(8,128)(2,1)S(1)}, bf16[256,256]{1,0:T(8,128)(2,1)S(1)}, u32[]{:S(2)}, u32[]{:S(2)}) collective-permute-start(bf16[256,256]{1,0:T(8,128)(2,1)S(1)} %collective-permute-done.6.refs_1_), channel_id=1, source_target_pairs={{0,4},{1,5},{2,6},{3,7},{4,12},{5,13},{6,14},{7,15},{8,0},{9,1},{1... | collective-permute-start | bytes 393224 | tf_op jit(solution)/shard_map/ppermute | solution.py:358
  38.0 8.6 %copy-start.4 = (bf16[128,1024]{1,0:T(8,128)(2,1)S(1)}, bf16[128,1024]{1,0:T(8,128)(2,1)}, u32[]{:S(2)}) copy-start(bf16[128,1024]{1,0:T(8,128)(2,1)} %g0.2) | copy-start | bytes 786436
  38.0 25.6 %copy-start.9 = (bf16[16,256,128]{2,1,0:T(8,128)(2,1)S(1)}, bf16[16,256,128]{2,1,0:T(8,128)(2,1)}, u32[]{:S(2)}) copy-start(bf16[16,256,128]{2,1,0:T(8,128)(2,1)} %constant.17.clone.refs_9_) | copy-start | bytes 3145732
  39.3 7.3 %collective-permute-start.12 = (bf16[512,256]{1,0:T(8,128)(2,1)S(1)}, bf16[512,256]{1,0:T(8,128)(2,1)S(1)}, u32[]{:S(2)}, u32[]{:S(2)}) collective-permute-start(bf16[512,256]{1,0:T(8,128)(2,1)S(1)} %get-tuple-element.54), channel_id=1, source_target_pairs={{0,2},{1,3},{2,0},{3,1},{4,6},{5,7},{6,4},{7,5},{8,10},{9,11},{10,... | collective-permute-start | bytes 786440 | tf_op jit(solution)/shard_map/ppermute | solution.py:358
  40.6 6.0 %copy-start.8 = (f32[1024]{0:T(1024)S(1)}, f32[1024]{0:T(1024)}, u32[]{:S(2)}) copy-start(f32[1024]{0:T(1024)} %param.13) | copy-start | bytes 12292
  40.6 23.0 %copy-start.10 = (bf16[16,256,128]{2,1,0:T(8,128)(2,1)S(1)}, bf16[16,256,128]{2,1,0:T(8,128)(2,1)}, u32[]{:S(2)}) copy-start(bf16[16,256,128]{2,1,0:T(8,128)(2,1)} %constant.16.clone.refs_8_) | copy-start | bytes 3145732
  40.6 6.8 %collective-permute-start.18 = (bf16[2,2,128,128]{3,2,1,0:T(8,128)(2,1)S(1)}, bf16[2,2,128,128]{3,2,1,0:T(8,128)(2,1)S(1)}, u32[]{:S(2)}, u32[]{:S(2)}) collective-permute-start(bf16[2,2,128,128]{3,2,1,0:T(8,128)(2,1)S(1)} %get-tuple-element.61), channel_id=1, source_target_pairs={{0,8},{1,9},{2,10},{3,11},{4,0},{5,1},{6,2},{7,3},{8,12},{9,13},{1... | collective-permute-start | bytes 393224 | tf_op jit(solution)/shard_map/ppermute | solution.py:358
  40.6 9.3 %collective-permute-start.23 = (bf16[256,256]{1,0:T(8,128)(2,1)S(1)}, bf16[256,256]{1,0:T(8,128)(2,1)S(1)}, u32[]{:S(2)}, u32[]{:S(2)}) collective-permute-start(bf16[256,256]{1,0:T(8,128)(2,1)S(1)} %collective-permute-done.8.refs_3_), channel_id=1, source_target_pairs={{0,4},{1,5},{2,6},{3,7},{4,12},{5,13},{6,14},{7,15},{8,0},{9,1},{1... | collective-permute-start | bytes 393224 | tf_op jit(solution)/shard_map/ppermute | solution.py:358
  42.6 20.9 %collective-permute-start.16 = (bf16[2,2,128,128]{3,2,1,0:T(8,128)(2,1)S(1)}, bf16[2,2,128,128]{3,2,1,0:T(8,128)(2,1)S(1)}, u32[]{:S(2)}, u32[]{:S(2)}) collective-permute-start(bf16[2,2,128,128]{3,2,1,0:T(8,128)(2,1)S(1)} %get-tuple-element.59), channel_id=1, source_target_pairs={{0,4},{1,5},{2,6},{3,7},{4,12},{5,13},{6,14},{7,15},{8,0},{9,1},{1... | collective-permute-start | bytes 393224 | tf_op jit(solution)/shard_map/ppermute | solution.py:358
  43.6 20.0 %collective-permute-start.17 = (bf16[2,2,128,128]{3,2,1,0:T(8,128)(2,1)S(1)}, bf16[2,2,128,128]{3,2,1,0:T(8,128)(2,1)S(1)}, u32[]{:S(2)}, u32[]{:S(2)}) collective-permute-start(bf16[2,2,128,128]{3,2,1,0:T(8,128)(2,1)S(1)} %get-tuple-element.60), channel_id=1, source_target_pairs={{0,12},{1,13},{2,14},{3,15},{4,8},{5,9},{6,10},{7,11},{8,4},{9,5},... | collective-permute-start | bytes 393224 | tf_op jit(solution)/shard_map/ppermute | solution.py:358
  46.9 14.3 %collective-permute-start.13 = (bf16[256,128]{1,0:T(8,128)(2,1)S(1)}, bf16[256,128]{1,0:T(8,128)(2,1)S(1)}, u32[]{:S(2)}, u32[]{:S(2)}) collective-permute-start(bf16[256,128]{1,0:T(8,128)(2,1)S(1)} %get-tuple-element.56), channel_id=1, source_target_pairs={{0,4},{1,5},{2,6},{3,7},{4,12},{5,13},{6,14},{7,15},{8,0},{9,1},{1... | collective-permute-start | bytes 196616 | tf_op jit(solution)/shard_map/ppermute | solution.py:358
  47.4 13.8 %collective-permute-start.14 = (bf16[256,128]{1,0:T(8,128)(2,1)S(1)}, bf16[256,128]{1,0:T(8,128)(2,1)S(1)}, u32[]{:S(2)}, u32[]{:S(2)}) collective-permute-start(bf16[256,128]{1,0:T(8,128)(2,1)S(1)} %get-tuple-element.57), channel_id=1, source_target_pairs={{0,12},{1,13},{2,14},{3,15},{4,8},{5,9},{6,10},{7,11},{8,4},{9,5},... | collective-permute-start | bytes 196616 | tf_op jit(solution)/shard_map/ppermute | solution.py:358
  49.9 11.3 %collective-permute-start.15 = (bf16[256,128]{1,0:T(8,128)(2,1)S(1)}, bf16[256,128]{1,0:T(8,128)(2,1)S(1)}, u32[]{:S(2)}, u32[]{:S(2)}) collective-permute-start(bf16[256,128]{1,0:T(8,128)(2,1)S(1)} %get-tuple-element.58), channel_id=1, source_target_pairs={{0,8},{1,9},{2,10},{3,11},{4,0},{5,1},{6,2},{7,3},{8,12},{9,13},{1... | collective-permute-start | bytes 196616 | tf_op jit(solution)/shard_map/ppermute | solution.py:358
  61.2 12.3 %collective-permute-start.24 = (bf16[256,256]{1,0:T(8,128)(2,1)S(1)}, bf16[256,256]{1,0:T(8,128)(2,1)S(1)}, u32[]{:S(2)}, u32[]{:S(2)}) collective-permute-start(bf16[256,256]{1,0:T(8,128)(2,1)S(1)} %collective-permute-done.3.refs_4_), channel_id=1, source_target_pairs={{0,4},{1,5},{2,6},{3,7},{4,12},{5,13},{6,14},{7,15},{8,0},{9,1},{1... | collective-permute-start | bytes 393224 | tf_op jit(solution)/shard_map/ppermute | solution.py:358
  62.5 11.0 %collective-permute-start.25 = (bf16[256,256]{1,0:T(8,128)(2,1)S(1)}, bf16[256,256]{1,0:T(8,128)(2,1)S(1)}, u32[]{:S(2)}, u32[]{:S(2)}) collective-permute-start(bf16[256,256]{1,0:T(8,128)(2,1)S(1)} %collective-permute-done.23.refs_5_), channel_id=1, source_target_pairs={{0,4},{1,5},{2,6},{3,7},{4,12},{5,13},{6,14},{7,15},{8,0},{9,1},{1... | collective-permute-start | bytes 393224 | tf_op jit(solution)/shard_map/ppermute | solution.py:358
  63.6 10.0 %copy-start.7 = (bf16[256,256]{1,0:T(8,128)(2,1)S(1)}, bf16[256,256]{1,0:T(8,128)(2,1)}, u32[]{:S(2)}) copy-start(bf16[256,256]{1,0:T(8,128)(2,1)} %get-tuple-element.42.refs_0_) | copy-start | bytes 393220
  65.4 6.6 %collective-permute-start.19 = (bf16[256,128]{1,0:T(8,128)(2,1)S(1)}, bf16[256,128]{1,0:T(8,128)(2,1)S(1)}, u32[]{:S(2)}, u32[]{:S(2)}) collective-permute-start(bf16[256,128]{1,0:T(8,128)(2,1)S(1)} %get-tuple-element.63), channel_id=1, source_target_pairs={{0,4},{1,5},{2,6},{3,7},{4,12},{5,13},{6,14},{7,15},{8,0},{9,1},{1... | collective-permute-start | bytes 196616 | tf_op jit(solution)/shard_map/ppermute | solution.py:358
  66.7 6.1 %collective-permute-start.20 = (bf16[256,128]{1,0:T(8,128)(2,1)S(1)}, bf16[256,128]{1,0:T(8,128)(2,1)S(1)}, u32[]{:S(2)}, u32[]{:S(2)}) collective-permute-start(bf16[256,128]{1,0:T(8,128)(2,1)S(1)} %get-tuple-element.64), channel_id=1, source_target_pairs={{0,12},{1,13},{2,14},{3,15},{4,8},{5,9},{6,10},{7,11},{8,4},{9,5},... | collective-permute-start | bytes 196616 | tf_op jit(solution)/shard_map/ppermute | solution.py:358
  68.8 5.0 %copy-start.6 = (bf16[128,1024]{1,0:T(8,128)(2,1)S(1)}, bf16[128,1024]{1,0:T(8,128)(2,1)}, u32[]{:S(2)}) copy-start(bf16[128,1024]{1,0:T(8,128)(2,1)} %g0.3) | copy-start | bytes 786436
  68.8 4.7 %collective-permute-start.21 = (bf16[256,128]{1,0:T(8,128)(2,1)S(1)}, bf16[256,128]{1,0:T(8,128)(2,1)S(1)}, u32[]{:S(2)}, u32[]{:S(2)}) collective-permute-start(bf16[256,128]{1,0:T(8,128)(2,1)S(1)} %get-tuple-element.65), channel_id=1, source_target_pairs={{0,8},{1,9},{2,10},{3,11},{4,0},{5,1},{6,2},{7,3},{8,12},{9,13},{1... | collective-permute-start | bytes 196616 | tf_op jit(solution)/shard_map/ppermute | solution.py:358
  73.7 2.4 %collective-permute-start.26 = (bf16[4,256,256]{2,1,0:T(8,128)(2,1)S(1)}, bf16[4,256,256]{2,1,0:T(8,128)(2,1)S(1)}, u32[]{:S(2)}, u32[]{:S(2)}) collective-permute-start(bf16[4,256,256]{2,1,0:T(8,128)(2,1)S(1)} %get-tuple-element.72), channel_id=1, source_target_pairs={{0,1},{1,0},{2,3},{3,2},{4,5},{5,4},{6,7},{7,6},{8,9},{9,8},{10,11... | collective-permute-start | bytes 1572872 | tf_op jit(solution)/shard_map/ppermute | solution.py:358
  74.1 2.0 %collective-permute-start.22 = (bf16[512,256]{1,0:T(8,128)(2,1)S(1)}, bf16[512,256]{1,0:T(8,128)(2,1)S(1)}, u32[]{:S(2)}, u32[]{:S(2)}) collective-permute-start(bf16[512,256]{1,0:T(8,128)(2,1)S(1)} %shard_map.97.gated), channel_id=1, source_target_pairs={{0,1},{1,0},{2,3},{3,2},{4,5},{5,4},{6,7},{7,6},{8,9},{9,8},{10,11... | collective-permute-start | bytes 786440 | tf_op jit(solution)/shard_map/ppermute | solution.py:358
  76.9 10.2 %collective-permute-start.27 = (bf16[128,1024]{1,0:T(8,128)(2,1)S(1)}, bf16[128,1024]{1,0:T(8,128)(2,1)S(1)}, u32[]{:S(2)}, u32[]{:S(2)}) collective-permute-start(bf16[128,1024]{1,0:T(8,128)(2,1)S(1)} %get-tuple-element.74), channel_id=1, source_target_pairs={{0,18},{1,19},{2,16},{3,17},{4,22},{5,23},{6,20},{7,21},{8,26},{9,... | collective-permute-start | bytes 786440 | tf_op jit(solution)/shard_map/ppermute | solution.py:358
  78.8 12.5 %collective-permute-start.28 = (bf16[128,1024]{1,0:T(8,128)(2,1)S(1)}, bf16[128,1024]{1,0:T(8,128)(2,1)S(1)}, u32[]{:S(2)}, u32[]{:S(2)}) collective-permute-start(bf16[128,1024]{1,0:T(8,128)(2,1)S(1)} %get-tuple-element.75), channel_id=1, source_target_pairs={{0,2},{1,3},{2,0},{3,1},{4,6},{5,7},{6,4},{7,5},{8,10},{9,11},{10,... | collective-permute-start | bytes 786440 | tf_op jit(solution)/shard_map/ppermute | solution.py:358
  80.1 11.8 %collective-permute-start.29 = (bf16[128,1024]{1,0:T(8,128)(2,1)S(1)}, bf16[128,1024]{1,0:T(8,128)(2,1)S(1)}, u32[]{:S(2)}, u32[]{:S(2)}) collective-permute-start(bf16[128,1024]{1,0:T(8,128)(2,1)S(1)} %get-tuple-element.76), channel_id=1, source_target_pairs={{0,16},{1,17},{2,18},{3,19},{4,20},{5,21},{6,22},{7,23},{8,24},{9,... | collective-permute-start | bytes 786440 | tf_op jit(solution)/shard_map/ppermute | solution.py:358

commit v18 on v17

--- a/solution.py
+++ b/solution.py
@@ -313,7 +313,7 @@
 
 
 def sort_weight(*refs):
-    pieces, keep, give = refs[:8], refs[8], refs[9]
+    pieces, keep, give = refs[:7], refs[7], refs[8]
     _, x, z, c = place()
     for r in range(4):
         owner = around(z, -r)
@@ -322,11 +322,11 @@
 
             @pl.when(owner // 2 == c)
             def _():
-                keep[to] = pieces[2 * r + k][...]
+                keep[to] = (pieces[2 * r + k][...] if r < 3 else pieces[6][k])
 
             @pl.when(owner // 2 != c)
             def _():
-                give[to] = pieces[2 * r + k][...]
+                give[to] = (pieces[2 * r + k][...] if r < 3 else pieces[6][k])
 
 
 def out_kernel(blocks, gated, other, keep, theirs, *outs):
@@ -417,8 +417,7 @@
         moved=2 << 20,
     )(keep, to_x(give), gate_k, *received, skip[None, :])
     columns = [sends[0]] + [to_z(sends[r], r) for r in (1, 2, 3)]
-    r3 = onward(after(r2, filters[3], columns[1]))
-    q3 = onward(after(q2, *columns[1:]))
+    last = onward(after(jnp.stack([q2, r2]), filters[3], *columns[1:]))
     table, table_t = tables()
     sends = in_vmem(
         conv_kernel,
@@ -434,7 +433,7 @@
     )(*columns, *filters, table, table_t)
     rows = [sends[0]] + [to_z(sends[r], r) for r in (1, 2, 3)]
 
-    hops = [own_o, got_o, q1, r1, q2, r2, q3, after(r3, *rows[1:])]
+    hops = [own_o, got_o, q1, r1, q2, r2, after(last, *rows[1:])]
     quad = shape((4, 256, 256), BF16)
     keep, give = in_vmem(sort_weight, [quad] * 2, moved=2 << 20)(*hops)
     theirs = to_core(give)

time: 92.9 us -> 92.8 us (level)
  starting transfers between devices: 36 us -> 34.7 us
  waiting for transfers between devices: 46.1 us -> 47.3 us
    ppermute x30 -> x29, starting transfers between devices: 36 us -> 34.7 us  [permute(): return lax.ppermute(values, AXES, pairs)]
    ppermute x30 -> x29, waiting for transfers between devices: 46.1 us -> 47.3 us  [permute(): return lax.ppermute(values, AXES, pairs)]
  transfers between devices with their start and end apart: 30 -> 29, of which waited for: 18 -> 16; matrix products, arithmetic and copies ran while one was open for 0% -> 0% of each run, Pallas kernels for 7% -> 7%
where the time goes in v18:
time: 92.8 us; the launch traced here: 92.6 us
  waiting for transfers between devices  47.3 us (51%)
  starting transfers between devices  34.7 us (37%)
  Pallas kernels  8.38 us (9%)
  local copies, waits for them, and re-layouts  1.11 us (1%)
    ppermute x29, waiting for transfers between devices, permute(): return lax.ppermute(values, AXES, pairs)  47.3 us
    ppermute x29, starting transfers between devices, permute(): return lax.ppermute(values, AXES, pairs)  34.7 us
    pallas_call x9, Pallas kernels, call(): pl.pallas_call(kernel, out_shape=out_shape, in_specs=specs, out_specs=jax...  5.8 us
    pallas_call x1, Pallas kernels, call(): pl.pallas_call(kernel, out_shape=out_shape, in_specs=[pl.BlockSpec(memory...  2.58 us
  transfers between devices with their start and end apart: 29, of which 16 were waited for; matrix products, arithmetic and copies ran while one was open for 0% of the time, Pallas kernels for 7%

profile of v18, /device:TPU:0, one launch (start us, length us, event | category | flops | bytes accessed | tf_op | source)
XLA Modules:
  0.0 92.6 jit_solution(679926126180306203)
XLA Ops:
  0.0 1.0 %copy-done = bf16[256,1024]{1,0:T(8,128)(2,1)S(1)} copy-done((bf16[256,1024]{1,0:T(8,128)(2,1)S(1)}, bf16[256,1024]{1,0:T(8,128)(2,1)}, u32[]{:S(2)}) %copy-start) | copy-done | bytes 524312
  1.1 0.0 copy-start.2
  1.1 0.0 copy-start.5
  1.1 3.1 %collective-permute-start.2 = (bf16[256,512]{1,0:T(8,128)(2,1)S(1)}, bf16[256,512]{1,0:T(8,128)(2,1)S(1)}, u32[]{:S(2)}, u32[]{:S(2)}) collective-permute-start(bf16[256,512]{1,0:T(8,128)(2,1)S(1)} %constant_dynamic-slice_fusion.after.w0), channel_id=1, source_target_pairs={{0,4},{1,5},{2,6},{3,7},{4,12},{5,13},{6,14},{7,15},{8,0},{9,1},{1... | collective-permute-start | bytes 786440 | tf_op jit(solution)/shard_map/ppermute | solution.py:358
  4.2 2.6 %shard_map.91 = (bf16[128,1024]{1,0:T(8,128)(2,1)}, bf16[128,1024]{1,0:T(8,128)(2,1)}, bf16[128,1024]{1,0:T(8,128)(2,1)}, bf16[256,256]{1,0:T(8,128)(2,1)}, bf16...) custom-call(bf16[128,1024]{1,0:T(8,128)(2,1)} %refs_0_.1, bf16[128,1024]{1,0:T(8,128)(2,1)} %g0.2, ...), custom_call_target="tpu_custom_call" | custom-call | tf_op jit(solution)/shard_map/pallas_call | solution.py:106
  6.8 0.0 copy-start.1
  6.8 2.6 %collective-permute-start.1 = (bf16[256,256]{1,0:T(8,128)(2,1)}, bf16[256,256]{1,0:T(8,128)(2,1)S(1)}, u32[]{:S(2)}, u32[]{:S(2)}) collective-permute-start(bf16[256,256]{1,0:T(8,128)(2,1)} %get-tuple-element.41.refs_0_), channel_id=1, source_target_pairs={{0,4},{1,5},{2,6},{3,7},{4,12},{5,13},{6,14},{7,15},{8,0},{9,1},{1... | collective-permute-start | bytes 393224 | tf_op jit(solution)/shard_map/ppermute | solution.py:358
  9.4 1.5 %collective-permute-start = (bf16[128,1024]{1,0:T(8,128)(2,1)}, bf16[128,1024]{1,0:T(8,128)(2,1)S(1)}, u32[]{:S(2)}, u32[]{:S(2)}) collective-permute-start(bf16[128,1024]{1,0:T(8,128)(2,1)} %get-tuple-element.40), channel_id=1, source_target_pairs={{0,2},{1,3},{2,0},{3,1},{4,6},{5,7},{6,4},{7,5},{8,10},{9,11},{10,... | collective-permute-start | bytes 786440 | tf_op jit(solution)/shard_map/ppermute | solution.py:358
  10.9 1.5 %collective-permute-start.4 = (bf16[128,1024]{1,0:T(8,128)(2,1)}, bf16[128,1024]{1,0:T(8,128)(2,1)S(1)}, u32[]{:S(2)}, u32[]{:S(2)}) collective-permute-start(bf16[128,1024]{1,0:T(8,128)(2,1)} %get-tuple-element.44), channel_id=1, source_target_pairs={{0,16},{1,17},{2,18},{3,19},{4,20},{5,21},{6,22},{7,23},{8,24},{9,... | collective-permute-start | bytes 786440 | tf_op jit(solution)/shard_map/ppermute | solution.py:358
  12.4 0.5 collective-permute-start.5
  12.9 1.4 %collective-permute-done.1.refs_2_ = bf16[256,256]{1,0:T(8,128)(2,1)S(1)} collective-permute-done((bf16[256,256]{1,0:T(8,128)(2,1)}, bf16[256,256]{1,0:T(8,128)(2,1)S(1)}, u32[]{:S(2)}, u32[]{:S(2)}) %collective-permute-start.1) | collective-permute-done | bytes 131104 | tf_op jit(solution)/shard_map/ppermute | solution.py:358
  14.3 0.9 %collective-permute-start.3 = (bf16[256,256]{1,0:T(8,128)(2,1)S(1)}, bf16[256,256]{1,0:T(8,128)(2,1)S(1)}, u32[]{:S(2)}, u32[]{:S(2)}) collective-permute-start(bf16[256,256]{1,0:T(8,128)(2,1)S(1)} %collective-permute-done.1.refs_2_), channel_id=1, source_target_pairs={{0,4},{1,5},{2,6},{3,7},{4,12},{5,13},{6,14},{7,15},{8,0},{9,1},{1... | collective-permute-start | bytes 393224 | tf_op jit(solution)/shard_map/ppermute | solution.py:358
  15.2 3.3 %collective-permute-start.7 = (bf16[256,512]{1,0:T(8,128)(2,1)S(1)}, bf16[256,512]{1,0:T(8,128)(2,1)S(1)}, u32[]{:S(2)}, u32[]{:S(2)}) collective-permute-start(bf16[256,512]{1,0:T(8,128)(2,1)S(1)} %collective-permute-done.2.w1), channel_id=1, source_target_pairs={{0,4},{1,5},{2,6},{3,7},{4,12},{5,13},{6,14},{7,15},{8,0},{9,1},{1... | collective-permute-start | bytes 786440 | tf_op jit(solution)/shard_map/ppermute | solution.py:358
  18.5 0.4 collective-permute-done.refs_1_.g1
  18.9 2.8 %collective-permute-done.3.refs_4_ = bf16[256,256]{1,0:T(8,128)(2,1)S(1)} collective-permute-done((bf16[256,256]{1,0:T(8,128)(2,1)S(1)}, bf16[256,256]{1,0:T(8,128)(2,1)S(1)}, u32[]{:S(2)}, u32[]{:S(2)}) %collective-permute-start.3) | collective-permute-done | bytes 131104 | tf_op jit(solution)/shard_map/ppermute | solution.py:358
  21.6 2.3 %collective-permute-done.4.refs_2_.g2 = bf16[128,1024]{1,0:T(8,128)(2,1)S(1)} collective-permute-done((bf16[128,1024]{1,0:T(8,128)(2,1)}, bf16[128,1024]{1,0:T(8,128)(2,1)S(1)}, u32[]{:S(2)}, u32[]{:S(2)}) %collective-permute-start.4) | collective-permute-done | bytes 262176 | tf_op jit(solution)/shard_map/ppermute | solution.py:358
  24.0 0.1 collective-permute-start.10
  24.1 1.3 %collective-permute-start.6 = (bf16[256,256]{1,0:T(8,128)(2,1)S(1)}, bf16[256,256]{1,0:T(8,128)(2,1)S(1)}, u32[]{:S(2)}, u32[]{:S(2)}) collective-permute-start(bf16[256,256]{1,0:T(8,128)(2,1)S(1)} %copy-done.12), channel_id=1, source_target_pairs={{0,2},{1,3},{2,0},{3,1},{4,6},{5,7},{6,4},{7,5},{8,10},{9,11},{10,... | collective-permute-start | bytes 393224 | tf_op jit(solution)/shard_map/ppermute | solution.py:358
  25.4 0.8 collective-permute-start.9
  26.2 0.0 collective-permute-done.7.w2
  26.2 0.9 collective-permute-start.11
  27.1 3.4 %collective-permute-done.6.refs_1_ = bf16[256,256]{1,0:T(8,128)(2,1)S(1)} collective-permute-done((bf16[256,256]{1,0:T(8,128)(2,1)S(1)}, bf16[256,256]{1,0:T(8,128)(2,1)S(1)}, u32[]{:S(2)}, u32[]{:S(2)}) %collective-permute-start.6) | collective-permute-done | bytes 131104 | tf_op jit(solution)/shard_map/ppermute | solution.py:358
  30.4 0.9 collective-permute-start.8
  31.4 4.3 %collective-permute-done.9.near = bf16[2,2,128,256]{3,2,1,0:T(8,128)(2,1)S(1)} collective-permute-done((bf16[2,2,128,256]{3,2,1,0:T(8,128)(2,1)S(1)}, bf16[2,2,128,256]{3,2,1,0:T(8,128)(2,1)S(1)}, u32[]{:S(2)}, u32[]{:S(2)}) %collective-permute-start.9) | collective-permute-done | bytes 262176 | tf_op jit(solution)/shard_map/ppermute | solution.py:358
  35.6 0.3 shard_map.93
  35.9 2.1 %collective-permute-done.8.refs_3_ = bf16[256,256]{1,0:T(8,128)(2,1)S(1)} collective-permute-done((bf16[256,256]{1,0:T(8,128)(2,1)S(1)}, bf16[256,256]{1,0:T(8,128)(2,1)S(1)}, u32[]{:S(2)}, u32[]{:S(2)}) %collective-permute-start.8) | collective-permute-done | bytes 131104 | tf_op jit(solution)/shard_map/ppermute | solution.py:358
  38.0 0.0 collective-permute-done.11.w3
  38.0 0.0 collective-permute-done.10.other
  38.0 1.3 %shard_map.94 = (f32[512,256]{1,0:T(8,128)S(1)}, bf16[512,256]{1,0:T(8,128)(2,1)S(1)}) custom-call(bf16[512,512]{1,0:T(8,128)(2,1)S(1)} %shard_map.92.mine, bf16[512,512]{1,0:T(8,128)(2,1)S(1)} %collective-permute-done.10.other, bf16[256,512]{1,0:T(8,128)(2,1)S(1)} %copy-done.3, bf16[256,512]{1,0:T(8,128)(2,1)S(1)} %collective-permute-done.2.w1, ...), custom_call_target="tpu_custom_call" | custom-call | flops 536870912 | bytes 2097152 | tf_op jit(solution)/shard_map/pallas_call | solution.py:37
  39.3 1.3 %collective-permute-start.12 = (bf16[512,256]{1,0:T(8,128)(2,1)S(1)}, bf16[512,256]{1,0:T(8,128)(2,1)S(1)}, u32[]{:S(2)}, u32[]{:S(2)}) collective-permute-start(bf16[512,256]{1,0:T(8,128)(2,1)S(1)} %get-tuple-element.53), channel_id=1, source_target_pairs={{0,2},{1,3},{2,0},{3,1},{4,6},{5,7},{6,4},{7,5},{8,10},{9,11},{10,... | collective-permute-start | bytes 786440 | tf_op jit(solution)/shard_map/ppermute | solution.py:358
  40.6 0.0 collective-permute-start.18
  40.6 2.0 %collective-permute-start.23 = (bf16[256,256]{1,0:T(8,128)(2,1)S(1)}, bf16[256,256]{1,0:T(8,128)(2,1)S(1)}, u32[]{:S(2)}, u32[]{:S(2)}) collective-permute-start(bf16[256,256]{1,0:T(8,128)(2,1)S(1)} %collective-permute-done.8.refs_3_), channel_id=1, source_target_pairs={{0,4},{1,5},{2,6},{3,7},{4,12},{5,13},{6,14},{7,15},{8,0},{9,1},{1... | collective-permute-start | bytes 393224 | tf_op jit(solution)/shard_map/ppermute | solution.py:358
  42.6 0.9 collective-permute-start.16
  43.5 1.5 %collective-permute-start.17 = (bf16[2,2,128,128]{3,2,1,0:T(8,128)(2,1)S(1)}, bf16[2,2,128,128]{3,2,1,0:T(8,128)(2,1)S(1)}, u32[]{:S(2)}, u32[]{:S(2)}) collective-permute-start(bf16[2,2,128,128]{3,2,1,0:T(8,128)(2,1)S(1)} %get-tuple-element.59), channel_id=1, source_target_pairs={{0,12},{1,13},{2,14},{3,15},{4,8},{5,9},{6,10},{7,11},{8,4},{9,5},... | collective-permute-start | bytes 393224 | tf_op jit(solution)/shard_map/ppermute | solution.py:358
  45.0 1.6 %collective-permute-done.12.taken = bf16[512,256]{1,0:T(8,128)(2,1)S(1)} collective-permute-done((bf16[512,256]{1,0:T(8,128)(2,1)S(1)}, bf16[512,256]{1,0:T(8,128)(2,1)S(1)}, u32[]{:S(2)}, u32[]{:S(2)}) %collective-permute-start.12) | collective-permute-done | bytes 262176 | tf_op jit(solution)/shard_map/ppermute | solution.py:358
  46.6 0.3 shard_map.95
  47.0 0.1 collective-permute-start.13
  47.0 0.4 collective-permute-done.18.refs_7_
  47.4 1.3 %collective-permute-start.14 = (bf16[256,128]{1,0:T(8,128)(2,1)S(1)}, bf16[256,128]{1,0:T(8,128)(2,1)S(1)}, u32[]{:S(2)}, u32[]{:S(2)}) collective-permute-start(bf16[256,128]{1,0:T(8,128)(2,1)S(1)} %get-tuple-element.56), channel_id=1, source_target_pairs={{0,12},{1,13},{2,14},{3,15},{4,8},{5,9},{6,10},{7,11},{8,4},{9,5},... | collective-permute-start | bytes 196616 | tf_op jit(solution)/shard_map/ppermute | solution.py:358
  48.7 1.2 %collective-permute-done.23.refs_5_ = bf16[256,256]{1,0:T(8,128)(2,1)S(1)} collective-permute-done((bf16[256,256]{1,0:T(8,128)(2,1)S(1)}, bf16[256,256]{1,0:T(8,128)(2,1)S(1)}, u32[]{:S(2)}, u32[]{:S(2)}) %collective-permute-start.23) | collective-permute-done | bytes 131104 | tf_op jit(solution)/shard_map/ppermute | solution.py:358
  49.9 0.9 collective-permute-start.15
  50.8 10.4 %collective-permute-done.13.refs_1_ = bf16[256,128]{1,0:T(8,128)(2,1)S(1)} collective-permute-done((bf16[256,128]{1,0:T(8,128)(2,1)S(1)}, bf16[256,128]{1,0:T(8,128)(2,1)S(1)}, u32[]{:S(2)}, u32[]{:S(2)}) %collective-permute-start.13) | collective-permute-done | bytes 65568 | tf_op jit(solution)/shard_map/ppermute | solution.py:358
  61.2 1.3 %collective-permute-start.24 = (bf16[2,256,256]{2,1,0:T(8,128)(2,1)S(1)}, bf16[2,256,256]{2,1,0:T(8,128)(2,1)S(1)}, u32[]{:S(2)}, u32[]{:S(2)}) collective-permute-start(bf16[2,256,256]{2,1,0:T(8,128)(2,1)S(1)} %pad_maximum_fusion), channel_id=1, source_target_pairs={{0,4},{1,5},{2,6},{3,7},{4,12},{5,13},{6,14},{7,15},{8,0},{9,1},{1... | collective-permute-start | bytes 786440 | tf_op jit(solution)/shard_map/ppermute | solution.py:358
  62.5 0.0 collective-permute-done.16.refs_5_
  62.5 0.0 collective-permute-done.17.refs_6_
  62.5 1.8 %shard_map.96 = (bf16[256,128]{1,0:T(8,128)(2,1)S(1)}, bf16[256,128]{1,0:T(8,128)(2,1)S(1)}, bf16[256,128]{1,0:T(8,128)(2,1)S(1)}, bf16[256,128]{1,0:T(8,128)(2,1)S(1)}) custom-call(bf16[256,128]{1,0:T(8,128)(2,1)S(1)} %get-tuple-element.54.refs_0_, bf16[256,128]{1,0:T(8,128)(2,1)S(1)} %collective-permute-done.13.refs_1_, ...), custom_call_target="tpu_custom_call" | custom-call | flops 1073741824 | bytes 5242880 | tf_op jit(solution)/shard_map/pallas_call | solution.py:37
  64.4 1.1 %collective-permute-start.19 = (bf16[256,128]{1,0:T(8,128)(2,1)S(1)}, bf16[256,128]{1,0:T(8,128)(2,1)S(1)}, u32[]{:S(2)}, u32[]{:S(2)}) collective-permute-start(bf16[256,128]{1,0:T(8,128)(2,1)S(1)} %get-tuple-element.62), channel_id=1, source_target_pairs={{0,4},{1,5},{2,6},{3,7},{4,12},{5,13},{6,14},{7,15},{8,0},{9,1},{1... | collective-permute-start | bytes 196616 | tf_op jit(solution)/shard_map/ppermute | solution.py:358
  65.5 2.1 %collective-permute-start.20 = (bf16[256,128]{1,0:T(8,128)(2,1)S(1)}, bf16[256,128]{1,0:T(8,128)(2,1)S(1)}, u32[]{:S(2)}, u32[]{:S(2)}) collective-permute-start(bf16[256,128]{1,0:T(8,128)(2,1)S(1)} %get-tuple-element.63), channel_id=1, source_target_pairs={{0,12},{1,13},{2,14},{3,15},{4,8},{5,9},{6,10},{7,11},{8,4},{9,5},... | collective-permute-start | bytes 196616 | tf_op jit(solution)/shard_map/ppermute | solution.py:358
  67.5 0.7 collective-permute-start.21
  68.2 5.2 %collective-permute-done.19.e1 = bf16[256,128]{1,0:T(8,128)(2,1)S(1)} collective-permute-done((bf16[256,128]{1,0:T(8,128)(2,1)S(1)}, bf16[256,128]{1,0:T(8,128)(2,1)S(1)}, u32[]{:S(2)}, u32[]{:S(2)}) %collective-permute-start.19) | collective-permute-done | bytes 65568 | tf_op jit(solution)/shard_map/ppermute | solution.py:358
  73.4 0.2 shard_map.98
  73.6 0.1 collective-permute-start.25
  73.7 0.2 shard_map.97.gated
  73.9 0.5 collective-permute-start.22
  74.5 1.5 %collective-permute-done.22.other = bf16[512,256]{1,0:T(8,128)(2,1)S(1)} collective-permute-done((bf16[512,256]{1,0:T(8,128)(2,1)S(1)}, bf16[512,256]{1,0:T(8,128)(2,1)S(1)}, u32[]{:S(2)}, u32[]{:S(2)}) %collective-permute-start.22) | collective-permute-done | bytes 262176 | tf_op jit(solution)/shard_map/ppermute | solution.py:358
  76.0 0.8 shard_map.100
  76.8 1.9 %collective-permute-start.26 = (bf16[128,1024]{1,0:T(8,128)(2,1)S(1)}, bf16[128,1024]{1,0:T(8,128)(2,1)S(1)}, u32[]{:S(2)}, u32[]{:S(2)}) collective-permute-start(bf16[128,1024]{1,0:T(8,128)(2,1)S(1)} %get-tuple-element.72), channel_id=1, source_target_pairs={{0,18},{1,19},{2,16},{3,17},{4,22},{5,23},{6,20},{7,21},{8,26},{9,... | collective-permute-start | bytes 786440 | tf_op jit(solution)/shard_map/ppermute | solution.py:358
  78.6 0.5 collective-permute-start.27
  79.2 0.8 shard_map.99
  80.0 1.2 %collective-permute-start.28 = (bf16[128,1024]{1,0:T(8,128)(2,1)S(1)}, bf16[128,1024]{1,0:T(8,128)(2,1)S(1)}, u32[]{:S(2)}, u32[]{:S(2)}) collective-permute-start(bf16[128,1024]{1,0:T(8,128)(2,1)S(1)} %get-tuple-element.74), channel_id=1, source_target_pairs={{0,16},{1,17},{2,18},{3,19},{4,20},{5,21},{6,22},{7,23},{8,24},{9,... | collective-permute-start | bytes 786440 | tf_op jit(solution)/shard_map/ppermute | solution.py:358
  81.2 5.7 %collective-permute-done.26 = bf16[128,1024]{1,0:T(8,128)(2,1)S(1)} collective-permute-done((bf16[128,1024]{1,0:T(8,128)(2,1)S(1)}, bf16[128,1024]{1,0:T(8,128)(2,1)S(1)}, u32[]{:S(2)}, u32[]{:S(2)}) %collective-permute-start.26) | collective-permute-done | bytes 262176 | tf_op jit(solution)/shard_map/ppermute | solution.py:358
  87.0 4.2 %collective-permute-done.27 = bf16[128,1024]{1,0:T(8,128)(2,1)S(1)} collective-permute-done((bf16[128,1024]{1,0:T(8,128)(2,1)S(1)}, bf16[128,1024]{1,0:T(8,128)(2,1)S(1)}, u32[]{:S(2)}, u32[]{:S(2)}) %collective-permute-start.27) | collective-permute-done | bytes 262176 | tf_op jit(solution)/shard_map/ppermute | solution.py:358
  91.2 0.6 collective-permute-done.28
  91.7 0.8 add_convert_fusion
  (33 shorter events, 0.1 us)
Async XLA Ops:
  0.0 1.0 %copy-start = (bf16[256,1024]{1,0:T(8,128)(2,1)S(1)}, bf16[256,1024]{1,0:T(8,128)(2,1)}, u32[]{:S(2)}) copy-start(bf16[256,1024]{1,0:T(8,128)(2,1)} %param.12) | copy-start | bytes 1572868
  1.1 3.1 %copy-start.2 = (bf16[256,512]{1,0:T(8,128)(2,1)}, bf16[256,512]{1,0:T(8,128)(2,1)S(1)}, u32[]{:S(2)}) copy-start(bf16[256,512]{1,0:T(8,128)(2,1)S(1)} %constant_dynamic-slice_fusion.after.w0) | copy-start | bytes 786436
  1.1 22.9 %copy-start.5 = (bf16[128,1024]{1,0:T(8,128)(2,1)S(1)}, bf16[128,1024]{1,0:T(8,128)(2,1)}, u32[]{:S(2)}) copy-start(bf16[128,1024]{1,0:T(8,128)(2,1)} %refs_0_.1) | copy-start | bytes 786436
  1.1 13.2 %collective-permute-start.2 = (bf16[256,512]{1,0:T(8,128)(2,1)S(1)}, bf16[256,512]{1,0:T(8,128)(2,1)S(1)}, u32[]{:S(2)}, u32[]{:S(2)}) collective-permute-start(bf16[256,512]{1,0:T(8,128)(2,1)S(1)} %constant_dynamic-slice_fusion.after.w0), channel_id=1, source_target_pairs={{0,4},{1,5},{2,6},{3,7},{4,12},{5,13},{6,14},{7,15},{8,0},{9,1},{1... | collective-permute-start | bytes 786440 | tf_op jit(solution)/shard_map/ppermute | solution.py:358
  6.8 28.8 %copy-start.1 = (bf16[2,2,128,1024]{3,2,1,0:T(8,128)(2,1)S(1)}, bf16[2,2,128,1024]{3,2,1,0:T(8,128)(2,1)}, u32[]{:S(2)}) copy-start(bf16[2,2,128,1024]{3,2,1,0:T(8,128)(2,1)} %filt.3) | copy-start | bytes 3145732
  6.8 7.5 %collective-permute-start.1 = (bf16[256,256]{1,0:T(8,128)(2,1)}, bf16[256,256]{1,0:T(8,128)(2,1)S(1)}, u32[]{:S(2)}, u32[]{:S(2)}) collective-permute-start(bf16[256,256]{1,0:T(8,128)(2,1)} %get-tuple-element.41.refs_0_), channel_id=1, source_target_pairs={{0,4},{1,5},{2,6},{3,7},{4,12},{5,13},{6,14},{7,15},{8,0},{9,1},{1... | collective-permute-start | bytes 393224 | tf_op jit(solution)/shard_map/ppermute | solution.py:358
  9.4 9.5 %collective-permute-start = (bf16[128,1024]{1,0:T(8,128)(2,1)}, bf16[128,1024]{1,0:T(8,128)(2,1)S(1)}, u32[]{:S(2)}, u32[]{:S(2)}) collective-permute-start(bf16[128,1024]{1,0:T(8,128)(2,1)} %get-tuple-element.40), channel_id=1, source_target_pairs={{0,2},{1,3},{2,0},{3,1},{4,6},{5,7},{6,4},{7,5},{8,10},{9,11},{10,... | collective-permute-start | bytes 786440 | tf_op jit(solution)/shard_map/ppermute | solution.py:358
  10.9 13.0 %collective-permute-start.4 = (bf16[128,1024]{1,0:T(8,128)(2,1)}, bf16[128,1024]{1,0:T(8,128)(2,1)S(1)}, u32[]{:S(2)}, u32[]{:S(2)}) collective-permute-start(bf16[128,1024]{1,0:T(8,128)(2,1)} %get-tuple-element.44), channel_id=1, source_target_pairs={{0,16},{1,17},{2,18},{3,19},{4,20},{5,21},{6,22},{7,23},{8,24},{9,... | collective-permute-start | bytes 786440 | tf_op jit(solution)/shard_map/ppermute | solution.py:358
  12.4 11.6 %copy-start.12 = (bf16[256,256]{1,0:T(8,128)(2,1)S(1)}, bf16[256,256]{1,0:T(8,128)(2,1)}, u32[]{:S(2)}) copy-start(bf16[256,256]{1,0:T(8,128)(2,1)} %get-tuple-element.47) | copy-start | bytes 393220
  12.4 13.0 %copy-start.11 = (bf16[2,2,128,256]{3,2,1,0:T(8,128)(2,1)S(1)}, bf16[2,2,128,256]{3,2,1,0:T(8,128)(2,1)}, u32[]{:S(2)}) copy-start(bf16[2,2,128,256]{3,2,1,0:T(8,128)(2,1)} %get-tuple-element.49) | copy-start | bytes 786436
  12.4 11.5 %collective-permute-start.5 = (bf16[128,1024]{1,0:T(8,128)(2,1)}, bf16[128,1024]{1,0:T(8,128)(2,1)S(1)}, u32[]{:S(2)}, u32[]{:S(2)}) collective-permute-start(bf16[128,1024]{1,0:T(8,128)(2,1)} %get-tuple-element.45), channel_id=1, source_target_pairs={{0,18},{1,19},{2,16},{3,17},{4,22},{5,23},{6,20},{7,21},{8,26},{9,... | collective-permute-start | bytes 786440 | tf_op jit(solution)/shard_map/ppermute | solution.py:358
  14.3 7.3 %collective-permute-start.3 = (bf16[256,256]{1,0:T(8,128)(2,1)S(1)}, bf16[256,256]{1,0:T(8,128)(2,1)S(1)}, u32[]{:S(2)}, u32[]{:S(2)}) collective-permute-start(bf16[256,256]{1,0:T(8,128)(2,1)S(1)} %collective-permute-done.1.refs_2_), channel_id=1, source_target_pairs={{0,4},{1,5},{2,6},{3,7},{4,12},{5,13},{6,14},{7,15},{8,0},{9,1},{1... | collective-permute-start | bytes 393224 | tf_op jit(solution)/shard_map/ppermute | solution.py:358
  15.2 10.9 %collective-permute-start.7 = (bf16[256,512]{1,0:T(8,128)(2,1)S(1)}, bf16[256,512]{1,0:T(8,128)(2,1)S(1)}, u32[]{:S(2)}, u32[]{:S(2)}) collective-permute-start(bf16[256,512]{1,0:T(8,128)(2,1)S(1)} %collective-permute-done.2.w1), channel_id=1, source_target_pairs={{0,4},{1,5},{2,6},{3,7},{4,12},{5,13},{6,14},{7,15},{8,0},{9,1},{1... | collective-permute-start | bytes 786440 | tf_op jit(solution)/shard_map/ppermute | solution.py:358
  24.0 14.0 %collective-permute-start.10 = (bf16[512,512]{1,0:T(8,128)(2,1)S(1)}, bf16[512,512]{1,0:T(8,128)(2,1)S(1)}, u32[]{:S(2)}, u32[]{:S(2)}) collective-permute-start(bf16[512,512]{1,0:T(8,128)(2,1)S(1)} %shard_map.92.mine), channel_id=1, source_target_pairs={{0,1},{1,0},{2,3},{3,2},{4,5},{5,4},{6,7},{7,6},{8,9},{9,8},{10,11... | collective-permute-start | bytes 1572872 | tf_op jit(solution)/shard_map/ppermute | solution.py:358
  24.1 6.4 %collective-permute-start.6 = (bf16[256,256]{1,0:T(8,128)(2,1)S(1)}, bf16[256,256]{1,0:T(8,128)(2,1)S(1)}, u32[]{:S(2)}, u32[]{:S(2)}) collective-permute-start(bf16[256,256]{1,0:T(8,128)(2,1)S(1)} %copy-done.12), channel_id=1, source_target_pairs={{0,2},{1,3},{2,0},{3,1},{4,6},{5,7},{6,4},{7,5},{8,10},{9,11},{10,... | collective-permute-start | bytes 393224 | tf_op jit(solution)/shard_map/ppermute | solution.py:358
  25.4 12.6 %copy-start.3 = (bf16[256,512]{1,0:T(8,128)(2,1)S(1)}, bf16[256,512]{1,0:T(8,128)(2,1)}, u32[]{:S(2)}) copy-start(bf16[256,512]{1,0:T(8,128)(2,1)} %copy-done.2) | copy-start | bytes 786436
  25.4 10.2 %collective-permute-start.9 = (bf16[2,2,128,256]{3,2,1,0:T(8,128)(2,1)S(1)}, bf16[2,2,128,256]{3,2,1,0:T(8,128)(2,1)S(1)}, u32[]{:S(2)}, u32[]{:S(2)}) collective-permute-start(bf16[2,2,128,256]{3,2,1,0:T(8,128)(2,1)S(1)} %copy-done.11), channel_id=1, source_target_pairs={{0,2},{1,3},{2,0},{3,1},{4,6},{5,7},{6,4},{7,5},{8,10},{9,11},{10,... | collective-permute-start | bytes 786440 | tf_op jit(solution)/shard_map/ppermute | solution.py:358
  26.2 11.8 %collective-permute-start.11 = (bf16[256,512]{1,0:T(8,128)(2,1)S(1)}, bf16[256,512]{1,0:T(8,128)(2,1)S(1)}, u32[]{:S(2)}, u32[]{:S(2)}) collective-permute-start(bf16[256,512]{1,0:T(8,128)(2,1)S(1)} %collective-permute-done.7.w2), channel_id=1, source_target_pairs={{0,4},{1,5},{2,6},{3,7},{4,12},{5,13},{6,14},{7,15},{8,0},{9,1},{1... | collective-permute-start | bytes 786440 | tf_op jit(solution)/shard_map/ppermute | solution.py:358
  30.4 7.5 %collective-permute-start.8 = (bf16[256,256]{1,0:T(8,128)(2,1)S(1)}, bf16[256,256]{1,0:T(8,128)(2,1)S(1)}, u32[]{:S(2)}, u32[]{:S(2)}) collective-permute-start(bf16[256,256]{1,0:T(8,128)(2,1)S(1)} %collective-permute-done.6.refs_1_), channel_id=1, source_target_pairs={{0,4},{1,5},{2,6},{3,7},{4,12},{5,13},{6,14},{7,15},{8,0},{9,1},{1... | collective-permute-start | bytes 393224 | tf_op jit(solution)/shard_map/ppermute | solution.py:358
  38.0 8.6 %copy-start.4 = (bf16[128,1024]{1,0:T(8,128)(2,1)S(1)}, bf16[128,1024]{1,0:T(8,128)(2,1)}, u32[]{:S(2)}) copy-start(bf16[128,1024]{1,0:T(8,128)(2,1)} %g0.2) | copy-start | bytes 786436
  39.3 7.3 %collective-permute-start.12 = (bf16[512,256]{1,0:T(8,128)(2,1)S(1)}, bf16[512,256]{1,0:T(8,128)(2,1)S(1)}, u32[]{:S(2)}, u32[]{:S(2)}) collective-permute-start(bf16[512,256]{1,0:T(8,128)(2,1)S(1)} %get-tuple-element.53), channel_id=1, source_target_pairs={{0,2},{1,3},{2,0},{3,1},{4,6},{5,7},{6,4},{7,5},{8,10},{9,11},{10,... | collective-permute-start | bytes 786440 | tf_op jit(solution)/shard_map/ppermute | solution.py:358
  40.6 6.0 %copy-start.8 = (f32[1024]{0:T(1024)S(1)}, f32[1024]{0:T(1024)}, u32[]{:S(2)}) copy-start(f32[1024]{0:T(1024)} %param.13) | copy-start | bytes 12292
  40.6 6.8 %collective-permute-start.18 = (bf16[2,2,128,128]{3,2,1,0:T(8,128)(2,1)S(1)}, bf16[2,2,128,128]{3,2,1,0:T(8,128)(2,1)S(1)}, u32[]{:S(2)}, u32[]{:S(2)}) collective-permute-start(bf16[2,2,128,128]{3,2,1,0:T(8,128)(2,1)S(1)} %get-tuple-element.60), channel_id=1, source_target_pairs={{0,8},{1,9},{2,10},{3,11},{4,0},{5,1},{6,2},{7,3},{8,12},{9,13},{1... | collective-permute-start | bytes 393224 | tf_op jit(solution)/shard_map/ppermute | solution.py:358
  40.6 9.3 %collective-permute-start.23 = (bf16[256,256]{1,0:T(8,128)(2,1)S(1)}, bf16[256,256]{1,0:T(8,128)(2,1)S(1)}, u32[]{:S(2)}, u32[]{:S(2)}) collective-permute-start(bf16[256,256]{1,0:T(8,128)(2,1)S(1)} %collective-permute-done.8.refs_3_), channel_id=1, source_target_pairs={{0,4},{1,5},{2,6},{3,7},{4,12},{5,13},{6,14},{7,15},{8,0},{9,1},{1... | collective-permute-start | bytes 393224 | tf_op jit(solution)/shard_map/ppermute | solution.py:358
  42.6 19.9 %collective-permute-start.16 = (bf16[2,2,128,128]{3,2,1,0:T(8,128)(2,1)S(1)}, bf16[2,2,128,128]{3,2,1,0:T(8,128)(2,1)S(1)}, u32[]{:S(2)}, u32[]{:S(2)}) collective-permute-start(bf16[2,2,128,128]{3,2,1,0:T(8,128)(2,1)S(1)} %get-tuple-element.58), channel_id=1, source_target_pairs={{0,4},{1,5},{2,6},{3,7},{4,12},{5,13},{6,14},{7,15},{8,0},{9,1},{1... | collective-permute-start | bytes 393224 | tf_op jit(solution)/shard_map/ppermute | solution.py:358
  43.5 19.0 %collective-permute-start.17 = (bf16[2,2,128,128]{3,2,1,0:T(8,128)(2,1)S(1)}, bf16[2,2,128,128]{3,2,1,0:T(8,128)(2,1)S(1)}, u32[]{:S(2)}, u32[]{:S(2)}) collective-permute-start(bf16[2,2,128,128]{3,2,1,0:T(8,128)(2,1)S(1)} %get-tuple-element.59), channel_id=1, source_target_pairs={{0,12},{1,13},{2,14},{3,15},{4,8},{5,9},{6,10},{7,11},{8,4},{9,5},... | collective-permute-start | bytes 393224 | tf_op jit(solution)/shard_map/ppermute | solution.py:358
  46.6 15.9 %copy-start.9 = (bf16[16,256,128]{2,1,0:T(8,128)(2,1)S(1)}, bf16[16,256,128]{2,1,0:T(8,128)(2,1)}, u32[]{:S(2)}) copy-start(bf16[16,256,128]{2,1,0:T(8,128)(2,1)} %constant.17.clone.refs_9_) | copy-start | bytes 3145732
  46.6 15.9 %copy-start.10 = (bf16[16,256,128]{2,1,0:T(8,128)(2,1)S(1)}, bf16[16,256,128]{2,1,0:T(8,128)(2,1)}, u32[]{:S(2)}) copy-start(bf16[16,256,128]{2,1,0:T(8,128)(2,1)} %constant.16.clone.refs_8_) | copy-start | bytes 3145732
  47.0 14.3 %collective-permute-start.13 = (bf16[256,128]{1,0:T(8,128)(2,1)S(1)}, bf16[256,128]{1,0:T(8,128)(2,1)S(1)}, u32[]{:S(2)}, u32[]{:S(2)}) collective-permute-start(bf16[256,128]{1,0:T(8,128)(2,1)S(1)} %get-tuple-element.55), channel_id=1, source_target_pairs={{0,4},{1,5},{2,6},{3,7},{4,12},{5,13},{6,14},{7,15},{8,0},{9,1},{1... | collective-permute-start | bytes 196616 | tf_op jit(solution)/shard_map/ppermute | solution.py:358
  47.4 13.8 %collective-permute-start.14 = (bf16[256,128]{1,0:T(8,128)(2,1)S(1)}, bf16[256,128]{1,0:T(8,128)(2,1)S(1)}, u32[]{:S(2)}, u32[]{:S(2)}) collective-permute-start(bf16[256,128]{1,0:T(8,128)(2,1)S(1)} %get-tuple-element.56), channel_id=1, source_target_pairs={{0,12},{1,13},{2,14},{3,15},{4,8},{5,9},{6,10},{7,11},{8,4},{9,5},... | collective-permute-start | bytes 196616 | tf_op jit(solution)/shard_map/ppermute | solution.py:358
  49.9 11.3 %collective-permute-start.15 = (bf16[256,128]{1,0:T(8,128)(2,1)S(1)}, bf16[256,128]{1,0:T(8,128)(2,1)S(1)}, u32[]{:S(2)}, u32[]{:S(2)}) collective-permute-start(bf16[256,128]{1,0:T(8,128)(2,1)S(1)} %get-tuple-element.57), channel_id=1, source_target_pairs={{0,8},{1,9},{2,10},{3,11},{4,0},{5,1},{6,2},{7,3},{8,12},{9,13},{1... | collective-permute-start | bytes 196616 | tf_op jit(solution)/shard_map/ppermute | solution.py:358
  61.2 12.2 %collective-permute-start.24 = (bf16[2,256,256]{2,1,0:T(8,128)(2,1)S(1)}, bf16[2,256,256]{2,1,0:T(8,128)(2,1)S(1)}, u32[]{:S(2)}, u32[]{:S(2)}) collective-permute-start(bf16[2,256,256]{2,1,0:T(8,128)(2,1)S(1)} %pad_maximum_fusion), channel_id=1, source_target_pairs={{0,4},{1,5},{2,6},{3,7},{4,12},{5,13},{6,14},{7,15},{8,0},{9,1},{1... | collective-permute-start | bytes 786440 | tf_op jit(solution)/shard_map/ppermute | solution.py:358
  62.5 10.9 %copy-start.7 = (bf16[256,256]{1,0:T(8,128)(2,1)S(1)}, bf16[256,256]{1,0:T(8,128)(2,1)}, u32[]{:S(2)}) copy-start(bf16[256,256]{1,0:T(8,128)(2,1)} %get-tuple-element.41.refs_0_) | copy-start | bytes 393220
  64.4 9.1 %collective-permute-start.19 = (bf16[256,128]{1,0:T(8,128)(2,1)S(1)}, bf16[256,128]{1,0:T(8,128)(2,1)S(1)}, u32[]{:S(2)}, u32[]{:S(2)}) collective-permute-start(bf16[256,128]{1,0:T(8,128)(2,1)S(1)} %get-tuple-element.62), channel_id=1, source_target_pairs={{0,4},{1,5},{2,6},{3,7},{4,12},{5,13},{6,14},{7,15},{8,0},{9,1},{1... | collective-permute-start | bytes 196616 | tf_op jit(solution)/shard_map/ppermute | solution.py:358
  65.5 8.0 %collective-permute-start.20 = (bf16[256,128]{1,0:T(8,128)(2,1)S(1)}, bf16[256,128]{1,0:T(8,128)(2,1)S(1)}, u32[]{:S(2)}, u32[]{:S(2)}) collective-permute-start(bf16[256,128]{1,0:T(8,128)(2,1)S(1)} %get-tuple-element.63), channel_id=1, source_target_pairs={{0,12},{1,13},{2,14},{3,15},{4,8},{5,9},{6,10},{7,11},{8,4},{9,5},... | collective-permute-start | bytes 196616 | tf_op jit(solution)/shard_map/ppermute | solution.py:358
  67.5 6.2 %copy-start.6 = (bf16[128,1024]{1,0:T(8,128)(2,1)S(1)}, bf16[128,1024]{1,0:T(8,128)(2,1)}, u32[]{:S(2)}) copy-start(bf16[128,1024]{1,0:T(8,128)(2,1)} %g0.3) | copy-start | bytes 786436
  67.5 5.9 %collective-permute-start.21 = (bf16[256,128]{1,0:T(8,128)(2,1)S(1)}, bf16[256,128]{1,0:T(8,128)(2,1)S(1)}, u32[]{:S(2)}, u32[]{:S(2)}) collective-permute-start(bf16[256,128]{1,0:T(8,128)(2,1)S(1)} %get-tuple-element.64), channel_id=1, source_target_pairs={{0,8},{1,9},{2,10},{3,11},{4,0},{5,1},{6,2},{7,3},{8,12},{9,13},{1... | collective-permute-start | bytes 196616 | tf_op jit(solution)/shard_map/ppermute | solution.py:358
  73.6 2.4 %collective-permute-start.25 = (bf16[4,256,256]{2,1,0:T(8,128)(2,1)S(1)}, bf16[4,256,256]{2,1,0:T(8,128)(2,1)S(1)}, u32[]{:S(2)}, u32[]{:S(2)}) collective-permute-start(bf16[4,256,256]{2,1,0:T(8,128)(2,1)S(1)} %get-tuple-element.70), channel_id=1, source_target_pairs={{0,1},{1,0},{2,3},{3,2},{4,5},{5,4},{6,7},{7,6},{8,9},{9,8},{10,11... | collective-permute-start | bytes 1572872 | tf_op jit(solution)/shard_map/ppermute | solution.py:358
  73.9 2.0 %collective-permute-start.22 = (bf16[512,256]{1,0:T(8,128)(2,1)S(1)}, bf16[512,256]{1,0:T(8,128)(2,1)S(1)}, u32[]{:S(2)}, u32[]{:S(2)}) collective-permute-start(bf16[512,256]{1,0:T(8,128)(2,1)S(1)} %shard_map.97.gated), channel_id=1, source_target_pairs={{0,1},{1,0},{2,3},{3,2},{4,5},{5,4},{6,7},{7,6},{8,9},{9,8},{10,11... | collective-permute-start | bytes 786440 | tf_op jit(solution)/shard_map/ppermute | solution.py:358
  76.8 10.2 %collective-permute-start.26 = (bf16[128,1024]{1,0:T(8,128)(2,1)S(1)}, bf16[128,1024]{1,0:T(8,128)(2,1)S(1)}, u32[]{:S(2)}, u32[]{:S(2)}) collective-permute-start(bf16[128,1024]{1,0:T(8,128)(2,1)S(1)} %get-tuple-element.72), channel_id=1, source_target_pairs={{0,18},{1,19},{2,16},{3,17},{4,22},{5,23},{6,20},{7,21},{8,26},{9,... | collective-permute-start | bytes 786440 | tf_op jit(solution)/shard_map/ppermute | solution.py:358
  78.6 12.5 %collective-permute-start.27 = (bf16[128,1024]{1,0:T(8,128)(2,1)S(1)}, bf16[128,1024]{1,0:T(8,128)(2,1)S(1)}, u32[]{:S(2)}, u32[]{:S(2)}) collective-permute-start(bf16[128,1024]{1,0:T(8,128)(2,1)S(1)} %get-tuple-element.73), channel_id=1, source_target_pairs={{0,2},{1,3},{2,0},{3,1},{4,6},{5,7},{6,4},{7,5},{8,10},{9,11},{10,... | collective-permute-start | bytes 786440 | tf_op jit(solution)/shard_map/ppermute | solution.py:358
  80.0 11.7 %collective-permute-start.28 = (bf16[128,1024]{1,0:T(8,128)(2,1)S(1)}, bf16[128,1024]{1,0:T(8,128)(2,1)S(1)}, u32[]{:S(2)}, u32[]{:S(2)}) collective-permute-start(bf16[128,1024]{1,0:T(8,128)(2,1)S(1)} %get-tuple-element.74), channel_id=1, source_target_pairs={{0,16},{1,17},{2,18},{3,19},{4,20},{5,21},{6,22},{7,23},{8,24},{9,... | collective-permute-start | bytes 786440 | tf_op jit(solution)/shard_map/ppermute | solution.py:358

commit v19 on v18

--- a/solution.py
+++ b/solution.py
@@ -273,8 +273,8 @@
         one, two = back(k), back(16 - k)
         sums[k, pl.ds(0, 128)] = one[0] + two[0]
         sums[k, pl.ds(128, 128)] = one[1] - two[1]
-    for i in range(16):
-        rows, below = pl.ds(8 * i, 8), pl.ds(128 + 8 * i, 8)
+    for i in range(8):
+        rows, below = pl.ds(16 * i, 16), pl.ds(128 + 16 * i, 16)
         scale = 1.0 / 2048
         re = [sums[k, rows, :] * scale for k in range(9)]
         im = [None] + [sums[k, below, :] * scale for k in range(1, 8)] + [None]

time: 92.8 us -> 92.8 us (level)
  no operation moved by 1% of the time
where the time goes in v19:
time: 92.8 us; the launch traced here: 92.6 us
  waiting for transfers between devices  47.3 us (51%)
  starting transfers between devices  34.7 us (37%)
  Pallas kernels  8.37 us (9%)
  local copies, waits for them, and re-layouts  1.11 us (1%)
    ppermute x29, waiting for transfers between devices, permute(): return lax.ppermute(values, AXES, pairs)  47.3 us
    ppermute x29, starting transfers between devices, permute(): return lax.ppermute(values, AXES, pairs)  34.7 us
    pallas_call x9, Pallas kernels, call(): pl.pallas_call(kernel, out_shape=out_shape, in_specs=specs, out_specs=jax...  5.79 us
    pallas_call x1, Pallas kernels, call(): pl.pallas_call(kernel, out_shape=out_shape, in_specs=[pl.BlockSpec(memory...  2.58 us
  transfers between devices with their start and end apart: 29, of which 16 were waited for; matrix products, arithmetic and copies ran while one was open for 0% of the time, Pallas kernels for 7%

profile of v19, /device:TPU:0, one launch (start us, length us, event | category | flops | bytes accessed | tf_op | source)
XLA Modules:
  0.0 92.6 jit_solution(6327944904576846154)
XLA Ops:
  0.0 1.0 %copy-done = bf16[256,1024]{1,0:T(8,128)(2,1)S(1)} copy-done((bf16[256,1024]{1,0:T(8,128)(2,1)S(1)}, bf16[256,1024]{1,0:T(8,128)(2,1)}, u32[]{:S(2)}) %copy-start) | copy-done | bytes 524312
  1.1 0.0 copy-start.2
  1.1 0.0 copy-start.5
  1.1 3.1 %collective-permute-start.2 = (bf16[256,512]{1,0:T(8,128)(2,1)S(1)}, bf16[256,512]{1,0:T(8,128)(2,1)S(1)}, u32[]{:S(2)}, u32[]{:S(2)}) collective-permute-start(bf16[256,512]{1,0:T(8,128)(2,1)S(1)} %constant_dynamic-slice_fusion.after.w0), channel_id=1, source_target_pairs={{0,4},{1,5},{2,6},{3,7},{4,12},{5,13},{6,14},{7,15},{8,0},{9,1},{1... | collective-permute-start | bytes 786440 | tf_op jit(solution)/shard_map/ppermute | solution.py:358
  4.2 2.6 %shard_map.91 = (bf16[128,1024]{1,0:T(8,128)(2,1)}, bf16[128,1024]{1,0:T(8,128)(2,1)}, bf16[128,1024]{1,0:T(8,128)(2,1)}, bf16[256,256]{1,0:T(8,128)(2,1)}, bf16...) custom-call(bf16[128,1024]{1,0:T(8,128)(2,1)} %refs_0_.1, bf16[128,1024]{1,0:T(8,128)(2,1)} %g0.2, ...), custom_call_target="tpu_custom_call" | custom-call | tf_op jit(solution)/shard_map/pallas_call | solution.py:106
  6.8 0.0 copy-start.1
  6.8 2.6 %collective-permute-start.1 = (bf16[256,256]{1,0:T(8,128)(2,1)}, bf16[256,256]{1,0:T(8,128)(2,1)S(1)}, u32[]{:S(2)}, u32[]{:S(2)}) collective-permute-start(bf16[256,256]{1,0:T(8,128)(2,1)} %get-tuple-element.41.refs_0_), channel_id=1, source_target_pairs={{0,4},{1,5},{2,6},{3,7},{4,12},{5,13},{6,14},{7,15},{8,0},{9,1},{1... | collective-permute-start | bytes 393224 | tf_op jit(solution)/shard_map/ppermute | solution.py:358
  9.4 1.5 %collective-permute-start = (bf16[128,1024]{1,0:T(8,128)(2,1)}, bf16[128,1024]{1,0:T(8,128)(2,1)S(1)}, u32[]{:S(2)}, u32[]{:S(2)}) collective-permute-start(bf16[128,1024]{1,0:T(8,128)(2,1)} %get-tuple-element.40), channel_id=1, source_target_pairs={{0,2},{1,3},{2,0},{3,1},{4,6},{5,7},{6,4},{7,5},{8,10},{9,11},{10,... | collective-permute-start | bytes 786440 | tf_op jit(solution)/shard_map/ppermute | solution.py:358
  10.9 1.5 %collective-permute-start.4 = (bf16[128,1024]{1,0:T(8,128)(2,1)}, bf16[128,1024]{1,0:T(8,128)(2,1)S(1)}, u32[]{:S(2)}, u32[]{:S(2)}) collective-permute-start(bf16[128,1024]{1,0:T(8,128)(2,1)} %get-tuple-element.44), channel_id=1, source_target_pairs={{0,16},{1,17},{2,18},{3,19},{4,20},{5,21},{6,22},{7,23},{8,24},{9,... | collective-permute-start | bytes 786440 | tf_op jit(solution)/shard_map/ppermute | solution.py:358
  12.4 0.5 collective-permute-start.5
  12.9 1.4 %collective-permute-done.1.refs_2_ = bf16[256,256]{1,0:T(8,128)(2,1)S(1)} collective-permute-done((bf16[256,256]{1,0:T(8,128)(2,1)}, bf16[256,256]{1,0:T(8,128)(2,1)S(1)}, u32[]{:S(2)}, u32[]{:S(2)}) %collective-permute-start.1) | collective-permute-done | bytes 131104 | tf_op jit(solution)/shard_map/ppermute | solution.py:358
  14.3 0.9 %collective-permute-start.3 = (bf16[256,256]{1,0:T(8,128)(2,1)S(1)}, bf16[256,256]{1,0:T(8,128)(2,1)S(1)}, u32[]{:S(2)}, u32[]{:S(2)}) collective-permute-start(bf16[256,256]{1,0:T(8,128)(2,1)S(1)} %collective-permute-done.1.refs_2_), channel_id=1, source_target_pairs={{0,4},{1,5},{2,6},{3,7},{4,12},{5,13},{6,14},{7,15},{8,0},{9,1},{1... | collective-permute-start | bytes 393224 | tf_op jit(solution)/shard_map/ppermute | solution.py:358
  15.2 3.3 %collective-permute-start.7 = (bf16[256,512]{1,0:T(8,128)(2,1)S(1)}, bf16[256,512]{1,0:T(8,128)(2,1)S(1)}, u32[]{:S(2)}, u32[]{:S(2)}) collective-permute-start(bf16[256,512]{1,0:T(8,128)(2,1)S(1)} %collective-permute-done.2.w1), channel_id=1, source_target_pairs={{0,4},{1,5},{2,6},{3,7},{4,12},{5,13},{6,14},{7,15},{8,0},{9,1},{1... | collective-permute-start | bytes 786440 | tf_op jit(solution)/shard_map/ppermute | solution.py:358
  18.5 0.4 collective-permute-done.refs_1_.g1
  18.9 2.8 %collective-permute-done.3.refs_4_ = bf16[256,256]{1,0:T(8,128)(2,1)S(1)} collective-permute-done((bf16[256,256]{1,0:T(8,128)(2,1)S(1)}, bf16[256,256]{1,0:T(8,128)(2,1)S(1)}, u32[]{:S(2)}, u32[]{:S(2)}) %collective-permute-start.3) | collective-permute-done | bytes 131104 | tf_op jit(solution)/shard_map/ppermute | solution.py:358
  21.6 2.3 %collective-permute-done.4.refs_2_.g2 = bf16[128,1024]{1,0:T(8,128)(2,1)S(1)} collective-permute-done((bf16[128,1024]{1,0:T(8,128)(2,1)}, bf16[128,1024]{1,0:T(8,128)(2,1)S(1)}, u32[]{:S(2)}, u32[]{:S(2)}) %collective-permute-start.4) | collective-permute-done | bytes 262176 | tf_op jit(solution)/shard_map/ppermute | solution.py:358
  24.0 0.1 collective-permute-start.10
  24.1 1.3 %collective-permute-start.6 = (bf16[256,256]{1,0:T(8,128)(2,1)S(1)}, bf16[256,256]{1,0:T(8,128)(2,1)S(1)}, u32[]{:S(2)}, u32[]{:S(2)}) collective-permute-start(bf16[256,256]{1,0:T(8,128)(2,1)S(1)} %copy-done.12), channel_id=1, source_target_pairs={{0,2},{1,3},{2,0},{3,1},{4,6},{5,7},{6,4},{7,5},{8,10},{9,11},{10,... | collective-permute-start | bytes 393224 | tf_op jit(solution)/shard_map/ppermute | solution.py:358
  25.4 0.8 collective-permute-start.9
  26.2 0.0 collective-permute-done.7.w2
  26.2 0.9 collective-permute-start.11
  27.1 3.4 %collective-permute-done.6.refs_1_ = bf16[256,256]{1,0:T(8,128)(2,1)S(1)} collective-permute-done((bf16[256,256]{1,0:T(8,128)(2,1)S(1)}, bf16[256,256]{1,0:T(8,128)(2,1)S(1)}, u32[]{:S(2)}, u32[]{:S(2)}) %collective-permute-start.6) | collective-permute-done | bytes 131104 | tf_op jit(solution)/shard_map/ppermute | solution.py:358
  30.4 0.9 collective-permute-start.8
  31.4 4.3 %collective-permute-done.9.near = bf16[2,2,128,256]{3,2,1,0:T(8,128)(2,1)S(1)} collective-permute-done((bf16[2,2,128,256]{3,2,1,0:T(8,128)(2,1)S(1)}, bf16[2,2,128,256]{3,2,1,0:T(8,128)(2,1)S(1)}, u32[]{:S(2)}, u32[]{:S(2)}) %collective-permute-start.9) | collective-permute-done | bytes 262176 | tf_op jit(solution)/shard_map/ppermute | solution.py:358
  35.6 0.3 shard_map.93
  35.9 2.1 %collective-permute-done.8.refs_3_ = bf16[256,256]{1,0:T(8,128)(2,1)S(1)} collective-permute-done((bf16[256,256]{1,0:T(8,128)(2,1)S(1)}, bf16[256,256]{1,0:T(8,128)(2,1)S(1)}, u32[]{:S(2)}, u32[]{:S(2)}) %collective-permute-start.8) | collective-permute-done | bytes 131104 | tf_op jit(solution)/shard_map/ppermute | solution.py:358
  38.0 0.0 collective-permute-done.11.w3
  38.0 0.0 collective-permute-done.10.other
  38.0 1.3 %shard_map.94 = (f32[512,256]{1,0:T(8,128)S(1)}, bf16[512,256]{1,0:T(8,128)(2,1)S(1)}) custom-call(bf16[512,512]{1,0:T(8,128)(2,1)S(1)} %shard_map.92.mine, bf16[512,512]{1,0:T(8,128)(2,1)S(1)} %collective-permute-done.10.other, bf16[256,512]{1,0:T(8,128)(2,1)S(1)} %copy-done.3, bf16[256,512]{1,0:T(8,128)(2,1)S(1)} %collective-permute-done.2.w1, ...), custom_call_target="tpu_custom_call" | custom-call | flops 536870912 | bytes 2097152 | tf_op jit(solution)/shard_map/pallas_call | solution.py:37
  39.3 1.3 %collective-permute-start.12 = (bf16[512,256]{1,0:T(8,128)(2,1)S(1)}, bf16[512,256]{1,0:T(8,128)(2,1)S(1)}, u32[]{:S(2)}, u32[]{:S(2)}) collective-permute-start(bf16[512,256]{1,0:T(8,128)(2,1)S(1)} %get-tuple-element.53), channel_id=1, source_target_pairs={{0,2},{1,3},{2,0},{3,1},{4,6},{5,7},{6,4},{7,5},{8,10},{9,11},{10,... | collective-permute-start | bytes 786440 | tf_op jit(solution)/shard_map/ppermute | solution.py:358
  40.6 0.0 collective-permute-start.18
  40.6 2.0 %collective-permute-start.23 = (bf16[256,256]{1,0:T(8,128)(2,1)S(1)}, bf16[256,256]{1,0:T(8,128)(2,1)S(1)}, u32[]{:S(2)}, u32[]{:S(2)}) collective-permute-start(bf16[256,256]{1,0:T(8,128)(2,1)S(1)} %collective-permute-done.8.refs_3_), channel_id=1, source_target_pairs={{0,4},{1,5},{2,6},{3,7},{4,12},{5,13},{6,14},{7,15},{8,0},{9,1},{1... | collective-permute-start | bytes 393224 | tf_op jit(solution)/shard_map/ppermute | solution.py:358
  42.6 0.9 collective-permute-start.16
  43.5 1.5 %collective-permute-start.17 = (bf16[2,2,128,128]{3,2,1,0:T(8,128)(2,1)S(1)}, bf16[2,2,128,128]{3,2,1,0:T(8,128)(2,1)S(1)}, u32[]{:S(2)}, u32[]{:S(2)}) collective-permute-start(bf16[2,2,128,128]{3,2,1,0:T(8,128)(2,1)S(1)} %get-tuple-element.59), channel_id=1, source_target_pairs={{0,12},{1,13},{2,14},{3,15},{4,8},{5,9},{6,10},{7,11},{8,4},{9,5},... | collective-permute-start | bytes 393224 | tf_op jit(solution)/shard_map/ppermute | solution.py:358
  45.0 1.6 %collective-permute-done.12.taken = bf16[512,256]{1,0:T(8,128)(2,1)S(1)} collective-permute-done((bf16[512,256]{1,0:T(8,128)(2,1)S(1)}, bf16[512,256]{1,0:T(8,128)(2,1)S(1)}, u32[]{:S(2)}, u32[]{:S(2)}) %collective-permute-start.12) | collective-permute-done | bytes 262176 | tf_op jit(solution)/shard_map/ppermute | solution.py:358
  46.6 0.3 shard_map.95
  47.0 0.1 collective-permute-start.13
  47.0 0.4 collective-permute-done.18.refs_7_
  47.4 1.3 %collective-permute-start.14 = (bf16[256,128]{1,0:T(8,128)(2,1)S(1)}, bf16[256,128]{1,0:T(8,128)(2,1)S(1)}, u32[]{:S(2)}, u32[]{:S(2)}) collective-permute-start(bf16[256,128]{1,0:T(8,128)(2,1)S(1)} %get-tuple-element.56), channel_id=1, source_target_pairs={{0,12},{1,13},{2,14},{3,15},{4,8},{5,9},{6,10},{7,11},{8,4},{9,5},... | collective-permute-start | bytes 196616 | tf_op jit(solution)/shard_map/ppermute | solution.py:358
  48.7 1.2 %collective-permute-done.23.refs_5_ = bf16[256,256]{1,0:T(8,128)(2,1)S(1)} collective-permute-done((bf16[256,256]{1,0:T(8,128)(2,1)S(1)}, bf16[256,256]{1,0:T(8,128)(2,1)S(1)}, u32[]{:S(2)}, u32[]{:S(2)}) %collective-permute-start.23) | collective-permute-done | bytes 131104 | tf_op jit(solution)/shard_map/ppermute | solution.py:358
  49.9 0.9 collective-permute-start.15
  50.8 10.4 %collective-permute-done.13.refs_1_ = bf16[256,128]{1,0:T(8,128)(2,1)S(1)} collective-permute-done((bf16[256,128]{1,0:T(8,128)(2,1)S(1)}, bf16[256,128]{1,0:T(8,128)(2,1)S(1)}, u32[]{:S(2)}, u32[]{:S(2)}) %collective-permute-start.13) | collective-permute-done | bytes 65568 | tf_op jit(solution)/shard_map/ppermute | solution.py:358
  61.2 1.3 %collective-permute-start.24 = (bf16[2,256,256]{2,1,0:T(8,128)(2,1)S(1)}, bf16[2,256,256]{2,1,0:T(8,128)(2,1)S(1)}, u32[]{:S(2)}, u32[]{:S(2)}) collective-permute-start(bf16[2,256,256]{2,1,0:T(8,128)(2,1)S(1)} %pad_maximum_fusion), channel_id=1, source_target_pairs={{0,4},{1,5},{2,6},{3,7},{4,12},{5,13},{6,14},{7,15},{8,0},{9,1},{1... | collective-permute-start | bytes 786440 | tf_op jit(solution)/shard_map/ppermute | solution.py:358
  62.5 0.0 collective-permute-done.16.refs_5_
  62.5 0.0 collective-permute-done.17.refs_6_
  62.5 1.8 %shard_map.96 = (bf16[256,128]{1,0:T(8,128)(2,1)S(1)}, bf16[256,128]{1,0:T(8,128)(2,1)S(1)}, bf16[256,128]{1,0:T(8,128)(2,1)S(1)}, bf16[256,128]{1,0:T(8,128)(2,1)S(1)}) custom-call(bf16[256,128]{1,0:T(8,128)(2,1)S(1)} %get-tuple-element.54.refs_0_, bf16[256,128]{1,0:T(8,128)(2,1)S(1)} %collective-permute-done.13.refs_1_, ...), custom_call_target="tpu_custom_call" | custom-call | flops 1073741824 | bytes 5242880 | tf_op jit(solution)/shard_map/pallas_call | solution.py:37
  64.3 1.1 %collective-permute-start.19 = (bf16[256,128]{1,0:T(8,128)(2,1)S(1)}, bf16[256,128]{1,0:T(8,128)(2,1)S(1)}, u32[]{:S(2)}, u32[]{:S(2)}) collective-permute-start(bf16[256,128]{1,0:T(8,128)(2,1)S(1)} %get-tuple-element.62), channel_id=1, source_target_pairs={{0,4},{1,5},{2,6},{3,7},{4,12},{5,13},{6,14},{7,15},{8,0},{9,1},{1... | collective-permute-start | bytes 196616 | tf_op jit(solution)/shard_map/ppermute | solution.py:358
  65.5 2.1 %collective-permute-start.20 = (bf16[256,128]{1,0:T(8,128)(2,1)S(1)}, bf16[256,128]{1,0:T(8,128)(2,1)S(1)}, u32[]{:S(2)}, u32[]{:S(2)}) collective-permute-start(bf16[256,128]{1,0:T(8,128)(2,1)S(1)} %get-tuple-element.63), channel_id=1, source_target_pairs={{0,12},{1,13},{2,14},{3,15},{4,8},{5,9},{6,10},{7,11},{8,4},{9,5},... | collective-permute-start | bytes 196616 | tf_op jit(solution)/shard_map/ppermute | solution.py:358
  67.5 0.7 collective-permute-start.21
  68.2 5.2 %collective-permute-done.19.e1 = bf16[256,128]{1,0:T(8,128)(2,1)S(1)} collective-permute-done((bf16[256,128]{1,0:T(8,128)(2,1)S(1)}, bf16[256,128]{1,0:T(8,128)(2,1)S(1)}, u32[]{:S(2)}, u32[]{:S(2)}) %collective-permute-start.19) | collective-permute-done | bytes 65568 | tf_op jit(solution)/shard_map/ppermute | solution.py:358
  73.4 0.2 shard_map.98
  73.6 0.1 collective-permute-start.25
  73.7 0.2 shard_map.97.gated
  73.9 0.5 collective-permute-start.22
  74.5 1.5 %collective-permute-done.22.other = bf16[512,256]{1,0:T(8,128)(2,1)S(1)} collective-permute-done((bf16[512,256]{1,0:T(8,128)(2,1)S(1)}, bf16[512,256]{1,0:T(8,128)(2,1)S(1)}, u32[]{:S(2)}, u32[]{:S(2)}) %collective-permute-start.22) | collective-permute-done | bytes 262176 | tf_op jit(solution)/shard_map/ppermute | solution.py:358
  76.0 0.8 shard_map.100
  76.8 1.9 %collective-permute-start.26 = (bf16[128,1024]{1,0:T(8,128)(2,1)S(1)}, bf16[128,1024]{1,0:T(8,128)(2,1)S(1)}, u32[]{:S(2)}, u32[]{:S(2)}) collective-permute-start(bf16[128,1024]{1,0:T(8,128)(2,1)S(1)} %get-tuple-element.72), channel_id=1, source_target_pairs={{0,18},{1,19},{2,16},{3,17},{4,22},{5,23},{6,20},{7,21},{8,26},{9,... | collective-permute-start | bytes 786440 | tf_op jit(solution)/shard_map/ppermute | solution.py:358
  78.6 0.5 collective-permute-start.27
  79.2 0.8 shard_map.99
  80.0 1.2 %collective-permute-start.28 = (bf16[128,1024]{1,0:T(8,128)(2,1)S(1)}, bf16[128,1024]{1,0:T(8,128)(2,1)S(1)}, u32[]{:S(2)}, u32[]{:S(2)}) collective-permute-start(bf16[128,1024]{1,0:T(8,128)(2,1)S(1)} %get-tuple-element.74), channel_id=1, source_target_pairs={{0,16},{1,17},{2,18},{3,19},{4,20},{5,21},{6,22},{7,23},{8,24},{9,... | collective-permute-start | bytes 786440 | tf_op jit(solution)/shard_map/ppermute | solution.py:358
  81.2 5.7 %collective-permute-done.26 = bf16[128,1024]{1,0:T(8,128)(2,1)S(1)} collective-permute-done((bf16[128,1024]{1,0:T(8,128)(2,1)S(1)}, bf16[128,1024]{1,0:T(8,128)(2,1)S(1)}, u32[]{:S(2)}, u32[]{:S(2)}) %collective-permute-start.26) | collective-permute-done | bytes 262176 | tf_op jit(solution)/shard_map/ppermute | solution.py:358
  87.0 4.2 %collective-permute-done.27 = bf16[128,1024]{1,0:T(8,128)(2,1)S(1)} collective-permute-done((bf16[128,1024]{1,0:T(8,128)(2,1)S(1)}, bf16[128,1024]{1,0:T(8,128)(2,1)S(1)}, u32[]{:S(2)}, u32[]{:S(2)}) %collective-permute-start.27) | collective-permute-done | bytes 262176 | tf_op jit(solution)/shard_map/ppermute | solution.py:358
  91.2 0.6 collective-permute-done.28
  91.7 0.8 add_convert_fusion
  (33 shorter events, 0.1 us)
Async XLA Ops:
  0.0 1.0 %copy-start = (bf16[256,1024]{1,0:T(8,128)(2,1)S(1)}, bf16[256,1024]{1,0:T(8,128)(2,1)}, u32[]{:S(2)}) copy-start(bf16[256,1024]{1,0:T(8,128)(2,1)} %param.12) | copy-start | bytes 1572868
  1.1 3.1 %copy-start.2 = (bf16[256,512]{1,0:T(8,128)(2,1)}, bf16[256,512]{1,0:T(8,128)(2,1)S(1)}, u32[]{:S(2)}) copy-start(bf16[256,512]{1,0:T(8,128)(2,1)S(1)} %constant_dynamic-slice_fusion.after.w0) | copy-start | bytes 786436
  1.1 22.9 %copy-start.5 = (bf16[128,1024]{1,0:T(8,128)(2,1)S(1)}, bf16[128,1024]{1,0:T(8,128)(2,1)}, u32[]{:S(2)}) copy-start(bf16[128,1024]{1,0:T(8,128)(2,1)} %refs_0_.1) | copy-start | bytes 786436
  1.1 13.2 %collective-permute-start.2 = (bf16[256,512]{1,0:T(8,128)(2,1)S(1)}, bf16[256,512]{1,0:T(8,128)(2,1)S(1)}, u32[]{:S(2)}, u32[]{:S(2)}) collective-permute-start(bf16[256,512]{1,0:T(8,128)(2,1)S(1)} %constant_dynamic-slice_fusion.after.w0), channel_id=1, source_target_pairs={{0,4},{1,5},{2,6},{3,7},{4,12},{5,13},{6,14},{7,15},{8,0},{9,1},{1... | collective-permute-start | bytes 786440 | tf_op jit(solution)/shard_map/ppermute | solution.py:358
  6.8 28.8 %copy-start.1 = (bf16[2,2,128,1024]{3,2,1,0:T(8,128)(2,1)S(1)}, bf16[2,2,128,1024]{3,2,1,0:T(8,128)(2,1)}, u32[]{:S(2)}) copy-start(bf16[2,2,128,1024]{3,2,1,0:T(8,128)(2,1)} %filt.3) | copy-start | bytes 3145732
  6.8 7.5 %collective-permute-start.1 = (bf16[256,256]{1,0:T(8,128)(2,1)}, bf16[256,256]{1,0:T(8,128)(2,1)S(1)}, u32[]{:S(2)}, u32[]{:S(2)}) collective-permute-start(bf16[256,256]{1,0:T(8,128)(2,1)} %get-tuple-element.41.refs_0_), channel_id=1, source_target_pairs={{0,4},{1,5},{2,6},{3,7},{4,12},{5,13},{6,14},{7,15},{8,0},{9,1},{1... | collective-permute-start | bytes 393224 | tf_op jit(solution)/shard_map/ppermute | solution.py:358
  9.4 9.5 %collective-permute-start = (bf16[128,1024]{1,0:T(8,128)(2,1)}, bf16[128,1024]{1,0:T(8,128)(2,1)S(1)}, u32[]{:S(2)}, u32[]{:S(2)}) collective-permute-start(bf16[128,1024]{1,0:T(8,128)(2,1)} %get-tuple-element.40), channel_id=1, source_target_pairs={{0,2},{1,3},{2,0},{3,1},{4,6},{5,7},{6,4},{7,5},{8,10},{9,11},{10,... | collective-permute-start | bytes 786440 | tf_op jit(solution)/shard_map/ppermute | solution.py:358
  10.9 13.0 %collective-permute-start.4 = (bf16[128,1024]{1,0:T(8,128)(2,1)}, bf16[128,1024]{1,0:T(8,128)(2,1)S(1)}, u32[]{:S(2)}, u32[]{:S(2)}) collective-permute-start(bf16[128,1024]{1,0:T(8,128)(2,1)} %get-tuple-element.44), channel_id=1, source_target_pairs={{0,16},{1,17},{2,18},{3,19},{4,20},{5,21},{6,22},{7,23},{8,24},{9,... | collective-permute-start | bytes 786440 | tf_op jit(solution)/shard_map/ppermute | solution.py:358
  12.4 11.6 %copy-start.12 = (bf16[256,256]{1,0:T(8,128)(2,1)S(1)}, bf16[256,256]{1,0:T(8,128)(2,1)}, u32[]{:S(2)}) copy-start(bf16[256,256]{1,0:T(8,128)(2,1)} %get-tuple-element.47) | copy-start | bytes 393220
  12.4 13.0 %copy-start.11 = (bf16[2,2,128,256]{3,2,1,0:T(8,128)(2,1)S(1)}, bf16[2,2,128,256]{3,2,1,0:T(8,128)(2,1)}, u32[]{:S(2)}) copy-start(bf16[2,2,128,256]{3,2,1,0:T(8,128)(2,1)} %get-tuple-element.49) | copy-start | bytes 786436
  12.4 11.5 %collective-permute-start.5 = (bf16[128,1024]{1,0:T(8,128)(2,1)}, bf16[128,1024]{1,0:T(8,128)(2,1)S(1)}, u32[]{:S(2)}, u32[]{:S(2)}) collective-permute-start(bf16[128,1024]{1,0:T(8,128)(2,1)} %get-tuple-element.45), channel_id=1, source_target_pairs={{0,18},{1,19},{2,16},{3,17},{4,22},{5,23},{6,20},{7,21},{8,26},{9,... | collective-permute-start | bytes 786440 | tf_op jit(solution)/shard_map/ppermute | solution.py:358
  14.3 7.3 %collective-permute-start.3 = (bf16[256,256]{1,0:T(8,128)(2,1)S(1)}, bf16[256,256]{1,0:T(8,128)(2,1)S(1)}, u32[]{:S(2)}, u32[]{:S(2)}) collective-permute-start(bf16[256,256]{1,0:T(8,128)(2,1)S(1)} %collective-permute-done.1.refs_2_), channel_id=1, source_target_pairs={{0,4},{1,5},{2,6},{3,7},{4,12},{5,13},{6,14},{7,15},{8,0},{9,1},{1... | collective-permute-start | bytes 393224 | tf_op jit(solution)/shard_map/ppermute | solution.py:358
  15.2 10.9 %collective-permute-start.7 = (bf16[256,512]{1,0:T(8,128)(2,1)S(1)}, bf16[256,512]{1,0:T(8,128)(2,1)S(1)}, u32[]{:S(2)}, u32[]{:S(2)}) collective-permute-start(bf16[256,512]{1,0:T(8,128)(2,1)S(1)} %collective-permute-done.2.w1), channel_id=1, source_target_pairs={{0,4},{1,5},{2,6},{3,7},{4,12},{5,13},{6,14},{7,15},{8,0},{9,1},{1... | collective-permute-start | bytes 786440 | tf_op jit(solution)/shard_map/ppermute | solution.py:358
  24.0 14.0 %collective-permute-start.10 = (bf16[512,512]{1,0:T(8,128)(2,1)S(1)}, bf16[512,512]{1,0:T(8,128)(2,1)S(1)}, u32[]{:S(2)}, u32[]{:S(2)}) collective-permute-start(bf16[512,512]{1,0:T(8,128)(2,1)S(1)} %shard_map.92.mine), channel_id=1, source_target_pairs={{0,1},{1,0},{2,3},{3,2},{4,5},{5,4},{6,7},{7,6},{8,9},{9,8},{10,11... | collective-permute-start | bytes 1572872 | tf_op jit(solution)/shard_map/ppermute | solution.py:358
  24.1 6.4 %collective-permute-start.6 = (bf16[256,256]{1,0:T(8,128)(2,1)S(1)}, bf16[256,256]{1,0:T(8,128)(2,1)S(1)}, u32[]{:S(2)}, u32[]{:S(2)}) collective-permute-start(bf16[256,256]{1,0:T(8,128)(2,1)S(1)} %copy-done.12), channel_id=1, source_target_pairs={{0,2},{1,3},{2,0},{3,1},{4,6},{5,7},{6,4},{7,5},{8,10},{9,11},{10,... | collective-permute-start | bytes 393224 | tf_op jit(solution)/shard_map/ppermute | solution.py:358
  25.4 12.6 %copy-start.3 = (bf16[256,512]{1,0:T(8,128)(2,1)S(1)}, bf16[256,512]{1,0:T(8,128)(2,1)}, u32[]{:S(2)}) copy-start(bf16[256,512]{1,0:T(8,128)(2,1)} %copy-done.2) | copy-start | bytes 786436
  25.4 10.2 %collective-permute-start.9 = (bf16[2,2,128,256]{3,2,1,0:T(8,128)(2,1)S(1)}, bf16[2,2,128,256]{3,2,1,0:T(8,128)(2,1)S(1)}, u32[]{:S(2)}, u32[]{:S(2)}) collective-permute-start(bf16[2,2,128,256]{3,2,1,0:T(8,128)(2,1)S(1)} %copy-done.11), channel_id=1, source_target_pairs={{0,2},{1,3},{2,0},{3,1},{4,6},{5,7},{6,4},{7,5},{8,10},{9,11},{10,... | collective-permute-start | bytes 786440 | tf_op jit(solution)/shard_map/ppermute | solution.py:358
  26.2 11.8 %collective-permute-start.11 = (bf16[256,512]{1,0:T(8,128)(2,1)S(1)}, bf16[256,512]{1,0:T(8,128)(2,1)S(1)}, u32[]{:S(2)}, u32[]{:S(2)}) collective-permute-start(bf16[256,512]{1,0:T(8,128)(2,1)S(1)} %collective-permute-done.7.w2), channel_id=1, source_target_pairs={{0,4},{1,5},{2,6},{3,7},{4,12},{5,13},{6,14},{7,15},{8,0},{9,1},{1... | collective-permute-start | bytes 786440 | tf_op jit(solution)/shard_map/ppermute | solution.py:358
  30.4 7.5 %collective-permute-start.8 = (bf16[256,256]{1,0:T(8,128)(2,1)S(1)}, bf16[256,256]{1,0:T(8,128)(2,1)S(1)}, u32[]{:S(2)}, u32[]{:S(2)}) collective-permute-start(bf16[256,256]{1,0:T(8,128)(2,1)S(1)} %collective-permute-done.6.refs_1_), channel_id=1, source_target_pairs={{0,4},{1,5},{2,6},{3,7},{4,12},{5,13},{6,14},{7,15},{8,0},{9,1},{1... | collective-permute-start | bytes 393224 | tf_op jit(solution)/shard_map/ppermute | solution.py:358
  38.0 8.6 %copy-start.4 = (bf16[128,1024]{1,0:T(8,128)(2,1)S(1)}, bf16[128,1024]{1,0:T(8,128)(2,1)}, u32[]{:S(2)}) copy-start(bf16[128,1024]{1,0:T(8,128)(2,1)} %g0.2) | copy-start | bytes 786436
  39.3 7.3 %collective-permute-start.12 = (bf16[512,256]{1,0:T(8,128)(2,1)S(1)}, bf16[512,256]{1,0:T(8,128)(2,1)S(1)}, u32[]{:S(2)}, u32[]{:S(2)}) collective-permute-start(bf16[512,256]{1,0:T(8,128)(2,1)S(1)} %get-tuple-element.53), channel_id=1, source_target_pairs={{0,2},{1,3},{2,0},{3,1},{4,6},{5,7},{6,4},{7,5},{8,10},{9,11},{10,... | collective-permute-start | bytes 786440 | tf_op jit(solution)/shard_map/ppermute | solution.py:358
  40.6 6.0 %copy-start.8 = (f32[1024]{0:T(1024)S(1)}, f32[1024]{0:T(1024)}, u32[]{:S(2)}) copy-start(f32[1024]{0:T(1024)} %param.13) | copy-start | bytes 12292
  40.6 6.8 %collective-permute-start.18 = (bf16[2,2,128,128]{3,2,1,0:T(8,128)(2,1)S(1)}, bf16[2,2,128,128]{3,2,1,0:T(8,128)(2,1)S(1)}, u32[]{:S(2)}, u32[]{:S(2)}) collective-permute-start(bf16[2,2,128,128]{3,2,1,0:T(8,128)(2,1)S(1)} %get-tuple-element.60), channel_id=1, source_target_pairs={{0,8},{1,9},{2,10},{3,11},{4,0},{5,1},{6,2},{7,3},{8,12},{9,13},{1... | collective-permute-start | bytes 393224 | tf_op jit(solution)/shard_map/ppermute | solution.py:358
  40.6 9.3 %collective-permute-start.23 = (bf16[256,256]{1,0:T(8,128)(2,1)S(1)}, bf16[256,256]{1,0:T(8,128)(2,1)S(1)}, u32[]{:S(2)}, u32[]{:S(2)}) collective-permute-start(bf16[256,256]{1,0:T(8,128)(2,1)S(1)} %collective-permute-done.8.refs_3_), channel_id=1, source_target_pairs={{0,4},{1,5},{2,6},{3,7},{4,12},{5,13},{6,14},{7,15},{8,0},{9,1},{1... | collective-permute-start | bytes 393224 | tf_op jit(solution)/shard_map/ppermute | solution.py:358
  42.6 19.9 %collective-permute-start.16 = (bf16[2,2,128,128]{3,2,1,0:T(8,128)(2,1)S(1)}, bf16[2,2,128,128]{3,2,1,0:T(8,128)(2,1)S(1)}, u32[]{:S(2)}, u32[]{:S(2)}) collective-permute-start(bf16[2,2,128,128]{3,2,1,0:T(8,128)(2,1)S(1)} %get-tuple-element.58), channel_id=1, source_target_pairs={{0,4},{1,5},{2,6},{3,7},{4,12},{5,13},{6,14},{7,15},{8,0},{9,1},{1... | collective-permute-start | bytes 393224 | tf_op jit(solution)/shard_map/ppermute | solution.py:358
  43.5 19.0 %collective-permute-start.17 = (bf16[2,2,128,128]{3,2,1,0:T(8,128)(2,1)S(1)}, bf16[2,2,128,128]{3,2,1,0:T(8,128)(2,1)S(1)}, u32[]{:S(2)}, u32[]{:S(2)}) collective-permute-start(bf16[2,2,128,128]{3,2,1,0:T(8,128)(2,1)S(1)} %get-tuple-element.59), channel_id=1, source_target_pairs={{0,12},{1,13},{2,14},{3,15},{4,8},{5,9},{6,10},{7,11},{8,4},{9,5},... | collective-permute-start | bytes 393224 | tf_op jit(solution)/shard_map/ppermute | solution.py:358
  46.6 15.9 %copy-start.9 = (bf16[16,256,128]{2,1,0:T(8,128)(2,1)S(1)}, bf16[16,256,128]{2,1,0:T(8,128)(2,1)}, u32[]{:S(2)}) copy-start(bf16[16,256,128]{2,1,0:T(8,128)(2,1)} %constant.17.clone.refs_9_) | copy-start | bytes 3145732
  46.6 15.9 %copy-start.10 = (bf16[16,256,128]{2,1,0:T(8,128)(2,1)S(1)}, bf16[16,256,128]{2,1,0:T(8,128)(2,1)}, u32[]{:S(2)}) copy-start(bf16[16,256,128]{2,1,0:T(8,128)(2,1)} %constant.16.clone.refs_8_) | copy-start | bytes 3145732
  47.0 14.3 %collective-permute-start.13 = (bf16[256,128]{1,0:T(8,128)(2,1)S(1)}, bf16[256,128]{1,0:T(8,128)(2,1)S(1)}, u32[]{:S(2)}, u32[]{:S(2)}) collective-permute-start(bf16[256,128]{1,0:T(8,128)(2,1)S(1)} %get-tuple-element.55), channel_id=1, source_target_pairs={{0,4},{1,5},{2,6},{3,7},{4,12},{5,13},{6,14},{7,15},{8,0},{9,1},{1... | collective-permute-start | bytes 196616 | tf_op jit(solution)/shard_map/ppermute | solution.py:358
  47.4 13.8 %collective-permute-start.14 = (bf16[256,128]{1,0:T(8,128)(2,1)S(1)}, bf16[256,128]{1,0:T(8,128)(2,1)S(1)}, u32[]{:S(2)}, u32[]{:S(2)}) collective-permute-start(bf16[256,128]{1,0:T(8,128)(2,1)S(1)} %get-tuple-element.56), channel_id=1, source_target_pairs={{0,12},{1,13},{2,14},{3,15},{4,8},{5,9},{6,10},{7,11},{8,4},{9,5},... | collective-permute-start | bytes 196616 | tf_op jit(solution)/shard_map/ppermute | solution.py:358
  49.9 11.3 %collective-permute-start.15 = (bf16[256,128]{1,0:T(8,128)(2,1)S(1)}, bf16[256,128]{1,0:T(8,128)(2,1)S(1)}, u32[]{:S(2)}, u32[]{:S(2)}) collective-permute-start(bf16[256,128]{1,0:T(8,128)(2,1)S(1)} %get-tuple-element.57), channel_id=1, source_target_pairs={{0,8},{1,9},{2,10},{3,11},{4,0},{5,1},{6,2},{7,3},{8,12},{9,13},{1... | collective-permute-start | bytes 196616 | tf_op jit(solution)/shard_map/ppermute | solution.py:358
  61.2 12.2 %collective-permute-start.24 = (bf16[2,256,256]{2,1,0:T(8,128)(2,1)S(1)}, bf16[2,256,256]{2,1,0:T(8,128)(2,1)S(1)}, u32[]{:S(2)}, u32[]{:S(2)}) collective-permute-start(bf16[2,256,256]{2,1,0:T(8,128)(2,1)S(1)} %pad_maximum_fusion), channel_id=1, source_target_pairs={{0,4},{1,5},{2,6},{3,7},{4,12},{5,13},{6,14},{7,15},{8,0},{9,1},{1... | collective-permute-start | bytes 786440 | tf_op jit(solution)/shard_map/ppermute | solution.py:358
  62.5 10.9 %copy-start.7 = (bf16[256,256]{1,0:T(8,128)(2,1)S(1)}, bf16[256,256]{1,0:T(8,128)(2,1)}, u32[]{:S(2)}) copy-start(bf16[256,256]{1,0:T(8,128)(2,1)} %get-tuple-element.41.refs_0_) | copy-start | bytes 393220
  64.3 9.1 %collective-permute-start.19 = (bf16[256,128]{1,0:T(8,128)(2,1)S(1)}, bf16[256,128]{1,0:T(8,128)(2,1)S(1)}, u32[]{:S(2)}, u32[]{:S(2)}) collective-permute-start(bf16[256,128]{1,0:T(8,128)(2,1)S(1)} %get-tuple-element.62), channel_id=1, source_target_pairs={{0,4},{1,5},{2,6},{3,7},{4,12},{5,13},{6,14},{7,15},{8,0},{9,1},{1... | collective-permute-start | bytes 196616 | tf_op jit(solution)/shard_map/ppermute | solution.py:358
  65.5 8.0 %collective-permute-start.20 = (bf16[256,128]{1,0:T(8,128)(2,1)S(1)}, bf16[256,128]{1,0:T(8,128)(2,1)S(1)}, u32[]{:S(2)}, u32[]{:S(2)}) collective-permute-start(bf16[256,128]{1,0:T(8,128)(2,1)S(1)} %get-tuple-element.63), channel_id=1, source_target_pairs={{0,12},{1,13},{2,14},{3,15},{4,8},{5,9},{6,10},{7,11},{8,4},{9,5},... | collective-permute-start | bytes 196616 | tf_op jit(solution)/shard_map/ppermute | solution.py:358
  67.5 6.2 %copy-start.6 = (bf16[128,1024]{1,0:T(8,128)(2,1)S(1)}, bf16[128,1024]{1,0:T(8,128)(2,1)}, u32[]{:S(2)}) copy-start(bf16[128,1024]{1,0:T(8,128)(2,1)} %g0.3) | copy-start | bytes 786436
  67.5 5.9 %collective-permute-start.21 = (bf16[256,128]{1,0:T(8,128)(2,1)S(1)}, bf16[256,128]{1,0:T(8,128)(2,1)S(1)}, u32[]{:S(2)}, u32[]{:S(2)}) collective-permute-start(bf16[256,128]{1,0:T(8,128)(2,1)S(1)} %get-tuple-element.64), channel_id=1, source_target_pairs={{0,8},{1,9},{2,10},{3,11},{4,0},{5,1},{6,2},{7,3},{8,12},{9,13},{1... | collective-permute-start | bytes 196616 | tf_op jit(solution)/shard_map/ppermute | solution.py:358
  73.6 2.4 %collective-permute-start.25 = (bf16[4,256,256]{2,1,0:T(8,128)(2,1)S(1)}, bf16[4,256,256]{2,1,0:T(8,128)(2,1)S(1)}, u32[]{:S(2)}, u32[]{:S(2)}) collective-permute-start(bf16[4,256,256]{2,1,0:T(8,128)(2,1)S(1)} %get-tuple-element.70), channel_id=1, source_target_pairs={{0,1},{1,0},{2,3},{3,2},{4,5},{5,4},{6,7},{7,6},{8,9},{9,8},{10,11... | collective-permute-start | bytes 1572872 | tf_op jit(solution)/shard_map/ppermute | solution.py:358
  73.9 2.0 %collective-permute-start.22 = (bf16[512,256]{1,0:T(8,128)(2,1)S(1)}, bf16[512,256]{1,0:T(8,128)(2,1)S(1)}, u32[]{:S(2)}, u32[]{:S(2)}) collective-permute-start(bf16[512,256]{1,0:T(8,128)(2,1)S(1)} %shard_map.97.gated), channel_id=1, source_target_pairs={{0,1},{1,0},{2,3},{3,2},{4,5},{5,4},{6,7},{7,6},{8,9},{9,8},{10,11... | collective-permute-start | bytes 786440 | tf_op jit(solution)/shard_map/ppermute | solution.py:358
  76.8 10.2 %collective-permute-start.26 = (bf16[128,1024]{1,0:T(8,128)(2,1)S(1)}, bf16[128,1024]{1,0:T(8,128)(2,1)S(1)}, u32[]{:S(2)}, u32[]{:S(2)}) collective-permute-start(bf16[128,1024]{1,0:T(8,128)(2,1)S(1)} %get-tuple-element.72), channel_id=1, source_target_pairs={{0,18},{1,19},{2,16},{3,17},{4,22},{5,23},{6,20},{7,21},{8,26},{9,... | collective-permute-start | bytes 786440 | tf_op jit(solution)/shard_map/ppermute | solution.py:358
  78.6 12.5 %collective-permute-start.27 = (bf16[128,1024]{1,0:T(8,128)(2,1)S(1)}, bf16[128,1024]{1,0:T(8,128)(2,1)S(1)}, u32[]{:S(2)}, u32[]{:S(2)}) collective-permute-start(bf16[128,1024]{1,0:T(8,128)(2,1)S(1)} %get-tuple-element.73), channel_id=1, source_target_pairs={{0,2},{1,3},{2,0},{3,1},{4,6},{5,7},{6,4},{7,5},{8,10},{9,11},{10,... | collective-permute-start | bytes 786440 | tf_op jit(solution)/shard_map/ppermute | solution.py:358
  80.0 11.7 %collective-permute-start.28 = (bf16[128,1024]{1,0:T(8,128)(2,1)S(1)}, bf16[128,1024]{1,0:T(8,128)(2,1)S(1)}, u32[]{:S(2)}, u32[]{:S(2)}) collective-permute-start(bf16[128,1024]{1,0:T(8,128)(2,1)S(1)} %get-tuple-element.74), channel_id=1, source_target_pairs={{0,16},{1,17},{2,18},{3,19},{4,20},{5,21},{6,22},{7,23},{8,24},{9,... | collective-permute-start | bytes 786440 | tf_op jit(solution)/shard_map/ppermute | solution.py:358

commit v20 on v18

--- a/solution.py
+++ b/solution.py
@@ -408,7 +408,7 @@
         [pltpu.VMEM((512, 512), F32)],
         flops=1 << 29,
         moved=2 << 20,
-    )(after(mine, r1, filters[0]), other, own_v, v1, v2, v3)
+    )(after(mine, filters[0], got_o), other, own_v, v1, v2, v3)
     r2 = onward(after(r1, keep))
     drive, *sends = in_vmem(
         drive_kernel,

time: 92.8 us -> 93.8 us (1.011)
  starting transfers between devices: 34.7 us -> 35.7 us
    ppermute x29, starting transfers between devices: 34.7 us -> 35.7 us  [permute(): return lax.ppermute(values, AXES, pairs)]
  transfers between devices with their start and end apart: 29 -> 29, of which waited for: 16 -> 17; matrix products, arithmetic and copies ran while one was open for 0% -> 0% of each run, Pallas kernels for 7% -> 6%
where the time goes in v20:
time: 93.8 us; the launch traced here: 93.7 us
  waiting for transfers between devices  47.4 us (51%)
  starting transfers between devices  35.7 us (38%)
  Pallas kernels  8.34 us (9%)
  local copies, waits for them, and re-layouts  1.12 us (1%)
    ppermute x29, waiting for transfers between devices, permute(): return lax.ppermute(values, AXES, pairs)  47.4 us
    ppermute x29, starting transfers between devices, permute(): return lax.ppermute(values, AXES, pairs)  35.7 us
    pallas_call x9, Pallas kernels, call(): pl.pallas_call(kernel, out_shape=out_shape, in_specs=specs, out_specs=jax...  5.76 us
    pallas_call x1, Pallas kernels, call(): pl.pallas_call(kernel, out_shape=out_shape, in_specs=[pl.BlockSpec(memory...  2.58 us
  transfers between devices with their start and end apart: 29, of which 17 were waited for; matrix products, arithmetic and copies ran while one was open for 0% of the time, Pallas kernels for 6%

profile of v20, /device:TPU:0, one launch (start us, length us, event | category | flops | bytes accessed | tf_op | source)
XLA Modules:
  0.0 93.7 jit_solution(11063307162345458264)
XLA Ops:
  0.0 1.0 %copy-done = bf16[256,1024]{1,0:T(8,128)(2,1)S(1)} copy-done((bf16[256,1024]{1,0:T(8,128)(2,1)S(1)}, bf16[256,1024]{1,0:T(8,128)(2,1)}, u32[]{:S(2)}) %copy-start) | copy-done | bytes 524312
  1.1 0.0 copy-start.2
  1.1 0.0 copy-start.5
  1.1 3.1 %collective-permute-start.2 = (bf16[256,512]{1,0:T(8,128)(2,1)S(1)}, bf16[256,512]{1,0:T(8,128)(2,1)S(1)}, u32[]{:S(2)}, u32[]{:S(2)}) collective-permute-start(bf16[256,512]{1,0:T(8,128)(2,1)S(1)} %constant_dynamic-slice_fusion.after.w0), channel_id=1, source_target_pairs={{0,4},{1,5},{2,6},{3,7},{4,12},{5,13},{6,14},{7,15},{8,0},{9,1},{1... | collective-permute-start | bytes 786440 | tf_op jit(solution)/shard_map/ppermute | solution.py:358
  4.2 2.6 %shard_map.91 = (bf16[128,1024]{1,0:T(8,128)(2,1)}, bf16[128,1024]{1,0:T(8,128)(2,1)}, bf16[128,1024]{1,0:T(8,128)(2,1)}, bf16[256,256]{1,0:T(8,128)(2,1)}, bf16...) custom-call(bf16[128,1024]{1,0:T(8,128)(2,1)} %refs_0_.1, bf16[128,1024]{1,0:T(8,128)(2,1)} %g0.2, ...), custom_call_target="tpu_custom_call" | custom-call | tf_op jit(solution)/shard_map/pallas_call | solution.py:106
  6.8 0.0 copy-start.1
  6.8 2.6 %collective-permute-start.1 = (bf16[256,256]{1,0:T(8,128)(2,1)}, bf16[256,256]{1,0:T(8,128)(2,1)S(1)}, u32[]{:S(2)}, u32[]{:S(2)}) collective-permute-start(bf16[256,256]{1,0:T(8,128)(2,1)} %get-tuple-element.41.refs_0_), channel_id=1, source_target_pairs={{0,4},{1,5},{2,6},{3,7},{4,12},{5,13},{6,14},{7,15},{8,0},{9,1},{1... | collective-permute-start | bytes 393224 | tf_op jit(solution)/shard_map/ppermute | solution.py:358
  9.4 1.5 %collective-permute-start = (bf16[128,1024]{1,0:T(8,128)(2,1)}, bf16[128,1024]{1,0:T(8,128)(2,1)S(1)}, u32[]{:S(2)}, u32[]{:S(2)}) collective-permute-start(bf16[128,1024]{1,0:T(8,128)(2,1)} %get-tuple-element.40), channel_id=1, source_target_pairs={{0,2},{1,3},{2,0},{3,1},{4,6},{5,7},{6,4},{7,5},{8,10},{9,11},{10,... | collective-permute-start | bytes 786440 | tf_op jit(solution)/shard_map/ppermute | solution.py:358
  10.9 1.5 %collective-permute-start.4 = (bf16[128,1024]{1,0:T(8,128)(2,1)}, bf16[128,1024]{1,0:T(8,128)(2,1)S(1)}, u32[]{:S(2)}, u32[]{:S(2)}) collective-permute-start(bf16[128,1024]{1,0:T(8,128)(2,1)} %get-tuple-element.44), channel_id=1, source_target_pairs={{0,16},{1,17},{2,18},{3,19},{4,20},{5,21},{6,22},{7,23},{8,24},{9,... | collective-permute-start | bytes 786440 | tf_op jit(solution)/shard_map/ppermute | solution.py:358
  12.4 0.5 collective-permute-start.5
  12.9 1.4 %collective-permute-done.1.refs_2_ = bf16[256,256]{1,0:T(8,128)(2,1)S(1)} collective-permute-done((bf16[256,256]{1,0:T(8,128)(2,1)}, bf16[256,256]{1,0:T(8,128)(2,1)S(1)}, u32[]{:S(2)}, u32[]{:S(2)}) %collective-permute-start.1) | collective-permute-done | bytes 131104 | tf_op jit(solution)/shard_map/ppermute | solution.py:358
  14.3 0.9 %collective-permute-start.3 = (bf16[256,256]{1,0:T(8,128)(2,1)S(1)}, bf16[256,256]{1,0:T(8,128)(2,1)S(1)}, u32[]{:S(2)}, u32[]{:S(2)}) collective-permute-start(bf16[256,256]{1,0:T(8,128)(2,1)S(1)} %collective-permute-done.1.refs_2_), channel_id=1, source_target_pairs={{0,4},{1,5},{2,6},{3,7},{4,12},{5,13},{6,14},{7,15},{8,0},{9,1},{1... | collective-permute-start | bytes 393224 | tf_op jit(solution)/shard_map/ppermute | solution.py:358
  15.2 3.3 %collective-permute-start.9 = (bf16[256,512]{1,0:T(8,128)(2,1)S(1)}, bf16[256,512]{1,0:T(8,128)(2,1)S(1)}, u32[]{:S(2)}, u32[]{:S(2)}) collective-permute-start(bf16[256,512]{1,0:T(8,128)(2,1)S(1)} %collective-permute-done.2.w1), channel_id=1, source_target_pairs={{0,4},{1,5},{2,6},{3,7},{4,12},{5,13},{6,14},{7,15},{8,0},{9,1},{1... | collective-permute-start | bytes 786440 | tf_op jit(solution)/shard_map/ppermute | solution.py:358
  18.5 0.4 collective-permute-done.refs_1_.g1
  18.9 2.8 %collective-permute-done.3.refs_4_ = bf16[256,256]{1,0:T(8,128)(2,1)S(1)} collective-permute-done((bf16[256,256]{1,0:T(8,128)(2,1)S(1)}, bf16[256,256]{1,0:T(8,128)(2,1)S(1)}, u32[]{:S(2)}, u32[]{:S(2)}) %collective-permute-start.3) | collective-permute-done | bytes 131104 | tf_op jit(solution)/shard_map/ppermute | solution.py:358
  21.6 2.3 %collective-permute-done.4.refs_2_.g2 = bf16[128,1024]{1,0:T(8,128)(2,1)S(1)} collective-permute-done((bf16[128,1024]{1,0:T(8,128)(2,1)}, bf16[128,1024]{1,0:T(8,128)(2,1)S(1)}, u32[]{:S(2)}, u32[]{:S(2)}) %collective-permute-start.4) | collective-permute-done | bytes 262176 | tf_op jit(solution)/shard_map/ppermute | solution.py:358
  24.0 0.1 collective-permute-start.8
  24.1 1.3 %collective-permute-start.6 = (bf16[2,2,128,256]{3,2,1,0:T(8,128)(2,1)S(1)}, bf16[2,2,128,256]{3,2,1,0:T(8,128)(2,1)S(1)}, u32[]{:S(2)}, u32[]{:S(2)}) collective-permute-start(bf16[2,2,128,256]{3,2,1,0:T(8,128)(2,1)S(1)} %copy-done.11), channel_id=1, source_target_pairs={{0,2},{1,3},{2,0},{3,1},{4,6},{5,7},{6,4},{7,5},{8,10},{9,11},{10,... | collective-permute-start | bytes 786440 | tf_op jit(solution)/shard_map/ppermute | solution.py:358
  25.4 0.1 collective-permute-done.9.w2
  25.5 0.8 collective-permute-start.10
  26.3 1.2 %collective-permute-start.7 = (bf16[256,256]{1,0:T(8,128)(2,1)S(1)}, bf16[256,256]{1,0:T(8,128)(2,1)S(1)}, u32[]{:S(2)}, u32[]{:S(2)}) collective-permute-start(bf16[256,256]{1,0:T(8,128)(2,1)S(1)} %copy-done.12), channel_id=1, source_target_pairs={{0,2},{1,3},{2,0},{3,1},{4,6},{5,7},{6,4},{7,5},{8,10},{9,11},{10,... | collective-permute-start | bytes 393224 | tf_op jit(solution)/shard_map/ppermute | solution.py:358
  27.5 5.7 %collective-permute-done.6.near = bf16[2,2,128,256]{3,2,1,0:T(8,128)(2,1)S(1)} collective-permute-done((bf16[2,2,128,256]{3,2,1,0:T(8,128)(2,1)S(1)}, bf16[2,2,128,256]{3,2,1,0:T(8,128)(2,1)S(1)}, u32[]{:S(2)}, u32[]{:S(2)}) %collective-permute-start.6) | collective-permute-done | bytes 262176 | tf_op jit(solution)/shard_map/ppermute | solution.py:358
  33.3 0.3 shard_map.93
  33.5 2.1 %collective-permute-done.7.refs_1_ = bf16[256,256]{1,0:T(8,128)(2,1)S(1)} collective-permute-done((bf16[256,256]{1,0:T(8,128)(2,1)S(1)}, bf16[256,256]{1,0:T(8,128)(2,1)S(1)}, u32[]{:S(2)}, u32[]{:S(2)}) %collective-permute-start.7) | collective-permute-done | bytes 131104 | tf_op jit(solution)/shard_map/ppermute | solution.py:358
  35.6 1.3 %shard_map.94 = (f32[512,256]{1,0:T(8,128)S(1)}, bf16[512,256]{1,0:T(8,128)(2,1)S(1)}) custom-call(bf16[512,512]{1,0:T(8,128)(2,1)S(1)} %shard_map.92.mine, bf16[512,512]{1,0:T(8,128)(2,1)S(1)} %collective-permute-done.8.other, bf16[256,512]{1,0:T(8,128)(2,1)S(1)} %copy-done.3, bf16[256,512]{1,0:T(8,128)(2,1)S(1)} %collective-permute-done.2.w1, ...), custom_call_target="tpu_custom_call" | custom-call | flops 536870912 | bytes 2097152 | tf_op jit(solution)/shard_map/pallas_call | solution.py:37
  36.9 1.3 %collective-permute-start.11 = (bf16[512,256]{1,0:T(8,128)(2,1)S(1)}, bf16[512,256]{1,0:T(8,128)(2,1)S(1)}, u32[]{:S(2)}, u32[]{:S(2)}) collective-permute-start(bf16[512,256]{1,0:T(8,128)(2,1)S(1)} %get-tuple-element.52), channel_id=1, source_target_pairs={{0,2},{1,3},{2,0},{3,1},{4,6},{5,7},{6,4},{7,5},{8,10},{9,11},{10,... | collective-permute-start | bytes 786440 | tf_op jit(solution)/shard_map/ppermute | solution.py:358
  38.2 0.9 collective-permute-start.22
  39.1 2.0 %collective-permute-start.17 = (bf16[2,2,128,128]{3,2,1,0:T(8,128)(2,1)S(1)}, bf16[2,2,128,128]{3,2,1,0:T(8,128)(2,1)S(1)}, u32[]{:S(2)}, u32[]{:S(2)}) collective-permute-start(bf16[2,2,128,128]{3,2,1,0:T(8,128)(2,1)S(1)} %get-tuple-element.59), channel_id=1, source_target_pairs={{0,8},{1,9},{2,10},{3,11},{4,0},{5,1},{6,2},{7,3},{8,12},{9,13},{1... | collective-permute-start | bytes 393224 | tf_op jit(solution)/shard_map/ppermute | solution.py:358
  41.2 6.0 %collective-permute-done.22.refs_3_ = bf16[256,256]{1,0:T(8,128)(2,1)S(1)} collective-permute-done((bf16[256,256]{1,0:T(8,128)(2,1)S(1)}, bf16[256,256]{1,0:T(8,128)(2,1)S(1)}, u32[]{:S(2)}, u32[]{:S(2)}) %collective-permute-start.22) | collective-permute-done | bytes 131104 | tf_op jit(solution)/shard_map/ppermute | solution.py:358
  47.2 0.2 collective-permute-start.15
  47.4 4.2 %collective-permute-start.16 = (bf16[2,2,128,128]{3,2,1,0:T(8,128)(2,1)S(1)}, bf16[2,2,128,128]{3,2,1,0:T(8,128)(2,1)S(1)}, u32[]{:S(2)}, u32[]{:S(2)}) collective-permute-start(bf16[2,2,128,128]{3,2,1,0:T(8,128)(2,1)S(1)} %get-tuple-element.58), channel_id=1, source_target_pairs={{0,12},{1,13},{2,14},{3,15},{4,8},{5,9},{6,10},{7,11},{8,4},{9,5},... | collective-permute-start | bytes 393224 | tf_op jit(solution)/shard_map/ppermute | solution.py:358
  51.6 0.0 copy-start.9
  51.6 0.0 copy-start.10
  51.6 0.3 shard_map.95
  51.9 0.1 collective-permute-start.12
  52.0 0.1 collective-permute-start.13
  52.1 5.2 %collective-permute-done.23.refs_5_ = bf16[256,256]{1,0:T(8,128)(2,1)S(1)} collective-permute-done((bf16[256,256]{1,0:T(8,128)(2,1)S(1)}, bf16[256,256]{1,0:T(8,128)(2,1)S(1)}, u32[]{:S(2)}, u32[]{:S(2)}) %collective-permute-start.23) | collective-permute-done | bytes 131104 | tf_op jit(solution)/shard_map/ppermute | solution.py:358
  57.3 0.0 collective-permute-start.14
  57.3 6.0 %collective-permute-done.12.refs_1_ = bf16[256,128]{1,0:T(8,128)(2,1)S(1)} collective-permute-done((bf16[256,128]{1,0:T(8,128)(2,1)S(1)}, bf16[256,128]{1,0:T(8,128)(2,1)S(1)}, u32[]{:S(2)}, u32[]{:S(2)}) %collective-permute-start.12) | collective-permute-done | bytes 65568 | tf_op jit(solution)/shard_map/ppermute | solution.py:358
  63.4 2.0 %collective-permute-start.24 = (bf16[2,256,256]{2,1,0:T(8,128)(2,1)S(1)}, bf16[2,256,256]{2,1,0:T(8,128)(2,1)S(1)}, u32[]{:S(2)}, u32[]{:S(2)}) collective-permute-start(bf16[2,256,256]{2,1,0:T(8,128)(2,1)S(1)} %pad_maximum_fusion), channel_id=1, source_target_pairs={{0,4},{1,5},{2,6},{3,7},{4,12},{5,13},{6,14},{7,15},{8,0},{9,1},{1... | collective-permute-start | bytes 786440 | tf_op jit(solution)/shard_map/ppermute | solution.py:358
  65.3 0.0 collective-permute-done.15.refs_5_
  65.3 0.0 collective-permute-done.16.refs_6_
  65.4 1.8 %shard_map.96 = (bf16[256,128]{1,0:T(8,128)(2,1)S(1)}, bf16[256,128]{1,0:T(8,128)(2,1)S(1)}, bf16[256,128]{1,0:T(8,128)(2,1)S(1)}, bf16[256,128]{1,0:T(8,128)(2,1)S(1)}) custom-call(bf16[256,128]{1,0:T(8,128)(2,1)S(1)} %get-tuple-element.53.refs_0_, bf16[256,128]{1,0:T(8,128)(2,1)S(1)} %collective-permute-done.12.refs_1_, ...), custom_call_target="tpu_custom_call" | custom-call | flops 1073741824 | bytes 5242880 | tf_op jit(solution)/shard_map/pallas_call | solution.py:37
  67.2 0.5 collective-permute-start.18
  67.7 2.0 %collective-permute-start.19 = (bf16[256,128]{1,0:T(8,128)(2,1)S(1)}, bf16[256,128]{1,0:T(8,128)(2,1)S(1)}, u32[]{:S(2)}, u32[]{:S(2)}) collective-permute-start(bf16[256,128]{1,0:T(8,128)(2,1)S(1)} %get-tuple-element.62), channel_id=1, source_target_pairs={{0,12},{1,13},{2,14},{3,15},{4,8},{5,9},{6,10},{7,11},{8,4},{9,5},... | collective-permute-start | bytes 196616 | tf_op jit(solution)/shard_map/ppermute | solution.py:358
  69.7 1.4 %collective-permute-start.20 = (bf16[256,128]{1,0:T(8,128)(2,1)S(1)}, bf16[256,128]{1,0:T(8,128)(2,1)S(1)}, u32[]{:S(2)}, u32[]{:S(2)}) collective-permute-start(bf16[256,128]{1,0:T(8,128)(2,1)S(1)} %get-tuple-element.63), channel_id=1, source_target_pairs={{0,8},{1,9},{2,10},{3,11},{4,0},{5,1},{6,2},{7,3},{8,12},{9,13},{1... | collective-permute-start | bytes 196616 | tf_op jit(solution)/shard_map/ppermute | solution.py:358
  71.1 1.6 %collective-permute-done.18.e1 = bf16[256,128]{1,0:T(8,128)(2,1)S(1)} collective-permute-done((bf16[256,128]{1,0:T(8,128)(2,1)S(1)}, bf16[256,128]{1,0:T(8,128)(2,1)S(1)}, u32[]{:S(2)}, u32[]{:S(2)}) %collective-permute-start.18) | collective-permute-done | bytes 65568 | tf_op jit(solution)/shard_map/ppermute | solution.py:358
  72.8 1.2 %collective-permute-done.19.e2 = bf16[256,128]{1,0:T(8,128)(2,1)S(1)} collective-permute-done((bf16[256,128]{1,0:T(8,128)(2,1)S(1)}, bf16[256,128]{1,0:T(8,128)(2,1)S(1)}, u32[]{:S(2)}, u32[]{:S(2)}) %collective-permute-start.19) | collective-permute-done | bytes 65568 | tf_op jit(solution)/shard_map/ppermute | solution.py:358
  73.9 0.6 collective-permute-done.20.e3
  74.5 0.0 collective-permute-done.24.refs_6_
  74.6 0.2 shard_map.98
  74.7 0.1 collective-permute-start.25
  74.8 0.2 shard_map.97.gated
  75.0 0.5 collective-permute-start.21
  75.6 1.5 %collective-permute-done.21.other = bf16[512,256]{1,0:T(8,128)(2,1)S(1)} collective-permute-done((bf16[512,256]{1,0:T(8,128)(2,1)S(1)}, bf16[512,256]{1,0:T(8,128)(2,1)S(1)}, u32[]{:S(2)}, u32[]{:S(2)}) %collective-permute-start.21) | collective-permute-done | bytes 262176 | tf_op jit(solution)/shard_map/ppermute | solution.py:358
  77.1 0.8 shard_map.100
  77.9 1.7 %collective-permute-start.26 = (bf16[128,1024]{1,0:T(8,128)(2,1)S(1)}, bf16[128,1024]{1,0:T(8,128)(2,1)S(1)}, u32[]{:S(2)}, u32[]{:S(2)}) collective-permute-start(bf16[128,1024]{1,0:T(8,128)(2,1)S(1)} %get-tuple-element.72), channel_id=1, source_target_pairs={{0,18},{1,19},{2,16},{3,17},{4,22},{5,23},{6,20},{7,21},{8,26},{9,... | collective-permute-start | bytes 786440 | tf_op jit(solution)/shard_map/ppermute | solution.py:358
  79.6 0.6 collective-permute-start.27
  80.2 0.8 shard_map.99
  81.0 1.3 %collective-permute-start.28 = (bf16[128,1024]{1,0:T(8,128)(2,1)S(1)}, bf16[128,1024]{1,0:T(8,128)(2,1)S(1)}, u32[]{:S(2)}, u32[]{:S(2)}) collective-permute-start(bf16[128,1024]{1,0:T(8,128)(2,1)S(1)} %get-tuple-element.74), channel_id=1, source_target_pairs={{0,16},{1,17},{2,18},{3,19},{4,20},{5,21},{6,22},{7,23},{8,24},{9,... | collective-permute-start | bytes 786440 | tf_op jit(solution)/shard_map/ppermute | solution.py:358
  82.3 5.7 %collective-permute-done.26 = bf16[128,1024]{1,0:T(8,128)(2,1)S(1)} collective-permute-done((bf16[128,1024]{1,0:T(8,128)(2,1)S(1)}, bf16[128,1024]{1,0:T(8,128)(2,1)S(1)}, u32[]{:S(2)}, u32[]{:S(2)}) %collective-permute-start.26) | collective-permute-done | bytes 262176 | tf_op jit(solution)/shard_map/ppermute | solution.py:358
  88.0 4.1 %collective-permute-done.27 = bf16[128,1024]{1,0:T(8,128)(2,1)S(1)} collective-permute-done((bf16[128,1024]{1,0:T(8,128)(2,1)S(1)}, bf16[128,1024]{1,0:T(8,128)(2,1)S(1)}, u32[]{:S(2)}, u32[]{:S(2)}) %collective-permute-start.27) | collective-permute-done | bytes 262176 | tf_op jit(solution)/shard_map/ppermute | solution.py:358
  92.2 0.6 collective-permute-done.28
  92.8 0.8 add_convert_fusion
  (33 shorter events, 0.1 us)
Async XLA Ops:
  0.0 1.0 %copy-start = (bf16[256,1024]{1,0:T(8,128)(2,1)S(1)}, bf16[256,1024]{1,0:T(8,128)(2,1)}, u32[]{:S(2)}) copy-start(bf16[256,1024]{1,0:T(8,128)(2,1)} %param.12) | copy-start | bytes 1572868
  1.1 3.1 %copy-start.2 = (bf16[256,512]{1,0:T(8,128)(2,1)}, bf16[256,512]{1,0:T(8,128)(2,1)S(1)}, u32[]{:S(2)}) copy-start(bf16[256,512]{1,0:T(8,128)(2,1)S(1)} %constant_dynamic-slice_fusion.after.w0) | copy-start | bytes 786436
  1.1 22.9 %copy-start.5 = (bf16[128,1024]{1,0:T(8,128)(2,1)S(1)}, bf16[128,1024]{1,0:T(8,128)(2,1)}, u32[]{:S(2)}) copy-start(bf16[128,1024]{1,0:T(8,128)(2,1)} %refs_0_.1) | copy-start | bytes 786436
  1.1 13.2 %collective-permute-start.2 = (bf16[256,512]{1,0:T(8,128)(2,1)S(1)}, bf16[256,512]{1,0:T(8,128)(2,1)S(1)}, u32[]{:S(2)}, u32[]{:S(2)}) collective-permute-start(bf16[256,512]{1,0:T(8,128)(2,1)S(1)} %constant_dynamic-slice_fusion.after.w0), channel_id=1, source_target_pairs={{0,4},{1,5},{2,6},{3,7},{4,12},{5,13},{6,14},{7,15},{8,0},{9,1},{1... | collective-permute-start | bytes 786440 | tf_op jit(solution)/shard_map/ppermute | solution.py:358
  6.8 26.5 %copy-start.1 = (bf16[2,2,128,1024]{3,2,1,0:T(8,128)(2,1)S(1)}, bf16[2,2,128,1024]{3,2,1,0:T(8,128)(2,1)}, u32[]{:S(2)}) copy-start(bf16[2,2,128,1024]{3,2,1,0:T(8,128)(2,1)} %filt.3) | copy-start | bytes 3145732
  6.8 7.5 %collective-permute-start.1 = (bf16[256,256]{1,0:T(8,128)(2,1)}, bf16[256,256]{1,0:T(8,128)(2,1)S(1)}, u32[]{:S(2)}, u32[]{:S(2)}) collective-permute-start(bf16[256,256]{1,0:T(8,128)(2,1)} %get-tuple-element.41.refs_0_), channel_id=1, source_target_pairs={{0,4},{1,5},{2,6},{3,7},{4,12},{5,13},{6,14},{7,15},{8,0},{9,1},{1... | collective-permute-start | bytes 393224 | tf_op jit(solution)/shard_map/ppermute | solution.py:358
  9.4 9.5 %collective-permute-start = (bf16[128,1024]{1,0:T(8,128)(2,1)}, bf16[128,1024]{1,0:T(8,128)(2,1)S(1)}, u32[]{:S(2)}, u32[]{:S(2)}) collective-permute-start(bf16[128,1024]{1,0:T(8,128)(2,1)} %get-tuple-element.40), channel_id=1, source_target_pairs={{0,2},{1,3},{2,0},{3,1},{4,6},{5,7},{6,4},{7,5},{8,10},{9,11},{10,... | collective-permute-start | bytes 786440 | tf_op jit(solution)/shard_map/ppermute | solution.py:358
  10.9 13.0 %collective-permute-start.4 = (bf16[128,1024]{1,0:T(8,128)(2,1)}, bf16[128,1024]{1,0:T(8,128)(2,1)S(1)}, u32[]{:S(2)}, u32[]{:S(2)}) collective-permute-start(bf16[128,1024]{1,0:T(8,128)(2,1)} %get-tuple-element.44), channel_id=1, source_target_pairs={{0,16},{1,17},{2,18},{3,19},{4,20},{5,21},{6,22},{7,23},{8,24},{9,... | collective-permute-start | bytes 786440 | tf_op jit(solution)/shard_map/ppermute | solution.py:358
  12.4 11.6 %copy-start.11 = (bf16[2,2,128,256]{3,2,1,0:T(8,128)(2,1)S(1)}, bf16[2,2,128,256]{3,2,1,0:T(8,128)(2,1)}, u32[]{:S(2)}) copy-start(bf16[2,2,128,256]{3,2,1,0:T(8,128)(2,1)} %get-tuple-element.46) | copy-start | bytes 786436
  12.4 13.9 %copy-start.12 = (bf16[256,256]{1,0:T(8,128)(2,1)S(1)}, bf16[256,256]{1,0:T(8,128)(2,1)}, u32[]{:S(2)}) copy-start(bf16[256,256]{1,0:T(8,128)(2,1)} %get-tuple-element.49) | copy-start | bytes 393220
  12.4 11.5 %collective-permute-start.5 = (bf16[128,1024]{1,0:T(8,128)(2,1)}, bf16[128,1024]{1,0:T(8,128)(2,1)S(1)}, u32[]{:S(2)}, u32[]{:S(2)}) collective-permute-start(bf16[128,1024]{1,0:T(8,128)(2,1)} %get-tuple-element.45), channel_id=1, source_target_pairs={{0,18},{1,19},{2,16},{3,17},{4,22},{5,23},{6,20},{7,21},{8,26},{9,... | collective-permute-start | bytes 786440 | tf_op jit(solution)/shard_map/ppermute | solution.py:358
  14.3 7.3 %collective-permute-start.3 = (bf16[256,256]{1,0:T(8,128)(2,1)S(1)}, bf16[256,256]{1,0:T(8,128)(2,1)S(1)}, u32[]{:S(2)}, u32[]{:S(2)}) collective-permute-start(bf16[256,256]{1,0:T(8,128)(2,1)S(1)} %collective-permute-done.1.refs_2_), channel_id=1, source_target_pairs={{0,4},{1,5},{2,6},{3,7},{4,12},{5,13},{6,14},{7,15},{8,0},{9,1},{1... | collective-permute-start | bytes 393224 | tf_op jit(solution)/shard_map/ppermute | solution.py:358
  15.2 10.3 %collective-permute-start.9 = (bf16[256,512]{1,0:T(8,128)(2,1)S(1)}, bf16[256,512]{1,0:T(8,128)(2,1)S(1)}, u32[]{:S(2)}, u32[]{:S(2)}) collective-permute-start(bf16[256,512]{1,0:T(8,128)(2,1)S(1)} %collective-permute-done.2.w1), channel_id=1, source_target_pairs={{0,4},{1,5},{2,6},{3,7},{4,12},{5,13},{6,14},{7,15},{8,0},{9,1},{1... | collective-permute-start | bytes 786440 | tf_op jit(solution)/shard_map/ppermute | solution.py:358
  24.0 11.6 %collective-permute-start.8 = (bf16[512,512]{1,0:T(8,128)(2,1)S(1)}, bf16[512,512]{1,0:T(8,128)(2,1)S(1)}, u32[]{:S(2)}, u32[]{:S(2)}) collective-permute-start(bf16[512,512]{1,0:T(8,128)(2,1)S(1)} %shard_map.92.mine), channel_id=1, source_target_pairs={{0,1},{1,0},{2,3},{3,2},{4,5},{5,4},{6,7},{7,6},{8,9},{9,8},{10,11... | collective-permute-start | bytes 1572872 | tf_op jit(solution)/shard_map/ppermute | solution.py:358
  24.1 9.2 %collective-permute-start.6 = (bf16[2,2,128,256]{3,2,1,0:T(8,128)(2,1)S(1)}, bf16[2,2,128,256]{3,2,1,0:T(8,128)(2,1)S(1)}, u32[]{:S(2)}, u32[]{:S(2)}) collective-permute-start(bf16[2,2,128,256]{3,2,1,0:T(8,128)(2,1)S(1)} %copy-done.11), channel_id=1, source_target_pairs={{0,2},{1,3},{2,0},{3,1},{4,6},{5,7},{6,4},{7,5},{8,10},{9,11},{10,... | collective-permute-start | bytes 786440 | tf_op jit(solution)/shard_map/ppermute | solution.py:358
  25.5 10.1 %collective-permute-start.10 = (bf16[256,512]{1,0:T(8,128)(2,1)S(1)}, bf16[256,512]{1,0:T(8,128)(2,1)S(1)}, u32[]{:S(2)}, u32[]{:S(2)}) collective-permute-start(bf16[256,512]{1,0:T(8,128)(2,1)S(1)} %collective-permute-done.9.w2), channel_id=1, source_target_pairs={{0,4},{1,5},{2,6},{3,7},{4,12},{5,13},{6,14},{7,15},{8,0},{9,1},{1... | collective-permute-start | bytes 786440 | tf_op jit(solution)/shard_map/ppermute | solution.py:358
  26.3 9.3 %copy-start.3 = (bf16[256,512]{1,0:T(8,128)(2,1)S(1)}, bf16[256,512]{1,0:T(8,128)(2,1)}, u32[]{:S(2)}) copy-start(bf16[256,512]{1,0:T(8,128)(2,1)} %copy-done.2) | copy-start | bytes 786436
  26.3 9.3 %collective-permute-start.7 = (bf16[256,256]{1,0:T(8,128)(2,1)S(1)}, bf16[256,256]{1,0:T(8,128)(2,1)S(1)}, u32[]{:S(2)}, u32[]{:S(2)}) collective-permute-start(bf16[256,256]{1,0:T(8,128)(2,1)S(1)} %copy-done.12), channel_id=1, source_target_pairs={{0,2},{1,3},{2,0},{3,1},{4,6},{5,7},{6,4},{7,5},{8,10},{9,11},{10,... | collective-permute-start | bytes 393224 | tf_op jit(solution)/shard_map/ppermute | solution.py:358
  35.6 15.9 %copy-start.4 = (bf16[128,1024]{1,0:T(8,128)(2,1)S(1)}, bf16[128,1024]{1,0:T(8,128)(2,1)}, u32[]{:S(2)}) copy-start(bf16[128,1024]{1,0:T(8,128)(2,1)} %g0.2) | copy-start | bytes 786436
  36.9 14.6 %collective-permute-start.11 = (bf16[512,256]{1,0:T(8,128)(2,1)S(1)}, bf16[512,256]{1,0:T(8,128)(2,1)S(1)}, u32[]{:S(2)}, u32[]{:S(2)}) collective-permute-start(bf16[512,256]{1,0:T(8,128)(2,1)S(1)} %get-tuple-element.52), channel_id=1, source_target_pairs={{0,2},{1,3},{2,0},{3,1},{4,6},{5,7},{6,4},{7,5},{8,10},{9,11},{10,... | collective-permute-start | bytes 786440 | tf_op jit(solution)/shard_map/ppermute | solution.py:358
  38.2 8.9 %collective-permute-start.22 = (bf16[256,256]{1,0:T(8,128)(2,1)S(1)}, bf16[256,256]{1,0:T(8,128)(2,1)S(1)}, u32[]{:S(2)}, u32[]{:S(2)}) collective-permute-start(bf16[256,256]{1,0:T(8,128)(2,1)S(1)} %collective-permute-done.7.refs_1_), channel_id=1, source_target_pairs={{0,4},{1,5},{2,6},{3,7},{4,12},{5,13},{6,14},{7,15},{8,0},{9,1},{1... | collective-permute-start | bytes 393224 | tf_op jit(solution)/shard_map/ppermute | solution.py:358
  39.1 12.4 %copy-start.8 = (f32[1024]{0:T(1024)S(1)}, f32[1024]{0:T(1024)}, u32[]{:S(2)}) copy-start(f32[1024]{0:T(1024)} %param.13) | copy-start | bytes 12292
  39.1 12.9 %collective-permute-start.17 = (bf16[2,2,128,128]{3,2,1,0:T(8,128)(2,1)S(1)}, bf16[2,2,128,128]{3,2,1,0:T(8,128)(2,1)S(1)}, u32[]{:S(2)}, u32[]{:S(2)}) collective-permute-start(bf16[2,2,128,128]{3,2,1,0:T(8,128)(2,1)S(1)} %get-tuple-element.59), channel_id=1, source_target_pairs={{0,8},{1,9},{2,10},{3,11},{4,0},{5,1},{6,2},{7,3},{8,12},{9,13},{1... | collective-permute-start | bytes 393224 | tf_op jit(solution)/shard_map/ppermute | solution.py:358
  47.2 10.1 %collective-permute-start.23 = (bf16[256,256]{1,0:T(8,128)(2,1)S(1)}, bf16[256,256]{1,0:T(8,128)(2,1)S(1)}, u32[]{:S(2)}, u32[]{:S(2)}) collective-permute-start(bf16[256,256]{1,0:T(8,128)(2,1)S(1)} %collective-permute-done.22.refs_3_), channel_id=1, source_target_pairs={{0,4},{1,5},{2,6},{3,7},{4,12},{5,13},{6,14},{7,15},{8,0},{9,1},{1... | collective-permute-start | bytes 393224 | tf_op jit(solution)/shard_map/ppermute | solution.py:358
  47.2 18.2 %collective-permute-start.15 = (bf16[2,2,128,128]{3,2,1,0:T(8,128)(2,1)S(1)}, bf16[2,2,128,128]{3,2,1,0:T(8,128)(2,1)S(1)}, u32[]{:S(2)}, u32[]{:S(2)}) collective-permute-start(bf16[2,2,128,128]{3,2,1,0:T(8,128)(2,1)S(1)} %get-tuple-element.57), channel_id=1, source_target_pairs={{0,4},{1,5},{2,6},{3,7},{4,12},{5,13},{6,14},{7,15},{8,0},{9,1},{1... | collective-permute-start | bytes 393224 | tf_op jit(solution)/shard_map/ppermute | solution.py:358
  47.4 18.0 %collective-permute-start.16 = (bf16[2,2,128,128]{3,2,1,0:T(8,128)(2,1)S(1)}, bf16[2,2,128,128]{3,2,1,0:T(8,128)(2,1)S(1)}, u32[]{:S(2)}, u32[]{:S(2)}) collective-permute-start(bf16[2,2,128,128]{3,2,1,0:T(8,128)(2,1)S(1)} %get-tuple-element.58), channel_id=1, source_target_pairs={{0,12},{1,13},{2,14},{3,15},{4,8},{5,9},{6,10},{7,11},{8,4},{9,5},... | collective-permute-start | bytes 393224 | tf_op jit(solution)/shard_map/ppermute | solution.py:358
  51.6 13.8 %copy-start.9 = (bf16[16,256,128]{2,1,0:T(8,128)(2,1)S(1)}, bf16[16,256,128]{2,1,0:T(8,128)(2,1)}, u32[]{:S(2)}) copy-start(bf16[16,256,128]{2,1,0:T(8,128)(2,1)} %constant.16.clone.refs_8_) | copy-start | bytes 3145732
  51.6 13.8 %copy-start.10 = (bf16[16,256,128]{2,1,0:T(8,128)(2,1)S(1)}, bf16[16,256,128]{2,1,0:T(8,128)(2,1)}, u32[]{:S(2)}) copy-start(bf16[16,256,128]{2,1,0:T(8,128)(2,1)} %constant.17.clone.refs_9_) | copy-start | bytes 3145732
  51.9 11.4 %collective-permute-start.12 = (bf16[256,128]{1,0:T(8,128)(2,1)S(1)}, bf16[256,128]{1,0:T(8,128)(2,1)S(1)}, u32[]{:S(2)}, u32[]{:S(2)}) collective-permute-start(bf16[256,128]{1,0:T(8,128)(2,1)S(1)} %get-tuple-element.54), channel_id=1, source_target_pairs={{0,4},{1,5},{2,6},{3,7},{4,12},{5,13},{6,14},{7,15},{8,0},{9,1},{1... | collective-permute-start | bytes 196616 | tf_op jit(solution)/shard_map/ppermute | solution.py:358
  52.0 11.4 %collective-permute-start.13 = (bf16[256,128]{1,0:T(8,128)(2,1)S(1)}, bf16[256,128]{1,0:T(8,128)(2,1)S(1)}, u32[]{:S(2)}, u32[]{:S(2)}) collective-permute-start(bf16[256,128]{1,0:T(8,128)(2,1)S(1)} %get-tuple-element.55), channel_id=1, source_target_pairs={{0,12},{1,13},{2,14},{3,15},{4,8},{5,9},{6,10},{7,11},{8,4},{9,5},... | collective-permute-start | bytes 196616 | tf_op jit(solution)/shard_map/ppermute | solution.py:358
  57.3 6.1 %collective-permute-start.14 = (bf16[256,128]{1,0:T(8,128)(2,1)S(1)}, bf16[256,128]{1,0:T(8,128)(2,1)S(1)}, u32[]{:S(2)}, u32[]{:S(2)}) collective-permute-start(bf16[256,128]{1,0:T(8,128)(2,1)S(1)} %get-tuple-element.56), channel_id=1, source_target_pairs={{0,8},{1,9},{2,10},{3,11},{4,0},{5,1},{6,2},{7,3},{8,12},{9,13},{1... | collective-permute-start | bytes 196616 | tf_op jit(solution)/shard_map/ppermute | solution.py:358
  63.4 11.2 %collective-permute-start.24 = (bf16[2,256,256]{2,1,0:T(8,128)(2,1)S(1)}, bf16[2,256,256]{2,1,0:T(8,128)(2,1)S(1)}, u32[]{:S(2)}, u32[]{:S(2)}) collective-permute-start(bf16[2,256,256]{2,1,0:T(8,128)(2,1)S(1)} %pad_maximum_fusion), channel_id=1, source_target_pairs={{0,4},{1,5},{2,6},{3,7},{4,12},{5,13},{6,14},{7,15},{8,0},{9,1},{1... | collective-permute-start | bytes 786440 | tf_op jit(solution)/shard_map/ppermute | solution.py:358
  65.4 9.2 %copy-start.7 = (bf16[256,256]{1,0:T(8,128)(2,1)S(1)}, bf16[256,256]{1,0:T(8,128)(2,1)}, u32[]{:S(2)}) copy-start(bf16[256,256]{1,0:T(8,128)(2,1)} %get-tuple-element.41.refs_0_) | copy-start | bytes 393220
  67.2 5.6 %collective-permute-start.18 = (bf16[256,128]{1,0:T(8,128)(2,1)S(1)}, bf16[256,128]{1,0:T(8,128)(2,1)S(1)}, u32[]{:S(2)}, u32[]{:S(2)}) collective-permute-start(bf16[256,128]{1,0:T(8,128)(2,1)S(1)} %get-tuple-element.61), channel_id=1, source_target_pairs={{0,4},{1,5},{2,6},{3,7},{4,12},{5,13},{6,14},{7,15},{8,0},{9,1},{1... | collective-permute-start | bytes 196616 | tf_op jit(solution)/shard_map/ppermute | solution.py:358
  67.7 6.2 %collective-permute-start.19 = (bf16[256,128]{1,0:T(8,128)(2,1)S(1)}, bf16[256,128]{1,0:T(8,128)(2,1)S(1)}, u32[]{:S(2)}, u32[]{:S(2)}) collective-permute-start(bf16[256,128]{1,0:T(8,128)(2,1)S(1)} %get-tuple-element.62), channel_id=1, source_target_pairs={{0,12},{1,13},{2,14},{3,15},{4,8},{5,9},{6,10},{7,11},{8,4},{9,5},... | collective-permute-start | bytes 196616 | tf_op jit(solution)/shard_map/ppermute | solution.py:358
  69.7 5.1 %copy-start.6 = (bf16[128,1024]{1,0:T(8,128)(2,1)S(1)}, bf16[128,1024]{1,0:T(8,128)(2,1)}, u32[]{:S(2)}) copy-start(bf16[128,1024]{1,0:T(8,128)(2,1)} %g0.3) | copy-start | bytes 786436
  69.7 4.9 %collective-permute-start.20 = (bf16[256,128]{1,0:T(8,128)(2,1)S(1)}, bf16[256,128]{1,0:T(8,128)(2,1)S(1)}, u32[]{:S(2)}, u32[]{:S(2)}) collective-permute-start(bf16[256,128]{1,0:T(8,128)(2,1)S(1)} %get-tuple-element.63), channel_id=1, source_target_pairs={{0,8},{1,9},{2,10},{3,11},{4,0},{5,1},{6,2},{7,3},{8,12},{9,13},{1... | collective-permute-start | bytes 196616 | tf_op jit(solution)/shard_map/ppermute | solution.py:358
  74.7 2.4 %collective-permute-start.25 = (bf16[4,256,256]{2,1,0:T(8,128)(2,1)S(1)}, bf16[4,256,256]{2,1,0:T(8,128)(2,1)S(1)}, u32[]{:S(2)}, u32[]{:S(2)}) collective-permute-start(bf16[4,256,256]{2,1,0:T(8,128)(2,1)S(1)} %get-tuple-element.70), channel_id=1, source_target_pairs={{0,1},{1,0},{2,3},{3,2},{4,5},{5,4},{6,7},{7,6},{8,9},{9,8},{10,11... | collective-permute-start | bytes 1572872 | tf_op jit(solution)/shard_map/ppermute | solution.py:358
  75.0 2.0 %collective-permute-start.21 = (bf16[512,256]{1,0:T(8,128)(2,1)S(1)}, bf16[512,256]{1,0:T(8,128)(2,1)S(1)}, u32[]{:S(2)}, u32[]{:S(2)}) collective-permute-start(bf16[512,256]{1,0:T(8,128)(2,1)S(1)} %shard_map.97.gated), channel_id=1, source_target_pairs={{0,1},{1,0},{2,3},{3,2},{4,5},{5,4},{6,7},{7,6},{8,9},{9,8},{10,11... | collective-permute-start | bytes 786440 | tf_op jit(solution)/shard_map/ppermute | solution.py:358
  77.9 10.2 %collective-permute-start.26 = (bf16[128,1024]{1,0:T(8,128)(2,1)S(1)}, bf16[128,1024]{1,0:T(8,128)(2,1)S(1)}, u32[]{:S(2)}, u32[]{:S(2)}) collective-permute-start(bf16[128,1024]{1,0:T(8,128)(2,1)S(1)} %get-tuple-element.72), channel_id=1, source_target_pairs={{0,18},{1,19},{2,16},{3,17},{4,22},{5,23},{6,20},{7,21},{8,26},{9,... | collective-permute-start | bytes 786440 | tf_op jit(solution)/shard_map/ppermute | solution.py:358
  79.6 12.6 %collective-permute-start.27 = (bf16[128,1024]{1,0:T(8,128)(2,1)S(1)}, bf16[128,1024]{1,0:T(8,128)(2,1)S(1)}, u32[]{:S(2)}, u32[]{:S(2)}) collective-permute-start(bf16[128,1024]{1,0:T(8,128)(2,1)S(1)} %get-tuple-element.73), channel_id=1, source_target_pairs={{0,2},{1,3},{2,0},{3,1},{4,6},{5,7},{6,4},{7,5},{8,10},{9,11},{10,... | collective-permute-start | bytes 786440 | tf_op jit(solution)/shard_map/ppermute | solution.py:358
  81.0 11.8 %collective-permute-start.28 = (bf16[128,1024]{1,0:T(8,128)(2,1)S(1)}, bf16[128,1024]{1,0:T(8,128)(2,1)S(1)}, u32[]{:S(2)}, u32[]{:S(2)}) collective-permute-start(bf16[128,1024]{1,0:T(8,128)(2,1)S(1)} %get-tuple-element.74), channel_id=1, source_target_pairs={{0,16},{1,17},{2,18},{3,19},{4,20},{5,21},{6,22},{7,23},{8,24},{9,... | collective-permute-start | bytes 786440 | tf_op jit(solution)/shard_map/ppermute | solution.py:358

commit v21 on v18

--- a/solution.py
+++ b/solution.py
@@ -409,13 +409,13 @@
         flops=1 << 29,
         moved=2 << 20,
     )(after(mine, r1, filters[0]), other, own_v, v1, v2, v3)
-    r2 = onward(after(r1, keep))
     drive, *sends = in_vmem(
         drive_kernel,
         [shape((512, 256), F32)] + [block] * 4,
         [pltpu.VMEM((512, 256), BF16), pltpu.VMEM((4, 256, 128), BF16)],
         moved=2 << 20,
     )(keep, to_x(give), gate_k, *received, skip[None, :])
+    r2 = onward(after(r1, drive))
     columns = [sends[0]] + [to_z(sends[r], r) for r in (1, 2, 3)]
     last = onward(after(jnp.stack([q2, r2]), filters[3], *columns[1:]))
     table, table_t = tables()

time: 92.8 us -> 95.4 us (1.028)
  waiting for transfers between devices: 47.3 us -> 51.8 us
  starting transfers between devices: 34.7 us -> 32.8 us
    ppermute x29, waiting for transfers between devices: 47.3 us -> 51.8 us  [permute(): return lax.ppermute(values, AXES, pairs)]
    ppermute x29, starting transfers between devices: 34.7 us -> 32.8 us  [permute(): return lax.ppermute(values, AXES, pairs)]
  transfers between devices with their start and end apart: 29 -> 29, of which waited for: 16 -> 15; matrix products, arithmetic and copies ran while one was open for 0% -> 0% of each run, Pallas kernels for 7% -> 6%
where the time goes in v21:
time: 95.4 us; the launch traced here: 95.2 us
  waiting for transfers between devices  51.8 us (54%)
  starting transfers between devices  32.8 us (34%)
  Pallas kernels  8.35 us (9%)
  local copies, waits for them, and re-layouts  1.11 us (1%)
    ppermute x29, waiting for transfers between devices, permute(): return lax.ppermute(values, AXES, pairs)  51.8 us
    ppermute x29, starting transfers between devices, permute(): return lax.ppermute(values, AXES, pairs)  32.8 us
    pallas_call x9, Pallas kernels, call(): pl.pallas_call(kernel, out_shape=out_shape, in_specs=specs, out_specs=jax...  5.76 us
    pallas_call x1, Pallas kernels, call(): pl.pallas_call(kernel, out_shape=out_shape, in_specs=[pl.BlockSpec(memory...  2.58 us
  transfers between devices with their start and end apart: 29, of which 15 were waited for; matrix products, arithmetic and copies ran while one was open for 0% of the time, Pallas kernels for 6%

profile of v21, /device:TPU:0, one launch (start us, length us, event | category | flops | bytes accessed | tf_op | source)
XLA Modules:
  0.0 95.2 jit_solution(10077519862967053657)
XLA Ops:
  0.0 1.0 %copy-done = bf16[256,1024]{1,0:T(8,128)(2,1)S(1)} copy-done((bf16[256,1024]{1,0:T(8,128)(2,1)S(1)}, bf16[256,1024]{1,0:T(8,128)(2,1)}, u32[]{:S(2)}) %copy-start) | copy-done | bytes 524312
  1.1 0.0 copy-start.2
  1.1 0.0 copy-start.5
  1.1 3.1 %collective-permute-start.2 = (bf16[256,512]{1,0:T(8,128)(2,1)S(1)}, bf16[256,512]{1,0:T(8,128)(2,1)S(1)}, u32[]{:S(2)}, u32[]{:S(2)}) collective-permute-start(bf16[256,512]{1,0:T(8,128)(2,1)S(1)} %constant_dynamic-slice_fusion.after.w0), channel_id=1, source_target_pairs={{0,4},{1,5},{2,6},{3,7},{4,12},{5,13},{6,14},{7,15},{8,0},{9,1},{1... | collective-permute-start | bytes 786440 | tf_op jit(solution)/shard_map/ppermute | solution.py:358
  4.2 2.6 %shard_map.91 = (bf16[128,1024]{1,0:T(8,128)(2,1)}, bf16[128,1024]{1,0:T(8,128)(2,1)}, bf16[128,1024]{1,0:T(8,128)(2,1)}, bf16[256,256]{1,0:T(8,128)(2,1)}, bf16...) custom-call(bf16[128,1024]{1,0:T(8,128)(2,1)} %refs_0_.1, bf16[128,1024]{1,0:T(8,128)(2,1)} %g0.2, ...), custom_call_target="tpu_custom_call" | custom-call | tf_op jit(solution)/shard_map/pallas_call | solution.py:106
  6.8 0.0 copy-start.1
  6.8 2.6 %collective-permute-start.1 = (bf16[256,256]{1,0:T(8,128)(2,1)}, bf16[256,256]{1,0:T(8,128)(2,1)S(1)}, u32[]{:S(2)}, u32[]{:S(2)}) collective-permute-start(bf16[256,256]{1,0:T(8,128)(2,1)} %get-tuple-element.41.refs_0_), channel_id=1, source_target_pairs={{0,4},{1,5},{2,6},{3,7},{4,12},{5,13},{6,14},{7,15},{8,0},{9,1},{1... | collective-permute-start | bytes 393224 | tf_op jit(solution)/shard_map/ppermute | solution.py:358
  9.4 1.5 %collective-permute-start = (bf16[128,1024]{1,0:T(8,128)(2,1)}, bf16[128,1024]{1,0:T(8,128)(2,1)S(1)}, u32[]{:S(2)}, u32[]{:S(2)}) collective-permute-start(bf16[128,1024]{1,0:T(8,128)(2,1)} %get-tuple-element.40), channel_id=1, source_target_pairs={{0,2},{1,3},{2,0},{3,1},{4,6},{5,7},{6,4},{7,5},{8,10},{9,11},{10,... | collective-permute-start | bytes 786440 | tf_op jit(solution)/shard_map/ppermute | solution.py:358
  10.9 1.5 %collective-permute-start.4 = (bf16[128,1024]{1,0:T(8,128)(2,1)}, bf16[128,1024]{1,0:T(8,128)(2,1)S(1)}, u32[]{:S(2)}, u32[]{:S(2)}) collective-permute-start(bf16[128,1024]{1,0:T(8,128)(2,1)} %get-tuple-element.44), channel_id=1, source_target_pairs={{0,16},{1,17},{2,18},{3,19},{4,20},{5,21},{6,22},{7,23},{8,24},{9,... | collective-permute-start | bytes 786440 | tf_op jit(solution)/shard_map/ppermute | solution.py:358
  12.4 0.5 collective-permute-start.5
  12.9 1.4 %collective-permute-done.1.refs_2_ = bf16[256,256]{1,0:T(8,128)(2,1)S(1)} collective-permute-done((bf16[256,256]{1,0:T(8,128)(2,1)}, bf16[256,256]{1,0:T(8,128)(2,1)S(1)}, u32[]{:S(2)}, u32[]{:S(2)}) %collective-permute-start.1) | collective-permute-done | bytes 131104 | tf_op jit(solution)/shard_map/ppermute | solution.py:358
  14.3 0.9 collective-permute-start.3
  15.2 3.3 %collective-permute-start.7 = (bf16[256,512]{1,0:T(8,128)(2,1)S(1)}, bf16[256,512]{1,0:T(8,128)(2,1)S(1)}, u32[]{:S(2)}, u32[]{:S(2)}) collective-permute-start(bf16[256,512]{1,0:T(8,128)(2,1)S(1)} %collective-permute-done.2.w1), channel_id=1, source_target_pairs={{0,4},{1,5},{2,6},{3,7},{4,12},{5,13},{6,14},{7,15},{8,0},{9,1},{1... | collective-permute-start | bytes 786440 | tf_op jit(solution)/shard_map/ppermute | solution.py:358
  18.5 0.4 collective-permute-done.refs_1_.g1
  18.9 2.8 %collective-permute-done.3.refs_4_ = bf16[256,256]{1,0:T(8,128)(2,1)S(1)} collective-permute-done((bf16[256,256]{1,0:T(8,128)(2,1)S(1)}, bf16[256,256]{1,0:T(8,128)(2,1)S(1)}, u32[]{:S(2)}, u32[]{:S(2)}) %collective-permute-start.3) | collective-permute-done | bytes 131104 | tf_op jit(solution)/shard_map/ppermute | solution.py:358
  21.6 2.3 %collective-permute-done.4.refs_2_.g2 = bf16[128,1024]{1,0:T(8,128)(2,1)S(1)} collective-permute-done((bf16[128,1024]{1,0:T(8,128)(2,1)}, bf16[128,1024]{1,0:T(8,128)(2,1)S(1)}, u32[]{:S(2)}, u32[]{:S(2)}) %collective-permute-start.4) | collective-permute-done | bytes 262176 | tf_op jit(solution)/shard_map/ppermute | solution.py:358
  24.0 0.1 collective-permute-start.10
  24.1 1.3 %collective-permute-start.6 = (bf16[256,256]{1,0:T(8,128)(2,1)S(1)}, bf16[256,256]{1,0:T(8,128)(2,1)S(1)}, u32[]{:S(2)}, u32[]{:S(2)}) collective-permute-start(bf16[256,256]{1,0:T(8,128)(2,1)S(1)} %copy-done.12), channel_id=1, source_target_pairs={{0,2},{1,3},{2,0},{3,1},{4,6},{5,7},{6,4},{7,5},{8,10},{9,11},{10,... | collective-permute-start | bytes 393224 | tf_op jit(solution)/shard_map/ppermute | solution.py:358
  25.4 0.8 collective-permute-start.9
  26.2 0.0 collective-permute-done.7.w2
  26.2 0.9 collective-permute-start.11
  27.1 3.4 %collective-permute-done.6.refs_1_ = bf16[256,256]{1,0:T(8,128)(2,1)S(1)} collective-permute-done((bf16[256,256]{1,0:T(8,128)(2,1)S(1)}, bf16[256,256]{1,0:T(8,128)(2,1)S(1)}, u32[]{:S(2)}, u32[]{:S(2)}) %collective-permute-start.6) | collective-permute-done | bytes 131104 | tf_op jit(solution)/shard_map/ppermute | solution.py:358
  30.4 0.9 collective-permute-start.8
  31.4 4.3 %collective-permute-done.9.near = bf16[2,2,128,256]{3,2,1,0:T(8,128)(2,1)S(1)} collective-permute-done((bf16[2,2,128,256]{3,2,1,0:T(8,128)(2,1)S(1)}, bf16[2,2,128,256]{3,2,1,0:T(8,128)(2,1)S(1)}, u32[]{:S(2)}, u32[]{:S(2)}) %collective-permute-start.9) | collective-permute-done | bytes 262176 | tf_op jit(solution)/shard_map/ppermute | solution.py:358
  35.6 0.3 shard_map.93
  35.9 2.1 %collective-permute-done.8.refs_3_ = bf16[256,256]{1,0:T(8,128)(2,1)S(1)} collective-permute-done((bf16[256,256]{1,0:T(8,128)(2,1)S(1)}, bf16[256,256]{1,0:T(8,128)(2,1)S(1)}, u32[]{:S(2)}, u32[]{:S(2)}) %collective-permute-start.8) | collective-permute-done | bytes 131104 | tf_op jit(solution)/shard_map/ppermute | solution.py:358
  38.0 0.0 collective-permute-done.11.w3
  38.0 0.0 collective-permute-done.10.other
  38.0 1.3 %shard_map.94 = (f32[512,256]{1,0:T(8,128)S(1)}, bf16[512,256]{1,0:T(8,128)(2,1)S(1)}) custom-call(bf16[512,512]{1,0:T(8,128)(2,1)S(1)} %shard_map.92.mine, bf16[512,512]{1,0:T(8,128)(2,1)S(1)} %collective-permute-done.10.other, bf16[256,512]{1,0:T(8,128)(2,1)S(1)} %copy-done.3, bf16[256,512]{1,0:T(8,128)(2,1)S(1)} %collective-permute-done.2.w1, ...), custom_call_target="tpu_custom_call" | custom-call | flops 536870912 | bytes 2097152 | tf_op jit(solution)/shard_map/pallas_call | solution.py:37
  39.3 0.0 copy-start.8
  39.3 1.3 %collective-permute-start.12 = (bf16[512,256]{1,0:T(8,128)(2,1)S(1)}, bf16[512,256]{1,0:T(8,128)(2,1)S(1)}, u32[]{:S(2)}, u32[]{:S(2)}) collective-permute-start(bf16[512,256]{1,0:T(8,128)(2,1)S(1)} %get-tuple-element.53), channel_id=1, source_target_pairs={{0,2},{1,3},{2,0},{3,1},{4,6},{5,7},{6,4},{7,5},{8,10},{9,11},{10,... | collective-permute-start | bytes 786440 | tf_op jit(solution)/shard_map/ppermute | solution.py:358
  40.6 0.0 collective-permute-start.18
  40.6 6.0 %collective-permute-done.12.taken = bf16[512,256]{1,0:T(8,128)(2,1)S(1)} collective-permute-done((bf16[512,256]{1,0:T(8,128)(2,1)S(1)}, bf16[512,256]{1,0:T(8,128)(2,1)S(1)}, u32[]{:S(2)}, u32[]{:S(2)}) %collective-permute-start.12) | collective-permute-done | bytes 262176 | tf_op jit(solution)/shard_map/ppermute | solution.py:358
  46.6 0.3 shard_map.95
  47.0 0.1 collective-permute-start.23
  47.0 1.1 %collective-permute-start.16 = (bf16[2,2,128,128]{3,2,1,0:T(8,128)(2,1)S(1)}, bf16[2,2,128,128]{3,2,1,0:T(8,128)(2,1)S(1)}, u32[]{:S(2)}, u32[]{:S(2)}) collective-permute-start(bf16[2,2,128,128]{3,2,1,0:T(8,128)(2,1)S(1)} %get-tuple-element.58), channel_id=1, source_target_pairs={{0,4},{1,5},{2,6},{3,7},{4,12},{5,13},{6,14},{7,15},{8,0},{9,1},{1... | collective-permute-start | bytes 393224 | tf_op jit(solution)/shard_map/ppermute | solution.py:358
  48.1 3.3 %collective-permute-start.17 = (bf16[2,2,128,128]{3,2,1,0:T(8,128)(2,1)S(1)}, bf16[2,2,128,128]{3,2,1,0:T(8,128)(2,1)S(1)}, u32[]{:S(2)}, u32[]{:S(2)}) collective-permute-start(bf16[2,2,128,128]{3,2,1,0:T(8,128)(2,1)S(1)} %get-tuple-element.59), channel_id=1, source_target_pairs={{0,12},{1,13},{2,14},{3,15},{4,8},{5,9},{6,10},{7,11},{8,4},{9,5},... | collective-permute-start | bytes 393224 | tf_op jit(solution)/shard_map/ppermute | solution.py:358
  51.4 0.0 collective-permute-start.13
  51.4 0.5 collective-permute-start.14
  51.9 3.8 %collective-permute-done.23.refs_5_ = bf16[256,256]{1,0:T(8,128)(2,1)S(1)} collective-permute-done((bf16[256,256]{1,0:T(8,128)(2,1)S(1)}, bf16[256,256]{1,0:T(8,128)(2,1)S(1)}, u32[]{:S(2)}, u32[]{:S(2)}) %collective-permute-start.23) | collective-permute-done | bytes 131104 | tf_op jit(solution)/shard_map/ppermute | solution.py:358
  55.8 8.9 %collective-permute-done.13.refs_1_ = bf16[256,128]{1,0:T(8,128)(2,1)S(1)} collective-permute-done((bf16[256,128]{1,0:T(8,128)(2,1)S(1)}, bf16[256,128]{1,0:T(8,128)(2,1)S(1)}, u32[]{:S(2)}, u32[]{:S(2)}) %collective-permute-start.13) | collective-permute-done | bytes 65568 | tf_op jit(solution)/shard_map/ppermute | solution.py:358
  64.7 0.0 collective-permute-done.14.refs_2_
  64.7 1.9 %collective-permute-start.24 = (bf16[2,256,256]{2,1,0:T(8,128)(2,1)S(1)}, bf16[2,256,256]{2,1,0:T(8,128)(2,1)S(1)}, u32[]{:S(2)}, u32[]{:S(2)}) collective-permute-start(bf16[2,256,256]{2,1,0:T(8,128)(2,1)S(1)} %pad_maximum_fusion), channel_id=1, source_target_pairs={{0,4},{1,5},{2,6},{3,7},{4,12},{5,13},{6,14},{7,15},{8,0},{9,1},{1... | collective-permute-start | bytes 786440 | tf_op jit(solution)/shard_map/ppermute | solution.py:358
  66.7 1.8 %shard_map.96 = (bf16[256,128]{1,0:T(8,128)(2,1)S(1)}, bf16[256,128]{1,0:T(8,128)(2,1)S(1)}, bf16[256,128]{1,0:T(8,128)(2,1)S(1)}, bf16[256,128]{1,0:T(8,128)(2,1)S(1)}) custom-call(bf16[256,128]{1,0:T(8,128)(2,1)S(1)} %get-tuple-element.54.refs_0_, bf16[256,128]{1,0:T(8,128)(2,1)S(1)} %collective-permute-done.13.refs_1_, ...), custom_call_target="tpu_custom_call" | custom-call | flops 1073741824 | bytes 5242880 | tf_op jit(solution)/shard_map/pallas_call | solution.py:37
  68.5 0.1 collective-permute-start.19
  68.6 2.4 %collective-permute-start.20 = (bf16[256,128]{1,0:T(8,128)(2,1)S(1)}, bf16[256,128]{1,0:T(8,128)(2,1)S(1)}, u32[]{:S(2)}, u32[]{:S(2)}) collective-permute-start(bf16[256,128]{1,0:T(8,128)(2,1)S(1)} %get-tuple-element.63), channel_id=1, source_target_pairs={{0,12},{1,13},{2,14},{3,15},{4,8},{5,9},{6,10},{7,11},{8,4},{9,5},... | collective-permute-start | bytes 196616 | tf_op jit(solution)/shard_map/ppermute | solution.py:358
  71.1 0.5 collective-permute-start.21
  71.5 3.8 %collective-permute-done.19.e1 = bf16[256,128]{1,0:T(8,128)(2,1)S(1)} collective-permute-done((bf16[256,128]{1,0:T(8,128)(2,1)S(1)}, bf16[256,128]{1,0:T(8,128)(2,1)S(1)}, u32[]{:S(2)}, u32[]{:S(2)}) %collective-permute-start.19) | collective-permute-done | bytes 65568 | tf_op jit(solution)/shard_map/ppermute | solution.py:358
  75.3 0.0 collective-permute-done.20.e2
  75.3 0.6 collective-permute-done.21.e3
  76.0 0.0 collective-permute-done.24.refs_6_
  76.0 0.2 shard_map.98
  76.1 0.1 collective-permute-start.25
  76.2 0.2 shard_map.97.gated
  76.4 0.5 collective-permute-start.22
  77.0 1.5 %collective-permute-done.22.other = bf16[512,256]{1,0:T(8,128)(2,1)S(1)} collective-permute-done((bf16[512,256]{1,0:T(8,128)(2,1)S(1)}, bf16[512,256]{1,0:T(8,128)(2,1)S(1)}, u32[]{:S(2)}, u32[]{:S(2)}) %collective-permute-start.22) | collective-permute-done | bytes 262176 | tf_op jit(solution)/shard_map/ppermute | solution.py:358
  78.5 0.8 shard_map.100
  79.3 1.5 %collective-permute-start.26 = (bf16[128,1024]{1,0:T(8,128)(2,1)S(1)}, bf16[128,1024]{1,0:T(8,128)(2,1)S(1)}, u32[]{:S(2)}, u32[]{:S(2)}) collective-permute-start(bf16[128,1024]{1,0:T(8,128)(2,1)S(1)} %get-tuple-element.72), channel_id=1, source_target_pairs={{0,18},{1,19},{2,16},{3,17},{4,22},{5,23},{6,20},{7,21},{8,26},{9,... | collective-permute-start | bytes 786440 | tf_op jit(solution)/shard_map/ppermute | solution.py:358
  80.8 1.5 %collective-permute-start.27 = (bf16[128,1024]{1,0:T(8,128)(2,1)S(1)}, bf16[128,1024]{1,0:T(8,128)(2,1)S(1)}, u32[]{:S(2)}, u32[]{:S(2)}) collective-permute-start(bf16[128,1024]{1,0:T(8,128)(2,1)S(1)} %get-tuple-element.73), channel_id=1, source_target_pairs={{0,2},{1,3},{2,0},{3,1},{4,6},{5,7},{6,4},{7,5},{8,10},{9,11},{10,... | collective-permute-start | bytes 786440 | tf_op jit(solution)/shard_map/ppermute | solution.py:358
  82.4 0.8 shard_map.99
  83.2 0.6 collective-permute-start.28
  83.7 5.7 %collective-permute-done.26 = bf16[128,1024]{1,0:T(8,128)(2,1)S(1)} collective-permute-done((bf16[128,1024]{1,0:T(8,128)(2,1)S(1)}, bf16[128,1024]{1,0:T(8,128)(2,1)S(1)}, u32[]{:S(2)}, u32[]{:S(2)}) %collective-permute-start.26) | collective-permute-done | bytes 262176 | tf_op jit(solution)/shard_map/ppermute | solution.py:358
  89.5 4.9 %collective-permute-done.27 = bf16[128,1024]{1,0:T(8,128)(2,1)S(1)} collective-permute-done((bf16[128,1024]{1,0:T(8,128)(2,1)S(1)}, bf16[128,1024]{1,0:T(8,128)(2,1)S(1)}, u32[]{:S(2)}, u32[]{:S(2)}) %collective-permute-start.27) | collective-permute-done | bytes 262176 | tf_op jit(solution)/shard_map/ppermute | solution.py:358
  94.4 0.8 add_convert_fusion
  (33 shorter events, 0.1 us)
Async XLA Ops:
  0.0 1.0 %copy-start = (bf16[256,1024]{1,0:T(8,128)(2,1)S(1)}, bf16[256,1024]{1,0:T(8,128)(2,1)}, u32[]{:S(2)}) copy-start(bf16[256,1024]{1,0:T(8,128)(2,1)} %param.12) | copy-start | bytes 1572868
  1.1 3.1 %copy-start.2 = (bf16[256,512]{1,0:T(8,128)(2,1)}, bf16[256,512]{1,0:T(8,128)(2,1)S(1)}, u32[]{:S(2)}) copy-start(bf16[256,512]{1,0:T(8,128)(2,1)S(1)} %constant_dynamic-slice_fusion.after.w0) | copy-start | bytes 786436
  1.1 22.9 %copy-start.5 = (bf16[128,1024]{1,0:T(8,128)(2,1)S(1)}, bf16[128,1024]{1,0:T(8,128)(2,1)}, u32[]{:S(2)}) copy-start(bf16[128,1024]{1,0:T(8,128)(2,1)} %refs_0_.1) | copy-start | bytes 786436
  1.1 13.2 %collective-permute-start.2 = (bf16[256,512]{1,0:T(8,128)(2,1)S(1)}, bf16[256,512]{1,0:T(8,128)(2,1)S(1)}, u32[]{:S(2)}, u32[]{:S(2)}) collective-permute-start(bf16[256,512]{1,0:T(8,128)(2,1)S(1)} %constant_dynamic-slice_fusion.after.w0), channel_id=1, source_target_pairs={{0,4},{1,5},{2,6},{3,7},{4,12},{5,13},{6,14},{7,15},{8,0},{9,1},{1... | collective-permute-start | bytes 786440 | tf_op jit(solution)/shard_map/ppermute | solution.py:358
  6.8 28.8 %copy-start.1 = (bf16[2,2,128,1024]{3,2,1,0:T(8,128)(2,1)S(1)}, bf16[2,2,128,1024]{3,2,1,0:T(8,128)(2,1)}, u32[]{:S(2)}) copy-start(bf16[2,2,128,1024]{3,2,1,0:T(8,128)(2,1)} %filt.3) | copy-start | bytes 3145732
  6.8 7.5 %collective-permute-start.1 = (bf16[256,256]{1,0:T(8,128)(2,1)}, bf16[256,256]{1,0:T(8,128)(2,1)S(1)}, u32[]{:S(2)}, u32[]{:S(2)}) collective-permute-start(bf16[256,256]{1,0:T(8,128)(2,1)} %get-tuple-element.41.refs_0_), channel_id=1, source_target_pairs={{0,4},{1,5},{2,6},{3,7},{4,12},{5,13},{6,14},{7,15},{8,0},{9,1},{1... | collective-permute-start | bytes 393224 | tf_op jit(solution)/shard_map/ppermute | solution.py:358
  9.4 9.5 %collective-permute-start = (bf16[128,1024]{1,0:T(8,128)(2,1)}, bf16[128,1024]{1,0:T(8,128)(2,1)S(1)}, u32[]{:S(2)}, u32[]{:S(2)}) collective-permute-start(bf16[128,1024]{1,0:T(8,128)(2,1)} %get-tuple-element.40), channel_id=1, source_target_pairs={{0,2},{1,3},{2,0},{3,1},{4,6},{5,7},{6,4},{7,5},{8,10},{9,11},{10,... | collective-permute-start | bytes 786440 | tf_op jit(solution)/shard_map/ppermute | solution.py:358
  10.9 13.0 %collective-permute-start.4 = (bf16[128,1024]{1,0:T(8,128)(2,1)}, bf16[128,1024]{1,0:T(8,128)(2,1)S(1)}, u32[]{:S(2)}, u32[]{:S(2)}) collective-permute-start(bf16[128,1024]{1,0:T(8,128)(2,1)} %get-tuple-element.44), channel_id=1, source_target_pairs={{0,16},{1,17},{2,18},{3,19},{4,20},{5,21},{6,22},{7,23},{8,24},{9,... | collective-permute-start | bytes 786440 | tf_op jit(solution)/shard_map/ppermute | solution.py:358
  12.4 11.6 %copy-start.12 = (bf16[256,256]{1,0:T(8,128)(2,1)S(1)}, bf16[256,256]{1,0:T(8,128)(2,1)}, u32[]{:S(2)}) copy-start(bf16[256,256]{1,0:T(8,128)(2,1)} %get-tuple-element.47) | copy-start | bytes 393220
  12.4 13.0 %copy-start.11 = (bf16[2,2,128,256]{3,2,1,0:T(8,128)(2,1)S(1)}, bf16[2,2,128,256]{3,2,1,0:T(8,128)(2,1)}, u32[]{:S(2)}) copy-start(bf16[2,2,128,256]{3,2,1,0:T(8,128)(2,1)} %get-tuple-element.49) | copy-start | bytes 786436
  12.4 11.5 %collective-permute-start.5 = (bf16[128,1024]{1,0:T(8,128)(2,1)}, bf16[128,1024]{1,0:T(8,128)(2,1)S(1)}, u32[]{:S(2)}, u32[]{:S(2)}) collective-permute-start(bf16[128,1024]{1,0:T(8,128)(2,1)} %get-tuple-element.45), channel_id=1, source_target_pairs={{0,18},{1,19},{2,16},{3,17},{4,22},{5,23},{6,20},{7,21},{8,26},{9,... | collective-permute-start | bytes 786440 | tf_op jit(solution)/shard_map/ppermute | solution.py:358
  14.3 7.3 %collective-permute-start.3 = (bf16[256,256]{1,0:T(8,128)(2,1)S(1)}, bf16[256,256]{1,0:T(8,128)(2,1)S(1)}, u32[]{:S(2)}, u32[]{:S(2)}) collective-permute-start(bf16[256,256]{1,0:T(8,128)(2,1)S(1)} %collective-permute-done.1.refs_2_), channel_id=1, source_target_pairs={{0,4},{1,5},{2,6},{3,7},{4,12},{5,13},{6,14},{7,15},{8,0},{9,1},{1... | collective-permute-start | bytes 393224 | tf_op jit(solution)/shard_map/ppermute | solution.py:358
  15.2 10.9 %collective-permute-start.7 = (bf16[256,512]{1,0:T(8,128)(2,1)S(1)}, bf16[256,512]{1,0:T(8,128)(2,1)S(1)}, u32[]{:S(2)}, u32[]{:S(2)}) collective-permute-start(bf16[256,512]{1,0:T(8,128)(2,1)S(1)} %collective-permute-done.2.w1), channel_id=1, source_target_pairs={{0,4},{1,5},{2,6},{3,7},{4,12},{5,13},{6,14},{7,15},{8,0},{9,1},{1... | collective-permute-start | bytes 786440 | tf_op jit(solution)/shard_map/ppermute | solution.py:358
  24.0 14.0 %collective-permute-start.10 = (bf16[512,512]{1,0:T(8,128)(2,1)S(1)}, bf16[512,512]{1,0:T(8,128)(2,1)S(1)}, u32[]{:S(2)}, u32[]{:S(2)}) collective-permute-start(bf16[512,512]{1,0:T(8,128)(2,1)S(1)} %shard_map.92.mine), channel_id=1, source_target_pairs={{0,1},{1,0},{2,3},{3,2},{4,5},{5,4},{6,7},{7,6},{8,9},{9,8},{10,11... | collective-permute-start | bytes 1572872 | tf_op jit(solution)/shard_map/ppermute | solution.py:358
  24.1 6.4 %collective-permute-start.6 = (bf16[256,256]{1,0:T(8,128)(2,1)S(1)}, bf16[256,256]{1,0:T(8,128)(2,1)S(1)}, u32[]{:S(2)}, u32[]{:S(2)}) collective-permute-start(bf16[256,256]{1,0:T(8,128)(2,1)S(1)} %copy-done.12), channel_id=1, source_target_pairs={{0,2},{1,3},{2,0},{3,1},{4,6},{5,7},{6,4},{7,5},{8,10},{9,11},{10,... | collective-permute-start | bytes 393224 | tf_op jit(solution)/shard_map/ppermute | solution.py:358
  25.4 12.6 %copy-start.3 = (bf16[256,512]{1,0:T(8,128)(2,1)S(1)}, bf16[256,512]{1,0:T(8,128)(2,1)}, u32[]{:S(2)}) copy-start(bf16[256,512]{1,0:T(8,128)(2,1)} %copy-done.2) | copy-start | bytes 786436
  25.4 10.2 %collective-permute-start.9 = (bf16[2,2,128,256]{3,2,1,0:T(8,128)(2,1)S(1)}, bf16[2,2,128,256]{3,2,1,0:T(8,128)(2,1)S(1)}, u32[]{:S(2)}, u32[]{:S(2)}) collective-permute-start(bf16[2,2,128,256]{3,2,1,0:T(8,128)(2,1)S(1)} %copy-done.11), channel_id=1, source_target_pairs={{0,2},{1,3},{2,0},{3,1},{4,6},{5,7},{6,4},{7,5},{8,10},{9,11},{10,... | collective-permute-start | bytes 786440 | tf_op jit(solution)/shard_map/ppermute | solution.py:358
  26.2 11.8 %collective-permute-start.11 = (bf16[256,512]{1,0:T(8,128)(2,1)S(1)}, bf16[256,512]{1,0:T(8,128)(2,1)S(1)}, u32[]{:S(2)}, u32[]{:S(2)}) collective-permute-start(bf16[256,512]{1,0:T(8,128)(2,1)S(1)} %collective-permute-done.7.w2), channel_id=1, source_target_pairs={{0,4},{1,5},{2,6},{3,7},{4,12},{5,13},{6,14},{7,15},{8,0},{9,1},{1... | collective-permute-start | bytes 786440 | tf_op jit(solution)/shard_map/ppermute | solution.py:358
  30.4 7.5 %collective-permute-start.8 = (bf16[256,256]{1,0:T(8,128)(2,1)S(1)}, bf16[256,256]{1,0:T(8,128)(2,1)S(1)}, u32[]{:S(2)}, u32[]{:S(2)}) collective-permute-start(bf16[256,256]{1,0:T(8,128)(2,1)S(1)} %collective-permute-done.6.refs_1_), channel_id=1, source_target_pairs={{0,4},{1,5},{2,6},{3,7},{4,12},{5,13},{6,14},{7,15},{8,0},{9,1},{1... | collective-permute-start | bytes 393224 | tf_op jit(solution)/shard_map/ppermute | solution.py:358
  38.0 8.6 %copy-start.4 = (bf16[128,1024]{1,0:T(8,128)(2,1)S(1)}, bf16[128,1024]{1,0:T(8,128)(2,1)}, u32[]{:S(2)}) copy-start(bf16[128,1024]{1,0:T(8,128)(2,1)} %g0.2) | copy-start | bytes 786436
  39.3 7.3 %copy-start.8 = (f32[1024]{0:T(1024)S(1)}, f32[1024]{0:T(1024)}, u32[]{:S(2)}) copy-start(f32[1024]{0:T(1024)} %param.13) | copy-start | bytes 12292
  39.3 7.3 %collective-permute-start.12 = (bf16[512,256]{1,0:T(8,128)(2,1)S(1)}, bf16[512,256]{1,0:T(8,128)(2,1)S(1)}, u32[]{:S(2)}, u32[]{:S(2)}) collective-permute-start(bf16[512,256]{1,0:T(8,128)(2,1)S(1)} %get-tuple-element.53), channel_id=1, source_target_pairs={{0,2},{1,3},{2,0},{3,1},{4,6},{5,7},{6,4},{7,5},{8,10},{9,11},{10,... | collective-permute-start | bytes 786440 | tf_op jit(solution)/shard_map/ppermute | solution.py:358
  40.6 10.8 %collective-permute-start.18 = (bf16[2,2,128,128]{3,2,1,0:T(8,128)(2,1)S(1)}, bf16[2,2,128,128]{3,2,1,0:T(8,128)(2,1)S(1)}, u32[]{:S(2)}, u32[]{:S(2)}) collective-permute-start(bf16[2,2,128,128]{3,2,1,0:T(8,128)(2,1)S(1)} %get-tuple-element.60), channel_id=1, source_target_pairs={{0,8},{1,9},{2,10},{3,11},{4,0},{5,1},{6,2},{7,3},{8,12},{9,13},{1... | collective-permute-start | bytes 393224 | tf_op jit(solution)/shard_map/ppermute | solution.py:358
  46.6 20.1 %copy-start.9 = (bf16[16,256,128]{2,1,0:T(8,128)(2,1)S(1)}, bf16[16,256,128]{2,1,0:T(8,128)(2,1)}, u32[]{:S(2)}) copy-start(bf16[16,256,128]{2,1,0:T(8,128)(2,1)} %constant.17.clone.refs_9_) | copy-start | bytes 3145732
  46.6 20.1 %copy-start.10 = (bf16[16,256,128]{2,1,0:T(8,128)(2,1)S(1)}, bf16[16,256,128]{2,1,0:T(8,128)(2,1)}, u32[]{:S(2)}) copy-start(bf16[16,256,128]{2,1,0:T(8,128)(2,1)} %constant.16.clone.refs_8_) | copy-start | bytes 3145732
  47.0 8.8 %collective-permute-start.23 = (bf16[256,256]{1,0:T(8,128)(2,1)S(1)}, bf16[256,256]{1,0:T(8,128)(2,1)S(1)}, u32[]{:S(2)}, u32[]{:S(2)}) collective-permute-start(bf16[256,256]{1,0:T(8,128)(2,1)S(1)} %collective-permute-done.8.refs_3_), channel_id=1, source_target_pairs={{0,4},{1,5},{2,6},{3,7},{4,12},{5,13},{6,14},{7,15},{8,0},{9,1},{1... | collective-permute-start | bytes 393224 | tf_op jit(solution)/shard_map/ppermute | solution.py:358
  47.0 19.7 %collective-permute-start.16 = (bf16[2,2,128,128]{3,2,1,0:T(8,128)(2,1)S(1)}, bf16[2,2,128,128]{3,2,1,0:T(8,128)(2,1)S(1)}, u32[]{:S(2)}, u32[]{:S(2)}) collective-permute-start(bf16[2,2,128,128]{3,2,1,0:T(8,128)(2,1)S(1)} %get-tuple-element.58), channel_id=1, source_target_pairs={{0,4},{1,5},{2,6},{3,7},{4,12},{5,13},{6,14},{7,15},{8,0},{9,1},{1... | collective-permute-start | bytes 393224 | tf_op jit(solution)/shard_map/ppermute | solution.py:358
  48.1 18.6 %collective-permute-start.17 = (bf16[2,2,128,128]{3,2,1,0:T(8,128)(2,1)S(1)}, bf16[2,2,128,128]{3,2,1,0:T(8,128)(2,1)S(1)}, u32[]{:S(2)}, u32[]{:S(2)}) collective-permute-start(bf16[2,2,128,128]{3,2,1,0:T(8,128)(2,1)S(1)} %get-tuple-element.59), channel_id=1, source_target_pairs={{0,12},{1,13},{2,14},{3,15},{4,8},{5,9},{6,10},{7,11},{8,4},{9,5},... | collective-permute-start | bytes 393224 | tf_op jit(solution)/shard_map/ppermute | solution.py:358
  51.4 13.3 %collective-permute-start.13 = (bf16[256,128]{1,0:T(8,128)(2,1)S(1)}, bf16[256,128]{1,0:T(8,128)(2,1)S(1)}, u32[]{:S(2)}, u32[]{:S(2)}) collective-permute-start(bf16[256,128]{1,0:T(8,128)(2,1)S(1)} %get-tuple-element.55), channel_id=1, source_target_pairs={{0,4},{1,5},{2,6},{3,7},{4,12},{5,13},{6,14},{7,15},{8,0},{9,1},{1... | collective-permute-start | bytes 196616 | tf_op jit(solution)/shard_map/ppermute | solution.py:358
  51.4 13.3 %collective-permute-start.14 = (bf16[256,128]{1,0:T(8,128)(2,1)S(1)}, bf16[256,128]{1,0:T(8,128)(2,1)S(1)}, u32[]{:S(2)}, u32[]{:S(2)}) collective-permute-start(bf16[256,128]{1,0:T(8,128)(2,1)S(1)} %get-tuple-element.56), channel_id=1, source_target_pairs={{0,12},{1,13},{2,14},{3,15},{4,8},{5,9},{6,10},{7,11},{8,4},{9,5},... | collective-permute-start | bytes 196616 | tf_op jit(solution)/shard_map/ppermute | solution.py:358
  55.8 9.0 %collective-permute-start.15 = (bf16[256,128]{1,0:T(8,128)(2,1)S(1)}, bf16[256,128]{1,0:T(8,128)(2,1)S(1)}, u32[]{:S(2)}, u32[]{:S(2)}) collective-permute-start(bf16[256,128]{1,0:T(8,128)(2,1)S(1)} %get-tuple-element.57), channel_id=1, source_target_pairs={{0,8},{1,9},{2,10},{3,11},{4,0},{5,1},{6,2},{7,3},{8,12},{9,13},{1... | collective-permute-start | bytes 196616 | tf_op jit(solution)/shard_map/ppermute | solution.py:358
  64.7 11.2 %collective-permute-start.24 = (bf16[2,256,256]{2,1,0:T(8,128)(2,1)S(1)}, bf16[2,256,256]{2,1,0:T(8,128)(2,1)S(1)}, u32[]{:S(2)}, u32[]{:S(2)}) collective-permute-start(bf16[2,256,256]{2,1,0:T(8,128)(2,1)S(1)} %pad_maximum_fusion), channel_id=1, source_target_pairs={{0,4},{1,5},{2,6},{3,7},{4,12},{5,13},{6,14},{7,15},{8,0},{9,1},{1... | collective-permute-start | bytes 786440 | tf_op jit(solution)/shard_map/ppermute | solution.py:358
  66.7 9.3 %copy-start.7 = (bf16[256,256]{1,0:T(8,128)(2,1)S(1)}, bf16[256,256]{1,0:T(8,128)(2,1)}, u32[]{:S(2)}) copy-start(bf16[256,256]{1,0:T(8,128)(2,1)} %get-tuple-element.41.refs_0_) | copy-start | bytes 393220
  68.5 6.8 %collective-permute-start.19 = (bf16[256,128]{1,0:T(8,128)(2,1)S(1)}, bf16[256,128]{1,0:T(8,128)(2,1)S(1)}, u32[]{:S(2)}, u32[]{:S(2)}) collective-permute-start(bf16[256,128]{1,0:T(8,128)(2,1)S(1)} %get-tuple-element.62), channel_id=1, source_target_pairs={{0,4},{1,5},{2,6},{3,7},{4,12},{5,13},{6,14},{7,15},{8,0},{9,1},{1... | collective-permute-start | bytes 196616 | tf_op jit(solution)/shard_map/ppermute | solution.py:358
  68.6 6.7 %collective-permute-start.20 = (bf16[256,128]{1,0:T(8,128)(2,1)S(1)}, bf16[256,128]{1,0:T(8,128)(2,1)S(1)}, u32[]{:S(2)}, u32[]{:S(2)}) collective-permute-start(bf16[256,128]{1,0:T(8,128)(2,1)S(1)} %get-tuple-element.63), channel_id=1, source_target_pairs={{0,12},{1,13},{2,14},{3,15},{4,8},{5,9},{6,10},{7,11},{8,4},{9,5},... | collective-permute-start | bytes 196616 | tf_op jit(solution)/shard_map/ppermute | solution.py:358
  71.1 5.2 %copy-start.6 = (bf16[128,1024]{1,0:T(8,128)(2,1)S(1)}, bf16[128,1024]{1,0:T(8,128)(2,1)}, u32[]{:S(2)}) copy-start(bf16[128,1024]{1,0:T(8,128)(2,1)} %g0.3) | copy-start | bytes 786436
  71.1 4.9 %collective-permute-start.21 = (bf16[256,128]{1,0:T(8,128)(2,1)S(1)}, bf16[256,128]{1,0:T(8,128)(2,1)S(1)}, u32[]{:S(2)}, u32[]{:S(2)}) collective-permute-start(bf16[256,128]{1,0:T(8,128)(2,1)S(1)} %get-tuple-element.64), channel_id=1, source_target_pairs={{0,8},{1,9},{2,10},{3,11},{4,0},{5,1},{6,2},{7,3},{8,12},{9,13},{1... | collective-permute-start | bytes 196616 | tf_op jit(solution)/shard_map/ppermute | solution.py:358
  76.1 2.4 %collective-permute-start.25 = (bf16[4,256,256]{2,1,0:T(8,128)(2,1)S(1)}, bf16[4,256,256]{2,1,0:T(8,128)(2,1)S(1)}, u32[]{:S(2)}, u32[]{:S(2)}) collective-permute-start(bf16[4,256,256]{2,1,0:T(8,128)(2,1)S(1)} %get-tuple-element.70), channel_id=1, source_target_pairs={{0,1},{1,0},{2,3},{3,2},{4,5},{5,4},{6,7},{7,6},{8,9},{9,8},{10,11... | collective-permute-start | bytes 1572872 | tf_op jit(solution)/shard_map/ppermute | solution.py:358
  76.4 2.0 %collective-permute-start.22 = (bf16[512,256]{1,0:T(8,128)(2,1)S(1)}, bf16[512,256]{1,0:T(8,128)(2,1)S(1)}, u32[]{:S(2)}, u32[]{:S(2)}) collective-permute-start(bf16[512,256]{1,0:T(8,128)(2,1)S(1)} %shard_map.97.gated), channel_id=1, source_target_pairs={{0,1},{1,0},{2,3},{3,2},{4,5},{5,4},{6,7},{7,6},{8,9},{9,8},{10,11... | collective-permute-start | bytes 786440 | tf_op jit(solution)/shard_map/ppermute | solution.py:358
  79.3 10.2 %collective-permute-start.26 = (bf16[128,1024]{1,0:T(8,128)(2,1)S(1)}, bf16[128,1024]{1,0:T(8,128)(2,1)S(1)}, u32[]{:S(2)}, u32[]{:S(2)}) collective-permute-start(bf16[128,1024]{1,0:T(8,128)(2,1)S(1)} %get-tuple-element.72), channel_id=1, source_target_pairs={{0,18},{1,19},{2,16},{3,17},{4,22},{5,23},{6,20},{7,21},{8,26},{9,... | collective-permute-start | bytes 786440 | tf_op jit(solution)/shard_map/ppermute | solution.py:358
  80.8 13.5 %collective-permute-start.27 = (bf16[128,1024]{1,0:T(8,128)(2,1)S(1)}, bf16[128,1024]{1,0:T(8,128)(2,1)S(1)}, u32[]{:S(2)}, u32[]{:S(2)}) collective-permute-start(bf16[128,1024]{1,0:T(8,128)(2,1)S(1)} %get-tuple-element.73), channel_id=1, source_target_pairs={{0,2},{1,3},{2,0},{3,1},{4,6},{5,7},{6,4},{7,5},{8,10},{9,11},{10,... | collective-permute-start | bytes 786440 | tf_op jit(solution)/shard_map/ppermute | solution.py:358
  83.2 11.2 %collective-permute-start.28 = (bf16[128,1024]{1,0:T(8,128)(2,1)S(1)}, bf16[128,1024]{1,0:T(8,128)(2,1)S(1)}, u32[]{:S(2)}, u32[]{:S(2)}) collective-permute-start(bf16[128,1024]{1,0:T(8,128)(2,1)S(1)} %get-tuple-element.74), channel_id=1, source_target_pairs={{0,16},{1,17},{2,18},{3,19},{4,20},{5,21},{6,22},{7,23},{8,24},{9,... | collective-permute-start | bytes 786440 | tf_op jit(solution)/shard_map/ppermute | solution.py:358
